TPU v7x, 32 devices: a whole 2x2x4 slice. The times are simulated.
32 devices in a mesh: dp: 16 (over z, y, x), mp: 2 (over core).
Axes of the slice: x: 2, y: 2, z: 4, core: 2. Of those that a mesh axis runs over, the one named last changes fastest.
Arguments:
- out_grad: bfloat16 [2048, 4096], P('dp'), may hold values from -40 to 40
- gate_pre: bfloat16 [2048, 5120], P('dp', 'mp'), may hold values from -6 to 6
- up_pre: bfloat16 [2048, 5120], P('dp', 'mp'), may hold values from -40 to 40
- down_weight: bfloat16 [4096, 5120], P('dp', 'mp'), may hold values from -0.078125 to 0.078125
- row_moment: float32 [4096], P('dp'), may hold values from 0.05 to 0.5
- col_moment: float32 [5120], P('mp'), may hold values from 0.05 to 0.5
Outputs:
- update: float32 [4096, 5120], P('dp', 'mp')
- row_moment_new: float32 [4096], P('dp')
- col_moment_new: float32 [5120], P('mp')
- row_mean: float32 [], replicated
- gate_grad: bfloat16 [2048, 5120], P('dp', 'mp')
- up_grad: bfloat16 [2048, 5120], P('dp', 'mp')
All inputs are finite; a program needn't handle non-finite values.
Results may differ from a plain program's by a relative error of at most 0.0034.
Values may be sent and summed in bfloat16 or wider, within the bound.
No kernel may reach another device: no remote copies, remote signals or barrier semaphores. Data moves between devices by JAX's collectives and lax.ppermute only.
A program may use at most 128 MiB of HBM per device.

v0:
```python
import math

import jax
import jax.numpy as jnp
from jax import lax
from jax.sharding import PartitionSpec as P

TRAIN_STEP = 3


def gelu_parts(values):
    factor = math.sqrt(2.0 / math.pi)
    inner = factor * (values + 0.044715 * values * values * values)
    tangent = jnp.tanh(inner)
    activated = 0.5 * values * (1.0 + tangent)
    derivative = 0.5 * (1.0 + tangent) + 0.5 * values * (1.0 - tangent * tangent) * factor * (
        1.0 + 3.0 * 0.044715 * values * values
    )
    return (activated, derivative)


def local(out_grad, gate_pre, up_pre, down_weight, row_moment, col_moment):
    gate_value = gate_pre.astype(jnp.float32)
    up_value = up_pre.astype(jnp.float32)
    activated, derivative = gelu_parts(gate_value)
    hidden = (activated * up_value).astype(jnp.bfloat16)
    local_rows = down_weight.shape[0]
    local_units = down_weight.shape[1]
    token_count = out_grad.shape[0]
    hidden_grad = jnp.dot(
        out_grad,
        lax.all_gather(down_weight, "dp", axis=0, tiled=True),
        preferred_element_type=jnp.float32,
    )
    gate_grad = (hidden_grad * up_value * derivative).astype(jnp.bfloat16)
    up_grad = (hidden_grad * activated).astype(jnp.bfloat16)
    feature_share = lax.all_to_all(out_grad, "dp", split_axis=1, concat_axis=0, tiled=True)
    all_tokens = token_count * lax.axis_size("dp")
    product = lax.dot_general(
        feature_share,
        lax.all_gather(hidden, "dp", axis=0, tiled=True),
        (((0,), (0,)), ((), ())),
        preferred_element_type=jnp.float32,
    )
    grad = product * (1.0 / math.sqrt(all_tokens))
    decay = 1.0 - TRAIN_STEP ** (-0.8)
    squares = grad * grad + 1e-30
    total_rows = local_rows * lax.axis_size("dp")
    total_units = local_units * lax.axis_size("mp")
    row_sum = lax.psum(jnp.sum(squares, axis=1), "mp")
    col_sum = lax.psum(jnp.sum(squares, axis=0), "dp")
    row_moment_new = decay * row_moment + (1.0 - decay) * (row_sum / total_units)
    col_moment_new = decay * col_moment + (1.0 - decay) * (col_sum / total_rows)
    row_mean = lax.psum(jnp.sum(row_moment_new), "dp") / total_rows
    unclipped = grad / jnp.sqrt(row_moment_new[:, None] * col_moment_new[None, :] / row_mean)
    square_sum = lax.psum(jnp.sum(unclipped * unclipped), ("dp", "mp"))
    clip_norm = jnp.sqrt(square_sum / (total_rows * total_units))
    update = unclipped / jnp.maximum(1.0, clip_norm)
    return (update, row_moment_new, col_moment_new, row_mean, gate_grad, up_grad)


def solution(mesh):
    in_specs = (P("dp", None), P("dp", "mp"), P("dp", "mp"), P("dp", "mp"), P("dp"), P("mp"))
    out_specs = (P("dp", "mp"), P("dp"), P("mp"), P(), P("dp", "mp"), P("dp", "mp"))
    return jax.shard_map(local, mesh=mesh, in_specs=in_specs, out_specs=out_specs, check_vma=False)
```

profile of v0, /device:TPU:0, one launch (start us, length us, event | category | flops | bytes accessed | tf_op | source)
XLA Modules:
  0.0 540.6 jit_solution(4468166028695479024)
XLA Ops:
  7.2 0.0 all-gather.5.cloned.1.call-start
  7.2 0.7 all-gather.5.cloned.1.call-update
  7.9 0.0 copy-start
  7.9 0.0 all-gather.3.cloned.1.call-start
  8.0 237.0 %all-gather.5.cloned.1.call-done = bf16[4096,2560]{1,0:T(8,128)(2,1)} async-done(((bf16[256,2560]{1,0:T(8,128)(2,1)}), bf16[4096,2560]{1,0:T(8,128)(2,1)}) %all-gather.5.cloned.1.call-update) | async-done | bytes 20971536 | tf_op jit(solution)/shard_map/all_gather | solution.py:32
  245.0 12.6 %multiply_convert_fusion = (bf16[128,2560]{1,0:T(8,128)(2,1)}, bf16[128,2560]{1,0:T(8,128)(2,1)}, bf16[128,2560]{1,0:T(8,128)(2,1)}) fusion(bf16[128,2560]{1,0:T(8,128)(2,1)} %param.7, bf16[128,2560]{1,0:T(8,128)(2,1)} %param.8, bf16[128,4096]{1,0:T(8,128)(2,1)} %param.6, bf16[4096,2560]{1,0:T(8,128)(2,1)} %all-gather.5.cloned.1.call-done), kind=kOutput, calls=%fused_computation.27 | convolution fusion | flops 2693201920 | bytes 25296896 | tf_op jit(solution)/shard_map/dot_general | solution.py:30
  257.6 0.0 all-gather.3.cloned.1.call-update
  257.6 0.0 copy-done
  257.6 0.7 copy.14
  258.3 44.1 %all_to_all.19 = bf16[128,16,256]{0,2,1:T(8,128)(2,1)S(1)} all-to-all(bf16[128,16,256]{0,2,1:T(8,128)(2,1)S(1)} %bitcast.10), channel_id=1, replica_groups=mesh['dp'=16,'mp'=2] {'dp'}, dimensions={1} | all-to-all | bytes 2097152 | tf_op jit(solution)/shard_map/all_to_all | solution.py:37
  302.3 1.3 copy.15
  303.7 100.7 %all-gather.3.cloned.1.call-done = bf16[2048,2560]{1,0:T(8,128)(2,1)} async-done(((bf16[128,2560]{1,0:T(8,128)(2,1)}), bf16[2048,2560]{1,0:T(8,128)(2,1)}) %all-gather.3.cloned.1.call-update) | async-done | bytes 10485776 | tf_op jit(solution)/shard_map/all_gather | solution.py:41
  404.4 6.2 %fusion.1 = (f32[2560]{0:T(1024)S(1)}, f32[256]{0:T(256)S(1)}, f32[256,2560]{0,1:T(8,128)S(1)}) fusion(bf16[2048,2560]{1,0:T(8,128)(2,1)} %all-gather.3.cloned.1.call-done, bf16[2048,256]{1,0:T(8,128)(2,1)} %bitcast.11), kind=kOutput, calls=%fused_computation.12 | convolution fusion | flops 2687628544 | bytes 14167040 | tf_op jit(solution)/shard_map/dot_general | solution.py:39
  410.5 2.5 psum.28
  413.0 0.0 copy-done.4
  413.0 0.6 fusion.14
  413.6 73.9 %all-reduce = (f32[]{:T(128)}, f32[2560]{0:T(1024)S(1)}) all-reduce(f32[]{:T(128)} %get-tuple-element.28, f32[2560]{0:T(1024)S(1)} %get-tuple-element.24), channel_id=1, replica_groups=mesh['dp'=16,'mp'=2] {'dp'}, use_global_device_ids=true, to_apply=%region_5.0 | all-reduce | flops 2561 | bytes 20488 | tf_op jit(solution)/shard_map/psum | solution.py:54
  488.2 0.0 copy-done.2
  488.2 0.0 copy-start.1
  488.2 1.5 multiply_reduce_fusion
  489.7 37.1 %psum.31 = f32[]{:T(128)} all-reduce(f32[]{:T(128)} %multiply_reduce_fusion), channel_id=1, replica_groups=mesh['dp'=16,'mp'=2] {'dp','mp'}, use_global_device_ids=true, to_apply=%region_7.0 | all-reduce | flops 1 | bytes 8 | tf_op jit(solution)/shard_map/psum | solution.py:56
  527.4 2.0 broadcast_divide_fusion
  529.4 0.0 copy-done.3
  529.5 3.2 copy.16
  (5 shorter events, 0.0 us)
Async XLA Ops:
  7.2 237.8 %all-gather.5.cloned.1.call-start = ((), (), s32[]{:S(2)}) async-start(), calls=%async_computation.2 | async-start | bytes 22282240 | tf_op jit(solution)/shard_map/all_gather | solution.py:32
  7.9 249.7 %copy-start = (bf16[128,4096]{1,0:T(8,128)(2,1)S(1)}, bf16[128,4096]{1,0:T(8,128)(2,1)}, u32[]{:S(2)}) copy-start(bf16[128,4096]{1,0:T(8,128)(2,1)} %param.6) | copy-start | bytes 3145732
  7.9 396.4 %all-gather.3.cloned.1.call-start = ((), (), s32[]{:S(2)}) async-start(), calls=%async_computation.1 | async-start | bytes 11141120 | tf_op jit(solution)/shard_map/all_gather | solution.py:41
  404.4 8.7 %copy-start.4 = (f32[256]{0:T(256)S(1)}, f32[256]{0:T(256)}, u32[]{:S(2)}) copy-start(f32[256]{0:T(256)} %param.10) | copy-start | bytes 3076
  404.4 83.8 %copy-start.2 = (f32[2560]{0:T(1024)S(1)}, f32[2560]{0:T(1024)}, u32[]{:S(2)}) copy-start(f32[2560]{0:T(1024)} %param.11) | copy-start | bytes 30724
  413.6 115.8 %copy-start.3 = (f32[256]{0:T(256)}, f32[256]{0:T(256)S(1)}, u32[]{:S(2)}) copy-start(f32[256]{0:T(256)S(1)} %get-tuple-element.29) | copy-start | bytes 3076
  488.2 41.3 %copy-start.1 = (f32[2560]{0:T(1024)}, f32[2560]{0:T(1024)S(1)}, u32[]{:S(2)}) copy-start(f32[2560]{0:T(1024)S(1)} %multiply_add_fusion.1) | copy-start | bytes 30724
Sparse Core Ops, SparseCore 0:
  10.8 234.1 all-gather.4
  257.7 146.6 all-gather.2
where the time goes:
time: 542 us; the launch traced here: 541 us
  waiting for transfers between devices  338 us (62%)
  blocking collectives  158 us (29%)
  matrix products  18.7 us (3%)
  between operations  16.6 us (3%)
    all_gather x1, waiting for transfers between devices, local(): lax.all_gather(down_weight, 'dp', axis=0, tiled=True)  237 us
    all_gather x1, waiting for transfers between devices, local(): lax.all_gather(hidden, 'dp', axis=0, tiled=True)  101 us
    psum x1, blocking collectives, local(): row_mean = lax.psum(jnp.sum(row_moment_new), 'dp') / total_rows  73.9 us
    all_to_all x1, blocking collectives, local(): lax.all_to_all(out_grad, 'dp', split_axis=1, concat_axis=0, tiled=True)  44.1 us
    psum x1, blocking collectives, local(): square_sum = lax.psum(jnp.sum(unclipped * unclipped), ('dp', 'mp'))  37.1 us
    dot_general x1, matrix products, local(): jnp.dot(out_grad, lax.all_gather(down_weight, 'dp', axis=0, tiled=True),...  12.6 us
  transfers between devices with their start and end apart: 2, of which 2 were waited for; matrix products, arithmetic and copies ran while one was open for 0% of the time, Pallas kernels for 0%

commit v1 on v0

v1 whole, which is shorter than its diff:
```python
import math

import jax
import jax.numpy as jnp
from jax import lax
from jax.sharding import PartitionSpec as P

TRAIN_STEP = 3
INNER_BITS = 2


def gelu_parts(values):
    factor = math.sqrt(2.0 / math.pi)
    inner = factor * (values + 0.044715 * values * values * values)
    tangent = jnp.tanh(inner)
    activated = 0.5 * values * (1.0 + tangent)
    derivative = 0.5 * (1.0 + tangent) + 0.5 * values * (1.0 - tangent * tangent) * factor * (
        1.0 + 3.0 * 0.044715 * values * values
    )
    return (activated, derivative)


def flip(value, bits):
    size = lax.axis_size("dp")
    return lax.ppermute(value, "dp", [(i, i ^ bits) for i in range(size)])


def gather(block, bits):
    half = block.shape[1] // 2
    if len(bits) == 2:
        first = flip(block, bits[0])
        second = flip(block, bits[1])
        left = [block[:, :half], first[:, :half], second[:, :half], flip(first[:, :half], bits[1])]
        right = [block[:, half:], first[:, half:], second[:, half:], flip(second[:, half:], bits[0])]
        return left, right
    blocks = [block]
    for bit in bits:
        blocks = blocks + [flip(b, bit) for b in blocks]
    return [b[:, :half] for b in blocks], [b[:, half:] for b in blocks]


def scatter(part, bits):
    def send(value, bit):
        return flip(value.astype(jnp.bfloat16), bit).astype(jnp.float32)

    if len(bits) == 2:
        low, high = bits
        left3 = send(part(3, 0), low)
        right3 = send(part(3, 1), high)
        left1 = send(part(1, 0), low)
        right2 = send(part(2, 1), high)
        left2 = send(part(2, 0) + left3, high)
        right1 = send(part(1, 1) + right3, low)
        return part(0, 0) + left1 + left2, part(0, 1) + right2 + right1
    sides = []
    for side in range(2):
        values = [part(j, side) for j in range(2 ** len(bits))]
        for level in reversed(range(len(bits))):
            count = 2**level
            values = [values[j] + send(values[j + count], bits[level]) for j in range(count)]
        sides.append(values[0])
    return tuple(sides)


def group_sum(value, bits):
    for at in range(0, len(bits), 2):
        pair = bits[at : at + 2]
        if len(pair) == 2:
            first, second = flip(value, pair[0]), flip(value, pair[1])
            value = (value + first) + (second + flip(value, pair[0] | pair[1]))
        else:
            value = value + flip(value, pair[0])
    return value


def local(out_grad, gate_pre, up_pre, down_weight, row_moment, col_moment):
    size = lax.axis_size("dp")
    me = lax.axis_index("dp")
    rows, units = down_weight.shape
    tokens = out_grad.shape[0]
    half = units // 2
    all_bits = [1 << b for b in range(size.bit_length() - 1)]
    inner_bits, outer_bits = all_bits[:INNER_BITS], all_bits[INNER_BITS:]
    inner, outer = 2 ** len(inner_bits), 2 ** len(outer_bits)

    gate_value = gate_pre.astype(jnp.float32)
    up_value = up_pre.astype(jnp.float32)
    activated, derivative = gelu_parts(gate_value)
    hidden = (activated * up_value).astype(jnp.bfloat16)

    by_block = out_grad.reshape(tokens, size, rows).transpose(1, 0, 2)

    def features_of(k):
        picks = [lax.dynamic_index_in_dim(by_block, me ^ (k * inner + j), 0, keepdims=False) for j in range(inner)]
        return jnp.concatenate(picks, axis=1)

    shares = [features_of(0)] + [flip(features_of(k), k * inner) for k in range(1, outer)]
    share = jnp.concatenate(shares, axis=0)

    hidden_sides = gather(hidden, outer_bits)
    hidden_sides = [jnp.concatenate(side, axis=0) for side in hidden_sides]
    weight_sides = gather(down_weight, inner_bits)
    weight_sides = [jnp.concatenate(side, axis=0) for side in weight_sides]

    def grad_part(j, side):
        return lax.dot_general(
            share[:, j * rows : (j + 1) * rows],
            hidden_sides[side],
            (((0,), (0,)), ((), ())),
            preferred_element_type=jnp.float32,
        )

    def hidden_grad_part(k, side):
        return jnp.dot(shares[k], weight_sides[side], preferred_element_type=jnp.float32)

    product = jnp.concatenate(scatter(grad_part, inner_bits), axis=1)
    hidden_grad = jnp.concatenate(scatter(hidden_grad_part, outer_bits), axis=1)

    gate_grad = (hidden_grad * up_value * derivative).astype(jnp.bfloat16)
    up_grad = (hidden_grad * activated).astype(jnp.bfloat16)

    grad = product * (1.0 / math.sqrt(tokens * size))
    decay = 1.0 - TRAIN_STEP ** (-0.8)
    total_rows = rows * size
    total_units = units * lax.axis_size("mp")
    powers = grad * grad
    squares = powers + 1e-30
    row_sum = lax.psum(jnp.sum(squares, axis=1), "mp")
    row_moment_new = decay * row_moment + (1.0 - decay) * (row_sum / total_units)
    col_part = jnp.sum(squares, axis=0)
    scaled_part = jnp.sum(powers / row_moment_new[:, None], axis=0)
    total_part = jnp.broadcast_to(jnp.sum(row_moment_new), (128,))
    sums = group_sum(jnp.concatenate([col_part, scaled_part, total_part]), all_bits)
    col_moment_new = decay * col_moment + (1.0 - decay) * (sums[:units] / total_rows)
    row_mean = sums[2 * units] / total_rows
    square_sum = row_mean * lax.psum(jnp.sum(sums[units : 2 * units] / col_moment_new), "mp")
    clip_norm = jnp.sqrt(square_sum / (total_rows * total_units))
    row_factor = jnp.sqrt(row_mean / row_moment_new) / jnp.maximum(1.0, clip_norm)
    col_factor = 1.0 / jnp.sqrt(col_moment_new)
    update = grad * row_factor[:, None] * col_factor[None, :]
    return (update, row_moment_new, col_moment_new, row_mean, gate_grad, up_grad)


def solution(mesh):
    in_specs = (P("dp", None), P("dp", "mp"), P("dp", "mp"), P("dp", "mp"), P("dp"), P("mp"))
    out_specs = (P("dp", "mp"), P("dp"), P("mp"), P(), P("dp", "mp"), P("dp", "mp"))
    return jax.shard_map(local, mesh=mesh, in_specs=in_specs, out_specs=out_specs, check_vma=False)
```

time: 542 us -> 226 us (0.42)
  waiting for transfers between devices: 338 us -> 133 us
  blocking collectives: 158 us -> 5.62 us
  starting transfers between devices: 0.08 us -> 41.3 us
  between operations: 16.6 us -> 3.67 us
  local copies, waits for them, and re-layouts: 5.2 us -> 15.7 us
  other arithmetic: 4.1 us -> 9.61 us
    all_gather x2 -> x0, waiting for transfers between devices: 338 us -> none  [the longest x1 237 us: local(): lax.all_gather(down_weight, 'dp', axis=0, tiled=True)]
    ppermute x0 -> x29, waiting for transfers between devices: none -> 133 us  [flip(): return lax.ppermute(value, 'dp', [(i, i ^ bits) for i in range(size)])]
    psum x2 -> x1, blocking collectives: 111 us -> 3.16 us  [local(): lax.psum(jnp.sum(sums[units:2 * units] / col_moment_new), 'mp')]
    all_to_all x1 -> x0, blocking collectives: 44.1 us -> none  [local(): lax.all_to_all(out_grad, 'dp', split_axis=1, concat_axis=0, tiled=True)]
    ppermute x0 -> x29, starting transfers between devices: none -> 41.3 us  [flip(): return lax.ppermute(value, 'dp', [(i, i ^ bits) for i in range(size)])]
    another operation x0 -> x17, local copies, waits for them, and re-layouts: none -> 9.34 us
    dot_general x2 -> x16, matrix products: 18.7 us -> 17.1 us  [the longest x8 12.8 us: hidden_grad_part(): jnp.dot(shares[k], weight_sides[side], preferred_element_type=jnp.float32)]
  transfers between devices with their start and end apart: 2 -> 29, of which waited for: 2 -> 19; matrix products, arithmetic and copies ran while one was open for 0% -> 15% of each run, Pallas kernels for 0% -> 0%
where the time goes in v1:
time: 226 us
  waiting for transfers between devices  133 us (59%)
  starting transfers between devices  41.3 us (18%)
  matrix products  17.1 us (8%)
  local copies, waits for them, and re-layouts  15.7 us (7%)
  other arithmetic  9.61 us (4%)
  blocking collectives  5.62 us (2%)
  between operations  3.67 us (2%)
    ppermute x29, waiting for transfers between devices, flip(): return lax.ppermute(value, 'dp', [(i, i ^ bits) for i in range(size)])  133 us
    ppermute x29, starting transfers between devices, flip(): return lax.ppermute(value, 'dp', [(i, i ^ bits) for i in range(size)])  41.3 us
    dot_general x8, matrix products, hidden_grad_part(): jnp.dot(shares[k], weight_sides[side], preferred_element_type=jnp.float32)  12.8 us
    another operation x17, local copies, waits for them, and re-layouts  9.34 us
  transfers between devices with their start and end apart: 29, of which 19 were waited for; matrix products, arithmetic and copies ran while one was open for 15% of the time, Pallas kernels for 0%

profile of v1, /device:TPU:0, one launch (start us, length us, event | category | flops | bytes accessed | tf_op | source)
XLA Modules:
  0.0 225.6 jit_solution(9844398021235240994)
XLA Ops:
  0.6 3.0 %collective-permute-start.19 = (bf16[256,2560]{1,0:T(8,128)(2,1)}, bf16[256,2560]{1,0:T(8,128)(2,1)}, u32[]{:S(2)}, u32[]{:S(2)}) collective-permute-start(bf16[256,2560]{1,0:T(8,128)(2,1)} %param.9), channel_id=1, source_target_pairs={{0,2},{2,0},{4,6},{6,4},{8,10},{10,8},{12,14},{14,12},{16,18},{18,... | collective-permute-start | bytes 3932168 | tf_op jit(solution)/shard_map/ppermute | solution.py:25
  9.0 3.6 %collective-permute-start.2 = (bf16[128,1024]{1,0:T(8,128)(2,1)}, bf16[128,1024]{1,0:T(8,128)(2,1)}, u32[]{:S(2)}, u32[]{:S(2)}) collective-permute-start(bf16[128,1024]{1,0:T(8,128)(2,1)} %pad_maximum_fusion.10), channel_id=1, source_target_pairs={{0,24},{2,26},{4,28},{6,30},{8,16},{10,18},{12,20},{14,22},{16,8},... | collective-permute-start | bytes 786440 | tf_op jit(solution)/shard_map/ppermute | solution.py:25
  22.5 10.3 %collective-permute-done.19 = bf16[256,2560]{1,0:T(8,128)(2,1)} collective-permute-done((bf16[256,2560]{1,0:T(8,128)(2,1)}, bf16[256,2560]{1,0:T(8,128)(2,1)}, u32[]{:S(2)}, u32[]{:S(2)}) %collective-permute-start.19) | collective-permute-done | bytes 1310752 | tf_op jit(solution)/shard_map/ppermute | solution.py:25
  32.7 2.2 fusion.35
  40.0 11.2 %collective-permute-done.21 = bf16[256,1280]{1,0:T(8,128)(2,1)} collective-permute-done((bf16[256,1280]{1,0:T(8,128)(2,1)}, bf16[256,1280]{1,0:T(8,128)(2,1)}, u32[]{:S(2)}, u32[]{:S(2)}) %collective-permute-start.21) | collective-permute-done | bytes 655392 | tf_op jit(solution)/shard_map/ppermute | solution.py:25
  58.6 2.6 %collective-permute-start.27 = (bf16[128,1280]{1,0:T(8,128)(2,1)S(1)}, bf16[128,1280]{1,0:T(8,128)(2,1)S(1)}, u32[]{:S(2)}, u32[]{:S(2)}) collective-permute-start(bf16[128,1280]{1,0:T(8,128)(2,1)S(1)} %convolution_convert_fusion.4), channel_id=1, source_target_pairs={{0,16},{2,18},{4,20},{6,22},{8,24},{10,26},{12,28},{14,30},{16,0},... | collective-permute-start | bytes 983048 | tf_op jit(solution)/shard_map/ppermute | solution.py:25
  63.2 10.5 %collective-permute-done.23 = bf16[128,1280]{1,0:T(8,128)(2,1)S(1)} collective-permute-done((bf16[128,1280]{1,0:T(8,128)(2,1)S(1)}, bf16[128,1280]{1,0:T(8,128)(2,1)S(1)}, u32[]{:S(2)}, u32[]{:S(2)}) %collective-permute-start.23) | collective-permute-done | bytes 327712 | tf_op jit(solution)/shard_map/ppermute | solution.py:25
  75.6 13.1 %collective-permute-done.27 = bf16[128,1280]{1,0:T(8,128)(2,1)S(1)} collective-permute-done((bf16[128,1280]{1,0:T(8,128)(2,1)S(1)}, bf16[128,1280]{1,0:T(8,128)(2,1)S(1)}, u32[]{:S(2)}, u32[]{:S(2)}) %collective-permute-start.27) | collective-permute-done | bytes 327712 | tf_op jit(solution)/shard_map/ppermute | solution.py:25
  90.5 2.5 %collective-permute-start.28 = (bf16[128,1280]{1,0:T(8,128)(2,1)S(1)}, bf16[128,1280]{1,0:T(8,128)(2,1)S(1)}, u32[]{:S(2)}, u32[]{:S(2)}) collective-permute-start(bf16[128,1280]{1,0:T(8,128)(2,1)S(1)} %fusion.7), channel_id=1, source_target_pairs={{0,8},{2,10},{4,12},{6,14},{8,0},{10,2},{12,4},{14,6},{16,24},{18,... | collective-permute-start | bytes 983048 | tf_op jit(solution)/shard_map/ppermute | solution.py:25
  93.0 9.3 %collective-permute-done.24 = bf16[128,1280]{1,0:T(8,128)(2,1)S(1)} collective-permute-done((bf16[128,1280]{1,0:T(8,128)(2,1)S(1)}, bf16[128,1280]{1,0:T(8,128)(2,1)S(1)}, u32[]{:S(2)}, u32[]{:S(2)}) %collective-permute-start.24) | collective-permute-done | bytes 327712 | tf_op jit(solution)/shard_map/ppermute | solution.py:25
  106.2 2.2 multiply_convert_fusion
  109.6 3.8 %collective-permute-start.4 = (bf16[128,2560]{1,0:T(8,128)(2,1)S(1)}, bf16[128,2560]{1,0:T(8,128)(2,1)S(1)}, u32[]{:S(2)}, u32[]{:S(2)}) collective-permute-start(bf16[128,2560]{1,0:T(8,128)(2,1)S(1)} %get-tuple-element.14), channel_id=1, source_target_pairs={{0,16},{2,18},{4,20},{6,22},{8,24},{10,26},{12,28},{14,30},{16,0},... | collective-permute-start | bytes 1966088 | tf_op jit(solution)/shard_map/ppermute | solution.py:25
  113.5 20.2 %collective-permute-done.3 = bf16[128,2560]{1,0:T(8,128)(2,1)S(1)} collective-permute-done((bf16[128,2560]{1,0:T(8,128)(2,1)S(1)}, bf16[128,2560]{1,0:T(8,128)(2,1)S(1)}, u32[]{:S(2)}, u32[]{:S(2)}) %collective-permute-start.3) | collective-permute-done | bytes 655392 | tf_op jit(solution)/shard_map/ppermute | solution.py:25
  133.8 12.5 %collective-permute-done.4 = bf16[128,2560]{1,0:T(8,128)(2,1)S(1)} collective-permute-done((bf16[128,2560]{1,0:T(8,128)(2,1)S(1)}, bf16[128,2560]{1,0:T(8,128)(2,1)S(1)}, u32[]{:S(2)}, u32[]{:S(2)}) %collective-permute-start.4) | collective-permute-done | bytes 655392 | tf_op jit(solution)/shard_map/ppermute | solution.py:25
  147.4 4.6 %collective-permute-done.5 = bf16[128,1280]{1,0:T(8,128)(2,1)S(1)} collective-permute-done((bf16[128,1280]{1,0:T(8,128)(2,1)S(1)}, bf16[128,1280]{1,0:T(8,128)(2,1)S(1)}, u32[]{:S(2)}, u32[]{:S(2)}) %collective-permute-start.5) | collective-permute-done | bytes 327712 | tf_op jit(solution)/shard_map/ppermute | solution.py:25
  159.7 10.7 %collective-permute-done.7 = bf16[256,1280]{1,0:T(8,128)(2,1)S(1)} collective-permute-done((bf16[256,1280]{1,0:T(8,128)(2,1)S(1)}, bf16[256,1280]{1,0:T(8,128)(2,1)S(1)}, u32[]{:S(2)}, u32[]{:S(2)}) %collective-permute-start.7) | collective-permute-done | bytes 655392 | tf_op jit(solution)/shard_map/ppermute | solution.py:25
  175.7 8.7 %collective-permute-done.6 = bf16[256,1280]{1,0:T(8,128)(2,1)S(1)} collective-permute-done((bf16[256,1280]{1,0:T(8,128)(2,1)S(1)}, bf16[256,1280]{1,0:T(8,128)(2,1)S(1)}, u32[]{:S(2)}, u32[]{:S(2)}) %collective-permute-start.6) | collective-permute-done | bytes 655392 | tf_op jit(solution)/shard_map/ppermute | solution.py:25
  184.4 4.2 %collective-permute-done.8 = bf16[256,1280]{1,0:T(8,128)(2,1)S(1)} collective-permute-done((bf16[256,1280]{1,0:T(8,128)(2,1)S(1)}, bf16[256,1280]{1,0:T(8,128)(2,1)S(1)}, u32[]{:S(2)}, u32[]{:S(2)}) %collective-permute-start.8) | collective-permute-done | bytes 655392 | tf_op jit(solution)/shard_map/ppermute | solution.py:25
  189.2 8.6 %collective-permute-done.10 = bf16[256,1280]{1,0:T(8,128)(2,1)S(1)} collective-permute-done((bf16[256,1280]{1,0:T(8,128)(2,1)S(1)}, bf16[256,1280]{1,0:T(8,128)(2,1)S(1)}, u32[]{:S(2)}, u32[]{:S(2)}) %collective-permute-start.10) | collective-permute-done | bytes 655392 | tf_op jit(solution)/shard_map/ppermute | solution.py:25
  198.8 2.5 %psum.14 = f32[256]{0:T(256)S(1)} all-reduce(f32[256]{0:T(256)S(1)} %add_reduce_fusion), channel_id=1, replica_groups=mesh['dp'=16,'mp'=2] {'mp'}, use_global_device_ids=true, to_apply=%region_2.3 | all-reduce | flops 256 | bytes 2048 | tf_op jit(solution)/shard_map/psum | solution.py:128
  207.6 2.4 %collective-permute-done.15 = f32[5248]{0:T(1024)S(1)} collective-permute-done((f32[5248]{0:T(1024)S(1)}, f32[5248]{0:T(1024)S(1)}, u32[]{:S(2)}, u32[]{:S(2)}) %collective-permute-start.15) | collective-permute-done | bytes 21024 | tf_op jit(solution)/shard_map/ppermute | solution.py:25
  211.4 3.1 %collective-permute-start.18 = (f32[5248]{0:T(1024)S(1)}, f32[5248]{0:T(1024)S(1)}, u32[]{:S(2)}, u32[]{:S(2)}) collective-permute-start(f32[5248]{0:T(1024)S(1)} %add_add_fusion.1), channel_id=1, source_target_pairs={{0,24},{2,26},{4,28},{6,30},{8,16},{10,18},{12,20},{14,22},{16,8},... | collective-permute-start | bytes 62984 | tf_op jit(solution)/shard_map/ppermute | solution.py:25
  214.9 2.1 collective-permute-done.18
  218.1 3.2 %psum.15 = f32[]{:T(128)} all-reduce(f32[]{:T(128)} %get-tuple-element.8), channel_id=1, replica_groups=mesh['dp'=16,'mp'=2] {'mp'}, use_global_device_ids=true, to_apply=%region_6.7 | all-reduce | flops 1 | bytes 8 | tf_op jit(solution)/shard_map/psum | solution.py:136
  (111 shorter events, 64.9 us)
Async XLA Ops:
  0.6 32.1 %collective-permute-start.19 = (bf16[256,2560]{1,0:T(8,128)(2,1)}, bf16[256,2560]{1,0:T(8,128)(2,1)}, u32[]{:S(2)}, u32[]{:S(2)}) collective-permute-start(bf16[256,2560]{1,0:T(8,128)(2,1)} %param.9), channel_id=1, source_target_pairs={{0,2},{2,0},{4,6},{6,4},{8,10},{10,8},{12,14},{14,12},{16,18},{18,... | collective-permute-start | bytes 3932168 | tf_op jit(solution)/shard_map/ppermute | solution.py:25
  3.6 34.7 %collective-permute-start.20 = (bf16[256,2560]{1,0:T(8,128)(2,1)}, bf16[256,2560]{1,0:T(8,128)(2,1)S(1)}, u32[]{:S(2)}, u32[]{:S(2)}) collective-permute-start(bf16[256,2560]{1,0:T(8,128)(2,1)} %param.9), channel_id=1, source_target_pairs={{0,4},{2,6},{4,0},{6,2},{8,12},{10,14},{12,8},{14,10},{16,20},{18,... | collective-permute-start | bytes 3932168 | tf_op jit(solution)/shard_map/ppermute | solution.py:25
  9.0 30.9 %collective-permute-start.2 = (bf16[128,1024]{1,0:T(8,128)(2,1)}, bf16[128,1024]{1,0:T(8,128)(2,1)}, u32[]{:S(2)}, u32[]{:S(2)}) collective-permute-start(bf16[128,1024]{1,0:T(8,128)(2,1)} %pad_maximum_fusion.10), channel_id=1, source_target_pairs={{0,24},{2,26},{4,28},{6,30},{8,16},{10,18},{12,20},{14,22},{16,8},... | collective-permute-start | bytes 786440 | tf_op jit(solution)/shard_map/ppermute | solution.py:25
  17.1 44.1 %collective-permute-start.1 = (bf16[128,1024]{1,0:T(8,128)(2,1)}, bf16[128,1024]{1,0:T(8,128)(2,1)}, u32[]{:S(2)}, u32[]{:S(2)}) collective-permute-start(bf16[128,1024]{1,0:T(8,128)(2,1)} %pad_maximum_fusion.9), channel_id=1, source_target_pairs={{0,16},{2,18},{4,20},{6,22},{8,24},{10,26},{12,28},{14,30},{16,0},... | collective-permute-start | bytes 786440 | tf_op jit(solution)/shard_map/ppermute | solution.py:25
  21.7 33.0 %collective-permute-start = (bf16[128,1024]{1,0:T(8,128)(2,1)}, bf16[128,1024]{1,0:T(8,128)(2,1)}, u32[]{:S(2)}, u32[]{:S(2)}) collective-permute-start(bf16[128,1024]{1,0:T(8,128)(2,1)} %pad_maximum_fusion.8), channel_id=1, source_target_pairs={{0,8},{2,10},{4,12},{6,14},{8,0},{10,2},{12,4},{14,6},{16,24},{18,... | collective-permute-start | bytes 786440 | tf_op jit(solution)/shard_map/ppermute | solution.py:25
  34.9 16.2 %collective-permute-start.21 = (bf16[256,1280]{1,0:T(8,128)(2,1)}, bf16[256,1280]{1,0:T(8,128)(2,1)}, u32[]{:S(2)}, u32[]{:S(2)}) collective-permute-start(bf16[256,1280]{1,0:T(8,128)(2,1)} %get-tuple-element.19), channel_id=1, source_target_pairs={{0,4},{2,6},{4,0},{6,2},{8,12},{10,14},{12,8},{14,10},{16,20},{18,... | collective-permute-start | bytes 1966088 | tf_op jit(solution)/shard_map/ppermute | solution.py:25
  38.4 18.7 %collective-permute-start.25 = (bf16[256,1280]{1,0:T(8,128)(2,1)S(1)}, bf16[256,1280]{1,0:T(8,128)(2,1)S(1)}, u32[]{:S(2)}, u32[]{:S(2)}) collective-permute-start(bf16[256,1280]{1,0:T(8,128)(2,1)S(1)} %get-tuple-element.18), channel_id=1, source_target_pairs={{0,2},{2,0},{4,6},{6,4},{8,10},{10,8},{12,14},{14,12},{16,18},{18,... | collective-permute-start | bytes 1966088 | tf_op jit(solution)/shard_map/ppermute | solution.py:25
  53.1 20.6 %collective-permute-start.23 = (bf16[128,1280]{1,0:T(8,128)(2,1)S(1)}, bf16[128,1280]{1,0:T(8,128)(2,1)S(1)}, u32[]{:S(2)}, u32[]{:S(2)}) collective-permute-start(bf16[128,1280]{1,0:T(8,128)(2,1)S(1)} %convolution_convert_fusion.6), channel_id=1, source_target_pairs={{0,8},{2,10},{4,12},{6,14},{8,0},{10,2},{12,4},{14,6},{16,24},{18,... | collective-permute-start | bytes 983048 | tf_op jit(solution)/shard_map/ppermute | solution.py:25
  56.6 36.4 %collective-permute-start.22 = (bf16[128,1280]{1,0:T(8,128)(2,1)S(1)}, bf16[128,1280]{1,0:T(8,128)(2,1)S(1)}, u32[]{:S(2)}, u32[]{:S(2)}) collective-permute-start(bf16[128,1280]{1,0:T(8,128)(2,1)S(1)} %convolution_convert_fusion.7), channel_id=1, source_target_pairs={{0,8},{2,10},{4,12},{6,14},{8,0},{10,2},{12,4},{14,6},{16,24},{18,... | collective-permute-start | bytes 983048 | tf_op jit(solution)/shard_map/ppermute | solution.py:25
  58.6 30.1 %collective-permute-start.27 = (bf16[128,1280]{1,0:T(8,128)(2,1)S(1)}, bf16[128,1280]{1,0:T(8,128)(2,1)S(1)}, u32[]{:S(2)}, u32[]{:S(2)}) collective-permute-start(bf16[128,1280]{1,0:T(8,128)(2,1)S(1)} %convolution_convert_fusion.4), channel_id=1, source_target_pairs={{0,16},{2,18},{4,20},{6,22},{8,24},{10,26},{12,28},{14,30},{16,0},... | collective-permute-start | bytes 983048 | tf_op jit(solution)/shard_map/ppermute | solution.py:25
  62.7 41.5 %collective-permute-start.26 = (bf16[128,1280]{1,0:T(8,128)(2,1)S(1)}, bf16[128,1280]{1,0:T(8,128)(2,1)S(1)}, u32[]{:S(2)}, u32[]{:S(2)}) collective-permute-start(bf16[128,1280]{1,0:T(8,128)(2,1)S(1)} %convolution_convert_fusion.5), channel_id=1, source_target_pairs={{0,16},{2,18},{4,20},{6,22},{8,24},{10,26},{12,28},{14,30},{16,0},... | collective-permute-start | bytes 983048 | tf_op jit(solution)/shard_map/ppermute | solution.py:25
  75.6 26.7 %collective-permute-start.24 = (bf16[128,1280]{1,0:T(8,128)(2,1)S(1)}, bf16[128,1280]{1,0:T(8,128)(2,1)S(1)}, u32[]{:S(2)}, u32[]{:S(2)}) collective-permute-start(bf16[128,1280]{1,0:T(8,128)(2,1)S(1)} %fusion.6), channel_id=1, source_target_pairs={{0,16},{2,18},{4,20},{6,22},{8,24},{10,26},{12,28},{14,30},{16,0},... | collective-permute-start | bytes 983048 | tf_op jit(solution)/shard_map/ppermute | solution.py:25
  90.5 15.2 %collective-permute-start.28 = (bf16[128,1280]{1,0:T(8,128)(2,1)S(1)}, bf16[128,1280]{1,0:T(8,128)(2,1)S(1)}, u32[]{:S(2)}, u32[]{:S(2)}) collective-permute-start(bf16[128,1280]{1,0:T(8,128)(2,1)S(1)} %fusion.7), channel_id=1, source_target_pairs={{0,8},{2,10},{4,12},{6,14},{8,0},{10,2},{12,4},{14,6},{16,24},{18,... | collective-permute-start | bytes 983048 | tf_op jit(solution)/shard_map/ppermute | solution.py:25
  108.4 25.3 %collective-permute-start.3 = (bf16[128,2560]{1,0:T(8,128)(2,1)S(1)}, bf16[128,2560]{1,0:T(8,128)(2,1)S(1)}, u32[]{:S(2)}, u32[]{:S(2)}) collective-permute-start(bf16[128,2560]{1,0:T(8,128)(2,1)S(1)} %get-tuple-element.14), channel_id=1, source_target_pairs={{0,8},{2,10},{4,12},{6,14},{8,0},{10,2},{12,4},{14,6},{16,24},{18,... | collective-permute-start | bytes 1966088 | tf_op jit(solution)/shard_map/ppermute | solution.py:25
  109.6 36.7 %collective-permute-start.4 = (bf16[128,2560]{1,0:T(8,128)(2,1)S(1)}, bf16[128,2560]{1,0:T(8,128)(2,1)S(1)}, u32[]{:S(2)}, u32[]{:S(2)}) collective-permute-start(bf16[128,2560]{1,0:T(8,128)(2,1)S(1)} %get-tuple-element.14), channel_id=1, source_target_pairs={{0,16},{2,18},{4,20},{6,22},{8,24},{10,26},{12,28},{14,30},{16,0},... | collective-permute-start | bytes 1966088 | tf_op jit(solution)/shard_map/ppermute | solution.py:25
  133.7 18.3 %collective-permute-start.5 = (bf16[128,1280]{1,0:T(8,128)(2,1)S(1)}, bf16[128,1280]{1,0:T(8,128)(2,1)S(1)}, u32[]{:S(2)}, u32[]{:S(2)}) collective-permute-start(bf16[128,1280]{1,0:T(8,128)(2,1)S(1)} %get-tuple-element.41), channel_id=1, source_target_pairs={{0,16},{2,18},{4,20},{6,22},{8,24},{10,26},{12,28},{14,30},{16,0},... | collective-permute-start | bytes 983048 | tf_op jit(solution)/shard_map/ppermute | solution.py:25
  146.4 9.1 %collective-permute-start.9 = (bf16[128,1280]{1,0:T(8,128)(2,1)S(1)}, bf16[128,1280]{1,0:T(8,128)(2,1)S(1)}, u32[]{:S(2)}, u32[]{:S(2)}) collective-permute-start(bf16[128,1280]{1,0:T(8,128)(2,1)S(1)} %get-tuple-element.40), channel_id=1, source_target_pairs={{0,8},{2,10},{4,12},{6,14},{8,0},{10,2},{12,4},{14,6},{16,24},{18,... | collective-permute-start | bytes 983048 | tf_op jit(solution)/shard_map/ppermute | solution.py:25
  152.6 17.7 %collective-permute-start.7 = (bf16[256,1280]{1,0:T(8,128)(2,1)S(1)}, bf16[256,1280]{1,0:T(8,128)(2,1)S(1)}, u32[]{:S(2)}, u32[]{:S(2)}) collective-permute-start(bf16[256,1280]{1,0:T(8,128)(2,1)S(1)} %convolution_convert_fusion.2), channel_id=1, source_target_pairs={{0,2},{2,0},{4,6},{6,4},{8,10},{10,8},{12,14},{14,12},{16,18},{18,... | collective-permute-start | bytes 1966088 | tf_op jit(solution)/shard_map/ppermute | solution.py:25
  156.0 17.6 %collective-permute-start.11 = (bf16[256,1280]{1,0:T(8,128)(2,1)S(1)}, bf16[256,1280]{1,0:T(8,128)(2,1)S(1)}, u32[]{:S(2)}, u32[]{:S(2)}) collective-permute-start(bf16[256,1280]{1,0:T(8,128)(2,1)S(1)} %convolution_convert_fusion), channel_id=1, source_target_pairs={{0,4},{2,6},{4,0},{6,2},{8,12},{10,14},{12,8},{14,10},{16,20},{18,... | collective-permute-start | bytes 1966088 | tf_op jit(solution)/shard_map/ppermute | solution.py:25
  158.1 26.2 %collective-permute-start.6 = (bf16[256,1280]{1,0:T(8,128)(2,1)S(1)}, bf16[256,1280]{1,0:T(8,128)(2,1)S(1)}, u32[]{:S(2)}, u32[]{:S(2)}) collective-permute-start(bf16[256,1280]{1,0:T(8,128)(2,1)S(1)} %convolution_convert_fusion.3), channel_id=1, source_target_pairs={{0,2},{2,0},{4,6},{6,4},{8,10},{10,8},{12,14},{14,12},{16,18},{18,... | collective-permute-start | bytes 1966088 | tf_op jit(solution)/shard_map/ppermute | solution.py:25
  170.9 17.7 %collective-permute-start.8 = (bf16[256,1280]{1,0:T(8,128)(2,1)S(1)}, bf16[256,1280]{1,0:T(8,128)(2,1)S(1)}, u32[]{:S(2)}, u32[]{:S(2)}) collective-permute-start(bf16[256,1280]{1,0:T(8,128)(2,1)S(1)} %fusion.2), channel_id=1, source_target_pairs={{0,4},{2,6},{4,0},{6,2},{8,12},{10,14},{12,8},{14,10},{16,20},{18,... | collective-permute-start | bytes 1966088 | tf_op jit(solution)/shard_map/ppermute | solution.py:25
  173.0 24.8 %collective-permute-start.10 = (bf16[256,1280]{1,0:T(8,128)(2,1)S(1)}, bf16[256,1280]{1,0:T(8,128)(2,1)S(1)}, u32[]{:S(2)}, u32[]{:S(2)}) collective-permute-start(bf16[256,1280]{1,0:T(8,128)(2,1)S(1)} %convolution_convert_fusion.1), channel_id=1, source_target_pairs={{0,4},{2,6},{4,0},{6,2},{8,12},{10,14},{12,8},{14,10},{16,20},{18,... | collective-permute-start | bytes 1966088 | tf_op jit(solution)/shard_map/ppermute | solution.py:25
  174.1 23.7 %collective-permute-start.12 = (bf16[256,1280]{1,0:T(8,128)(2,1)S(1)}, bf16[256,1280]{1,0:T(8,128)(2,1)S(1)}, u32[]{:S(2)}, u32[]{:S(2)}) collective-permute-start(bf16[256,1280]{1,0:T(8,128)(2,1)S(1)} %fusion.3), channel_id=1, source_target_pairs={{0,2},{2,0},{4,6},{6,4},{8,10},{10,8},{12,14},{14,12},{16,18},{18,... | collective-permute-start | bytes 1966088 | tf_op jit(solution)/shard_map/ppermute | solution.py:25
  211.4 5.6 %collective-permute-start.18 = (f32[5248]{0:T(1024)S(1)}, f32[5248]{0:T(1024)S(1)}, u32[]{:S(2)}, u32[]{:S(2)}) collective-permute-start(f32[5248]{0:T(1024)S(1)} %add_add_fusion.1), channel_id=1, source_target_pairs={{0,24},{2,26},{4,28},{6,30},{8,16},{10,18},{12,20},{14,22},{16,8},... | collective-permute-start | bytes 62984 | tf_op jit(solution)/shard_map/ppermute | solution.py:25
  (14 other events, 122.6 us)

commit v2 on v1

--- a/solution.py
+++ b/solution.py
@@ -83,10 +83,8 @@
     inner_bits, outer_bits = all_bits[:INNER_BITS], all_bits[INNER_BITS:]
     inner, outer = 2 ** len(inner_bits), 2 ** len(outer_bits)
 
-    gate_value = gate_pre.astype(jnp.float32)
-    up_value = up_pre.astype(jnp.float32)
-    activated, derivative = gelu_parts(gate_value)
-    hidden = (activated * up_value).astype(jnp.bfloat16)
+    activated, _ = gelu_parts(gate_pre.astype(jnp.float32))
+    hidden = (activated * up_pre.astype(jnp.float32)).astype(jnp.bfloat16)
 
     by_block = out_grad.reshape(tokens, size, rows).transpose(1, 0, 2)
 
@@ -116,7 +114,9 @@
     product = jnp.concatenate(scatter(grad_part, inner_bits), axis=1)
     hidden_grad = jnp.concatenate(scatter(hidden_grad_part, outer_bits), axis=1)
 
-    gate_grad = (hidden_grad * up_value * derivative).astype(jnp.bfloat16)
+    gate_late, up_late, hidden_grad = lax.optimization_barrier((gate_pre, up_pre, hidden_grad))
+    activated, derivative = gelu_parts(gate_late.astype(jnp.float32))
+    gate_grad = (hidden_grad * up_late.astype(jnp.float32) * derivative).astype(jnp.bfloat16)
     up_grad = (hidden_grad * activated).astype(jnp.bfloat16)
 
     grad = product * (1.0 / math.sqrt(tokens * size))

time: 226 us -> 205 us (0.907)
  waiting for transfers between devices: 133 us -> 107 us
  matrix products: 17.1 us -> 21.6 us
  local copies, waits for them, and re-layouts: 15.7 us -> 11.7 us
    ppermute x29, waiting for transfers between devices: 133 us -> 107 us  [flip(): return lax.ppermute(value, 'dp', [(i, i ^ bits) for i in range(size)])]
    another operation x17, local copies, waits for them, and re-layouts: 9.34 us -> 3.5 us
    dot_general x8, matrix products: 12.8 us -> 17.3 us  [hidden_grad_part(): jnp.dot(shares[k], weight_sides[side], preferred_element_type=jnp.float32)]
  transfers between devices with their start and end apart: 29 -> 29, of which waited for: 19 -> 12; matrix products, arithmetic and copies ran while one was open for 15% -> 17% of each run, Pallas kernels for 0% -> 0%
where the time goes in v2:
time: 205 us; the launch traced here: 204 us
  waiting for transfers between devices  107 us (52%)
  starting transfers between devices  43.5 us (21%)
  matrix products  21.6 us (11%)
  local copies, waits for them, and re-layouts  11.7 us (6%)
  other arithmetic  10.2 us (5%)
  blocking collectives  5.78 us (3%)
  between operations  3.88 us (2%)
    ppermute x29, waiting for transfers between devices, flip(): return lax.ppermute(value, 'dp', [(i, i ^ bits) for i in range(size)])  107 us
    ppermute x29, starting transfers between devices, flip(): return lax.ppermute(value, 'dp', [(i, i ^ bits) for i in range(size)])  43.5 us
    dot_general x8, matrix products, hidden_grad_part(): jnp.dot(shares[k], weight_sides[side], preferred_element_type=jnp.float32)  17.3 us
    dot_general x8, matrix products, grad_part(): lax.dot_general(share[:, j * rows:(j + 1) * rows], hidden_sides[side], ((...  4.27 us
  transfers between devices with their start and end apart: 29, of which 12 were waited for; matrix products, arithmetic and copies ran while one was open for 17% of the time, Pallas kernels for 0%

profile of v2, /device:TPU:0, one launch (start us, length us, event | category | flops | bytes accessed | tf_op | source)
XLA Modules:
  0.0 203.9 jit_solution(14628933487906181977)
XLA Ops:
  4.6 5.0 %collective-permute-start.2 = (bf16[128,1024]{1,0:T(8,128)(2,1)}, bf16[128,1024]{1,0:T(8,128)(2,1)}, u32[]{:S(2)}, u32[]{:S(2)}) collective-permute-start(bf16[128,1024]{1,0:T(8,128)(2,1)} %pad_maximum_fusion.10), channel_id=1, source_target_pairs={{0,24},{2,26},{4,28},{6,30},{8,16},{10,18},{12,20},{14,22},{16,8},... | collective-permute-start | bytes 786440 | tf_op jit(solution)/shard_map/ppermute | solution.py:25
  20.0 12.3 %collective-permute-done.1 = bf16[128,1024]{1,0:T(8,128)(2,1)} collective-permute-done((bf16[128,1024]{1,0:T(8,128)(2,1)}, bf16[128,1024]{1,0:T(8,128)(2,1)}, u32[]{:S(2)}, u32[]{:S(2)}) %collective-permute-start.1) | collective-permute-done | bytes 262176 | tf_op jit(solution)/shard_map/ppermute | solution.py:25
  33.6 14.7 %collective-permute-done.3 = bf16[128,2560]{1,0:T(8,128)(2,1)} collective-permute-done((bf16[128,2560]{1,0:T(8,128)(2,1)S(1)}, bf16[128,2560]{1,0:T(8,128)(2,1)}, u32[]{:S(2)}, u32[]{:S(2)}) %collective-permute-start.3) | collective-permute-done | bytes 655392 | tf_op jit(solution)/shard_map/ppermute | solution.py:25
  49.4 2.7 %collective-permute-start.5 = (bf16[128,1280]{1,0:T(8,128)(2,1)S(1)}, bf16[128,1280]{1,0:T(8,128)(2,1)S(1)}, u32[]{:S(2)}, u32[]{:S(2)}) collective-permute-start(bf16[128,1280]{1,0:T(8,128)(2,1)S(1)} %get-tuple-element.46), channel_id=1, source_target_pairs={{0,16},{2,18},{4,20},{6,22},{8,24},{10,26},{12,28},{14,30},{16,0},... | collective-permute-start | bytes 983048 | tf_op jit(solution)/shard_map/ppermute | solution.py:25
  52.2 19.9 %collective-permute-done.4 = bf16[128,2560]{1,0:T(8,128)(2,1)S(1)} collective-permute-done((bf16[128,2560]{1,0:T(8,128)(2,1)S(1)}, bf16[128,2560]{1,0:T(8,128)(2,1)S(1)}, u32[]{:S(2)}, u32[]{:S(2)}) %collective-permute-start.4) | collective-permute-done | bytes 655392 | tf_op jit(solution)/shard_map/ppermute | solution.py:25
  72.2 5.0 %collective-permute-done.5 = bf16[128,1280]{1,0:T(8,128)(2,1)S(1)} collective-permute-done((bf16[128,1280]{1,0:T(8,128)(2,1)S(1)}, bf16[128,1280]{1,0:T(8,128)(2,1)S(1)}, u32[]{:S(2)}, u32[]{:S(2)}) %collective-permute-start.5) | collective-permute-done | bytes 327712 | tf_op jit(solution)/shard_map/ppermute | solution.py:25
  80.5 3.7 %collective-permute-done.9 = bf16[128,1280]{1,0:T(8,128)(2,1)S(1)} collective-permute-done((bf16[128,1280]{1,0:T(8,128)(2,1)S(1)}, bf16[128,1280]{1,0:T(8,128)(2,1)S(1)}, u32[]{:S(2)}, u32[]{:S(2)}) %collective-permute-start.9) | collective-permute-done | bytes 327712 | tf_op jit(solution)/shard_map/ppermute | solution.py:25
  90.5 5.0 %collective-permute-done.7 = bf16[256,1280]{1,0:T(8,128)(2,1)S(1)} collective-permute-done((bf16[256,1280]{1,0:T(8,128)(2,1)S(1)}, bf16[256,1280]{1,0:T(8,128)(2,1)S(1)}, u32[]{:S(2)}, u32[]{:S(2)}) %collective-permute-start.7) | collective-permute-done | bytes 655392 | tf_op jit(solution)/shard_map/ppermute | solution.py:25
  97.5 18.9 %collective-permute-done.11 = bf16[256,1280]{1,0:T(8,128)(2,1)S(1)} collective-permute-done((bf16[256,1280]{1,0:T(8,128)(2,1)S(1)}, bf16[256,1280]{1,0:T(8,128)(2,1)S(1)}, u32[]{:S(2)}, u32[]{:S(2)}) %collective-permute-start.11) | collective-permute-done | bytes 655392 | tf_op jit(solution)/shard_map/ppermute | solution.py:25
  118.4 12.0 %collective-permute-done.21 = bf16[256,1280]{1,0:T(8,128)(2,1)S(1)} collective-permute-done((bf16[256,1280]{1,0:T(8,128)(2,1)S(1)}, bf16[256,1280]{1,0:T(8,128)(2,1)S(1)}, u32[]{:S(2)}, u32[]{:S(2)}) %collective-permute-start.21) | collective-permute-done | bytes 655392 | tf_op jit(solution)/shard_map/ppermute | solution.py:25
  131.9 2.2 %convolution_convert_fusion.6 = bf16[128,1280]{1,0:T(8,128)(2,1)} fusion(bf16[128,1024]{1,0:T(8,128)(2,1)} %collective-permute-done.2, bf16[256,1280]{1,0:T(8,128)(2,1)S(1)} %collective-permute-done.21, bf16[256,1280]{1,0:T(8,128)(2,1)S(1)} %get-tuple-element.22, bf16[256,1280]{1,0:T(8,128)(2,1)S(1)} %get-tuple-element.24, bf16[256,1280]{1,0:T(8,128)(2,1)S(1)} %copy-done.7), kind=kOutput, calls=%fused_computation.42 | convolution fusion | flops 346193920 | bytes 3211264 | tf_op jit(solution)/shard_map/dot_general | solution.py:112
  134.2 2.2 %convolution_convert_fusion.7 = bf16[128,1280]{1,0:T(8,128)(2,1)} fusion(bf16[128,1024]{1,0:T(8,128)(2,1)} %collective-permute-done, bf16[256,1280]{1,0:T(8,128)(2,1)S(1)} %collective-permute-done.21, bf16[256,1280]{1,0:T(8,128)(2,1)S(1)} %get-tuple-element.22, bf16[256,1280]{1,0:T(8,128)(2,1)S(1)} %get-tuple-element.24, bf16[256,1280]{1,0:T(8,128)(2,1)S(1)} %copy-done.7), kind=kOutput, calls=%fused_computation.43 | convolution fusion | flops 346193920 | bytes 3211264 | tf_op jit(solution)/shard_map/dot_general | solution.py:112
  136.4 2.4 %convolution_convert_fusion.4 = bf16[128,1280]{1,0:T(8,128)(2,1)} fusion(bf16[128,1024]{1,0:T(8,128)(2,1)} %collective-permute-done.2, bf16[256,1280]{1,0:T(8,128)(2,1)S(1)} %collective-permute-done.25, bf16[256,1280]{1,0:T(8,128)(2,1)S(1)} %get-tuple-element.23, bf16[256,1280]{1,0:T(8,128)(2,1)S(1)} %get-tuple-element.25, ...), kind=kOutput, calls=%fused_computation.40 | convolution fusion | flops 346193920 | bytes 3211264 | tf_op jit(solution)/shard_map/dot_general | solution.py:112
  138.8 2.2 %convolution_convert_fusion.5 = bf16[128,1280]{1,0:T(8,128)(2,1)} fusion(bf16[128,1024]{1,0:T(8,128)(2,1)} %collective-permute-done.1, bf16[256,1280]{1,0:T(8,128)(2,1)S(1)} %collective-permute-done.25, bf16[256,1280]{1,0:T(8,128)(2,1)S(1)} %get-tuple-element.23, bf16[256,1280]{1,0:T(8,128)(2,1)S(1)} %get-tuple-element.25, ...), kind=kOutput, calls=%fused_computation.41 | convolution fusion | flops 346193920 | bytes 3211264 | tf_op jit(solution)/shard_map/dot_general | solution.py:112
  141.0 1.8 collective-permute-start.22
  146.3 2.6 %psum.14 = f32[256]{0:T(256)S(1)} all-reduce(f32[256]{0:T(256)S(1)} %add_reduce_fusion), channel_id=1, replica_groups=mesh['dp'=16,'mp'=2] {'mp'}, use_global_device_ids=true, to_apply=%region_2.3 | all-reduce | flops 256 | bytes 2048 | tf_op jit(solution)/shard_map/psum | solution.py:128
  154.4 2.5 %fusion.6 = bf16[128,1280]{1,0:T(8,128)(2,1)} fusion(bf16[128,1024]{1,0:T(8,128)(2,1)} %collective-permute-done.1, bf16[128,1280]{1,0:T(8,128)(2,1)} %collective-permute-done.23, bf16[256,1280]{1,0:T(8,128)(2,1)S(1)} %copy-done.33, bf16[256,1280]{1,0:T(8,128)(2,1)S(1)} %copy-done.20, bf16[256,1280]{1,0:T(8,128)(2,1)S(1)} %copy-done.17, ...), kind=kOutput, calls=%fused_computation.38 | convolution fusion | flops 346521600 | bytes 3538944 | tf_op jit(solution)/shard_map/dot_general | solution.py:112
  161.6 9.7 %collective-permute-start.18 = (f32[5248]{0:T(1024)S(1)}, f32[5248]{0:T(1024)S(1)}, u32[]{:S(2)}, u32[]{:S(2)}) collective-permute-start(f32[5248]{0:T(1024)S(1)} %add_add_fusion.1), channel_id=1, source_target_pairs={{0,24},{2,26},{4,28},{6,30},{8,16},{10,18},{12,20},{14,22},{16,8},... | collective-permute-start | bytes 62984 | tf_op jit(solution)/shard_map/ppermute | solution.py:25
  171.4 2.5 %fusion.7 = bf16[128,1280]{1,0:T(8,128)(2,1)} fusion(bf16[128,1024]{1,0:T(8,128)(2,1)} %collective-permute-done, bf16[128,1280]{1,0:T(8,128)(2,1)} %collective-permute-done.27, bf16[256,1280]{1,0:T(8,128)(2,1)S(1)} %copy-done.30, bf16[256,1280]{1,0:T(8,128)(2,1)S(1)} %copy-done.14, bf16[256,1280]{1,0:T(8,128)(2,1)S(1)} %copy-done.11, ...), kind=kOutput, calls=%fused_computation.39 | convolution fusion | flops 346521600 | bytes 3538944 | tf_op jit(solution)/shard_map/dot_general | solution.py:112
  173.9 9.9 %collective-permute-done.17 = f32[5248]{0:T(1024)S(1)} collective-permute-done((f32[5248]{0:T(1024)S(1)}, f32[5248]{0:T(1024)S(1)}, u32[]{:S(2)}, u32[]{:S(2)}) %collective-permute-start.17) | collective-permute-done | bytes 21024 | tf_op jit(solution)/shard_map/ppermute | solution.py:25
  185.0 3.1 %psum.15 = f32[]{:T(128)} all-reduce(f32[]{:T(128)} %get-tuple-element.14), channel_id=1, replica_groups=mesh['dp'=16,'mp'=2] {'mp'}, use_global_device_ids=true, to_apply=%region_6.7 | all-reduce | flops 1 | bytes 8 | tf_op jit(solution)/shard_map/psum | solution.py:136
  189.5 1.8 multiply_multiply_fusion
  193.8 4.1 %collective-permute-done.28 = bf16[128,1280]{1,0:T(8,128)(2,1)} collective-permute-done((bf16[128,1280]{1,0:T(8,128)(2,1)}, bf16[128,1280]{1,0:T(8,128)(2,1)}, u32[]{:S(2)}, u32[]{:S(2)}) %collective-permute-start.28) | collective-permute-done | bytes 327712 | tf_op jit(solution)/shard_map/ppermute | solution.py:25
  200.6 2.1 %fusion.16 = (bf16[128,2560]{1,0:T(8,128)(2,1)}, bf16[128,2560]{1,0:T(8,128)(2,1)}) fusion(f32[128,2560]{1,0:T(8,128)S(1)} %pad_maximum_fusion.5, bf16[128,2560]{1,0:T(8,128)(2,1)S(1)} %copy-done, bf16[128,2560]{1,0:T(8,128)(2,1)S(1)} %copy-done.2), kind=kLoop, calls=%fused_computation.52 | loop fusion | flops 8192000 | bytes 3932160 | tf_op jit(solution)/shard_map/convert_element_type | solution.py:120
  (165 shorter events, 51.3 us)
Async XLA Ops:
  9.6 77.2 %collective-permute-start.19 = (bf16[256,2560]{1,0:T(8,128)(2,1)}, bf16[256,2560]{1,0:T(8,128)(2,1)}, u32[]{:S(2)}, u32[]{:S(2)}) collective-permute-start(bf16[256,2560]{1,0:T(8,128)(2,1)} %param.9), channel_id=1, source_target_pairs={{0,2},{2,0},{4,6},{6,4},{8,10},{10,8},{12,14},{14,12},{16,18},{18,... | collective-permute-start | bytes 3932168 | tf_op jit(solution)/shard_map/ppermute | solution.py:25
  12.3 20.1 %collective-permute-start.1 = (bf16[128,1024]{1,0:T(8,128)(2,1)}, bf16[128,1024]{1,0:T(8,128)(2,1)}, u32[]{:S(2)}, u32[]{:S(2)}) collective-permute-start(bf16[128,1024]{1,0:T(8,128)(2,1)} %pad_maximum_fusion.9), channel_id=1, source_target_pairs={{0,16},{2,18},{4,20},{6,22},{8,24},{10,26},{12,28},{14,30},{16,0},... | collective-permute-start | bytes 786440 | tf_op jit(solution)/shard_map/ppermute | solution.py:25
  13.5 18.9 %collective-permute-start = (bf16[128,1024]{1,0:T(8,128)(2,1)}, bf16[128,1024]{1,0:T(8,128)(2,1)}, u32[]{:S(2)}, u32[]{:S(2)}) collective-permute-start(bf16[128,1024]{1,0:T(8,128)(2,1)} %pad_maximum_fusion.8), channel_id=1, source_target_pairs={{0,8},{2,10},{4,12},{6,14},{8,0},{10,2},{12,4},{14,6},{16,24},{18,... | collective-permute-start | bytes 786440 | tf_op jit(solution)/shard_map/ppermute | solution.py:25
  14.8 33.5 %collective-permute-start.3 = (bf16[128,2560]{1,0:T(8,128)(2,1)S(1)}, bf16[128,2560]{1,0:T(8,128)(2,1)}, u32[]{:S(2)}, u32[]{:S(2)}) collective-permute-start(bf16[128,2560]{1,0:T(8,128)(2,1)S(1)} %fusion.19), channel_id=1, source_target_pairs={{0,8},{2,10},{4,12},{6,14},{8,0},{10,2},{12,4},{14,6},{16,24},{18,... | collective-permute-start | bytes 1966088 | tf_op jit(solution)/shard_map/ppermute | solution.py:25
  18.5 70.3 %collective-permute-start.20 = (bf16[256,2560]{1,0:T(8,128)(2,1)S(1)}, bf16[256,2560]{1,0:T(8,128)(2,1)S(1)}, u32[]{:S(2)}, u32[]{:S(2)}) collective-permute-start(bf16[256,2560]{1,0:T(8,128)(2,1)S(1)} %copy-done.3), channel_id=1, source_target_pairs={{0,4},{2,6},{4,0},{6,2},{8,12},{10,14},{12,8},{14,10},{16,20},{18,... | collective-permute-start | bytes 3932168 | tf_op jit(solution)/shard_map/ppermute | solution.py:25
  32.4 39.7 %collective-permute-start.4 = (bf16[128,2560]{1,0:T(8,128)(2,1)S(1)}, bf16[128,2560]{1,0:T(8,128)(2,1)S(1)}, u32[]{:S(2)}, u32[]{:S(2)}) collective-permute-start(bf16[128,2560]{1,0:T(8,128)(2,1)S(1)} %fusion.19), channel_id=1, source_target_pairs={{0,16},{2,18},{4,20},{6,22},{8,24},{10,26},{12,28},{14,30},{16,0},... | collective-permute-start | bytes 1966088 | tf_op jit(solution)/shard_map/ppermute | solution.py:25
  49.4 27.8 %collective-permute-start.5 = (bf16[128,1280]{1,0:T(8,128)(2,1)S(1)}, bf16[128,1280]{1,0:T(8,128)(2,1)S(1)}, u32[]{:S(2)}, u32[]{:S(2)}) collective-permute-start(bf16[128,1280]{1,0:T(8,128)(2,1)S(1)} %get-tuple-element.46), channel_id=1, source_target_pairs={{0,16},{2,18},{4,20},{6,22},{8,24},{10,26},{12,28},{14,30},{16,0},... | collective-permute-start | bytes 983048 | tf_op jit(solution)/shard_map/ppermute | solution.py:25
  77.8 17.7 %collective-permute-start.7 = (bf16[256,1280]{1,0:T(8,128)(2,1)S(1)}, bf16[256,1280]{1,0:T(8,128)(2,1)S(1)}, u32[]{:S(2)}, u32[]{:S(2)}) collective-permute-start(bf16[256,1280]{1,0:T(8,128)(2,1)S(1)} %convolution_convert_fusion.2), channel_id=1, source_target_pairs={{0,2},{2,0},{4,6},{6,4},{8,10},{10,8},{12,14},{14,12},{16,18},{18,... | collective-permute-start | bytes 1966088 | tf_op jit(solution)/shard_map/ppermute | solution.py:25
  79.9 61.1 %collective-permute-start.6 = (bf16[256,1280]{1,0:T(8,128)(2,1)S(1)}, bf16[256,1280]{1,0:T(8,128)(2,1)S(1)}, u32[]{:S(2)}, u32[]{:S(2)}) collective-permute-start(bf16[256,1280]{1,0:T(8,128)(2,1)S(1)} %convolution_convert_fusion.3), channel_id=1, source_target_pairs={{0,2},{2,0},{4,6},{6,4},{8,10},{10,8},{12,14},{14,12},{16,18},{18,... | collective-permute-start | bytes 1966088 | tf_op jit(solution)/shard_map/ppermute | solution.py:25
  84.7 59.8 %collective-permute-start.10 = (bf16[256,1280]{1,0:T(8,128)(2,1)S(1)}, bf16[256,1280]{1,0:T(8,128)(2,1)S(1)}, u32[]{:S(2)}, u32[]{:S(2)}) collective-permute-start(bf16[256,1280]{1,0:T(8,128)(2,1)S(1)} %convolution_convert_fusion.1), channel_id=1, source_target_pairs={{0,4},{2,6},{4,0},{6,2},{8,12},{10,14},{12,8},{14,10},{16,20},{18,... | collective-permute-start | bytes 1966088 | tf_op jit(solution)/shard_map/ppermute | solution.py:25
  86.8 29.6 %collective-permute-start.11 = (bf16[256,1280]{1,0:T(8,128)(2,1)S(1)}, bf16[256,1280]{1,0:T(8,128)(2,1)S(1)}, u32[]{:S(2)}, u32[]{:S(2)}) collective-permute-start(bf16[256,1280]{1,0:T(8,128)(2,1)S(1)} %convolution_convert_fusion), channel_id=1, source_target_pairs={{0,4},{2,6},{4,0},{6,2},{8,12},{10,14},{12,8},{14,10},{16,20},{18,... | collective-permute-start | bytes 1966088 | tf_op jit(solution)/shard_map/ppermute | solution.py:25
  88.8 41.6 %collective-permute-start.21 = (bf16[256,1280]{1,0:T(8,128)(2,1)S(1)}, bf16[256,1280]{1,0:T(8,128)(2,1)S(1)}, u32[]{:S(2)}, u32[]{:S(2)}) collective-permute-start(bf16[256,1280]{1,0:T(8,128)(2,1)S(1)} %get-tuple-element.24), channel_id=1, source_target_pairs={{0,4},{2,6},{4,0},{6,2},{8,12},{10,14},{12,8},{14,10},{16,20},{18,... | collective-permute-start | bytes 1966088 | tf_op jit(solution)/shard_map/ppermute | solution.py:25
  95.5 40.9 %collective-permute-start.25 = (bf16[256,1280]{1,0:T(8,128)(2,1)S(1)}, bf16[256,1280]{1,0:T(8,128)(2,1)S(1)}, u32[]{:S(2)}, u32[]{:S(2)}) collective-permute-start(bf16[256,1280]{1,0:T(8,128)(2,1)S(1)} %get-tuple-element.23), channel_id=1, source_target_pairs={{0,2},{2,0},{4,6},{6,4},{8,10},{10,8},{12,14},{14,12},{16,18},{18,... | collective-permute-start | bytes 1966088 | tf_op jit(solution)/shard_map/ppermute | solution.py:25
  116.4 27.1 %collective-permute-start.8 = (bf16[256,1280]{1,0:T(8,128)(2,1)S(1)}, bf16[256,1280]{1,0:T(8,128)(2,1)S(1)}, u32[]{:S(2)}, u32[]{:S(2)}) collective-permute-start(bf16[256,1280]{1,0:T(8,128)(2,1)S(1)} %fusion.2), channel_id=1, source_target_pairs={{0,4},{2,6},{4,0},{6,2},{8,12},{10,14},{12,8},{14,10},{16,20},{18,... | collective-permute-start | bytes 1966088 | tf_op jit(solution)/shard_map/ppermute | solution.py:25
  130.4 14.9 %collective-permute-start.12 = (bf16[256,1280]{1,0:T(8,128)(2,1)S(1)}, bf16[256,1280]{1,0:T(8,128)(2,1)S(1)}, u32[]{:S(2)}, u32[]{:S(2)}) collective-permute-start(bf16[256,1280]{1,0:T(8,128)(2,1)S(1)} %fusion.3), channel_id=1, source_target_pairs={{0,2},{2,0},{4,6},{6,4},{8,10},{10,8},{12,14},{14,12},{16,18},{18,... | collective-permute-start | bytes 1966088 | tf_op jit(solution)/shard_map/ppermute | solution.py:25
  136.4 17.6 %collective-permute-start.23 = (bf16[128,1280]{1,0:T(8,128)(2,1)}, bf16[128,1280]{1,0:T(8,128)(2,1)}, u32[]{:S(2)}, u32[]{:S(2)}) collective-permute-start(bf16[128,1280]{1,0:T(8,128)(2,1)} %convolution_convert_fusion.6), channel_id=1, source_target_pairs={{0,8},{2,10},{4,12},{6,14},{8,0},{10,2},{12,4},{14,6},{16,24},{18,... | collective-permute-start | bytes 983048 | tf_op jit(solution)/shard_map/ppermute | solution.py:25
  141.0 50.4 %collective-permute-start.22 = (bf16[128,1280]{1,0:T(8,128)(2,1)}, bf16[128,1280]{1,0:T(8,128)(2,1)}, u32[]{:S(2)}, u32[]{:S(2)}) collective-permute-start(bf16[128,1280]{1,0:T(8,128)(2,1)} %convolution_convert_fusion.7), channel_id=1, source_target_pairs={{0,8},{2,10},{4,12},{6,14},{8,0},{10,2},{12,4},{14,6},{16,24},{18,... | collective-permute-start | bytes 983048 | tf_op jit(solution)/shard_map/ppermute | solution.py:25
  143.5 18.1 %collective-permute-start.27 = (bf16[128,1280]{1,0:T(8,128)(2,1)}, bf16[128,1280]{1,0:T(8,128)(2,1)}, u32[]{:S(2)}, u32[]{:S(2)}) collective-permute-start(bf16[128,1280]{1,0:T(8,128)(2,1)} %convolution_convert_fusion.4), channel_id=1, source_target_pairs={{0,16},{2,18},{4,20},{6,22},{8,24},{10,26},{12,28},{14,30},{16,0},... | collective-permute-start | bytes 983048 | tf_op jit(solution)/shard_map/ppermute | solution.py:25
  156.9 36.8 %collective-permute-start.26 = (bf16[128,1280]{1,0:T(8,128)(2,1)}, bf16[128,1280]{1,0:T(8,128)(2,1)}, u32[]{:S(2)}, u32[]{:S(2)}) collective-permute-start(bf16[128,1280]{1,0:T(8,128)(2,1)} %convolution_convert_fusion.5), channel_id=1, source_target_pairs={{0,16},{2,18},{4,20},{6,22},{8,24},{10,26},{12,28},{14,30},{16,0},... | collective-permute-start | bytes 983048 | tf_op jit(solution)/shard_map/ppermute | solution.py:25
  158.7 15.2 %collective-permute-start.16 = (f32[5248]{0:T(1024)S(1)}, f32[5248]{0:T(1024)S(1)}, u32[]{:S(2)}, u32[]{:S(2)}) collective-permute-start(f32[5248]{0:T(1024)S(1)} %add_add_fusion.1), channel_id=1, source_target_pairs={{0,8},{2,10},{4,12},{6,14},{8,0},{10,2},{12,4},{14,6},{16,24},{18,... | collective-permute-start | bytes 62984 | tf_op jit(solution)/shard_map/ppermute | solution.py:25
  160.4 23.5 %collective-permute-start.17 = (f32[5248]{0:T(1024)S(1)}, f32[5248]{0:T(1024)S(1)}, u32[]{:S(2)}, u32[]{:S(2)}) collective-permute-start(f32[5248]{0:T(1024)S(1)} %add_add_fusion.1), channel_id=1, source_target_pairs={{0,16},{2,18},{4,20},{6,22},{8,24},{10,26},{12,28},{14,30},{16,0},... | collective-permute-start | bytes 62984 | tf_op jit(solution)/shard_map/ppermute | solution.py:25
  161.6 22.2 %collective-permute-start.18 = (f32[5248]{0:T(1024)S(1)}, f32[5248]{0:T(1024)S(1)}, u32[]{:S(2)}, u32[]{:S(2)}) collective-permute-start(f32[5248]{0:T(1024)S(1)} %add_add_fusion.1), channel_id=1, source_target_pairs={{0,24},{2,26},{4,28},{6,30},{8,16},{10,18},{12,20},{14,22},{16,8},... | collective-permute-start | bytes 62984 | tf_op jit(solution)/shard_map/ppermute | solution.py:25
  173.9 17.4 %collective-permute-start.24 = (bf16[128,1280]{1,0:T(8,128)(2,1)}, bf16[128,1280]{1,0:T(8,128)(2,1)}, u32[]{:S(2)}, u32[]{:S(2)}) collective-permute-start(bf16[128,1280]{1,0:T(8,128)(2,1)} %fusion.6), channel_id=1, source_target_pairs={{0,16},{2,18},{4,20},{6,22},{8,24},{10,26},{12,28},{14,30},{16,0},... | collective-permute-start | bytes 983048 | tf_op jit(solution)/shard_map/ppermute | solution.py:25
  183.9 14.0 %collective-permute-start.28 = (bf16[128,1280]{1,0:T(8,128)(2,1)}, bf16[128,1280]{1,0:T(8,128)(2,1)}, u32[]{:S(2)}, u32[]{:S(2)}) collective-permute-start(bf16[128,1280]{1,0:T(8,128)(2,1)} %fusion.7), channel_id=1, source_target_pairs={{0,8},{2,10},{4,12},{6,14},{8,0},{10,2},{12,4},{14,6},{16,24},{18,... | collective-permute-start | bytes 983048 | tf_op jit(solution)/shard_map/ppermute | solution.py:25
  (40 other events, 657.5 us)

commit v3 on v2

--- a/solution.py
+++ b/solution.py
@@ -3,6 +3,8 @@
 import jax
 import jax.numpy as jnp
 from jax import lax
+from jax.experimental import pallas as pl
+from jax.experimental.pallas import tpu as pltpu
 from jax.sharding import PartitionSpec as P
 
 TRAIN_STEP = 3
@@ -20,16 +22,19 @@
     return (activated, derivative)
 
 
-def flip(value, bits):
-    size = lax.axis_size("dp")
-    return lax.ppermute(value, "dp", [(i, i ^ bits) for i in range(size)])
-
-
-def gather(block, bits):
+def flip(value, bits, axis="dp"):
+    size = lax.axis_size(axis)
+    return lax.ppermute(value, axis, [(i, i ^ bits) for i in range(size)])
+
+
+def first_messages(block, bits):
+    return [flip(block, bit) for bit in bits]
+
+
+def gathered(block, messages, bits):
     half = block.shape[1] // 2
     if len(bits) == 2:
-        first = flip(block, bits[0])
-        second = flip(block, bits[1])
+        first, second = messages
         left = [block[:, :half], first[:, :half], second[:, :half], flip(first[:, :half], bits[1])]
         right = [block[:, half:], first[:, half:], second[:, half:], flip(second[:, half:], bits[0])]
         return left, right
@@ -37,6 +42,46 @@
     for bit in bits:
         blocks = blocks + [flip(b, bit) for b in blocks]
     return [b[:, :half] for b in blocks], [b[:, half:] for b in blocks]
+
+
+def arrange(out_grad, me, core, size, inner, halves):
+    tokens, width = out_grad.shape
+    rows = width // size
+    outer = size // inner
+    part = tokens // halves
+
+    def kernel(place, source, own, *others):
+        for k in range(outer):
+            for j in range(inner):
+                at = pl.multiple_of((place[0] ^ (k * inner + j)) * rows, rows)
+                columns = pl.ds(j * rows, rows)
+                if k == 0:
+                    own[:, columns] = source[:, pl.ds(at, rows)]
+                else:
+                    start = pl.multiple_of(place[1] * part, part)
+                    others[k - 1][:, columns] = source[pl.ds(start, part), pl.ds(at, rows)]
+
+    result = pl.pallas_call(
+        kernel,
+        out_shape=[jax.ShapeDtypeStruct((tokens, inner * rows), out_grad.dtype)]
+        + [jax.ShapeDtypeStruct((part, inner * rows), out_grad.dtype)] * (outer - 1),
+        in_specs=[pl.BlockSpec(memory_space=pltpu.SMEM), pl.BlockSpec(memory_space=pltpu.VMEM)],
+        out_specs=[pl.BlockSpec(memory_space=pltpu.VMEM)] * outer,
+        compiler_params=pltpu.CompilerParams(vmem_limit_bytes=16 << 20),
+        cost_estimate=pl.CostEstimate(flops=0, bytes_accessed=4 * tokens * width, transcendentals=0),
+    )(jnp.stack([me, core]).astype(jnp.int32), out_grad)
+    return result[0], result[1:]
+
+
+def arrange_plain(out_grad, me, size, inner):
+    tokens, width = out_grad.shape
+    by_block = out_grad.reshape(tokens, size, width // size).transpose(1, 0, 2)
+
+    def features_of(k):
+        picks = [lax.dynamic_index_in_dim(by_block, me ^ (k * inner + j), 0, keepdims=False) for j in range(inner)]
+        return jnp.concatenate(picks, axis=1)
+
+    return features_of(0), [features_of(k) for k in range(1, size // inner)]
 
 
 def scatter(part, bits):
@@ -86,18 +131,30 @@
     activated, _ = gelu_parts(gate_pre.astype(jnp.float32))
     hidden = (activated * up_pre.astype(jnp.float32)).astype(jnp.bfloat16)
 
-    by_block = out_grad.reshape(tokens, size, rows).transpose(1, 0, 2)
-
-    def features_of(k):
-        picks = [lax.dynamic_index_in_dim(by_block, me ^ (k * inner + j), 0, keepdims=False) for j in range(inner)]
-        return jnp.concatenate(picks, axis=1)
-
-    shares = [features_of(0)] + [flip(features_of(k), k * inner) for k in range(1, outer)]
+    core = lax.axis_index("mp")
+    split = lax.axis_size("mp") == 2 and tokens % 32 == 0 and rows % 128 == 0
+    weight_messages = first_messages(down_weight, inner_bits)
+    hidden_messages = first_messages(hidden, outer_bits)
+    if rows % 128 == 0:
+        own_share, others = arrange(out_grad, me, core, size, inner, 2 if split else 1)
+    else:
+        own_share, others = arrange_plain(out_grad, me, size, inner)
+    arrived = [flip(value, (k + 1) * inner) for k, value in enumerate(others)]
+    weight_messages, hidden_messages, arrived = lax.optimization_barrier((weight_messages, hidden_messages, arrived))
+    weight_sides = gathered(down_weight, weight_messages, inner_bits)
+    hidden_sides = gathered(hidden, hidden_messages, outer_bits)
+    if split:
+        swapped = [flip(value, 1, "mp") for value in arrived]
+        shares = [own_share] + [
+            jnp.concatenate([jnp.where(core == 0, a, b), jnp.where(core == 0, b, a)], axis=0)
+            for a, b in zip(arrived, swapped)
+        ]
+    else:
+        shares = [own_share] + arrived
     share = jnp.concatenate(shares, axis=0)
-
-    hidden_sides = gather(hidden, outer_bits)
+    share, weight_sides, hidden_sides = lax.optimization_barrier((share, weight_sides, hidden_sides))
+    shares = [share[k * tokens : (k + 1) * tokens] for k in range(outer)]
     hidden_sides = [jnp.concatenate(side, axis=0) for side in hidden_sides]
-    weight_sides = gather(down_weight, inner_bits)
     weight_sides = [jnp.concatenate(side, axis=0) for side in weight_sides]
 
     def grad_part(j, side):

time: 205 us -> 177 us (0.86)
  matrix products: 21.6 us -> 9.21 us
  waiting for transfers between devices: 107 us -> 96.9 us
  local copies, waits for them, and re-layouts: 11.7 us -> 8.1 us
    dot_general x8, matrix products: 17.3 us -> 4.95 us  [hidden_grad_part(): jnp.dot(shares[k], weight_sides[side], preferred_element_type=jnp.float32)]
    ppermute x29 -> x32, waiting for transfers between devices: 107 us -> 96.9 us  [flip(): return lax.ppermute(value, axis, [(i, i ^ bits) for i in range(size)])]
    another operation x17 -> x0, local copies, waits for them, and re-layouts: 3.5 us -> none
    concatenate x3 -> x0, other arithmetic: 2.18 us -> none  [features_of(): return jnp.concatenate(picks, axis=1)]
    ppermute x29 -> x32, starting transfers between devices: 43.5 us -> 44.3 us  [flip(): return lax.ppermute(value, axis, [(i, i ^ bits) for i in range(size)])]
  transfers between devices with their start and end apart: 29 -> 32, of which waited for: 12 -> 12; matrix products, arithmetic and copies ran while one was open for 17% -> 8% of each run, Pallas kernels for 0% -> 0%
where the time goes in v3:
time: 177 us
  waiting for transfers between devices  96.9 us (55%)
  starting transfers between devices  44.3 us (25%)
  matrix products  9.21 us (5%)
  other arithmetic  8.18 us (5%)
  local copies, waits for them, and re-layouts  8.1 us (5%)
  blocking collectives  5.71 us (3%)
  between operations  3.59 us (2%)
    ppermute x32, waiting for transfers between devices, flip(): return lax.ppermute(value, axis, [(i, i ^ bits) for i in range(size)])  96.9 us
    ppermute x32, starting transfers between devices, flip(): return lax.ppermute(value, axis, [(i, i ^ bits) for i in range(size)])  44.3 us
    dot_general x8, matrix products, hidden_grad_part(): jnp.dot(shares[k], weight_sides[side], preferred_element_type=jnp.float32)  4.95 us
    dot_general x8, matrix products, grad_part(): lax.dot_general(share[:, j * rows:(j + 1) * rows], hidden_sides[side], ((...  4.26 us
  transfers between devices with their start and end apart: 32, of which 12 were waited for; matrix products, arithmetic and copies ran while one was open for 8% of the time, Pallas kernels for 0%

profile of v3, /device:TPU:0, one launch (start us, length us, event | category | flops | bytes accessed | tf_op | source)
XLA Modules:
  0.0 176.6 jit_solution(12158136294956598563)
XLA Ops:
  0.6 3.0 %collective-permute-start = (bf16[256,2560]{1,0:T(8,128)(2,1)}, bf16[256,2560]{1,0:T(8,128)(2,1)}, u32[]{:S(2)}, u32[]{:S(2)}) collective-permute-start(bf16[256,2560]{1,0:T(8,128)(2,1)} %param.9), channel_id=1, source_target_pairs={{0,2},{2,0},{4,6},{6,4},{8,10},{10,8},{12,14},{14,12},{16,18},{18,... | collective-permute-start | bytes 3932168 | tf_op jit(solution)/shard_map/ppermute | solution.py:27
  7.1 1.6 collective-permute-start.4
  8.7 1.6 fusion.19
  10.9 2.6 %collective-permute-start.3 = (bf16[128,2560]{1,0:T(8,128)(2,1)S(1)}, bf16[128,2560]{1,0:T(8,128)(2,1)}, u32[]{:S(2)}, u32[]{:S(2)}) collective-permute-start(bf16[128,2560]{1,0:T(8,128)(2,1)S(1)} %fusion.19), channel_id=1, source_target_pairs={{0,16},{2,18},{4,20},{6,22},{8,24},{10,26},{12,28},{14,30},{16,0},... | collective-permute-start | bytes 1966088 | tf_op jit(solution)/shard_map/ppermute | solution.py:27
  15.1 32.0 %collective-permute-done.5 = bf16[64,1024]{1,0:T(8,128)(2,1)S(1)} collective-permute-done((bf16[64,1024]{1,0:T(8,128)(2,1)S(1)}, bf16[64,1024]{1,0:T(8,128)(2,1)S(1)}, u32[]{:S(2)}, u32[]{:S(2)}) %collective-permute-start.5) | collective-permute-done | bytes 131104 | tf_op jit(solution)/shard_map/ppermute | solution.py:27
  47.0 4.8 %collective-permute-start.6 = (bf16[64,1024]{1,0:T(8,128)(2,1)S(1)}, bf16[64,1024]{1,0:T(8,128)(2,1)S(1)}, u32[]{:S(2)}, u32[]{:S(2)}) collective-permute-start(bf16[64,1024]{1,0:T(8,128)(2,1)S(1)} %get-tuple-element.40), channel_id=1, source_target_pairs={{0,24},{2,26},{4,28},{6,30},{8,16},{10,18},{12,20},{14,22},{16,8},... | collective-permute-start | bytes 393224 | tf_op jit(solution)/shard_map/ppermute | solution.py:27
  51.9 2.9 %collective-permute-done.6 = bf16[64,1024]{1,0:T(8,128)(2,1)S(1)} collective-permute-done((bf16[64,1024]{1,0:T(8,128)(2,1)S(1)}, bf16[64,1024]{1,0:T(8,128)(2,1)S(1)}, u32[]{:S(2)}, u32[]{:S(2)}) %collective-permute-start.6) | collective-permute-done | bytes 131104 | tf_op jit(solution)/shard_map/ppermute | solution.py:27
  61.9 4.4 %collective-permute-start.13 = (bf16[128,1280]{1,0:T(8,128)(2,1)S(1)}, bf16[128,1280]{1,0:T(8,128)(2,1)S(1)}, u32[]{:S(2)}, u32[]{:S(2)}) collective-permute-start(bf16[128,1280]{1,0:T(8,128)(2,1)S(1)} %get-tuple-element.55), channel_id=1, source_target_pairs={{0,8},{2,10},{4,12},{6,14},{8,0},{10,2},{12,4},{14,6},{16,24},{18,... | collective-permute-start | bytes 983048 | tf_op jit(solution)/shard_map/ppermute | solution.py:27
  66.4 12.9 %collective-permute-done.12 = bf16[128,1280]{1,0:T(8,128)(2,1)S(1)} collective-permute-done((bf16[128,1280]{1,0:T(8,128)(2,1)S(1)}, bf16[128,1280]{1,0:T(8,128)(2,1)S(1)}, u32[]{:S(2)}, u32[]{:S(2)}) %collective-permute-start.12) | collective-permute-done | bytes 327712 | tf_op jit(solution)/shard_map/ppermute | solution.py:27
  83.3 3.3 %collective-permute-start.30 = (bf16[128,1280]{1,0:T(8,128)(2,1)S(1)}, bf16[128,1280]{1,0:T(8,128)(2,1)S(1)}, u32[]{:S(2)}, u32[]{:S(2)}) collective-permute-start(bf16[128,1280]{1,0:T(8,128)(2,1)S(1)} %convolution_convert_fusion.4), channel_id=1, source_target_pairs={{0,16},{2,18},{4,20},{6,22},{8,24},{10,26},{12,28},{14,30},{16,0},... | collective-permute-start | bytes 983048 | tf_op jit(solution)/shard_map/ppermute | solution.py:27
  91.0 14.6 %collective-permute-done.27 = bf16[128,1280]{1,0:T(8,128)(2,1)S(1)} collective-permute-done((bf16[128,1280]{1,0:T(8,128)(2,1)S(1)}, bf16[128,1280]{1,0:T(8,128)(2,1)S(1)}, u32[]{:S(2)}, u32[]{:S(2)}) %collective-permute-start.27) | collective-permute-done | bytes 327712 | tf_op jit(solution)/shard_map/ppermute | solution.py:27
  107.7 1.5 collective-permute-start.14
  110.4 12.7 %collective-permute-done.18 = bf16[256,1280]{1,0:T(8,128)(2,1)S(1)} collective-permute-done((bf16[256,1280]{1,0:T(8,128)(2,1)S(1)}, bf16[256,1280]{1,0:T(8,128)(2,1)S(1)}, u32[]{:S(2)}, u32[]{:S(2)}) %collective-permute-start.18) | collective-permute-done | bytes 655392 | tf_op jit(solution)/shard_map/ppermute | solution.py:27
  125.3 3.2 %collective-permute-done.28 = bf16[128,1280]{1,0:T(8,128)(2,1)S(1)} collective-permute-done((bf16[128,1280]{1,0:T(8,128)(2,1)S(1)}, bf16[128,1280]{1,0:T(8,128)(2,1)S(1)}, u32[]{:S(2)}, u32[]{:S(2)}) %collective-permute-start.28) | collective-permute-done | bytes 327712 | tf_op jit(solution)/shard_map/ppermute | solution.py:27
  128.4 1.6 collective-permute-start.16
  130.5 1.6 collective-permute-start.19
  133.7 14.1 %collective-permute-done.16 = bf16[256,1280]{1,0:T(8,128)(2,1)S(1)} collective-permute-done((bf16[256,1280]{1,0:T(8,128)(2,1)S(1)}, bf16[256,1280]{1,0:T(8,128)(2,1)S(1)}, u32[]{:S(2)}, u32[]{:S(2)}) %collective-permute-start.16) | collective-permute-done | bytes 655392 | tf_op jit(solution)/shard_map/ppermute | solution.py:27
  149.3 2.6 %psum.14 = f32[256]{0:T(256)S(1)} all-reduce(f32[256]{0:T(256)S(1)} %add_reduce_fusion), channel_id=1, replica_groups=mesh['dp'=16,'mp'=2] {'mp'}, use_global_device_ids=true, to_apply=%region_2.3 | all-reduce | flops 256 | bytes 2048 | tf_op jit(solution)/shard_map/psum | solution.py:185
  153.8 1.6 collective-permute-start.20
  159.2 2.4 %collective-permute-done.22 = f32[5248]{0:T(1024)S(1)} collective-permute-done((f32[5248]{0:T(1024)S(1)}, f32[5248]{0:T(1024)S(1)}, u32[]{:S(2)}, u32[]{:S(2)}) %collective-permute-start.22) | collective-permute-done | bytes 21024 | tf_op jit(solution)/shard_map/ppermute | solution.py:27
  161.8 4.3 %collective-permute-start.25 = (f32[5248]{0:T(1024)S(1)}, f32[5248]{0:T(1024)S(1)}, u32[]{:S(2)}, u32[]{:S(2)}) collective-permute-start(f32[5248]{0:T(1024)S(1)} %add_add_fusion.1), channel_id=1, source_target_pairs={{0,24},{2,26},{4,28},{6,30},{8,16},{10,18},{12,20},{14,22},{16,8},... | collective-permute-start | bytes 62984 | tf_op jit(solution)/shard_map/ppermute | solution.py:27
  166.1 2.1 %fusion.16 = (bf16[128,2560]{1,0:T(8,128)(2,1)}, bf16[128,2560]{1,0:T(8,128)(2,1)}) fusion(f32[128,2560]{1,0:T(8,128)S(1)} %pad_maximum_fusion.1, bf16[128,2560]{1,0:T(8,128)(2,1)S(1)} %copy-done.3, bf16[128,2560]{1,0:T(8,128)(2,1)S(1)} %copy-done.4), kind=kLoop, calls=%fused_computation.50 | loop fusion | flops 8192000 | bytes 3932160 | tf_op jit(solution)/shard_map/convert_element_type | solution.py:177
  169.3 3.1 %psum.15 = f32[]{:T(128)} all-reduce(f32[]{:T(128)} %get-tuple-element.70), channel_id=1, replica_groups=mesh['dp'=16,'mp'=2] {'mp'}, use_global_device_ids=true, to_apply=%region_6.7 | all-reduce | flops 1 | bytes 8 | tf_op jit(solution)/shard_map/psum | solution.py:193
  173.7 1.8 %multiply_multiply_fusion = f32[256,2560]{1,0:T(8,128)} fusion(f32[256,1280]{1,0:T(8,128)S(1)} %fusion, f32[256,1280]{1,0:T(8,128)S(1)} %fusion.1, f32[2560]{0:T(1024)S(1)} %sqrt.11, f32[256]{0:T(256)S(1)} %divide_multiply_fusion), kind=kLoop, calls=%fused_computation.14 | loop fusion | flops 1966080 | bytes 5254144 | tf_op jit(solution)/shard_map/mul | solution.py:197
  (124 shorter events, 36.9 us)
Async XLA Ops:
  0.6 54.2 %collective-permute-start = (bf16[256,2560]{1,0:T(8,128)(2,1)}, bf16[256,2560]{1,0:T(8,128)(2,1)}, u32[]{:S(2)}, u32[]{:S(2)}) collective-permute-start(bf16[256,2560]{1,0:T(8,128)(2,1)} %param.9), channel_id=1, source_target_pairs={{0,2},{2,0},{4,6},{6,4},{8,10},{10,8},{12,14},{14,12},{16,18},{18,... | collective-permute-start | bytes 3932168 | tf_op jit(solution)/shard_map/ppermute | solution.py:27
  3.6 51.2 %collective-permute-start.1 = (bf16[256,2560]{1,0:T(8,128)(2,1)}, bf16[256,2560]{1,0:T(8,128)(2,1)}, u32[]{:S(2)}, u32[]{:S(2)}) collective-permute-start(bf16[256,2560]{1,0:T(8,128)(2,1)} %param.9), channel_id=1, source_target_pairs={{0,4},{2,6},{4,0},{6,2},{8,12},{10,14},{12,8},{14,10},{16,20},{18,... | collective-permute-start | bytes 3932168 | tf_op jit(solution)/shard_map/ppermute | solution.py:27
  10.4 44.5 %collective-permute-start.2 = (bf16[128,2560]{1,0:T(8,128)(2,1)S(1)}, bf16[128,2560]{1,0:T(8,128)(2,1)}, u32[]{:S(2)}, u32[]{:S(2)}) collective-permute-start(bf16[128,2560]{1,0:T(8,128)(2,1)S(1)} %fusion.19), channel_id=1, source_target_pairs={{0,8},{2,10},{4,12},{6,14},{8,0},{10,2},{12,4},{14,6},{16,24},{18,... | collective-permute-start | bytes 1966088 | tf_op jit(solution)/shard_map/ppermute | solution.py:27
  10.9 44.0 %collective-permute-start.3 = (bf16[128,2560]{1,0:T(8,128)(2,1)S(1)}, bf16[128,2560]{1,0:T(8,128)(2,1)}, u32[]{:S(2)}, u32[]{:S(2)}) collective-permute-start(bf16[128,2560]{1,0:T(8,128)(2,1)S(1)} %fusion.19), channel_id=1, source_target_pairs={{0,16},{2,18},{4,20},{6,22},{8,24},{10,26},{12,28},{14,30},{16,0},... | collective-permute-start | bytes 1966088 | tf_op jit(solution)/shard_map/ppermute | solution.py:27
  13.5 33.6 %collective-permute-start.5 = (bf16[64,1024]{1,0:T(8,128)(2,1)S(1)}, bf16[64,1024]{1,0:T(8,128)(2,1)S(1)}, u32[]{:S(2)}, u32[]{:S(2)}) collective-permute-start(bf16[64,1024]{1,0:T(8,128)(2,1)S(1)} %get-tuple-element.39), channel_id=1, source_target_pairs={{0,16},{2,18},{4,20},{6,22},{8,24},{10,26},{12,28},{14,30},{16,0},... | collective-permute-start | bytes 393224 | tf_op jit(solution)/shard_map/ppermute | solution.py:27
  47.0 7.8 %collective-permute-start.6 = (bf16[64,1024]{1,0:T(8,128)(2,1)S(1)}, bf16[64,1024]{1,0:T(8,128)(2,1)S(1)}, u32[]{:S(2)}, u32[]{:S(2)}) collective-permute-start(bf16[64,1024]{1,0:T(8,128)(2,1)S(1)} %get-tuple-element.40), channel_id=1, source_target_pairs={{0,24},{2,26},{4,28},{6,30},{8,16},{10,18},{12,20},{14,22},{16,8},... | collective-permute-start | bytes 393224 | tf_op jit(solution)/shard_map/ppermute | solution.py:27
  54.9 6.9 %collective-permute-start.8 = (bf16[64,1024]{1,0:T(8,128)(2,1)S(1)}, bf16[64,1024]{1,0:T(8,128)(2,1)S(1)}, u32[]{:S(2)}, u32[]{:S(2)}) collective-permute-start(bf16[64,1024]{1,0:T(8,128)(2,1)S(1)} %collective-permute-done.5), channel_id=1, source_target_pairs={{0,1},{1,0},{2,3},{3,2},{4,5},{5,4},{6,7},{7,6},{8,9},{9,8},{10,11... | collective-permute-start | bytes 393224 | tf_op jit(solution)/shard_map/ppermute | solution.py:27
  55.4 10.9 %collective-permute-start.9 = (bf16[64,1024]{1,0:T(8,128)(2,1)S(1)}, bf16[64,1024]{1,0:T(8,128)(2,1)S(1)}, u32[]{:S(2)}, u32[]{:S(2)}) collective-permute-start(bf16[64,1024]{1,0:T(8,128)(2,1)S(1)} %collective-permute-done.6), channel_id=1, source_target_pairs={{0,1},{1,0},{2,3},{3,2},{4,5},{5,4},{6,7},{7,6},{8,9},{9,8},{10,11... | collective-permute-start | bytes 393224 | tf_op jit(solution)/shard_map/ppermute | solution.py:27
  56.9 22.6 %collective-permute-start.10 = (bf16[256,1280]{1,0:T(8,128)(2,1)S(1)}, bf16[256,1280]{1,0:T(8,128)(2,1)S(1)}, u32[]{:S(2)}, u32[]{:S(2)}) collective-permute-start(bf16[256,1280]{1,0:T(8,128)(2,1)S(1)} %get-tuple-element.58), channel_id=1, source_target_pairs={{0,4},{2,6},{4,0},{6,2},{8,12},{10,14},{12,8},{14,10},{16,20},{18,... | collective-permute-start | bytes 1966088 | tf_op jit(solution)/shard_map/ppermute | solution.py:27
  58.8 20.7 %collective-permute-start.11 = (bf16[256,1280]{1,0:T(8,128)(2,1)S(1)}, bf16[256,1280]{1,0:T(8,128)(2,1)S(1)}, u32[]{:S(2)}, u32[]{:S(2)}) collective-permute-start(bf16[256,1280]{1,0:T(8,128)(2,1)S(1)} %get-tuple-element.63), channel_id=1, source_target_pairs={{0,2},{2,0},{4,6},{6,4},{8,10},{10,8},{12,14},{14,12},{16,18},{18,... | collective-permute-start | bytes 1966088 | tf_op jit(solution)/shard_map/ppermute | solution.py:27
  61.7 17.6 %collective-permute-start.12 = (bf16[128,1280]{1,0:T(8,128)(2,1)S(1)}, bf16[128,1280]{1,0:T(8,128)(2,1)S(1)}, u32[]{:S(2)}, u32[]{:S(2)}) collective-permute-start(bf16[128,1280]{1,0:T(8,128)(2,1)S(1)} %get-tuple-element.50), channel_id=1, source_target_pairs={{0,16},{2,18},{4,20},{6,22},{8,24},{10,26},{12,28},{14,30},{16,0},... | collective-permute-start | bytes 983048 | tf_op jit(solution)/shard_map/ppermute | solution.py:27
  61.9 17.7 %collective-permute-start.13 = (bf16[128,1280]{1,0:T(8,128)(2,1)S(1)}, bf16[128,1280]{1,0:T(8,128)(2,1)S(1)}, u32[]{:S(2)}, u32[]{:S(2)}) collective-permute-start(bf16[128,1280]{1,0:T(8,128)(2,1)S(1)} %get-tuple-element.55), channel_id=1, source_target_pairs={{0,8},{2,10},{4,12},{6,14},{8,0},{10,2},{12,4},{14,6},{16,24},{18,... | collective-permute-start | bytes 983048 | tf_op jit(solution)/shard_map/ppermute | solution.py:27
  83.2 22.4 %collective-permute-start.27 = (bf16[128,1280]{1,0:T(8,128)(2,1)S(1)}, bf16[128,1280]{1,0:T(8,128)(2,1)S(1)}, u32[]{:S(2)}, u32[]{:S(2)}) collective-permute-start(bf16[128,1280]{1,0:T(8,128)(2,1)S(1)} %convolution_convert_fusion.6), channel_id=1, source_target_pairs={{0,8},{2,10},{4,12},{6,14},{8,0},{10,2},{12,4},{14,6},{16,24},{18,... | collective-permute-start | bytes 983048 | tf_op jit(solution)/shard_map/ppermute | solution.py:27
  83.3 24.4 %collective-permute-start.30 = (bf16[128,1280]{1,0:T(8,128)(2,1)S(1)}, bf16[128,1280]{1,0:T(8,128)(2,1)S(1)}, u32[]{:S(2)}, u32[]{:S(2)}) collective-permute-start(bf16[128,1280]{1,0:T(8,128)(2,1)S(1)} %convolution_convert_fusion.4), channel_id=1, source_target_pairs={{0,16},{2,18},{4,20},{6,22},{8,24},{10,26},{12,28},{14,30},{16,0},... | collective-permute-start | bytes 983048 | tf_op jit(solution)/shard_map/ppermute | solution.py:27
  86.6 23.2 %collective-permute-start.15 = (bf16[256,1280]{1,0:T(8,128)(2,1)S(1)}, bf16[256,1280]{1,0:T(8,128)(2,1)S(1)}, u32[]{:S(2)}, u32[]{:S(2)}) collective-permute-start(bf16[256,1280]{1,0:T(8,128)(2,1)S(1)} %convolution_convert_fusion.2), channel_id=1, source_target_pairs={{0,2},{2,0},{4,6},{6,4},{8,10},{10,8},{12,14},{14,12},{16,18},{18,... | collective-permute-start | bytes 1966088 | tf_op jit(solution)/shard_map/ppermute | solution.py:27
  89.3 35.9 %collective-permute-start.26 = (bf16[128,1280]{1,0:T(8,128)(2,1)S(1)}, bf16[128,1280]{1,0:T(8,128)(2,1)S(1)}, u32[]{:S(2)}, u32[]{:S(2)}) collective-permute-start(bf16[128,1280]{1,0:T(8,128)(2,1)S(1)} %convolution_convert_fusion.7), channel_id=1, source_target_pairs={{0,8},{2,10},{4,12},{6,14},{8,0},{10,2},{12,4},{14,6},{16,24},{18,... | collective-permute-start | bytes 983048 | tf_op jit(solution)/shard_map/ppermute | solution.py:27
  89.5 41.0 %collective-permute-start.29 = (bf16[128,1280]{1,0:T(8,128)(2,1)S(1)}, bf16[128,1280]{1,0:T(8,128)(2,1)S(1)}, u32[]{:S(2)}, u32[]{:S(2)}) collective-permute-start(bf16[128,1280]{1,0:T(8,128)(2,1)S(1)} %convolution_convert_fusion.5), channel_id=1, source_target_pairs={{0,16},{2,18},{4,20},{6,22},{8,24},{10,26},{12,28},{14,30},{16,0},... | collective-permute-start | bytes 983048 | tf_op jit(solution)/shard_map/ppermute | solution.py:27
  105.6 17.5 %collective-permute-start.18 = (bf16[256,1280]{1,0:T(8,128)(2,1)S(1)}, bf16[256,1280]{1,0:T(8,128)(2,1)S(1)}, u32[]{:S(2)}, u32[]{:S(2)}) collective-permute-start(bf16[256,1280]{1,0:T(8,128)(2,1)S(1)} %convolution_convert_fusion), channel_id=1, source_target_pairs={{0,4},{2,6},{4,0},{6,2},{8,12},{10,14},{12,8},{14,10},{16,20},{18,... | collective-permute-start | bytes 1966088 | tf_op jit(solution)/shard_map/ppermute | solution.py:27
  107.7 26.0 %collective-permute-start.14 = (bf16[256,1280]{1,0:T(8,128)(2,1)S(1)}, bf16[256,1280]{1,0:T(8,128)(2,1)S(1)}, u32[]{:S(2)}, u32[]{:S(2)}) collective-permute-start(bf16[256,1280]{1,0:T(8,128)(2,1)S(1)} %convolution_convert_fusion.3), channel_id=1, source_target_pairs={{0,2},{2,0},{4,6},{6,4},{8,10},{10,8},{12,14},{14,12},{16,18},{18,... | collective-permute-start | bytes 1966088 | tf_op jit(solution)/shard_map/ppermute | solution.py:27
  109.7 18.7 %collective-permute-start.28 = (bf16[128,1280]{1,0:T(8,128)(2,1)S(1)}, bf16[128,1280]{1,0:T(8,128)(2,1)S(1)}, u32[]{:S(2)}, u32[]{:S(2)}) collective-permute-start(bf16[128,1280]{1,0:T(8,128)(2,1)S(1)} %fusion.6), channel_id=1, source_target_pairs={{0,16},{2,18},{4,20},{6,22},{8,24},{10,26},{12,28},{14,30},{16,0},... | collective-permute-start | bytes 983048 | tf_op jit(solution)/shard_map/ppermute | solution.py:27
  123.1 25.2 %collective-permute-start.17 = (bf16[256,1280]{1,0:T(8,128)(2,1)S(1)}, bf16[256,1280]{1,0:T(8,128)(2,1)S(1)}, u32[]{:S(2)}, u32[]{:S(2)}) collective-permute-start(bf16[256,1280]{1,0:T(8,128)(2,1)S(1)} %convolution_convert_fusion.1), channel_id=1, source_target_pairs={{0,4},{2,6},{4,0},{6,2},{8,12},{10,14},{12,8},{14,10},{16,20},{18,... | collective-permute-start | bytes 1966088 | tf_op jit(solution)/shard_map/ppermute | solution.py:27
  125.2 7.1 %collective-permute-start.31 = (bf16[128,1280]{1,0:T(8,128)(2,1)S(1)}, bf16[128,1280]{1,0:T(8,128)(2,1)S(1)}, u32[]{:S(2)}, u32[]{:S(2)}) collective-permute-start(bf16[128,1280]{1,0:T(8,128)(2,1)S(1)} %fusion.7), channel_id=1, source_target_pairs={{0,8},{2,10},{4,12},{6,14},{8,0},{10,2},{12,4},{14,6},{16,24},{18,... | collective-permute-start | bytes 983048 | tf_op jit(solution)/shard_map/ppermute | solution.py:27
  128.4 19.3 %collective-permute-start.16 = (bf16[256,1280]{1,0:T(8,128)(2,1)S(1)}, bf16[256,1280]{1,0:T(8,128)(2,1)S(1)}, u32[]{:S(2)}, u32[]{:S(2)}) collective-permute-start(bf16[256,1280]{1,0:T(8,128)(2,1)S(1)} %fusion.2), channel_id=1, source_target_pairs={{0,4},{2,6},{4,0},{6,2},{8,12},{10,14},{12,8},{14,10},{16,20},{18,... | collective-permute-start | bytes 1966088 | tf_op jit(solution)/shard_map/ppermute | solution.py:27
  130.5 17.8 %collective-permute-start.19 = (bf16[256,1280]{1,0:T(8,128)(2,1)S(1)}, bf16[256,1280]{1,0:T(8,128)(2,1)S(1)}, u32[]{:S(2)}, u32[]{:S(2)}) collective-permute-start(bf16[256,1280]{1,0:T(8,128)(2,1)S(1)} %fusion.3), channel_id=1, source_target_pairs={{0,2},{2,0},{4,6},{6,4},{8,10},{10,8},{12,14},{14,12},{16,18},{18,... | collective-permute-start | bytes 1966088 | tf_op jit(solution)/shard_map/ppermute | solution.py:27
  (18 other events, 124.1 us)

commit v4 on v2

v4 whole, which is shorter than its diff:
```python
import math

import jax
import jax.numpy as jnp
from jax import lax
from jax.experimental import pallas as pl
from jax.experimental.pallas import tpu as pltpu
from jax.sharding import PartitionSpec as P

TRAIN_STEP = 3
INNER_BITS = 2
PIECES = ((0, 0), (0, 1), (1, 0), (3, 0), (2, 1), (3, 1), (2, 0), (1, 1))


def gelu_parts(values):
    factor = math.sqrt(2.0 / math.pi)
    inner = factor * (values + 0.044715 * values * values * values)
    tangent = jnp.tanh(inner)
    activated = 0.5 * values * (1.0 + tangent)
    derivative = 0.5 * (1.0 + tangent) + 0.5 * values * (1.0 - tangent * tangent) * factor * (
        1.0 + 3.0 * 0.044715 * values * values
    )
    return (activated, derivative)


def flip(value, bits, axis="dp"):
    size = lax.axis_size(axis)
    return lax.ppermute(value, axis, [(i, i ^ bits) for i in range(size)])


def group_sum(value, bits):
    for at in range(0, len(bits), 2):
        pair = bits[at : at + 2]
        if len(pair) == 2:
            first, second = flip(value, pair[0]), flip(value, pair[1])
            value = (value + first) + (second + flip(value, pair[0] | pair[1]))
        else:
            value = value + flip(value, pair[0])
    return value


def general_products(out_grad, gate_pre, up_pre, down_weight, inner_bits, outer_bits):
    size = lax.axis_size("dp")
    me = lax.axis_index("dp")
    tokens, rows = out_grad.shape[0], down_weight.shape[0]
    inner = 2 ** len(inner_bits)
    activated, _ = gelu_parts(gate_pre.astype(jnp.float32))
    hidden = (activated * up_pre.astype(jnp.float32)).astype(jnp.bfloat16)
    by_block = out_grad.reshape(tokens, size, rows).transpose(1, 0, 2)

    def features_of(k):
        picks = [lax.dynamic_index_in_dim(by_block, me ^ (k * inner + j), 0, keepdims=False) for j in range(inner)]
        return jnp.concatenate(picks, axis=1)

    def gather(block, bits):
        blocks = [block]
        for bit in bits:
            blocks = blocks + [flip(b, bit) for b in blocks]
        return jnp.concatenate(blocks, axis=0)

    def scatter(values, bits):
        for level in reversed(range(len(bits))):
            count = 2**level
            values = [
                values[j] + flip(values[j + count].astype(jnp.bfloat16), bits[level]).astype(jnp.float32)
                for j in range(count)
            ]
        return values[0]

    shares = [features_of(0)] + [flip(features_of(k), k * inner) for k in range(1, size // inner)]
    share = jnp.concatenate(shares, axis=0)
    hidden_all = gather(hidden, outer_bits)
    weight_all = gather(down_weight, inner_bits)
    product = scatter(
        [
            lax.dot_general(
                share[:, j * rows : (j + 1) * rows],
                hidden_all,
                (((0,), (0,)), ((), ())),
                preferred_element_type=jnp.float32,
            )
            for j in range(inner)
        ],
        inner_bits,
    )
    hidden_grad = scatter(
        [jnp.dot(x, weight_all, preferred_element_type=jnp.float32) for x in shares],
        outer_bits,
    )
    return product, hidden_grad


def first_stage(out_grad, gate_pre, up_pre, place, rows):
    tokens, units = gate_pre.shape
    quarter = rows // 2
    share_width = 4 * rows
    step = 32

    def kernel(place, source, gate, up, own, hidden, message1, message2, message3):
        me, core = place[0], place[1]

        def column(k, block, half):
            at = (me ^ (4 * k + block)) * rows + half * quarter
            return pl.ds(pl.multiple_of(at, quarter), quarter)

        for p, (block, half) in enumerate(PIECES):
            own[:, p * quarter : (p + 1) * quarter] = source[:, column(0, block, half)]
        for k, target, base in ((1, message1, units), (2, message2, units), (3, message3, 0)):
            for p in range(4):
                block = jnp.where(core == 0, PIECES[p][0], PIECES[p + 4][0])
                half = jnp.where(core == 0, PIECES[p][1], PIECES[p + 4][1])
                target[:, base + p * quarter : base + (p + 1) * quarter] = source[:, column(k, block, half)]

        @pl.loop(0, tokens // step)
        def _(i):
            here = pl.ds(pl.multiple_of(i * step, step), step)
            activated, _ = gelu_parts(gate[here, :].astype(jnp.float32))
            value = (activated * up[here, :].astype(jnp.float32)).astype(jnp.bfloat16)
            hidden[here, :] = value
            message1[here, :units] = value
            message2[here, :units] = value

    wide = jax.ShapeDtypeStruct((tokens, units + share_width // 2), jnp.bfloat16)
    vmem = pl.BlockSpec(memory_space=pltpu.VMEM)
    return pl.pallas_call(
        kernel,
        out_shape=[
            jax.ShapeDtypeStruct((tokens, share_width), jnp.bfloat16),
            jax.ShapeDtypeStruct((tokens, units), jnp.bfloat16),
            wide,
            wide,
            jax.ShapeDtypeStruct((tokens, share_width // 2), jnp.bfloat16),
        ],
        in_specs=[pl.BlockSpec(memory_space=pltpu.SMEM), vmem, vmem, vmem],
        out_specs=[vmem] * 5,
        compiler_params=pltpu.CompilerParams(vmem_limit_bytes=24 << 20),
        cost_estimate=pl.CostEstimate(
            flops=20 * tokens * units, bytes_accessed=16 * tokens * units, transcendentals=tokens * units
        ),
    )(place, out_grad, gate_pre, up_pre)


def staged_products(out_grad, gate_pre, up_pre, down_weight):
    x_bit, y_bit, z_bit, w_bit = 1, 2, 4, 8
    me, core = lax.axis_index("dp"), lax.axis_index("mp")
    tokens, units = gate_pre.shape
    rows = down_weight.shape[0]
    q, t = rows // 2, tokens // 2
    place = jnp.stack([me, core]).astype(jnp.int32)
    own, hidden, message1, message2, message3 = first_stage(out_grad, gate_pre, up_pre, place, rows)

    weight1, weight2 = flip(down_weight, x_bit), flip(down_weight, y_bit)
    message1, message2, message3 = flip(message1, z_bit), flip(message2, w_bit), flip(message3, z_bit | w_bit)
    weight1, weight2, message1, message2, message3 = lax.optimization_barrier(
        (weight1, weight2, message1, message2, message3)
    )

    hidden3a = flip(message1[:t, :units], w_bit)
    hidden3b = flip(message2[t:, :units], z_bit)
    weight3a = flip(weight1[:q], y_bit)
    weight3b = flip(weight2[q:], x_bit)
    mine = jnp.concatenate([message1[:, units:], message2[:, units:], message3], axis=1)
    theirs = flip(mine, 1, "mp")
    hidden3a, hidden3b, weight3a, weight3b, theirs = lax.optimization_barrier(
        (hidden3a, hidden3b, weight3a, weight3b, theirs)
    )

    def features(k):
        a, b = mine[:, (k - 1) * 2 * rows : k * 2 * rows], theirs[:, (k - 1) * 2 * rows : k * 2 * rows]
        return jnp.concatenate([jnp.where(core == 0, a, b), jnp.where(core == 0, b, a)], axis=1)

    peers = [own] + [features(k) for k in range(1, 4)]
    share = jnp.concatenate([peers[k][h * t : (h + 1) * t] for k, h in PIECES], axis=0)
    hidden_all = jnp.concatenate(
        [hidden, message1[:t, :units], hidden3a, message2[t:, :units], hidden3b, message2[:t, :units], message1[t:, :units]],
        axis=0,
    )
    weight_all = jnp.concatenate(
        [down_weight, weight1[:q], weight3a, weight2[q:], weight3b, weight2[:q], weight1[q:]], axis=0
    )

    def grad_rows(begin, end):
        return lax.dot_general(
            share[:, begin * q : end * q], hidden_all, (((0,), (0,)), ((), ())), preferred_element_type=jnp.float32
        )

    def hidden_grad_rows(begin, end):
        return jnp.dot(share[begin * t : end * t], weight_all, preferred_element_type=jnp.float32)

    def scatter(part, size, low, high):
        from_low = flip(part(2, 4).astype(jnp.bfloat16), low)
        from_high = flip(part(4, 6).astype(jnp.bfloat16), high)
        last_a = flip((part(6, 7) + from_low[size:].astype(jnp.float32)).astype(jnp.bfloat16), high)
        last_b = flip((part(7, 8) + from_high[size:].astype(jnp.float32)).astype(jnp.bfloat16), low)
        kept = jnp.concatenate([from_low[:size], from_high[:size]], axis=0).astype(jnp.float32)
        last = jnp.concatenate([last_a, last_b], axis=0).astype(jnp.float32)
        return part(0, 2) + kept + last

    product = scatter(grad_rows, q, x_bit, y_bit)
    hidden_grad = scatter(hidden_grad_rows, t, z_bit, w_bit)
    return product, hidden_grad


def local(out_grad, gate_pre, up_pre, down_weight, row_moment, col_moment):
    size = lax.axis_size("dp")
    rows, units = down_weight.shape
    tokens = out_grad.shape[0]
    all_bits = [1 << b for b in range(size.bit_length() - 1)]
    staged = size == 16 and lax.axis_size("mp") == 2 and rows % 256 == 0 and tokens % 32 == 0 and units % 128 == 0
    if staged:
        product, hidden_grad = staged_products(out_grad, gate_pre, up_pre, down_weight)
    else:
        product, hidden_grad = general_products(
            out_grad, gate_pre, up_pre, down_weight, all_bits[:INNER_BITS], all_bits[INNER_BITS:]
        )

    gate_late, up_late, hidden_grad = lax.optimization_barrier((gate_pre, up_pre, hidden_grad))
    activated, derivative = gelu_parts(gate_late.astype(jnp.float32))
    gate_grad = (hidden_grad * up_late.astype(jnp.float32) * derivative).astype(jnp.bfloat16)
    up_grad = (hidden_grad * activated).astype(jnp.bfloat16)

    grad = product * (1.0 / math.sqrt(tokens * size))
    decay = 1.0 - TRAIN_STEP ** (-0.8)
    total_rows = rows * size
    total_units = units * lax.axis_size("mp")
    powers = grad * grad
    squares = powers + 1e-30
    row_sum = lax.psum(jnp.sum(squares, axis=1), "mp")
    row_moment_new = decay * row_moment + (1.0 - decay) * (row_sum / total_units)
    col_part = jnp.sum(squares, axis=0)
    scaled_part = jnp.sum(powers / row_moment_new[:, None], axis=0)
    total_part = jnp.broadcast_to(jnp.sum(row_moment_new), (128,))
    sums = group_sum(jnp.concatenate([col_part, scaled_part, total_part]), all_bits)
    col_moment_new = decay * col_moment + (1.0 - decay) * (sums[:units] / total_rows)
    row_mean = sums[2 * units] / total_rows
    square_sum = row_mean * lax.psum(jnp.sum(sums[units : 2 * units] / col_moment_new), "mp")
    clip_norm = jnp.sqrt(square_sum / (total_rows * total_units))
    row_factor = jnp.sqrt(row_mean / row_moment_new) / jnp.maximum(1.0, clip_norm)
    col_factor = 1.0 / jnp.sqrt(col_moment_new)
    update = grad * row_factor[:, None] * col_factor[None, :]
    return (update, row_moment_new, col_moment_new, row_mean, gate_grad, up_grad)


def solution(mesh):
    in_specs = (P("dp", None), P("dp", "mp"), P("dp", "mp"), P("dp", "mp"), P("dp"), P("mp"))
    out_specs = (P("dp", "mp"), P("dp"), P("mp"), P(), P("dp", "mp"), P("dp", "mp"))
    return jax.shard_map(local, mesh=mesh, in_specs=in_specs, out_specs=out_specs, check_vma=False)
```

time: 205 us -> 178 us (0.87)
  waiting for transfers between devices: 107 us -> 75.5 us
  starting transfers between devices: 43.5 us -> 31.1 us
  local copies, waits for them, and re-layouts: 11.7 us -> 23.8 us
  matrix products: 21.6 us -> 24.8 us
    ppermute x29 -> x24, waiting for transfers between devices: 107 us -> 75.5 us  [flip(): return lax.ppermute(value, axis, [(i, i ^ bits) for i in range(size)])]
    unnamed x71 -> x48, local copies, waits for them, and re-layouts: 3.47 us -> 17 us
    ppermute x29 -> x24, starting transfers between devices: 43.5 us -> 31.1 us  [flip(): return lax.ppermute(value, axis, [(i, i ^ bits) for i in range(size)])]
    another operation x17 -> x0, local copies, waits for them, and re-layouts: 3.5 us -> none
    dot_general x16 -> x10, matrix products: 21.6 us -> 24.8 us  [the longest x5 19.2 us: hidden_grad_rows(): jnp.dot(share[begin * t:end * t], weight_all, preferred_element_type=jnp....]
    concatenate x5 -> x2, other arithmetic: 3.49 us -> 0.8 us  [the longest x1 0.79 us: staged_products(): jnp.concatenate([message1[:, units:], message2[:, units:], message3], axi...]
  transfers between devices with their start and end apart: 29 -> 24, of which waited for: 12 -> 9; matrix products, arithmetic and copies ran while one was open for 17% -> 24% of each run, Pallas kernels for 0% -> 1%
where the time goes in v4:
time: 178 us; the launch traced here: 177 us
  waiting for transfers between devices  75.5 us (42%)
  starting transfers between devices  31.1 us (17%)
  matrix products  24.8 us (14%)
  local copies, waits for them, and re-layouts  23.8 us (13%)
  other arithmetic  11.2 us (6%)
  blocking collectives  5.86 us (3%)
  between operations  3.36 us (2%)
    ppermute x24, waiting for transfers between devices, flip(): return lax.ppermute(value, axis, [(i, i ^ bits) for i in range(size)])  75.5 us
    ppermute x24, starting transfers between devices, flip(): return lax.ppermute(value, axis, [(i, i ^ bits) for i in range(size)])  31.1 us
    dot_general x5, matrix products, hidden_grad_rows(): jnp.dot(share[begin * t:end * t], weight_all, preferred_element_type=jnp....  19.2 us
    unnamed x48, local copies, waits for them, and re-layouts  17 us
    dot_general x5, matrix products, grad_rows(): lax.dot_general(share[:, begin * q:end * q], hidden_all, (((0,), (0,)), (...  5.66 us
  transfers between devices with their start and end apart: 24, of which 9 were waited for; matrix products, arithmetic and copies ran while one was open for 24% of the time, Pallas kernels for 1%

profile of v4, /device:TPU:0, one launch (start us, length us, event | category | flops | bytes accessed | tf_op | source)
XLA Modules:
  0.0 176.9 jit_solution(10463173373808653955)
XLA Ops:
  0.6 3.0 %collective-permute-start = (bf16[256,2560]{1,0:T(8,128)(2,1)}, bf16[256,2560]{1,0:T(8,128)(2,1)}, u32[]{:S(2)}, u32[]{:S(2)}) collective-permute-start(bf16[256,2560]{1,0:T(8,128)(2,1)} %param.9), channel_id=1, source_target_pairs={{0,2},{2,0},{4,6},{6,4},{8,10},{10,8},{12,14},{14,12},{16,18},{18,... | collective-permute-start | bytes 3932168 | tf_op jit(solution)/shard_map/ppermute | solution.py:28
  11.6 2.6 %collective-permute-start.3 = (bf16[128,3072]{1,0:T(8,128)(2,1)S(1)}, bf16[128,3072]{1,0:T(8,128)(2,1)S(1)}, u32[]{:S(2)}, u32[]{:S(2)}) collective-permute-start(bf16[128,3072]{1,0:T(8,128)(2,1)S(1)} %get-tuple-element.26), channel_id=1, source_target_pairs={{0,16},{2,18},{4,20},{6,22},{8,24},{10,26},{12,28},{14,30},{16,0},... | collective-permute-start | bytes 2359304 | tf_op jit(solution)/shard_map/ppermute | solution.py:28
  15.6 34.9 %collective-permute-done.4 = bf16[128,512]{1,0:T(8,128)(2,1)S(1)} collective-permute-done((bf16[128,512]{1,0:T(8,128)(2,1)S(1)}, bf16[128,512]{1,0:T(8,128)(2,1)S(1)}, u32[]{:S(2)}, u32[]{:S(2)}) %collective-permute-start.4) | collective-permute-done | bytes 131104 | tf_op jit(solution)/shard_map/ppermute | solution.py:28
  52.0 2.5 %constant_dynamic-update-slice_fusion.15 = (bf16[1024,2560]{1,0:T(8,128)(2,1)}, bf16[128,2560]{1,0:T(8,128)(2,1)}) fusion(bf16[1024,2560]{1,0:T(8,128)(2,1)} %constant_dynamic-update-slice_fusion.16, bf16[256,2560]{1,0:T(8,128)(2,1)} %collective-permute-done), kind=kLoop, calls=%fused_computation.86 | loop fusion | bytes 1966080
  59.9 3.2 %collective-permute-start.5 = (bf16[64,2560]{1,0:T(8,128)(2,1)}, bf16[64,2560]{1,0:T(8,128)(2,1)}, u32[]{:S(2)}, u32[]{:S(2)}) collective-permute-start(bf16[64,2560]{1,0:T(8,128)(2,1)} %get-tuple-element.64), channel_id=1, source_target_pairs={{0,16},{2,18},{4,20},{6,22},{8,24},{10,26},{12,28},{14,30},{16,0},... | collective-permute-start | bytes 983048 | tf_op jit(solution)/shard_map/ppermute | solution.py:28
  63.1 15.8 %collective-permute-done.5 = bf16[64,2560]{1,0:T(8,128)(2,1)} collective-permute-done((bf16[64,2560]{1,0:T(8,128)(2,1)}, bf16[64,2560]{1,0:T(8,128)(2,1)}, u32[]{:S(2)}, u32[]{:S(2)}) %collective-permute-start.5) | collective-permute-done | bytes 327712 | tf_op jit(solution)/shard_map/ppermute | solution.py:28
  89.2 2.0 %constant_dynamic-update-slice_fusion.13 = bf16[1024,2560]{1,0:T(8,128)(2,1)} fusion(bf16[1024,2560]{1,0:T(8,128)(2,1)} %constant_dynamic-update-slice_fusion.14, bf16[256,2560]{1,0:T(8,128)(2,1)} %collective-permute-done.1), kind=kLoop, calls=%fused_computation.84 | loop fusion | bytes 1310720
  93.1 2.0 %slice_dynamic-update-slice_fusion.1 = bf16[1024,2560]{1,0:T(8,128)(2,1)} fusion(bf16[1024,2560]{1,0:T(8,128)(2,1)} %constant_dynamic-update-slice_fusion.12, bf16[256,2560]{1,0:T(8,128)(2,1)} %collective-permute-done.1), kind=kLoop, calls=%fused_computation.35 | loop fusion | bytes 1310720
  95.1 2.0 %slice_dynamic-update-slice_fusion = bf16[1024,2560]{1,0:T(8,128)(2,1)} fusion(bf16[1024,2560]{1,0:T(8,128)(2,1)} %slice_dynamic-update-slice_fusion.1, bf16[256,2560]{1,0:T(8,128)(2,1)} %collective-permute-done), kind=kLoop, calls=%fused_computation.34 | loop fusion | bytes 1310720 | tf_op jit(solution)/shard_map/concatenate | solution.py:178
  97.1 3.4 %convolution_convert_fusion.2 = bf16[128,2560]{1,0:T(8,128)(2,1)S(1)} fusion(bf16[1024,2560]{1,0:T(8,128)(2,1)} %slice_dynamic-update-slice_fusion, bf16[64,1024]{1,0:T(8,128)(2,1)S(1)} %get-tuple-element.49, bf16[64,1024]{1,0:T(8,128)(2,1)S(1)} %get-tuple-element.51), kind=kOutput, calls=%fused_computation.2 | convolution fusion | flops 671940608 | bytes 6160384 | tf_op jit(solution)/shard_map/dot_general | solution.py:188
  101.9 3.4 %convolution_convert_fusion.3 = bf16[128,2560]{1,0:T(8,128)(2,1)S(1)} fusion(bf16[1024,2560]{1,0:T(8,128)(2,1)} %slice_dynamic-update-slice_fusion, bf16[64,1024]{1,0:T(8,128)(2,1)S(1)} %get-tuple-element.53, bf16[64,1024]{1,0:T(8,128)(2,1)S(1)} %get-tuple-element.55), kind=kOutput, calls=%fused_computation.3 | convolution fusion | flops 671940608 | bytes 6160384 | tf_op jit(solution)/shard_map/dot_general | solution.py:188
  106.1 9.5 %collective-permute-done.11 = bf16[256,2560]{1,0:T(8,128)(2,1)S(1)} collective-permute-done((bf16[256,2560]{1,0:T(8,128)(2,1)S(1)}, bf16[256,2560]{1,0:T(8,128)(2,1)S(1)}, u32[]{:S(2)}, u32[]{:S(2)}) %collective-permute-start.11) | collective-permute-done | bytes 1310752 | tf_op jit(solution)/shard_map/ppermute | solution.py:28
  119.9 11.4 %collective-permute-done.21 = bf16[128,2560]{1,0:T(8,128)(2,1)S(1)} collective-permute-done((bf16[128,2560]{1,0:T(8,128)(2,1)S(1)}, bf16[128,2560]{1,0:T(8,128)(2,1)S(1)}, u32[]{:S(2)}, u32[]{:S(2)}) %collective-permute-start.21) | collective-permute-done | bytes 655392 | tf_op jit(solution)/shard_map/ppermute | solution.py:28
  131.4 4.5 %add_convert_fusion.2 = bf16[64,2560]{1,0:T(8,128)(2,1)} fusion(bf16[128,2560]{1,0:T(8,128)(2,1)S(1)} %collective-permute-done.21, bf16[1024,2560]{1,0:T(8,128)(2,1)} %slice_dynamic-update-slice_fusion, bf16[128,512]{1,0:T(8,128)(2,1)S(1)} %get-tuple-element.70, bf16[128,512]{1,0:T(8,128)(2,1)S(1)} %get-tuple-element.71), kind=kOutput, calls=%fused_computation.32 | convolution fusion | flops 336297984 | bytes 6160384 | tf_op jit(solution)/shard_map/dot_general | solution.py:188
  135.9 4.5 %add_convert_fusion.3 = bf16[64,2560]{1,0:T(8,128)(2,1)} fusion(bf16[128,2560]{1,0:T(8,128)(2,1)S(1)} %collective-permute-done.20, bf16[1024,2560]{1,0:T(8,128)(2,1)} %slice_dynamic-update-slice_fusion, bf16[128,512]{1,0:T(8,128)(2,1)S(1)} %get-tuple-element.61, bf16[128,512]{1,0:T(8,128)(2,1)S(1)} %get-tuple-element.60), kind=kOutput, calls=%fused_computation.33 | convolution fusion | flops 336297984 | bytes 6160384 | tf_op jit(solution)/shard_map/dot_general | solution.py:188
  140.3 2.2 %collective-permute-start.22 = (bf16[64,2560]{1,0:T(8,128)(2,1)}, bf16[64,2560]{1,0:T(8,128)(2,1)}, u32[]{:S(2)}, u32[]{:S(2)}) collective-permute-start(bf16[64,2560]{1,0:T(8,128)(2,1)} %add_convert_fusion.3), channel_id=1, source_target_pairs={{0,16},{2,18},{4,20},{6,22},{8,24},{10,26},{12,28},{14,30},{16,0},... | collective-permute-start | bytes 983048 | tf_op jit(solution)/shard_map/ppermute | solution.py:28
  142.7 2.8 %add_reduce_fusion = (f32[256]{0:T(256)S(1)}, f32[256,2560]{1,0:T(8,128)}) fusion(bf16[128,2560]{1,0:T(8,128)(2,1)S(1)} %collective-permute-done.13, bf16[128,2560]{1,0:T(8,128)(2,1)S(1)} %collective-permute-done.12, bf16[128,2560]{1,0:T(8,128)(2,1)S(1)} %slice.162, bf16[128,2560]{1,0:T(8,128)(2,1)S(1)} %slice.160, ...), kind=kOutput, calls=%fused_computation.15 | convolution fusion | flops 680263424 | bytes 8127488 | tf_op jit(solution)/shard_map/dot_general | solution.py:183
  145.5 2.8 %psum.14 = f32[256]{0:T(256)S(1)} all-reduce(f32[256]{0:T(256)S(1)} %get-tuple-element.72), channel_id=1, replica_groups=mesh['dp'=16,'mp'=2] {'mp'}, use_global_device_ids=true, to_apply=%region_2.3 | all-reduce | flops 256 | bytes 2048 | tf_op jit(solution)/shard_map/psum | solution.py:228
  148.9 2.3 %add_reduce_fusion.1 = (f32[2560]{0:T(1024)S(1)}, f32[2560]{0:T(1024)S(1)}) fusion(f32[256,2560]{1,0:T(8,128)} %get-tuple-element.73, f32[256]{0:T(256)S(1)} %get-tuple-element.47), kind=kLoop, calls=%fused_computation.16 | loop fusion | flops 3927040 | bytes 2642944 | tf_op jit(solution)/shard_map/reduce_sum | solution.py:230
  157.2 3.5 %convert_add_fusion.2 = f32[128,2560]{1,0:T(8,128)S(1)} fusion(bf16[64,2560]{1,0:T(8,128)(2,1)S(1)} %slice-done, bf16[64,2560]{1,0:T(8,128)(2,1)S(1)} %slice-done.1, bf16[64,2560]{1,0:T(8,128)(2,1)} %collective-permute-done.23, bf16[64,2560]{1,0:T(8,128)(2,1)} %collective-permute-done.22, bf16[128,1024]{1,0:T(8,128)(2,1)S(1)} %get-tuple-element.24, ...), kind=kOutput, calls=%fused_computation.29 | convolution fusion | flops 674365440 | bytes 8126464 | tf_op jit(solution)/shard_map/dot_general | solution.py:188
  160.8 2.0 %collective-permute-start.19 = (f32[5248]{0:T(1024)S(1)}, f32[5248]{0:T(1024)S(1)}, u32[]{:S(2)}, u32[]{:S(2)}) collective-permute-start(f32[5248]{0:T(1024)S(1)} %add_add_fusion.1), channel_id=1, source_target_pairs={{0,24},{2,26},{4,28},{6,30},{8,16},{10,18},{12,20},{14,22},{16,8},... | collective-permute-start | bytes 62984 | tf_op jit(solution)/shard_map/ppermute | solution.py:28
  164.3 2.1 %fusion.8 = (bf16[128,2560]{1,0:T(8,128)(2,1)}, bf16[128,2560]{1,0:T(8,128)(2,1)}) fusion(f32[128,2560]{1,0:T(8,128)S(1)} %convert_add_fusion.2, bf16[128,2560]{1,0:T(8,128)(2,1)S(1)} %copy-done.1, bf16[128,2560]{1,0:T(8,128)(2,1)S(1)} %copy-done.3), kind=kLoop, calls=%fused_computation.25 | loop fusion | flops 8192000 | bytes 3932160 | tf_op jit(solution)/shard_map/convert_element_type | solution.py:220
  167.9 3.1 %psum.15 = f32[]{:T(128)} all-reduce(f32[]{:T(128)} %get-tuple-element.44), channel_id=1, replica_groups=mesh['dp'=16,'mp'=2] {'mp'}, use_global_device_ids=true, to_apply=%region_6.7 | all-reduce | flops 1 | bytes 8 | tf_op jit(solution)/shard_map/psum | solution.py:236
  172.3 3.5 %multiply_multiply_fusion = f32[256,2560]{1,0:T(8,128)} fusion(f32[256,2560]{1,0:T(8,128)} %get-tuple-element.73, f32[2560]{0:T(1024)S(1)} %sqrt.11, f32[256]{0:T(256)S(1)} %divide_multiply_fusion), kind=kLoop, calls=%fused_computation.11 | loop fusion | flops 1310720 | bytes 5254144 | tf_op jit(solution)/shard_map/mul | solution.py:240
  (119 shorter events, 44.7 us)
Async XLA Ops:
  0.6 51.4 %collective-permute-start = (bf16[256,2560]{1,0:T(8,128)(2,1)}, bf16[256,2560]{1,0:T(8,128)(2,1)}, u32[]{:S(2)}, u32[]{:S(2)}) collective-permute-start(bf16[256,2560]{1,0:T(8,128)(2,1)} %param.9), channel_id=1, source_target_pairs={{0,2},{2,0},{4,6},{6,4},{8,10},{10,8},{12,14},{14,12},{16,18},{18,... | collective-permute-start | bytes 3932168 | tf_op jit(solution)/shard_map/ppermute | solution.py:28
  3.6 48.4 %collective-permute-start.1 = (bf16[256,2560]{1,0:T(8,128)(2,1)}, bf16[256,2560]{1,0:T(8,128)(2,1)}, u32[]{:S(2)}, u32[]{:S(2)}) collective-permute-start(bf16[256,2560]{1,0:T(8,128)(2,1)} %param.9), channel_id=1, source_target_pairs={{0,4},{2,6},{4,0},{6,2},{8,12},{10,14},{12,8},{14,10},{16,20},{18,... | collective-permute-start | bytes 3932168 | tf_op jit(solution)/shard_map/ppermute | solution.py:28
  9.9 40.6 %collective-permute-start.2 = (bf16[128,3072]{1,0:T(8,128)(2,1)S(1)}, bf16[128,3072]{1,0:T(8,128)(2,1)S(1)}, u32[]{:S(2)}, u32[]{:S(2)}) collective-permute-start(bf16[128,3072]{1,0:T(8,128)(2,1)S(1)} %get-tuple-element.25), channel_id=1, source_target_pairs={{0,8},{2,10},{4,12},{6,14},{8,0},{10,2},{12,4},{14,6},{16,24},{18,... | collective-permute-start | bytes 2359304 | tf_op jit(solution)/shard_map/ppermute | solution.py:28
  11.6 40.5 %collective-permute-start.3 = (bf16[128,3072]{1,0:T(8,128)(2,1)S(1)}, bf16[128,3072]{1,0:T(8,128)(2,1)S(1)}, u32[]{:S(2)}, u32[]{:S(2)}) collective-permute-start(bf16[128,3072]{1,0:T(8,128)(2,1)S(1)} %get-tuple-element.26), channel_id=1, source_target_pairs={{0,16},{2,18},{4,20},{6,22},{8,24},{10,26},{12,28},{14,30},{16,0},... | collective-permute-start | bytes 2359304 | tf_op jit(solution)/shard_map/ppermute | solution.py:28
  14.2 36.3 %collective-permute-start.4 = (bf16[128,512]{1,0:T(8,128)(2,1)S(1)}, bf16[128,512]{1,0:T(8,128)(2,1)S(1)}, u32[]{:S(2)}, u32[]{:S(2)}) collective-permute-start(bf16[128,512]{1,0:T(8,128)(2,1)S(1)} %get-tuple-element.27), channel_id=1, source_target_pairs={{0,24},{2,26},{4,28},{6,30},{8,16},{10,18},{12,20},{14,22},{16,8},... | collective-permute-start | bytes 393224 | tf_op jit(solution)/shard_map/ppermute | solution.py:28
  54.5 24.6 %collective-permute-start.7 = (bf16[128,2560]{1,0:T(8,128)(2,1)}, bf16[128,2560]{1,0:T(8,128)(2,1)S(1)}, u32[]{:S(2)}, u32[]{:S(2)}) collective-permute-start(bf16[128,2560]{1,0:T(8,128)(2,1)} %get-tuple-element.59), channel_id=1, source_target_pairs={{0,4},{2,6},{4,0},{6,2},{8,12},{10,14},{12,8},{14,10},{16,20},{18,... | collective-permute-start | bytes 1966088 | tf_op jit(solution)/shard_map/ppermute | solution.py:28
  57.0 22.1 %collective-permute-start.8 = (bf16[128,2560]{1,0:T(8,128)(2,1)}, bf16[128,2560]{1,0:T(8,128)(2,1)}, u32[]{:S(2)}, u32[]{:S(2)}) collective-permute-start(bf16[128,2560]{1,0:T(8,128)(2,1)} %slice.121), channel_id=1, source_target_pairs={{0,2},{2,0},{4,6},{6,4},{8,10},{10,8},{12,14},{14,12},{16,18},{18,... | collective-permute-start | bytes 1966088 | tf_op jit(solution)/shard_map/ppermute | solution.py:28
  58.4 20.7 %collective-permute-start.9 = (bf16[128,1536]{1,0:T(8,128)(2,1)}, bf16[128,1536]{1,0:T(8,128)(2,1)}, u32[]{:S(2)}, u32[]{:S(2)}) collective-permute-start(bf16[128,1536]{1,0:T(8,128)(2,1)} %pad_maximum_fusion), channel_id=1, source_target_pairs={{0,1},{1,0},{2,3},{3,2},{4,5},{5,4},{6,7},{7,6},{8,9},{9,8},{10,11... | collective-permute-start | bytes 1179656 | tf_op jit(solution)/shard_map/ppermute | solution.py:28
  59.9 19.0 %collective-permute-start.5 = (bf16[64,2560]{1,0:T(8,128)(2,1)}, bf16[64,2560]{1,0:T(8,128)(2,1)}, u32[]{:S(2)}, u32[]{:S(2)}) collective-permute-start(bf16[64,2560]{1,0:T(8,128)(2,1)} %get-tuple-element.64), channel_id=1, source_target_pairs={{0,16},{2,18},{4,20},{6,22},{8,24},{10,26},{12,28},{14,30},{16,0},... | collective-permute-start | bytes 983048 | tf_op jit(solution)/shard_map/ppermute | solution.py:28
  63.1 16.0 %collective-permute-start.6 = (bf16[64,2560]{1,0:T(8,128)(2,1)}, bf16[64,2560]{1,0:T(8,128)(2,1)}, u32[]{:S(2)}, u32[]{:S(2)}) collective-permute-start(bf16[64,2560]{1,0:T(8,128)(2,1)} %slice.119), channel_id=1, source_target_pairs={{0,8},{2,10},{4,12},{6,14},{8,0},{10,2},{12,4},{14,6},{16,24},{18,... | collective-permute-start | bytes 983048 | tf_op jit(solution)/shard_map/ppermute | solution.py:28
  85.2 30.4 %collective-permute-start.11 = (bf16[256,2560]{1,0:T(8,128)(2,1)S(1)}, bf16[256,2560]{1,0:T(8,128)(2,1)S(1)}, u32[]{:S(2)}, u32[]{:S(2)}) collective-permute-start(bf16[256,2560]{1,0:T(8,128)(2,1)S(1)} %convolution_convert_fusion), channel_id=1, source_target_pairs={{0,4},{2,6},{4,0},{6,2},{8,12},{10,14},{12,8},{14,10},{16,20},{18,... | collective-permute-start | bytes 3932168 | tf_op jit(solution)/shard_map/ppermute | solution.py:28
  86.8 31.0 %collective-permute-start.10 = (bf16[256,2560]{1,0:T(8,128)(2,1)S(1)}, bf16[256,2560]{1,0:T(8,128)(2,1)S(1)}, u32[]{:S(2)}, u32[]{:S(2)}) collective-permute-start(bf16[256,2560]{1,0:T(8,128)(2,1)S(1)} %convolution_convert_fusion.1), channel_id=1, source_target_pairs={{0,2},{2,0},{4,6},{6,4},{8,10},{10,8},{12,14},{14,12},{16,18},{18,... | collective-permute-start | bytes 3932168 | tf_op jit(solution)/shard_map/ppermute | solution.py:28
  100.5 30.9 %collective-permute-start.21 = (bf16[128,2560]{1,0:T(8,128)(2,1)S(1)}, bf16[128,2560]{1,0:T(8,128)(2,1)S(1)}, u32[]{:S(2)}, u32[]{:S(2)}) collective-permute-start(bf16[128,2560]{1,0:T(8,128)(2,1)S(1)} %convolution_convert_fusion.2), channel_id=1, source_target_pairs={{0,16},{2,18},{4,20},{6,22},{8,24},{10,26},{12,28},{14,30},{16,0},... | collective-permute-start | bytes 1966088 | tf_op jit(solution)/shard_map/ppermute | solution.py:28
  105.3 30.6 %collective-permute-start.20 = (bf16[128,2560]{1,0:T(8,128)(2,1)S(1)}, bf16[128,2560]{1,0:T(8,128)(2,1)S(1)}, u32[]{:S(2)}, u32[]{:S(2)}) collective-permute-start(bf16[128,2560]{1,0:T(8,128)(2,1)S(1)} %convolution_convert_fusion.3), channel_id=1, source_target_pairs={{0,8},{2,10},{4,12},{6,14},{8,0},{10,2},{12,4},{14,6},{16,24},{18,... | collective-permute-start | bytes 1966088 | tf_op jit(solution)/shard_map/ppermute | solution.py:28
  116.2 26.4 %collective-permute-start.13 = (bf16[128,2560]{1,0:T(8,128)(2,1)S(1)}, bf16[128,2560]{1,0:T(8,128)(2,1)S(1)}, u32[]{:S(2)}, u32[]{:S(2)}) collective-permute-start(bf16[128,2560]{1,0:T(8,128)(2,1)S(1)} %add_convert_fusion), channel_id=1, source_target_pairs={{0,2},{2,0},{4,6},{6,4},{8,10},{10,8},{12,14},{14,12},{16,18},{18,... | collective-permute-start | bytes 1966088 | tf_op jit(solution)/shard_map/ppermute | solution.py:28
  118.3 24.3 %collective-permute-start.12 = (bf16[128,2560]{1,0:T(8,128)(2,1)S(1)}, bf16[128,2560]{1,0:T(8,128)(2,1)S(1)}, u32[]{:S(2)}, u32[]{:S(2)}) collective-permute-start(bf16[128,2560]{1,0:T(8,128)(2,1)S(1)} %add_convert_fusion.1), channel_id=1, source_target_pairs={{0,4},{2,6},{4,0},{6,2},{8,12},{10,14},{12,8},{14,10},{16,20},{18,... | collective-permute-start | bytes 1966088 | tf_op jit(solution)/shard_map/ppermute | solution.py:28
  135.8 19.6 %collective-permute-start.23 = (bf16[64,2560]{1,0:T(8,128)(2,1)}, bf16[64,2560]{1,0:T(8,128)(2,1)}, u32[]{:S(2)}, u32[]{:S(2)}) collective-permute-start(bf16[64,2560]{1,0:T(8,128)(2,1)} %add_convert_fusion.2), channel_id=1, source_target_pairs={{0,8},{2,10},{4,12},{6,14},{8,0},{10,2},{12,4},{14,6},{16,24},{18,... | collective-permute-start | bytes 983048 | tf_op jit(solution)/shard_map/ppermute | solution.py:28
  140.3 16.8 %collective-permute-start.22 = (bf16[64,2560]{1,0:T(8,128)(2,1)}, bf16[64,2560]{1,0:T(8,128)(2,1)}, u32[]{:S(2)}, u32[]{:S(2)}) collective-permute-start(bf16[64,2560]{1,0:T(8,128)(2,1)} %add_convert_fusion.3), channel_id=1, source_target_pairs={{0,16},{2,18},{4,20},{6,22},{8,24},{10,26},{12,28},{14,30},{16,0},... | collective-permute-start | bytes 983048 | tf_op jit(solution)/shard_map/ppermute | solution.py:28
  151.9 8.8 %collective-permute-start.15 = (f32[5248]{0:T(1024)S(1)}, f32[5248]{0:T(1024)S(1)}, u32[]{:S(2)}, u32[]{:S(2)}) collective-permute-start(f32[5248]{0:T(1024)S(1)} %pad_maximum_fusion.4), channel_id=1, source_target_pairs={{0,4},{2,6},{4,0},{6,2},{8,12},{10,14},{12,8},{14,10},{16,20},{18,... | collective-permute-start | bytes 62984 | tf_op jit(solution)/shard_map/ppermute | solution.py:28
  152.4 8.3 %collective-permute-start.16 = (f32[5248]{0:T(1024)S(1)}, f32[5248]{0:T(1024)S(1)}, u32[]{:S(2)}, u32[]{:S(2)}) collective-permute-start(f32[5248]{0:T(1024)S(1)} %pad_maximum_fusion.4), channel_id=1, source_target_pairs={{0,6},{2,4},{4,2},{6,0},{8,14},{10,12},{12,10},{14,8},{16,22},{18,... | collective-permute-start | bytes 62984 | tf_op jit(solution)/shard_map/ppermute | solution.py:28
  153.9 6.8 %collective-permute-start.14 = (f32[5248]{0:T(1024)S(1)}, f32[5248]{0:T(1024)S(1)}, u32[]{:S(2)}, u32[]{:S(2)}) collective-permute-start(f32[5248]{0:T(1024)S(1)} %pad_maximum_fusion.4), channel_id=1, source_target_pairs={{0,2},{2,0},{4,6},{6,4},{8,10},{10,8},{12,14},{14,12},{16,18},{18,... | collective-permute-start | bytes 62984 | tf_op jit(solution)/shard_map/ppermute | solution.py:28
  160.7 5.7 %collective-permute-start.18 = (f32[5248]{0:T(1024)S(1)}, f32[5248]{0:T(1024)S(1)}, u32[]{:S(2)}, u32[]{:S(2)}) collective-permute-start(f32[5248]{0:T(1024)S(1)} %add_add_fusion.1), channel_id=1, source_target_pairs={{0,16},{2,18},{4,20},{6,22},{8,24},{10,26},{12,28},{14,30},{16,0},... | collective-permute-start | bytes 62984 | tf_op jit(solution)/shard_map/ppermute | solution.py:28
  160.8 5.7 %collective-permute-start.19 = (f32[5248]{0:T(1024)S(1)}, f32[5248]{0:T(1024)S(1)}, u32[]{:S(2)}, u32[]{:S(2)}) collective-permute-start(f32[5248]{0:T(1024)S(1)} %add_add_fusion.1), channel_id=1, source_target_pairs={{0,24},{2,26},{4,28},{6,30},{8,16},{10,18},{12,20},{14,22},{16,8},... | collective-permute-start | bytes 62984 | tf_op jit(solution)/shard_map/ppermute | solution.py:28
  162.8 4.0 %collective-permute-start.17 = (f32[5248]{0:T(1024)S(1)}, f32[5248]{0:T(1024)S(1)}, u32[]{:S(2)}, u32[]{:S(2)}) collective-permute-start(f32[5248]{0:T(1024)S(1)} %add_add_fusion.1), channel_id=1, source_target_pairs={{0,8},{2,10},{4,12},{6,14},{8,0},{10,2},{12,4},{14,6},{16,24},{18,... | collective-permute-start | bytes 62984 | tf_op jit(solution)/shard_map/ppermute | solution.py:28
  (20 other events, 200.4 us)

commit v5 on v4

--- a/solution.py
+++ b/solution.py
@@ -29,13 +29,8 @@
 
 
 def group_sum(value, bits):
-    for at in range(0, len(bits), 2):
-        pair = bits[at : at + 2]
-        if len(pair) == 2:
-            first, second = flip(value, pair[0]), flip(value, pair[1])
-            value = (value + first) + (second + flip(value, pair[0] | pair[1]))
-        else:
-            value = value + flip(value, pair[0])
+    for bit in bits:
+        value = value + flip(value, bit)
     return value
 
 
@@ -140,6 +135,70 @@
     )(place, out_grad, gate_pre, up_pre)
 
 
+def cut(sources, parts):
+    def kernel(*refs):
+        ins, outs, sems = refs[: len(sources)], refs[len(sources) : -1], refs[-1]
+        copies = [
+            pltpu.make_async_copy(ins[i].at[pl.ds(*rows), pl.ds(*columns)], outs[n], sems.at[n])
+            for n, (i, rows, columns) in enumerate(parts)
+        ]
+        for copy in copies:
+            copy.start()
+        for copy in copies:
+            copy.wait()
+
+    shapes = [jax.ShapeDtypeStruct((rows[1], columns[1]), sources[i].dtype) for i, rows, columns in parts]
+    return pl.pallas_call(
+        kernel,
+        out_shape=shapes,
+        in_specs=[pl.BlockSpec(memory_space=pl.ANY)] * len(sources),
+        out_specs=[pl.BlockSpec(memory_space=pl.ANY)] * len(parts),
+        scratch_shapes=[pltpu.SemaphoreType.DMA((len(parts),))],
+        compiler_params=pltpu.CompilerParams(vmem_limit_bytes=4 << 20),
+        cost_estimate=pl.CostEstimate(
+            flops=0, bytes_accessed=sum(4 * r[1] * c[1] for _, r, c in parts), transcendentals=0
+        ),
+    )(*sources)
+
+
+def product(share, pieces, layout, outputs, over_rows, tile):
+    units = min(piece.shape[1] for piece in pieces)
+    depth = sum(rows for _, _, rows in layout)
+
+    def kernel(*refs):
+        share_ref, ins = refs[0], refs[1 : 1 + len(pieces)]
+        outs, stack = refs[1 + len(pieces) : -1], refs[-1]
+        at = 0
+        for piece, first, rows in layout:
+            stack[at : at + rows, :] = ins[piece][first : first + rows, :]
+            at += rows
+        for (begin, end, kind), out in zip(outputs, outs):
+            if over_rows:
+                value = lax.dot_general(
+                    share_ref[:, begin:end], stack[...], (((0,), (0,)), ((), ())), preferred_element_type=jnp.float32
+                )
+            else:
+                value = jnp.dot(share_ref[begin:end, :], stack[...], preferred_element_type=jnp.float32)
+            out[...] = value.astype(kind)
+
+    total = sum(end - begin for begin, end, _ in outputs)
+    return pl.pallas_call(
+        kernel,
+        grid=(units // tile,),
+        out_shape=[jax.ShapeDtypeStruct((end - begin, units), kind) for begin, end, kind in outputs],
+        in_specs=[pl.BlockSpec(share.shape, lambda i: (0, 0))]
+        + [pl.BlockSpec((piece.shape[0], tile), lambda i: (0, i)) for piece in pieces],
+        out_specs=[pl.BlockSpec((end - begin, tile), lambda i: (0, i)) for begin, end, _ in outputs],
+        scratch_shapes=[pltpu.VMEM((depth, tile), jnp.bfloat16)],
+        compiler_params=pltpu.CompilerParams(vmem_limit_bytes=24 << 20),
+        cost_estimate=pl.CostEstimate(
+            flops=2 * total * depth * units,
+            bytes_accessed=2 * (depth + 2 * total) * units + 2 * share.size,
+            transcendentals=0,
+        ),
+    )(share, *pieces)
+
+
 def staged_products(out_grad, gate_pre, up_pre, down_weight):
     x_bit, y_bit, z_bit, w_bit = 1, 2, 4, 8
     me, core = lax.axis_index("dp"), lax.axis_index("mp")
@@ -149,21 +208,21 @@
     place = jnp.stack([me, core]).astype(jnp.int32)
     own, hidden, message1, message2, message3 = first_stage(out_grad, gate_pre, up_pre, place, rows)
 
+    down_weight, message1 = lax.optimization_barrier((down_weight, message1))
+    message1, message2, message3 = flip(message1, z_bit), flip(message2, w_bit), flip(message3, z_bit | w_bit)
     weight1, weight2 = flip(down_weight, x_bit), flip(down_weight, y_bit)
-    message1, message2, message3 = flip(message1, z_bit), flip(message2, w_bit), flip(message3, z_bit | w_bit)
-    weight1, weight2, message1, message2, message3 = lax.optimization_barrier(
-        (weight1, weight2, message1, message2, message3)
+    whole, top, bottom = (0, units), (0, q), (q, q)
+    to_y, to_x = cut([weight1, weight2], [(0, top, whole), (1, bottom, whole)])
+    weight3a, weight3b = flip(to_y, y_bit), flip(to_x, x_bit)
+
+    message1, message2, message3, _, _ = lax.optimization_barrier((message1, message2, message3, weight1, weight2))
+    extra = (units, 2 * rows)
+    to_w, to_z, mine1, mine2 = cut(
+        [message1, message2], [(0, (0, t), whole), (1, (t, t), whole), (0, (0, tokens), extra), (1, (0, tokens), extra)]
     )
-
-    hidden3a = flip(message1[:t, :units], w_bit)
-    hidden3b = flip(message2[t:, :units], z_bit)
-    weight3a = flip(weight1[:q], y_bit)
-    weight3b = flip(weight2[q:], x_bit)
-    mine = jnp.concatenate([message1[:, units:], message2[:, units:], message3], axis=1)
+    hidden3a, hidden3b = flip(to_w, w_bit), flip(to_z, z_bit)
+    mine = jnp.concatenate([mine1, mine2, message3], axis=1)
     theirs = flip(mine, 1, "mp")
-    hidden3a, hidden3b, weight3a, weight3b, theirs = lax.optimization_barrier(
-        (hidden3a, hidden3b, weight3a, weight3b, theirs)
-    )
 
     def features(k):
         a, b = mine[:, (k - 1) * 2 * rows : k * 2 * rows], theirs[:, (k - 1) * 2 * rows : k * 2 * rows]
@@ -171,34 +230,34 @@
 
     peers = [own] + [features(k) for k in range(1, 4)]
     share = jnp.concatenate([peers[k][h * t : (h + 1) * t] for k, h in PIECES], axis=0)
-    hidden_all = jnp.concatenate(
-        [hidden, message1[:t, :units], hidden3a, message2[t:, :units], hidden3b, message2[:t, :units], message1[t:, :units]],
-        axis=0,
-    )
-    weight_all = jnp.concatenate(
-        [down_weight, weight1[:q], weight3a, weight2[q:], weight3b, weight2[:q], weight1[q:]], axis=0
-    )
-
-    def grad_rows(begin, end):
-        return lax.dot_general(
-            share[:, begin * q : end * q], hidden_all, (((0,), (0,)), ((), ())), preferred_element_type=jnp.float32
+
+    def layout(size):
+        return [(0, 0, 2 * size), (1, 0, size), (3, 0, size), (2, size, size), (4, 0, size), (2, 0, size), (1, size, size)]
+
+    def scatter(pieces, depth, size, low, high, over_rows):
+        tile = 512
+        send, keep = jnp.bfloat16, jnp.float32
+        low_part, high_part = product(
+            share, pieces, layout(depth), [(2 * size, 4 * size, send), (4 * size, 6 * size, send)], over_rows, tile
         )
-
-    def hidden_grad_rows(begin, end):
-        return jnp.dot(share[begin * t : end * t], weight_all, preferred_element_type=jnp.float32)
-
-    def scatter(part, size, low, high):
-        from_low = flip(part(2, 4).astype(jnp.bfloat16), low)
-        from_high = flip(part(4, 6).astype(jnp.bfloat16), high)
-        last_a = flip((part(6, 7) + from_low[size:].astype(jnp.float32)).astype(jnp.bfloat16), high)
-        last_b = flip((part(7, 8) + from_high[size:].astype(jnp.float32)).astype(jnp.bfloat16), low)
-        kept = jnp.concatenate([from_low[:size], from_high[:size]], axis=0).astype(jnp.float32)
-        last = jnp.concatenate([last_a, last_b], axis=0).astype(jnp.float32)
-        return part(0, 2) + kept + last
-
-    product = scatter(grad_rows, q, x_bit, y_bit)
-    hidden_grad = scatter(hidden_grad_rows, t, z_bit, w_bit)
-    return product, hidden_grad
+        from_low, from_high = flip(low_part, low), flip(high_part, high)
+        own_part, a_part, b_part = product(
+            share,
+            pieces,
+            layout(depth),
+            [(0, 2 * size, keep), (6 * size, 7 * size, keep), (7 * size, 8 * size, keep)],
+            over_rows,
+            tile,
+        )
+        last_a = flip((a_part + from_low[size:].astype(keep)).astype(send), high)
+        last_b = flip((b_part + from_high[size:].astype(keep)).astype(send), low)
+        kept = own_part + jnp.concatenate([from_low[:size], from_high[:size]], axis=0).astype(keep)
+        return kept + jnp.concatenate([last_a, last_b], axis=0).astype(keep), low_part
+
+    grad, sent = scatter([hidden, message1, message2, hidden3a, hidden3b], t, q, x_bit, y_bit, True)
+    weight3a, weight3b, _ = lax.optimization_barrier((weight3a, weight3b, sent))
+    hidden_grad, _ = scatter([down_weight, weight1, weight2, weight3a, weight3b], q, t, z_bit, w_bit, False)
+    return grad, hidden_grad
 
 
 def local(out_grad, gate_pre, up_pre, down_weight, row_moment, col_moment):
@@ -206,7 +265,7 @@
     rows, units = down_weight.shape
     tokens = out_grad.shape[0]
     all_bits = [1 << b for b in range(size.bit_length() - 1)]
-    staged = size == 16 and lax.axis_size("mp") == 2 and rows % 256 == 0 and tokens % 32 == 0 and units % 128 == 0
+    staged = size == 16 and lax.axis_size("mp") == 2 and rows % 256 == 0 and tokens % 32 == 0 and units % 512 == 0
     if staged:
         product, hidden_grad = staged_products(out_grad, gate_pre, up_pre, down_weight)
     else:
@@ -214,9 +273,8 @@
             out_grad, gate_pre, up_pre, down_weight, all_bits[:INNER_BITS], all_bits[INNER_BITS:]
         )
 
-    gate_late, up_late, hidden_grad = lax.optimization_barrier((gate_pre, up_pre, hidden_grad))
-    activated, derivative = gelu_parts(gate_late.astype(jnp.float32))
-    gate_grad = (hidden_grad * up_late.astype(jnp.float32) * derivative).astype(jnp.bfloat16)
+    activated, derivative = gelu_parts(gate_pre.astype(jnp.float32))
+    gate_grad = (hidden_grad * up_pre.astype(jnp.float32) * derivative).astype(jnp.bfloat16)
     up_grad = (hidden_grad * activated).astype(jnp.bfloat16)
 
     grad = product * (1.0 / math.sqrt(tokens * size))

time: 178 us -> 162 us (0.910)
  matrix products: 24.8 us -> 0 us
  Pallas kernels: 1.29 us -> 16.7 us
  local copies, waits for them, and re-layouts: 23.8 us -> 8.78 us
  waiting for transfers between devices: 75.5 us -> 88.8 us
  starting transfers between devices: 31.1 us -> 26.2 us
    dot_general x10 -> x0, matrix products: 24.8 us -> none  [the longest x5 19.2 us: hidden_grad_rows(): jnp.dot(share[begin * t:end * t], weight_all, preferred_element_type=jnp....]
    pallas_call x0 -> x6, Pallas kernels: none -> 15.4 us  [the longest x4 14.9 us: product(): pl.pallas_call(kernel, grid=(units // tile,), out_shape=[jax.ShapeDtypeSt...]
    ppermute x24 -> x22, waiting for transfers between devices: 75.5 us -> 88.8 us  [flip(): return lax.ppermute(value, axis, [(i, i ^ bits) for i in range(size)])]
    unnamed x48 -> x49, local copies, waits for them, and re-layouts: 17 us -> 7.44 us
    ppermute x24 -> x22, starting transfers between devices: 31.1 us -> 26.2 us  [flip(): return lax.ppermute(value, axis, [(i, i ^ bits) for i in range(size)])]
    slice x5 -> x0, local copies, waits for them, and re-layouts: 3.48 us -> none  [the longest x1 1.96 us: staged_products(): weight3b = flip(weight2[q:], x_bit)]
    concatenate x2 -> x0, local copies, waits for them, and re-layouts: 2.01 us -> none  [the longest x1 1.99 us: staged_products(): jnp.concatenate([down_weight, weight1[:q], weight3a, weight2[q:], weight3...]
    convert_element_type x0 -> x4, other arithmetic: none -> 1.85 us  [the longest x2 0.96 us: scatter(): last_a = flip((a_part + from_low[size:].astype(keep)).astype(send), high)]
  transfers between devices with their start and end apart: 24 -> 22, of which waited for: 9 -> 12; matrix products, arithmetic and copies ran while one was open for 24% -> 6% of each run, Pallas kernels for 1% -> 7%
where the time goes in v5:
time: 162 us; the launch traced here: 161 us
  waiting for transfers between devices  88.8 us (55%)
  starting transfers between devices  26.2 us (16%)
  Pallas kernels  16.7 us (10%)
  other arithmetic  11.7 us (7%)
  local copies, waits for them, and re-layouts  8.78 us (5%)
  blocking collectives  5.56 us (3%)
  between operations  3.4 us (2%)
    ppermute x22, waiting for transfers between devices, flip(): return lax.ppermute(value, axis, [(i, i ^ bits) for i in range(size)])  88.8 us
    ppermute x22, starting transfers between devices, flip(): return lax.ppermute(value, axis, [(i, i ^ bits) for i in range(size)])  26.2 us
    pallas_call x4, Pallas kernels, product(): pl.pallas_call(kernel, grid=(units // tile,), out_shape=[jax.ShapeDtypeSt...  14.9 us
    unnamed x49, local copies, waits for them, and re-layouts  7.44 us
    convert_element_type x1, other arithmetic, local(): up_grad = (hidden_grad * activated).astype(jnp.bfloat16)  3.36 us
  transfers between devices with their start and end apart: 22, of which 12 were waited for; matrix products, arithmetic and copies ran while one was open for 6% of the time, Pallas kernels for 7%

profile of v5, /device:TPU:0, one launch (start us, length us, event | category | flops | bytes accessed | tf_op | source)
XLA Modules:
  0.0 161.1 jit_solution(12994983836347641154)
XLA Ops:
  5.4 3.0 %collective-permute-start.4 = (bf16[256,2560]{1,0:T(8,128)(2,1)}, bf16[256,2560]{1,0:T(8,128)(2,1)S(1)}, u32[]{:S(2)}, u32[]{:S(2)}) collective-permute-start(bf16[256,2560]{1,0:T(8,128)(2,1)} %refs_1_.1), channel_id=1, source_target_pairs={{0,4},{2,6},{4,0},{6,2},{8,12},{10,14},{12,8},{14,10},{16,20},{18,... | collective-permute-start | bytes 3932168 | tf_op jit(solution)/shard_map/ppermute | solution.py:28
  10.0 1.6 collective-permute-start
  11.5 2.6 %collective-permute-start.1 = (bf16[128,3072]{1,0:T(8,128)(2,1)S(1)}, bf16[128,3072]{1,0:T(8,128)(2,1)S(1)}, u32[]{:S(2)}, u32[]{:S(2)}) collective-permute-start(bf16[128,3072]{1,0:T(8,128)(2,1)S(1)} %get-tuple-element.37), channel_id=1, source_target_pairs={{0,16},{2,18},{4,20},{6,22},{8,24},{10,26},{12,28},{14,30},{16,0},... | collective-permute-start | bytes 2359304 | tf_op jit(solution)/shard_map/ppermute | solution.py:28
  14.4 36.1 %collective-permute-done.2 = bf16[128,512]{1,0:T(8,128)(2,1)S(1)} collective-permute-done((bf16[128,512]{1,0:T(8,128)(2,1)S(1)}, bf16[128,512]{1,0:T(8,128)(2,1)S(1)}, u32[]{:S(2)}, u32[]{:S(2)}) %collective-permute-start.2) | collective-permute-done | bytes 131104 | tf_op jit(solution)/shard_map/ppermute | solution.py:28
  57.0 3.1 %collective-permute-start.6 = (bf16[64,2560]{1,0:T(8,128)(2,1)}, bf16[64,2560]{1,0:T(8,128)(2,1)S(1)}, u32[]{:S(2)}, u32[]{:S(2)}) collective-permute-start(bf16[64,2560]{1,0:T(8,128)(2,1)} %copy-done.15), channel_id=1, source_target_pairs={{0,16},{2,18},{4,20},{6,22},{8,24},{10,26},{12,28},{14,30},{16,0},... | collective-permute-start | bytes 983048 | tf_op jit(solution)/shard_map/ppermute | solution.py:28
  62.9 12.9 %collective-permute-done.6.refs_4_ = bf16[64,2560]{1,0:T(8,128)(2,1)S(1)} collective-permute-done((bf16[64,2560]{1,0:T(8,128)(2,1)}, bf16[64,2560]{1,0:T(8,128)(2,1)S(1)}, u32[]{:S(2)}, u32[]{:S(2)}) %collective-permute-start.6) | collective-permute-done | bytes 327712 | tf_op jit(solution)/shard_map/ppermute | solution.py:28
  76.0 2.7 %shard_map.112 = (bf16[256,2560]{1,0:T(8,128)(2,1)S(1)}, bf16[256,2560]{1,0:T(8,128)(2,1)S(1)}) custom-call(bf16[512,1024]{1,0:T(8,128)(2,1)S(1)} %fusion.18.refs_0_, bf16[128,2560]{1,0:T(8,128)(2,1)S(1)} %copy-done.13, bf16[128,3072]{1,0:T(8,128)(2,1)S(1)} %collective-permute-done.refs_0_.refs_2_, bf16[128,3072]{1,0:T(8,128)(2,1)S(1)} %copy-done.8, ...), custom_call_target="tpu_custom_call" | custom-call | flops 1342177280 | bytes 8912896 | tf_op jit(solution)/shard_map/pallas_call | solution.py:185
  78.7 4.3 %shard_map.115 = (bf16[128,2560]{1,0:T(8,128)(2,1)S(1)}, bf16[128,2560]{1,0:T(8,128)(2,1)S(1)}) custom-call(bf16[512,1024]{1,0:T(8,128)(2,1)S(1)} %fusion.18.refs_0_, bf16[256,2560]{1,0:T(8,128)(2,1)} %refs_1_.1, bf16[256,2560]{1,0:T(8,128)(2,1)S(1)} %collective-permute-done.3.refs_0_.refs_2_, bf16[256,2560]{1,0:T(8,128)(2,1)S(1)} %collective-permute-done.4.refs_1_.refs_3_, ...), custom_call_target="tpu_custom_call" | custom-call | flops 1342177280 | bytes 8912896 | tf_op jit(solution)/shard_map/pallas_call | solution.py:185
  83.0 1.6 collective-permute-start.18
  85.8 2.9 %shard_map.111 = (f32[256,2560]{1,0:T(8,128)S(1)}, f32[128,2560]{1,0:T(8,128)S(1)}, f32[128,2560]{1,0:T(8,128)S(1)}) custom-call(bf16[512,1024]{1,0:T(8,128)(2,1)S(1)} %fusion.18.refs_0_, bf16[128,2560]{1,0:T(8,128)(2,1)S(1)} %copy-done.13, bf16[128,3072]{1,0:T(8,128)(2,1)S(1)} %collective-permute-done.refs_0_.refs_2_, bf16[128,3072]{1,0:T(8,128)(2,1)S(1)} %copy-done.8, ...), custom_call_target="tpu_custom_call" | custom-call | flops 1342177280 | bytes 8912896 | tf_op jit(solution)/shard_map/pallas_call | solution.py:185
  89.5 4.9 %shard_map.114 = (f32[128,2560]{1,0:T(8,128)S(1)}, f32[64,2560]{1,0:T(8,128)S(1)}, f32[64,2560]{1,0:T(8,128)S(1)}) custom-call(bf16[512,1024]{1,0:T(8,128)(2,1)S(1)} %fusion.18.refs_0_, bf16[256,2560]{1,0:T(8,128)(2,1)} %refs_1_.1, bf16[256,2560]{1,0:T(8,128)(2,1)S(1)} %collective-permute-done.3.refs_0_.refs_2_, ...), custom_call_target="tpu_custom_call" | custom-call | flops 1342177280 | bytes 8912896 | tf_op jit(solution)/shard_map/pallas_call | solution.py:185
  94.4 14.3 %collective-permute-done.18 = bf16[128,2560]{1,0:T(8,128)(2,1)S(1)} collective-permute-done((bf16[128,2560]{1,0:T(8,128)(2,1)S(1)}, bf16[128,2560]{1,0:T(8,128)(2,1)S(1)}, u32[]{:S(2)}, u32[]{:S(2)}) %collective-permute-start.18) | collective-permute-done | bytes 655392 | tf_op jit(solution)/shard_map/ppermute | solution.py:28
  110.6 4.1 %collective-permute-done.9 = bf16[256,2560]{1,0:T(8,128)(2,1)S(1)} collective-permute-done((bf16[256,2560]{1,0:T(8,128)(2,1)S(1)}, bf16[256,2560]{1,0:T(8,128)(2,1)S(1)}, u32[]{:S(2)}, u32[]{:S(2)}) %collective-permute-start.9) | collective-permute-done | bytes 1310752 | tf_op jit(solution)/shard_map/ppermute | solution.py:28
  116.7 11.9 %collective-permute-done.19 = bf16[128,2560]{1,0:T(8,128)(2,1)S(1)} collective-permute-done((bf16[128,2560]{1,0:T(8,128)(2,1)S(1)}, bf16[128,2560]{1,0:T(8,128)(2,1)S(1)}, u32[]{:S(2)}, u32[]{:S(2)}) %collective-permute-start.19) | collective-permute-done | bytes 655392 | tf_op jit(solution)/shard_map/ppermute | solution.py:28
  131.3 2.5 %psum.14 = f32[256]{0:T(256)S(1)} all-reduce(f32[256]{0:T(256)S(1)} %get-tuple-element.68), channel_id=1, replica_groups=mesh['dp'=16,'mp'=2] {'mp'}, use_global_device_ids=true, to_apply=%region_2.3 | all-reduce | flops 256 | bytes 2048 | tf_op jit(solution)/shard_map/psum | solution.py:286
  135.8 1.6 collective-permute-start.12
  137.3 2.3 %collective-permute-done.12 = f32[5248]{0:T(1024)S(1)} collective-permute-done((f32[5248]{0:T(1024)S(1)}, f32[5248]{0:T(1024)S(1)}, u32[]{:S(2)}, u32[]{:S(2)}) %collective-permute-start.12) | collective-permute-done | bytes 21024 | tf_op jit(solution)/shard_map/ppermute | solution.py:28
  141.0 2.6 %collective-permute-done.13 = f32[5248]{0:T(1024)S(1)} collective-permute-done((f32[5248]{0:T(1024)S(1)}, f32[5248]{0:T(1024)S(1)}, u32[]{:S(2)}, u32[]{:S(2)}) %collective-permute-start.13) | collective-permute-done | bytes 21024 | tf_op jit(solution)/shard_map/ppermute | solution.py:28
  143.6 2.0 %collective-permute-start.14 = (f32[5248]{0:T(1024)S(1)}, f32[5248]{0:T(1024)S(1)}, u32[]{:S(2)}, u32[]{:S(2)}) collective-permute-start(f32[5248]{0:T(1024)S(1)} %add.73), channel_id=1, source_target_pairs={{0,8},{2,10},{4,12},{6,14},{8,0},{10,2},{12,4},{14,6},{16,24},{18,... | collective-permute-start | bytes 62984 | tf_op jit(solution)/shard_map/ppermute | solution.py:28
  145.6 1.8 %collective-permute-done.14 = f32[5248]{0:T(1024)S(1)} collective-permute-done((f32[5248]{0:T(1024)S(1)}, f32[5248]{0:T(1024)S(1)}, u32[]{:S(2)}, u32[]{:S(2)}) %collective-permute-start.14) | collective-permute-done | bytes 21024 | tf_op jit(solution)/shard_map/ppermute | solution.py:28
  147.4 1.9 %collective-permute-start.15 = (f32[5248]{0:T(1024)S(1)}, f32[5248]{0:T(1024)S(1)}, u32[]{:S(2)}, u32[]{:S(2)}) collective-permute-start(f32[5248]{0:T(1024)S(1)} %add.74), channel_id=1, source_target_pairs={{0,16},{2,18},{4,20},{6,22},{8,24},{10,26},{12,28},{14,30},{16,0},... | collective-permute-start | bytes 62984 | tf_op jit(solution)/shard_map/ppermute | solution.py:28
  149.3 3.4 %fusion.8 = (bf16[128,2560]{1,0:T(8,128)(2,1)}, bf16[128,2560]{1,0:T(8,128)(2,1)}) fusion(bf16[128,2560]{1,0:T(8,128)(2,1)S(1)} %copy-done.1, bf16[64,2560]{1,0:T(8,128)(2,1)} %collective-permute-done.21, bf16[64,2560]{1,0:T(8,128)(2,1)} %collective-permute-done.20, f32[128,2560]{1,0:T(8,128)S(1)} %copy-done.5, bf16[64,2560]{1,0:T(8,128)(2,1)S(1)} %slice.100, ...), kind=kLoop, calls=%fused_computation.21 | loop fusion | flops 11468800 | bytes 5242880 | tf_op jit(solution)/shard_map/convert_element_type | solution.py:278
  153.8 3.1 %psum.15 = f32[]{:T(128)} all-reduce(f32[]{:T(128)} %get-tuple-element.64), channel_id=1, replica_groups=mesh['dp'=16,'mp'=2] {'mp'}, use_global_device_ids=true, to_apply=%region_6.7 | all-reduce | flops 1 | bytes 8 | tf_op jit(solution)/shard_map/psum | solution.py:294
  158.2 1.8 %multiply_multiply_fusion = f32[256,2560]{1,0:T(8,128)} fusion(f32[256,2560]{1,0:T(8,128)S(1)} %get-tuple-element.69, f32[2560]{0:T(1024)S(1)} %sqrt.11, f32[256]{0:T(256)S(1)} %divide_multiply_fusion), kind=kLoop, calls=%fused_computation.7 | loop fusion | flops 1310720 | bytes 5254144 | tf_op jit(solution)/shard_map/mul | solution.py:298
  (112 shorter events, 29.0 us)
Async XLA Ops:
  5.4 50.5 %copy-start.11 = (bf16[128,1024]{1,0:T(8,128)(2,1)}, bf16[128,1024]{1,0:T(8,128)(2,1)S(1)}, u32[]{:S(2)}) copy-start(bf16[128,1024]{1,0:T(8,128)(2,1)S(1)} %get-tuple-element.34) | copy-start | bytes 786436
  5.4 50.5 %copy-start.12 = (bf16[128,2560]{1,0:T(8,128)(2,1)}, bf16[128,2560]{1,0:T(8,128)(2,1)S(1)}, u32[]{:S(2)}) copy-start(bf16[128,2560]{1,0:T(8,128)(2,1)S(1)} %get-tuple-element.45.refs_1_) | copy-start | bytes 1966084
  5.4 46.6 %collective-permute-start.4 = (bf16[256,2560]{1,0:T(8,128)(2,1)}, bf16[256,2560]{1,0:T(8,128)(2,1)S(1)}, u32[]{:S(2)}, u32[]{:S(2)}) collective-permute-start(bf16[256,2560]{1,0:T(8,128)(2,1)} %refs_1_.1), channel_id=1, source_target_pairs={{0,4},{2,6},{4,0},{6,2},{8,12},{10,14},{12,8},{14,10},{16,20},{18,... | collective-permute-start | bytes 3932168 | tf_op jit(solution)/shard_map/ppermute | solution.py:28
  8.5 43.5 %collective-permute-start.3 = (bf16[256,2560]{1,0:T(8,128)(2,1)}, bf16[256,2560]{1,0:T(8,128)(2,1)S(1)}, u32[]{:S(2)}, u32[]{:S(2)}) collective-permute-start(bf16[256,2560]{1,0:T(8,128)(2,1)} %refs_1_.1), channel_id=1, source_target_pairs={{0,2},{2,0},{4,6},{6,4},{8,10},{10,8},{12,14},{14,12},{16,18},{18,... | collective-permute-start | bytes 3932168 | tf_op jit(solution)/shard_map/ppermute | solution.py:28
  10.0 40.5 %collective-permute-start = (bf16[128,3072]{1,0:T(8,128)(2,1)S(1)}, bf16[128,3072]{1,0:T(8,128)(2,1)S(1)}, u32[]{:S(2)}, u32[]{:S(2)}) collective-permute-start(bf16[128,3072]{1,0:T(8,128)(2,1)S(1)} %get-tuple-element.36), channel_id=1, source_target_pairs={{0,8},{2,10},{4,12},{6,14},{8,0},{10,2},{12,4},{14,6},{16,24},{18,... | collective-permute-start | bytes 2359304 | tf_op jit(solution)/shard_map/ppermute | solution.py:28
  11.5 40.5 %collective-permute-start.1 = (bf16[128,3072]{1,0:T(8,128)(2,1)S(1)}, bf16[128,3072]{1,0:T(8,128)(2,1)S(1)}, u32[]{:S(2)}, u32[]{:S(2)}) collective-permute-start(bf16[128,3072]{1,0:T(8,128)(2,1)S(1)} %get-tuple-element.37), channel_id=1, source_target_pairs={{0,16},{2,18},{4,20},{6,22},{8,24},{10,26},{12,28},{14,30},{16,0},... | collective-permute-start | bytes 2359304 | tf_op jit(solution)/shard_map/ppermute | solution.py:28
  14.1 36.3 %collective-permute-start.2 = (bf16[128,512]{1,0:T(8,128)(2,1)S(1)}, bf16[128,512]{1,0:T(8,128)(2,1)S(1)}, u32[]{:S(2)}, u32[]{:S(2)}) collective-permute-start(bf16[128,512]{1,0:T(8,128)(2,1)S(1)} %get-tuple-element.38), channel_id=1, source_target_pairs={{0,24},{2,26},{4,28},{6,30},{8,16},{10,18},{12,20},{14,22},{16,8},... | collective-permute-start | bytes 393224 | tf_op jit(solution)/shard_map/ppermute | solution.py:28
  55.9 5.7 %collective-permute-start.5 = (bf16[128,1536]{1,0:T(8,128)(2,1)}, bf16[128,1536]{1,0:T(8,128)(2,1)}, u32[]{:S(2)}, u32[]{:S(2)}) collective-permute-start(bf16[128,1536]{1,0:T(8,128)(2,1)} %pad_maximum_fusion), channel_id=1, source_target_pairs={{0,1},{1,0},{2,3},{3,2},{4,5},{5,4},{6,7},{7,6},{8,9},{9,8},{10,11... | collective-permute-start | bytes 1179656 | tf_op jit(solution)/shard_map/ppermute | solution.py:28
  57.0 18.8 %collective-permute-start.6 = (bf16[64,2560]{1,0:T(8,128)(2,1)}, bf16[64,2560]{1,0:T(8,128)(2,1)S(1)}, u32[]{:S(2)}, u32[]{:S(2)}) collective-permute-start(bf16[64,2560]{1,0:T(8,128)(2,1)} %copy-done.15), channel_id=1, source_target_pairs={{0,16},{2,18},{4,20},{6,22},{8,24},{10,26},{12,28},{14,30},{16,0},... | collective-permute-start | bytes 983048 | tf_op jit(solution)/shard_map/ppermute | solution.py:28
  60.1 15.9 %collective-permute-start.7 = (bf16[64,2560]{1,0:T(8,128)(2,1)}, bf16[64,2560]{1,0:T(8,128)(2,1)S(1)}, u32[]{:S(2)}, u32[]{:S(2)}) collective-permute-start(bf16[64,2560]{1,0:T(8,128)(2,1)} %copy-done.14), channel_id=1, source_target_pairs={{0,8},{2,10},{4,12},{6,14},{8,0},{10,2},{12,4},{14,6},{16,24},{18,... | collective-permute-start | bytes 983048 | tf_op jit(solution)/shard_map/ppermute | solution.py:28
  60.5 18.2 %collective-permute-start.16 = (bf16[128,2560]{1,0:T(8,128)(2,1)S(1)}, bf16[128,2560]{1,0:T(8,128)(2,1)S(1)}, u32[]{:S(2)}, u32[]{:S(2)}) collective-permute-start(bf16[128,2560]{1,0:T(8,128)(2,1)S(1)} %get-tuple-element.53), channel_id=1, source_target_pairs={{0,4},{2,6},{4,0},{6,2},{8,12},{10,14},{12,8},{14,10},{16,20},{18,... | collective-permute-start | bytes 1966088 | tf_op jit(solution)/shard_map/ppermute | solution.py:28
  61.1 17.6 %collective-permute-start.17 = (bf16[128,2560]{1,0:T(8,128)(2,1)S(1)}, bf16[128,2560]{1,0:T(8,128)(2,1)S(1)}, u32[]{:S(2)}, u32[]{:S(2)}) collective-permute-start(bf16[128,2560]{1,0:T(8,128)(2,1)S(1)} %get-tuple-element.54), channel_id=1, source_target_pairs={{0,2},{2,0},{4,6},{6,4},{8,10},{10,8},{12,14},{14,12},{16,18},{18,... | collective-permute-start | bytes 1966088 | tf_op jit(solution)/shard_map/ppermute | solution.py:28
  83.0 25.7 %collective-permute-start.18 = (bf16[128,2560]{1,0:T(8,128)(2,1)S(1)}, bf16[128,2560]{1,0:T(8,128)(2,1)S(1)}, u32[]{:S(2)}, u32[]{:S(2)}) collective-permute-start(bf16[128,2560]{1,0:T(8,128)(2,1)S(1)} %get-tuple-element.58), channel_id=1, source_target_pairs={{0,8},{2,10},{4,12},{6,14},{8,0},{10,2},{12,4},{14,6},{16,24},{18,... | collective-permute-start | bytes 1966088 | tf_op jit(solution)/shard_map/ppermute | solution.py:28
  84.6 30.1 %collective-permute-start.9 = (bf16[256,2560]{1,0:T(8,128)(2,1)S(1)}, bf16[256,2560]{1,0:T(8,128)(2,1)S(1)}, u32[]{:S(2)}, u32[]{:S(2)}) collective-permute-start(bf16[256,2560]{1,0:T(8,128)(2,1)S(1)} %get-tuple-element.50), channel_id=1, source_target_pairs={{0,4},{2,6},{4,0},{6,2},{8,12},{10,14},{12,8},{14,10},{16,20},{18,... | collective-permute-start | bytes 3932168 | tf_op jit(solution)/shard_map/ppermute | solution.py:28
  85.3 30.2 %collective-permute-start.8 = (bf16[256,2560]{1,0:T(8,128)(2,1)S(1)}, bf16[256,2560]{1,0:T(8,128)(2,1)S(1)}, u32[]{:S(2)}, u32[]{:S(2)}) collective-permute-start(bf16[256,2560]{1,0:T(8,128)(2,1)S(1)} %get-tuple-element.49), channel_id=1, source_target_pairs={{0,2},{2,0},{4,6},{6,4},{8,10},{10,8},{12,14},{14,12},{16,18},{18,... | collective-permute-start | bytes 3932168 | tf_op jit(solution)/shard_map/ppermute | solution.py:28
  88.7 39.8 %collective-permute-start.19 = (bf16[128,2560]{1,0:T(8,128)(2,1)S(1)}, bf16[128,2560]{1,0:T(8,128)(2,1)S(1)}, u32[]{:S(2)}, u32[]{:S(2)}) collective-permute-start(bf16[128,2560]{1,0:T(8,128)(2,1)S(1)} %get-tuple-element.59), channel_id=1, source_target_pairs={{0,16},{2,18},{4,20},{6,22},{8,24},{10,26},{12,28},{14,30},{16,0},... | collective-permute-start | bytes 1966088 | tf_op jit(solution)/shard_map/ppermute | solution.py:28
  109.6 39.7 %collective-permute-start.20 = (bf16[64,2560]{1,0:T(8,128)(2,1)}, bf16[64,2560]{1,0:T(8,128)(2,1)}, u32[]{:S(2)}, u32[]{:S(2)}) collective-permute-start(bf16[64,2560]{1,0:T(8,128)(2,1)} %add_convert_fusion.3), channel_id=1, source_target_pairs={{0,16},{2,18},{4,20},{6,22},{8,24},{10,26},{12,28},{14,30},{16,0},... | collective-permute-start | bytes 983048 | tf_op jit(solution)/shard_map/ppermute | solution.py:28
  114.8 15.2 %collective-permute-start.11 = (bf16[128,2560]{1,0:T(8,128)(2,1)S(1)}, bf16[128,2560]{1,0:T(8,128)(2,1)S(1)}, u32[]{:S(2)}, u32[]{:S(2)}) collective-permute-start(bf16[128,2560]{1,0:T(8,128)(2,1)S(1)} %add_convert_fusion), channel_id=1, source_target_pairs={{0,2},{2,0},{4,6},{6,4},{8,10},{10,8},{12,14},{14,12},{16,18},{18,... | collective-permute-start | bytes 1966088 | tf_op jit(solution)/shard_map/ppermute | solution.py:28
  115.5 14.9 %collective-permute-start.10 = (bf16[128,2560]{1,0:T(8,128)(2,1)S(1)}, bf16[128,2560]{1,0:T(8,128)(2,1)S(1)}, u32[]{:S(2)}, u32[]{:S(2)}) collective-permute-start(bf16[128,2560]{1,0:T(8,128)(2,1)S(1)} %add_convert_fusion.1), channel_id=1, source_target_pairs={{0,4},{2,6},{4,0},{6,2},{8,12},{10,14},{12,8},{14,10},{16,20},{18,... | collective-permute-start | bytes 1966088 | tf_op jit(solution)/shard_map/ppermute | solution.py:28
  129.3 19.9 %collective-permute-start.21 = (bf16[64,2560]{1,0:T(8,128)(2,1)}, bf16[64,2560]{1,0:T(8,128)(2,1)}, u32[]{:S(2)}, u32[]{:S(2)}) collective-permute-start(bf16[64,2560]{1,0:T(8,128)(2,1)} %add_convert_fusion.2), channel_id=1, source_target_pairs={{0,8},{2,10},{4,12},{6,14},{8,0},{10,2},{12,4},{14,6},{16,24},{18,... | collective-permute-start | bytes 983048 | tf_op jit(solution)/shard_map/ppermute | solution.py:28
  135.8 3.9 %collective-permute-start.12 = (f32[5248]{0:T(1024)S(1)}, f32[5248]{0:T(1024)S(1)}, u32[]{:S(2)}, u32[]{:S(2)}) collective-permute-start(f32[5248]{0:T(1024)S(1)} %pad_maximum_fusion.4), channel_id=1, source_target_pairs={{0,2},{2,0},{4,6},{6,4},{8,10},{10,8},{12,14},{14,12},{16,18},{18,... | collective-permute-start | bytes 62984 | tf_op jit(solution)/shard_map/ppermute | solution.py:28
  139.7 3.9 %collective-permute-start.13 = (f32[5248]{0:T(1024)S(1)}, f32[5248]{0:T(1024)S(1)}, u32[]{:S(2)}, u32[]{:S(2)}) collective-permute-start(f32[5248]{0:T(1024)S(1)} %fusion.23), channel_id=1, source_target_pairs={{0,4},{2,6},{4,0},{6,2},{8,12},{10,14},{12,8},{14,10},{16,20},{18,... | collective-permute-start | bytes 62984 | tf_op jit(solution)/shard_map/ppermute | solution.py:28
  143.6 3.8 %collective-permute-start.14 = (f32[5248]{0:T(1024)S(1)}, f32[5248]{0:T(1024)S(1)}, u32[]{:S(2)}, u32[]{:S(2)}) collective-permute-start(f32[5248]{0:T(1024)S(1)} %add.73), channel_id=1, source_target_pairs={{0,8},{2,10},{4,12},{6,14},{8,0},{10,2},{12,4},{14,6},{16,24},{18,... | collective-permute-start | bytes 62984 | tf_op jit(solution)/shard_map/ppermute | solution.py:28
  147.4 5.3 %collective-permute-start.15 = (f32[5248]{0:T(1024)S(1)}, f32[5248]{0:T(1024)S(1)}, u32[]{:S(2)}, u32[]{:S(2)}) collective-permute-start(f32[5248]{0:T(1024)S(1)} %add.74), channel_id=1, source_target_pairs={{0,16},{2,18},{4,20},{6,22},{8,24},{10,26},{12,28},{14,30},{16,0},... | collective-permute-start | bytes 62984 | tf_op jit(solution)/shard_map/ppermute | solution.py:28
  (24 other events, 179.2 us)

commit v6 on v5

--- a/solution.py
+++ b/solution.py
@@ -29,8 +29,10 @@
 
 
 def group_sum(value, bits):
+    size = lax.axis_size("dp")
     for bit in bits:
-        value = value + flip(value, bit)
+        pairs = [[i, i | bit] for i in range(size) if not i & bit]
+        value = lax.psum(value, "dp", axis_index_groups=pairs)
     return value
 
 
@@ -91,20 +93,21 @@
     share_width = 4 * rows
     step = 32
 
-    def kernel(place, source, gate, up, own, hidden, message1, message2, message3):
+    def kernel(place, source_hbm, gate_hbm, up_hbm, own, hidden, message1, message2, message3, source, gate, up, sems):
+        copies = [
+            pltpu.make_async_copy(there, here, sems.at[n])
+            for n, (there, here) in enumerate(((gate_hbm, gate), (up_hbm, up), (source_hbm, source)))
+        ]
+        for copy in copies:
+            copy.start()
         me, core = place[0], place[1]
 
         def column(k, block, half):
             at = (me ^ (4 * k + block)) * rows + half * quarter
             return pl.ds(pl.multiple_of(at, quarter), quarter)
 
-        for p, (block, half) in enumerate(PIECES):
-            own[:, p * quarter : (p + 1) * quarter] = source[:, column(0, block, half)]
-        for k, target, base in ((1, message1, units), (2, message2, units), (3, message3, 0)):
-            for p in range(4):
-                block = jnp.where(core == 0, PIECES[p][0], PIECES[p + 4][0])
-                half = jnp.where(core == 0, PIECES[p][1], PIECES[p + 4][1])
-                target[:, base + p * quarter : base + (p + 1) * quarter] = source[:, column(k, block, half)]
+        copies[0].wait()
+        copies[1].wait()
 
         @pl.loop(0, tokens // step)
         def _(i):
@@ -114,6 +117,15 @@
             hidden[here, :] = value
             message1[here, :units] = value
             message2[here, :units] = value
+
+        copies[2].wait()
+        for p, (block, half) in enumerate(PIECES):
+            own[:, p * quarter : (p + 1) * quarter] = source[:, column(0, block, half)]
+        for k, target, base in ((1, message1, units), (2, message2, units), (3, message3, 0)):
+            for p in range(4):
+                block = jnp.where(core == 0, PIECES[p][0], PIECES[p + 4][0])
+                half = jnp.where(core == 0, PIECES[p][1], PIECES[p + 4][1])
+                target[:, base + p * quarter : base + (p + 1) * quarter] = source[:, column(k, block, half)]
 
     wide = jax.ShapeDtypeStruct((tokens, units + share_width // 2), jnp.bfloat16)
     vmem = pl.BlockSpec(memory_space=pltpu.VMEM)
@@ -126,37 +138,44 @@
             wide,
             jax.ShapeDtypeStruct((tokens, share_width // 2), jnp.bfloat16),
         ],
-        in_specs=[pl.BlockSpec(memory_space=pltpu.SMEM), vmem, vmem, vmem],
+        in_specs=[pl.BlockSpec(memory_space=pltpu.SMEM)] + [pl.BlockSpec(memory_space=pltpu.HBM)] * 3,
         out_specs=[vmem] * 5,
-        compiler_params=pltpu.CompilerParams(vmem_limit_bytes=24 << 20),
+        scratch_shapes=[
+            pltpu.VMEM(out_grad.shape, jnp.bfloat16),
+            pltpu.VMEM(gate_pre.shape, jnp.bfloat16),
+            pltpu.VMEM(up_pre.shape, jnp.bfloat16),
+            pltpu.SemaphoreType.DMA((3,)),
+        ],
+        compiler_params=pltpu.CompilerParams(vmem_limit_bytes=16 << 20),
         cost_estimate=pl.CostEstimate(
             flops=20 * tokens * units, bytes_accessed=16 * tokens * units, transcendentals=tokens * units
         ),
     )(place, out_grad, gate_pre, up_pre)
 
 
-def cut(sources, parts):
+def cut(sources, parts, shapes):
     def kernel(*refs):
         ins, outs, sems = refs[: len(sources)], refs[len(sources) : -1], refs[-1]
         copies = [
-            pltpu.make_async_copy(ins[i].at[pl.ds(*rows), pl.ds(*columns)], outs[n], sems.at[n])
-            for n, (i, rows, columns) in enumerate(parts)
+            pltpu.make_async_copy(
+                ins[i].at[pl.ds(*rows), pl.ds(*columns)], outs[o].at[:, pl.ds(at, columns[1])], sems.at[n]
+            )
+            for n, (i, rows, columns, o, at) in enumerate(parts)
         ]
         for copy in copies:
             copy.start()
         for copy in copies:
             copy.wait()
 
-    shapes = [jax.ShapeDtypeStruct((rows[1], columns[1]), sources[i].dtype) for i, rows, columns in parts]
     return pl.pallas_call(
         kernel,
-        out_shape=shapes,
-        in_specs=[pl.BlockSpec(memory_space=pl.ANY)] * len(sources),
-        out_specs=[pl.BlockSpec(memory_space=pl.ANY)] * len(parts),
+        out_shape=[jax.ShapeDtypeStruct(shape, jnp.bfloat16) for shape in shapes],
+        in_specs=[pl.BlockSpec(memory_space=pltpu.HBM)] * len(sources),
+        out_specs=[pl.BlockSpec(memory_space=pltpu.HBM)] * len(shapes),
         scratch_shapes=[pltpu.SemaphoreType.DMA((len(parts),))],
         compiler_params=pltpu.CompilerParams(vmem_limit_bytes=4 << 20),
         cost_estimate=pl.CostEstimate(
-            flops=0, bytes_accessed=sum(4 * r[1] * c[1] for _, r, c in parts), transcendentals=0
+            flops=0, bytes_accessed=sum(4 * math.prod(shape) for shape in shapes), transcendentals=0
         ),
     )(*sources)
 
@@ -211,18 +230,25 @@
     down_weight, message1 = lax.optimization_barrier((down_weight, message1))
     message1, message2, message3 = flip(message1, z_bit), flip(message2, w_bit), flip(message3, z_bit | w_bit)
     weight1, weight2 = flip(down_weight, x_bit), flip(down_weight, y_bit)
-    whole, top, bottom = (0, units), (0, q), (q, q)
-    to_y, to_x = cut([weight1, weight2], [(0, top, whole), (1, bottom, whole)])
+    whole = (0, units)
+    to_y, to_x = cut([weight1, weight2], [(0, (0, q), whole, 0, 0), (1, (q, q), whole, 1, 0)], [(q, units)] * 2)
     weight3a, weight3b = flip(to_y, y_bit), flip(to_x, x_bit)
 
-    message1, message2, message3, _, _ = lax.optimization_barrier((message1, message2, message3, weight1, weight2))
-    extra = (units, 2 * rows)
-    to_w, to_z, mine1, mine2 = cut(
-        [message1, message2], [(0, (0, t), whole), (1, (t, t), whole), (0, (0, tokens), extra), (1, (0, tokens), extra)]
+    message1, message2, message3, _, _ = lax.optimization_barrier((message1, message2, message3, to_y, to_x))
+    extra, every = (units, 2 * rows), (0, tokens)
+    to_w, to_z, mine = cut(
+        [message1, message2, message3],
+        [
+            (0, (0, t), whole, 0, 0),
+            (1, (t, t), whole, 1, 0),
+            (0, every, extra, 2, 0),
+            (1, every, extra, 2, 2 * rows),
+            (2, every, (0, 2 * rows), 2, 4 * rows),
+        ],
+        [(t, units), (t, units), (tokens, 6 * rows)],
     )
+    theirs = flip(mine, 1, "mp")
     hidden3a, hidden3b = flip(to_w, w_bit), flip(to_z, z_bit)
-    mine = jnp.concatenate([mine1, mine2, message3], axis=1)
-    theirs = flip(mine, 1, "mp")
 
     def features(k):
         a, b = mine[:, (k - 1) * 2 * rows : k * 2 * rows], theirs[:, (k - 1) * 2 * rows : k * 2 * rows]
@@ -234,29 +260,36 @@
     def layout(size):
         return [(0, 0, 2 * size), (1, 0, size), (3, 0, size), (2, size, size), (4, 0, size), (2, 0, size), (1, size, size)]
 
-    def scatter(pieces, depth, size, low, high, over_rows):
-        tile = 512
+    def send_parts(pieces, depth, size, over_rows):
+        kind = jnp.bfloat16
+        return product(
+            share, pieces, layout(depth), [(2 * size, 4 * size, kind), (4 * size, 6 * size, kind)], over_rows, 512
+        )
+
+    def keep_parts(pieces, depth, size, over_rows):
+        kind = jnp.float32
+        bounds = [(0, 2 * size, kind), (6 * size, 7 * size, kind), (7 * size, 8 * size, kind)]
+        return product(share, pieces, layout(depth), bounds, over_rows, 512)
+
+    def finish(parts, from_low, from_high, size, low, high):
         send, keep = jnp.bfloat16, jnp.float32
-        low_part, high_part = product(
-            share, pieces, layout(depth), [(2 * size, 4 * size, send), (4 * size, 6 * size, send)], over_rows, tile
-        )
-        from_low, from_high = flip(low_part, low), flip(high_part, high)
-        own_part, a_part, b_part = product(
-            share,
-            pieces,
-            layout(depth),
-            [(0, 2 * size, keep), (6 * size, 7 * size, keep), (7 * size, 8 * size, keep)],
-            over_rows,
-            tile,
-        )
+        own_part, a_part, b_part = parts
         last_a = flip((a_part + from_low[size:].astype(keep)).astype(send), high)
         last_b = flip((b_part + from_high[size:].astype(keep)).astype(send), low)
         kept = own_part + jnp.concatenate([from_low[:size], from_high[:size]], axis=0).astype(keep)
-        return kept + jnp.concatenate([last_a, last_b], axis=0).astype(keep), low_part
-
-    grad, sent = scatter([hidden, message1, message2, hidden3a, hidden3b], t, q, x_bit, y_bit, True)
-    weight3a, weight3b, _ = lax.optimization_barrier((weight3a, weight3b, sent))
-    hidden_grad, _ = scatter([down_weight, weight1, weight2, weight3a, weight3b], q, t, z_bit, w_bit, False)
+        return kept + jnp.concatenate([last_a, last_b], axis=0).astype(keep)
+
+    weights = [down_weight, weight1, weight2, weight3a, weight3b]
+    to_z, to_w = send_parts(weights, q, t, False)
+    from_z, from_w = flip(to_z, z_bit), flip(to_w, w_bit)
+    hidden3a, hidden3b, _ = lax.optimization_barrier((hidden3a, hidden3b, to_z))
+    hiddens = [hidden, message1, message2, hidden3a, hidden3b]
+    to_x, to_y = send_parts(hiddens, t, q, True)
+    from_x, from_y = flip(to_x, x_bit), flip(to_y, y_bit)
+    share, weight3a, weight3b, _ = lax.optimization_barrier((share, weight3a, weight3b, to_x))
+    weights = [down_weight, weight1, weight2, weight3a, weight3b]
+    grad = finish(keep_parts(hiddens, t, q, True), from_x, from_y, q, x_bit, y_bit)
+    hidden_grad = finish(keep_parts(weights, q, t, False), from_z, from_w, t, z_bit, w_bit)
     return grad, hidden_grad
 
 
@@ -291,7 +324,8 @@
     sums = group_sum(jnp.concatenate([col_part, scaled_part, total_part]), all_bits)
     col_moment_new = decay * col_moment + (1.0 - decay) * (sums[:units] / total_rows)
     row_mean = sums[2 * units] / total_rows
-    square_sum = row_mean * lax.psum(jnp.sum(sums[units : 2 * units] / col_moment_new), "mp")
+    ratios = jnp.sum((sums[units : 2 * units] / col_moment_new).reshape(-1, 128), axis=0)
+    square_sum = row_mean * jnp.sum(lax.psum(ratios, "mp"))
     clip_norm = jnp.sqrt(square_sum / (total_rows * total_units))
     row_factor = jnp.sqrt(row_mean / row_moment_new) / jnp.maximum(1.0, clip_norm)
     col_factor = 1.0 / jnp.sqrt(col_moment_new)

time: 162 us -> 187 us (1.15)
  blocking collectives: 5.56 us -> 38.9 us
  starting transfers between devices: 26.2 us -> 21.6 us
  waiting for transfers between devices: 88.8 us -> 85 us
  other arithmetic: 11.7 us -> 8.46 us
  local copies, waits for them, and re-layouts: 8.78 us -> 10.8 us
    psum x1 -> x5, blocking collectives: 3.09 us -> 36.5 us  [the longest x4 34 us: group_sum(): value = lax.psum(value, 'dp', axis_index_groups=pairs)]
    ppermute x22 -> x18, starting transfers between devices: 26.2 us -> 21.6 us  [flip(): return lax.ppermute(value, axis, [(i, i ^ bits) for i in range(size)])]
    ppermute x22 -> x18, waiting for transfers between devices: 88.8 us -> 85 us  [flip(): return lax.ppermute(value, axis, [(i, i ^ bits) for i in range(size)])]
    unnamed x49 -> x43, local copies, waits for them, and re-layouts: 7.44 us -> 9.14 us
  transfers between devices with their start and end apart: 22 -> 18, of which waited for: 12 -> 11; matrix products, arithmetic and copies ran while one was open for 6% -> 3% of each run, Pallas kernels for 7% -> 8%
where the time goes in v6:
time: 187 us; the launch traced here: 186 us
  waiting for transfers between devices  85 us (45%)
  blocking collectives  38.9 us (21%)
  starting transfers between devices  21.6 us (12%)
  Pallas kernels  18 us (10%)
  local copies, waits for them, and re-layouts  10.8 us (6%)
  other arithmetic  8.46 us (5%)
  between operations  3.46 us (2%)
    ppermute x18, waiting for transfers between devices, flip(): return lax.ppermute(value, axis, [(i, i ^ bits) for i in range(size)])  85 us
    psum x4, blocking collectives, group_sum(): value = lax.psum(value, 'dp', axis_index_groups=pairs)  34 us
    ppermute x18, starting transfers between devices, flip(): return lax.ppermute(value, axis, [(i, i ^ bits) for i in range(size)])  21.6 us
    pallas_call x4, Pallas kernels, product(): pl.pallas_call(kernel, grid=(units // tile,), out_shape=[jax.ShapeDtypeSt...  14.9 us
    unnamed x43, local copies, waits for them, and re-layouts  9.14 us
  transfers between devices with their start and end apart: 18, of which 11 were waited for; matrix products, arithmetic and copies ran while one was open for 3% of the time, Pallas kernels for 8%

profile of v6, /device:TPU:0, one launch (start us, length us, event | category | flops | bytes accessed | tf_op | source)
XLA Modules:
  0.0 186.2 jit_solution(15443787462776033396)
XLA Ops:
  4.1 1.8 shard_map.109
  5.9 3.0 %collective-permute-start.3 = (bf16[256,2560]{1,0:T(8,128)(2,1)}, bf16[256,2560]{1,0:T(8,128)(2,1)S(1)}, u32[]{:S(2)}, u32[]{:S(2)}) collective-permute-start(bf16[256,2560]{1,0:T(8,128)(2,1)} %refs_1_.1), channel_id=1, source_target_pairs={{0,2},{2,0},{4,6},{6,4},{8,10},{10,8},{12,14},{14,12},{16,18},{18,... | collective-permute-start | bytes 3932168 | tf_op jit(solution)/shard_map/ppermute | solution.py:28
  12.0 2.6 %collective-permute-start.1 = (bf16[128,3072]{1,0:T(8,128)(2,1)S(1)}, bf16[128,3072]{1,0:T(8,128)(2,1)S(1)}, u32[]{:S(2)}, u32[]{:S(2)}) collective-permute-start(bf16[128,3072]{1,0:T(8,128)(2,1)S(1)} %get-tuple-element.39), channel_id=1, source_target_pairs={{0,16},{2,18},{4,20},{6,22},{8,24},{10,26},{12,28},{14,30},{16,0},... | collective-permute-start | bytes 2359304 | tf_op jit(solution)/shard_map/ppermute | solution.py:28
  14.9 23.1 %collective-permute-done.3.refs_0_.refs_2_ = bf16[256,2560]{1,0:T(8,128)(2,1)S(1)} collective-permute-done((bf16[256,2560]{1,0:T(8,128)(2,1)}, bf16[256,2560]{1,0:T(8,128)(2,1)S(1)}, u32[]{:S(2)}, u32[]{:S(2)}) %collective-permute-start.3) | collective-permute-done | bytes 1310752 | tf_op jit(solution)/shard_map/ppermute | solution.py:28
  41.6 9.4 %collective-permute-done.2.refs_2_ = bf16[128,512]{1,0:T(8,128)(2,1)S(1)} collective-permute-done((bf16[128,512]{1,0:T(8,128)(2,1)S(1)}, bf16[128,512]{1,0:T(8,128)(2,1)S(1)}, u32[]{:S(2)}, u32[]{:S(2)}) %collective-permute-start.2) | collective-permute-done | bytes 131104 | tf_op jit(solution)/shard_map/ppermute | solution.py:28
  57.8 3.0 %collective-permute-start.8 = (bf16[64,2560]{1,0:T(8,128)(2,1)}, bf16[64,2560]{1,0:T(8,128)(2,1)S(1)}, u32[]{:S(2)}, u32[]{:S(2)}) collective-permute-start(bf16[64,2560]{1,0:T(8,128)(2,1)} %copy-done.13), channel_id=1, source_target_pairs={{0,16},{2,18},{4,20},{6,22},{8,24},{10,26},{12,28},{14,30},{16,0},... | collective-permute-start | bytes 983048 | tf_op jit(solution)/shard_map/ppermute | solution.py:28
  62.3 11.9 %collective-permute-done.6.refs_4_ = bf16[128,2560]{1,0:T(8,128)(2,1)S(1)} collective-permute-done((bf16[128,2560]{1,0:T(8,128)(2,1)}, bf16[128,2560]{1,0:T(8,128)(2,1)S(1)}, u32[]{:S(2)}, u32[]{:S(2)}) %collective-permute-start.6) | collective-permute-done | bytes 655392 | tf_op jit(solution)/shard_map/ppermute | solution.py:28
  74.4 4.3 %shard_map.112 = (bf16[128,2560]{1,0:T(8,128)(2,1)S(1)}, bf16[128,2560]{1,0:T(8,128)(2,1)S(1)}) custom-call(bf16[512,1024]{1,0:T(8,128)(2,1)S(1)} %fusion.18.refs_0_, bf16[256,2560]{1,0:T(8,128)(2,1)} %refs_1_.1, bf16[256,2560]{1,0:T(8,128)(2,1)S(1)} %collective-permute-done.3.refs_0_.refs_2_, bf16[256,2560]{1,0:T(8,128)(2,1)S(1)} %collective-permute-done.4.refs_1_.refs_3_, ...), custom_call_target="tpu_custom_call" | custom-call | flops 1342177280 | bytes 8912896 | tf_op jit(solution)/shard_map/pallas_call | solution.py:204
  78.7 2.0 %collective-permute-start.14 = (bf16[128,2560]{1,0:T(8,128)(2,1)S(1)}, bf16[128,2560]{1,0:T(8,128)(2,1)S(1)}, u32[]{:S(2)}, u32[]{:S(2)}) collective-permute-start(bf16[128,2560]{1,0:T(8,128)(2,1)S(1)} %get-tuple-element.51), channel_id=1, source_target_pairs={{0,8},{2,10},{4,12},{6,14},{8,0},{10,2},{12,4},{14,6},{16,24},{18,... | collective-permute-start | bytes 1966088 | tf_op jit(solution)/shard_map/ppermute | solution.py:28
  80.7 2.8 %shard_map.113 = (bf16[256,2560]{1,0:T(8,128)(2,1)S(1)}, bf16[256,2560]{1,0:T(8,128)(2,1)S(1)}) custom-call(bf16[512,1024]{1,0:T(8,128)(2,1)S(1)} %fusion.18.refs_0_, bf16[128,2560]{1,0:T(8,128)(2,1)S(1)} %copy-done.9, bf16[128,3072]{1,0:T(8,128)(2,1)S(1)} %collective-permute-done.refs_0_.refs_2_, bf16[128,3072]{1,0:T(8,128)(2,1)S(1)} %copy-done.6, ...), custom_call_target="tpu_custom_call" | custom-call | flops 1342177280 | bytes 8912896 | tf_op jit(solution)/shard_map/pallas_call | solution.py:204
  86.7 2.9 %shard_map.114 = (f32[256,2560]{1,0:T(8,128)S(1)}, f32[128,2560]{1,0:T(8,128)S(1)}, f32[128,2560]{1,0:T(8,128)S(1)}) custom-call(bf16[512,1024]{1,0:T(8,128)(2,1)S(1)} %fusion.18.refs_0_, bf16[128,2560]{1,0:T(8,128)(2,1)S(1)} %copy-done.9, bf16[128,3072]{1,0:T(8,128)(2,1)S(1)} %collective-permute-done.refs_0_.refs_2_, bf16[128,3072]{1,0:T(8,128)(2,1)S(1)} %copy-done.6, ...), custom_call_target="tpu_custom_call" | custom-call | flops 1342177280 | bytes 8912896 | tf_op jit(solution)/shard_map/pallas_call | solution.py:204
  89.6 4.9 %shard_map.115 = (f32[128,2560]{1,0:T(8,128)S(1)}, f32[64,2560]{1,0:T(8,128)S(1)}, f32[64,2560]{1,0:T(8,128)S(1)}) custom-call(bf16[512,1024]{1,0:T(8,128)(2,1)S(1)} %fusion.18.refs_0_, bf16[256,2560]{1,0:T(8,128)(2,1)} %refs_1_.1, bf16[256,2560]{1,0:T(8,128)(2,1)S(1)} %collective-permute-done.3.refs_0_.refs_2_, ...), custom_call_target="tpu_custom_call" | custom-call | flops 1342177280 | bytes 8912896 | tf_op jit(solution)/shard_map/pallas_call | solution.py:204
  94.5 11.4 %collective-permute-done.14 = bf16[128,2560]{1,0:T(8,128)(2,1)S(1)} collective-permute-done((bf16[128,2560]{1,0:T(8,128)(2,1)S(1)}, bf16[128,2560]{1,0:T(8,128)(2,1)S(1)}, u32[]{:S(2)}, u32[]{:S(2)}) %collective-permute-start.14) | collective-permute-done | bytes 655392 | tf_op jit(solution)/shard_map/ppermute | solution.py:28
  106.0 17.8 %collective-permute-done.15 = bf16[128,2560]{1,0:T(8,128)(2,1)S(1)} collective-permute-done((bf16[128,2560]{1,0:T(8,128)(2,1)S(1)}, bf16[128,2560]{1,0:T(8,128)(2,1)S(1)}, u32[]{:S(2)}, u32[]{:S(2)}) %collective-permute-start.15) | collective-permute-done | bytes 655392 | tf_op jit(solution)/shard_map/ppermute | solution.py:28
  124.8 1.6 collective-permute-start.12
  128.8 6.9 %collective-permute-done.17 = bf16[64,2560]{1,0:T(8,128)(2,1)S(1)} collective-permute-done((bf16[64,2560]{1,0:T(8,128)(2,1)S(1)}, bf16[64,2560]{1,0:T(8,128)(2,1)S(1)}, u32[]{:S(2)}, u32[]{:S(2)}) %collective-permute-start.17) | collective-permute-done | bytes 327712 | tf_op jit(solution)/shard_map/ppermute | solution.py:28
  135.7 2.3 %fusion.8 = (bf16[128,2560]{1,0:T(8,128)(2,1)}, bf16[128,2560]{1,0:T(8,128)(2,1)}) fusion(bf16[128,2560]{1,0:T(8,128)(2,1)S(1)} %copy-done.1, bf16[64,2560]{1,0:T(8,128)(2,1)S(1)} %collective-permute-done.17, bf16[64,2560]{1,0:T(8,128)(2,1)S(1)} %collective-permute-done.16, f32[128,2560]{1,0:T(8,128)S(1)} %get-tuple-element.62, ...), kind=kLoop, calls=%fused_computation.21 | loop fusion | flops 11468800 | bytes 5242880 | tf_op jit(solution)/shard_map/convert_element_type | solution.py:311
  139.9 2.5 %psum.42 = f32[256]{0:T(256)S(1)} all-reduce(f32[256]{0:T(256)S(1)} %get-tuple-element.72), channel_id=1, replica_groups=mesh['dp'=16,'mp'=2] {'mp'}, use_global_device_ids=true, to_apply=%region_2.3 | all-reduce | flops 256 | bytes 2048 | tf_op jit(solution)/shard_map/psum | solution.py:319
  144.3 8.3 %psum.43 = f32[5248]{0:T(1024)S(1)} all-reduce(f32[5248]{0:T(1024)S(1)} %pad_maximum_fusion.3), channel_id=1, replica_groups={{0,2},{4,6},{8,10},{12,14},{16,18},{20,22},{24,26},{28,30},{1,3},{5,7},..., use_global_device_ids=true, to_apply=%region_5.6 | all-reduce | flops 5248 | bytes 41984 | tf_op jit(solution)/shard_map/psum | solution.py:35
  152.6 8.2 %psum.44 = f32[5248]{0:T(1024)S(1)} all-reduce(f32[5248]{0:T(1024)S(1)} %psum.43), channel_id=1, replica_groups={{0,4},{2,6},{8,12},{10,14},{16,20},{18,22},{24,28},{26,30},{1,5},{3,7},..., use_global_device_ids=true, to_apply=%region_6.7 | all-reduce | flops 5248 | bytes 41984 | tf_op jit(solution)/shard_map/psum | solution.py:35
  160.8 6.8 %psum.45 = f32[5248]{0:T(1024)S(1)} all-reduce(f32[5248]{0:T(1024)S(1)} %psum.44), channel_id=1, replica_groups={{0,8},{2,10},{4,12},{6,14},{16,24},{18,26},{20,28},{22,30},{1,9},{3,11}..., use_global_device_ids=true, to_apply=%region_7.8 | all-reduce | flops 5248 | bytes 41984 | tf_op jit(solution)/shard_map/psum | solution.py:35
  167.6 10.7 %psum.46 = f32[5248]{0:T(1024)S(1)} all-reduce(f32[5248]{0:T(1024)S(1)} %psum.45), channel_id=1, replica_groups={{0,16},{2,18},{4,20},{6,22},{8,24},{10,26},{12,28},{14,30},{1,17},{3,19..., use_global_device_ids=true, to_apply=%region_8.9 | all-reduce | flops 5248 | bytes 41984 | tf_op jit(solution)/shard_map/psum | solution.py:35
  178.8 2.5 %psum.47 = f32[128]{0:T(128)S(1)} all-reduce(f32[128]{0:T(128)S(1)} %get-tuple-element.68), channel_id=1, replica_groups=mesh['dp'=16,'mp'=2] {'mp'}, use_global_device_ids=true, to_apply=%region_10.11 | all-reduce | flops 128 | bytes 1024 | tf_op jit(solution)/shard_map/psum | solution.py:328
  183.3 1.8 multiply_multiply_fusion
  (99 shorter events, 30.4 us)
Async XLA Ops:
  5.9 33.9 %copy-start.7 = (bf16[128,1024]{1,0:T(8,128)(2,1)}, bf16[128,1024]{1,0:T(8,128)(2,1)S(1)}, u32[]{:S(2)}) copy-start(bf16[128,1024]{1,0:T(8,128)(2,1)S(1)} %get-tuple-element.36) | copy-start | bytes 786436
  5.9 33.9 %copy-start.8 = (bf16[128,2560]{1,0:T(8,128)(2,1)}, bf16[128,2560]{1,0:T(8,128)(2,1)S(1)}, u32[]{:S(2)}) copy-start(bf16[128,2560]{1,0:T(8,128)(2,1)S(1)} %get-tuple-element.48.refs_1_) | copy-start | bytes 1966084
  5.9 32.0 %collective-permute-start.3 = (bf16[256,2560]{1,0:T(8,128)(2,1)}, bf16[256,2560]{1,0:T(8,128)(2,1)S(1)}, u32[]{:S(2)}, u32[]{:S(2)}) collective-permute-start(bf16[256,2560]{1,0:T(8,128)(2,1)} %refs_1_.1), channel_id=1, source_target_pairs={{0,2},{2,0},{4,6},{6,4},{8,10},{10,8},{12,14},{14,12},{16,18},{18,... | collective-permute-start | bytes 3932168 | tf_op jit(solution)/shard_map/ppermute | solution.py:28
  8.9 30.5 %collective-permute-start.4 = (bf16[256,2560]{1,0:T(8,128)(2,1)}, bf16[256,2560]{1,0:T(8,128)(2,1)S(1)}, u32[]{:S(2)}, u32[]{:S(2)}) collective-permute-start(bf16[256,2560]{1,0:T(8,128)(2,1)} %refs_1_.1), channel_id=1, source_target_pairs={{0,4},{2,6},{4,0},{6,2},{8,12},{10,14},{12,8},{14,10},{16,20},{18,... | collective-permute-start | bytes 3932168 | tf_op jit(solution)/shard_map/ppermute | solution.py:28
  10.5 40.5 %collective-permute-start = (bf16[128,3072]{1,0:T(8,128)(2,1)S(1)}, bf16[128,3072]{1,0:T(8,128)(2,1)S(1)}, u32[]{:S(2)}, u32[]{:S(2)}) collective-permute-start(bf16[128,3072]{1,0:T(8,128)(2,1)S(1)} %get-tuple-element.38), channel_id=1, source_target_pairs={{0,8},{2,10},{4,12},{6,14},{8,0},{10,2},{12,4},{14,6},{16,24},{18,... | collective-permute-start | bytes 2359304 | tf_op jit(solution)/shard_map/ppermute | solution.py:28
  12.0 40.5 %collective-permute-start.1 = (bf16[128,3072]{1,0:T(8,128)(2,1)S(1)}, bf16[128,3072]{1,0:T(8,128)(2,1)S(1)}, u32[]{:S(2)}, u32[]{:S(2)}) collective-permute-start(bf16[128,3072]{1,0:T(8,128)(2,1)S(1)} %get-tuple-element.39), channel_id=1, source_target_pairs={{0,16},{2,18},{4,20},{6,22},{8,24},{10,26},{12,28},{14,30},{16,0},... | collective-permute-start | bytes 2359304 | tf_op jit(solution)/shard_map/ppermute | solution.py:28
  14.6 36.3 %collective-permute-start.2 = (bf16[128,512]{1,0:T(8,128)(2,1)S(1)}, bf16[128,512]{1,0:T(8,128)(2,1)S(1)}, u32[]{:S(2)}, u32[]{:S(2)}) collective-permute-start(bf16[128,512]{1,0:T(8,128)(2,1)S(1)} %get-tuple-element.40), channel_id=1, source_target_pairs={{0,24},{2,26},{4,28},{6,30},{8,16},{10,18},{12,20},{14,22},{16,8},... | collective-permute-start | bytes 393224 | tf_op jit(solution)/shard_map/ppermute | solution.py:28
  55.7 5.1 %collective-permute-start.5 = (bf16[128,1536]{1,0:T(8,128)(2,1)}, bf16[128,1536]{1,0:T(8,128)(2,1)}, u32[]{:S(2)}, u32[]{:S(2)}) collective-permute-start(bf16[128,1536]{1,0:T(8,128)(2,1)} %get-tuple-element.47), channel_id=1, source_target_pairs={{0,1},{1,0},{2,3},{3,2},{4,5},{5,4},{6,7},{7,6},{8,9},{9,8},{10,11... | collective-permute-start | bytes 1179656 | tf_op jit(solution)/shard_map/ppermute | solution.py:28
  56.7 17.4 %collective-permute-start.6 = (bf16[128,2560]{1,0:T(8,128)(2,1)}, bf16[128,2560]{1,0:T(8,128)(2,1)S(1)}, u32[]{:S(2)}, u32[]{:S(2)}) collective-permute-start(bf16[128,2560]{1,0:T(8,128)(2,1)} %copy-done.11), channel_id=1, source_target_pairs={{0,4},{2,6},{4,0},{6,2},{8,12},{10,14},{12,8},{14,10},{16,20},{18,... | collective-permute-start | bytes 1966088 | tf_op jit(solution)/shard_map/ppermute | solution.py:28
  57.3 17.1 %collective-permute-start.7 = (bf16[128,2560]{1,0:T(8,128)(2,1)}, bf16[128,2560]{1,0:T(8,128)(2,1)S(1)}, u32[]{:S(2)}, u32[]{:S(2)}) collective-permute-start(bf16[128,2560]{1,0:T(8,128)(2,1)} %copy-done.10), channel_id=1, source_target_pairs={{0,2},{2,0},{4,6},{6,4},{8,10},{10,8},{12,14},{14,12},{16,18},{18,... | collective-permute-start | bytes 1966088 | tf_op jit(solution)/shard_map/ppermute | solution.py:28
  57.8 22.9 %collective-permute-start.8 = (bf16[64,2560]{1,0:T(8,128)(2,1)}, bf16[64,2560]{1,0:T(8,128)(2,1)S(1)}, u32[]{:S(2)}, u32[]{:S(2)}) collective-permute-start(bf16[64,2560]{1,0:T(8,128)(2,1)} %copy-done.13), channel_id=1, source_target_pairs={{0,16},{2,18},{4,20},{6,22},{8,24},{10,26},{12,28},{14,30},{16,0},... | collective-permute-start | bytes 983048 | tf_op jit(solution)/shard_map/ppermute | solution.py:28
  60.8 19.9 %collective-permute-start.9 = (bf16[64,2560]{1,0:T(8,128)(2,1)}, bf16[64,2560]{1,0:T(8,128)(2,1)S(1)}, u32[]{:S(2)}, u32[]{:S(2)}) collective-permute-start(bf16[64,2560]{1,0:T(8,128)(2,1)} %copy-done.12), channel_id=1, source_target_pairs={{0,8},{2,10},{4,12},{6,14},{8,0},{10,2},{12,4},{14,6},{16,24},{18,... | collective-permute-start | bytes 983048 | tf_op jit(solution)/shard_map/ppermute | solution.py:28
  62.2 18.5 %copy-start.6 = (bf16[128,3072]{1,0:T(8,128)(2,1)S(1)}, bf16[128,3072]{1,0:T(8,128)(2,1)}, u32[]{:S(2)}) copy-start(bf16[128,3072]{1,0:T(8,128)(2,1)} %copy-done.5) | copy-start | bytes 2359300
  62.2 18.5 %copy-start.9 = (bf16[128,2560]{1,0:T(8,128)(2,1)S(1)}, bf16[128,2560]{1,0:T(8,128)(2,1)}, u32[]{:S(2)}) copy-start(bf16[128,2560]{1,0:T(8,128)(2,1)} %copy-done.8) | copy-start | bytes 1966084
  78.7 27.3 %collective-permute-start.14 = (bf16[128,2560]{1,0:T(8,128)(2,1)S(1)}, bf16[128,2560]{1,0:T(8,128)(2,1)S(1)}, u32[]{:S(2)}, u32[]{:S(2)}) collective-permute-start(bf16[128,2560]{1,0:T(8,128)(2,1)S(1)} %get-tuple-element.51), channel_id=1, source_target_pairs={{0,8},{2,10},{4,12},{6,14},{8,0},{10,2},{12,4},{14,6},{16,24},{18,... | collective-permute-start | bytes 1966088 | tf_op jit(solution)/shard_map/ppermute | solution.py:28
  83.5 41.2 %collective-permute-start.10 = (bf16[256,2560]{1,0:T(8,128)(2,1)S(1)}, bf16[256,2560]{1,0:T(8,128)(2,1)S(1)}, u32[]{:S(2)}, u32[]{:S(2)}) collective-permute-start(bf16[256,2560]{1,0:T(8,128)(2,1)S(1)} %get-tuple-element.54), channel_id=1, source_target_pairs={{0,2},{2,0},{4,6},{6,4},{8,10},{10,8},{12,14},{14,12},{16,18},{18,... | collective-permute-start | bytes 3932168 | tf_op jit(solution)/shard_map/ppermute | solution.py:28
  84.1 39.7 %collective-permute-start.15 = (bf16[128,2560]{1,0:T(8,128)(2,1)S(1)}, bf16[128,2560]{1,0:T(8,128)(2,1)S(1)}, u32[]{:S(2)}, u32[]{:S(2)}) collective-permute-start(bf16[128,2560]{1,0:T(8,128)(2,1)S(1)} %get-tuple-element.63), channel_id=1, source_target_pairs={{0,16},{2,18},{4,20},{6,22},{8,24},{10,26},{12,28},{14,30},{16,0},... | collective-permute-start | bytes 1966088 | tf_op jit(solution)/shard_map/ppermute | solution.py:28
  85.1 41.2 %collective-permute-start.11 = (bf16[256,2560]{1,0:T(8,128)(2,1)S(1)}, bf16[256,2560]{1,0:T(8,128)(2,1)S(1)}, u32[]{:S(2)}, u32[]{:S(2)}) collective-permute-start(bf16[256,2560]{1,0:T(8,128)(2,1)S(1)} %get-tuple-element.57), channel_id=1, source_target_pairs={{0,4},{2,6},{4,0},{6,2},{8,12},{10,14},{12,8},{14,10},{16,20},{18,... | collective-permute-start | bytes 3932168 | tf_op jit(solution)/shard_map/ppermute | solution.py:28
  106.0 22.8 %collective-permute-start.16 = (bf16[64,2560]{1,0:T(8,128)(2,1)S(1)}, bf16[64,2560]{1,0:T(8,128)(2,1)S(1)}, u32[]{:S(2)}, u32[]{:S(2)}) collective-permute-start(bf16[64,2560]{1,0:T(8,128)(2,1)S(1)} %add_convert_fusion.3), channel_id=1, source_target_pairs={{0,16},{2,18},{4,20},{6,22},{8,24},{10,26},{12,28},{14,30},{16,0},... | collective-permute-start | bytes 983048 | tf_op jit(solution)/shard_map/ppermute | solution.py:28
  123.9 11.8 %collective-permute-start.17 = (bf16[64,2560]{1,0:T(8,128)(2,1)S(1)}, bf16[64,2560]{1,0:T(8,128)(2,1)S(1)}, u32[]{:S(2)}, u32[]{:S(2)}) collective-permute-start(bf16[64,2560]{1,0:T(8,128)(2,1)S(1)} %add_convert_fusion.2), channel_id=1, source_target_pairs={{0,8},{2,10},{4,12},{6,14},{8,0},{10,2},{12,4},{14,6},{16,24},{18,... | collective-permute-start | bytes 983048 | tf_op jit(solution)/shard_map/ppermute | solution.py:28
  124.8 13.3 %collective-permute-start.12 = (bf16[128,2560]{1,0:T(8,128)(2,1)S(1)}, bf16[128,2560]{1,0:T(8,128)(2,1)S(1)}, u32[]{:S(2)}, u32[]{:S(2)}) collective-permute-start(bf16[128,2560]{1,0:T(8,128)(2,1)S(1)} %add_convert_fusion.1), channel_id=1, source_target_pairs={{0,4},{2,6},{4,0},{6,2},{8,12},{10,14},{12,8},{14,10},{16,20},{18,... | collective-permute-start | bytes 1966088 | tf_op jit(solution)/shard_map/ppermute | solution.py:28
  126.5 12.2 %collective-permute-start.13 = (bf16[128,2560]{1,0:T(8,128)(2,1)S(1)}, bf16[128,2560]{1,0:T(8,128)(2,1)S(1)}, u32[]{:S(2)}, u32[]{:S(2)}) collective-permute-start(bf16[128,2560]{1,0:T(8,128)(2,1)S(1)} %add_convert_fusion), channel_id=1, source_target_pairs={{0,2},{2,0},{4,6},{6,4},{8,10},{10,8},{12,14},{14,12},{16,18},{18,... | collective-permute-start | bytes 1966088 | tf_op jit(solution)/shard_map/ppermute | solution.py:28
  143.0 40.2 %copy-start.19 = (f32[256]{0:T(256)}, f32[256]{0:T(256)S(1)}, u32[]{:S(2)}) copy-start(f32[256]{0:T(256)S(1)} %get-tuple-element.71) | copy-start | bytes 3076
  143.0 35.8 %copy-start.18 = (f32[2560]{0:T(1024)S(1)}, f32[2560]{0:T(1024)}, u32[]{:S(2)}) copy-start(f32[2560]{0:T(1024)} %param.11) | copy-start | bytes 30724
  (18 other events, 87.7 us)

commit v7 on v6

--- a/solution.py
+++ b/solution.py
@@ -9,6 +9,7 @@
 
 TRAIN_STEP = 3
 INNER_BITS = 2
+EAGER = pl.CostEstimate(flops=0, bytes_accessed=0, transcendentals=0)
 PIECES = ((0, 0), (0, 1), (1, 0), (3, 0), (2, 1), (3, 1), (2, 0), (1, 1))
 
 
@@ -29,10 +30,13 @@
 
 
 def group_sum(value, bits):
-    size = lax.axis_size("dp")
-    for bit in bits:
-        pairs = [[i, i | bit] for i in range(size) if not i & bit]
-        value = lax.psum(value, "dp", axis_index_groups=pairs)
+    for at in range(0, len(bits), 2):
+        pair = bits[at : at + 2]
+        if len(pair) == 2:
+            first, second = flip(value, pair[0]), flip(value, pair[1])
+            value = (value + first) + (second + flip(value, pair[0] | pair[1]))
+        else:
+            value = value + flip(value, pair[0])
     return value
 
 
@@ -146,10 +150,8 @@
             pltpu.VMEM(up_pre.shape, jnp.bfloat16),
             pltpu.SemaphoreType.DMA((3,)),
         ],
-        compiler_params=pltpu.CompilerParams(vmem_limit_bytes=16 << 20),
-        cost_estimate=pl.CostEstimate(
-            flops=20 * tokens * units, bytes_accessed=16 * tokens * units, transcendentals=tokens * units
-        ),
+        compiler_params=pltpu.CompilerParams(vmem_limit_bytes=56 << 20),
+        cost_estimate=EAGER,
     )(place, out_grad, gate_pre, up_pre)
 
 
@@ -173,48 +175,50 @@
         in_specs=[pl.BlockSpec(memory_space=pltpu.HBM)] * len(sources),
         out_specs=[pl.BlockSpec(memory_space=pltpu.HBM)] * len(shapes),
         scratch_shapes=[pltpu.SemaphoreType.DMA((len(parts),))],
-        compiler_params=pltpu.CompilerParams(vmem_limit_bytes=4 << 20),
-        cost_estimate=pl.CostEstimate(
-            flops=0, bytes_accessed=sum(4 * math.prod(shape) for shape in shapes), transcendentals=0
-        ),
+        compiler_params=pltpu.CompilerParams(vmem_limit_bytes=1 << 20),
+        cost_estimate=EAGER,
     )(*sources)
 
 
-def product(share, pieces, layout, outputs, over_rows, tile):
-    units = min(piece.shape[1] for piece in pieces)
-    depth = sum(rows for _, _, rows in layout)
+def products(share, groups, tile):
+    units = min(piece.shape[1] for piece in groups[0][0])
+    pieces = [piece for group in groups for piece in group[0]]
+    depths = [sum(rows for _, _, rows in group[1]) for group in groups]
+    bounds = [output for group in groups for output in group[2]]
 
     def kernel(*refs):
         share_ref, ins = refs[0], refs[1 : 1 + len(pieces)]
-        outs, stack = refs[1 + len(pieces) : -1], refs[-1]
-        at = 0
-        for piece, first, rows in layout:
-            stack[at : at + rows, :] = ins[piece][first : first + rows, :]
-            at += rows
-        for (begin, end, kind), out in zip(outputs, outs):
-            if over_rows:
-                value = lax.dot_general(
-                    share_ref[:, begin:end], stack[...], (((0,), (0,)), ((), ())), preferred_element_type=jnp.float32
-                )
-            else:
-                value = jnp.dot(share_ref[begin:end, :], stack[...], preferred_element_type=jnp.float32)
-            out[...] = value.astype(kind)
-
-    total = sum(end - begin for begin, end, _ in outputs)
+        outs, stacks = refs[1 + len(pieces) : -len(groups)], refs[-len(groups) :]
+        n = o = 0
+        for (own, layout, outputs, over_rows), stack in zip(groups, stacks):
+            at = 0
+            for piece, first, rows in layout:
+                stack[at : at + rows, :] = ins[n + piece][first : first + rows, :]
+                at += rows
+            for begin, end, kind in outputs:
+                if over_rows:
+                    value = lax.dot_general(
+                        share_ref[:, begin:end],
+                        stack[...],
+                        (((0,), (0,)), ((), ())),
+                        preferred_element_type=jnp.float32,
+                    )
+                else:
+                    value = jnp.dot(share_ref[begin:end, :], stack[...], preferred_element_type=jnp.float32)
+                outs[o][...] = value.astype(kind)
+                o += 1
+            n += len(own)
+
     return pl.pallas_call(
         kernel,
         grid=(units // tile,),
-        out_shape=[jax.ShapeDtypeStruct((end - begin, units), kind) for begin, end, kind in outputs],
+        out_shape=[jax.ShapeDtypeStruct((end - begin, units), kind) for begin, end, kind in bounds],
         in_specs=[pl.BlockSpec(share.shape, lambda i: (0, 0))]
         + [pl.BlockSpec((piece.shape[0], tile), lambda i: (0, i)) for piece in pieces],
-        out_specs=[pl.BlockSpec((end - begin, tile), lambda i: (0, i)) for begin, end, _ in outputs],
-        scratch_shapes=[pltpu.VMEM((depth, tile), jnp.bfloat16)],
-        compiler_params=pltpu.CompilerParams(vmem_limit_bytes=24 << 20),
-        cost_estimate=pl.CostEstimate(
-            flops=2 * total * depth * units,
-            bytes_accessed=2 * (depth + 2 * total) * units + 2 * share.size,
-            transcendentals=0,
-        ),
+        out_specs=[pl.BlockSpec((end - begin, tile), lambda i: (0, i)) for begin, end, _ in bounds],
+        scratch_shapes=[pltpu.VMEM((depth, tile), jnp.bfloat16) for depth in depths],
+        compiler_params=pltpu.CompilerParams(vmem_limit_bytes=14 << 20),
+        cost_estimate=EAGER,
     )(share, *pieces)
 
 
@@ -229,26 +233,25 @@
 
     down_weight, message1 = lax.optimization_barrier((down_weight, message1))
     message1, message2, message3 = flip(message1, z_bit), flip(message2, w_bit), flip(message3, z_bit | w_bit)
-    weight1, weight2 = flip(down_weight, x_bit), flip(down_weight, y_bit)
-    whole = (0, units)
-    to_y, to_x = cut([weight1, weight2], [(0, (0, q), whole, 0, 0), (1, (q, q), whole, 1, 0)], [(q, units)] * 2)
-    weight3a, weight3b = flip(to_y, y_bit), flip(to_x, x_bit)
-
-    message1, message2, message3, _, _ = lax.optimization_barrier((message1, message2, message3, to_y, to_x))
-    extra, every = (units, 2 * rows), (0, tokens)
-    to_w, to_z, mine = cut(
-        [message1, message2, message3],
+    whole, extra, every = (0, units), (units, 2 * rows), (0, tokens)
+    (to_peers,) = cut([down_weight], [(0, (0, rows), whole, 0, 0)], [(rows, units)])
+    weight1, weight2 = flip(to_peers, x_bit), flip(to_peers, y_bit)
+    to_w, to_z, mine, to_y, to_x = cut(
+        [message1, message2, message3, weight1, weight2],
         [
             (0, (0, t), whole, 0, 0),
             (1, (t, t), whole, 1, 0),
             (0, every, extra, 2, 0),
             (1, every, extra, 2, 2 * rows),
             (2, every, (0, 2 * rows), 2, 4 * rows),
+            (3, (0, q), whole, 3, 0),
+            (4, (q, q), whole, 4, 0),
         ],
-        [(t, units), (t, units), (tokens, 6 * rows)],
+        [(t, units), (t, units), (tokens, 6 * rows), (q, units), (q, units)],
     )
     theirs = flip(mine, 1, "mp")
     hidden3a, hidden3b = flip(to_w, w_bit), flip(to_z, z_bit)
+    weight3a, weight3b = flip(to_y, y_bit), flip(to_x, x_bit)
 
     def features(k):
         a, b = mine[:, (k - 1) * 2 * rows : k * 2 * rows], theirs[:, (k - 1) * 2 * rows : k * 2 * rows]
@@ -260,16 +263,11 @@
     def layout(size):
         return [(0, 0, 2 * size), (1, 0, size), (3, 0, size), (2, size, size), (4, 0, size), (2, 0, size), (1, size, size)]
 
-    def send_parts(pieces, depth, size, over_rows):
-        kind = jnp.bfloat16
-        return product(
-            share, pieces, layout(depth), [(2 * size, 4 * size, kind), (4 * size, 6 * size, kind)], over_rows, 512
-        )
-
-    def keep_parts(pieces, depth, size, over_rows):
-        kind = jnp.float32
-        bounds = [(0, 2 * size, kind), (6 * size, 7 * size, kind), (7 * size, 8 * size, kind)]
-        return product(share, pieces, layout(depth), bounds, over_rows, 512)
+    def sent(size):
+        return [(2 * size, 4 * size, jnp.bfloat16), (4 * size, 6 * size, jnp.bfloat16)]
+
+    def kept(size):
+        return [(0, 2 * size, jnp.float32), (6 * size, 7 * size, jnp.float32), (7 * size, 8 * size, jnp.float32)]
 
     def finish(parts, from_low, from_high, size, low, high):
         send, keep = jnp.bfloat16, jnp.float32
@@ -279,17 +277,17 @@
         kept = own_part + jnp.concatenate([from_low[:size], from_high[:size]], axis=0).astype(keep)
         return kept + jnp.concatenate([last_a, last_b], axis=0).astype(keep)
 
+    hiddens = [hidden, message1, message2, hidden3a, hidden3b]
     weights = [down_weight, weight1, weight2, weight3a, weight3b]
-    to_z, to_w = send_parts(weights, q, t, False)
+    to_x, to_y, to_z, to_w = products(
+        share, [(hiddens, layout(t), sent(q), True), (weights, layout(q), sent(t), False)], 512
+    )
+    from_x, from_y = flip(to_x, x_bit), flip(to_y, y_bit)
     from_z, from_w = flip(to_z, z_bit), flip(to_w, w_bit)
-    hidden3a, hidden3b, _ = lax.optimization_barrier((hidden3a, hidden3b, to_z))
-    hiddens = [hidden, message1, message2, hidden3a, hidden3b]
-    to_x, to_y = send_parts(hiddens, t, q, True)
-    from_x, from_y = flip(to_x, x_bit), flip(to_y, y_bit)
-    share, weight3a, weight3b, _ = lax.optimization_barrier((share, weight3a, weight3b, to_x))
-    weights = [down_weight, weight1, weight2, weight3a, weight3b]
-    grad = finish(keep_parts(hiddens, t, q, True), from_x, from_y, q, x_bit, y_bit)
-    hidden_grad = finish(keep_parts(weights, q, t, False), from_z, from_w, t, z_bit, w_bit)
+    share, _ = lax.optimization_barrier((share, to_x))
+    parts = products(share, [(hiddens, layout(t), kept(q), True), (weights, layout(q), kept(t), False)], 512)
+    grad = finish(parts[:3], from_x, from_y, q, x_bit, y_bit)
+    hidden_grad = finish(parts[3:], from_z, from_w, t, z_bit, w_bit)
     return grad, hidden_grad
 
 

time: 187 us -> 156 us (0.83)
  blocking collectives: 38.9 us -> 4.94 us
  starting transfers between devices: 21.6 us -> 28.1 us
  local copies, waits for them, and re-layouts: 10.8 us -> 6.07 us
  other arithmetic: 8.46 us -> 10.7 us
  Pallas kernels: 18 us -> 15.9 us
    psum x4 -> x0, blocking collectives: 34 us -> none  [group_sum(): value = lax.psum(value, 'dp', axis_index_groups=pairs)]
    ppermute x18 -> x24, starting transfers between devices: 21.6 us -> 28.1 us  [flip(): return lax.ppermute(value, axis, [(i, i ^ bits) for i in range(size)])]
    unnamed x43 -> x49, local copies, waits for them, and re-layouts: 9.14 us -> 4.74 us
    pallas_call x4 -> x2, Pallas kernels: 14.9 us -> 10.6 us  [products(): pl.pallas_call(kernel, grid=(units // tile,), out_shape=[jax.ShapeDtypeSt...]
    pallas_call x1, Pallas kernels: 1.8 us -> 4.19 us  [first_stage(): pl.pallas_call(kernel, out_shape=[jax.ShapeDtypeStruct((tokens, share_wid...]
    ppermute x18 -> x24, waiting for transfers between devices: 85 us -> 86.7 us  [flip(): return lax.ppermute(value, axis, [(i, i ^ bits) for i in range(size)])]
  transfers between devices with their start and end apart: 18 -> 24, of which waited for: 11 -> 16; matrix products, arithmetic and copies ran while one was open for 3% -> 6% of each run, Pallas kernels for 8% -> 4%
where the time goes in v7:
time: 156 us
  waiting for transfers between devices  86.7 us (56%)
  starting transfers between devices  28.1 us (18%)
  Pallas kernels  15.9 us (10%)
  other arithmetic  10.7 us (7%)
  local copies, waits for them, and re-layouts  6.07 us (4%)
  blocking collectives  4.94 us (3%)
  between operations  3.47 us (2%)
    ppermute x24, waiting for transfers between devices, flip(): return lax.ppermute(value, axis, [(i, i ^ bits) for i in range(size)])  86.7 us
    ppermute x24, starting transfers between devices, flip(): return lax.ppermute(value, axis, [(i, i ^ bits) for i in range(size)])  28.1 us
    pallas_call x2, Pallas kernels, products(): pl.pallas_call(kernel, grid=(units // tile,), out_shape=[jax.ShapeDtypeSt...  10.6 us
    unnamed x49, local copies, waits for them, and re-layouts  4.74 us
    pallas_call x1, Pallas kernels, first_stage(): pl.pallas_call(kernel, out_shape=[jax.ShapeDtypeStruct((tokens, share_wid...  4.19 us
  transfers between devices with their start and end apart: 24, of which 16 were waited for; matrix products, arithmetic and copies ran while one was open for 6% of the time, Pallas kernels for 4%

profile of v7, /device:TPU:0, one launch (start us, length us, event | category | flops | bytes accessed | tf_op | source)
XLA Modules:
  0.0 155.8 jit_solution(18241610843738877911)
XLA Ops:
  1.2 4.2 %shard_map.109 = (bf16[128,1024]{1,0:T(8,128)(2,1)}, bf16[128,2560]{1,0:T(8,128)(2,1)}, bf16[128,3072]{1,0:T(8,128)(2,1)}, bf16[128,3072]{1,0:T(8,128)(2,1)}, bf16[128,512]{1,0:T(8,128)(2,1)}) custom-call(s32[2]{0:T(128)} %pad_add_fusion.place, bf16[128,4096]{1,0:T(8,128)(2,1)} %source_hbm.1, bf16[128,2560]{1,0:T(8,128)(2,1)} %gate_hbm.1, ...), custom_call_target="tpu_custom_call" | custom-call | tf_op jit(solution)/shard_map/pallas_call | solution.py:136
  5.6 3.0 %collective-permute-start.4 = (bf16[256,2560]{1,0:T(8,128)(2,1)S(1)}, bf16[256,2560]{1,0:T(8,128)(2,1)S(1)}, u32[]{:S(2)}, u32[]{:S(2)}) collective-permute-start(bf16[256,2560]{1,0:T(8,128)(2,1)S(1)} %shard_map.110), channel_id=1, source_target_pairs={{0,4},{2,6},{4,0},{6,2},{8,12},{10,14},{12,8},{14,10},{16,20},{18,... | collective-permute-start | bytes 3932168 | tf_op jit(solution)/shard_map/ppermute | solution.py:29
  8.6 1.5 collective-permute-start.3
  10.1 1.6 %collective-permute-start = (bf16[128,3072]{1,0:T(8,128)(2,1)S(1)}, bf16[128,3072]{1,0:T(8,128)(2,1)S(1)}, u32[]{:S(2)}, u32[]{:S(2)}) collective-permute-start(bf16[128,3072]{1,0:T(8,128)(2,1)S(1)} %copy-done.22), channel_id=1, source_target_pairs={{0,8},{2,10},{4,12},{6,14},{8,0},{10,2},{12,4},{14,6},{16,24},{18,... | collective-permute-start | bytes 2359304 | tf_op jit(solution)/shard_map/ppermute | solution.py:29
  11.7 2.6 %collective-permute-start.1 = (bf16[128,3072]{1,0:T(8,128)(2,1)S(1)}, bf16[128,3072]{1,0:T(8,128)(2,1)S(1)}, u32[]{:S(2)}, u32[]{:S(2)}) collective-permute-start(bf16[128,3072]{1,0:T(8,128)(2,1)S(1)} %copy-done.21), channel_id=1, source_target_pairs={{0,16},{2,18},{4,20},{6,22},{8,24},{10,26},{12,28},{14,30},{16,0},... | collective-permute-start | bytes 2359304 | tf_op jit(solution)/shard_map/ppermute | solution.py:29
  14.5 36.1 %collective-permute-done.2.refs_2_ = bf16[128,512]{1,0:T(8,128)(2,1)S(1)} collective-permute-done((bf16[128,512]{1,0:T(8,128)(2,1)S(1)}, bf16[128,512]{1,0:T(8,128)(2,1)S(1)}, u32[]{:S(2)}, u32[]{:S(2)}) %collective-permute-start.2) | collective-permute-done | bytes 131104 | tf_op jit(solution)/shard_map/ppermute | solution.py:29
  50.6 1.5 collective-permute-done.1.refs_1_.refs_3_
  57.7 3.1 %collective-permute-start.6 = (bf16[64,2560]{1,0:T(8,128)(2,1)}, bf16[64,2560]{1,0:T(8,128)(2,1)S(1)}, u32[]{:S(2)}, u32[]{:S(2)}) collective-permute-start(bf16[64,2560]{1,0:T(8,128)(2,1)} %copy-done.11), channel_id=1, source_target_pairs={{0,16},{2,18},{4,20},{6,22},{8,24},{10,26},{12,28},{14,30},{16,0},... | collective-permute-start | bytes 983048 | tf_op jit(solution)/shard_map/ppermute | solution.py:29
  63.9 12.7 %collective-permute-done.6.refs_4_ = bf16[64,2560]{1,0:T(8,128)(2,1)S(1)} collective-permute-done((bf16[64,2560]{1,0:T(8,128)(2,1)}, bf16[64,2560]{1,0:T(8,128)(2,1)S(1)}, u32[]{:S(2)}, u32[]{:S(2)}) %collective-permute-start.6) | collective-permute-done | bytes 327712 | tf_op jit(solution)/shard_map/ppermute | solution.py:29
  78.1 4.7 %shard_map.112 = (bf16[256,2560]{1,0:T(8,128)(2,1)S(1)}, bf16[256,2560]{1,0:T(8,128)(2,1)S(1)}, bf16[128,2560]{1,0:T(8,128)(2,1)S(1)}, bf16[128,2560]{1,0:T(8,128)(2,1)S(1)}) custom-call(bf16[512,1024]{1,0:T(8,128)(2,1)S(1)} %fusion.18.refs_0_, bf16[128,2560]{1,0:T(8,128)(2,1)S(1)} %copy-done.5, bf16[128,3072]{1,0:T(8,128)(2,1)S(1)} %collective-permute-done.refs_0_.refs_2_, ...), custom_call_target="tpu_custom_call" | custom-call | tf_op jit(solution)/shard_map/pallas_call | solution.py:212
  82.8 1.8 %collective-permute-start.20 = (bf16[128,2560]{1,0:T(8,128)(2,1)S(1)}, bf16[128,2560]{1,0:T(8,128)(2,1)S(1)}, u32[]{:S(2)}, u32[]{:S(2)}) collective-permute-start(bf16[128,2560]{1,0:T(8,128)(2,1)S(1)} %get-tuple-element.48), channel_id=1, source_target_pairs={{0,8},{2,10},{4,12},{6,14},{8,0},{10,2},{12,4},{14,6},{16,24},{18,... | collective-permute-start | bytes 1966088 | tf_op jit(solution)/shard_map/ppermute | solution.py:29
  84.6 1.5 collective-permute-start.11
  87.0 5.9 %shard_map.113 = (f32[256,2560]{1,0:T(8,128)S(1)}, f32[128,2560]{1,0:T(8,128)S(1)}, f32[128,2560]{1,0:T(8,128)S(1)}, f32[128,2560]{1,0:T(8,128)S(1)}, f32[64,2560]{1,0:T(8,128)S(1)}, /*index=5*/f32[64,2560]{1,0:T(8,128)S(1)}) custom-call(bf16[512,1024]{1,0:T(8,128)(2,1)S(1)} %fusion.18.refs_0_, bf16[128,2560]{1,0:T(8,128)(2,1)S(1)} %copy-done.5, ...), custom_call_target="tpu_custom_call" | custom-call | tf_op jit(solution)/shard_map/pallas_call | solution.py:212
  93.0 17.1 %collective-permute-done.20 = bf16[128,2560]{1,0:T(8,128)(2,1)S(1)} collective-permute-done((bf16[128,2560]{1,0:T(8,128)(2,1)S(1)}, bf16[128,2560]{1,0:T(8,128)(2,1)S(1)}, u32[]{:S(2)}, u32[]{:S(2)}) %collective-permute-start.20) | collective-permute-done | bytes 655392 | tf_op jit(solution)/shard_map/ppermute | solution.py:29
  111.7 2.2 %collective-permute-done.11 = bf16[256,2560]{1,0:T(8,128)(2,1)S(1)} collective-permute-done((bf16[256,2560]{1,0:T(8,128)(2,1)S(1)}, bf16[256,2560]{1,0:T(8,128)(2,1)S(1)}, u32[]{:S(2)}, u32[]{:S(2)}) %collective-permute-start.11) | collective-permute-done | bytes 1310752 | tf_op jit(solution)/shard_map/ppermute | solution.py:29
  116.2 9.6 %collective-permute-done.21 = bf16[128,2560]{1,0:T(8,128)(2,1)S(1)} collective-permute-done((bf16[128,2560]{1,0:T(8,128)(2,1)S(1)}, bf16[128,2560]{1,0:T(8,128)(2,1)S(1)}, u32[]{:S(2)}, u32[]{:S(2)}) %collective-permute-start.21) | collective-permute-done | bytes 655392 | tf_op jit(solution)/shard_map/ppermute | solution.py:29
  126.8 2.2 %collective-permute-done.13 = bf16[128,2560]{1,0:T(8,128)(2,1)S(1)} collective-permute-done((bf16[128,2560]{1,0:T(8,128)(2,1)S(1)}, bf16[128,2560]{1,0:T(8,128)(2,1)S(1)}, u32[]{:S(2)}, u32[]{:S(2)}) %collective-permute-start.13) | collective-permute-done | bytes 655392 | tf_op jit(solution)/shard_map/ppermute | solution.py:29
  130.0 2.5 %psum.14 = f32[256]{0:T(256)S(1)} all-reduce(f32[256]{0:T(256)S(1)} %get-tuple-element.58), channel_id=1, replica_groups=mesh['dp'=16,'mp'=2] {'mp'}, use_global_device_ids=true, to_apply=%region_2.3 | all-reduce | flops 256 | bytes 2048 | tf_op jit(solution)/shard_map/psum | solution.py:317
  135.5 1.6 %collective-permute-start.16 = (f32[5248]{0:T(1024)S(1)}, f32[5248]{0:T(1024)S(1)}, u32[]{:S(2)}, u32[]{:S(2)}) collective-permute-start(f32[5248]{0:T(1024)S(1)} %pad_maximum_fusion.3), channel_id=1, source_target_pairs={{0,6},{2,4},{4,2},{6,0},{8,14},{10,12},{12,10},{14,8},{16,22},{18,... | collective-permute-start | bytes 62984 | tf_op jit(solution)/shard_map/ppermute | solution.py:29
  138.4 2.0 %collective-permute-done.16 = f32[5248]{0:T(1024)S(1)} collective-permute-done((f32[5248]{0:T(1024)S(1)}, f32[5248]{0:T(1024)S(1)}, u32[]{:S(2)}, u32[]{:S(2)}) %collective-permute-start.16) | collective-permute-done | bytes 21024 | tf_op jit(solution)/shard_map/ppermute | solution.py:29
  142.4 1.7 %collective-permute-start.18 = (f32[5248]{0:T(1024)S(1)}, f32[5248]{0:T(1024)S(1)}, u32[]{:S(2)}, u32[]{:S(2)}) collective-permute-start(f32[5248]{0:T(1024)S(1)} %add_add_fusion.1), channel_id=1, source_target_pairs={{0,16},{2,18},{4,20},{6,22},{8,24},{10,26},{12,28},{14,30},{16,0},... | collective-permute-start | bytes 62984 | tf_op jit(solution)/shard_map/ppermute | solution.py:29
  145.5 2.3 %fusion.8 = (bf16[128,2560]{1,0:T(8,128)(2,1)}, bf16[128,2560]{1,0:T(8,128)(2,1)}) fusion(bf16[128,2560]{1,0:T(8,128)(2,1)S(1)} %copy-done.13, bf16[64,2560]{1,0:T(8,128)(2,1)S(1)} %collective-permute-done.23, bf16[64,2560]{1,0:T(8,128)(2,1)S(1)} %collective-permute-done.22, f32[128,2560]{1,0:T(8,128)S(1)} %copy-done.7, bf16[64,2560]{1,0:T(8,128)(2,1)S(1)} %slice-done.2, ...), kind=kLoop, calls=%fused_computation.21 | loop fusion | flops 11468800 | bytes 5242880 | tf_op jit(solution)/shard_map/convert_element_type | solution.py:309
  148.5 2.5 %psum.15 = f32[128]{0:T(128)S(1)} all-reduce(f32[128]{0:T(128)S(1)} %get-tuple-element.54), channel_id=1, replica_groups=mesh['dp'=16,'mp'=2] {'mp'}, use_global_device_ids=true, to_apply=%region_6.7 | all-reduce | flops 128 | bytes 1024 | tf_op jit(solution)/shard_map/psum | solution.py:326
  152.9 1.8 %multiply_multiply_fusion = f32[256,2560]{1,0:T(8,128)} fusion(f32[256,2560]{1,0:T(8,128)S(1)} %get-tuple-element.59, f32[2560]{0:T(1024)S(1)} %sqrt.11, f32[256]{0:T(256)S(1)} %divide_multiply_fusion), kind=kLoop, calls=%fused_computation.7 | loop fusion | flops 1310720 | bytes 5254144 | tf_op jit(solution)/shard_map/mul | solution.py:330
  (113 shorter events, 26.8 us)
Async XLA Ops:
  5.6 46.6 %collective-permute-start.4 = (bf16[256,2560]{1,0:T(8,128)(2,1)S(1)}, bf16[256,2560]{1,0:T(8,128)(2,1)S(1)}, u32[]{:S(2)}, u32[]{:S(2)}) collective-permute-start(bf16[256,2560]{1,0:T(8,128)(2,1)S(1)} %shard_map.110), channel_id=1, source_target_pairs={{0,4},{2,6},{4,0},{6,2},{8,12},{10,14},{12,8},{14,10},{16,20},{18,... | collective-permute-start | bytes 3932168 | tf_op jit(solution)/shard_map/ppermute | solution.py:29
  8.6 43.5 %collective-permute-start.3 = (bf16[256,2560]{1,0:T(8,128)(2,1)S(1)}, bf16[256,2560]{1,0:T(8,128)(2,1)S(1)}, u32[]{:S(2)}, u32[]{:S(2)}) collective-permute-start(bf16[256,2560]{1,0:T(8,128)(2,1)S(1)} %shard_map.110), channel_id=1, source_target_pairs={{0,2},{2,0},{4,6},{6,4},{8,10},{10,8},{12,14},{14,12},{16,18},{18,... | collective-permute-start | bytes 3932168 | tf_op jit(solution)/shard_map/ppermute | solution.py:29
  10.1 40.5 %collective-permute-start = (bf16[128,3072]{1,0:T(8,128)(2,1)S(1)}, bf16[128,3072]{1,0:T(8,128)(2,1)S(1)}, u32[]{:S(2)}, u32[]{:S(2)}) collective-permute-start(bf16[128,3072]{1,0:T(8,128)(2,1)S(1)} %copy-done.22), channel_id=1, source_target_pairs={{0,8},{2,10},{4,12},{6,14},{8,0},{10,2},{12,4},{14,6},{16,24},{18,... | collective-permute-start | bytes 2359304 | tf_op jit(solution)/shard_map/ppermute | solution.py:29
  11.7 40.5 %collective-permute-start.1 = (bf16[128,3072]{1,0:T(8,128)(2,1)S(1)}, bf16[128,3072]{1,0:T(8,128)(2,1)S(1)}, u32[]{:S(2)}, u32[]{:S(2)}) collective-permute-start(bf16[128,3072]{1,0:T(8,128)(2,1)S(1)} %copy-done.21), channel_id=1, source_target_pairs={{0,16},{2,18},{4,20},{6,22},{8,24},{10,26},{12,28},{14,30},{16,0},... | collective-permute-start | bytes 2359304 | tf_op jit(solution)/shard_map/ppermute | solution.py:29
  14.3 36.3 %collective-permute-start.2 = (bf16[128,512]{1,0:T(8,128)(2,1)S(1)}, bf16[128,512]{1,0:T(8,128)(2,1)S(1)}, u32[]{:S(2)}, u32[]{:S(2)}) collective-permute-start(bf16[128,512]{1,0:T(8,128)(2,1)S(1)} %copy-done.23), channel_id=1, source_target_pairs={{0,24},{2,26},{4,28},{6,30},{8,16},{10,18},{12,20},{14,22},{16,8},... | collective-permute-start | bytes 393224 | tf_op jit(solution)/shard_map/ppermute | solution.py:29
  56.8 5.6 %collective-permute-start.5 = (bf16[128,1536]{1,0:T(8,128)(2,1)}, bf16[128,1536]{1,0:T(8,128)(2,1)}, u32[]{:S(2)}, u32[]{:S(2)}) collective-permute-start(bf16[128,1536]{1,0:T(8,128)(2,1)} %get-tuple-element.35), channel_id=1, source_target_pairs={{0,1},{1,0},{2,3},{3,2},{4,5},{5,4},{6,7},{7,6},{8,9},{9,8},{10,11... | collective-permute-start | bytes 1179656 | tf_op jit(solution)/shard_map/ppermute | solution.py:29
  57.7 18.8 %collective-permute-start.6 = (bf16[64,2560]{1,0:T(8,128)(2,1)}, bf16[64,2560]{1,0:T(8,128)(2,1)S(1)}, u32[]{:S(2)}, u32[]{:S(2)}) collective-permute-start(bf16[64,2560]{1,0:T(8,128)(2,1)} %copy-done.11), channel_id=1, source_target_pairs={{0,16},{2,18},{4,20},{6,22},{8,24},{10,26},{12,28},{14,30},{16,0},... | collective-permute-start | bytes 983048 | tf_op jit(solution)/shard_map/ppermute | solution.py:29
  60.8 15.9 %collective-permute-start.7 = (bf16[64,2560]{1,0:T(8,128)(2,1)}, bf16[64,2560]{1,0:T(8,128)(2,1)S(1)}, u32[]{:S(2)}, u32[]{:S(2)}) collective-permute-start(bf16[64,2560]{1,0:T(8,128)(2,1)} %copy-done.10), channel_id=1, source_target_pairs={{0,8},{2,10},{4,12},{6,14},{8,0},{10,2},{12,4},{14,6},{16,24},{18,... | collective-permute-start | bytes 983048 | tf_op jit(solution)/shard_map/ppermute | solution.py:29
  60.8 17.0 %collective-permute-start.8 = (bf16[128,2560]{1,0:T(8,128)(2,1)}, bf16[128,2560]{1,0:T(8,128)(2,1)S(1)}, u32[]{:S(2)}, u32[]{:S(2)}) collective-permute-start(bf16[128,2560]{1,0:T(8,128)(2,1)} %copy-done.9), channel_id=1, source_target_pairs={{0,4},{2,6},{4,0},{6,2},{8,12},{10,14},{12,8},{14,10},{16,20},{18,... | collective-permute-start | bytes 1966088 | tf_op jit(solution)/shard_map/ppermute | solution.py:29
  61.4 16.7 %collective-permute-start.9 = (bf16[128,2560]{1,0:T(8,128)(2,1)}, bf16[128,2560]{1,0:T(8,128)(2,1)S(1)}, u32[]{:S(2)}, u32[]{:S(2)}) collective-permute-start(bf16[128,2560]{1,0:T(8,128)(2,1)} %copy-done.8), channel_id=1, source_target_pairs={{0,2},{2,0},{4,6},{6,4},{8,10},{10,8},{12,14},{14,12},{16,18},{18,... | collective-permute-start | bytes 1966088 | tf_op jit(solution)/shard_map/ppermute | solution.py:29
  82.8 27.2 %collective-permute-start.20 = (bf16[128,2560]{1,0:T(8,128)(2,1)S(1)}, bf16[128,2560]{1,0:T(8,128)(2,1)S(1)}, u32[]{:S(2)}, u32[]{:S(2)}) collective-permute-start(bf16[128,2560]{1,0:T(8,128)(2,1)S(1)} %get-tuple-element.48), channel_id=1, source_target_pairs={{0,8},{2,10},{4,12},{6,14},{8,0},{10,2},{12,4},{14,6},{16,24},{18,... | collective-permute-start | bytes 1966088 | tf_op jit(solution)/shard_map/ppermute | solution.py:29
  84.6 29.3 %collective-permute-start.11 = (bf16[256,2560]{1,0:T(8,128)(2,1)S(1)}, bf16[256,2560]{1,0:T(8,128)(2,1)S(1)}, u32[]{:S(2)}, u32[]{:S(2)}) collective-permute-start(bf16[256,2560]{1,0:T(8,128)(2,1)S(1)} %get-tuple-element.44), channel_id=1, source_target_pairs={{0,4},{2,6},{4,0},{6,2},{8,12},{10,14},{12,8},{14,10},{16,20},{18,... | collective-permute-start | bytes 3932168 | tf_op jit(solution)/shard_map/ppermute | solution.py:29
  86.1 29.5 %collective-permute-start.10 = (bf16[256,2560]{1,0:T(8,128)(2,1)S(1)}, bf16[256,2560]{1,0:T(8,128)(2,1)S(1)}, u32[]{:S(2)}, u32[]{:S(2)}) collective-permute-start(bf16[256,2560]{1,0:T(8,128)(2,1)S(1)} %get-tuple-element.41), channel_id=1, source_target_pairs={{0,2},{2,0},{4,6},{6,4},{8,10},{10,8},{12,14},{14,12},{16,18},{18,... | collective-permute-start | bytes 3932168 | tf_op jit(solution)/shard_map/ppermute | solution.py:29
  86.7 39.2 %collective-permute-start.21 = (bf16[128,2560]{1,0:T(8,128)(2,1)S(1)}, bf16[128,2560]{1,0:T(8,128)(2,1)S(1)}, u32[]{:S(2)}, u32[]{:S(2)}) collective-permute-start(bf16[128,2560]{1,0:T(8,128)(2,1)S(1)} %get-tuple-element.49), channel_id=1, source_target_pairs={{0,16},{2,18},{4,20},{6,22},{8,24},{10,26},{12,28},{14,30},{16,0},... | collective-permute-start | bytes 1966088 | tf_op jit(solution)/shard_map/ppermute | solution.py:29
  110.9 34.5 %collective-permute-start.22 = (bf16[64,2560]{1,0:T(8,128)(2,1)}, bf16[64,2560]{1,0:T(8,128)(2,1)S(1)}, u32[]{:S(2)}, u32[]{:S(2)}) collective-permute-start(bf16[64,2560]{1,0:T(8,128)(2,1)} %add_convert_fusion.3), channel_id=1, source_target_pairs={{0,16},{2,18},{4,20},{6,22},{8,24},{10,26},{12,28},{14,30},{16,0},... | collective-permute-start | bytes 983048 | tf_op jit(solution)/shard_map/ppermute | solution.py:29
  114.0 15.0 %collective-permute-start.13 = (bf16[128,2560]{1,0:T(8,128)(2,1)S(1)}, bf16[128,2560]{1,0:T(8,128)(2,1)S(1)}, u32[]{:S(2)}, u32[]{:S(2)}) collective-permute-start(bf16[128,2560]{1,0:T(8,128)(2,1)S(1)} %add_convert_fusion), channel_id=1, source_target_pairs={{0,2},{2,0},{4,6},{6,4},{8,10},{10,8},{12,14},{14,12},{16,18},{18,... | collective-permute-start | bytes 1966088 | tf_op jit(solution)/shard_map/ppermute | solution.py:29
  115.8 13.4 %collective-permute-start.12 = (bf16[128,2560]{1,0:T(8,128)(2,1)S(1)}, bf16[128,2560]{1,0:T(8,128)(2,1)S(1)}, u32[]{:S(2)}, u32[]{:S(2)}) collective-permute-start(bf16[128,2560]{1,0:T(8,128)(2,1)S(1)} %add_convert_fusion.1), channel_id=1, source_target_pairs={{0,4},{2,6},{4,0},{6,2},{8,12},{10,14},{12,8},{14,10},{16,20},{18,... | collective-permute-start | bytes 1966088 | tf_op jit(solution)/shard_map/ppermute | solution.py:29
  126.7 18.7 %collective-permute-start.23 = (bf16[64,2560]{1,0:T(8,128)(2,1)}, bf16[64,2560]{1,0:T(8,128)(2,1)S(1)}, u32[]{:S(2)}, u32[]{:S(2)}) collective-permute-start(bf16[64,2560]{1,0:T(8,128)(2,1)} %add_convert_fusion.2), channel_id=1, source_target_pairs={{0,8},{2,10},{4,12},{6,14},{8,0},{10,2},{12,4},{14,6},{16,24},{18,... | collective-permute-start | bytes 983048 | tf_op jit(solution)/shard_map/ppermute | solution.py:29
  134.5 3.9 %collective-permute-start.15 = (f32[5248]{0:T(1024)S(1)}, f32[5248]{0:T(1024)S(1)}, u32[]{:S(2)}, u32[]{:S(2)}) collective-permute-start(f32[5248]{0:T(1024)S(1)} %pad_maximum_fusion.3), channel_id=1, source_target_pairs={{0,4},{2,6},{4,0},{6,2},{8,12},{10,14},{12,8},{14,10},{16,20},{18,... | collective-permute-start | bytes 62984 | tf_op jit(solution)/shard_map/ppermute | solution.py:29
  135.5 4.9 %collective-permute-start.16 = (f32[5248]{0:T(1024)S(1)}, f32[5248]{0:T(1024)S(1)}, u32[]{:S(2)}, u32[]{:S(2)}) collective-permute-start(f32[5248]{0:T(1024)S(1)} %pad_maximum_fusion.3), channel_id=1, source_target_pairs={{0,6},{2,4},{4,2},{6,0},{8,14},{10,12},{12,10},{14,8},{16,22},{18,... | collective-permute-start | bytes 62984 | tf_op jit(solution)/shard_map/ppermute | solution.py:29
  137.2 3.8 %collective-permute-start.14 = (f32[5248]{0:T(1024)S(1)}, f32[5248]{0:T(1024)S(1)}, u32[]{:S(2)}, u32[]{:S(2)}) collective-permute-start(f32[5248]{0:T(1024)S(1)} %pad_maximum_fusion.3), channel_id=1, source_target_pairs={{0,2},{2,0},{4,6},{6,4},{8,10},{10,8},{12,14},{14,12},{16,18},{18,... | collective-permute-start | bytes 62984 | tf_op jit(solution)/shard_map/ppermute | solution.py:29
  141.0 6.8 %collective-permute-start.19 = (f32[5248]{0:T(1024)S(1)}, f32[5248]{0:T(1024)S(1)}, u32[]{:S(2)}, u32[]{:S(2)}) collective-permute-start(f32[5248]{0:T(1024)S(1)} %add_add_fusion.1), channel_id=1, source_target_pairs={{0,24},{2,26},{4,28},{6,30},{8,16},{10,18},{12,20},{14,22},{16,8},... | collective-permute-start | bytes 62984 | tf_op jit(solution)/shard_map/ppermute | solution.py:29
  142.4 5.4 %collective-permute-start.18 = (f32[5248]{0:T(1024)S(1)}, f32[5248]{0:T(1024)S(1)}, u32[]{:S(2)}, u32[]{:S(2)}) collective-permute-start(f32[5248]{0:T(1024)S(1)} %add_add_fusion.1), channel_id=1, source_target_pairs={{0,16},{2,18},{4,20},{6,22},{8,24},{10,26},{12,28},{14,30},{16,0},... | collective-permute-start | bytes 62984 | tf_op jit(solution)/shard_map/ppermute | solution.py:29
  144.1 3.8 %collective-permute-start.17 = (f32[5248]{0:T(1024)S(1)}, f32[5248]{0:T(1024)S(1)}, u32[]{:S(2)}, u32[]{:S(2)}) collective-permute-start(f32[5248]{0:T(1024)S(1)} %add_add_fusion.1), channel_id=1, source_target_pairs={{0,8},{2,10},{4,12},{6,14},{8,0},{10,2},{12,4},{14,6},{16,24},{18,... | collective-permute-start | bytes 62984 | tf_op jit(solution)/shard_map/ppermute | solution.py:29
  (27 other events, 209.4 us)

commit v8 on v7

--- a/solution.py
+++ b/solution.py
@@ -10,7 +10,6 @@
 TRAIN_STEP = 3
 INNER_BITS = 2
 EAGER = pl.CostEstimate(flops=0, bytes_accessed=0, transcendentals=0)
-PIECES = ((0, 0), (0, 1), (1, 0), (3, 0), (2, 1), (3, 1), (2, 0), (1, 1))
 
 
 def gelu_parts(values):
@@ -93,11 +92,10 @@
 
 def first_stage(out_grad, gate_pre, up_pre, place, rows):
     tokens, units = gate_pre.shape
-    quarter = rows // 2
-    share_width = 4 * rows
+    half = units // 2
     step = 32
 
-    def kernel(place, source_hbm, gate_hbm, up_hbm, own, hidden, message1, message2, message3, source, gate, up, sems):
+    def kernel(place, source_hbm, gate_hbm, up_hbm, own, left, right, message1, message2, message3, source, gate, up, sems):
         copies = [
             pltpu.make_async_copy(there, here, sems.at[n])
             for n, (there, here) in enumerate(((gate_hbm, gate), (up_hbm, up), (source_hbm, source)))
@@ -106,9 +104,8 @@
             copy.start()
         me, core = place[0], place[1]
 
-        def column(k, block, half):
-            at = (me ^ (4 * k + block)) * rows + half * quarter
-            return pl.ds(pl.multiple_of(at, quarter), quarter)
+        def block(k, j):
+            return pl.ds(pl.multiple_of((me ^ (4 * k + j)) * rows, rows), rows)
 
         copies[0].wait()
         copies[1].wait()
@@ -118,39 +115,32 @@
             here = pl.ds(pl.multiple_of(i * step, step), step)
             activated, _ = gelu_parts(gate[here, :].astype(jnp.float32))
             value = (activated * up[here, :].astype(jnp.float32)).astype(jnp.bfloat16)
-            hidden[here, :] = value
-            message1[here, :units] = value
-            message2[here, :units] = value
+            left[here, :] = value[:, :half]
+            right[here, :] = value[:, half:]
+            message1[here, :half] = value[:, :half]
+            message2[here, :half] = value[:, :half]
 
         copies[2].wait()
-        for p, (block, half) in enumerate(PIECES):
-            own[:, p * quarter : (p + 1) * quarter] = source[:, column(0, block, half)]
-        for k, target, base in ((1, message1, units), (2, message2, units), (3, message3, 0)):
-            for p in range(4):
-                block = jnp.where(core == 0, PIECES[p][0], PIECES[p + 4][0])
-                half = jnp.where(core == 0, PIECES[p][1], PIECES[p + 4][1])
-                target[:, base + p * quarter : base + (p + 1) * quarter] = source[:, column(k, block, half)]
-
-    wide = jax.ShapeDtypeStruct((tokens, units + share_width // 2), jnp.bfloat16)
+        for j in range(4):
+            own[:, j * rows : (j + 1) * rows] = source[:, block(0, j)]
+        for k, target, base in ((1, message1, half), (2, message2, half), (3, message3, 0)):
+            for j in range(2):
+                target[:, base + j * rows : base + (j + 1) * rows] = source[:, block(k, 2 * core + j)]
+
     vmem = pl.BlockSpec(memory_space=pltpu.VMEM)
-    return pl.pallas_call(
-        kernel,
-        out_shape=[
-            jax.ShapeDtypeStruct((tokens, share_width), jnp.bfloat16),
-            jax.ShapeDtypeStruct((tokens, units), jnp.bfloat16),
-            wide,
-            wide,
-            jax.ShapeDtypeStruct((tokens, share_width // 2), jnp.bfloat16),
-        ],
+    widths = [4 * rows, half, half, half + 2 * rows, half + 2 * rows, 2 * rows]
+    return pl.pallas_call(
+        kernel,
+        out_shape=[jax.ShapeDtypeStruct((tokens, width), jnp.bfloat16) for width in widths],
         in_specs=[pl.BlockSpec(memory_space=pltpu.SMEM)] + [pl.BlockSpec(memory_space=pltpu.HBM)] * 3,
-        out_specs=[vmem] * 5,
+        out_specs=[vmem] * len(widths),
         scratch_shapes=[
             pltpu.VMEM(out_grad.shape, jnp.bfloat16),
             pltpu.VMEM(gate_pre.shape, jnp.bfloat16),
             pltpu.VMEM(up_pre.shape, jnp.bfloat16),
             pltpu.SemaphoreType.DMA((3,)),
         ],
-        compiler_params=pltpu.CompilerParams(vmem_limit_bytes=56 << 20),
+        compiler_params=pltpu.CompilerParams(vmem_limit_bytes=16 << 20),
         cost_estimate=EAGER,
     )(place, out_grad, gate_pre, up_pre)
 
@@ -180,46 +170,88 @@
     )(*sources)
 
 
-def products(share, groups, tile):
-    units = min(piece.shape[1] for piece in groups[0][0])
-    pieces = [piece for group in groups for piece in group[0]]
-    depths = [sum(rows for _, _, rows in group[1]) for group in groups]
-    bounds = [output for group in groups for output in group[2]]
+def assemble(own, mine, theirs, place, rows):
+    tokens = own.shape[0]
+
+    def kernel(place, own, mine, theirs, share):
+        share[:tokens, :] = own[...]
+        for k in range(3):
+            here = pl.ds((k + 1) * tokens, tokens)
+            half = slice(k * 2 * rows, (k + 1) * 2 * rows)
+            a, b = mine[:, half], theirs[:, half]
+            share[here, : 2 * rows] = jnp.where(place[1] == 0, a, b)
+            share[here, 2 * rows :] = jnp.where(place[1] == 0, b, a)
+
+    vmem = pl.BlockSpec(memory_space=pltpu.VMEM)
+    return pl.pallas_call(
+        kernel,
+        out_shape=jax.ShapeDtypeStruct((4 * tokens, 4 * rows), jnp.bfloat16),
+        in_specs=[pl.BlockSpec(memory_space=pltpu.SMEM), vmem, vmem, vmem],
+        out_specs=vmem,
+        compiler_params=pltpu.CompilerParams(vmem_limit_bytes=8 << 20),
+        cost_estimate=EAGER,
+    )(place, own, mine, theirs)
+
+
+def add_tail(part, arrived):
+    rows = part.shape[0]
+
+    def kernel(part, arrived, out):
+        out[...] = (part[...] + arrived[rows:, :].astype(jnp.float32)).astype(jnp.bfloat16)
+
+    vmem = pl.BlockSpec(memory_space=pltpu.VMEM)
+    return pl.pallas_call(
+        kernel,
+        out_shape=jax.ShapeDtypeStruct(part.shape, jnp.bfloat16),
+        in_specs=[vmem, vmem],
+        out_specs=vmem,
+        compiler_params=pltpu.CompilerParams(vmem_limit_bytes=8 << 20),
+        cost_estimate=EAGER,
+    )(part, arrived)
+
+
+def products(share, groups, steps):
+    pieces = [(piece, group[1]) for group in groups for piece in group[0]]
+    bounds = [(output, group[1]) for group in groups for output in group[2]]
 
     def kernel(*refs):
         share_ref, ins = refs[0], refs[1 : 1 + len(pieces)]
         outs, stacks = refs[1 + len(pieces) : -len(groups)], refs[-len(groups) :]
         n = o = 0
-        for (own, layout, outputs, over_rows), stack in zip(groups, stacks):
+        for (own, _, outputs, over_rows), stack in zip(groups, stacks):
             at = 0
-            for piece, first, rows in layout:
-                stack[at : at + rows, :] = ins[n + piece][first : first + rows, :]
-                at += rows
-            for begin, end, kind in outputs:
+            for piece in own:
+                stack[at : at + piece.shape[0], :] = ins[n][...]
+                at += piece.shape[0]
+                n += 1
+            for ranges, kind in outputs:
                 if over_rows:
+                    side = jnp.concatenate([share_ref[:, begin:end] for begin, end in ranges], axis=1)
                     value = lax.dot_general(
-                        share_ref[:, begin:end],
-                        stack[...],
-                        (((0,), (0,)), ((), ())),
-                        preferred_element_type=jnp.float32,
+                        side, stack[...], (((0,), (0,)), ((), ())), preferred_element_type=jnp.float32
                     )
                 else:
-                    value = jnp.dot(share_ref[begin:end, :], stack[...], preferred_element_type=jnp.float32)
+                    side = jnp.concatenate([share_ref[begin:end, :] for begin, end in ranges], axis=0)
+                    value = jnp.dot(side, stack[...], preferred_element_type=jnp.float32)
                 outs[o][...] = value.astype(kind)
                 o += 1
-            n += len(own)
-
-    return pl.pallas_call(
-        kernel,
-        grid=(units // tile,),
-        out_shape=[jax.ShapeDtypeStruct((end - begin, units), kind) for begin, end, kind in bounds],
+
+    def height(ranges):
+        return sum(end - begin for begin, end in ranges)
+
+    return pl.pallas_call(
+        kernel,
+        grid=(steps,),
+        out_shape=[jax.ShapeDtypeStruct((height(ranges), columns), kind) for (ranges, kind), columns in bounds],
         in_specs=[pl.BlockSpec(share.shape, lambda i: (0, 0))]
-        + [pl.BlockSpec((piece.shape[0], tile), lambda i: (0, i)) for piece in pieces],
-        out_specs=[pl.BlockSpec((end - begin, tile), lambda i: (0, i)) for begin, end, _ in bounds],
-        scratch_shapes=[pltpu.VMEM((depth, tile), jnp.bfloat16) for depth in depths],
+        + [pl.BlockSpec((piece.shape[0], columns // steps), lambda i: (0, i)) for piece, columns in pieces],
+        out_specs=[pl.BlockSpec((height(ranges), columns // steps), lambda i: (0, i)) for (ranges, _), columns in bounds],
+        scratch_shapes=[
+            pltpu.VMEM((sum(piece.shape[0] for piece in group[0]), group[1] // steps), jnp.bfloat16) for group in groups
+        ],
         compiler_params=pltpu.CompilerParams(vmem_limit_bytes=14 << 20),
         cost_estimate=EAGER,
-    )(share, *pieces)
+    )(share, *[piece for piece, _ in pieces])
 
 
 def staged_products(out_grad, gate_pre, up_pre, down_weight):
@@ -227,68 +259,79 @@
     me, core = lax.axis_index("dp"), lax.axis_index("mp")
     tokens, units = gate_pre.shape
     rows = down_weight.shape[0]
-    q, t = rows // 2, tokens // 2
+    q, t, half = rows // 2, tokens // 2, units // 2
+    steps = units // 512
+    barrier = lax.optimization_barrier
     place = jnp.stack([me, core]).astype(jnp.int32)
-    own, hidden, message1, message2, message3 = first_stage(out_grad, gate_pre, up_pre, place, rows)
-
-    down_weight, message1 = lax.optimization_barrier((down_weight, message1))
-    message1, message2, message3 = flip(message1, z_bit), flip(message2, w_bit), flip(message3, z_bit | w_bit)
-    whole, extra, every = (0, units), (units, 2 * rows), (0, tokens)
-    (to_peers,) = cut([down_weight], [(0, (0, rows), whole, 0, 0)], [(rows, units)])
-    weight1, weight2 = flip(to_peers, x_bit), flip(to_peers, y_bit)
-    to_w, to_z, mine, to_y, to_x = cut(
-        [message1, message2, message3, weight1, weight2],
+    own, left, right, message1, message2, message3 = first_stage(out_grad, gate_pre, up_pre, place, rows)
+
+    down_weight, message1 = barrier((down_weight, message1))
+    left1, left2, message3 = flip(message1, z_bit), flip(message2, w_bit), flip(message3, z_bit | w_bit)
+    weight1, weight2 = flip(down_weight, x_bit), flip(down_weight, y_bit)
+
+    left1, left2, message3, weight1, weight2, right = barrier((left1, left2, message3, weight1, weight2, right))
+    left3 = flip(left2, z_bit)
+    right2 = flip(right, w_bit)
+    extra, every = (half, 2 * rows), (0, tokens)
+    mine, to_y, to_x = cut(
+        [left1, left2, message3, weight1, weight2],
         [
-            (0, (0, t), whole, 0, 0),
-            (1, (t, t), whole, 1, 0),
-            (0, every, extra, 2, 0),
-            (1, every, extra, 2, 2 * rows),
-            (2, every, (0, 2 * rows), 2, 4 * rows),
-            (3, (0, q), whole, 3, 0),
-            (4, (q, q), whole, 4, 0),
+            (0, every, extra, 0, 0),
+            (1, every, extra, 0, 2 * rows),
+            (2, every, (0, 2 * rows), 0, 4 * rows),
+            (3, (0, q), (0, units), 1, 0),
+            (4, (q, q), (0, units), 2, 0),
         ],
-        [(t, units), (t, units), (tokens, 6 * rows), (q, units), (q, units)],
+        [(tokens, 6 * rows), (q, units), (q, units)],
     )
     theirs = flip(mine, 1, "mp")
-    hidden3a, hidden3b = flip(to_w, w_bit), flip(to_z, z_bit)
     weight3a, weight3b = flip(to_y, y_bit), flip(to_x, x_bit)
-
-    def features(k):
-        a, b = mine[:, (k - 1) * 2 * rows : k * 2 * rows], theirs[:, (k - 1) * 2 * rows : k * 2 * rows]
-        return jnp.concatenate([jnp.where(core == 0, a, b), jnp.where(core == 0, b, a)], axis=1)
-
-    peers = [own] + [features(k) for k in range(1, 4)]
-    share = jnp.concatenate([peers[k][h * t : (h + 1) * t] for k, h in PIECES], axis=0)
-
-    def layout(size):
-        return [(0, 0, 2 * size), (1, 0, size), (3, 0, size), (2, size, size), (4, 0, size), (2, 0, size), (1, size, size)]
+    share = assemble(own, mine, theirs, place, rows)
+
+    left3, right2, share, weight3a, weight3b, right = barrier((left3, right2, share, weight3a, weight3b, right))
+    right1, right3 = flip(right, z_bit), flip(right2, z_bit)
+
+    def low_sent(size):
+        return [(2 * size, 3 * size), (6 * size, 7 * size)]
+
+    def high_sent(size):
+        return [(5 * size, 6 * size), (7 * size, 8 * size)]
 
     def sent(size):
-        return [(2 * size, 4 * size, jnp.bfloat16), (4 * size, 6 * size, jnp.bfloat16)]
+        return [(low_sent(size), jnp.bfloat16), (high_sent(size), jnp.bfloat16)]
 
     def kept(size):
-        return [(0, 2 * size, jnp.float32), (6 * size, 7 * size, jnp.float32), (7 * size, 8 * size, jnp.float32)]
+        ranges = [(0, 2 * size)], [(4 * size, 5 * size)], [(3 * size, 4 * size)]
+        return [(r, jnp.float32) for r in ranges]
+
+    lefts = [left, left1, left2, left3]
+    weights = [down_weight, weight1, weight2, weight3a, weight3b]
+    left_to_x, left_to_y = products(share, [(lefts, half, sent(q), True)], steps)
+    left_from_x, left_from_y = flip(left_to_x, x_bit), flip(left_to_y, y_bit)
+    share, _ = barrier((share, left_to_x))
+    to_z, to_w, *left_kept = products(
+        share, [(weights, units, sent(t), False), (lefts, half, kept(q), True)], steps
+    )
+
+    right1, right3, to_z, to_w, share = barrier((right1, right3, to_z, to_w, share))
+    from_z, from_w = flip(to_z, z_bit), flip(to_w, w_bit)
+    rights = [right, right1, right2, right3]
+    right_to_x, right_to_y = products(share, [(rights, half, sent(q), True)], steps)
+    right_from_x, right_from_y = flip(right_to_x, x_bit), flip(right_to_y, y_bit)
+    share, _ = barrier((share, right_to_x))
+    parts = products(share, [(rights, half, kept(q), True), (weights, units, kept(t), False)], steps)
 
     def finish(parts, from_low, from_high, size, low, high):
-        send, keep = jnp.bfloat16, jnp.float32
         own_part, a_part, b_part = parts
-        last_a = flip((a_part + from_low[size:].astype(keep)).astype(send), high)
-        last_b = flip((b_part + from_high[size:].astype(keep)).astype(send), low)
-        kept = own_part + jnp.concatenate([from_low[:size], from_high[:size]], axis=0).astype(keep)
-        return kept + jnp.concatenate([last_a, last_b], axis=0).astype(keep)
-
-    hiddens = [hidden, message1, message2, hidden3a, hidden3b]
-    weights = [down_weight, weight1, weight2, weight3a, weight3b]
-    to_x, to_y, to_z, to_w = products(
-        share, [(hiddens, layout(t), sent(q), True), (weights, layout(q), sent(t), False)], 512
-    )
-    from_x, from_y = flip(to_x, x_bit), flip(to_y, y_bit)
-    from_z, from_w = flip(to_z, z_bit), flip(to_w, w_bit)
-    share, _ = lax.optimization_barrier((share, to_x))
-    parts = products(share, [(hiddens, layout(t), kept(q), True), (weights, layout(q), kept(t), False)], 512)
-    grad = finish(parts[:3], from_x, from_y, q, x_bit, y_bit)
+        last_a = flip(add_tail(a_part, from_low), high)
+        last_b = flip(add_tail(b_part, from_high), low)
+        arrived = jnp.concatenate([from_low[:size], from_high[:size]], axis=0).astype(jnp.float32)
+        return own_part + arrived + jnp.concatenate([last_a, last_b], axis=0).astype(jnp.float32)
+
+    left_grad = finish(left_kept, left_from_x, left_from_y, q, x_bit, y_bit)
+    right_grad = finish(parts[:3], right_from_x, right_from_y, q, x_bit, y_bit)
     hidden_grad = finish(parts[3:], from_z, from_w, t, z_bit, w_bit)
-    return grad, hidden_grad
+    return jnp.concatenate([left_grad, right_grad], axis=1), hidden_grad
 
 
 def local(out_grad, gate_pre, up_pre, down_weight, row_moment, col_moment):

time: 156 us -> 165 us (1.058)
  starting transfers between devices: 28.1 us -> 44 us
  waiting for transfers between devices: 86.7 us -> 80.6 us
  other arithmetic: 10.7 us -> 8.73 us
    ppermute x24 -> x30, starting transfers between devices: 28.1 us -> 44 us  [flip(): return lax.ppermute(value, axis, [(i, i ^ bits) for i in range(size)])]
    ppermute x24 -> x30, waiting for transfers between devices: 86.7 us -> 80.6 us  [flip(): return lax.ppermute(value, axis, [(i, i ^ bits) for i in range(size)])]
    convert_element_type x4 -> x0, other arithmetic: 1.96 us -> none  [the longest x2 0.98 us: finish(): last_a = flip((a_part + from_low[size:].astype(keep)).astype(send), high)]
    reduce_sum x1, other arithmetic: 0.57 us -> 2.38 us  [local(): col_part = jnp.sum(squares, axis=0)]
    unnamed x49 -> x36, local copies, waits for them, and re-layouts: 4.74 us -> 5.57 us
    pallas_call x3 -> x12, Pallas kernels: 14.8 us -> 15.6 us  [the longest x4 12.9 us: products(): pl.pallas_call(kernel, grid=(steps,), out_shape=[jax.ShapeDtypeStruct((he...]
  transfers between devices with their start and end apart: 24 -> 30, of which waited for: 16 -> 13; matrix products, arithmetic and copies ran while one was open for 6% -> 4% of each run, Pallas kernels for 4% -> 8%
where the time goes in v8:
time: 165 us
  waiting for transfers between devices  80.6 us (49%)
  starting transfers between devices  44 us (27%)
  Pallas kernels  16.1 us (10%)
  other arithmetic  8.73 us (5%)
  local copies, waits for them, and re-layouts  6.94 us (4%)
  blocking collectives  4.93 us (3%)
  between operations  3.51 us (2%)
    ppermute x30, waiting for transfers between devices, flip(): return lax.ppermute(value, axis, [(i, i ^ bits) for i in range(size)])  80.6 us
    ppermute x30, starting transfers between devices, flip(): return lax.ppermute(value, axis, [(i, i ^ bits) for i in range(size)])  44 us
    pallas_call x4, Pallas kernels, products(): pl.pallas_call(kernel, grid=(steps,), out_shape=[jax.ShapeDtypeStruct((he...  12.9 us
    unnamed x36, local copies, waits for them, and re-layouts  5.57 us
  transfers between devices with their start and end apart: 30, of which 13 were waited for; matrix products, arithmetic and copies ran while one was open for 4% of the time, Pallas kernels for 8%

profile of v8, /device:TPU:0, one launch (start us, length us, event | category | flops | bytes accessed | tf_op | source)
XLA Modules:
  0.0 164.8 jit_solution(8629052942238721056)
XLA Ops:
  4.2 1.7 %shard_map.109 = (bf16[128,1024]{1,0:T(8,128)(2,1)S(1)}, bf16[128,1280]{1,0:T(8,128)(2,1)S(1)}, bf16[128,1280]{1,0:T(8,128)(2,1)S(1)}, bf16[128,1792]{1,0:T(8,12...) custom-call(s32[2]{0:T(128)S(1)} %pad_add_fusion.place, bf16[128,4096]{1,0:T(8,128)(2,1)S(1)} %copy-done.9, ...), custom_call_target="tpu_custom_call" | custom-call | tf_op jit(solution)/shard_map/pallas_call | solution.py:132
  5.9 3.0 %collective-permute-start.4 = (bf16[256,2560]{1,0:T(8,128)(2,1)S(1)}, bf16[256,2560]{1,0:T(8,128)(2,1)S(1)}, u32[]{:S(2)}, u32[]{:S(2)}) collective-permute-start(bf16[256,2560]{1,0:T(8,128)(2,1)S(1)} %copy-done), channel_id=1, source_target_pairs={{0,4},{2,6},{4,0},{6,2},{8,12},{10,14},{12,8},{14,10},{16,20},{18,... | collective-permute-start | bytes 3932168 | tf_op jit(solution)/shard_map/ppermute | solution.py:28
  12.0 2.6 %collective-permute-start.1 = (bf16[128,1792]{1,0:T(8,128)(2,1)S(1)}, bf16[128,1792]{1,0:T(8,128)(2,1)S(1)}, u32[]{:S(2)}, u32[]{:S(2)}) collective-permute-start(bf16[128,1792]{1,0:T(8,128)(2,1)S(1)} %get-tuple-element.53), channel_id=1, source_target_pairs={{0,16},{2,18},{4,20},{6,22},{8,24},{10,26},{12,28},{14,30},{16,0},... | collective-permute-start | bytes 1376264 | tf_op jit(solution)/shard_map/ppermute | solution.py:28
  14.9 22.1 %collective-permute-done.2.refs_2_ = bf16[128,512]{1,0:T(8,128)(2,1)S(1)} collective-permute-done((bf16[128,512]{1,0:T(8,128)(2,1)S(1)}, bf16[128,512]{1,0:T(8,128)(2,1)S(1)}, u32[]{:S(2)}, u32[]{:S(2)}) %collective-permute-start.2) | collective-permute-done | bytes 131104 | tf_op jit(solution)/shard_map/ppermute | solution.py:28
  43.4 2.6 %collective-permute-start.6 = (bf16[128,1280]{1,0:T(8,128)(2,1)S(1)}, bf16[128,1280]{1,0:T(8,128)(2,1)S(1)}, u32[]{:S(2)}, u32[]{:S(2)}) collective-permute-start(bf16[128,1280]{1,0:T(8,128)(2,1)S(1)} %get-tuple-element.78.refs_1_), channel_id=1, source_target_pairs={{0,16},{2,18},{4,20},{6,22},{8,24},{10,26},{12,28},{14,30},{16,0},... | collective-permute-start | bytes 983048 | tf_op jit(solution)/shard_map/ppermute | solution.py:28
  46.6 12.0 %collective-permute-done.6.refs_3_ = bf16[128,1280]{1,0:T(8,128)(2,1)S(1)} collective-permute-done((bf16[128,1280]{1,0:T(8,128)(2,1)S(1)}, bf16[128,1280]{1,0:T(8,128)(2,1)S(1)}, u32[]{:S(2)}, u32[]{:S(2)}) %collective-permute-start.6) | collective-permute-done | bytes 327712 | tf_op jit(solution)/shard_map/ppermute | solution.py:28
  59.4 2.7 %collective-permute-start.14 = (bf16[128,1280]{1,0:T(8,128)(2,1)S(1)}, bf16[128,1280]{1,0:T(8,128)(2,1)S(1)}, u32[]{:S(2)}, u32[]{:S(2)}) collective-permute-start(bf16[128,1280]{1,0:T(8,128)(2,1)S(1)} %get-tuple-element.78.refs_1_), channel_id=1, source_target_pairs={{0,8},{2,10},{4,12},{6,14},{8,0},{10,2},{12,4},{14,6},{16,24},{18,... | collective-permute-start | bytes 983048 | tf_op jit(solution)/shard_map/ppermute | solution.py:28
  62.2 2.0 %shard_map.112 = (bf16[256,1280]{1,0:T(8,128)(2,1)S(1)}, bf16[256,1280]{1,0:T(8,128)(2,1)S(1)}) custom-call(bf16[512,1024]{1,0:T(8,128)(2,1)S(1)} %shard_map.111.refs_0_, bf16[128,1280]{1,0:T(8,128)(2,1)S(1)} %get-tuple-element.68.refs_1_.refs_6_, bf16[128,1792]{1,0:T(8,128)(2,1)S(1)} %collective-permute-done.refs_0_.refs_2_.refs_7_, ...), custom_call_target="tpu_custom_call" | custom-call | tf_op jit(solution)/shard_map/pallas_call | solution.py:242
  64.8 2.9 %collective-permute-start.11 = (bf16[256,1280]{1,0:T(8,128)(2,1)S(1)}, bf16[256,1280]{1,0:T(8,128)(2,1)S(1)}, u32[]{:S(2)}, u32[]{:S(2)}) collective-permute-start(bf16[256,1280]{1,0:T(8,128)(2,1)S(1)} %get-tuple-element.75), channel_id=1, source_target_pairs={{0,4},{2,6},{4,0},{6,2},{8,12},{10,14},{12,8},{14,10},{16,20},{18,... | collective-permute-start | bytes 1966088 | tf_op jit(solution)/shard_map/ppermute | solution.py:28
  67.7 3.8 %shard_map.113 = (bf16[128,2560]{1,0:T(8,128)(2,1)S(1)}, bf16[128,2560]{1,0:T(8,128)(2,1)S(1)}, f32[256,1280]{1,0:T(8,128)S(1)}, f32[128,1280]{1,0:T(8,128)S(1)}, f32[128,1280]{1,0:T(8,128)S(1)}) custom-call(bf16[512,1024]{1,0:T(8,128)(2,1)S(1)} %shard_map.111.refs_0_, bf16[256,2560]{1,0:T(8,128)(2,1)S(1)} %copy-done, ...), custom_call_target="tpu_custom_call" | custom-call | tf_op jit(solution)/shard_map/pallas_call | solution.py:242
  71.6 4.1 %collective-permute-done.15.refs_4_ = bf16[128,1280]{1,0:T(8,128)(2,1)S(1)} collective-permute-done((bf16[128,1280]{1,0:T(8,128)(2,1)S(1)}, bf16[128,1280]{1,0:T(8,128)(2,1)S(1)}, u32[]{:S(2)}, u32[]{:S(2)}) %collective-permute-start.15) | collective-permute-done | bytes 327712 | tf_op jit(solution)/shard_map/ppermute | solution.py:28
  75.7 2.0 %shard_map.116 = (bf16[256,1280]{1,0:T(8,128)(2,1)S(1)}, bf16[256,1280]{1,0:T(8,128)(2,1)S(1)}) custom-call(bf16[512,1024]{1,0:T(8,128)(2,1)S(1)} %shard_map.111.refs_0_, bf16[128,1280]{1,0:T(8,128)(2,1)S(1)} %get-tuple-element.78.refs_1_, bf16[128,1280]{1,0:T(8,128)(2,1)S(1)} %collective-permute-done.14.refs_2_, ...), custom_call_target="tpu_custom_call" | custom-call | tf_op jit(solution)/shard_map/pallas_call | solution.py:242
  83.3 1.8 %collective-permute-start.26 = (bf16[128,2560]{1,0:T(8,128)(2,1)S(1)}, bf16[128,2560]{1,0:T(8,128)(2,1)S(1)}, u32[]{:S(2)}, u32[]{:S(2)}) collective-permute-start(bf16[128,2560]{1,0:T(8,128)(2,1)S(1)} %get-tuple-element.92), channel_id=1, source_target_pairs={{0,8},{2,10},{4,12},{6,14},{8,0},{10,2},{12,4},{14,6},{16,24},{18,... | collective-permute-start | bytes 1966088 | tf_op jit(solution)/shard_map/ppermute | solution.py:28
  85.1 10.3 %collective-permute-done.17.arrived = bf16[256,1280]{1,0:T(8,128)(2,1)S(1)} collective-permute-done((bf16[256,1280]{1,0:T(8,128)(2,1)S(1)}, bf16[256,1280]{1,0:T(8,128)(2,1)S(1)}, u32[]{:S(2)}, u32[]{:S(2)}) %collective-permute-start.17) | collective-permute-done | bytes 655392 | tf_op jit(solution)/shard_map/ppermute | solution.py:28
  95.4 3.5 %collective-permute-start.27 = (bf16[128,2560]{1,0:T(8,128)(2,1)S(1)}, bf16[128,2560]{1,0:T(8,128)(2,1)S(1)}, u32[]{:S(2)}, u32[]{:S(2)}) collective-permute-start(bf16[128,2560]{1,0:T(8,128)(2,1)S(1)} %get-tuple-element.93), channel_id=1, source_target_pairs={{0,16},{2,18},{4,20},{6,22},{8,24},{10,26},{12,28},{14,30},{16,0},... | collective-permute-start | bytes 1966088 | tf_op jit(solution)/shard_map/ppermute | solution.py:28
  99.0 5.0 %shard_map.117 = (f32[256,1280]{1,0:T(8,128)S(1)}, f32[128,1280]{1,0:T(8,128)S(1)}, f32[128,1280]{1,0:T(8,128)S(1)}, f32[128,2560]{1,0:T(8,128)S(1)}, f32[64,2560]{1,0:T(8,128)S(1)}, /*index=5*/f32[64,2560]{1,0:T(8,128)S(1)}) custom-call(bf16[512,1024]{1,0:T(8,128)(2,1)S(1)} %shard_map.111.refs_0_, bf16[128,1280]{1,0:T(8,128)(2,1)S(1)} %get-tuple-element.78.refs_1_, ...), custom_call_target="tpu_custom_call" | custom-call | tf_op jit(solution)/shard_map/pallas_call | solution.py:242
  109.2 25.0 %collective-permute-done.27.arrived = bf16[128,2560]{1,0:T(8,128)(2,1)S(1)} collective-permute-done((bf16[128,2560]{1,0:T(8,128)(2,1)S(1)}, bf16[128,2560]{1,0:T(8,128)(2,1)S(1)}, u32[]{:S(2)}, u32[]{:S(2)}) %collective-permute-start.27) | collective-permute-done | bytes 655392 | tf_op jit(solution)/shard_map/ppermute | solution.py:28
  136.1 2.5 %psum.14 = f32[256]{0:T(256)S(1)} all-reduce(f32[256]{0:T(256)S(1)} %add_reduce_fusion), channel_id=1, replica_groups=mesh['dp'=16,'mp'=2] {'mp'}, use_global_device_ids=true, to_apply=%region_2.0 | all-reduce | flops 256 | bytes 2048 | tf_op jit(solution)/shard_map/psum | solution.py:360
  139.2 2.4 %add_reduce_fusion.1 = (f32[2560]{0:T(1024)S(1)}, f32[2560]{0:T(1024)S(1)}) fusion(f32[256,1280]{1,0:T(8,128)} %copy-done.12, f32[256,1280]{1,0:T(8,128)} %copy-done.10, f32[256]{0:T(256)S(1)} %get-tuple-element.101), kind=kLoop, calls=%fused_computation.12 | loop fusion | flops 4582400 | bytes 2642944 | tf_op jit(solution)/shard_map/reduce_sum | solution.py:362
  146.3 2.7 %collective-permute-done.22 = f32[5248]{0:T(1024)S(1)} collective-permute-done((f32[5248]{0:T(1024)S(1)}, f32[5248]{0:T(1024)S(1)}, u32[]{:S(2)}, u32[]{:S(2)}) %collective-permute-start.22) | collective-permute-done | bytes 21024 | tf_op jit(solution)/shard_map/ppermute | solution.py:28
  151.0 1.9 %collective-permute-start.24 = (f32[5248]{0:T(1024)S(1)}, f32[5248]{0:T(1024)S(1)}, u32[]{:S(2)}, u32[]{:S(2)}) collective-permute-start(f32[5248]{0:T(1024)S(1)} %add_add_fusion.1), channel_id=1, source_target_pairs={{0,16},{2,18},{4,20},{6,22},{8,24},{10,26},{12,28},{14,30},{16,0},... | collective-permute-start | bytes 62984 | tf_op jit(solution)/shard_map/ppermute | solution.py:28
  153.9 2.3 %fusion.8 = (bf16[128,2560]{1,0:T(8,128)(2,1)}, bf16[128,2560]{1,0:T(8,128)(2,1)}) fusion(bf16[128,2560]{1,0:T(8,128)(2,1)S(1)} %copy-done.2, bf16[64,2560]{1,0:T(8,128)(2,1)S(1)} %collective-permute-done.29, bf16[64,2560]{1,0:T(8,128)(2,1)S(1)} %collective-permute-done.28, f32[128,2560]{1,0:T(8,128)S(1)} %copy-done.8, bf16[64,2560]{1,0:T(8,128)(2,1)S(1)} %slice.44, ...), kind=kLoop, calls=%fused_computation.21 | loop fusion | flops 11468800 | bytes 5242880 | tf_op jit(solution)/shard_map/convert_element_type | solution.py:352
  157.3 2.5 %psum.15 = f32[128]{0:T(128)S(1)} all-reduce(f32[128]{0:T(128)S(1)} %get-tuple-element.98), channel_id=1, replica_groups=mesh['dp'=16,'mp'=2] {'mp'}, use_global_device_ids=true, to_apply=%region_6.0 | all-reduce | flops 128 | bytes 1024 | tf_op jit(solution)/shard_map/psum | solution.py:369
  161.9 1.8 %multiply_multiply_fusion = f32[256,2560]{1,0:T(8,128)} fusion(f32[256,1280]{1,0:T(8,128)S(1)} %copy-done.13, f32[256,1280]{1,0:T(8,128)S(1)} %copy-done.11, f32[2560]{0:T(1024)S(1)} %sqrt.11, f32[256]{0:T(256)S(1)} %divide_multiply_fusion), kind=kLoop, calls=%fused_computation.8 | loop fusion | flops 1966080 | bytes 5254144 | tf_op jit(solution)/shard_map/mul | solution.py:373
  (112 shorter events, 38.2 us)
Async XLA Ops:
  5.9 32.5 %collective-permute-start.4 = (bf16[256,2560]{1,0:T(8,128)(2,1)S(1)}, bf16[256,2560]{1,0:T(8,128)(2,1)S(1)}, u32[]{:S(2)}, u32[]{:S(2)}) collective-permute-start(bf16[256,2560]{1,0:T(8,128)(2,1)S(1)} %copy-done), channel_id=1, source_target_pairs={{0,4},{2,6},{4,0},{6,2},{8,12},{10,14},{12,8},{14,10},{16,20},{18,... | collective-permute-start | bytes 3932168 | tf_op jit(solution)/shard_map/ppermute | solution.py:28
  9.0 30.2 %collective-permute-start.3 = (bf16[256,2560]{1,0:T(8,128)(2,1)S(1)}, bf16[256,2560]{1,0:T(8,128)(2,1)S(1)}, u32[]{:S(2)}, u32[]{:S(2)}) collective-permute-start(bf16[256,2560]{1,0:T(8,128)(2,1)S(1)} %copy-done), channel_id=1, source_target_pairs={{0,2},{2,0},{4,6},{6,4},{8,10},{10,8},{12,14},{14,12},{16,18},{18,... | collective-permute-start | bytes 3932168 | tf_op jit(solution)/shard_map/ppermute | solution.py:28
  10.5 26.5 %collective-permute-start = (bf16[128,1792]{1,0:T(8,128)(2,1)S(1)}, bf16[128,1792]{1,0:T(8,128)(2,1)S(1)}, u32[]{:S(2)}, u32[]{:S(2)}) collective-permute-start(bf16[128,1792]{1,0:T(8,128)(2,1)S(1)} %get-tuple-element.52), channel_id=1, source_target_pairs={{0,8},{2,10},{4,12},{6,14},{8,0},{10,2},{12,4},{14,6},{16,24},{18,... | collective-permute-start | bytes 1376264 | tf_op jit(solution)/shard_map/ppermute | solution.py:28
  12.0 26.4 %collective-permute-start.1 = (bf16[128,1792]{1,0:T(8,128)(2,1)S(1)}, bf16[128,1792]{1,0:T(8,128)(2,1)S(1)}, u32[]{:S(2)}, u32[]{:S(2)}) collective-permute-start(bf16[128,1792]{1,0:T(8,128)(2,1)S(1)} %get-tuple-element.53), channel_id=1, source_target_pairs={{0,16},{2,18},{4,20},{6,22},{8,24},{10,26},{12,28},{14,30},{16,0},... | collective-permute-start | bytes 1376264 | tf_op jit(solution)/shard_map/ppermute | solution.py:28
  14.6 22.3 %collective-permute-start.2 = (bf16[128,512]{1,0:T(8,128)(2,1)S(1)}, bf16[128,512]{1,0:T(8,128)(2,1)S(1)}, u32[]{:S(2)}, u32[]{:S(2)}) collective-permute-start(bf16[128,512]{1,0:T(8,128)(2,1)S(1)} %get-tuple-element.54), channel_id=1, source_target_pairs={{0,24},{2,26},{4,28},{6,30},{8,16},{10,18},{12,20},{14,22},{16,8},... | collective-permute-start | bytes 393224 | tf_op jit(solution)/shard_map/ppermute | solution.py:28
  39.7 19.7 %collective-permute-start.8 = (bf16[128,2560]{1,0:T(8,128)(2,1)S(1)}, bf16[128,2560]{1,0:T(8,128)(2,1)S(1)}, u32[]{:S(2)}, u32[]{:S(2)}) collective-permute-start(bf16[128,2560]{1,0:T(8,128)(2,1)S(1)} %get-tuple-element.65), channel_id=1, source_target_pairs={{0,4},{2,6},{4,0},{6,2},{8,12},{10,14},{12,8},{14,10},{16,20},{18,... | collective-permute-start | bytes 1966088 | tf_op jit(solution)/shard_map/ppermute | solution.py:28
  40.1 19.3 %collective-permute-start.9 = (bf16[128,2560]{1,0:T(8,128)(2,1)S(1)}, bf16[128,2560]{1,0:T(8,128)(2,1)S(1)}, u32[]{:S(2)}, u32[]{:S(2)}) collective-permute-start(bf16[128,2560]{1,0:T(8,128)(2,1)S(1)} %get-tuple-element.66), channel_id=1, source_target_pairs={{0,2},{2,0},{4,6},{6,4},{8,10},{10,8},{12,14},{14,12},{16,18},{18,... | collective-permute-start | bytes 1966088 | tf_op jit(solution)/shard_map/ppermute | solution.py:28
  41.8 17.6 %collective-permute-start.5 = (bf16[128,1792]{1,0:T(8,128)(2,1)S(1)}, bf16[128,1792]{1,0:T(8,128)(2,1)S(1)}, u32[]{:S(2)}, u32[]{:S(2)}) collective-permute-start(bf16[128,1792]{1,0:T(8,128)(2,1)S(1)} %collective-permute-done.1.refs_1_.refs_3_.refs_8_), channel_id=1, source_target_pairs={{0,8},{2,10},{4,12},{6,14},{8,0},{10,2},{12,4},{14,6},{16,24},{18,... | collective-permute-start | bytes 1376264 | tf_op jit(solution)/shard_map/ppermute | solution.py:28
  43.4 15.2 %collective-permute-start.6 = (bf16[128,1280]{1,0:T(8,128)(2,1)S(1)}, bf16[128,1280]{1,0:T(8,128)(2,1)S(1)}, u32[]{:S(2)}, u32[]{:S(2)}) collective-permute-start(bf16[128,1280]{1,0:T(8,128)(2,1)S(1)} %get-tuple-element.78.refs_1_), channel_id=1, source_target_pairs={{0,16},{2,18},{4,20},{6,22},{8,24},{10,26},{12,28},{14,30},{16,0},... | collective-permute-start | bytes 983048 | tf_op jit(solution)/shard_map/ppermute | solution.py:28
  59.4 12.2 %collective-permute-start.14 = (bf16[128,1280]{1,0:T(8,128)(2,1)S(1)}, bf16[128,1280]{1,0:T(8,128)(2,1)S(1)}, u32[]{:S(2)}, u32[]{:S(2)}) collective-permute-start(bf16[128,1280]{1,0:T(8,128)(2,1)S(1)} %get-tuple-element.78.refs_1_), channel_id=1, source_target_pairs={{0,8},{2,10},{4,12},{6,14},{8,0},{10,2},{12,4},{14,6},{16,24},{18,... | collective-permute-start | bytes 983048 | tf_op jit(solution)/shard_map/ppermute | solution.py:28
  62.1 13.6 %collective-permute-start.15 = (bf16[128,1280]{1,0:T(8,128)(2,1)S(1)}, bf16[128,1280]{1,0:T(8,128)(2,1)S(1)}, u32[]{:S(2)}, u32[]{:S(2)}) collective-permute-start(bf16[128,1280]{1,0:T(8,128)(2,1)S(1)} %collective-permute-done.6.refs_3_), channel_id=1, source_target_pairs={{0,8},{2,10},{4,12},{6,14},{8,0},{10,2},{12,4},{14,6},{16,24},{18,... | collective-permute-start | bytes 983048 | tf_op jit(solution)/shard_map/ppermute | solution.py:28
  64.2 15.7 %collective-permute-start.10 = (bf16[256,1280]{1,0:T(8,128)(2,1)S(1)}, bf16[256,1280]{1,0:T(8,128)(2,1)S(1)}, u32[]{:S(2)}, u32[]{:S(2)}) collective-permute-start(bf16[256,1280]{1,0:T(8,128)(2,1)S(1)} %get-tuple-element.70), channel_id=1, source_target_pairs={{0,2},{2,0},{4,6},{6,4},{8,10},{10,8},{12,14},{14,12},{16,18},{18,... | collective-permute-start | bytes 1966088 | tf_op jit(solution)/shard_map/ppermute | solution.py:28
  64.8 16.8 %collective-permute-start.11 = (bf16[256,1280]{1,0:T(8,128)(2,1)S(1)}, bf16[256,1280]{1,0:T(8,128)(2,1)S(1)}, u32[]{:S(2)}, u32[]{:S(2)}) collective-permute-start(bf16[256,1280]{1,0:T(8,128)(2,1)S(1)} %get-tuple-element.75), channel_id=1, source_target_pairs={{0,4},{2,6},{4,0},{6,2},{8,12},{10,14},{12,8},{14,10},{16,20},{18,... | collective-permute-start | bytes 1966088 | tf_op jit(solution)/shard_map/ppermute | solution.py:28
  77.7 17.7 %collective-permute-start.17 = (bf16[256,1280]{1,0:T(8,128)(2,1)S(1)}, bf16[256,1280]{1,0:T(8,128)(2,1)S(1)}, u32[]{:S(2)}, u32[]{:S(2)}) collective-permute-start(bf16[256,1280]{1,0:T(8,128)(2,1)S(1)} %get-tuple-element.88), channel_id=1, source_target_pairs={{0,4},{2,6},{4,0},{6,2},{8,12},{10,14},{12,8},{14,10},{16,20},{18,... | collective-permute-start | bytes 1966088 | tf_op jit(solution)/shard_map/ppermute | solution.py:28
  79.3 25.8 %collective-permute-start.16 = (bf16[256,1280]{1,0:T(8,128)(2,1)S(1)}, bf16[256,1280]{1,0:T(8,128)(2,1)S(1)}, u32[]{:S(2)}, u32[]{:S(2)}) collective-permute-start(bf16[256,1280]{1,0:T(8,128)(2,1)S(1)} %get-tuple-element.85), channel_id=1, source_target_pairs={{0,2},{2,0},{4,6},{6,4},{8,10},{10,8},{12,14},{14,12},{16,18},{18,... | collective-permute-start | bytes 1966088 | tf_op jit(solution)/shard_map/ppermute | solution.py:28
  80.0 25.8 %collective-permute-start.12 = (bf16[128,1280]{1,0:T(8,128)(2,1)S(1)}, bf16[128,1280]{1,0:T(8,128)(2,1)S(1)}, u32[]{:S(2)}, u32[]{:S(2)}) collective-permute-start(bf16[128,1280]{1,0:T(8,128)(2,1)S(1)} %shard_map.114), channel_id=1, source_target_pairs={{0,4},{2,6},{4,0},{6,2},{8,12},{10,14},{12,8},{14,10},{16,20},{18,... | collective-permute-start | bytes 983048 | tf_op jit(solution)/shard_map/ppermute | solution.py:28
  81.6 25.7 %collective-permute-start.13 = (bf16[128,1280]{1,0:T(8,128)(2,1)S(1)}, bf16[128,1280]{1,0:T(8,128)(2,1)S(1)}, u32[]{:S(2)}, u32[]{:S(2)}) collective-permute-start(bf16[128,1280]{1,0:T(8,128)(2,1)S(1)} %shard_map.115), channel_id=1, source_target_pairs={{0,2},{2,0},{4,6},{6,4},{8,10},{10,8},{12,14},{14,12},{16,18},{18,... | collective-permute-start | bytes 983048 | tf_op jit(solution)/shard_map/ppermute | solution.py:28
  83.3 24.3 %collective-permute-start.26 = (bf16[128,2560]{1,0:T(8,128)(2,1)S(1)}, bf16[128,2560]{1,0:T(8,128)(2,1)S(1)}, u32[]{:S(2)}, u32[]{:S(2)}) collective-permute-start(bf16[128,2560]{1,0:T(8,128)(2,1)S(1)} %get-tuple-element.92), channel_id=1, source_target_pairs={{0,8},{2,10},{4,12},{6,14},{8,0},{10,2},{12,4},{14,6},{16,24},{18,... | collective-permute-start | bytes 1966088 | tf_op jit(solution)/shard_map/ppermute | solution.py:28
  95.4 38.8 %collective-permute-start.27 = (bf16[128,2560]{1,0:T(8,128)(2,1)S(1)}, bf16[128,2560]{1,0:T(8,128)(2,1)S(1)}, u32[]{:S(2)}, u32[]{:S(2)}) collective-permute-start(bf16[128,2560]{1,0:T(8,128)(2,1)S(1)} %get-tuple-element.93), channel_id=1, source_target_pairs={{0,16},{2,18},{4,20},{6,22},{8,24},{10,26},{12,28},{14,30},{16,0},... | collective-permute-start | bytes 1966088 | tf_op jit(solution)/shard_map/ppermute | solution.py:28
  105.1 29.3 %collective-permute-start.19 = (bf16[128,1280]{1,0:T(8,128)(2,1)S(1)}, bf16[128,1280]{1,0:T(8,128)(2,1)S(1)}, u32[]{:S(2)}, u32[]{:S(2)}) collective-permute-start(bf16[128,1280]{1,0:T(8,128)(2,1)S(1)} %shard_map.119), channel_id=1, source_target_pairs={{0,2},{2,0},{4,6},{6,4},{8,10},{10,8},{12,14},{14,12},{16,18},{18,... | collective-permute-start | bytes 983048 | tf_op jit(solution)/shard_map/ppermute | solution.py:28
  105.7 28.7 %collective-permute-start.18 = (bf16[128,1280]{1,0:T(8,128)(2,1)S(1)}, bf16[128,1280]{1,0:T(8,128)(2,1)S(1)}, u32[]{:S(2)}, u32[]{:S(2)}) collective-permute-start(bf16[128,1280]{1,0:T(8,128)(2,1)S(1)} %shard_map.118), channel_id=1, source_target_pairs={{0,4},{2,6},{4,0},{6,2},{8,12},{10,14},{12,8},{14,10},{16,20},{18,... | collective-permute-start | bytes 983048 | tf_op jit(solution)/shard_map/ppermute | solution.py:28
  107.6 46.2 %collective-permute-start.28 = (bf16[64,2560]{1,0:T(8,128)(2,1)S(1)}, bf16[64,2560]{1,0:T(8,128)(2,1)S(1)}, u32[]{:S(2)}, u32[]{:S(2)}) collective-permute-start(bf16[64,2560]{1,0:T(8,128)(2,1)S(1)} %shard_map.120), channel_id=1, source_target_pairs={{0,16},{2,18},{4,20},{6,22},{8,24},{10,26},{12,28},{14,30},{16,0},... | collective-permute-start | bytes 983048 | tf_op jit(solution)/shard_map/ppermute | solution.py:28
  134.3 19.6 %collective-permute-start.29 = (bf16[64,2560]{1,0:T(8,128)(2,1)S(1)}, bf16[64,2560]{1,0:T(8,128)(2,1)S(1)}, u32[]{:S(2)}, u32[]{:S(2)}) collective-permute-start(bf16[64,2560]{1,0:T(8,128)(2,1)S(1)} %shard_map.121), channel_id=1, source_target_pairs={{0,8},{2,10},{4,12},{6,14},{8,0},{10,2},{12,4},{14,6},{16,24},{18,... | collective-permute-start | bytes 983048 | tf_op jit(solution)/shard_map/ppermute | solution.py:28
  149.4 6.8 %collective-permute-start.25 = (f32[5248]{0:T(1024)S(1)}, f32[5248]{0:T(1024)S(1)}, u32[]{:S(2)}, u32[]{:S(2)}) collective-permute-start(f32[5248]{0:T(1024)S(1)} %add_add_fusion.1), channel_id=1, source_target_pairs={{0,24},{2,26},{4,28},{6,30},{8,16},{10,18},{12,20},{14,22},{16,8},... | collective-permute-start | bytes 62984 | tf_op jit(solution)/shard_map/ppermute | solution.py:28
  (26 other events, 205.7 us)

commit v9 on v8

--- a/solution.py
+++ b/solution.py
@@ -9,6 +9,7 @@
 
 TRAIN_STEP = 3
 INNER_BITS = 2
+LEFT = 3
 EAGER = pl.CostEstimate(flops=0, bytes_accessed=0, transcendentals=0)
 
 
@@ -92,10 +93,10 @@
 
 def first_stage(out_grad, gate_pre, up_pre, place, rows):
     tokens, units = gate_pre.shape
-    half = units // 2
+    half = units * LEFT // 5
     step = 32
 
-    def kernel(place, source_hbm, gate_hbm, up_hbm, own, left, right, message1, message2, message3, source, gate, up, sems):
+    def kernel(place, source_hbm, gate_hbm, up_hbm, own, right, message1, message2, message3, source, gate, up, sems):
         copies = [
             pltpu.make_async_copy(there, here, sems.at[n])
             for n, (there, here) in enumerate(((gate_hbm, gate), (up_hbm, up), (source_hbm, source)))
@@ -115,7 +116,6 @@
             here = pl.ds(pl.multiple_of(i * step, step), step)
             activated, _ = gelu_parts(gate[here, :].astype(jnp.float32))
             value = (activated * up[here, :].astype(jnp.float32)).astype(jnp.bfloat16)
-            left[here, :] = value[:, :half]
             right[here, :] = value[:, half:]
             message1[here, :half] = value[:, :half]
             message2[here, :half] = value[:, :half]
@@ -128,7 +128,7 @@
                 target[:, base + j * rows : base + (j + 1) * rows] = source[:, block(k, 2 * core + j)]
 
     vmem = pl.BlockSpec(memory_space=pltpu.VMEM)
-    widths = [4 * rows, half, half, half + 2 * rows, half + 2 * rows, 2 * rows]
+    widths = [4 * rows, units - half, half + 2 * rows, half + 2 * rows, 2 * rows]
     return pl.pallas_call(
         kernel,
         out_shape=[jax.ShapeDtypeStruct((tokens, width), jnp.bfloat16) for width in widths],
@@ -193,21 +193,100 @@
     )(place, own, mine, theirs)
 
 
-def add_tail(part, arrived):
-    rows = part.shape[0]
-
-    def kernel(part, arrived, out):
-        out[...] = (part[...] + arrived[rows:, :].astype(jnp.float32)).astype(jnp.bfloat16)
+def add_tail(parts, arrived):
+    rows = parts[0].shape[0]
+    widths = [part.shape[1] for part in parts]
+
+    def kernel(*refs):
+        out, at = refs[-1], 0
+        for part, other, width in zip(refs, refs[len(parts) :], widths):
+            out[:, at : at + width] = (part[...] + other[rows:, :].astype(jnp.float32)).astype(jnp.bfloat16)
+            at += width
 
     vmem = pl.BlockSpec(memory_space=pltpu.VMEM)
     return pl.pallas_call(
         kernel,
-        out_shape=jax.ShapeDtypeStruct(part.shape, jnp.bfloat16),
-        in_specs=[vmem, vmem],
+        out_shape=jax.ShapeDtypeStruct((rows, sum(widths)), jnp.bfloat16),
+        in_specs=[vmem] * (2 * len(parts)),
         out_specs=vmem,
         compiler_params=pltpu.CompilerParams(vmem_limit_bytes=8 << 20),
         cost_estimate=EAGER,
-    )(part, arrived)
+    )(*parts, *arrived)
+
+
+def flat(column):
+    return jnp.broadcast_to(column, (128, 128)).T[0:1, :]
+
+
+def upright(row):
+    return jnp.broadcast_to(row, (128, 128)).T[:, 0:1]
+
+
+def sum_up(kept, from_low, from_high, last_a, last_b, scale):
+    rows = kept[0].shape[0]
+    q = rows // 2
+    widths = [part.shape[1] for part in kept]
+    units = sum(widths)
+
+    def kernel(*refs):
+        kept_refs, low_refs, high_refs = refs[:2], refs[2:4], refs[4:6]
+        last_refs, grad, row_part = refs[6:8], refs[8], refs[9]
+        for h, arrived in enumerate((low_refs, high_refs)):
+            for at in range(0, q, 128):
+                total = jnp.zeros((128, 1), jnp.float32)
+                here = slice(h * q + at, h * q + at + 128)
+                column = 0
+                for part, other, width in zip(kept_refs, arrived, widths):
+                    there = slice(column, column + width)
+                    value = part[here, :] + other[at : at + 128, :].astype(jnp.float32)
+                    value = (value + last_refs[h][at : at + 128, there].astype(jnp.float32)) * scale
+                    grad[here, there] = value
+                    total = total + jnp.sum(value * value + 1e-30, axis=1, keepdims=True)
+                    column += width
+                row_part[:, here] = flat(total)
+
+    vmem = pl.BlockSpec(memory_space=pltpu.VMEM)
+    return pl.pallas_call(
+        kernel,
+        out_shape=[jax.ShapeDtypeStruct((rows, units), jnp.float32), jax.ShapeDtypeStruct((1, rows), jnp.float32)],
+        in_specs=[vmem] * 8,
+        out_specs=[vmem] * 2,
+        compiler_params=pltpu.CompilerParams(vmem_limit_bytes=14 << 20),
+        cost_estimate=EAGER,
+    )(*kept, *from_low, *from_high, last_a, last_b)
+
+
+def column_sums(grad, row_sum, row_moment, decay, total_units):
+    rows, units = grad.shape
+
+    def kernel(grad, row_sum, row_moment, row_moment_new, sums):
+        new = decay * row_moment[...] + (1.0 - decay) * (row_sum[...] / total_units)
+        row_moment_new[...] = new
+        sums[:, 2 * units :] = jnp.broadcast_to(jnp.sum(new, axis=1, keepdims=True), (1, 128))
+        inverse = [1.0 / upright(new[:, at : at + 128]) for at in range(0, rows, 128)]
+        for column in range(0, units, 256):
+            there = slice(column, column + 256)
+            squares, scaled = jnp.zeros((1, 256), jnp.float32), jnp.zeros((1, 256), jnp.float32)
+            for n, at in enumerate(range(0, rows, 128)):
+                power = grad[at : at + 128, there]
+                power = power * power
+                squares = squares + jnp.sum(power + 1e-30, axis=0, keepdims=True)
+                scaled = scaled + jnp.sum(power * inverse[n], axis=0, keepdims=True)
+            sums[:, there] = squares
+            sums[:, units + column : units + column + 256] = scaled
+
+    vmem = pl.BlockSpec(memory_space=pltpu.VMEM)
+    return pl.pallas_call(
+        kernel,
+        out_shape=[
+            jax.ShapeDtypeStruct((1, rows), jnp.float32),
+            jax.ShapeDtypeStruct((1, 2 * units + 128), jnp.float32),
+        ],
+        in_specs=[vmem] * 3,
+        out_specs=[vmem] * 2,
+        compiler_params=pltpu.CompilerParams(vmem_limit_bytes=14 << 20),
+        cost_estimate=EAGER,
+    )(grad, row_sum, row_moment)
 
 
 def products(share, groups, steps):
@@ -259,37 +338,37 @@
     me, core = lax.axis_index("dp"), lax.axis_index("mp")
     tokens, units = gate_pre.shape
     rows = down_weight.shape[0]
-    q, t, half = rows // 2, tokens // 2, units // 2
-    steps = units // 512
+    q, t = rows // 2, tokens // 2
+    steps = 4
+    split = units * LEFT // 5
     barrier = lax.optimization_barrier
     place = jnp.stack([me, core]).astype(jnp.int32)
-    own, left, right, message1, message2, message3 = first_stage(out_grad, gate_pre, up_pre, place, rows)
+    own, right, message1, message2, message3 = first_stage(out_grad, gate_pre, up_pre, place, rows)
 
     down_weight, message1 = barrier((down_weight, message1))
+    extra, every, whole = (split, 2 * rows), (0, tokens), (0, units)
     left1, left2, message3 = flip(message1, z_bit), flip(message2, w_bit), flip(message3, z_bit | w_bit)
     weight1, weight2 = flip(down_weight, x_bit), flip(down_weight, y_bit)
 
-    left1, left2, message3, weight1, weight2, right = barrier((left1, left2, message3, weight1, weight2, right))
-    left3 = flip(left2, z_bit)
-    right2 = flip(right, w_bit)
-    extra, every = (half, 2 * rows), (0, tokens)
-    mine, to_y, to_x = cut(
-        [left1, left2, message3, weight1, weight2],
+    to_y, to_x = cut([weight1, weight2], [(0, (0, q), whole, 0, 0), (1, (q, q), whole, 1, 0)], [(q, units)] * 2)
+    weight3a, weight3b = flip(to_y, y_bit), flip(to_x, x_bit)
+    left1, left2, message3, _, _ = barrier((left1, left2, message3, to_y, to_x))
+    to_z, mine = cut(
+        [left1, left2, message3],
         [
-            (0, every, extra, 0, 0),
-            (1, every, extra, 0, 2 * rows),
-            (2, every, (0, 2 * rows), 0, 4 * rows),
-            (3, (0, q), (0, units), 1, 0),
-            (4, (q, q), (0, units), 2, 0),
+            (1, every, (0, split), 0, 0),
+            (0, every, extra, 1, 0),
+            (1, every, extra, 1, 2 * rows),
+            (2, every, (0, 2 * rows), 1, 4 * rows),
         ],
-        [(tokens, 6 * rows), (q, units), (q, units)],
-    )
+        [(tokens, split), (tokens, 6 * rows)],
+    )
+    left3 = flip(to_z, z_bit)
     theirs = flip(mine, 1, "mp")
-    weight3a, weight3b = flip(to_y, y_bit), flip(to_x, x_bit)
     share = assemble(own, mine, theirs, place, rows)
 
-    left3, right2, share, weight3a, weight3b, right = barrier((left3, right2, share, weight3a, weight3b, right))
-    right1, right3 = flip(right, z_bit), flip(right2, z_bit)
+    left3, share, right = barrier((left3, share, right))
+    right1, right2 = flip(right, z_bit), flip(right, w_bit)
 
     def low_sent(size):
         return [(2 * size, 3 * size), (6 * size, 7 * size)]
@@ -304,34 +383,46 @@
         ranges = [(0, 2 * size)], [(4 * size, 5 * size)], [(3 * size, 4 * size)]
         return [(r, jnp.float32) for r in ranges]
 
-    lefts = [left, left1, left2, left3]
+    lefts = [message1, left1, left2, left3]
+    share, weight3a, weight3b = barrier((share, weight3a, weight3b))
+    left_to_x, left_to_y = products(share, [(lefts, split, sent(q), True)], steps)
+    left_from_x, left_from_y = flip(left_to_x, x_bit), flip(left_to_y, y_bit)
+    right2, share, _ = barrier((right2, share, left_to_x))
+    right3 = flip(right2, z_bit)
+
     weights = [down_weight, weight1, weight2, weight3a, weight3b]
-    left_to_x, left_to_y = products(share, [(lefts, half, sent(q), True)], steps)
-    left_from_x, left_from_y = flip(left_to_x, x_bit), flip(left_to_y, y_bit)
-    share, _ = barrier((share, left_to_x))
-    to_z, to_w, *left_kept = products(
-        share, [(weights, units, sent(t), False), (lefts, half, kept(q), True)], steps
-    )
-
-    right1, right3, to_z, to_w, share = barrier((right1, right3, to_z, to_w, share))
+    to_z, to_w, *left_parts = products(
+        share, [(weights, units, sent(t), False), (lefts, split, kept(q), True)], steps
+    )
     from_z, from_w = flip(to_z, z_bit), flip(to_w, w_bit)
+
+    right1, right3, left_from_x, left_from_y, share, _ = barrier(
+        (right1, right3, left_from_x, left_from_y, share, to_z)
+    )
     rights = [right, right1, right2, right3]
-    right_to_x, right_to_y = products(share, [(rights, half, sent(q), True)], steps)
+    right_to_x, right_to_y = products(share, [(rights, units - split, sent(q), True)], steps)
     right_from_x, right_from_y = flip(right_to_x, x_bit), flip(right_to_y, y_bit)
     share, _ = barrier((share, right_to_x))
-    parts = products(share, [(rights, half, kept(q), True), (weights, units, kept(t), False)], steps)
-
-    def finish(parts, from_low, from_high, size, low, high):
-        own_part, a_part, b_part = parts
-        last_a = flip(add_tail(a_part, from_low), high)
-        last_b = flip(add_tail(b_part, from_high), low)
-        arrived = jnp.concatenate([from_low[:size], from_high[:size]], axis=0).astype(jnp.float32)
-        return own_part + arrived + jnp.concatenate([last_a, last_b], axis=0).astype(jnp.float32)
-
-    left_grad = finish(left_kept, left_from_x, left_from_y, q, x_bit, y_bit)
-    right_grad = finish(parts[:3], right_from_x, right_from_y, q, x_bit, y_bit)
-    hidden_grad = finish(parts[3:], from_z, from_w, t, z_bit, w_bit)
-    return jnp.concatenate([left_grad, right_grad], axis=1), hidden_grad
+    parts = products(share, [(rights, units - split, kept(q), True), (weights, units, kept(t), False)], steps)
+
+    grad_a = flip(add_tail([left_parts[1], parts[1]], [left_from_x, right_from_x]), y_bit)
+    grad_b = flip(add_tail([left_parts[2], parts[2]], [left_from_y, right_from_y]), x_bit)
+    grad_a, grad_b, from_z, from_w = barrier((grad_a, grad_b, from_z, from_w))
+    grad, row_part = sum_up(
+        [left_parts[0], parts[0]],
+        [left_from_x, right_from_x],
+        [left_from_y, right_from_y],
+        grad_a,
+        grad_b,
+        1.0 / math.sqrt(tokens * lax.axis_size("dp")),
+    )
+
+    to_w, to_z = add_tail([parts[4]], [from_z]), add_tail([parts[5]], [from_w])
+    row_sum = lax.psum(row_part, "mp")
+    row_sum, to_w, to_z = barrier((row_sum, to_w, to_z))
+    last_a, last_b = flip(to_w, w_bit), flip(to_z, z_bit)
+    arrived = jnp.concatenate([from_z[:t], from_w[:t]], axis=0)
+    return grad, row_sum, (parts[3], arrived, last_a, last_b)
 
 
 def local(out_grad, gate_pre, up_pre, down_weight, row_moment, col_moment):
@@ -339,30 +430,35 @@
     rows, units = down_weight.shape
     tokens = out_grad.shape[0]
     all_bits = [1 << b for b in range(size.bit_length() - 1)]
-    staged = size == 16 and lax.axis_size("mp") == 2 and rows % 256 == 0 and tokens % 32 == 0 and units % 512 == 0
+    decay = 1.0 - TRAIN_STEP ** (-0.8)
+    total_rows = rows * size
+    total_units = units * lax.axis_size("mp")
+    staged = size == 16 and lax.axis_size("mp") == 2 and rows % 256 == 0 and tokens % 32 == 0 and units % 2560 == 0
     if staged:
-        product, hidden_grad = staged_products(out_grad, gate_pre, up_pre, down_weight)
+        grad, row_sum, (own_part, arrived, last_a, last_b) = staged_products(out_grad, gate_pre, up_pre, down_weight)
+        row_moment_new, sums = column_sums(grad, row_sum, row_moment[None, :], decay, total_units)
+        row_moment_new, sums = row_moment_new[0], group_sum(sums[0], all_bits[:INNER_BITS])
+        sums, last_a, last_b = lax.optimization_barrier((sums, last_a, last_b))
+        hidden_grad = own_part + arrived.astype(jnp.float32) + jnp.concatenate([last_a, last_b], axis=0).astype(jnp.float32)
     else:
         product, hidden_grad = general_products(
             out_grad, gate_pre, up_pre, down_weight, all_bits[:INNER_BITS], all_bits[INNER_BITS:]
         )
+        grad = product * (1.0 / math.sqrt(tokens * size))
+        powers = grad * grad
+        squares = powers + 1e-30
+        row_sum = lax.psum(jnp.sum(squares, axis=1), "mp")
+        row_moment_new = decay * row_moment + (1.0 - decay) * (row_sum / total_units)
+        col_part = jnp.sum(squares, axis=0)
+        scaled_part = jnp.sum(powers / row_moment_new[:, None], axis=0)
+        sums = jnp.concatenate([col_part, scaled_part, jnp.broadcast_to(jnp.sum(row_moment_new), (128,))])
+        sums = group_sum(sums, all_bits[:INNER_BITS])
 
     activated, derivative = gelu_parts(gate_pre.astype(jnp.float32))
     gate_grad = (hidden_grad * up_pre.astype(jnp.float32) * derivative).astype(jnp.bfloat16)
     up_grad = (hidden_grad * activated).astype(jnp.bfloat16)
 
-    grad = product * (1.0 / math.sqrt(tokens * size))
-    decay = 1.0 - TRAIN_STEP ** (-0.8)
-    total_rows = rows * size
-    total_units = units * lax.axis_size("mp")
-    powers = grad * grad
-    squares = powers + 1e-30
-    row_sum = lax.psum(jnp.sum(squares, axis=1), "mp")
-    row_moment_new = decay * row_moment + (1.0 - decay) * (row_sum / total_units)
-    col_part = jnp.sum(squares, axis=0)
-    scaled_part = jnp.sum(powers / row_moment_new[:, None], axis=0)
-    total_part = jnp.broadcast_to(jnp.sum(row_moment_new), (128,))
-    sums = group_sum(jnp.concatenate([col_part, scaled_part, total_part]), all_bits)
+    sums = group_sum(sums, all_bits[INNER_BITS:])
     col_moment_new = decay * col_moment + (1.0 - decay) * (sums[:units] / total_rows)
     row_mean = sums[2 * units] / total_rows
     ratios = jnp.sum((sums[units : 2 * units] / col_moment_new).reshape(-1, 128), axis=0)

time: 165 us -> 163 us (0.988)
  waiting for transfers between devices: 80.6 us -> 71.5 us
  Pallas kernels: 16.1 us -> 20.2 us
  local copies, waits for them, and re-layouts: 6.94 us -> 9.43 us
  starting transfers between devices: 44 us -> 46.4 us
  other arithmetic: 8.73 us -> 6.38 us
    ppermute x30 -> x28, waiting for transfers between devices: 80.6 us -> 71.5 us  [flip(): return lax.ppermute(value, axis, [(i, i ^ bits) for i in range(size)])]
    reduce_sum x3 -> x0, other arithmetic: 3.42 us -> none  [the longest x1 2.38 us: local(): col_part = jnp.sum(squares, axis=0)]
    pallas_call x6, Pallas kernels: 0.34 us -> 3.21 us  [the longest x4 1.78 us: add_tail(): pl.pallas_call(kernel, out_shape=jax.ShapeDtypeStruct((rows, sum(widths))...]
    ppermute x30 -> x28, starting transfers between devices: 44 us -> 46.4 us  [flip(): return lax.ppermute(value, axis, [(i, i ^ bits) for i in range(size)])]
    slice x8 -> x2, local copies, waits for them, and re-layouts: 0.1 us -> 1.99 us  [staged_products(): arrived = jnp.concatenate([from_z[:t], from_w[:t]], axis=0)]
  transfers between devices with their start and end apart: 30 -> 28, of which waited for: 13 -> 14; matrix products, arithmetic and copies ran while one was open for 4% -> 4% of each run, Pallas kernels for 8% -> 7%
where the time goes in v9:
time: 163 us; the launch traced here: 162 us
  waiting for transfers between devices  71.5 us (44%)
  starting transfers between devices  46.4 us (28%)
  Pallas kernels  20.2 us (12%)
  local copies, waits for them, and re-layouts  9.43 us (6%)
  other arithmetic  6.38 us (4%)
  blocking collectives  4.94 us (3%)
  between operations  3.36 us (2%)
    ppermute x28, waiting for transfers between devices, flip(): return lax.ppermute(value, axis, [(i, i ^ bits) for i in range(size)])  71.5 us
    ppermute x28, starting transfers between devices, flip(): return lax.ppermute(value, axis, [(i, i ^ bits) for i in range(size)])  46.4 us
    pallas_call x4, Pallas kernels, products(): pl.pallas_call(kernel, grid=(steps,), out_shape=[jax.ShapeDtypeStruct((he...  14.1 us
    unnamed x36, local copies, waits for them, and re-layouts  6.92 us
    convert_element_type x1, other arithmetic, local(): up_grad = (hidden_grad * activated).astype(jnp.bfloat16)  3.83 us
  transfers between devices with their start and end apart: 28, of which 14 were waited for; matrix products, arithmetic and copies ran while one was open for 4% of the time, Pallas kernels for 7%

profile of v9, /device:TPU:0, one launch (start us, length us, event | category | flops | bytes accessed | tf_op | source)
XLA Modules:
  0.0 162.3 jit_solution(5336423435447162186)
XLA Ops:
  4.2 1.7 %shard_map.109 = (bf16[128,1024]{1,0:T(8,128)(2,1)S(1)}, bf16[128,1024]{1,0:T(8,128)(2,1)S(1)}, bf16[128,2048]{1,0:T(8,128)(2,1)S(1)}, bf16[128,2048]{1,0:T(8,128)(2,1)S(1)}, bf16[128,512]{1,0:T(8,128)(2,1)S(1)}) custom-call(s32[2]{0:T(128)S(1)} %pad_add_fusion.place, bf16[128,4096]{1,0:T(8,128)(2,1)S(1)} %copy-done.9, bf16[128,2560]{1,0:T(8,128)(2,1)S(1)} %copy-done.1, ...), custom_call_target="tpu_custom_call" | custom-call | tf_op jit(solution)/shard_map/pallas_call | solution.py:132
  5.9 3.0 %collective-permute-start.4 = (bf16[256,2560]{1,0:T(8,128)(2,1)S(1)}, bf16[256,2560]{1,0:T(8,128)(2,1)S(1)}, u32[]{:S(2)}, u32[]{:S(2)}) collective-permute-start(bf16[256,2560]{1,0:T(8,128)(2,1)S(1)} %copy-done), channel_id=1, source_target_pairs={{0,4},{2,6},{4,0},{6,2},{8,12},{10,14},{12,8},{14,10},{16,20},{18,... | collective-permute-start | bytes 3932168 | tf_op jit(solution)/shard_map/ppermute | solution.py:29
  12.0 2.6 %collective-permute-start.1 = (bf16[128,2048]{1,0:T(8,128)(2,1)S(1)}, bf16[128,2048]{1,0:T(8,128)(2,1)S(1)}, u32[]{:S(2)}, u32[]{:S(2)}) collective-permute-start(bf16[128,2048]{1,0:T(8,128)(2,1)S(1)} %get-tuple-element.65), channel_id=1, source_target_pairs={{0,16},{2,18},{4,20},{6,22},{8,24},{10,26},{12,28},{14,30},{16,0},... | collective-permute-start | bytes 1572872 | tf_op jit(solution)/shard_map/ppermute | solution.py:29
  14.6 23.1 %collective-permute-done.4.refs_1_.refs_3_.refs_7_ = bf16[256,2560]{1,0:T(8,128)(2,1)S(1)} collective-permute-done((bf16[256,2560]{1,0:T(8,128)(2,1)S(1)}, bf16[256,2560]{1,0:T(8,128)(2,1)S(1)}, u32[]{:S(2)}, u32[]{:S(2)}) %collective-permute-start.4) | collective-permute-done | bytes 1310752 | tf_op jit(solution)/shard_map/ppermute | solution.py:29
  41.7 3.6 %collective-permute-start.2 = (bf16[128,512]{1,0:T(8,128)(2,1)S(1)}, bf16[128,512]{1,0:T(8,128)(2,1)S(1)}, u32[]{:S(2)}, u32[]{:S(2)}) collective-permute-start(bf16[128,512]{1,0:T(8,128)(2,1)S(1)} %get-tuple-element.66), channel_id=1, source_target_pairs={{0,24},{2,26},{4,28},{6,30},{8,16},{10,18},{12,20},{14,22},{16,8},... | collective-permute-start | bytes 393224 | tf_op jit(solution)/shard_map/ppermute | solution.py:29
  45.3 3.3 %collective-permute-done.2.refs_2_ = bf16[128,512]{1,0:T(8,128)(2,1)S(1)} collective-permute-done((bf16[128,512]{1,0:T(8,128)(2,1)S(1)}, bf16[128,512]{1,0:T(8,128)(2,1)S(1)}, u32[]{:S(2)}, u32[]{:S(2)}) %collective-permute-start.2) | collective-permute-done | bytes 131104 | tf_op jit(solution)/shard_map/ppermute | solution.py:29
  51.1 9.2 %collective-permute-done.5.refs_4_.refs_9_ = bf16[128,1536]{1,0:T(8,128)(2,1)S(1)} collective-permute-done((bf16[128,1536]{1,0:T(8,128)(2,1)S(1)}, bf16[128,1536]{1,0:T(8,128)(2,1)S(1)}, u32[]{:S(2)}, u32[]{:S(2)}) %collective-permute-start.5) | collective-permute-done | bytes 393248 | tf_op jit(solution)/shard_map/ppermute | solution.py:29
  60.3 2.7 %shard_map.113 = (bf16[256,1536]{1,0:T(8,128)(2,1)S(1)}, bf16[256,1536]{1,0:T(8,128)(2,1)S(1)}) custom-call(bf16[512,1024]{1,0:T(8,128)(2,1)S(1)} %shard_map.112.refs_0_, bf16[128,2048]{1,0:T(8,128)(2,1)S(1)} %get-tuple-element.64.refs_1_.refs_6_, bf16[128,2048]{1,0:T(8,128)(2,1)S(1)} %collective-permute-done.refs_0_.refs_2_.refs_7_, ...), custom_call_target="tpu_custom_call" | custom-call | tf_op jit(solution)/shard_map/pallas_call | solution.py:321
  65.2 2.3 %collective-permute-start.7 = (bf16[128,1024]{1,0:T(8,128)(2,1)S(1)}, bf16[128,1024]{1,0:T(8,128)(2,1)S(1)}, u32[]{:S(2)}, u32[]{:S(2)}) collective-permute-start(bf16[128,1024]{1,0:T(8,128)(2,1)S(1)} %get-tuple-element.77.refs_1_), channel_id=1, source_target_pairs={{0,16},{2,18},{4,20},{6,22},{8,24},{10,26},{12,28},{14,30},{16,0},... | collective-permute-start | bytes 786440 | tf_op jit(solution)/shard_map/ppermute | solution.py:29
  67.5 1.8 %collective-permute-start.10 = (bf16[128,1024]{1,0:T(8,128)(2,1)S(1)}, bf16[128,1024]{1,0:T(8,128)(2,1)S(1)}, u32[]{:S(2)}, u32[]{:S(2)}) collective-permute-start(bf16[128,1024]{1,0:T(8,128)(2,1)S(1)} %get-tuple-element.77.refs_1_), channel_id=1, source_target_pairs={{0,8},{2,10},{4,12},{6,14},{8,0},{10,2},{12,4},{14,6},{16,24},{18,... | collective-permute-start | bytes 786440 | tf_op jit(solution)/shard_map/ppermute | solution.py:29
  69.3 9.9 %collective-permute-done.7.refs_3_ = bf16[128,1024]{1,0:T(8,128)(2,1)S(1)} collective-permute-done((bf16[128,1024]{1,0:T(8,128)(2,1)S(1)}, bf16[128,1024]{1,0:T(8,128)(2,1)S(1)}, u32[]{:S(2)}, u32[]{:S(2)}) %collective-permute-start.7) | collective-permute-done | bytes 262176 | tf_op jit(solution)/shard_map/ppermute | solution.py:29
  79.6 5.1 %shard_map.114 = (bf16[128,2560]{1,0:T(8,128)(2,1)S(1)}, bf16[128,2560]{1,0:T(8,128)(2,1)S(1)}, f32[256,1536]{1,0:T(8,128)S(1)}, f32[128,1536]{1,0:T(8,128)S(1)}, f32[128,1536]{1,0:T(8,128)S(1)}) custom-call(bf16[512,1024]{1,0:T(8,128)(2,1)S(1)} %shard_map.112.refs_0_, bf16[256,2560]{1,0:T(8,128)(2,1)S(1)} %copy-done, ...), custom_call_target="tpu_custom_call" | custom-call | tf_op jit(solution)/shard_map/pallas_call | solution.py:321
  86.4 1.7 %shard_map.115 = (bf16[256,1024]{1,0:T(8,128)(2,1)S(1)}, bf16[256,1024]{1,0:T(8,128)(2,1)S(1)}) custom-call(bf16[512,1024]{1,0:T(8,128)(2,1)S(1)} %shard_map.112.refs_0_, bf16[128,1024]{1,0:T(8,128)(2,1)S(1)} %get-tuple-element.77.refs_1_, bf16[128,1024]{1,0:T(8,128)(2,1)S(1)} %collective-permute-done.10.refs_2_, ...), custom_call_target="tpu_custom_call" | custom-call | tf_op jit(solution)/shard_map/pallas_call | solution.py:321
  91.6 3.4 %collective-permute-start.19 = (bf16[128,2560]{1,0:T(8,128)(2,1)S(1)}, bf16[128,2560]{1,0:T(8,128)(2,1)S(1)}, u32[]{:S(2)}, u32[]{:S(2)}) collective-permute-start(bf16[128,2560]{1,0:T(8,128)(2,1)S(1)} %get-tuple-element.102), channel_id=1, source_target_pairs={{0,16},{2,18},{4,20},{6,22},{8,24},{10,26},{12,28},{14,30},{16,0},... | collective-permute-start | bytes 1966088 | tf_op jit(solution)/shard_map/ppermute | solution.py:29
  95.0 4.6 %shard_map.116 = (f32[256,1024]{1,0:T(8,128)S(1)}, f32[128,1024]{1,0:T(8,128)S(1)}, f32[128,1024]{1,0:T(8,128)S(1)}, f32[128,2560]{1,0:T(8,128)S(1)}, f32[64,2560]{1,0:T(8,128)S(1)}, /*index=5*/f32[64,2560]{1,0:T(8,128)S(1)}) custom-call(bf16[512,1024]{1,0:T(8,128)(2,1)S(1)} %shard_map.112.refs_0_, bf16[128,1024]{1,0:T(8,128)(2,1)S(1)} %get-tuple-element.77.refs_1_, ...), custom_call_target="tpu_custom_call" | custom-call | tf_op jit(solution)/shard_map/pallas_call | solution.py:321
  103.3 15.2 %collective-permute-done.19.refs_1_ = bf16[128,2560]{1,0:T(8,128)(2,1)S(1)} collective-permute-done((bf16[128,2560]{1,0:T(8,128)(2,1)S(1)}, bf16[128,2560]{1,0:T(8,128)(2,1)S(1)}, u32[]{:S(2)}, u32[]{:S(2)}) %collective-permute-start.19) | collective-permute-done | bytes 655392 | tf_op jit(solution)/shard_map/ppermute | solution.py:29
  120.0 2.5 %psum.14.row_sum = f32[1,256]{1,0:T(1,128)S(1)} all-reduce(f32[1,256]{1,0:T(1,128)S(1)} %get-tuple-element.106), channel_id=1, replica_groups=mesh['dp'=16,'mp'=2] {'mp'}, use_global_device_ids=true, to_apply=%region_0.0 | all-reduce | flops 256 | bytes 2048 | tf_op jit(solution)/shard_map/psum | solution.py:421
  126.6 2.8 %collective-permute-start.23 = (bf16[64,2560]{1,0:T(8,128)(2,1)}, bf16[64,2560]{1,0:T(8,128)(2,1)}, u32[]{:S(2)}, u32[]{:S(2)}) collective-permute-start(bf16[64,2560]{1,0:T(8,128)(2,1)} %shard_map.120), channel_id=1, source_target_pairs={{0,16},{2,18},{4,20},{6,22},{8,24},{10,26},{12,28},{14,30},{16,0},... | collective-permute-start | bytes 983048 | tf_op jit(solution)/shard_map/ppermute | solution.py:29
  129.4 3.7 %collective-permute-start.24 = (bf16[64,2560]{1,0:T(8,128)(2,1)}, bf16[64,2560]{1,0:T(8,128)(2,1)}, u32[]{:S(2)}, u32[]{:S(2)}) collective-permute-start(bf16[64,2560]{1,0:T(8,128)(2,1)} %shard_map.121), channel_id=1, source_target_pairs={{0,8},{2,10},{4,12},{6,14},{8,0},{10,2},{12,4},{14,6},{16,24},{18,... | collective-permute-start | bytes 983048 | tf_op jit(solution)/shard_map/ppermute | solution.py:29
  139.7 5.2 %collective-permute-done.23 = bf16[64,2560]{1,0:T(8,128)(2,1)} collective-permute-done((bf16[64,2560]{1,0:T(8,128)(2,1)}, bf16[64,2560]{1,0:T(8,128)(2,1)}, u32[]{:S(2)}, u32[]{:S(2)}) %collective-permute-start.23) | collective-permute-done | bytes 327712 | tf_op jit(solution)/shard_map/ppermute | solution.py:29
  144.9 4.6 %collective-permute-start.27 = (f32[5248]{0:T(1024)S(1)}, f32[5248]{0:T(1024)S(1)}, u32[]{:S(2)}, u32[]{:S(2)}) collective-permute-start(f32[5248]{0:T(1024)S(1)} %add_add_fusion.1), channel_id=1, source_target_pairs={{0,24},{2,26},{4,28},{6,30},{8,16},{10,18},{12,20},{14,22},{16,8},... | collective-permute-start | bytes 62984 | tf_op jit(solution)/shard_map/ppermute | solution.py:29
  150.2 3.8 %fusion.8 = (bf16[128,2560]{1,0:T(8,128)(2,1)}, bf16[128,2560]{1,0:T(8,128)(2,1)}) fusion(bf16[128,2560]{1,0:T(8,128)(2,1)S(1)} %copy-done.2, bf16[64,2560]{1,0:T(8,128)(2,1)} %collective-permute-done.24, bf16[64,2560]{1,0:T(8,128)(2,1)} %collective-permute-done.23, f32[128,2560]{1,0:T(8,128)} %copy-done.8, bf16[64,2560]{1,0:T(8,128)(2,1)S(1)} %slice.19, ...), kind=kLoop, calls=%fused_computation.16 | loop fusion | flops 11468800 | bytes 5242880 | tf_op jit(solution)/shard_map/convert_element_type | solution.py:459
  154.9 2.5 %psum.15 = f32[128]{0:T(128)S(1)} all-reduce(f32[128]{0:T(128)S(1)} %get-tuple-element.120), channel_id=1, replica_groups=mesh['dp'=16,'mp'=2] {'mp'}, use_global_device_ids=true, to_apply=%region_2.0 | all-reduce | flops 128 | bytes 1024 | tf_op jit(solution)/shard_map/psum | solution.py:465
  159.3 1.8 %multiply_multiply_fusion = f32[256,2560]{1,0:T(8,128)} fusion(f32[256,2560]{1,0:T(8,128)S(1)} %get-tuple-element.105.grad, f32[2560]{0:T(1024)S(1)} %sqrt.15, f32[256]{0:T(256)S(1)} %sqrt_divide_fusion), kind=kLoop, calls=%fused_computation.7 | loop fusion | flops 1310720 | bytes 5254144 | tf_op jit(solution)/shard_map/mul | solution.py:469
  (97 shorter events, 38.9 us)
Async XLA Ops:
  5.9 31.8 %collective-permute-start.4 = (bf16[256,2560]{1,0:T(8,128)(2,1)S(1)}, bf16[256,2560]{1,0:T(8,128)(2,1)S(1)}, u32[]{:S(2)}, u32[]{:S(2)}) collective-permute-start(bf16[256,2560]{1,0:T(8,128)(2,1)S(1)} %copy-done), channel_id=1, source_target_pairs={{0,4},{2,6},{4,0},{6,2},{8,12},{10,14},{12,8},{14,10},{16,20},{18,... | collective-permute-start | bytes 3932168 | tf_op jit(solution)/shard_map/ppermute | solution.py:29
  9.0 30.2 %collective-permute-start.3 = (bf16[256,2560]{1,0:T(8,128)(2,1)S(1)}, bf16[256,2560]{1,0:T(8,128)(2,1)S(1)}, u32[]{:S(2)}, u32[]{:S(2)}) collective-permute-start(bf16[256,2560]{1,0:T(8,128)(2,1)S(1)} %copy-done), channel_id=1, source_target_pairs={{0,2},{2,0},{4,6},{6,4},{8,10},{10,8},{12,14},{14,12},{16,18},{18,... | collective-permute-start | bytes 3932168 | tf_op jit(solution)/shard_map/ppermute | solution.py:29
  10.5 38.1 %collective-permute-start = (bf16[128,2048]{1,0:T(8,128)(2,1)S(1)}, bf16[128,2048]{1,0:T(8,128)(2,1)S(1)}, u32[]{:S(2)}, u32[]{:S(2)}) collective-permute-start(bf16[128,2048]{1,0:T(8,128)(2,1)S(1)} %get-tuple-element.64.refs_1_.refs_6_), channel_id=1, source_target_pairs={{0,8},{2,10},{4,12},{6,14},{8,0},{10,2},{12,4},{14,6},{16,24},{18,... | collective-permute-start | bytes 1572872 | tf_op jit(solution)/shard_map/ppermute | solution.py:29
  12.0 36.5 %collective-permute-start.1 = (bf16[128,2048]{1,0:T(8,128)(2,1)S(1)}, bf16[128,2048]{1,0:T(8,128)(2,1)S(1)}, u32[]{:S(2)}, u32[]{:S(2)}) collective-permute-start(bf16[128,2048]{1,0:T(8,128)(2,1)S(1)} %get-tuple-element.65), channel_id=1, source_target_pairs={{0,16},{2,18},{4,20},{6,22},{8,24},{10,26},{12,28},{14,30},{16,0},... | collective-permute-start | bytes 1572872 | tf_op jit(solution)/shard_map/ppermute | solution.py:29
  39.6 20.7 %collective-permute-start.8 = (bf16[128,2560]{1,0:T(8,128)(2,1)S(1)}, bf16[128,2560]{1,0:T(8,128)(2,1)S(1)}, u32[]{:S(2)}, u32[]{:S(2)}) collective-permute-start(bf16[128,2560]{1,0:T(8,128)(2,1)S(1)} %get-tuple-element.68), channel_id=1, source_target_pairs={{0,4},{2,6},{4,0},{6,2},{8,12},{10,14},{12,8},{14,10},{16,20},{18,... | collective-permute-start | bytes 1966088 | tf_op jit(solution)/shard_map/ppermute | solution.py:29
  40.1 20.3 %collective-permute-start.9 = (bf16[128,2560]{1,0:T(8,128)(2,1)S(1)}, bf16[128,2560]{1,0:T(8,128)(2,1)S(1)}, u32[]{:S(2)}, u32[]{:S(2)}) collective-permute-start(bf16[128,2560]{1,0:T(8,128)(2,1)S(1)} %get-tuple-element.69), channel_id=1, source_target_pairs={{0,2},{2,0},{4,6},{6,4},{8,10},{10,8},{12,14},{14,12},{16,18},{18,... | collective-permute-start | bytes 1966088 | tf_op jit(solution)/shard_map/ppermute | solution.py:29
  41.7 6.9 %collective-permute-start.2 = (bf16[128,512]{1,0:T(8,128)(2,1)S(1)}, bf16[128,512]{1,0:T(8,128)(2,1)S(1)}, u32[]{:S(2)}, u32[]{:S(2)}) collective-permute-start(bf16[128,512]{1,0:T(8,128)(2,1)S(1)} %get-tuple-element.66), channel_id=1, source_target_pairs={{0,24},{2,26},{4,28},{6,30},{8,16},{10,18},{12,20},{14,22},{16,8},... | collective-permute-start | bytes 393224 | tf_op jit(solution)/shard_map/ppermute | solution.py:29
  48.8 11.5 %collective-permute-start.5 = (bf16[128,1536]{1,0:T(8,128)(2,1)S(1)}, bf16[128,1536]{1,0:T(8,128)(2,1)S(1)}, u32[]{:S(2)}, u32[]{:S(2)}) collective-permute-start(bf16[128,1536]{1,0:T(8,128)(2,1)S(1)} %get-tuple-element.73), channel_id=1, source_target_pairs={{0,8},{2,10},{4,12},{6,14},{8,0},{10,2},{12,4},{14,6},{16,24},{18,... | collective-permute-start | bytes 1179656 | tf_op jit(solution)/shard_map/ppermute | solution.py:29
  63.1 23.3 %collective-permute-start.13 = (bf16[256,1536]{1,0:T(8,128)(2,1)S(1)}, bf16[256,1536]{1,0:T(8,128)(2,1)S(1)}, u32[]{:S(2)}, u32[]{:S(2)}) collective-permute-start(bf16[256,1536]{1,0:T(8,128)(2,1)S(1)} %get-tuple-element.87), channel_id=1, source_target_pairs={{0,4},{2,6},{4,0},{6,2},{8,12},{10,14},{12,8},{14,10},{16,20},{18,... | collective-permute-start | bytes 2359304 | tf_op jit(solution)/shard_map/ppermute | solution.py:29
  64.7 21.7 %collective-permute-start.12 = (bf16[256,1536]{1,0:T(8,128)(2,1)S(1)}, bf16[256,1536]{1,0:T(8,128)(2,1)S(1)}, u32[]{:S(2)}, u32[]{:S(2)}) collective-permute-start(bf16[256,1536]{1,0:T(8,128)(2,1)S(1)} %get-tuple-element.81), channel_id=1, source_target_pairs={{0,2},{2,0},{4,6},{6,4},{8,10},{10,8},{12,14},{14,12},{16,18},{18,... | collective-permute-start | bytes 2359304 | tf_op jit(solution)/shard_map/ppermute | solution.py:29
  65.2 13.9 %collective-permute-start.7 = (bf16[128,1024]{1,0:T(8,128)(2,1)S(1)}, bf16[128,1024]{1,0:T(8,128)(2,1)S(1)}, u32[]{:S(2)}, u32[]{:S(2)}) collective-permute-start(bf16[128,1024]{1,0:T(8,128)(2,1)S(1)} %get-tuple-element.77.refs_1_), channel_id=1, source_target_pairs={{0,16},{2,18},{4,20},{6,22},{8,24},{10,26},{12,28},{14,30},{16,0},... | collective-permute-start | bytes 786440 | tf_op jit(solution)/shard_map/ppermute | solution.py:29
  67.5 17.2 %collective-permute-start.10 = (bf16[128,1024]{1,0:T(8,128)(2,1)S(1)}, bf16[128,1024]{1,0:T(8,128)(2,1)S(1)}, u32[]{:S(2)}, u32[]{:S(2)}) collective-permute-start(bf16[128,1024]{1,0:T(8,128)(2,1)S(1)} %get-tuple-element.77.refs_1_), channel_id=1, source_target_pairs={{0,8},{2,10},{4,12},{6,14},{8,0},{10,2},{12,4},{14,6},{16,24},{18,... | collective-permute-start | bytes 786440 | tf_op jit(solution)/shard_map/ppermute | solution.py:29
  79.1 7.2 %collective-permute-start.11 = (bf16[128,1024]{1,0:T(8,128)(2,1)S(1)}, bf16[128,1024]{1,0:T(8,128)(2,1)S(1)}, u32[]{:S(2)}, u32[]{:S(2)}) collective-permute-start(bf16[128,1024]{1,0:T(8,128)(2,1)S(1)} %collective-permute-done.7.refs_3_), channel_id=1, source_target_pairs={{0,8},{2,10},{4,12},{6,14},{8,0},{10,2},{12,4},{14,6},{16,24},{18,... | collective-permute-start | bytes 786440 | tf_op jit(solution)/shard_map/ppermute | solution.py:29
  88.1 12.0 %collective-permute-start.14 = (bf16[256,1024]{1,0:T(8,128)(2,1)S(1)}, bf16[256,1024]{1,0:T(8,128)(2,1)S(1)}, u32[]{:S(2)}, u32[]{:S(2)}) collective-permute-start(bf16[256,1024]{1,0:T(8,128)(2,1)S(1)} %get-tuple-element.92), channel_id=1, source_target_pairs={{0,2},{2,0},{4,6},{6,4},{8,10},{10,8},{12,14},{14,12},{16,18},{18,... | collective-permute-start | bytes 1572872 | tf_op jit(solution)/shard_map/ppermute | solution.py:29
  89.7 12.9 %collective-permute-start.15 = (bf16[256,1024]{1,0:T(8,128)(2,1)S(1)}, bf16[256,1024]{1,0:T(8,128)(2,1)S(1)}, u32[]{:S(2)}, u32[]{:S(2)}) collective-permute-start(bf16[256,1024]{1,0:T(8,128)(2,1)S(1)} %get-tuple-element.97), channel_id=1, source_target_pairs={{0,4},{2,6},{4,0},{6,2},{8,12},{10,14},{12,8},{14,10},{16,20},{18,... | collective-permute-start | bytes 1572872 | tf_op jit(solution)/shard_map/ppermute | solution.py:29
  90.2 29.0 %collective-permute-start.18 = (bf16[128,2560]{1,0:T(8,128)(2,1)S(1)}, bf16[128,2560]{1,0:T(8,128)(2,1)S(1)}, u32[]{:S(2)}, u32[]{:S(2)}) collective-permute-start(bf16[128,2560]{1,0:T(8,128)(2,1)S(1)} %get-tuple-element.88), channel_id=1, source_target_pairs={{0,8},{2,10},{4,12},{6,14},{8,0},{10,2},{12,4},{14,6},{16,24},{18,... | collective-permute-start | bytes 1966088 | tf_op jit(solution)/shard_map/ppermute | solution.py:29
  91.6 26.9 %collective-permute-start.19 = (bf16[128,2560]{1,0:T(8,128)(2,1)S(1)}, bf16[128,2560]{1,0:T(8,128)(2,1)S(1)}, u32[]{:S(2)}, u32[]{:S(2)}) collective-permute-start(bf16[128,2560]{1,0:T(8,128)(2,1)S(1)} %get-tuple-element.102), channel_id=1, source_target_pairs={{0,16},{2,18},{4,20},{6,22},{8,24},{10,26},{12,28},{14,30},{16,0},... | collective-permute-start | bytes 1966088 | tf_op jit(solution)/shard_map/ppermute | solution.py:29
  101.1 18.1 %collective-permute-start.16 = (bf16[128,2560]{1,0:T(8,128)(2,1)S(1)}, bf16[128,2560]{1,0:T(8,128)(2,1)S(1)}, u32[]{:S(2)}, u32[]{:S(2)}) collective-permute-start(bf16[128,2560]{1,0:T(8,128)(2,1)S(1)} %shard_map.117), channel_id=1, source_target_pairs={{0,4},{2,6},{4,0},{6,2},{8,12},{10,14},{12,8},{14,10},{16,20},{18,... | collective-permute-start | bytes 1966088 | tf_op jit(solution)/shard_map/ppermute | solution.py:29
  102.7 16.5 %collective-permute-start.17 = (bf16[128,2560]{1,0:T(8,128)(2,1)S(1)}, bf16[128,2560]{1,0:T(8,128)(2,1)S(1)}, u32[]{:S(2)}, u32[]{:S(2)}) collective-permute-start(bf16[128,2560]{1,0:T(8,128)(2,1)S(1)} %shard_map.118), channel_id=1, source_target_pairs={{0,2},{2,0},{4,6},{6,4},{8,10},{10,8},{12,14},{14,12},{16,18},{18,... | collective-permute-start | bytes 1966088 | tf_op jit(solution)/shard_map/ppermute | solution.py:29
  126.6 18.3 %collective-permute-start.23 = (bf16[64,2560]{1,0:T(8,128)(2,1)}, bf16[64,2560]{1,0:T(8,128)(2,1)}, u32[]{:S(2)}, u32[]{:S(2)}) collective-permute-start(bf16[64,2560]{1,0:T(8,128)(2,1)} %shard_map.120), channel_id=1, source_target_pairs={{0,16},{2,18},{4,20},{6,22},{8,24},{10,26},{12,28},{14,30},{16,0},... | collective-permute-start | bytes 983048 | tf_op jit(solution)/shard_map/ppermute | solution.py:29
  129.4 15.6 %collective-permute-start.24 = (bf16[64,2560]{1,0:T(8,128)(2,1)}, bf16[64,2560]{1,0:T(8,128)(2,1)}, u32[]{:S(2)}, u32[]{:S(2)}) collective-permute-start(bf16[64,2560]{1,0:T(8,128)(2,1)} %shard_map.121), channel_id=1, source_target_pairs={{0,8},{2,10},{4,12},{6,14},{8,0},{10,2},{12,4},{14,6},{16,24},{18,... | collective-permute-start | bytes 983048 | tf_op jit(solution)/shard_map/ppermute | solution.py:29
  133.8 5.6 %collective-permute-start.22 = (f32[5248]{0:T(1024)S(1)}, f32[5248]{0:T(1024)S(1)}, u32[]{:S(2)}, u32[]{:S(2)}) collective-permute-start(f32[5248]{0:T(1024)S(1)} %reduce), channel_id=1, source_target_pairs={{0,6},{2,4},{4,2},{6,0},{8,14},{10,12},{12,10},{14,8},{16,22},{18,... | collective-permute-start | bytes 62984 | tf_op jit(solution)/shard_map/ppermute | solution.py:29
  144.9 9.1 %collective-permute-start.27 = (f32[5248]{0:T(1024)S(1)}, f32[5248]{0:T(1024)S(1)}, u32[]{:S(2)}, u32[]{:S(2)}) collective-permute-start(f32[5248]{0:T(1024)S(1)} %add_add_fusion.1), channel_id=1, source_target_pairs={{0,24},{2,26},{4,28},{6,30},{8,16},{10,18},{12,20},{14,22},{16,8},... | collective-permute-start | bytes 62984 | tf_op jit(solution)/shard_map/ppermute | solution.py:29
  149.6 4.7 %collective-permute-start.26 = (f32[5248]{0:T(1024)S(1)}, f32[5248]{0:T(1024)S(1)}, u32[]{:S(2)}, u32[]{:S(2)}) collective-permute-start(f32[5248]{0:T(1024)S(1)} %add_add_fusion.1), channel_id=1, source_target_pairs={{0,16},{2,18},{4,20},{6,22},{8,24},{10,26},{12,28},{14,30},{16,0},... | collective-permute-start | bytes 62984 | tf_op jit(solution)/shard_map/ppermute | solution.py:29
  (22 other events, 99.4 us)

commit v10 on v9

--- a/solution.py
+++ b/solution.py
@@ -200,7 +200,7 @@
     def kernel(*refs):
         out, at = refs[-1], 0
         for part, other, width in zip(refs, refs[len(parts) :], widths):
-            out[:, at : at + width] = (part[...] + other[rows:, :].astype(jnp.float32)).astype(jnp.bfloat16)
+            out[:, at : at + width] = (part[...] + other[-rows:, :].astype(jnp.float32)).astype(jnp.bfloat16)
             at += width
 
     vmem = pl.BlockSpec(memory_space=pltpu.VMEM)
@@ -349,10 +349,10 @@
     extra, every, whole = (split, 2 * rows), (0, tokens), (0, units)
     left1, left2, message3 = flip(message1, z_bit), flip(message2, w_bit), flip(message3, z_bit | w_bit)
     weight1, weight2 = flip(down_weight, x_bit), flip(down_weight, y_bit)
-
+    message3, weight1, weight2 = barrier((message3, weight1, weight2))
     to_y, to_x = cut([weight1, weight2], [(0, (0, q), whole, 0, 0), (1, (q, q), whole, 1, 0)], [(q, units)] * 2)
     weight3a, weight3b = flip(to_y, y_bit), flip(to_x, x_bit)
-    left1, left2, message3, _, _ = barrier((left1, left2, message3, to_y, to_x))
+    left1, left2, message3, right, _, _ = barrier((left1, left2, message3, right, to_y, to_x))
     to_z, mine = cut(
         [left1, left2, message3],
         [
@@ -364,11 +364,12 @@
         [(tokens, split), (tokens, 6 * rows)],
     )
     left3 = flip(to_z, z_bit)
+    right2 = flip(right, w_bit)
     theirs = flip(mine, 1, "mp")
     share = assemble(own, mine, theirs, place, rows)
 
-    left3, share, right = barrier((left3, share, right))
-    right1, right2 = flip(right, z_bit), flip(right, w_bit)
+    left3, right2, share, right, weight3a, weight3b = barrier((left3, right2, share, right, weight3a, weight3b))
+    right1, right3 = flip(right, z_bit), flip(right2, z_bit)
 
     def low_sent(size):
         return [(2 * size, 3 * size), (6 * size, 7 * size)]
@@ -384,30 +385,28 @@
         return [(r, jnp.float32) for r in ranges]
 
     lefts = [message1, left1, left2, left3]
-    share, weight3a, weight3b = barrier((share, weight3a, weight3b))
     left_to_x, left_to_y = products(share, [(lefts, split, sent(q), True)], steps)
     left_from_x, left_from_y = flip(left_to_x, x_bit), flip(left_to_y, y_bit)
-    right2, share, _ = barrier((right2, share, left_to_x))
-    right3 = flip(right2, z_bit)
+    share, _ = barrier((share, left_to_x))
 
     weights = [down_weight, weight1, weight2, weight3a, weight3b]
-    to_z, to_w, *left_parts = products(
-        share, [(weights, units, sent(t), False), (lefts, split, kept(q), True)], steps
-    )
-    from_z, from_w = flip(to_z, z_bit), flip(to_w, w_bit)
-
-    right1, right3, left_from_x, left_from_y, share, _ = barrier(
-        (right1, right3, left_from_x, left_from_y, share, to_z)
+    first = [(high_sent(t)[1:], jnp.bfloat16), (high_sent(t)[:1], jnp.bfloat16), (low_sent(t), jnp.bfloat16)]
+    to_w1, to_w2, to_z = products(share, [(weights, units, first, False)], steps)
+    from_w1, from_w2, from_z = flip(to_w1, w_bit), flip(to_w2, w_bit), flip(to_z, z_bit)
+
+    right1, right3, left_from_x, left_from_y, from_w1, share = barrier(
+        (right1, right3, left_from_x, left_from_y, from_w1, share)
     )
     rights = [right, right1, right2, right3]
     right_to_x, right_to_y = products(share, [(rights, units - split, sent(q), True)], steps)
     right_from_x, right_from_y = flip(right_to_x, x_bit), flip(right_to_y, y_bit)
     share, _ = barrier((share, right_to_x))
+    left_parts = products(share, [(lefts, split, kept(q), True)], steps)
     parts = products(share, [(rights, units - split, kept(q), True), (weights, units, kept(t), False)], steps)
 
     grad_a = flip(add_tail([left_parts[1], parts[1]], [left_from_x, right_from_x]), y_bit)
     grad_b = flip(add_tail([left_parts[2], parts[2]], [left_from_y, right_from_y]), x_bit)
-    grad_a, grad_b, from_z, from_w = barrier((grad_a, grad_b, from_z, from_w))
+    grad_a, grad_b, from_z, from_w2 = barrier((grad_a, grad_b, from_z, from_w2))
     grad, row_part = sum_up(
         [left_parts[0], parts[0]],
         [left_from_x, right_from_x],
@@ -417,12 +416,38 @@
         1.0 / math.sqrt(tokens * lax.axis_size("dp")),
     )
 
-    to_w, to_z = add_tail([parts[4]], [from_z]), add_tail([parts[5]], [from_w])
+    to_w, to_z = add_tail([parts[4]], [from_z]), add_tail([parts[5]], [from_w1])
     row_sum = lax.psum(row_part, "mp")
     row_sum, to_w, to_z = barrier((row_sum, to_w, to_z))
     last_a, last_b = flip(to_w, w_bit), flip(to_z, z_bit)
-    arrived = jnp.concatenate([from_z[:t], from_w[:t]], axis=0)
-    return grad, row_sum, (parts[3], arrived, last_a, last_b)
+    return grad, row_sum, (parts[3], from_z, from_w2, last_a, last_b)
+
+
+def hidden_gradients(gate_pre, up_pre, own_part, from_low, from_high, last_a, last_b):
+    tokens, units = gate_pre.shape
+    half, step = tokens // 2, 16
+
+    def kernel(gate, up, own, low, high, last_a, last_b, gate_grad, up_grad):
+        for h, (other, last) in enumerate(((low, last_a), (high, last_b))):
+
+            @pl.loop(0, half // step)
+            def _(i):
+                here = pl.ds(pl.multiple_of(i * step, step), step)
+                there = pl.ds(pl.multiple_of(h * half + i * step, step), step)
+                value = own[there, :] + other[here, :].astype(jnp.float32) + last[here, :].astype(jnp.float32)
+                activated, derivative = gelu_parts(gate[there, :].astype(jnp.float32))
+                gate_grad[there, :] = (value * up[there, :].astype(jnp.float32) * derivative).astype(jnp.bfloat16)
+                up_grad[there, :] = (value * activated).astype(jnp.bfloat16)
+
+    vmem = pl.BlockSpec(memory_space=pltpu.VMEM)
+    return pl.pallas_call(
+        kernel,
+        out_shape=[jax.ShapeDtypeStruct((tokens, units), jnp.bfloat16)] * 2,
+        in_specs=[vmem] * 7,
+        out_specs=[vmem] * 2,
+        compiler_params=pltpu.CompilerParams(vmem_limit_bytes=12 << 20),
+        cost_estimate=EAGER,
+    )(gate_pre, up_pre, own_part, from_low, from_high, last_a, last_b)
 
 
 def local(out_grad, gate_pre, up_pre, down_weight, row_moment, col_moment):
@@ -435,11 +460,11 @@
     total_units = units * lax.axis_size("mp")
     staged = size == 16 and lax.axis_size("mp") == 2 and rows % 256 == 0 and tokens % 32 == 0 and units % 2560 == 0
     if staged:
-        grad, row_sum, (own_part, arrived, last_a, last_b) = staged_products(out_grad, gate_pre, up_pre, down_weight)
+        grad, row_sum, terms = staged_products(out_grad, gate_pre, up_pre, down_weight)
         row_moment_new, sums = column_sums(grad, row_sum, row_moment[None, :], decay, total_units)
         row_moment_new, sums = row_moment_new[0], group_sum(sums[0], all_bits[:INNER_BITS])
-        sums, last_a, last_b = lax.optimization_barrier((sums, last_a, last_b))
-        hidden_grad = own_part + arrived.astype(jnp.float32) + jnp.concatenate([last_a, last_b], axis=0).astype(jnp.float32)
+        sums, terms = lax.optimization_barrier((sums, terms))
+        gate_grad, up_grad = hidden_gradients(gate_pre, up_pre, *terms)
     else:
         product, hidden_grad = general_products(
             out_grad, gate_pre, up_pre, down_weight, all_bits[:INNER_BITS], all_bits[INNER_BITS:]
@@ -453,10 +478,9 @@
         scaled_part = jnp.sum(powers / row_moment_new[:, None], axis=0)
         sums = jnp.concatenate([col_part, scaled_part, jnp.broadcast_to(jnp.sum(row_moment_new), (128,))])
         sums = group_sum(sums, all_bits[:INNER_BITS])
-
-    activated, derivative = gelu_parts(gate_pre.astype(jnp.float32))
-    gate_grad = (hidden_grad * up_pre.astype(jnp.float32) * derivative).astype(jnp.bfloat16)
-    up_grad = (hidden_grad * activated).astype(jnp.bfloat16)
+        activated, derivative = gelu_parts(gate_pre.astype(jnp.float32))
+        gate_grad = (hidden_grad * up_pre.astype(jnp.float32) * derivative).astype(jnp.bfloat16)
+        up_grad = (hidden_grad * activated).astype(jnp.bfloat16)
 
     sums = group_sum(sums, all_bits[INNER_BITS:])
     col_moment_new = decay * col_moment + (1.0 - decay) * (sums[:units] / total_rows)

time: 163 us -> 168 us (1.031)
  waiting for transfers between devices: 71.5 us -> 79 us
  starting transfers between devices: 46.4 us -> 40.1 us
  Pallas kernels: 20.2 us -> 24.8 us
  other arithmetic: 6.38 us -> 2.56 us
  local copies, waits for them, and re-layouts: 9.43 us -> 12.9 us
    ppermute x28 -> x29, waiting for transfers between devices: 71.5 us -> 79 us  [flip(): return lax.ppermute(value, axis, [(i, i ^ bits) for i in range(size)])]
    ppermute x28 -> x29, starting transfers between devices: 46.4 us -> 40.1 us  [flip(): return lax.ppermute(value, axis, [(i, i ^ bits) for i in range(size)])]
    unnamed x36 -> x40, local copies, waits for them, and re-layouts: 6.92 us -> 12.3 us
    convert_element_type x1 -> x0, other arithmetic: 3.83 us -> none  [local(): up_grad = (hidden_grad * activated).astype(jnp.bfloat16)]
    pallas_call x0 -> x1, Pallas kernels: none -> 3.47 us  [hidden_gradients(): pl.pallas_call(kernel, out_shape=[jax.ShapeDtypeStruct((tokens, units), j...]
    slice x2 -> x0, local copies, waits for them, and re-layouts: 1.99 us -> none  [staged_products(): arrived = jnp.concatenate([from_z[:t], from_w[:t]], axis=0)]
    pallas_call x4 -> x5, Pallas kernels: 14.1 us -> 15.9 us  [products(): pl.pallas_call(kernel, grid=(steps,), out_shape=[jax.ShapeDtypeStruct((he...]
  transfers between devices with their start and end apart: 28 -> 29, of which waited for: 14 -> 12; matrix products, arithmetic and copies ran while one was open for 4% -> 0% of each run, Pallas kernels for 7% -> 10%
where the time goes in v10:
time: 168 us
  waiting for transfers between devices  79 us (47%)
  starting transfers between devices  40.1 us (24%)
  Pallas kernels  24.8 us (15%)
  local copies, waits for them, and re-layouts  12.9 us (8%)
  blocking collectives  5.07 us (3%)
  between operations  3.35 us (2%)
  other arithmetic  2.56 us (2%)
    ppermute x29, waiting for transfers between devices, flip(): return lax.ppermute(value, axis, [(i, i ^ bits) for i in range(size)])  79 us
    ppermute x29, starting transfers between devices, flip(): return lax.ppermute(value, axis, [(i, i ^ bits) for i in range(size)])  40.1 us
    pallas_call x5, Pallas kernels, products(): pl.pallas_call(kernel, grid=(steps,), out_shape=[jax.ShapeDtypeStruct((he...  15.9 us
    unnamed x40, local copies, waits for them, and re-layouts  12.3 us
    pallas_call x1, Pallas kernels, hidden_gradients(): pl.pallas_call(kernel, out_shape=[jax.ShapeDtypeStruct((tokens, units), j...  3.47 us
  transfers between devices with their start and end apart: 29, of which 12 were waited for; matrix products, arithmetic and copies ran while one was open for 0% of the time, Pallas kernels for 10%

profile of v10, /device:TPU:0, one launch (start us, length us, event | category | flops | bytes accessed | tf_op | source)
XLA Modules:
  0.0 167.7 jit_solution(10427173208270057036)
XLA Ops:
  5.8 3.0 %collective-permute-start.4 = (bf16[256,2560]{1,0:T(8,128)(2,1)}, bf16[256,2560]{1,0:T(8,128)(2,1)S(1)}, u32[]{:S(2)}, u32[]{:S(2)}) collective-permute-start(bf16[256,2560]{1,0:T(8,128)(2,1)} %refs_5_), channel_id=1, source_target_pairs={{0,4},{2,6},{4,0},{6,2},{8,12},{10,14},{12,8},{14,10},{16,20},{18,... | collective-permute-start | bytes 3932168 | tf_op jit(solution)/shard_map/ppermute | solution.py:29
  11.9 2.6 %collective-permute-start.1 = (bf16[128,2048]{1,0:T(8,128)(2,1)S(1)}, bf16[128,2048]{1,0:T(8,128)(2,1)S(1)}, u32[]{:S(2)}, u32[]{:S(2)}) collective-permute-start(bf16[128,2048]{1,0:T(8,128)(2,1)S(1)} %get-tuple-element.75), channel_id=1, source_target_pairs={{0,16},{2,18},{4,20},{6,22},{8,24},{10,26},{12,28},{14,30},{16,0},... | collective-permute-start | bytes 1572872 | tf_op jit(solution)/shard_map/ppermute | solution.py:29
  14.7 24.9 %collective-permute-done.2.refs_2_ = bf16[128,512]{1,0:T(8,128)(2,1)S(1)} collective-permute-done((bf16[128,512]{1,0:T(8,128)(2,1)S(1)}, bf16[128,512]{1,0:T(8,128)(2,1)S(1)}, u32[]{:S(2)}, u32[]{:S(2)}) %collective-permute-start.2) | collective-permute-done | bytes 131104 | tf_op jit(solution)/shard_map/ppermute | solution.py:29
  42.0 2.9 %collective-permute-start.5 = (bf16[128,1536]{1,0:T(8,128)(2,1)S(1)}, bf16[128,1536]{1,0:T(8,128)(2,1)S(1)}, u32[]{:S(2)}, u32[]{:S(2)}) collective-permute-start(bf16[128,1536]{1,0:T(8,128)(2,1)S(1)} %get-tuple-element.87), channel_id=1, source_target_pairs={{0,8},{2,10},{4,12},{6,14},{8,0},{10,2},{12,4},{14,6},{16,24},{18,... | collective-permute-start | bytes 1179656 | tf_op jit(solution)/shard_map/ppermute | solution.py:29
  46.9 12.7 %collective-permute-done.6.refs_3_ = bf16[128,1024]{1,0:T(8,128)(2,1)S(1)} collective-permute-done((bf16[128,1024]{1,0:T(8,128)(2,1)S(1)}, bf16[128,1024]{1,0:T(8,128)(2,1)S(1)}, u32[]{:S(2)}, u32[]{:S(2)}) %collective-permute-start.6) | collective-permute-done | bytes 262176 | tf_op jit(solution)/shard_map/ppermute | solution.py:29
  60.3 2.7 %shard_map.113 = (bf16[256,1536]{1,0:T(8,128)(2,1)S(1)}, bf16[256,1536]{1,0:T(8,128)(2,1)S(1)}) custom-call(bf16[512,1024]{1,0:T(8,128)(2,1)S(1)} %shard_map.112.refs_0_, bf16[128,2048]{1,0:T(8,128)(2,1)S(1)} %get-tuple-element.74.refs_1_, bf16[128,2048]{1,0:T(8,128)(2,1)S(1)} %collective-permute-done.refs_0_.refs_2_, ...), custom_call_target="tpu_custom_call" | custom-call | tf_op jit(solution)/shard_map/pallas_call | solution.py:321
  66.1 4.1 %shard_map.114 = (bf16[64,2560]{1,0:T(8,128)(2,1)S(1)}, bf16[64,2560]{1,0:T(8,128)(2,1)S(1)}, bf16[128,2560]{1,0:T(8,128)(2,1)S(1)}) custom-call(bf16[512,1024]{1,0:T(8,128)(2,1)S(1)} %shard_map.112.refs_0_, bf16[256,2560]{1,0:T(8,128)(2,1)S(1)} %copy-done, bf16[256,2560]{1,0:T(8,128)(2,1)S(1)} %collective-permute-done.3.refs_0_.refs_2_.refs_6_, ...), custom_call_target="tpu_custom_call" | custom-call | tf_op jit(solution)/shard_map/pallas_call | solution.py:321
  70.2 2.8 %collective-permute-start.14 = (bf16[64,2560]{1,0:T(8,128)(2,1)S(1)}, bf16[64,2560]{1,0:T(8,128)(2,1)S(1)}, u32[]{:S(2)}, u32[]{:S(2)}) collective-permute-start(bf16[64,2560]{1,0:T(8,128)(2,1)S(1)} %get-tuple-element.100), channel_id=1, source_target_pairs={{0,16},{2,18},{4,20},{6,22},{8,24},{10,26},{12,28},{14,30},{16,0},... | collective-permute-start | bytes 983048 | tf_op jit(solution)/shard_map/ppermute | solution.py:29
  75.0 11.8 %collective-permute-done.10.refs_2_ = bf16[128,1024]{1,0:T(8,128)(2,1)S(1)} collective-permute-done((bf16[128,1024]{1,0:T(8,128)(2,1)S(1)}, bf16[128,1024]{1,0:T(8,128)(2,1)S(1)}, u32[]{:S(2)}, u32[]{:S(2)}) %collective-permute-start.10) | collective-permute-done | bytes 262176 | tf_op jit(solution)/shard_map/ppermute | solution.py:29
  86.8 4.6 %collective-permute-done.11.refs_4_ = bf16[128,1024]{1,0:T(8,128)(2,1)S(1)} collective-permute-done((bf16[128,1024]{1,0:T(8,128)(2,1)S(1)}, bf16[128,1024]{1,0:T(8,128)(2,1)S(1)}, u32[]{:S(2)}, u32[]{:S(2)}) %collective-permute-start.11) | collective-permute-done | bytes 262176 | tf_op jit(solution)/shard_map/ppermute | solution.py:29
  91.3 1.7 %shard_map.115 = (bf16[256,1024]{1,0:T(8,128)(2,1)S(1)}, bf16[256,1024]{1,0:T(8,128)(2,1)S(1)}) custom-call(bf16[512,1024]{1,0:T(8,128)(2,1)S(1)} %shard_map.112.refs_0_, bf16[128,1024]{1,0:T(8,128)(2,1)S(1)} %get-tuple-element.91.refs_1_, bf16[128,1024]{1,0:T(8,128)(2,1)S(1)} %collective-permute-done.10.refs_2_, ...), custom_call_target="tpu_custom_call" | custom-call | tf_op jit(solution)/shard_map/pallas_call | solution.py:321
  95.9 4.5 %shard_map.117 = (f32[256,1024]{1,0:T(8,128)S(1)}, f32[128,1024]{1,0:T(8,128)S(1)}, f32[128,1024]{1,0:T(8,128)S(1)}, f32[128,2560]{1,0:T(8,128)S(1)}, f32[64,2560]{1,0:T(8,128)S(1)}, /*index=5*/f32[64,2560]{1,0:T(8,128)S(1)}) custom-call(bf16[512,1024]{1,0:T(8,128)(2,1)S(1)} %shard_map.112.refs_0_, bf16[128,1024]{1,0:T(8,128)(2,1)S(1)} %get-tuple-element.91.refs_1_, ...), custom_call_target="tpu_custom_call" | custom-call | tf_op jit(solution)/shard_map/pallas_call | solution.py:321
  100.4 2.8 %shard_map.116 = (f32[256,1536]{1,0:T(8,128)S(1)}, f32[128,1536]{1,0:T(8,128)S(1)}, f32[128,1536]{1,0:T(8,128)S(1)}) custom-call(bf16[512,1024]{1,0:T(8,128)(2,1)S(1)} %shard_map.112.refs_0_, bf16[128,2048]{1,0:T(8,128)(2,1)S(1)} %get-tuple-element.74.refs_1_, bf16[128,2048]{1,0:T(8,128)(2,1)S(1)} %collective-permute-done.refs_0_.refs_2_, ...), custom_call_target="tpu_custom_call" | custom-call | tf_op jit(solution)/shard_map/pallas_call | solution.py:321
  103.3 2.4 %collective-permute-done.15.refs_3_ = bf16[256,1024]{1,0:T(8,128)(2,1)S(1)} collective-permute-done((bf16[256,1024]{1,0:T(8,128)(2,1)S(1)}, bf16[256,1024]{1,0:T(8,128)(2,1)S(1)}, u32[]{:S(2)}, u32[]{:S(2)}) %collective-permute-start.15) | collective-permute-done | bytes 524320 | tf_op jit(solution)/shard_map/ppermute | solution.py:29
  108.1 2.7 %collective-permute-start.20 = (bf16[64,2560]{1,0:T(8,128)(2,1)S(1)}, bf16[64,2560]{1,0:T(8,128)(2,1)S(1)}, u32[]{:S(2)}, u32[]{:S(2)}) collective-permute-start(bf16[64,2560]{1,0:T(8,128)(2,1)S(1)} %get-tuple-element.116), channel_id=1, source_target_pairs={{0,16},{2,18},{4,20},{6,22},{8,24},{10,26},{12,28},{14,30},{16,0},... | collective-permute-start | bytes 983048 | tf_op jit(solution)/shard_map/ppermute | solution.py:29
  111.6 10.8 %collective-permute-done.20.high = bf16[64,2560]{1,0:T(8,128)(2,1)S(1)} collective-permute-done((bf16[64,2560]{1,0:T(8,128)(2,1)S(1)}, bf16[64,2560]{1,0:T(8,128)(2,1)S(1)}, u32[]{:S(2)}, u32[]{:S(2)}) %collective-permute-start.20) | collective-permute-done | bytes 327712 | tf_op jit(solution)/shard_map/ppermute | solution.py:29
  124.7 2.6 %psum.14.row_sum = f32[1,256]{1,0:T(1,128)S(1)} all-reduce(f32[1,256]{1,0:T(1,128)S(1)} %get-tuple-element.120), channel_id=1, replica_groups=mesh['dp'=16,'mp'=2] {'mp'}, use_global_device_ids=true, to_apply=%region_0.0 | all-reduce | flops 256 | bytes 2048 | tf_op jit(solution)/shard_map/psum | solution.py:420
  132.7 2.0 %collective-permute-start.23 = (f32[5248]{0:T(1024)S(1)}, f32[5248]{0:T(1024)S(1)}, u32[]{:S(2)}, u32[]{:S(2)}) collective-permute-start(f32[5248]{0:T(1024)S(1)} %reduce), channel_id=1, source_target_pairs={{0,6},{2,4},{4,2},{6,0},{8,14},{10,12},{12,10},{14,8},{16,22},{18,... | collective-permute-start | bytes 62984 | tf_op jit(solution)/shard_map/ppermute | solution.py:29
  139.1 7.8 %collective-permute-done.24.last_a = bf16[64,2560]{1,0:T(8,128)(2,1)} collective-permute-done((bf16[64,2560]{1,0:T(8,128)(2,1)}, bf16[64,2560]{1,0:T(8,128)(2,1)}, u32[]{:S(2)}, u32[]{:S(2)}) %collective-permute-start.24) | collective-permute-done | bytes 327712 | tf_op jit(solution)/shard_map/ppermute | solution.py:29
  147.4 2.2 %collective-permute-start.28 = (f32[5248]{0:T(1024)S(1)}, f32[5248]{0:T(1024)S(1)}, u32[]{:S(2)}, u32[]{:S(2)}) collective-permute-start(f32[5248]{0:T(1024)S(1)} %add_add_fusion.1), channel_id=1, source_target_pairs={{0,24},{2,26},{4,28},{6,30},{8,16},{10,18},{12,20},{14,22},{16,8},... | collective-permute-start | bytes 62984 | tf_op jit(solution)/shard_map/ppermute | solution.py:29
  149.7 2.1 %collective-permute-start.26 = (f32[5248]{0:T(1024)S(1)}, f32[5248]{0:T(1024)S(1)}, u32[]{:S(2)}, u32[]{:S(2)}) collective-permute-start(f32[5248]{0:T(1024)S(1)} %add_add_fusion.1), channel_id=1, source_target_pairs={{0,8},{2,10},{4,12},{6,14},{8,0},{10,2},{12,4},{14,6},{16,24},{18,... | collective-permute-start | bytes 62984 | tf_op jit(solution)/shard_map/ppermute | solution.py:29
  156.3 3.5 %shard_map.124 = (bf16[128,2560]{1,0:T(8,128)(2,1)}, bf16[128,2560]{1,0:T(8,128)(2,1)}) custom-call(bf16[128,2560]{1,0:T(8,128)(2,1)S(1)} %copy-done.2, bf16[128,2560]{1,0:T(8,128)(2,1)S(1)} %copy-done.4, f32[128,2560]{1,0:T(8,128)S(1)} %copy-done.9, bf16[128,2560]{1,0:T(8,128)(2,1)S(1)} %copy-done.7, bf16[64,2560]{1,0:T(8,128)(2,1)S(1)} %copy-done.14, ...), custom_call_target="tpu_custom_call" | custom-call | tf_op jit(solution)/shard_map/pallas_call | solution.py:443
  160.3 2.5 %psum.15 = f32[128]{0:T(128)S(1)} all-reduce(f32[128]{0:T(128)S(1)} %get-tuple-element.140), channel_id=1, replica_groups=mesh['dp'=16,'mp'=2] {'mp'}, use_global_device_ids=true, to_apply=%region_2.0 | all-reduce | flops 128 | bytes 1024 | tf_op jit(solution)/shard_map/psum | solution.py:489
  164.8 1.8 %multiply_multiply_fusion = f32[256,2560]{1,0:T(8,128)} fusion(f32[256,2560]{1,0:T(8,128)S(1)} %get-tuple-element.119.grad, f32[2560]{0:T(1024)S(1)} %sqrt.15, f32[256]{0:T(256)S(1)} %sqrt_divide_fusion), kind=kLoop, calls=%fused_computation | loop fusion | flops 1310720 | bytes 5254144 | tf_op jit(solution)/shard_map/mul | solution.py:493
  (102 shorter events, 42.8 us)
Async XLA Ops:
  5.8 33.8 %collective-permute-start.4 = (bf16[256,2560]{1,0:T(8,128)(2,1)}, bf16[256,2560]{1,0:T(8,128)(2,1)S(1)}, u32[]{:S(2)}, u32[]{:S(2)}) collective-permute-start(bf16[256,2560]{1,0:T(8,128)(2,1)} %refs_5_), channel_id=1, source_target_pairs={{0,4},{2,6},{4,0},{6,2},{8,12},{10,14},{12,8},{14,10},{16,20},{18,... | collective-permute-start | bytes 3932168 | tf_op jit(solution)/shard_map/ppermute | solution.py:29
  8.9 30.8 %collective-permute-start.3 = (bf16[256,2560]{1,0:T(8,128)(2,1)}, bf16[256,2560]{1,0:T(8,128)(2,1)S(1)}, u32[]{:S(2)}, u32[]{:S(2)}) collective-permute-start(bf16[256,2560]{1,0:T(8,128)(2,1)} %refs_5_), channel_id=1, source_target_pairs={{0,2},{2,0},{4,6},{6,4},{8,10},{10,8},{12,14},{14,12},{16,18},{18,... | collective-permute-start | bytes 3932168 | tf_op jit(solution)/shard_map/ppermute | solution.py:29
  10.4 31.5 %collective-permute-start = (bf16[128,2048]{1,0:T(8,128)(2,1)S(1)}, bf16[128,2048]{1,0:T(8,128)(2,1)S(1)}, u32[]{:S(2)}, u32[]{:S(2)}) collective-permute-start(bf16[128,2048]{1,0:T(8,128)(2,1)S(1)} %get-tuple-element.74.refs_1_), channel_id=1, source_target_pairs={{0,8},{2,10},{4,12},{6,14},{8,0},{10,2},{12,4},{14,6},{16,24},{18,... | collective-permute-start | bytes 1572872 | tf_op jit(solution)/shard_map/ppermute | solution.py:29
  11.9 29.9 %collective-permute-start.1 = (bf16[128,2048]{1,0:T(8,128)(2,1)S(1)}, bf16[128,2048]{1,0:T(8,128)(2,1)S(1)}, u32[]{:S(2)}, u32[]{:S(2)}) collective-permute-start(bf16[128,2048]{1,0:T(8,128)(2,1)S(1)} %get-tuple-element.75), channel_id=1, source_target_pairs={{0,16},{2,18},{4,20},{6,22},{8,24},{10,26},{12,28},{14,30},{16,0},... | collective-permute-start | bytes 1572872 | tf_op jit(solution)/shard_map/ppermute | solution.py:29
  14.5 25.1 %collective-permute-start.2 = (bf16[128,512]{1,0:T(8,128)(2,1)S(1)}, bf16[128,512]{1,0:T(8,128)(2,1)S(1)}, u32[]{:S(2)}, u32[]{:S(2)}) collective-permute-start(bf16[128,512]{1,0:T(8,128)(2,1)S(1)} %get-tuple-element.76), channel_id=1, source_target_pairs={{0,24},{2,26},{4,28},{6,30},{8,16},{10,18},{12,20},{14,22},{16,8},... | collective-permute-start | bytes 393224 | tf_op jit(solution)/shard_map/ppermute | solution.py:29
  40.1 20.2 %collective-permute-start.8 = (bf16[128,2560]{1,0:T(8,128)(2,1)S(1)}, bf16[128,2560]{1,0:T(8,128)(2,1)S(1)}, u32[]{:S(2)}, u32[]{:S(2)}) collective-permute-start(bf16[128,2560]{1,0:T(8,128)(2,1)S(1)} %get-tuple-element.82), channel_id=1, source_target_pairs={{0,4},{2,6},{4,0},{6,2},{8,12},{10,14},{12,8},{14,10},{16,20},{18,... | collective-permute-start | bytes 1966088 | tf_op jit(solution)/shard_map/ppermute | solution.py:29
  40.6 19.7 %collective-permute-start.9 = (bf16[128,2560]{1,0:T(8,128)(2,1)S(1)}, bf16[128,2560]{1,0:T(8,128)(2,1)S(1)}, u32[]{:S(2)}, u32[]{:S(2)}) collective-permute-start(bf16[128,2560]{1,0:T(8,128)(2,1)S(1)} %get-tuple-element.83), channel_id=1, source_target_pairs={{0,2},{2,0},{4,6},{6,4},{8,10},{10,8},{12,14},{14,12},{16,18},{18,... | collective-permute-start | bytes 1966088 | tf_op jit(solution)/shard_map/ppermute | solution.py:29
  42.0 18.3 %collective-permute-start.5 = (bf16[128,1536]{1,0:T(8,128)(2,1)S(1)}, bf16[128,1536]{1,0:T(8,128)(2,1)S(1)}, u32[]{:S(2)}, u32[]{:S(2)}) collective-permute-start(bf16[128,1536]{1,0:T(8,128)(2,1)S(1)} %get-tuple-element.87), channel_id=1, source_target_pairs={{0,8},{2,10},{4,12},{6,14},{8,0},{10,2},{12,4},{14,6},{16,24},{18,... | collective-permute-start | bytes 1179656 | tf_op jit(solution)/shard_map/ppermute | solution.py:29
  45.0 14.6 %collective-permute-start.6 = (bf16[128,1024]{1,0:T(8,128)(2,1)S(1)}, bf16[128,1024]{1,0:T(8,128)(2,1)S(1)}, u32[]{:S(2)}, u32[]{:S(2)}) collective-permute-start(bf16[128,1024]{1,0:T(8,128)(2,1)S(1)} %get-tuple-element.91.refs_1_), channel_id=1, source_target_pairs={{0,16},{2,18},{4,20},{6,22},{8,24},{10,26},{12,28},{14,30},{16,0},... | collective-permute-start | bytes 786440 | tf_op jit(solution)/shard_map/ppermute | solution.py:29
  63.1 28.3 %collective-permute-start.13 = (bf16[256,1536]{1,0:T(8,128)(2,1)S(1)}, bf16[256,1536]{1,0:T(8,128)(2,1)S(1)}, u32[]{:S(2)}, u32[]{:S(2)}) collective-permute-start(bf16[256,1536]{1,0:T(8,128)(2,1)S(1)} %get-tuple-element.96), channel_id=1, source_target_pairs={{0,4},{2,6},{4,0},{6,2},{8,12},{10,14},{12,8},{14,10},{16,20},{18,... | collective-permute-start | bytes 2359304 | tf_op jit(solution)/shard_map/ppermute | solution.py:29
  64.6 26.7 %collective-permute-start.12 = (bf16[256,1536]{1,0:T(8,128)(2,1)S(1)}, bf16[256,1536]{1,0:T(8,128)(2,1)S(1)}, u32[]{:S(2)}, u32[]{:S(2)}) collective-permute-start(bf16[256,1536]{1,0:T(8,128)(2,1)S(1)} %get-tuple-element.95), channel_id=1, source_target_pairs={{0,2},{2,0},{4,6},{6,4},{8,10},{10,8},{12,14},{14,12},{16,18},{18,... | collective-permute-start | bytes 2359304 | tf_op jit(solution)/shard_map/ppermute | solution.py:29
  70.2 21.1 %collective-permute-start.14 = (bf16[64,2560]{1,0:T(8,128)(2,1)S(1)}, bf16[64,2560]{1,0:T(8,128)(2,1)S(1)}, u32[]{:S(2)}, u32[]{:S(2)}) collective-permute-start(bf16[64,2560]{1,0:T(8,128)(2,1)S(1)} %get-tuple-element.100), channel_id=1, source_target_pairs={{0,16},{2,18},{4,20},{6,22},{8,24},{10,26},{12,28},{14,30},{16,0},... | collective-permute-start | bytes 983048 | tf_op jit(solution)/shard_map/ppermute | solution.py:29
  73.0 13.8 %collective-permute-start.10 = (bf16[128,1024]{1,0:T(8,128)(2,1)S(1)}, bf16[128,1024]{1,0:T(8,128)(2,1)S(1)}, u32[]{:S(2)}, u32[]{:S(2)}) collective-permute-start(bf16[128,1024]{1,0:T(8,128)(2,1)S(1)} %get-tuple-element.91.refs_1_), channel_id=1, source_target_pairs={{0,8},{2,10},{4,12},{6,14},{8,0},{10,2},{12,4},{14,6},{16,24},{18,... | collective-permute-start | bytes 786440 | tf_op jit(solution)/shard_map/ppermute | solution.py:29
  73.3 18.0 %collective-permute-start.11 = (bf16[128,1024]{1,0:T(8,128)(2,1)S(1)}, bf16[128,1024]{1,0:T(8,128)(2,1)S(1)}, u32[]{:S(2)}, u32[]{:S(2)}) collective-permute-start(bf16[128,1024]{1,0:T(8,128)(2,1)S(1)} %collective-permute-done.6.refs_3_), channel_id=1, source_target_pairs={{0,8},{2,10},{4,12},{6,14},{8,0},{10,2},{12,4},{14,6},{16,24},{18,... | collective-permute-start | bytes 786440 | tf_op jit(solution)/shard_map/ppermute | solution.py:29
  93.1 12.6 %collective-permute-start.15 = (bf16[256,1024]{1,0:T(8,128)(2,1)S(1)}, bf16[256,1024]{1,0:T(8,128)(2,1)S(1)}, u32[]{:S(2)}, u32[]{:S(2)}) collective-permute-start(bf16[256,1024]{1,0:T(8,128)(2,1)S(1)} %get-tuple-element.104), channel_id=1, source_target_pairs={{0,2},{2,0},{4,6},{6,4},{8,10},{10,8},{12,14},{14,12},{16,18},{18,... | collective-permute-start | bytes 1572872 | tf_op jit(solution)/shard_map/ppermute | solution.py:29
  93.7 12.7 %collective-permute-start.16 = (bf16[256,1024]{1,0:T(8,128)(2,1)S(1)}, bf16[256,1024]{1,0:T(8,128)(2,1)S(1)}, u32[]{:S(2)}, u32[]{:S(2)}) collective-permute-start(bf16[256,1024]{1,0:T(8,128)(2,1)S(1)} %get-tuple-element.110), channel_id=1, source_target_pairs={{0,4},{2,6},{4,0},{6,2},{8,12},{10,14},{12,8},{14,10},{16,20},{18,... | collective-permute-start | bytes 1572872 | tf_op jit(solution)/shard_map/ppermute | solution.py:29
  94.2 28.9 %collective-permute-start.19 = (bf16[128,2560]{1,0:T(8,128)(2,1)S(1)}, bf16[128,2560]{1,0:T(8,128)(2,1)S(1)}, u32[]{:S(2)}, u32[]{:S(2)}) collective-permute-start(bf16[128,2560]{1,0:T(8,128)(2,1)S(1)} %get-tuple-element.115), channel_id=1, source_target_pairs={{0,8},{2,10},{4,12},{6,14},{8,0},{10,2},{12,4},{14,6},{16,24},{18,... | collective-permute-start | bytes 1966088 | tf_op jit(solution)/shard_map/ppermute | solution.py:29
  105.8 18.1 %collective-permute-start.17 = (bf16[128,2560]{1,0:T(8,128)(2,1)S(1)}, bf16[128,2560]{1,0:T(8,128)(2,1)S(1)}, u32[]{:S(2)}, u32[]{:S(2)}) collective-permute-start(bf16[128,2560]{1,0:T(8,128)(2,1)S(1)} %shard_map.118), channel_id=1, source_target_pairs={{0,4},{2,6},{4,0},{6,2},{8,12},{10,14},{12,8},{14,10},{16,20},{18,... | collective-permute-start | bytes 1966088 | tf_op jit(solution)/shard_map/ppermute | solution.py:29
  106.5 17.4 %collective-permute-start.18 = (bf16[128,2560]{1,0:T(8,128)(2,1)S(1)}, bf16[128,2560]{1,0:T(8,128)(2,1)S(1)}, u32[]{:S(2)}, u32[]{:S(2)}) collective-permute-start(bf16[128,2560]{1,0:T(8,128)(2,1)S(1)} %shard_map.119), channel_id=1, source_target_pairs={{0,2},{2,0},{4,6},{6,4},{8,10},{10,8},{12,14},{14,12},{16,18},{18,... | collective-permute-start | bytes 1966088 | tf_op jit(solution)/shard_map/ppermute | solution.py:29
  108.1 14.3 %collective-permute-start.20 = (bf16[64,2560]{1,0:T(8,128)(2,1)S(1)}, bf16[64,2560]{1,0:T(8,128)(2,1)S(1)}, u32[]{:S(2)}, u32[]{:S(2)}) collective-permute-start(bf16[64,2560]{1,0:T(8,128)(2,1)S(1)} %get-tuple-element.116), channel_id=1, source_target_pairs={{0,16},{2,18},{4,20},{6,22},{8,24},{10,26},{12,28},{14,30},{16,0},... | collective-permute-start | bytes 983048 | tf_op jit(solution)/shard_map/ppermute | solution.py:29
  130.3 16.6 %collective-permute-start.24 = (bf16[64,2560]{1,0:T(8,128)(2,1)}, bf16[64,2560]{1,0:T(8,128)(2,1)}, u32[]{:S(2)}, u32[]{:S(2)}) collective-permute-start(bf16[64,2560]{1,0:T(8,128)(2,1)} %shard_map.121), channel_id=1, source_target_pairs={{0,16},{2,18},{4,20},{6,22},{8,24},{10,26},{12,28},{14,30},{16,0},... | collective-permute-start | bytes 983048 | tf_op jit(solution)/shard_map/ppermute | solution.py:29
  130.3 17.1 %collective-permute-start.25 = (bf16[64,2560]{1,0:T(8,128)(2,1)}, bf16[64,2560]{1,0:T(8,128)(2,1)}, u32[]{:S(2)}, u32[]{:S(2)}) collective-permute-start(bf16[64,2560]{1,0:T(8,128)(2,1)} %copy-done.15), channel_id=1, source_target_pairs={{0,8},{2,10},{4,12},{6,14},{8,0},{10,2},{12,4},{14,6},{16,24},{18,... | collective-permute-start | bytes 983048 | tf_op jit(solution)/shard_map/ppermute | solution.py:29
  147.4 12.3 %collective-permute-start.28 = (f32[5248]{0:T(1024)S(1)}, f32[5248]{0:T(1024)S(1)}, u32[]{:S(2)}, u32[]{:S(2)}) collective-permute-start(f32[5248]{0:T(1024)S(1)} %add_add_fusion.1), channel_id=1, source_target_pairs={{0,24},{2,26},{4,28},{6,30},{8,16},{10,18},{12,20},{14,22},{16,8},... | collective-permute-start | bytes 62984 | tf_op jit(solution)/shard_map/ppermute | solution.py:29
  149.6 10.1 %collective-permute-start.27 = (f32[5248]{0:T(1024)S(1)}, f32[5248]{0:T(1024)S(1)}, u32[]{:S(2)}, u32[]{:S(2)}) collective-permute-start(f32[5248]{0:T(1024)S(1)} %add_add_fusion.1), channel_id=1, source_target_pairs={{0,16},{2,18},{4,20},{6,22},{8,24},{10,26},{12,28},{14,30},{16,0},... | collective-permute-start | bytes 62984 | tf_op jit(solution)/shard_map/ppermute | solution.py:29
  (25 other events, 175.2 us)

commit v11 on v10

--- a/solution.py
+++ b/solution.py
@@ -9,7 +9,6 @@
 
 TRAIN_STEP = 3
 INNER_BITS = 2
-LEFT = 3
 EAGER = pl.CostEstimate(flops=0, bytes_accessed=0, transcendentals=0)
 
 
@@ -93,7 +92,7 @@
 
 def first_stage(out_grad, gate_pre, up_pre, place, rows):
     tokens, units = gate_pre.shape
-    half = units * LEFT // 5
+    half = units // 2
     step = 32
 
     def kernel(place, source_hbm, gate_hbm, up_hbm, own, right, message1, message2, message3, source, gate, up, sems):
@@ -339,8 +338,8 @@
     tokens, units = gate_pre.shape
     rows = down_weight.shape[0]
     q, t = rows // 2, tokens // 2
-    steps = 4
-    split = units * LEFT // 5
+    steps = 5
+    split = units // 2
     barrier = lax.optimization_barrier
     place = jnp.stack([me, core]).astype(jnp.int32)
     own, right, message1, message2, message3 = first_stage(out_grad, gate_pre, up_pre, place, rows)
@@ -368,9 +367,6 @@
     theirs = flip(mine, 1, "mp")
     share = assemble(own, mine, theirs, place, rows)
 
-    left3, right2, share, right, weight3a, weight3b = barrier((left3, right2, share, right, weight3a, weight3b))
-    right1, right3 = flip(right, z_bit), flip(right2, z_bit)
-
     def low_sent(size):
         return [(2 * size, 3 * size), (6 * size, 7 * size)]
 
@@ -384,29 +380,30 @@
         ranges = [(0, 2 * size)], [(4 * size, 5 * size)], [(3 * size, 4 * size)]
         return [(r, jnp.float32) for r in ranges]
 
+    weights = [down_weight, weight1, weight2, weight3a, weight3b]
+    first = [(high_sent(t)[1:], jnp.bfloat16), (high_sent(t)[:1], jnp.bfloat16), (low_sent(t), jnp.bfloat16)]
+    to_w1, to_w2, to_z = products(share, [(weights, units, first, False)], steps)
+    left3, right2, share, right, to_w1 = barrier((left3, right2, share, right, to_w1))
+    right1, right3 = flip(right, z_bit), flip(right2, z_bit)
+    from_w1 = flip(to_w1, w_bit)
+
     lefts = [message1, left1, left2, left3]
     left_to_x, left_to_y = products(share, [(lefts, split, sent(q), True)], steps)
     left_from_x, left_from_y = flip(left_to_x, x_bit), flip(left_to_y, y_bit)
-    share, _ = barrier((share, left_to_x))
-
-    weights = [down_weight, weight1, weight2, weight3a, weight3b]
-    first = [(high_sent(t)[1:], jnp.bfloat16), (high_sent(t)[:1], jnp.bfloat16), (low_sent(t), jnp.bfloat16)]
-    to_w1, to_w2, to_z = products(share, [(weights, units, first, False)], steps)
-    from_w1, from_w2, from_z = flip(to_w1, w_bit), flip(to_w2, w_bit), flip(to_z, z_bit)
-
-    right1, right3, left_from_x, left_from_y, from_w1, share = barrier(
-        (right1, right3, left_from_x, left_from_y, from_w1, share)
-    )
+
+    right1, right3, from_w1, share, _ = barrier((right1, right3, from_w1, share, left_to_x))
     rights = [right, right1, right2, right3]
     right_to_x, right_to_y = products(share, [(rights, units - split, sent(q), True)], steps)
     right_from_x, right_from_y = flip(right_to_x, x_bit), flip(right_to_y, y_bit)
-    share, _ = barrier((share, right_to_x))
+    from_w2, from_z = flip(to_w2, w_bit), flip(to_z, z_bit)
+    share, left_from_x, left_from_y, _ = barrier((share, left_from_x, left_from_y, right_to_x))
     left_parts = products(share, [(lefts, split, kept(q), True)], steps)
     parts = products(share, [(rights, units - split, kept(q), True), (weights, units, kept(t), False)], steps)
 
     grad_a = flip(add_tail([left_parts[1], parts[1]], [left_from_x, right_from_x]), y_bit)
     grad_b = flip(add_tail([left_parts[2], parts[2]], [left_from_y, right_from_y]), x_bit)
-    grad_a, grad_b, from_z, from_w2 = barrier((grad_a, grad_b, from_z, from_w2))
+    last_b = flip(add_tail([parts[5]], [from_w1]), z_bit)
+    grad_a, grad_b, from_z, from_w2, last_b = barrier((grad_a, grad_b, from_z, from_w2, last_b))
     grad, row_part = sum_up(
         [left_parts[0], parts[0]],
         [left_from_x, right_from_x],
@@ -416,10 +413,10 @@
         1.0 / math.sqrt(tokens * lax.axis_size("dp")),
     )
 
-    to_w, to_z = add_tail([parts[4]], [from_z]), add_tail([parts[5]], [from_w1])
+    to_w = add_tail([parts[4]], [from_z])
     row_sum = lax.psum(row_part, "mp")
-    row_sum, to_w, to_z = barrier((row_sum, to_w, to_z))
-    last_a, last_b = flip(to_w, w_bit), flip(to_z, z_bit)
+    row_sum, to_w = barrier((row_sum, to_w))
+    last_a = flip(to_w, w_bit)
     return grad, row_sum, (parts[3], from_z, from_w2, last_a, last_b)
 
 

time: 168 us -> 167 us (level)
  starting transfers between devices: 40.1 us -> 36.3 us
  waiting for transfers between devices: 79 us -> 81.8 us
    ppermute x29, starting transfers between devices: 40.1 us -> 36.3 us  [flip(): return lax.ppermute(value, axis, [(i, i ^ bits) for i in range(size)])]
    ppermute x29, waiting for transfers between devices: 79 us -> 81.8 us  [flip(): return lax.ppermute(value, axis, [(i, i ^ bits) for i in range(size)])]
    unnamed x40 -> x42, local copies, waits for them, and re-layouts: 12.3 us -> 13.3 us
  transfers between devices with their start and end apart: 29 -> 29, of which waited for: 12 -> 17; matrix products, arithmetic and copies ran while one was open for 0% -> 0% of each run, Pallas kernels for 10% -> 12%
where the time goes in v11:
time: 167 us
  waiting for transfers between devices  81.8 us (49%)
  starting transfers between devices  36.3 us (22%)
  Pallas kernels  23.8 us (14%)
  local copies, waits for them, and re-layouts  13.8 us (8%)
  blocking collectives  5.08 us (3%)
  between operations  3.34 us (2%)
  other arithmetic  2.56 us (2%)
    ppermute x29, waiting for transfers between devices, flip(): return lax.ppermute(value, axis, [(i, i ^ bits) for i in range(size)])  81.8 us
    ppermute x29, starting transfers between devices, flip(): return lax.ppermute(value, axis, [(i, i ^ bits) for i in range(size)])  36.3 us
    pallas_call x5, Pallas kernels, products(): pl.pallas_call(kernel, grid=(steps,), out_shape=[jax.ShapeDtypeStruct((he...  15.1 us
    unnamed x42, local copies, waits for them, and re-layouts  13.3 us
    pallas_call x1, Pallas kernels, hidden_gradients(): pl.pallas_call(kernel, out_shape=[jax.ShapeDtypeStruct((tokens, units), j...  3.38 us
  transfers between devices with their start and end apart: 29, of which 17 were waited for; matrix products, arithmetic and copies ran while one was open for 0% of the time, Pallas kernels for 12%

profile of v11, /device:TPU:0, one launch (start us, length us, event | category | flops | bytes accessed | tf_op | source)
XLA Modules:
  0.0 166.7 jit_solution(2144951481990613627)
XLA Ops:
  4.1 1.7 %shard_map.109 = (bf16[128,1024]{1,0:T(8,128)(2,1)S(1)}, bf16[128,1280]{1,0:T(8,128)(2,1)S(1)}, bf16[128,1792]{1,0:T(8,128)(2,1)S(1)}, bf16[128,1792]{1,0:T(8,128)(2,1)S(1)}, bf16[128,512]{1,0:T(8,128)(2,1)S(1)}) custom-call(s32[2]{0:T(128)S(1)} %pad_add_fusion.place, bf16[128,4096]{1,0:T(8,128)(2,1)S(1)} %copy-done.10, bf16[128,2560]{1,0:T(8,128)(2,1)S(1)} %copy-done.1, ...), custom_call_target="tpu_custom_call" | custom-call | tf_op jit(solution)/shard_map/pallas_call | solution.py:131
  5.8 3.0 %collective-permute-start.4 = (bf16[256,2560]{1,0:T(8,128)(2,1)}, bf16[256,2560]{1,0:T(8,128)(2,1)S(1)}, u32[]{:S(2)}, u32[]{:S(2)}) collective-permute-start(bf16[256,2560]{1,0:T(8,128)(2,1)} %refs_5_), channel_id=1, source_target_pairs={{0,4},{2,6},{4,0},{6,2},{8,12},{10,14},{12,8},{14,10},{16,20},{18,... | collective-permute-start | bytes 3932168 | tf_op jit(solution)/shard_map/ppermute | solution.py:28
  11.9 2.6 %collective-permute-start.1 = (bf16[128,1792]{1,0:T(8,128)(2,1)S(1)}, bf16[128,1792]{1,0:T(8,128)(2,1)S(1)}, u32[]{:S(2)}, u32[]{:S(2)}) collective-permute-start(bf16[128,1792]{1,0:T(8,128)(2,1)S(1)} %get-tuple-element.73), channel_id=1, source_target_pairs={{0,16},{2,18},{4,20},{6,22},{8,24},{10,26},{12,28},{14,30},{16,0},... | collective-permute-start | bytes 1376264 | tf_op jit(solution)/shard_map/ppermute | solution.py:28
  14.7 22.1 %collective-permute-done.2.refs_2_ = bf16[128,512]{1,0:T(8,128)(2,1)S(1)} collective-permute-done((bf16[128,512]{1,0:T(8,128)(2,1)S(1)}, bf16[128,512]{1,0:T(8,128)(2,1)S(1)}, u32[]{:S(2)}, u32[]{:S(2)}) %collective-permute-start.2) | collective-permute-done | bytes 131104 | tf_op jit(solution)/shard_map/ppermute | solution.py:28
  42.0 2.7 %collective-permute-start.6 = (bf16[128,1280]{1,0:T(8,128)(2,1)S(1)}, bf16[128,1280]{1,0:T(8,128)(2,1)S(1)}, u32[]{:S(2)}, u32[]{:S(2)}) collective-permute-start(bf16[128,1280]{1,0:T(8,128)(2,1)S(1)} %get-tuple-element.90.refs_1_), channel_id=1, source_target_pairs={{0,16},{2,18},{4,20},{6,22},{8,24},{10,26},{12,28},{14,30},{16,0},... | collective-permute-start | bytes 983048 | tf_op jit(solution)/shard_map/ppermute | solution.py:28
  46.9 8.2 %collective-permute-done.8.refs_4_.refs_8_ = bf16[128,2560]{1,0:T(8,128)(2,1)S(1)} collective-permute-done((bf16[128,2560]{1,0:T(8,128)(2,1)S(1)}, bf16[128,2560]{1,0:T(8,128)(2,1)S(1)}, u32[]{:S(2)}, u32[]{:S(2)}) %collective-permute-start.8) | collective-permute-done | bytes 655392 | tf_op jit(solution)/shard_map/ppermute | solution.py:28
  55.5 3.9 %shard_map.113 = (bf16[64,2560]{1,0:T(8,128)(2,1)S(1)}, bf16[64,2560]{1,0:T(8,128)(2,1)S(1)}, bf16[128,2560]{1,0:T(8,128)(2,1)S(1)}) custom-call(bf16[512,1024]{1,0:T(8,128)(2,1)S(1)} %shard_map.112.refs_0_, bf16[256,2560]{1,0:T(8,128)(2,1)S(1)} %copy-done, bf16[256,2560]{1,0:T(8,128)(2,1)S(1)} %collective-permute-done.3.refs_0_.refs_2_.refs_6_, ...), custom_call_target="tpu_custom_call" | custom-call | tf_op jit(solution)/shard_map/pallas_call | solution.py:320
  62.0 2.1 %collective-permute-start.10 = (bf16[128,1280]{1,0:T(8,128)(2,1)S(1)}, bf16[128,1280]{1,0:T(8,128)(2,1)S(1)}, u32[]{:S(2)}, u32[]{:S(2)}) collective-permute-start(bf16[128,1280]{1,0:T(8,128)(2,1)S(1)} %get-tuple-element.90.refs_1_), channel_id=1, source_target_pairs={{0,8},{2,10},{4,12},{6,14},{8,0},{10,2},{12,4},{14,6},{16,24},{18,... | collective-permute-start | bytes 983048 | tf_op jit(solution)/shard_map/ppermute | solution.py:28
  64.1 2.0 %shard_map.114 = (bf16[256,1280]{1,0:T(8,128)(2,1)S(1)}, bf16[256,1280]{1,0:T(8,128)(2,1)S(1)}) custom-call(bf16[512,1024]{1,0:T(8,128)(2,1)S(1)} %shard_map.112.refs_0_, bf16[128,1792]{1,0:T(8,128)(2,1)S(1)} %get-tuple-element.72.refs_1_, bf16[128,1792]{1,0:T(8,128)(2,1)S(1)} %collective-permute-done.refs_0_.refs_2_, ...), custom_call_target="tpu_custom_call" | custom-call | tf_op jit(solution)/shard_map/pallas_call | solution.py:320
  69.1 8.3 %collective-permute-done.12.refs_1_ = bf16[64,2560]{1,0:T(8,128)(2,1)S(1)} collective-permute-done((bf16[64,2560]{1,0:T(8,128)(2,1)S(1)}, bf16[64,2560]{1,0:T(8,128)(2,1)S(1)}, u32[]{:S(2)}, u32[]{:S(2)}) %collective-permute-start.12) | collective-permute-done | bytes 327712 | tf_op jit(solution)/shard_map/ppermute | solution.py:28
  78.4 6.1 %collective-permute-done.11.refs_4_ = bf16[128,1280]{1,0:T(8,128)(2,1)S(1)} collective-permute-done((bf16[128,1280]{1,0:T(8,128)(2,1)S(1)}, bf16[128,1280]{1,0:T(8,128)(2,1)S(1)}, u32[]{:S(2)}, u32[]{:S(2)}) %collective-permute-start.11) | collective-permute-done | bytes 327712 | tf_op jit(solution)/shard_map/ppermute | solution.py:28
  84.5 2.0 %shard_map.115 = (bf16[256,1280]{1,0:T(8,128)(2,1)S(1)}, bf16[256,1280]{1,0:T(8,128)(2,1)S(1)}) custom-call(bf16[512,1024]{1,0:T(8,128)(2,1)S(1)} %shard_map.112.refs_0_, bf16[128,1280]{1,0:T(8,128)(2,1)S(1)} %get-tuple-element.90.refs_1_, bf16[128,1280]{1,0:T(8,128)(2,1)S(1)} %collective-permute-done.10.refs_2_, ...), custom_call_target="tpu_custom_call" | custom-call | tf_op jit(solution)/shard_map/pallas_call | solution.py:320
  89.2 2.1 %shard_map.116 = (f32[256,1280]{1,0:T(8,128)S(1)}, f32[128,1280]{1,0:T(8,128)S(1)}, f32[128,1280]{1,0:T(8,128)S(1)}) custom-call(bf16[512,1024]{1,0:T(8,128)(2,1)S(1)} %shard_map.112.refs_0_, bf16[128,1792]{1,0:T(8,128)(2,1)S(1)} %get-tuple-element.72.refs_1_, bf16[128,1792]{1,0:T(8,128)(2,1)S(1)} %collective-permute-done.refs_0_.refs_2_, ...), custom_call_target="tpu_custom_call" | custom-call | tf_op jit(solution)/shard_map/pallas_call | solution.py:320
  91.3 5.0 %shard_map.117 = (f32[256,1280]{1,0:T(8,128)S(1)}, f32[128,1280]{1,0:T(8,128)S(1)}, f32[128,1280]{1,0:T(8,128)S(1)}, f32[128,2560]{1,0:T(8,128)S(1)}, f32[64,2560]{1,0:T(8,128)S(1)}, /*index=5*/f32[64,2560]{1,0:T(8,128)S(1)}) custom-call(bf16[512,1024]{1,0:T(8,128)(2,1)S(1)} %shard_map.112.refs_0_, bf16[128,1280]{1,0:T(8,128)(2,1)S(1)} %get-tuple-element.90.refs_1_, ...), custom_call_target="tpu_custom_call" | custom-call | tf_op jit(solution)/shard_map/pallas_call | solution.py:320
  96.4 6.1 %collective-permute-done.16.refs_3_.refs_5_ = bf16[256,1280]{1,0:T(8,128)(2,1)S(1)} collective-permute-done((bf16[256,1280]{1,0:T(8,128)(2,1)S(1)}, bf16[256,1280]{1,0:T(8,128)(2,1)S(1)}, u32[]{:S(2)}, u32[]{:S(2)}) %collective-permute-start.16) | collective-permute-done | bytes 655392 | tf_op jit(solution)/shard_map/ppermute | solution.py:28
  104.4 1.7 %collective-permute-start.20 = (bf16[64,2560]{1,0:T(8,128)(2,1)S(1)}, bf16[64,2560]{1,0:T(8,128)(2,1)S(1)}, u32[]{:S(2)}, u32[]{:S(2)}) collective-permute-start(bf16[64,2560]{1,0:T(8,128)(2,1)S(1)} %get-tuple-element.112), channel_id=1, source_target_pairs={{0,16},{2,18},{4,20},{6,22},{8,24},{10,26},{12,28},{14,30},{16,0},... | collective-permute-start | bytes 983048 | tf_op jit(solution)/shard_map/ppermute | solution.py:28
  107.7 11.3 %collective-permute-done.20.high = bf16[64,2560]{1,0:T(8,128)(2,1)S(1)} collective-permute-done((bf16[64,2560]{1,0:T(8,128)(2,1)S(1)}, bf16[64,2560]{1,0:T(8,128)(2,1)S(1)}, u32[]{:S(2)}, u32[]{:S(2)}) %collective-permute-start.20) | collective-permute-done | bytes 327712 | tf_op jit(solution)/shard_map/ppermute | solution.py:28
  122.1 2.6 %psum.14.row_sum = f32[1,256]{1,0:T(1,128)S(1)} all-reduce(f32[1,256]{1,0:T(1,128)S(1)} %get-tuple-element.118), channel_id=1, replica_groups=mesh['dp'=16,'mp'=2] {'mp'}, use_global_device_ids=true, to_apply=%region_0.0 | all-reduce | flops 256 | bytes 2048 | tf_op jit(solution)/shard_map/psum | solution.py:417
  128.4 1.7 %collective-permute-start.24 = (f32[5248]{0:T(1024)S(1)}, f32[5248]{0:T(1024)S(1)}, u32[]{:S(2)}, u32[]{:S(2)}) collective-permute-start(f32[5248]{0:T(1024)S(1)} %reduce), channel_id=1, source_target_pairs={{0,6},{2,4},{4,2},{6,0},{8,14},{10,12},{12,10},{14,8},{16,22},{18,... | collective-permute-start | bytes 62984 | tf_op jit(solution)/shard_map/ppermute | solution.py:28
  135.3 10.2 %collective-permute-done.25.last_a = bf16[64,2560]{1,0:T(8,128)(2,1)} collective-permute-done((bf16[64,2560]{1,0:T(8,128)(2,1)}, bf16[64,2560]{1,0:T(8,128)(2,1)}, u32[]{:S(2)}, u32[]{:S(2)}) %collective-permute-start.25) | collective-permute-done | bytes 327712 | tf_op jit(solution)/shard_map/ppermute | solution.py:28
  146.8 3.1 %collective-permute-start.26 = (f32[5248]{0:T(1024)S(1)}, f32[5248]{0:T(1024)S(1)}, u32[]{:S(2)}, u32[]{:S(2)}) collective-permute-start(f32[5248]{0:T(1024)S(1)} %add_add_fusion.1), channel_id=1, source_target_pairs={{0,8},{2,10},{4,12},{6,14},{8,0},{10,2},{12,4},{14,6},{16,24},{18,... | collective-permute-start | bytes 62984 | tf_op jit(solution)/shard_map/ppermute | solution.py:28
  155.4 3.4 %shard_map.124 = (bf16[128,2560]{1,0:T(8,128)(2,1)}, bf16[128,2560]{1,0:T(8,128)(2,1)}) custom-call(bf16[128,2560]{1,0:T(8,128)(2,1)S(1)} %copy-done.2, bf16[128,2560]{1,0:T(8,128)(2,1)S(1)} %copy-done.4, f32[128,2560]{1,0:T(8,128)S(1)} %copy-done.9, bf16[128,2560]{1,0:T(8,128)(2,1)S(1)} %copy-done.7, bf16[64,2560]{1,0:T(8,128)(2,1)S(1)} %copy-done.14, ...), custom_call_target="tpu_custom_call" | custom-call | tf_op jit(solution)/shard_map/pallas_call | solution.py:440
  159.4 2.5 %psum.15 = f32[128]{0:T(128)S(1)} all-reduce(f32[128]{0:T(128)S(1)} %get-tuple-element.136), channel_id=1, replica_groups=mesh['dp'=16,'mp'=2] {'mp'}, use_global_device_ids=true, to_apply=%region_2.0 | all-reduce | flops 128 | bytes 1024 | tf_op jit(solution)/shard_map/psum | solution.py:486
  163.8 1.8 %multiply_multiply_fusion = f32[256,2560]{1,0:T(8,128)} fusion(f32[256,2560]{1,0:T(8,128)S(1)} %get-tuple-element.117.grad, f32[2560]{0:T(1024)S(1)} %sqrt.15, f32[256]{0:T(256)S(1)} %sqrt_divide_fusion), kind=kLoop, calls=%fused_computation | loop fusion | flops 1310720 | bytes 5254144 | tf_op jit(solution)/shard_map/mul | solution.py:490
  (104 shorter events, 47.0 us)
Async XLA Ops:
  5.8 32.0 %collective-permute-start.4 = (bf16[256,2560]{1,0:T(8,128)(2,1)}, bf16[256,2560]{1,0:T(8,128)(2,1)S(1)}, u32[]{:S(2)}, u32[]{:S(2)}) collective-permute-start(bf16[256,2560]{1,0:T(8,128)(2,1)} %refs_5_), channel_id=1, source_target_pairs={{0,4},{2,6},{4,0},{6,2},{8,12},{10,14},{12,8},{14,10},{16,20},{18,... | collective-permute-start | bytes 3932168 | tf_op jit(solution)/shard_map/ppermute | solution.py:28
  8.9 30.4 %collective-permute-start.3 = (bf16[256,2560]{1,0:T(8,128)(2,1)}, bf16[256,2560]{1,0:T(8,128)(2,1)S(1)}, u32[]{:S(2)}, u32[]{:S(2)}) collective-permute-start(bf16[256,2560]{1,0:T(8,128)(2,1)} %refs_5_), channel_id=1, source_target_pairs={{0,2},{2,0},{4,6},{6,4},{8,10},{10,8},{12,14},{14,12},{16,18},{18,... | collective-permute-start | bytes 3932168 | tf_op jit(solution)/shard_map/ppermute | solution.py:28
  10.4 31.5 %collective-permute-start = (bf16[128,1792]{1,0:T(8,128)(2,1)S(1)}, bf16[128,1792]{1,0:T(8,128)(2,1)S(1)}, u32[]{:S(2)}, u32[]{:S(2)}) collective-permute-start(bf16[128,1792]{1,0:T(8,128)(2,1)S(1)} %get-tuple-element.72.refs_1_), channel_id=1, source_target_pairs={{0,8},{2,10},{4,12},{6,14},{8,0},{10,2},{12,4},{14,6},{16,24},{18,... | collective-permute-start | bytes 1376264 | tf_op jit(solution)/shard_map/ppermute | solution.py:28
  11.9 29.9 %collective-permute-start.1 = (bf16[128,1792]{1,0:T(8,128)(2,1)S(1)}, bf16[128,1792]{1,0:T(8,128)(2,1)S(1)}, u32[]{:S(2)}, u32[]{:S(2)}) collective-permute-start(bf16[128,1792]{1,0:T(8,128)(2,1)S(1)} %get-tuple-element.73), channel_id=1, source_target_pairs={{0,16},{2,18},{4,20},{6,22},{8,24},{10,26},{12,28},{14,30},{16,0},... | collective-permute-start | bytes 1376264 | tf_op jit(solution)/shard_map/ppermute | solution.py:28
  14.5 22.3 %collective-permute-start.2 = (bf16[128,512]{1,0:T(8,128)(2,1)S(1)}, bf16[128,512]{1,0:T(8,128)(2,1)S(1)}, u32[]{:S(2)}, u32[]{:S(2)}) collective-permute-start(bf16[128,512]{1,0:T(8,128)(2,1)S(1)} %get-tuple-element.74), channel_id=1, source_target_pairs={{0,24},{2,26},{4,28},{6,30},{8,16},{10,18},{12,20},{14,22},{16,8},... | collective-permute-start | bytes 393224 | tf_op jit(solution)/shard_map/ppermute | solution.py:28
  39.7 15.3 %collective-permute-start.8 = (bf16[128,2560]{1,0:T(8,128)(2,1)S(1)}, bf16[128,2560]{1,0:T(8,128)(2,1)S(1)}, u32[]{:S(2)}, u32[]{:S(2)}) collective-permute-start(bf16[128,2560]{1,0:T(8,128)(2,1)S(1)} %get-tuple-element.80), channel_id=1, source_target_pairs={{0,4},{2,6},{4,0},{6,2},{8,12},{10,14},{12,8},{14,10},{16,20},{18,... | collective-permute-start | bytes 1966088 | tf_op jit(solution)/shard_map/ppermute | solution.py:28
  40.2 15.3 %collective-permute-start.9 = (bf16[128,2560]{1,0:T(8,128)(2,1)S(1)}, bf16[128,2560]{1,0:T(8,128)(2,1)S(1)}, u32[]{:S(2)}, u32[]{:S(2)}) collective-permute-start(bf16[128,2560]{1,0:T(8,128)(2,1)S(1)} %get-tuple-element.81), channel_id=1, source_target_pairs={{0,2},{2,0},{4,6},{6,4},{8,10},{10,8},{12,14},{14,12},{16,18},{18,... | collective-permute-start | bytes 1966088 | tf_op jit(solution)/shard_map/ppermute | solution.py:28
  42.0 18.2 %collective-permute-start.6 = (bf16[128,1280]{1,0:T(8,128)(2,1)S(1)}, bf16[128,1280]{1,0:T(8,128)(2,1)S(1)}, u32[]{:S(2)}, u32[]{:S(2)}) collective-permute-start(bf16[128,1280]{1,0:T(8,128)(2,1)S(1)} %get-tuple-element.90.refs_1_), channel_id=1, source_target_pairs={{0,16},{2,18},{4,20},{6,22},{8,24},{10,26},{12,28},{14,30},{16,0},... | collective-permute-start | bytes 983048 | tf_op jit(solution)/shard_map/ppermute | solution.py:28
  44.7 15.7 %collective-permute-start.5 = (bf16[128,1280]{1,0:T(8,128)(2,1)S(1)}, bf16[128,1280]{1,0:T(8,128)(2,1)S(1)}, u32[]{:S(2)}, u32[]{:S(2)}) collective-permute-start(bf16[128,1280]{1,0:T(8,128)(2,1)S(1)} %get-tuple-element.85), channel_id=1, source_target_pairs={{0,8},{2,10},{4,12},{6,14},{8,0},{10,2},{12,4},{14,6},{16,24},{18,... | collective-permute-start | bytes 983048 | tf_op jit(solution)/shard_map/ppermute | solution.py:28
  60.3 17.1 %collective-permute-start.12 = (bf16[64,2560]{1,0:T(8,128)(2,1)S(1)}, bf16[64,2560]{1,0:T(8,128)(2,1)S(1)}, u32[]{:S(2)}, u32[]{:S(2)}) collective-permute-start(bf16[64,2560]{1,0:T(8,128)(2,1)S(1)} %get-tuple-element.92), channel_id=1, source_target_pairs={{0,16},{2,18},{4,20},{6,22},{8,24},{10,26},{12,28},{14,30},{16,0},... | collective-permute-start | bytes 983048 | tf_op jit(solution)/shard_map/ppermute | solution.py:28
  62.0 16.4 %collective-permute-start.10 = (bf16[128,1280]{1,0:T(8,128)(2,1)S(1)}, bf16[128,1280]{1,0:T(8,128)(2,1)S(1)}, u32[]{:S(2)}, u32[]{:S(2)}) collective-permute-start(bf16[128,1280]{1,0:T(8,128)(2,1)S(1)} %get-tuple-element.90.refs_1_), channel_id=1, source_target_pairs={{0,8},{2,10},{4,12},{6,14},{8,0},{10,2},{12,4},{14,6},{16,24},{18,... | collective-permute-start | bytes 983048 | tf_op jit(solution)/shard_map/ppermute | solution.py:28
  64.1 20.4 %collective-permute-start.11 = (bf16[128,1280]{1,0:T(8,128)(2,1)S(1)}, bf16[128,1280]{1,0:T(8,128)(2,1)S(1)}, u32[]{:S(2)}, u32[]{:S(2)}) collective-permute-start(bf16[128,1280]{1,0:T(8,128)(2,1)S(1)} %collective-permute-done.6.refs_3_), channel_id=1, source_target_pairs={{0,8},{2,10},{4,12},{6,14},{8,0},{10,2},{12,4},{14,6},{16,24},{18,... | collective-permute-start | bytes 983048 | tf_op jit(solution)/shard_map/ppermute | solution.py:28
  66.2 23.0 %collective-permute-start.14 = (bf16[256,1280]{1,0:T(8,128)(2,1)S(1)}, bf16[256,1280]{1,0:T(8,128)(2,1)S(1)}, u32[]{:S(2)}, u32[]{:S(2)}) collective-permute-start(bf16[256,1280]{1,0:T(8,128)(2,1)S(1)} %get-tuple-element.97), channel_id=1, source_target_pairs={{0,4},{2,6},{4,0},{6,2},{8,12},{10,14},{12,8},{14,10},{16,20},{18,... | collective-permute-start | bytes 1966088 | tf_op jit(solution)/shard_map/ppermute | solution.py:28
  67.8 21.4 %collective-permute-start.13 = (bf16[256,1280]{1,0:T(8,128)(2,1)S(1)}, bf16[256,1280]{1,0:T(8,128)(2,1)S(1)}, u32[]{:S(2)}, u32[]{:S(2)}) collective-permute-start(bf16[256,1280]{1,0:T(8,128)(2,1)S(1)} %get-tuple-element.95), channel_id=1, source_target_pairs={{0,2},{2,0},{4,6},{6,4},{8,10},{10,8},{12,14},{14,12},{16,18},{18,... | collective-permute-start | bytes 1966088 | tf_op jit(solution)/shard_map/ppermute | solution.py:28
  86.5 15.9 %collective-permute-start.16 = (bf16[256,1280]{1,0:T(8,128)(2,1)S(1)}, bf16[256,1280]{1,0:T(8,128)(2,1)S(1)}, u32[]{:S(2)}, u32[]{:S(2)}) collective-permute-start(bf16[256,1280]{1,0:T(8,128)(2,1)S(1)} %get-tuple-element.106), channel_id=1, source_target_pairs={{0,4},{2,6},{4,0},{6,2},{8,12},{10,14},{12,8},{14,10},{16,20},{18,... | collective-permute-start | bytes 1966088 | tf_op jit(solution)/shard_map/ppermute | solution.py:28
  88.1 15.7 %collective-permute-start.15 = (bf16[256,1280]{1,0:T(8,128)(2,1)S(1)}, bf16[256,1280]{1,0:T(8,128)(2,1)S(1)}, u32[]{:S(2)}, u32[]{:S(2)}) collective-permute-start(bf16[256,1280]{1,0:T(8,128)(2,1)S(1)} %get-tuple-element.100), channel_id=1, source_target_pairs={{0,2},{2,0},{4,6},{6,4},{8,10},{10,8},{12,14},{14,12},{16,18},{18,... | collective-permute-start | bytes 1966088 | tf_op jit(solution)/shard_map/ppermute | solution.py:28
  88.7 31.1 %collective-permute-start.19 = (bf16[128,2560]{1,0:T(8,128)(2,1)S(1)}, bf16[128,2560]{1,0:T(8,128)(2,1)S(1)}, u32[]{:S(2)}, u32[]{:S(2)}) collective-permute-start(bf16[128,2560]{1,0:T(8,128)(2,1)S(1)} %get-tuple-element.111), channel_id=1, source_target_pairs={{0,8},{2,10},{4,12},{6,14},{8,0},{10,2},{12,4},{14,6},{16,24},{18,... | collective-permute-start | bytes 1966088 | tf_op jit(solution)/shard_map/ppermute | solution.py:28
  102.6 18.7 %collective-permute-start.18 = (bf16[128,2560]{1,0:T(8,128)(2,1)S(1)}, bf16[128,2560]{1,0:T(8,128)(2,1)S(1)}, u32[]{:S(2)}, u32[]{:S(2)}) collective-permute-start(bf16[128,2560]{1,0:T(8,128)(2,1)S(1)} %shard_map.119), channel_id=1, source_target_pairs={{0,2},{2,0},{4,6},{6,4},{8,10},{10,8},{12,14},{14,12},{16,18},{18,... | collective-permute-start | bytes 1966088 | tf_op jit(solution)/shard_map/ppermute | solution.py:28
  103.9 17.3 %collective-permute-start.17 = (bf16[128,2560]{1,0:T(8,128)(2,1)S(1)}, bf16[128,2560]{1,0:T(8,128)(2,1)S(1)}, u32[]{:S(2)}, u32[]{:S(2)}) collective-permute-start(bf16[128,2560]{1,0:T(8,128)(2,1)S(1)} %shard_map.118), channel_id=1, source_target_pairs={{0,4},{2,6},{4,0},{6,2},{8,12},{10,14},{12,8},{14,10},{16,20},{18,... | collective-permute-start | bytes 1966088 | tf_op jit(solution)/shard_map/ppermute | solution.py:28
  104.4 14.6 %collective-permute-start.20 = (bf16[64,2560]{1,0:T(8,128)(2,1)S(1)}, bf16[64,2560]{1,0:T(8,128)(2,1)S(1)}, u32[]{:S(2)}, u32[]{:S(2)}) collective-permute-start(bf16[64,2560]{1,0:T(8,128)(2,1)S(1)} %get-tuple-element.112), channel_id=1, source_target_pairs={{0,16},{2,18},{4,20},{6,22},{8,24},{10,26},{12,28},{14,30},{16,0},... | collective-permute-start | bytes 983048 | tf_op jit(solution)/shard_map/ppermute | solution.py:28
  106.2 14.4 %collective-permute-start.21 = (bf16[64,2560]{1,0:T(8,128)(2,1)S(1)}, bf16[64,2560]{1,0:T(8,128)(2,1)S(1)}, u32[]{:S(2)}, u32[]{:S(2)}) collective-permute-start(bf16[64,2560]{1,0:T(8,128)(2,1)S(1)} %shard_map.120), channel_id=1, source_target_pairs={{0,8},{2,10},{4,12},{6,14},{8,0},{10,2},{12,4},{14,6},{16,24},{18,... | collective-permute-start | bytes 983048 | tf_op jit(solution)/shard_map/ppermute | solution.py:28
  127.6 18.0 %collective-permute-start.25 = (bf16[64,2560]{1,0:T(8,128)(2,1)}, bf16[64,2560]{1,0:T(8,128)(2,1)}, u32[]{:S(2)}, u32[]{:S(2)}) collective-permute-start(bf16[64,2560]{1,0:T(8,128)(2,1)} %shard_map.122), channel_id=1, source_target_pairs={{0,16},{2,18},{4,20},{6,22},{8,24},{10,26},{12,28},{14,30},{16,0},... | collective-permute-start | bytes 983048 | tf_op jit(solution)/shard_map/ppermute | solution.py:28
  145.6 13.2 %collective-permute-start.28 = (f32[5248]{0:T(1024)S(1)}, f32[5248]{0:T(1024)S(1)}, u32[]{:S(2)}, u32[]{:S(2)}) collective-permute-start(f32[5248]{0:T(1024)S(1)} %add_add_fusion.1), channel_id=1, source_target_pairs={{0,24},{2,26},{4,28},{6,30},{8,16},{10,18},{12,20},{14,22},{16,8},... | collective-permute-start | bytes 62984 | tf_op jit(solution)/shard_map/ppermute | solution.py:28
  146.8 12.0 %collective-permute-start.27 = (f32[5248]{0:T(1024)S(1)}, f32[5248]{0:T(1024)S(1)}, u32[]{:S(2)}, u32[]{:S(2)}) collective-permute-start(f32[5248]{0:T(1024)S(1)} %add_add_fusion.1), channel_id=1, source_target_pairs={{0,16},{2,18},{4,20},{6,22},{8,24},{10,26},{12,28},{14,30},{16,0},... | collective-permute-start | bytes 62984 | tf_op jit(solution)/shard_map/ppermute | solution.py:28
  (26 other events, 205.2 us)

commit v12 on v11

--- a/solution.py
+++ b/solution.py
@@ -288,19 +288,26 @@
     )(grad, row_sum, row_moment)
 
 
-def products(share, groups, steps):
+def products(place, share, groups, steps):
     pieces = [(piece, group[1]) for group in groups for piece in group[0]]
     bounds = [(output, group[1]) for group in groups for output in group[2]]
 
-    def kernel(*refs):
+    def kernel(place, *refs):
         share_ref, ins = refs[0], refs[1 : 1 + len(pieces)]
         outs, stacks = refs[1 + len(pieces) : -len(groups)], refs[-len(groups) :]
         n = o = 0
         for (own, _, outputs, over_rows), stack in zip(groups, stacks):
             at = 0
-            for piece in own:
-                stack[at : at + piece.shape[0], :] = ins[n][...]
-                at += piece.shape[0]
+            if over_rows:
+                for piece in own:
+                    stack[at : at + piece.shape[0], :] = ins[n][...]
+                    at += piece.shape[0]
+                    n += 1
+            else:
+                rows = own[0].shape[0] // 4
+                for j in range(4):
+                    there = pl.multiple_of(((place[0] ^ j) & 3) * rows, rows)
+                    stack[j * rows : (j + 1) * rows, :] = ins[n][pl.ds(there, rows), :]
                 n += 1
             for ranges, kind in outputs:
                 if over_rows:
@@ -321,7 +328,7 @@
         kernel,
         grid=(steps,),
         out_shape=[jax.ShapeDtypeStruct((height(ranges), columns), kind) for (ranges, kind), columns in bounds],
-        in_specs=[pl.BlockSpec(share.shape, lambda i: (0, 0))]
+        in_specs=[pl.BlockSpec(memory_space=pltpu.SMEM), pl.BlockSpec(share.shape, lambda i: (0, 0))]
         + [pl.BlockSpec((piece.shape[0], columns // steps), lambda i: (0, i)) for piece, columns in pieces],
         out_specs=[pl.BlockSpec((height(ranges), columns // steps), lambda i: (0, i)) for (ranges, _), columns in bounds],
         scratch_shapes=[
@@ -329,7 +336,7 @@
         ],
         compiler_params=pltpu.CompilerParams(vmem_limit_bytes=14 << 20),
         cost_estimate=EAGER,
-    )(share, *[piece for piece, _ in pieces])
+    )(place, share, *[piece for piece, _ in pieces])
 
 
 def staged_products(out_grad, gate_pre, up_pre, down_weight):
@@ -344,14 +351,11 @@
     place = jnp.stack([me, core]).astype(jnp.int32)
     own, right, message1, message2, message3 = first_stage(out_grad, gate_pre, up_pre, place, rows)
 
-    down_weight, message1 = barrier((down_weight, message1))
-    extra, every, whole = (split, 2 * rows), (0, tokens), (0, units)
+    planes = [[4 * o + i for i in range(4)] for o in range(lax.axis_size("dp") // 4)]
+    weight_all = lax.all_gather(down_weight, "dp", axis=0, tiled=True, axis_index_groups=planes)
+    extra, every = (split, 2 * rows), (0, tokens)
     left1, left2, message3 = flip(message1, z_bit), flip(message2, w_bit), flip(message3, z_bit | w_bit)
-    weight1, weight2 = flip(down_weight, x_bit), flip(down_weight, y_bit)
-    message3, weight1, weight2 = barrier((message3, weight1, weight2))
-    to_y, to_x = cut([weight1, weight2], [(0, (0, q), whole, 0, 0), (1, (q, q), whole, 1, 0)], [(q, units)] * 2)
-    weight3a, weight3b = flip(to_y, y_bit), flip(to_x, x_bit)
-    left1, left2, message3, right, _, _ = barrier((left1, left2, message3, right, to_y, to_x))
+    left1, left2, message3, right = barrier((left1, left2, message3, right))
     to_z, mine = cut(
         [left1, left2, message3],
         [
@@ -363,7 +367,7 @@
         [(tokens, split), (tokens, 6 * rows)],
     )
     left3 = flip(to_z, z_bit)
-    right2 = flip(right, w_bit)
+    right1, right2 = flip(right, z_bit), flip(right, w_bit)
     theirs = flip(mine, 1, "mp")
     share = assemble(own, mine, theirs, place, rows)
 
@@ -380,30 +384,34 @@
         ranges = [(0, 2 * size)], [(4 * size, 5 * size)], [(3 * size, 4 * size)]
         return [(r, jnp.float32) for r in ranges]
 
-    weights = [down_weight, weight1, weight2, weight3a, weight3b]
-    first = [(high_sent(t)[1:], jnp.bfloat16), (high_sent(t)[:1], jnp.bfloat16), (low_sent(t), jnp.bfloat16)]
-    to_w1, to_w2, to_z = products(share, [(weights, units, first, False)], steps)
-    left3, right2, share, right, to_w1 = barrier((left3, right2, share, right, to_w1))
-    right1, right3 = flip(right, z_bit), flip(right2, z_bit)
-    from_w1 = flip(to_w1, w_bit)
-
     lefts = [message1, left1, left2, left3]
-    left_to_x, left_to_y = products(share, [(lefts, split, sent(q), True)], steps)
+    left3, right1, right2 = barrier((left3, right1, right2))
+    right3 = flip(right2, z_bit)
+    left_to_x, left_to_y = products(place, share, [(lefts[:3] + [left3], split, sent(q), True)], steps)
     left_from_x, left_from_y = flip(left_to_x, x_bit), flip(left_to_y, y_bit)
 
-    right1, right3, from_w1, share, _ = barrier((right1, right3, from_w1, share, left_to_x))
+    right1, right3, share, _ = barrier((right1, right3, share, left_to_x))
     rights = [right, right1, right2, right3]
-    right_to_x, right_to_y = products(share, [(rights, units - split, sent(q), True)], steps)
+    right_to_x, right_to_y, to_w, to_z = products(
+        place,
+        share,
+        [
+            (rights, units - split, sent(q), True),
+            ([weight_all], units, [(high_sent(t), jnp.bfloat16), (low_sent(t), jnp.bfloat16)], False),
+        ],
+        steps,
+    )
     right_from_x, right_from_y = flip(right_to_x, x_bit), flip(right_to_y, y_bit)
-    from_w2, from_z = flip(to_w2, w_bit), flip(to_z, z_bit)
+    from_w, from_z = flip(to_w, w_bit), flip(to_z, z_bit)
     share, left_from_x, left_from_y, _ = barrier((share, left_from_x, left_from_y, right_to_x))
-    left_parts = products(share, [(lefts, split, kept(q), True)], steps)
-    parts = products(share, [(rights, units - split, kept(q), True), (weights, units, kept(t), False)], steps)
+    left_parts = products(place, share, [(lefts, split, kept(q), True)], steps)
+    parts = products(
+        place, share, [(rights, units - split, kept(q), True), ([weight_all], units, kept(t), False)], steps
+    )
 
     grad_a = flip(add_tail([left_parts[1], parts[1]], [left_from_x, right_from_x]), y_bit)
     grad_b = flip(add_tail([left_parts[2], parts[2]], [left_from_y, right_from_y]), x_bit)
-    last_b = flip(add_tail([parts[5]], [from_w1]), z_bit)
-    grad_a, grad_b, from_z, from_w2, last_b = barrier((grad_a, grad_b, from_z, from_w2, last_b))
+    grad_a, grad_b, from_z, from_w = barrier((grad_a, grad_b, from_z, from_w))
     grad, row_part = sum_up(
         [left_parts[0], parts[0]],
         [left_from_x, right_from_x],
@@ -413,36 +421,37 @@
         1.0 / math.sqrt(tokens * lax.axis_size("dp")),
     )
 
-    to_w = add_tail([parts[4]], [from_z])
+    to_w, to_z = add_tail([parts[4]], [from_z]), add_tail([parts[5]], [from_w])
     row_sum = lax.psum(row_part, "mp")
-    row_sum, to_w = barrier((row_sum, to_w))
-    last_a = flip(to_w, w_bit)
-    return grad, row_sum, (parts[3], from_z, from_w2, last_a, last_b)
+    row_sum, to_w, to_z = barrier((row_sum, to_w, to_z))
+    last_a, last_b = flip(to_w, w_bit), flip(to_z, z_bit)
+    return grad, row_sum, (parts[3], from_z, from_w, last_a, last_b)
 
 
 def hidden_gradients(gate_pre, up_pre, own_part, from_low, from_high, last_a, last_b):
     tokens, units = gate_pre.shape
-    half, step = tokens // 2, 16
+    step = 32
+    per_half = tokens // 2 // step
 
     def kernel(gate, up, own, low, high, last_a, last_b, gate_grad, up_grad):
-        for h, (other, last) in enumerate(((low, last_a), (high, last_b))):
-
-            @pl.loop(0, half // step)
-            def _(i):
-                here = pl.ds(pl.multiple_of(i * step, step), step)
-                there = pl.ds(pl.multiple_of(h * half + i * step, step), step)
-                value = own[there, :] + other[here, :].astype(jnp.float32) + last[here, :].astype(jnp.float32)
-                activated, derivative = gelu_parts(gate[there, :].astype(jnp.float32))
-                gate_grad[there, :] = (value * up[there, :].astype(jnp.float32) * derivative).astype(jnp.bfloat16)
-                up_grad[there, :] = (value * activated).astype(jnp.bfloat16)
-
-    vmem = pl.BlockSpec(memory_space=pltpu.VMEM)
-    return pl.pallas_call(
-        kernel,
+        in_low = pl.program_id(0) < per_half
+        other = jnp.where(in_low, low[...].astype(jnp.float32), high[...].astype(jnp.float32))
+        last = jnp.where(in_low, last_a[...].astype(jnp.float32), last_b[...].astype(jnp.float32))
+        value = own[...] + other + last
+        activated, derivative = gelu_parts(gate[...].astype(jnp.float32))
+        gate_grad[...] = (value * up[...].astype(jnp.float32) * derivative).astype(jnp.bfloat16)
+        up_grad[...] = (value * activated).astype(jnp.bfloat16)
+
+    whole = pl.BlockSpec((step, units), lambda i: (i, 0))
+    first = pl.BlockSpec((step, units), lambda i: (jnp.minimum(i, per_half - 1), 0))
+    second = pl.BlockSpec((step, units), lambda i: (jnp.maximum(i - per_half, 0), 0))
+    return pl.pallas_call(
+        kernel,
+        grid=(tokens // step,),
         out_shape=[jax.ShapeDtypeStruct((tokens, units), jnp.bfloat16)] * 2,
-        in_specs=[vmem] * 7,
-        out_specs=[vmem] * 2,
-        compiler_params=pltpu.CompilerParams(vmem_limit_bytes=12 << 20),
+        in_specs=[whole, whole, whole, first, second, first, second],
+        out_specs=[whole] * 2,
+        compiler_params=pltpu.CompilerParams(vmem_limit_bytes=56 << 20),
         cost_estimate=EAGER,
     )(gate_pre, up_pre, own_part, from_low, from_high, last_a, last_b)
 

time: 167 us -> 175 us (1.048)
  between operations: 3.34 us -> 16.8 us
  waiting for transfers between devices: 81.8 us -> 74.5 us
  starting transfers between devices: 36.3 us -> 30.8 us
  local copies, waits for them, and re-layouts: 13.8 us -> 17.6 us
  Pallas kernels: 23.8 us -> 26.6 us
    ppermute x29 -> x24, waiting for transfers between devices: 81.8 us -> 73.8 us  [flip(): return lax.ppermute(value, axis, [(i, i ^ bits) for i in range(size)])]
    ppermute x29 -> x24, starting transfers between devices: 36.3 us -> 30.8 us  [flip(): return lax.ppermute(value, axis, [(i, i ^ bits) for i in range(size)])]
    unnamed x42 -> x68, local copies, waits for them, and re-layouts: 13.3 us -> 17.1 us
    pallas_call x5 -> x4, Pallas kernels: 15.1 us -> 16.1 us  [products(): pl.pallas_call(kernel, grid=(steps,), out_shape=[jax.ShapeDtypeStruct((he...]
  transfers between devices with their start and end apart: 29 -> 25, of which waited for: 17 -> 13; matrix products, arithmetic and copies ran while one was open for 0% -> 0% of each run, Pallas kernels for 12% -> 14%
where the time goes in v12:
time: 175 us; the launch traced here: 174 us
  waiting for transfers between devices  74.5 us (43%)
  starting transfers between devices  30.8 us (18%)
  Pallas kernels  26.6 us (15%)
  local copies, waits for them, and re-layouts  17.6 us (10%)
  between operations  16.8 us (10%)
  blocking collectives  5.08 us (3%)
  other arithmetic  2.56 us (1%)
    ppermute x24, waiting for transfers between devices, flip(): return lax.ppermute(value, axis, [(i, i ^ bits) for i in range(size)])  73.8 us
    ppermute x24, starting transfers between devices, flip(): return lax.ppermute(value, axis, [(i, i ^ bits) for i in range(size)])  30.8 us
    unnamed x68, local copies, waits for them, and re-layouts  17.1 us
    pallas_call x4, Pallas kernels, products(): pl.pallas_call(kernel, grid=(steps,), out_shape=[jax.ShapeDtypeStruct((he...  16.1 us
    pallas_call x1, Pallas kernels, hidden_gradients(): pl.pallas_call(kernel, grid=(tokens // step,), out_shape=[jax.ShapeDtypeS...  4.75 us
  transfers between devices with their start and end apart: 25, of which 13 were waited for; matrix products, arithmetic and copies ran while one was open for 0% of the time, Pallas kernels for 14%

profile of v12, /device:TPU:0, one launch (start us, length us, event | category | flops | bytes accessed | tf_op | source)
XLA Modules:
  0.0 173.9 jit_solution(14392797334251402898)
XLA Ops:
  11.4 1.7 shard_map.109
  13.1 4.1 %collective-permute-start.1 = (bf16[128,1792]{1,0:T(8,128)(2,1)S(1)}, bf16[128,1792]{1,0:T(8,128)(2,1)S(1)}, u32[]{:S(2)}, u32[]{:S(2)}) collective-permute-start(bf16[128,1792]{1,0:T(8,128)(2,1)S(1)} %get-tuple-element.61), channel_id=1, source_target_pairs={{0,16},{2,18},{4,20},{6,22},{8,24},{10,26},{12,28},{14,30},{16,0},... | collective-permute-start | bytes 1376264 | tf_op jit(solution)/shard_map/ppermute | solution.py:28
  18.8 22.8 %collective-permute-done.2.refs_2_ = bf16[128,512]{1,0:T(8,128)(2,1)S(1)} collective-permute-done((bf16[128,512]{1,0:T(8,128)(2,1)S(1)}, bf16[128,512]{1,0:T(8,128)(2,1)S(1)}, u32[]{:S(2)}, u32[]{:S(2)}) %collective-permute-start.2) | collective-permute-done | bytes 131104 | tf_op jit(solution)/shard_map/ppermute | solution.py:28
  41.6 4.2 %collective-permute-start.5 = (bf16[128,1280]{1,0:T(8,128)(2,1)S(1)}, bf16[128,1280]{1,0:T(8,128)(2,1)S(1)}, u32[]{:S(2)}, u32[]{:S(2)}) collective-permute-start(bf16[128,1280]{1,0:T(8,128)(2,1)S(1)} %get-tuple-element.68.refs_1_), channel_id=1, source_target_pairs={{0,16},{2,18},{4,20},{6,22},{8,24},{10,26},{12,28},{14,30},{16,0},... | collective-permute-start | bytes 983048 | tf_op jit(solution)/shard_map/ppermute | solution.py:28
  45.9 2.1 %collective-permute-start.3 = (bf16[128,1280]{1,0:T(8,128)(2,1)S(1)}, bf16[128,1280]{1,0:T(8,128)(2,1)S(1)}, u32[]{:S(2)}, u32[]{:S(2)}) collective-permute-start(bf16[128,1280]{1,0:T(8,128)(2,1)S(1)} %get-tuple-element.67), channel_id=1, source_target_pairs={{0,8},{2,10},{4,12},{6,14},{8,0},{10,2},{12,4},{14,6},{16,24},{18,... | collective-permute-start | bytes 983048 | tf_op jit(solution)/shard_map/ppermute | solution.py:28
  48.0 12.8 %collective-permute-done.5.refs_3_ = bf16[128,1280]{1,0:T(8,128)(2,1)S(1)} collective-permute-done((bf16[128,1280]{1,0:T(8,128)(2,1)S(1)}, bf16[128,1280]{1,0:T(8,128)(2,1)S(1)}, u32[]{:S(2)}, u32[]{:S(2)}) %collective-permute-start.5) | collective-permute-done | bytes 327712 | tf_op jit(solution)/shard_map/ppermute | solution.py:28
  60.9 2.4 %collective-permute-done.4.refs_2_ = bf16[128,1280]{1,0:T(8,128)(2,1)S(1)} collective-permute-done((bf16[128,1280]{1,0:T(8,128)(2,1)S(1)}, bf16[128,1280]{1,0:T(8,128)(2,1)S(1)}, u32[]{:S(2)}, u32[]{:S(2)}) %collective-permute-start.4) | collective-permute-done | bytes 327712 | tf_op jit(solution)/shard_map/ppermute | solution.py:28
  63.9 5.0 %collective-permute-done.3.refs_4_ = bf16[128,1280]{1,0:T(8,128)(2,1)S(1)} collective-permute-done((bf16[128,1280]{1,0:T(8,128)(2,1)S(1)}, bf16[128,1280]{1,0:T(8,128)(2,1)S(1)}, u32[]{:S(2)}, u32[]{:S(2)}) %collective-permute-start.3) | collective-permute-done | bytes 327712 | tf_op jit(solution)/shard_map/ppermute | solution.py:28
  70.2 3.8 %shard_map.112 = (bf16[256,1280]{1,0:T(8,128)(2,1)}, bf16[256,1280]{1,0:T(8,128)(2,1)}) custom-call(s32[2]{0:T(128)S(1)} %pad_add_fusion.place, bf16[512,1024]{1,0:T(8,128)(2,1)S(1)} %shard_map.111.refs_0_, bf16[128,1792]{1,0:T(8,128)(2,1)S(1)} %get-tuple-element.60.refs_1_, bf16[128,1792]{1,0:T(8,128)(2,1)S(1)} %collective-permute-done.refs_0_.refs_2_, ...), custom_call_target="tpu_custom_call" | custom-call | tf_op jit(solution)/shard_map/pallas_call | solution.py:327
  74.0 1.6 collective-permute-start.9
  78.3 2.5 %copy-done = bf16[1024,2560]{1,0:T(8,128)(2,1)S(1)} copy-done((bf16[1024,2560]{1,0:T(8,128)(2,1)S(1)}, bf16[1024,2560]{1,0:T(8,128)(2,1)}, u32[]{:S(2)}) %copy-start) | copy-done | bytes 5242904
  84.6 4.3 %shard_map.113 = (bf16[256,1280]{1,0:T(8,128)(2,1)S(1)}, bf16[256,1280]{1,0:T(8,128)(2,1)S(1)}, bf16[128,2560]{1,0:T(8,128)(2,1)S(1)}, bf16[128,2560]{1,0:T(8,128)(2,1)S(1)}) custom-call(s32[2]{0:T(128)S(1)} %pad_add_fusion.place, bf16[512,1024]{1,0:T(8,128)(2,1)S(1)} %shard_map.111.refs_0_, bf16[128,1280]{1,0:T(8,128)(2,1)S(1)} %copy-done.16, ...), custom_call_target="tpu_custom_call" | custom-call | tf_op jit(solution)/shard_map/pallas_call | solution.py:327
  88.9 1.6 collective-permute-start.11
  94.7 5.4 %shard_map.115 = (f32[256,1280]{1,0:T(8,128)S(1)}, f32[128,1280]{1,0:T(8,128)S(1)}, f32[128,1280]{1,0:T(8,128)S(1)}, f32[128,2560]{1,0:T(8,128)S(1)}, f32[64,2560]{1,0:T(8,128)S(1)}, /*index=5*/f32[64,2560]{1,0:T(8,128)S(1)}) custom-call(s32[2]{0:T(128)S(1)} %pad_add_fusion.place, bf16[512,1024]{1,0:T(8,128)(2,1)S(1)} %shard_map.111.refs_0_, ...), custom_call_target="tpu_custom_call" | custom-call | tf_op jit(solution)/shard_map/pallas_call | solution.py:327
  100.2 2.7 %shard_map.114 = (f32[256,1280]{1,0:T(8,128)S(1)}, f32[128,1280]{1,0:T(8,128)S(1)}, f32[128,1280]{1,0:T(8,128)S(1)}) custom-call(s32[2]{0:T(128)S(1)} %pad_add_fusion.place, bf16[512,1024]{1,0:T(8,128)(2,1)S(1)} %shard_map.111.refs_0_, bf16[128,1792]{1,0:T(8,128)(2,1)S(1)} %copy-done.11, bf16[128,1792]{1,0:T(8,128)(2,1)S(1)} %collective-permute-done.refs_0_.refs_2_, ...), custom_call_target="tpu_custom_call" | custom-call | tf_op jit(solution)/shard_map/pallas_call | solution.py:327
  107.4 12.6 %collective-permute-done.14.refs_1_.low = bf16[128,2560]{1,0:T(8,128)(2,1)S(1)} collective-permute-done((bf16[128,2560]{1,0:T(8,128)(2,1)S(1)}, bf16[128,2560]{1,0:T(8,128)(2,1)S(1)}, u32[]{:S(2)}, u32[]{:S(2)}) %collective-permute-start.14) | collective-permute-done | bytes 655392 | tf_op jit(solution)/shard_map/ppermute | solution.py:28
  120.0 3.8 %collective-permute-done.15.refs_1_.high = bf16[128,2560]{1,0:T(8,128)(2,1)S(1)} collective-permute-done((bf16[128,2560]{1,0:T(8,128)(2,1)S(1)}, bf16[128,2560]{1,0:T(8,128)(2,1)S(1)}, u32[]{:S(2)}, u32[]{:S(2)}) %collective-permute-start.15) | collective-permute-done | bytes 655392 | tf_op jit(solution)/shard_map/ppermute | solution.py:28
  125.4 2.6 %psum.14.row_sum = f32[1,256]{1,0:T(1,128)S(1)} all-reduce(f32[1,256]{1,0:T(1,128)S(1)} %get-tuple-element.95), channel_id=1, replica_groups=mesh['dp'=16,'mp'=2] {'mp'}, use_global_device_ids=true, to_apply=%region_0.0 | all-reduce | flops 256 | bytes 2048 | tf_op jit(solution)/shard_map/psum | solution.py:425
  133.9 2.4 %collective-permute-start.18 = (f32[5248]{0:T(1024)S(1)}, f32[5248]{0:T(1024)S(1)}, u32[]{:S(2)}, u32[]{:S(2)}) collective-permute-start(f32[5248]{0:T(1024)S(1)} %reduce), channel_id=1, source_target_pairs={{0,6},{2,4},{4,2},{6,0},{8,14},{10,12},{12,10},{14,8},{16,22},{18,... | collective-permute-start | bytes 62984 | tf_op jit(solution)/shard_map/ppermute | solution.py:28
  140.1 8.8 %collective-permute-done.19.last_a = bf16[64,2560]{1,0:T(8,128)(2,1)S(1)} collective-permute-done((bf16[64,2560]{1,0:T(8,128)(2,1)}, bf16[64,2560]{1,0:T(8,128)(2,1)S(1)}, u32[]{:S(2)}, u32[]{:S(2)}) %collective-permute-start.19) | collective-permute-done | bytes 327712 | tf_op jit(solution)/shard_map/ppermute | solution.py:28
  151.7 2.6 %collective-permute-start.21 = (f32[5248]{0:T(1024)S(1)}, f32[5248]{0:T(1024)S(1)}, u32[]{:S(2)}, u32[]{:S(2)}) collective-permute-start(f32[5248]{0:T(1024)S(1)} %add_add_fusion.1), channel_id=1, source_target_pairs={{0,8},{2,10},{4,12},{6,14},{8,0},{10,2},{12,4},{14,6},{16,24},{18,... | collective-permute-start | bytes 62984 | tf_op jit(solution)/shard_map/ppermute | solution.py:28
  154.3 4.8 %shard_map.122 = (bf16[128,2560]{1,0:T(8,128)(2,1)}, bf16[128,2560]{1,0:T(8,128)(2,1)}) custom-call(bf16[128,2560]{1,0:T(8,128)(2,1)} %gate.1, bf16[128,2560]{1,0:T(8,128)(2,1)} %up.1, f32[128,2560]{1,0:T(8,128)} %copy-done.14, bf16[128,2560]{1,0:T(8,128)(2,1)} %copy-done.3, bf16[128,2560]{1,0:T(8,128)(2,1)} %copy-done.4, bf16[64,2560]{1,0:T(8,128)(2,1)} %copy-done.30, ...), custom_call_target="tpu_custom_call" | custom-call | tf_op jit(solution)/shard_map/pallas_call | solution.py:448
  159.7 2.5 %psum.15 = f32[128]{0:T(128)S(1)} all-reduce(f32[128]{0:T(128)S(1)} %get-tuple-element.114), channel_id=1, replica_groups=mesh['dp'=16,'mp'=2] {'mp'}, use_global_device_ids=true, to_apply=%region_2.0 | all-reduce | flops 128 | bytes 1024 | tf_op jit(solution)/shard_map/psum | solution.py:495
  164.1 1.8 %multiply_multiply_fusion = f32[256,2560]{1,0:T(8,128)} fusion(f32[256,2560]{1,0:T(8,128)S(1)} %get-tuple-element.94.grad, f32[2560]{0:T(1024)S(1)} %sqrt.15, f32[256]{0:T(256)S(1)} %sqrt_divide_fusion), kind=kLoop, calls=%fused_computation | loop fusion | flops 1310720 | bytes 5254144 | tf_op jit(solution)/shard_map/mul | solution.py:499
  (121 shorter events, 38.4 us)
Async XLA Ops:
  7.2 71.1 %all-gather.2.cloned.1.call-start = ((), (), s32[]{:S(2)}) async-start(), calls=%async_computation | async-start | bytes 6553600 | tf_op jit(solution)/shard_map/all_gather | solution.py:355
  13.1 28.5 %collective-permute-start.1 = (bf16[128,1792]{1,0:T(8,128)(2,1)S(1)}, bf16[128,1792]{1,0:T(8,128)(2,1)S(1)}, u32[]{:S(2)}, u32[]{:S(2)}) collective-permute-start(bf16[128,1792]{1,0:T(8,128)(2,1)S(1)} %get-tuple-element.61), channel_id=1, source_target_pairs={{0,16},{2,18},{4,20},{6,22},{8,24},{10,26},{12,28},{14,30},{16,0},... | collective-permute-start | bytes 1376264 | tf_op jit(solution)/shard_map/ppermute | solution.py:28
  17.2 24.4 %collective-permute-start = (bf16[128,1792]{1,0:T(8,128)(2,1)S(1)}, bf16[128,1792]{1,0:T(8,128)(2,1)S(1)}, u32[]{:S(2)}, u32[]{:S(2)}) collective-permute-start(bf16[128,1792]{1,0:T(8,128)(2,1)S(1)} %get-tuple-element.60.refs_1_), channel_id=1, source_target_pairs={{0,8},{2,10},{4,12},{6,14},{8,0},{10,2},{12,4},{14,6},{16,24},{18,... | collective-permute-start | bytes 1376264 | tf_op jit(solution)/shard_map/ppermute | solution.py:28
  18.8 22.8 %collective-permute-start.2 = (bf16[128,512]{1,0:T(8,128)(2,1)S(1)}, bf16[128,512]{1,0:T(8,128)(2,1)S(1)}, u32[]{:S(2)}, u32[]{:S(2)}) collective-permute-start(bf16[128,512]{1,0:T(8,128)(2,1)S(1)} %get-tuple-element.62), channel_id=1, source_target_pairs={{0,24},{2,26},{4,28},{6,30},{8,16},{10,18},{12,20},{14,22},{16,8},... | collective-permute-start | bytes 393224 | tf_op jit(solution)/shard_map/ppermute | solution.py:28
  41.6 19.3 %collective-permute-start.5 = (bf16[128,1280]{1,0:T(8,128)(2,1)S(1)}, bf16[128,1280]{1,0:T(8,128)(2,1)S(1)}, u32[]{:S(2)}, u32[]{:S(2)}) collective-permute-start(bf16[128,1280]{1,0:T(8,128)(2,1)S(1)} %get-tuple-element.68.refs_1_), channel_id=1, source_target_pairs={{0,16},{2,18},{4,20},{6,22},{8,24},{10,26},{12,28},{14,30},{16,0},... | collective-permute-start | bytes 983048 | tf_op jit(solution)/shard_map/ppermute | solution.py:28
  45.8 17.4 %collective-permute-start.4 = (bf16[128,1280]{1,0:T(8,128)(2,1)S(1)}, bf16[128,1280]{1,0:T(8,128)(2,1)S(1)}, u32[]{:S(2)}, u32[]{:S(2)}) collective-permute-start(bf16[128,1280]{1,0:T(8,128)(2,1)S(1)} %get-tuple-element.68.refs_1_), channel_id=1, source_target_pairs={{0,8},{2,10},{4,12},{6,14},{8,0},{10,2},{12,4},{14,6},{16,24},{18,... | collective-permute-start | bytes 983048 | tf_op jit(solution)/shard_map/ppermute | solution.py:28
  45.9 23.0 %collective-permute-start.3 = (bf16[128,1280]{1,0:T(8,128)(2,1)S(1)}, bf16[128,1280]{1,0:T(8,128)(2,1)S(1)}, u32[]{:S(2)}, u32[]{:S(2)}) collective-permute-start(bf16[128,1280]{1,0:T(8,128)(2,1)S(1)} %get-tuple-element.67), channel_id=1, source_target_pairs={{0,8},{2,10},{4,12},{6,14},{8,0},{10,2},{12,4},{14,6},{16,24},{18,... | collective-permute-start | bytes 983048 | tf_op jit(solution)/shard_map/ppermute | solution.py:28
  48.0 21.5 %collective-permute-start.7 = (bf16[128,1536]{1,0:T(8,128)(2,1)S(1)}, bf16[128,1536]{1,0:T(8,128)(2,1)S(1)}, u32[]{:S(2)}, u32[]{:S(2)}) collective-permute-start(bf16[128,1536]{1,0:T(8,128)(2,1)S(1)} %get-tuple-element.72.mine), channel_id=1, source_target_pairs={{0,1},{1,0},{2,3},{3,2},{4,5},{5,4},{6,7},{7,6},{8,9},{9,8},{10,11... | collective-permute-start | bytes 1179656 | tf_op jit(solution)/shard_map/ppermute | solution.py:28
  69.0 8.6 %collective-permute-start.6 = (bf16[128,1280]{1,0:T(8,128)(2,1)S(1)}, bf16[128,1280]{1,0:T(8,128)(2,1)S(1)}, u32[]{:S(2)}, u32[]{:S(2)}) collective-permute-start(bf16[128,1280]{1,0:T(8,128)(2,1)S(1)} %collective-permute-done.5.refs_3_), channel_id=1, source_target_pairs={{0,8},{2,10},{4,12},{6,14},{8,0},{10,2},{12,4},{14,6},{16,24},{18,... | collective-permute-start | bytes 983048 | tf_op jit(solution)/shard_map/ppermute | solution.py:28
  74.0 18.0 %collective-permute-start.9 = (bf16[256,1280]{1,0:T(8,128)(2,1)}, bf16[256,1280]{1,0:T(8,128)(2,1)S(1)}, u32[]{:S(2)}, u32[]{:S(2)}) collective-permute-start(bf16[256,1280]{1,0:T(8,128)(2,1)} %get-tuple-element.76), channel_id=1, source_target_pairs={{0,4},{2,6},{4,0},{6,2},{8,12},{10,14},{12,8},{14,10},{16,20},{18,... | collective-permute-start | bytes 1966088 | tf_op jit(solution)/shard_map/ppermute | solution.py:28
  75.6 17.3 %collective-permute-start.8 = (bf16[256,1280]{1,0:T(8,128)(2,1)}, bf16[256,1280]{1,0:T(8,128)(2,1)S(1)}, u32[]{:S(2)}, u32[]{:S(2)}) collective-permute-start(bf16[256,1280]{1,0:T(8,128)(2,1)} %get-tuple-element.74), channel_id=1, source_target_pairs={{0,2},{2,0},{4,6},{6,4},{8,10},{10,8},{12,14},{14,12},{16,18},{18,... | collective-permute-start | bytes 1966088 | tf_op jit(solution)/shard_map/ppermute | solution.py:28
  88.9 15.0 %collective-permute-start.11 = (bf16[256,1280]{1,0:T(8,128)(2,1)S(1)}, bf16[256,1280]{1,0:T(8,128)(2,1)S(1)}, u32[]{:S(2)}, u32[]{:S(2)}) collective-permute-start(bf16[256,1280]{1,0:T(8,128)(2,1)S(1)} %get-tuple-element.85), channel_id=1, source_target_pairs={{0,4},{2,6},{4,0},{6,2},{8,12},{10,14},{12,8},{14,10},{16,20},{18,... | collective-permute-start | bytes 1966088 | tf_op jit(solution)/shard_map/ppermute | solution.py:28
  90.5 15.6 %collective-permute-start.10 = (bf16[256,1280]{1,0:T(8,128)(2,1)S(1)}, bf16[256,1280]{1,0:T(8,128)(2,1)S(1)}, u32[]{:S(2)}, u32[]{:S(2)}) collective-permute-start(bf16[256,1280]{1,0:T(8,128)(2,1)S(1)} %get-tuple-element.79), channel_id=1, source_target_pairs={{0,2},{2,0},{4,6},{6,4},{8,10},{10,8},{12,14},{14,12},{16,18},{18,... | collective-permute-start | bytes 1966088 | tf_op jit(solution)/shard_map/ppermute | solution.py:28
  93.7 26.3 %collective-permute-start.14 = (bf16[128,2560]{1,0:T(8,128)(2,1)S(1)}, bf16[128,2560]{1,0:T(8,128)(2,1)S(1)}, u32[]{:S(2)}, u32[]{:S(2)}) collective-permute-start(bf16[128,2560]{1,0:T(8,128)(2,1)S(1)} %get-tuple-element.90), channel_id=1, source_target_pairs={{0,8},{2,10},{4,12},{6,14},{8,0},{10,2},{12,4},{14,6},{16,24},{18,... | collective-permute-start | bytes 1966088 | tf_op jit(solution)/shard_map/ppermute | solution.py:28
  94.6 29.1 %collective-permute-start.15 = (bf16[128,2560]{1,0:T(8,128)(2,1)S(1)}, bf16[128,2560]{1,0:T(8,128)(2,1)S(1)}, u32[]{:S(2)}, u32[]{:S(2)}) collective-permute-start(bf16[128,2560]{1,0:T(8,128)(2,1)S(1)} %get-tuple-element.91), channel_id=1, source_target_pairs={{0,16},{2,18},{4,20},{6,22},{8,24},{10,26},{12,28},{14,30},{16,0},... | collective-permute-start | bytes 1966088 | tf_op jit(solution)/shard_map/ppermute | solution.py:28
  104.1 20.5 %collective-permute-start.13 = (bf16[128,2560]{1,0:T(8,128)(2,1)S(1)}, bf16[128,2560]{1,0:T(8,128)(2,1)S(1)}, u32[]{:S(2)}, u32[]{:S(2)}) collective-permute-start(bf16[128,2560]{1,0:T(8,128)(2,1)S(1)} %shard_map.117), channel_id=1, source_target_pairs={{0,2},{2,0},{4,6},{6,4},{8,10},{10,8},{12,14},{14,12},{16,18},{18,... | collective-permute-start | bytes 1966088 | tf_op jit(solution)/shard_map/ppermute | solution.py:28
  106.2 18.4 %collective-permute-start.12 = (bf16[128,2560]{1,0:T(8,128)(2,1)S(1)}, bf16[128,2560]{1,0:T(8,128)(2,1)S(1)}, u32[]{:S(2)}, u32[]{:S(2)}) collective-permute-start(bf16[128,2560]{1,0:T(8,128)(2,1)S(1)} %shard_map.116), channel_id=1, source_target_pairs={{0,4},{2,6},{4,0},{6,2},{8,12},{10,14},{12,8},{14,10},{16,20},{18,... | collective-permute-start | bytes 1966088 | tf_op jit(solution)/shard_map/ppermute | solution.py:28
  132.8 16.1 %collective-permute-start.19 = (bf16[64,2560]{1,0:T(8,128)(2,1)}, bf16[64,2560]{1,0:T(8,128)(2,1)S(1)}, u32[]{:S(2)}, u32[]{:S(2)}) collective-permute-start(bf16[64,2560]{1,0:T(8,128)(2,1)} %shard_map.119), channel_id=1, source_target_pairs={{0,16},{2,18},{4,20},{6,22},{8,24},{10,26},{12,28},{14,30},{16,0},... | collective-permute-start | bytes 983048 | tf_op jit(solution)/shard_map/ppermute | solution.py:28
  133.0 16.9 %collective-permute-start.20 = (bf16[64,2560]{1,0:T(8,128)(2,1)}, bf16[64,2560]{1,0:T(8,128)(2,1)}, u32[]{:S(2)}, u32[]{:S(2)}) collective-permute-start(bf16[64,2560]{1,0:T(8,128)(2,1)} %shard_map.120), channel_id=1, source_target_pairs={{0,8},{2,10},{4,12},{6,14},{8,0},{10,2},{12,4},{14,6},{16,24},{18,... | collective-permute-start | bytes 983048 | tf_op jit(solution)/shard_map/ppermute | solution.py:28
  133.9 4.8 %collective-permute-start.18 = (f32[5248]{0:T(1024)S(1)}, f32[5248]{0:T(1024)S(1)}, u32[]{:S(2)}, u32[]{:S(2)}) collective-permute-start(f32[5248]{0:T(1024)S(1)} %reduce), channel_id=1, source_target_pairs={{0,6},{2,4},{4,2},{6,0},{8,14},{10,12},{12,10},{14,8},{16,22},{18,... | collective-permute-start | bytes 62984 | tf_op jit(solution)/shard_map/ppermute | solution.py:28
  136.3 3.8 %collective-permute-start.17 = (f32[5248]{0:T(1024)S(1)}, f32[5248]{0:T(1024)S(1)}, u32[]{:S(2)}, u32[]{:S(2)}) collective-permute-start(f32[5248]{0:T(1024)S(1)} %reduce), channel_id=1, source_target_pairs={{0,4},{2,6},{4,0},{6,2},{8,12},{10,14},{12,8},{14,10},{16,20},{18,... | collective-permute-start | bytes 62984 | tf_op jit(solution)/shard_map/ppermute | solution.py:28
  149.9 9.1 %collective-permute-start.23 = (f32[5248]{0:T(1024)S(1)}, f32[5248]{0:T(1024)S(1)}, u32[]{:S(2)}, u32[]{:S(2)}) collective-permute-start(f32[5248]{0:T(1024)S(1)} %add_add_fusion.1), channel_id=1, source_target_pairs={{0,24},{2,26},{4,28},{6,30},{8,16},{10,18},{12,20},{14,22},{16,8},... | collective-permute-start | bytes 62984 | tf_op jit(solution)/shard_map/ppermute | solution.py:28
  150.8 8.3 %collective-permute-start.22 = (f32[5248]{0:T(1024)S(1)}, f32[5248]{0:T(1024)S(1)}, u32[]{:S(2)}, u32[]{:S(2)}) collective-permute-start(f32[5248]{0:T(1024)S(1)} %add_add_fusion.1), channel_id=1, source_target_pairs={{0,16},{2,18},{4,20},{6,22},{8,24},{10,26},{12,28},{14,30},{16,0},... | collective-permute-start | bytes 62984 | tf_op jit(solution)/shard_map/ppermute | solution.py:28
  151.7 7.4 %collective-permute-start.21 = (f32[5248]{0:T(1024)S(1)}, f32[5248]{0:T(1024)S(1)}, u32[]{:S(2)}, u32[]{:S(2)}) collective-permute-start(f32[5248]{0:T(1024)S(1)} %add_add_fusion.1), channel_id=1, source_target_pairs={{0,8},{2,10},{4,12},{6,14},{8,0},{10,2},{12,4},{14,6},{16,24},{18,... | collective-permute-start | bytes 62984 | tf_op jit(solution)/shard_map/ppermute | solution.py:28
  (35 other events, 293.0 us)
Sparse Core Ops, SparseCore 0:
  9.8 64.1 all-gather.1

commit v13 on v9

--- a/solution.py
+++ b/solution.py
@@ -9,7 +9,6 @@
 
 TRAIN_STEP = 3
 INNER_BITS = 2
-LEFT = 3
 EAGER = pl.CostEstimate(flops=0, bytes_accessed=0, transcendentals=0)
 
 
@@ -93,7 +92,7 @@
 
 def first_stage(out_grad, gate_pre, up_pre, place, rows):
     tokens, units = gate_pre.shape
-    half = units * LEFT // 5
+    half = units // 2
     step = 32
 
     def kernel(place, source_hbm, gate_hbm, up_hbm, own, right, message1, message2, message3, source, gate, up, sems):
@@ -200,7 +199,7 @@
     def kernel(*refs):
         out, at = refs[-1], 0
         for part, other, width in zip(refs, refs[len(parts) :], widths):
-            out[:, at : at + width] = (part[...] + other[rows:, :].astype(jnp.float32)).astype(jnp.bfloat16)
+            out[:, at : at + width] = (part[...] + other[-rows:, :].astype(jnp.float32)).astype(jnp.bfloat16)
             at += width
 
     vmem = pl.BlockSpec(memory_space=pltpu.VMEM)
@@ -299,7 +298,7 @@
         n = o = 0
         for (own, _, outputs, over_rows), stack in zip(groups, stacks):
             at = 0
-            for piece in own:
+            for piece, _ in own:
                 stack[at : at + piece.shape[0], :] = ins[n][...]
                 at += piece.shape[0]
                 n += 1
@@ -323,14 +322,17 @@
         grid=(steps,),
         out_shape=[jax.ShapeDtypeStruct((height(ranges), columns), kind) for (ranges, kind), columns in bounds],
         in_specs=[pl.BlockSpec(share.shape, lambda i: (0, 0))]
-        + [pl.BlockSpec((piece.shape[0], columns // steps), lambda i: (0, i)) for piece, columns in pieces],
+        + [
+            pl.BlockSpec((piece.shape[0], columns // steps), lambda i, skip=first * steps // columns: (0, i + skip))
+            for (piece, first), columns in pieces
+        ],
         out_specs=[pl.BlockSpec((height(ranges), columns // steps), lambda i: (0, i)) for (ranges, _), columns in bounds],
         scratch_shapes=[
-            pltpu.VMEM((sum(piece.shape[0] for piece in group[0]), group[1] // steps), jnp.bfloat16) for group in groups
+            pltpu.VMEM((sum(piece.shape[0] for piece, _ in group[0]), group[1] // steps), jnp.bfloat16) for group in groups
         ],
         compiler_params=pltpu.CompilerParams(vmem_limit_bytes=14 << 20),
         cost_estimate=EAGER,
-    )(share, *[piece for piece, _ in pieces])
+    )(share, *[piece for (piece, _), _ in pieces])
 
 
 def staged_products(out_grad, gate_pre, up_pre, down_weight):
@@ -339,8 +341,8 @@
     tokens, units = gate_pre.shape
     rows = down_weight.shape[0]
     q, t = rows // 2, tokens // 2
-    steps = 4
-    split = units * LEFT // 5
+    steps = 5
+    split = units // 2
     barrier = lax.optimization_barrier
     place = jnp.stack([me, core]).astype(jnp.int32)
     own, right, message1, message2, message3 = first_stage(out_grad, gate_pre, up_pre, place, rows)
@@ -349,26 +351,25 @@
     extra, every, whole = (split, 2 * rows), (0, tokens), (0, units)
     left1, left2, message3 = flip(message1, z_bit), flip(message2, w_bit), flip(message3, z_bit | w_bit)
     weight1, weight2 = flip(down_weight, x_bit), flip(down_weight, y_bit)
-
+    message3, weight1, weight2 = barrier((message3, weight1, weight2))
     to_y, to_x = cut([weight1, weight2], [(0, (0, q), whole, 0, 0), (1, (q, q), whole, 1, 0)], [(q, units)] * 2)
     weight3a, weight3b = flip(to_y, y_bit), flip(to_x, x_bit)
-    left1, left2, message3, _, _ = barrier((left1, left2, message3, to_y, to_x))
+    left1, left2, message3, right, _, _ = barrier((left1, left2, message3, right, to_y, to_x))
     to_z, mine = cut(
-        [left1, left2, message3],
+        [left1, left2, message3, right],
         [
             (1, every, (0, split), 0, 0),
+            (3, every, (0, units - split), 0, split),
             (0, every, extra, 1, 0),
             (1, every, extra, 1, 2 * rows),
             (2, every, (0, 2 * rows), 1, 4 * rows),
         ],
-        [(tokens, split), (tokens, 6 * rows)],
-    )
-    left3 = flip(to_z, z_bit)
+        [(tokens, units), (tokens, 6 * rows)],
+    )
+    from_near = flip(to_z, z_bit)
+    right2 = flip(right, w_bit)
     theirs = flip(mine, 1, "mp")
     share = assemble(own, mine, theirs, place, rows)
-
-    left3, share, right = barrier((left3, share, right))
-    right1, right2 = flip(right, z_bit), flip(right, w_bit)
 
     def low_sent(size):
         return [(2 * size, 3 * size), (6 * size, 7 * size)]
@@ -383,31 +384,31 @@
         ranges = [(0, 2 * size)], [(4 * size, 5 * size)], [(3 * size, 4 * size)]
         return [(r, jnp.float32) for r in ranges]
 
-    lefts = [message1, left1, left2, left3]
-    share, weight3a, weight3b = barrier((share, weight3a, weight3b))
+    from_near, right2, share = barrier((from_near, right2, share))
+    right3 = flip(right2, z_bit)
+    lefts = [(message1, 0), (left1, 0), (left2, 0), (from_near, 0)]
     left_to_x, left_to_y = products(share, [(lefts, split, sent(q), True)], steps)
     left_from_x, left_from_y = flip(left_to_x, x_bit), flip(left_to_y, y_bit)
-    right2, share, _ = barrier((right2, share, left_to_x))
-    right3 = flip(right2, z_bit)
-
-    weights = [down_weight, weight1, weight2, weight3a, weight3b]
-    to_z, to_w, *left_parts = products(
-        share, [(weights, units, sent(t), False), (lefts, split, kept(q), True)], steps
-    )
-    from_z, from_w = flip(to_z, z_bit), flip(to_w, w_bit)
-
-    right1, right3, left_from_x, left_from_y, share, _ = barrier(
-        (right1, right3, left_from_x, left_from_y, share, to_z)
-    )
-    rights = [right, right1, right2, right3]
+
+    share, _ = barrier((share, left_to_x))
+    weights = [(piece, 0) for piece in (down_weight, weight1, weight2, weight3a, weight3b)]
+    to_w, to_z = products(
+        share, [(weights, units, [(high_sent(t), jnp.bfloat16), (low_sent(t), jnp.bfloat16)], False)], steps
+    )
+    right3, share, to_w, to_z = barrier((right3, share, to_w, to_z))
+    from_w, from_z = flip(to_w, w_bit), flip(to_z, z_bit)
+    rights = [(right, 0), (from_near, split), (right2, 0), (right3, 0)]
     right_to_x, right_to_y = products(share, [(rights, units - split, sent(q), True)], steps)
     right_from_x, right_from_y = flip(right_to_x, x_bit), flip(right_to_y, y_bit)
-    share, _ = barrier((share, right_to_x))
+    share, left_from_x, left_from_y, _ = barrier((share, left_from_x, left_from_y, right_to_x))
+    left_parts = products(share, [(lefts, split, kept(q), True)], steps)
     parts = products(share, [(rights, units - split, kept(q), True), (weights, units, kept(t), False)], steps)
 
     grad_a = flip(add_tail([left_parts[1], parts[1]], [left_from_x, right_from_x]), y_bit)
     grad_b = flip(add_tail([left_parts[2], parts[2]], [left_from_y, right_from_y]), x_bit)
-    grad_a, grad_b, from_z, from_w = barrier((grad_a, grad_b, from_z, from_w))
+    to_w, to_z = add_tail([parts[4]], [from_z]), add_tail([parts[5]], [from_w])
+    last_a, last_b = flip(to_w, w_bit), flip(to_z, z_bit)
+    grad_a, grad_b, _, _ = barrier((grad_a, grad_b, to_w, to_z))
     grad, row_part = sum_up(
         [left_parts[0], parts[0]],
         [left_from_x, right_from_x],
@@ -417,12 +418,8 @@
         1.0 / math.sqrt(tokens * lax.axis_size("dp")),
     )
 
-    to_w, to_z = add_tail([parts[4]], [from_z]), add_tail([parts[5]], [from_w])
     row_sum = lax.psum(row_part, "mp")
-    row_sum, to_w, to_z = barrier((row_sum, to_w, to_z))
-    last_a, last_b = flip(to_w, w_bit), flip(to_z, z_bit)
-    arrived = jnp.concatenate([from_z[:t], from_w[:t]], axis=0)
-    return grad, row_sum, (parts[3], arrived, last_a, last_b)
+    return grad, row_sum, (parts[3], from_z[:t], from_w[:t], last_a, last_b)
 
 
 def local(out_grad, gate_pre, up_pre, down_weight, row_moment, col_moment):
@@ -435,11 +432,13 @@
     total_units = units * lax.axis_size("mp")
     staged = size == 16 and lax.axis_size("mp") == 2 and rows % 256 == 0 and tokens % 32 == 0 and units % 2560 == 0
     if staged:
-        grad, row_sum, (own_part, arrived, last_a, last_b) = staged_products(out_grad, gate_pre, up_pre, down_weight)
+        grad, row_sum, terms = staged_products(out_grad, gate_pre, up_pre, down_weight)
         row_moment_new, sums = column_sums(grad, row_sum, row_moment[None, :], decay, total_units)
         row_moment_new, sums = row_moment_new[0], group_sum(sums[0], all_bits[:INNER_BITS])
-        sums, last_a, last_b = lax.optimization_barrier((sums, last_a, last_b))
-        hidden_grad = own_part + arrived.astype(jnp.float32) + jnp.concatenate([last_a, last_b], axis=0).astype(jnp.float32)
+        sums, terms = lax.optimization_barrier((sums, terms))
+        own_part, from_low, from_high, last_a, last_b = terms
+        arrived = jnp.concatenate([from_low, from_high], axis=0).astype(jnp.float32)
+        hidden_grad = own_part + arrived + jnp.concatenate([last_a, last_b], axis=0).astype(jnp.float32)
     else:
         product, hidden_grad = general_products(
             out_grad, gate_pre, up_pre, down_weight, all_bits[:INNER_BITS], all_bits[INNER_BITS:]

time: 163 us -> 140 us (0.86)
  starting transfers between devices: 46.4 us -> 34.8 us
  waiting for transfers between devices: 71.5 us -> 64.1 us
  local copies, waits for them, and re-layouts: 9.43 us -> 6.04 us
    ppermute x28 -> x27, starting transfers between devices: 46.4 us -> 34.8 us  [flip(): return lax.ppermute(value, axis, [(i, i ^ bits) for i in range(size)])]
    ppermute x28 -> x27, waiting for transfers between devices: 71.5 us -> 64.1 us  [flip(): return lax.ppermute(value, axis, [(i, i ^ bits) for i in range(size)])]
    unnamed x36 -> x26, local copies, waits for them, and re-layouts: 6.92 us -> 3.53 us
    pallas_call x4 -> x5, Pallas kernels: 14.1 us -> 14 us  [products(): pl.pallas_call(kernel, grid=(steps,), out_shape=[jax.ShapeDtypeStruct((he...]
  transfers between devices with their start and end apart: 28 -> 27, of which waited for: 14 -> 13; matrix products, arithmetic and copies ran while one was open for 4% -> 4% of each run, Pallas kernels for 7% -> 13%
where the time goes in v13:
time: 140 us
  waiting for transfers between devices  64.1 us (46%)
  starting transfers between devices  34.8 us (25%)
  Pallas kernels  20.3 us (14%)
  other arithmetic  6.37 us (5%)
  local copies, waits for them, and re-layouts  6.04 us (4%)
  blocking collectives  4.94 us (4%)
  between operations  3.37 us (2%)
    ppermute x27, waiting for transfers between devices, flip(): return lax.ppermute(value, axis, [(i, i ^ bits) for i in range(size)])  64.1 us
    ppermute x27, starting transfers between devices, flip(): return lax.ppermute(value, axis, [(i, i ^ bits) for i in range(size)])  34.8 us
    pallas_call x5, Pallas kernels, products(): pl.pallas_call(kernel, grid=(steps,), out_shape=[jax.ShapeDtypeStruct((he...  14 us
    convert_element_type x1, other arithmetic, local(): up_grad = (hidden_grad * activated).astype(jnp.bfloat16)  3.81 us
    unnamed x26, local copies, waits for them, and re-layouts  3.53 us
  transfers between devices with their start and end apart: 27, of which 13 were waited for; matrix products, arithmetic and copies ran while one was open for 4% of the time, Pallas kernels for 13%

profile of v13, /device:TPU:0, one launch (start us, length us, event | category | flops | bytes accessed | tf_op | source)
XLA Modules:
  0.0 139.8 jit_solution(16968815695535605258)
XLA Ops:
  4.2 1.7 %shard_map.109 = (bf16[128,1024]{1,0:T(8,128)(2,1)S(1)}, bf16[128,1280]{1,0:T(8,128)(2,1)S(1)}, bf16[128,1792]{1,0:T(8,128)(2,1)S(1)}, bf16[128,1792]{1,0:T(8,128)(2,1)S(1)}, bf16[128,512]{1,0:T(8,128)(2,1)S(1)}) custom-call(s32[2]{0:T(128)S(1)} %pad_add_fusion.place, bf16[128,4096]{1,0:T(8,128)(2,1)S(1)} %copy-done.8, bf16[128,2560]{1,0:T(8,128)(2,1)S(1)} %copy-done.1, ...), custom_call_target="tpu_custom_call" | custom-call | tf_op jit(solution)/shard_map/pallas_call | solution.py:131
  5.9 3.0 %collective-permute-start.3 = (bf16[256,2560]{1,0:T(8,128)(2,1)S(1)}, bf16[256,2560]{1,0:T(8,128)(2,1)S(1)}, u32[]{:S(2)}, u32[]{:S(2)}) collective-permute-start(bf16[256,2560]{1,0:T(8,128)(2,1)S(1)} %copy-done), channel_id=1, source_target_pairs={{0,2},{2,0},{4,6},{6,4},{8,10},{10,8},{12,14},{14,12},{16,18},{18,... | collective-permute-start | bytes 3932168 | tf_op jit(solution)/shard_map/ppermute | solution.py:28
  12.0 2.6 %collective-permute-start.1 = (bf16[128,1792]{1,0:T(8,128)(2,1)S(1)}, bf16[128,1792]{1,0:T(8,128)(2,1)S(1)}, u32[]{:S(2)}, u32[]{:S(2)}) collective-permute-start(bf16[128,1792]{1,0:T(8,128)(2,1)S(1)} %get-tuple-element.64), channel_id=1, source_target_pairs={{0,16},{2,18},{4,20},{6,22},{8,24},{10,26},{12,28},{14,30},{16,0},... | collective-permute-start | bytes 1376264 | tf_op jit(solution)/shard_map/ppermute | solution.py:28
  14.9 22.1 %collective-permute-done.2.refs_2_ = bf16[128,512]{1,0:T(8,128)(2,1)S(1)} collective-permute-done((bf16[128,512]{1,0:T(8,128)(2,1)S(1)}, bf16[128,512]{1,0:T(8,128)(2,1)S(1)}, u32[]{:S(2)}, u32[]{:S(2)}) %collective-permute-start.2) | collective-permute-done | bytes 131104 | tf_op jit(solution)/shard_map/ppermute | solution.py:28
  41.4 2.6 %collective-permute-start.6 = (bf16[128,1280]{1,0:T(8,128)(2,1)S(1)}, bf16[128,1280]{1,0:T(8,128)(2,1)S(1)}, u32[]{:S(2)}, u32[]{:S(2)}) collective-permute-start(bf16[128,1280]{1,0:T(8,128)(2,1)S(1)} %get-tuple-element.76.refs_3_.refs_1_), channel_id=1, source_target_pairs={{0,16},{2,18},{4,20},{6,22},{8,24},{10,26},{12,28},{14,30},{16,0},... | collective-permute-start | bytes 983048 | tf_op jit(solution)/shard_map/ppermute | solution.py:28
  46.7 14.6 %collective-permute-done.6.refs_3_ = bf16[128,1280]{1,0:T(8,128)(2,1)S(1)} collective-permute-done((bf16[128,1280]{1,0:T(8,128)(2,1)S(1)}, bf16[128,1280]{1,0:T(8,128)(2,1)S(1)}, u32[]{:S(2)}, u32[]{:S(2)}) %collective-permute-start.6) | collective-permute-done | bytes 327712 | tf_op jit(solution)/shard_map/ppermute | solution.py:28
  62.2 2.6 %collective-permute-start.8 = (bf16[128,1280]{1,0:T(8,128)(2,1)S(1)}, bf16[128,1280]{1,0:T(8,128)(2,1)S(1)}, u32[]{:S(2)}, u32[]{:S(2)}) collective-permute-start(bf16[128,1280]{1,0:T(8,128)(2,1)S(1)} %collective-permute-done.6.refs_3_), channel_id=1, source_target_pairs={{0,8},{2,10},{4,12},{6,14},{8,0},{10,2},{12,4},{14,6},{16,24},{18,... | collective-permute-start | bytes 983048 | tf_op jit(solution)/shard_map/ppermute | solution.py:28
  64.7 2.0 %shard_map.113 = (bf16[256,1280]{1,0:T(8,128)(2,1)S(1)}, bf16[256,1280]{1,0:T(8,128)(2,1)S(1)}) custom-call(bf16[512,1024]{1,0:T(8,128)(2,1)S(1)} %shard_map.112.refs_0_, bf16[128,1792]{1,0:T(8,128)(2,1)S(1)} %get-tuple-element.63.refs_1_, bf16[128,1792]{1,0:T(8,128)(2,1)S(1)} %collective-permute-done.refs_0_.refs_2_, ...), custom_call_target="tpu_custom_call" | custom-call | tf_op jit(solution)/shard_map/pallas_call | solution.py:320
  69.0 2.8 %shard_map.114 = (bf16[128,2560]{1,0:T(8,128)(2,1)S(1)}, bf16[128,2560]{1,0:T(8,128)(2,1)S(1)}) custom-call(bf16[512,1024]{1,0:T(8,128)(2,1)S(1)} %shard_map.112.refs_0_, bf16[256,2560]{1,0:T(8,128)(2,1)S(1)} %copy-done, bf16[256,2560]{1,0:T(8,128)(2,1)S(1)} %collective-permute-done.3.refs_0_.refs_2_.refs_6_, ...), custom_call_target="tpu_custom_call" | custom-call | tf_op jit(solution)/shard_map/pallas_call | solution.py:320
  71.8 2.1 %shard_map.115 = (bf16[256,1280]{1,0:T(8,128)(2,1)S(1)}, bf16[256,1280]{1,0:T(8,128)(2,1)S(1)}) custom-call(bf16[512,1024]{1,0:T(8,128)(2,1)S(1)} %shard_map.112.refs_0_, bf16[128,1280]{1,0:T(8,128)(2,1)S(1)} %get-tuple-element.76.refs_3_.refs_1_, bf16[128,2560]{1,0:T(8,128)(2,1)S(1)} %collective-permute-done.5.refs_4_.refs_2_, ...), custom_call_target="tpu_custom_call" | custom-call | tf_op jit(solution)/shard_map/pallas_call | solution.py:320
  77.4 7.1 %collective-permute-done.11.refs_2_ = bf16[256,1280]{1,0:T(8,128)(2,1)S(1)} collective-permute-done((bf16[256,1280]{1,0:T(8,128)(2,1)S(1)}, bf16[256,1280]{1,0:T(8,128)(2,1)S(1)}, u32[]{:S(2)}, u32[]{:S(2)}) %collective-permute-start.11) | collective-permute-done | bytes 655392 | tf_op jit(solution)/shard_map/ppermute | solution.py:28
  85.1 2.1 %shard_map.116 = (f32[256,1280]{1,0:T(8,128)S(1)}, f32[128,1280]{1,0:T(8,128)S(1)}, f32[128,1280]{1,0:T(8,128)S(1)}) custom-call(bf16[512,1024]{1,0:T(8,128)(2,1)S(1)} %shard_map.112.refs_0_, bf16[128,1792]{1,0:T(8,128)(2,1)S(1)} %get-tuple-element.63.refs_1_, bf16[128,1792]{1,0:T(8,128)(2,1)S(1)} %collective-permute-done.refs_0_.refs_2_, ...), custom_call_target="tpu_custom_call" | custom-call | tf_op jit(solution)/shard_map/pallas_call | solution.py:320
  87.2 5.1 %shard_map.117 = (f32[256,1280]{1,0:T(8,128)S(1)}, f32[128,1280]{1,0:T(8,128)S(1)}, f32[128,1280]{1,0:T(8,128)S(1)}, f32[128,2560]{1,0:T(8,128)S(1)}, f32[64,2560]{1,0:T(8,128)S(1)}, /*index=5*/f32[64,2560]{1,0:T(8,128)S(1)}) custom-call(bf16[512,1024]{1,0:T(8,128)(2,1)S(1)} %shard_map.112.refs_0_, bf16[128,1280]{1,0:T(8,128)(2,1)S(1)} %get-tuple-element.76.refs_3_.refs_1_, ...), custom_call_target="tpu_custom_call" | custom-call | tf_op jit(solution)/shard_map/pallas_call | solution.py:320
  92.3 3.1 %collective-permute-done.14.refs_3_.refs_5_ = bf16[256,1280]{1,0:T(8,128)(2,1)S(1)} collective-permute-done((bf16[256,1280]{1,0:T(8,128)(2,1)S(1)}, bf16[256,1280]{1,0:T(8,128)(2,1)S(1)}, u32[]{:S(2)}, u32[]{:S(2)}) %collective-permute-start.14) | collective-permute-done | bytes 655392 | tf_op jit(solution)/shard_map/ppermute | solution.py:28
  98.9 4.9 %collective-permute-done.18.refs_1_ = bf16[128,2560]{1,0:T(8,128)(2,1)S(1)} collective-permute-done((bf16[128,2560]{1,0:T(8,128)(2,1)S(1)}, bf16[128,2560]{1,0:T(8,128)(2,1)S(1)}, u32[]{:S(2)}, u32[]{:S(2)}) %collective-permute-start.18) | collective-permute-done | bytes 655392 | tf_op jit(solution)/shard_map/ppermute | solution.py:28
  104.7 3.9 %collective-permute-done.17.refs_1_ = bf16[128,2560]{1,0:T(8,128)(2,1)S(1)} collective-permute-done((bf16[128,2560]{1,0:T(8,128)(2,1)S(1)}, bf16[128,2560]{1,0:T(8,128)(2,1)S(1)}, u32[]{:S(2)}, u32[]{:S(2)}) %collective-permute-start.17) | collective-permute-done | bytes 655392 | tf_op jit(solution)/shard_map/ppermute | solution.py:28
  110.5 2.5 %psum.14.row_sum = f32[1,256]{1,0:T(1,128)S(1)} all-reduce(f32[1,256]{1,0:T(1,128)S(1)} %get-tuple-element.108), channel_id=1, replica_groups=mesh['dp'=16,'mp'=2] {'mp'}, use_global_device_ids=true, to_apply=%region_0.0 | all-reduce | flops 256 | bytes 2048 | tf_op jit(solution)/shard_map/psum | solution.py:421
  119.2 1.8 %collective-permute-done.21 = f32[5248]{0:T(1024)S(1)} collective-permute-done((f32[5248]{0:T(1024)S(1)}, f32[5248]{0:T(1024)S(1)}, u32[]{:S(2)}, u32[]{:S(2)}) %collective-permute-start.21) | collective-permute-done | bytes 21024 | tf_op jit(solution)/shard_map/ppermute | solution.py:28
  121.1 2.6 %collective-permute-done.22 = bf16[64,2560]{1,0:T(8,128)(2,1)} collective-permute-done((bf16[64,2560]{1,0:T(8,128)(2,1)}, bf16[64,2560]{1,0:T(8,128)(2,1)}, u32[]{:S(2)}, u32[]{:S(2)}) %collective-permute-start.22) | collective-permute-done | bytes 327712 | tf_op jit(solution)/shard_map/ppermute | solution.py:28
  123.7 2.2 %collective-permute-start.25 = (f32[5248]{0:T(1024)S(1)}, f32[5248]{0:T(1024)S(1)}, u32[]{:S(2)}, u32[]{:S(2)}) collective-permute-start(f32[5248]{0:T(1024)S(1)} %add_add_fusion.1), channel_id=1, source_target_pairs={{0,16},{2,18},{4,20},{6,22},{8,24},{10,26},{12,28},{14,30},{16,0},... | collective-permute-start | bytes 62984 | tf_op jit(solution)/shard_map/ppermute | solution.py:28
  125.9 2.2 %collective-permute-start.26 = (f32[5248]{0:T(1024)S(1)}, f32[5248]{0:T(1024)S(1)}, u32[]{:S(2)}, u32[]{:S(2)}) collective-permute-start(f32[5248]{0:T(1024)S(1)} %add_add_fusion.1), channel_id=1, source_target_pairs={{0,24},{2,26},{4,28},{6,30},{8,16},{10,18},{12,20},{14,22},{16,8},... | collective-permute-start | bytes 62984 | tf_op jit(solution)/shard_map/ppermute | solution.py:28
  128.1 3.8 %fusion.8 = (bf16[128,2560]{1,0:T(8,128)(2,1)}, bf16[128,2560]{1,0:T(8,128)(2,1)}) fusion(bf16[128,2560]{1,0:T(8,128)(2,1)S(1)} %copy-done.2, bf16[64,2560]{1,0:T(8,128)(2,1)} %collective-permute-done.23, bf16[64,2560]{1,0:T(8,128)(2,1)} %collective-permute-done.22, f32[128,2560]{1,0:T(8,128)} %copy-done.7, bf16[64,2560]{1,0:T(8,128)(2,1)S(1)} %slice.21, ...), kind=kLoop, calls=%fused_computation.16 | loop fusion | flops 11468800 | bytes 5242880 | tf_op jit(solution)/shard_map/convert_element_type | solution.py:458
  132.5 2.5 %psum.15 = f32[128]{0:T(128)S(1)} all-reduce(f32[128]{0:T(128)S(1)} %get-tuple-element.118), channel_id=1, replica_groups=mesh['dp'=16,'mp'=2] {'mp'}, use_global_device_ids=true, to_apply=%region_2.0 | all-reduce | flops 128 | bytes 1024 | tf_op jit(solution)/shard_map/psum | solution.py:464
  136.9 1.8 %multiply_multiply_fusion = f32[256,2560]{1,0:T(8,128)} fusion(f32[256,2560]{1,0:T(8,128)S(1)} %get-tuple-element.107.grad, f32[2560]{0:T(1024)S(1)} %sqrt.15, f32[256]{0:T(256)S(1)} %sqrt_divide_fusion), kind=kLoop, calls=%fused_computation.7 | loop fusion | flops 1310720 | bytes 5254144 | tf_op jit(solution)/shard_map/mul | solution.py:468
  (86 shorter events, 35.0 us)
Async XLA Ops:
  5.9 31.8 %collective-permute-start.3 = (bf16[256,2560]{1,0:T(8,128)(2,1)S(1)}, bf16[256,2560]{1,0:T(8,128)(2,1)S(1)}, u32[]{:S(2)}, u32[]{:S(2)}) collective-permute-start(bf16[256,2560]{1,0:T(8,128)(2,1)S(1)} %copy-done), channel_id=1, source_target_pairs={{0,2},{2,0},{4,6},{6,4},{8,10},{10,8},{12,14},{14,12},{16,18},{18,... | collective-permute-start | bytes 3932168 | tf_op jit(solution)/shard_map/ppermute | solution.py:28
  8.9 30.2 %collective-permute-start.4 = (bf16[256,2560]{1,0:T(8,128)(2,1)S(1)}, bf16[256,2560]{1,0:T(8,128)(2,1)S(1)}, u32[]{:S(2)}, u32[]{:S(2)}) collective-permute-start(bf16[256,2560]{1,0:T(8,128)(2,1)S(1)} %copy-done), channel_id=1, source_target_pairs={{0,4},{2,6},{4,0},{6,2},{8,12},{10,14},{12,8},{14,10},{16,20},{18,... | collective-permute-start | bytes 3932168 | tf_op jit(solution)/shard_map/ppermute | solution.py:28
  10.5 29.2 %collective-permute-start = (bf16[128,1792]{1,0:T(8,128)(2,1)S(1)}, bf16[128,1792]{1,0:T(8,128)(2,1)S(1)}, u32[]{:S(2)}, u32[]{:S(2)}) collective-permute-start(bf16[128,1792]{1,0:T(8,128)(2,1)S(1)} %get-tuple-element.63.refs_1_), channel_id=1, source_target_pairs={{0,8},{2,10},{4,12},{6,14},{8,0},{10,2},{12,4},{14,6},{16,24},{18,... | collective-permute-start | bytes 1376264 | tf_op jit(solution)/shard_map/ppermute | solution.py:28
  12.0 27.6 %collective-permute-start.1 = (bf16[128,1792]{1,0:T(8,128)(2,1)S(1)}, bf16[128,1792]{1,0:T(8,128)(2,1)S(1)}, u32[]{:S(2)}, u32[]{:S(2)}) collective-permute-start(bf16[128,1792]{1,0:T(8,128)(2,1)S(1)} %get-tuple-element.64), channel_id=1, source_target_pairs={{0,16},{2,18},{4,20},{6,22},{8,24},{10,26},{12,28},{14,30},{16,0},... | collective-permute-start | bytes 1376264 | tf_op jit(solution)/shard_map/ppermute | solution.py:28
  14.6 22.3 %collective-permute-start.2 = (bf16[128,512]{1,0:T(8,128)(2,1)S(1)}, bf16[128,512]{1,0:T(8,128)(2,1)S(1)}, u32[]{:S(2)}, u32[]{:S(2)}) collective-permute-start(bf16[128,512]{1,0:T(8,128)(2,1)S(1)} %get-tuple-element.65), channel_id=1, source_target_pairs={{0,24},{2,26},{4,28},{6,30},{8,16},{10,18},{12,20},{14,22},{16,8},... | collective-permute-start | bytes 393224 | tf_op jit(solution)/shard_map/ppermute | solution.py:28
  39.8 22.4 %collective-permute-start.5 = (bf16[128,2560]{1,0:T(8,128)(2,1)S(1)}, bf16[128,2560]{1,0:T(8,128)(2,1)S(1)}, u32[]{:S(2)}, u32[]{:S(2)}) collective-permute-start(bf16[128,2560]{1,0:T(8,128)(2,1)S(1)} %get-tuple-element.77), channel_id=1, source_target_pairs={{0,8},{2,10},{4,12},{6,14},{8,0},{10,2},{12,4},{14,6},{16,24},{18,... | collective-permute-start | bytes 1966088 | tf_op jit(solution)/shard_map/ppermute | solution.py:28
  41.4 19.8 %collective-permute-start.6 = (bf16[128,1280]{1,0:T(8,128)(2,1)S(1)}, bf16[128,1280]{1,0:T(8,128)(2,1)S(1)}, u32[]{:S(2)}, u32[]{:S(2)}) collective-permute-start(bf16[128,1280]{1,0:T(8,128)(2,1)S(1)} %get-tuple-element.76.refs_3_.refs_1_), channel_id=1, source_target_pairs={{0,16},{2,18},{4,20},{6,22},{8,24},{10,26},{12,28},{14,30},{16,0},... | collective-permute-start | bytes 983048 | tf_op jit(solution)/shard_map/ppermute | solution.py:28
  44.0 25.0 %collective-permute-start.10 = (bf16[128,2560]{1,0:T(8,128)(2,1)S(1)}, bf16[128,2560]{1,0:T(8,128)(2,1)S(1)}, u32[]{:S(2)}, u32[]{:S(2)}) collective-permute-start(bf16[128,2560]{1,0:T(8,128)(2,1)S(1)} %get-tuple-element.72), channel_id=1, source_target_pairs={{0,2},{2,0},{4,6},{6,4},{8,10},{10,8},{12,14},{14,12},{16,18},{18,... | collective-permute-start | bytes 1966088 | tf_op jit(solution)/shard_map/ppermute | solution.py:28
  44.6 24.4 %collective-permute-start.9 = (bf16[128,2560]{1,0:T(8,128)(2,1)S(1)}, bf16[128,2560]{1,0:T(8,128)(2,1)S(1)}, u32[]{:S(2)}, u32[]{:S(2)}) collective-permute-start(bf16[128,2560]{1,0:T(8,128)(2,1)S(1)} %get-tuple-element.71), channel_id=1, source_target_pairs={{0,4},{2,6},{4,0},{6,2},{8,12},{10,14},{12,8},{14,10},{16,20},{18,... | collective-permute-start | bytes 1966088 | tf_op jit(solution)/shard_map/ppermute | solution.py:28
  62.2 9.6 %collective-permute-start.8 = (bf16[128,1280]{1,0:T(8,128)(2,1)S(1)}, bf16[128,1280]{1,0:T(8,128)(2,1)S(1)}, u32[]{:S(2)}, u32[]{:S(2)}) collective-permute-start(bf16[128,1280]{1,0:T(8,128)(2,1)S(1)} %collective-permute-done.6.refs_3_), channel_id=1, source_target_pairs={{0,8},{2,10},{4,12},{6,14},{8,0},{10,2},{12,4},{14,6},{16,24},{18,... | collective-permute-start | bytes 983048 | tf_op jit(solution)/shard_map/ppermute | solution.py:28
  66.8 17.7 %collective-permute-start.11 = (bf16[256,1280]{1,0:T(8,128)(2,1)S(1)}, bf16[256,1280]{1,0:T(8,128)(2,1)S(1)}, u32[]{:S(2)}, u32[]{:S(2)}) collective-permute-start(bf16[256,1280]{1,0:T(8,128)(2,1)S(1)} %get-tuple-element.83), channel_id=1, source_target_pairs={{0,2},{2,0},{4,6},{6,4},{8,10},{10,8},{12,14},{14,12},{16,18},{18,... | collective-permute-start | bytes 1966088 | tf_op jit(solution)/shard_map/ppermute | solution.py:28
  67.5 17.7 %collective-permute-start.12 = (bf16[256,1280]{1,0:T(8,128)(2,1)S(1)}, bf16[256,1280]{1,0:T(8,128)(2,1)S(1)}, u32[]{:S(2)}, u32[]{:S(2)}) collective-permute-start(bf16[256,1280]{1,0:T(8,128)(2,1)S(1)} %get-tuple-element.88), channel_id=1, source_target_pairs={{0,4},{2,6},{4,0},{6,2},{8,12},{10,14},{12,8},{14,10},{16,20},{18,... | collective-permute-start | bytes 1966088 | tf_op jit(solution)/shard_map/ppermute | solution.py:28
  73.8 21.5 %collective-permute-start.14 = (bf16[256,1280]{1,0:T(8,128)(2,1)S(1)}, bf16[256,1280]{1,0:T(8,128)(2,1)S(1)}, u32[]{:S(2)}, u32[]{:S(2)}) collective-permute-start(bf16[256,1280]{1,0:T(8,128)(2,1)S(1)} %get-tuple-element.96), channel_id=1, source_target_pairs={{0,4},{2,6},{4,0},{6,2},{8,12},{10,14},{12,8},{14,10},{16,20},{18,... | collective-permute-start | bytes 1966088 | tf_op jit(solution)/shard_map/ppermute | solution.py:28
  74.4 22.8 %collective-permute-start.13 = (bf16[256,1280]{1,0:T(8,128)(2,1)S(1)}, bf16[256,1280]{1,0:T(8,128)(2,1)S(1)}, u32[]{:S(2)}, u32[]{:S(2)}) collective-permute-start(bf16[256,1280]{1,0:T(8,128)(2,1)S(1)} %get-tuple-element.90), channel_id=1, source_target_pairs={{0,2},{2,0},{4,6},{6,4},{8,10},{10,8},{12,14},{14,12},{16,18},{18,... | collective-permute-start | bytes 1966088 | tf_op jit(solution)/shard_map/ppermute | solution.py:28
  75.9 28.0 %collective-permute-start.18 = (bf16[128,2560]{1,0:T(8,128)(2,1)S(1)}, bf16[128,2560]{1,0:T(8,128)(2,1)S(1)}, u32[]{:S(2)}, u32[]{:S(2)}) collective-permute-start(bf16[128,2560]{1,0:T(8,128)(2,1)S(1)} %get-tuple-element.104), channel_id=1, source_target_pairs={{0,16},{2,18},{4,20},{6,22},{8,24},{10,26},{12,28},{14,30},{16,0},... | collective-permute-start | bytes 1966088 | tf_op jit(solution)/shard_map/ppermute | solution.py:28
  84.5 24.1 %collective-permute-start.17 = (bf16[128,2560]{1,0:T(8,128)(2,1)S(1)}, bf16[128,2560]{1,0:T(8,128)(2,1)S(1)}, u32[]{:S(2)}, u32[]{:S(2)}) collective-permute-start(bf16[128,2560]{1,0:T(8,128)(2,1)S(1)} %get-tuple-element.102), channel_id=1, source_target_pairs={{0,8},{2,10},{4,12},{6,14},{8,0},{10,2},{12,4},{14,6},{16,24},{18,... | collective-permute-start | bytes 1966088 | tf_op jit(solution)/shard_map/ppermute | solution.py:28
  95.5 14.0 %collective-permute-start.16 = (bf16[128,2560]{1,0:T(8,128)(2,1)S(1)}, bf16[128,2560]{1,0:T(8,128)(2,1)S(1)}, u32[]{:S(2)}, u32[]{:S(2)}) collective-permute-start(bf16[128,2560]{1,0:T(8,128)(2,1)S(1)} %shard_map.119), channel_id=1, source_target_pairs={{0,2},{2,0},{4,6},{6,4},{8,10},{10,8},{12,14},{14,12},{16,18},{18,... | collective-permute-start | bytes 1966088 | tf_op jit(solution)/shard_map/ppermute | solution.py:28
  97.3 12.4 %collective-permute-start.15 = (bf16[128,2560]{1,0:T(8,128)(2,1)S(1)}, bf16[128,2560]{1,0:T(8,128)(2,1)S(1)}, u32[]{:S(2)}, u32[]{:S(2)}) collective-permute-start(bf16[128,2560]{1,0:T(8,128)(2,1)S(1)} %shard_map.118), channel_id=1, source_target_pairs={{0,4},{2,6},{4,0},{6,2},{8,12},{10,14},{12,8},{14,10},{16,20},{18,... | collective-permute-start | bytes 1966088 | tf_op jit(solution)/shard_map/ppermute | solution.py:28
  104.7 16.4 %collective-permute-start.23 = (bf16[64,2560]{1,0:T(8,128)(2,1)}, bf16[64,2560]{1,0:T(8,128)(2,1)}, u32[]{:S(2)}, u32[]{:S(2)}) collective-permute-start(bf16[64,2560]{1,0:T(8,128)(2,1)} %shard_map.121), channel_id=1, source_target_pairs={{0,8},{2,10},{4,12},{6,14},{8,0},{10,2},{12,4},{14,6},{16,24},{18,... | collective-permute-start | bytes 983048 | tf_op jit(solution)/shard_map/ppermute | solution.py:28
  109.5 14.2 %collective-permute-start.22 = (bf16[64,2560]{1,0:T(8,128)(2,1)}, bf16[64,2560]{1,0:T(8,128)(2,1)}, u32[]{:S(2)}, u32[]{:S(2)}) collective-permute-start(bf16[64,2560]{1,0:T(8,128)(2,1)} %shard_map.120), channel_id=1, source_target_pairs={{0,16},{2,18},{4,20},{6,22},{8,24},{10,26},{12,28},{14,30},{16,0},... | collective-permute-start | bytes 983048 | tf_op jit(solution)/shard_map/ppermute | solution.py:28
  113.7 5.6 %collective-permute-start.19 = (f32[5248]{0:T(1024)S(1)}, f32[5248]{0:T(1024)S(1)}, u32[]{:S(2)}, u32[]{:S(2)}) collective-permute-start(f32[5248]{0:T(1024)S(1)} %reduce), channel_id=1, source_target_pairs={{0,2},{2,0},{4,6},{6,4},{8,10},{10,8},{12,14},{14,12},{16,18},{18,... | collective-permute-start | bytes 62984 | tf_op jit(solution)/shard_map/ppermute | solution.py:28
  123.7 8.2 %collective-permute-start.24 = (f32[5248]{0:T(1024)S(1)}, f32[5248]{0:T(1024)S(1)}, u32[]{:S(2)}, u32[]{:S(2)}) collective-permute-start(f32[5248]{0:T(1024)S(1)} %add_add_fusion.1), channel_id=1, source_target_pairs={{0,8},{2,10},{4,12},{6,14},{8,0},{10,2},{12,4},{14,6},{16,24},{18,... | collective-permute-start | bytes 62984 | tf_op jit(solution)/shard_map/ppermute | solution.py:28
  123.7 8.2 %collective-permute-start.25 = (f32[5248]{0:T(1024)S(1)}, f32[5248]{0:T(1024)S(1)}, u32[]{:S(2)}, u32[]{:S(2)}) collective-permute-start(f32[5248]{0:T(1024)S(1)} %add_add_fusion.1), channel_id=1, source_target_pairs={{0,16},{2,18},{4,20},{6,22},{8,24},{10,26},{12,28},{14,30},{16,0},... | collective-permute-start | bytes 62984 | tf_op jit(solution)/shard_map/ppermute | solution.py:28
  125.9 6.0 %collective-permute-start.26 = (f32[5248]{0:T(1024)S(1)}, f32[5248]{0:T(1024)S(1)}, u32[]{:S(2)}, u32[]{:S(2)}) collective-permute-start(f32[5248]{0:T(1024)S(1)} %add_add_fusion.1), channel_id=1, source_target_pairs={{0,24},{2,26},{4,28},{6,30},{8,16},{10,18},{12,20},{14,22},{16,8},... | collective-permute-start | bytes 62984 | tf_op jit(solution)/shard_map/ppermute | solution.py:28
  (16 other events, 93.7 us)

commit v14 on v13

--- a/solution.py
+++ b/solution.py
@@ -95,51 +95,32 @@
     half = units // 2
     step = 32
 
-    def kernel(place, source_hbm, gate_hbm, up_hbm, own, right, message1, message2, message3, source, gate, up, sems):
-        copies = [
-            pltpu.make_async_copy(there, here, sems.at[n])
-            for n, (there, here) in enumerate(((gate_hbm, gate), (up_hbm, up), (source_hbm, source)))
-        ]
-        for copy in copies:
-            copy.start()
+    def kernel(place, source, gate, up, own, right, message1, message2, message3):
         me, core = place[0], place[1]
 
         def block(k, j):
             return pl.ds(pl.multiple_of((me ^ (4 * k + j)) * rows, rows), rows)
 
-        copies[0].wait()
-        copies[1].wait()
-
-        @pl.loop(0, tokens // step)
-        def _(i):
-            here = pl.ds(pl.multiple_of(i * step, step), step)
-            activated, _ = gelu_parts(gate[here, :].astype(jnp.float32))
-            value = (activated * up[here, :].astype(jnp.float32)).astype(jnp.bfloat16)
-            right[here, :] = value[:, half:]
-            message1[here, :half] = value[:, :half]
-            message2[here, :half] = value[:, :half]
-
-        copies[2].wait()
+        activated, _ = gelu_parts(gate[...].astype(jnp.float32))
+        value = (activated * up[...].astype(jnp.float32)).astype(jnp.bfloat16)
+        right[...] = value[:, half:]
+        message1[:, :half] = value[:, :half]
+        message2[:, :half] = value[:, :half]
         for j in range(4):
             own[:, j * rows : (j + 1) * rows] = source[:, block(0, j)]
         for k, target, base in ((1, message1, half), (2, message2, half), (3, message3, 0)):
             for j in range(2):
                 target[:, base + j * rows : base + (j + 1) * rows] = source[:, block(k, 2 * core + j)]
 
-    vmem = pl.BlockSpec(memory_space=pltpu.VMEM)
     widths = [4 * rows, units - half, half + 2 * rows, half + 2 * rows, 2 * rows]
     return pl.pallas_call(
         kernel,
+        grid=(tokens // step,),
         out_shape=[jax.ShapeDtypeStruct((tokens, width), jnp.bfloat16) for width in widths],
-        in_specs=[pl.BlockSpec(memory_space=pltpu.SMEM)] + [pl.BlockSpec(memory_space=pltpu.HBM)] * 3,
-        out_specs=[vmem] * len(widths),
-        scratch_shapes=[
-            pltpu.VMEM(out_grad.shape, jnp.bfloat16),
-            pltpu.VMEM(gate_pre.shape, jnp.bfloat16),
-            pltpu.VMEM(up_pre.shape, jnp.bfloat16),
-            pltpu.SemaphoreType.DMA((3,)),
-        ],
-        compiler_params=pltpu.CompilerParams(vmem_limit_bytes=16 << 20),
+        in_specs=[pl.BlockSpec(memory_space=pltpu.SMEM)]
+        + [pl.BlockSpec((step, array.shape[1]), lambda i: (i, 0)) for array in (out_grad, gate_pre, up_pre)],
+        out_specs=[pl.BlockSpec((step, width), lambda i: (i, 0)) for width in widths],
+        compiler_params=pltpu.CompilerParams(vmem_limit_bytes=56 << 20),
         cost_estimate=EAGER,
     )(place, out_grad, gate_pre, up_pre)
 
@@ -286,6 +267,64 @@
         compiler_params=pltpu.CompilerParams(vmem_limit_bytes=14 << 20),
         cost_estimate=EAGER,
     )(grad, row_sum, row_moment)
+
+
+def column_step(sums, col_moment, decay, total_rows):
+    units = col_moment.shape[1]
+
+    def kernel(sums, col_moment, col_moment_new, terms):
+        total = jnp.zeros((1, 128), jnp.float32)
+        for at in range(0, units, 128):
+            here = slice(at, at + 128)
+            new = decay * col_moment[:, here] + (1.0 - decay) * (sums[:, here] / total_rows)
+            col_moment_new[:, here] = new
+            total = total + sums[:, units + at : units + at + 128] / new
+        terms[...] = total
+
+    vmem = pl.BlockSpec(memory_space=pltpu.VMEM)
+    return pl.pallas_call(
+        kernel,
+        out_shape=[jax.ShapeDtypeStruct((1, units), jnp.float32), jax.ShapeDtypeStruct((1, 128), jnp.float32)],
+        in_specs=[vmem] * 2,
+        out_specs=[vmem] * 2,
+        compiler_params=pltpu.CompilerParams(vmem_limit_bytes=4 << 20),
+        cost_estimate=EAGER,
+    )(sums, col_moment)
+
+
+def final_update(grad, row_moment_new, col_moment_new, terms, sums, total_rows, total_units):
+    rows, units = grad.shape
+    tile = units // 5
+
+    def kernel(grad, row_moment_new, col_moment_new, terms, row_total, update, row_mean):
+        mean = row_total[...] / total_rows
+        row_mean[...] = mean
+        square_sum = mean[:, 0:1] * jnp.sum(terms[...], axis=1, keepdims=True)
+        clip = jnp.maximum(1.0, jnp.sqrt(square_sum / (total_rows * total_units)))
+        col_factor = 1.0 / jnp.sqrt(col_moment_new[...])
+        for at in range(0, rows, 128):
+            here = slice(at, at + 128)
+            row_factor = jnp.sqrt(mean / row_moment_new[:, here]) / clip
+            update[here, :] = grad[here, :] * upright(row_factor) * col_factor
+
+    def fixed(width, block=0):
+        return pl.BlockSpec((1, width), lambda i: (0, block))
+
+    return pl.pallas_call(
+        kernel,
+        grid=(units // tile,),
+        out_shape=[jax.ShapeDtypeStruct((rows, units), jnp.float32), jax.ShapeDtypeStruct((1, 128), jnp.float32)],
+        in_specs=[
+            pl.BlockSpec((rows, tile), lambda i: (0, i)),
+            fixed(rows),
+            pl.BlockSpec((1, tile), lambda i: (0, i)),
+            fixed(128),
+            fixed(128, 2 * units // 128),
+        ],
+        out_specs=[pl.BlockSpec((rows, tile), lambda i: (0, i)), fixed(128)],
+        compiler_params=pltpu.CompilerParams(vmem_limit_bytes=14 << 20),
+        cost_estimate=EAGER,
+    )(grad, row_moment_new, col_moment_new, terms, sums)
 
 
 def products(share, groups, steps):
@@ -356,17 +395,16 @@
     weight3a, weight3b = flip(to_y, y_bit), flip(to_x, x_bit)
     left1, left2, message3, right, _, _ = barrier((left1, left2, message3, right, to_y, to_x))
     to_z, mine = cut(
-        [left1, left2, message3, right],
+        [left1, left2, message3],
         [
             (1, every, (0, split), 0, 0),
-            (3, every, (0, units - split), 0, split),
             (0, every, extra, 1, 0),
             (1, every, extra, 1, 2 * rows),
             (2, every, (0, 2 * rows), 1, 4 * rows),
         ],
-        [(tokens, units), (tokens, 6 * rows)],
-    )
-    from_near = flip(to_z, z_bit)
+        [(tokens, split), (tokens, 6 * rows)],
+    )
+    left3 = flip(to_z, z_bit)
     right2 = flip(right, w_bit)
     theirs = flip(mine, 1, "mp")
     share = assemble(own, mine, theirs, place, rows)
@@ -384,9 +422,14 @@
         ranges = [(0, 2 * size)], [(4 * size, 5 * size)], [(3 * size, 4 * size)]
         return [(r, jnp.float32) for r in ranges]
 
-    from_near, right2, share = barrier((from_near, right2, share))
-    right3 = flip(right2, z_bit)
-    lefts = [(message1, 0), (left1, 0), (left2, 0), (from_near, 0)]
+    left3, right2, share = barrier((left3, right2, share))
+    (to_z,) = cut(
+        [right2, right],
+        [(0, every, (0, units - split), 0, 0), (1, every, (0, units - split), 0, units - split)],
+        [(tokens, 2 * (units - split))],
+    )
+    from_near = flip(to_z, z_bit)
+    lefts = [(message1, 0), (left1, 0), (left2, 0), (left3, 0)]
     left_to_x, left_to_y = products(share, [(lefts, split, sent(q), True)], steps)
     left_from_x, left_from_y = flip(left_to_x, x_bit), flip(left_to_y, y_bit)
 
@@ -395,9 +438,9 @@
     to_w, to_z = products(
         share, [(weights, units, [(high_sent(t), jnp.bfloat16), (low_sent(t), jnp.bfloat16)], False)], steps
     )
-    right3, share, to_w, to_z = barrier((right3, share, to_w, to_z))
+    from_near, share, to_w, to_z = barrier((from_near, share, to_w, to_z))
     from_w, from_z = flip(to_w, w_bit), flip(to_z, z_bit)
-    rights = [(right, 0), (from_near, split), (right2, 0), (right3, 0)]
+    rights = [(right, 0), (from_near, units - split), (right2, 0), (from_near, 0)]
     right_to_x, right_to_y = products(share, [(rights, units - split, sent(q), True)], steps)
     right_from_x, right_from_y = flip(right_to_x, x_bit), flip(right_to_y, y_bit)
     share, left_from_x, left_from_y, _ = barrier((share, left_from_x, left_from_y, right_to_x))
@@ -434,11 +477,16 @@
     if staged:
         grad, row_sum, terms = staged_products(out_grad, gate_pre, up_pre, down_weight)
         row_moment_new, sums = column_sums(grad, row_sum, row_moment[None, :], decay, total_units)
-        row_moment_new, sums = row_moment_new[0], group_sum(sums[0], all_bits[:INNER_BITS])
+        sums = group_sum(sums[0], all_bits[:INNER_BITS])
         sums, terms = lax.optimization_barrier((sums, terms))
         own_part, from_low, from_high, last_a, last_b = terms
         arrived = jnp.concatenate([from_low, from_high], axis=0).astype(jnp.float32)
         hidden_grad = own_part + arrived + jnp.concatenate([last_a, last_b], axis=0).astype(jnp.float32)
+        sums = group_sum(sums, all_bits[INNER_BITS:])[None, :]
+        col_moment_new, ratios = column_step(sums, col_moment[None, :], decay, total_rows)
+        ratios = lax.psum(ratios, "mp")
+        update, row_mean = final_update(grad, row_moment_new, col_moment_new, ratios, sums, total_rows, total_units)
+        row_moment_new, col_moment_new, row_mean = row_moment_new[0], col_moment_new[0], row_mean[0, 0]
     else:
         product, hidden_grad = general_products(
             out_grad, gate_pre, up_pre, down_weight, all_bits[:INNER_BITS], all_bits[INNER_BITS:]
@@ -451,21 +499,18 @@
         col_part = jnp.sum(squares, axis=0)
         scaled_part = jnp.sum(powers / row_moment_new[:, None], axis=0)
         sums = jnp.concatenate([col_part, scaled_part, jnp.broadcast_to(jnp.sum(row_moment_new), (128,))])
-        sums = group_sum(sums, all_bits[:INNER_BITS])
+        sums = group_sum(sums, all_bits)
+        col_moment_new = decay * col_moment + (1.0 - decay) * (sums[:units] / total_rows)
+        row_mean = sums[2 * units] / total_rows
+        ratios = lax.psum(jnp.sum(sums[units : 2 * units] / col_moment_new), "mp")
+        clip_norm = jnp.sqrt(row_mean * ratios / (total_rows * total_units))
+        row_factor = jnp.sqrt(row_mean / row_moment_new) / jnp.maximum(1.0, clip_norm)
+        col_factor = 1.0 / jnp.sqrt(col_moment_new)
+        update = grad * row_factor[:, None] * col_factor[None, :]
 
     activated, derivative = gelu_parts(gate_pre.astype(jnp.float32))
     gate_grad = (hidden_grad * up_pre.astype(jnp.float32) * derivative).astype(jnp.bfloat16)
     up_grad = (hidden_grad * activated).astype(jnp.bfloat16)
-
-    sums = group_sum(sums, all_bits[INNER_BITS:])
-    col_moment_new = decay * col_moment + (1.0 - decay) * (sums[:units] / total_rows)
-    row_mean = sums[2 * units] / total_rows
-    ratios = jnp.sum((sums[units : 2 * units] / col_moment_new).reshape(-1, 128), axis=0)
-    square_sum = row_mean * jnp.sum(lax.psum(ratios, "mp"))
-    clip_norm = jnp.sqrt(square_sum / (total_rows * total_units))
-    row_factor = jnp.sqrt(row_mean / row_moment_new) / jnp.maximum(1.0, clip_norm)
-    col_factor = 1.0 / jnp.sqrt(col_moment_new)
-    update = grad * row_factor[:, None] * col_factor[None, :]
     return (update, row_moment_new, col_moment_new, row_mean, gate_grad, up_grad)
 
 

time: 140 us -> 144 us (1.029)
  Pallas kernels: 20.3 us -> 26.3 us
  local copies, waits for them, and re-layouts: 6.04 us -> 0.11 us
  starting transfers between devices: 34.8 us -> 39.3 us
  waiting for transfers between devices: 64.1 us -> 66.7 us
  between operations: 3.37 us -> 0.88 us
    pallas_call x1 -> x3, Pallas kernels: 1.72 us -> 7.76 us  [the longest x1 3.89 us: final_update(): pl.pallas_call(kernel, grid=(units // tile,), out_shape=[jax.ShapeDtypeSt...]
    ppermute x27, starting transfers between devices: 34.8 us -> 39.3 us  [flip(): return lax.ppermute(value, axis, [(i, i ^ bits) for i in range(size)])]
    unnamed x26 -> x22, local copies, waits for them, and re-layouts: 3.53 us -> 0.05 us
    ppermute x27, waiting for transfers between devices: 64.1 us -> 66.7 us  [flip(): return lax.ppermute(value, axis, [(i, i ^ bits) for i in range(size)])]
    slice x2 -> x3, local copies, waits for them, and re-layouts: 1.99 us -> 0.03 us  [staged_products(): return (grad, row_sum, (parts[3], from_z[:t], from_w[:t], last_a, last_b))]
    mul x1 -> x0, other arithmetic: 1.78 us -> none  [local(): update = grad * row_factor[:, None] * col_factor[None, :]]
  transfers between devices with their start and end apart: 27 -> 27, of which waited for: 13 -> 13; matrix products, arithmetic and copies ran while one was open for 4% -> 3% of each run, Pallas kernels for 13% -> 13%
where the time goes in v14:
time: 144 us; the launch traced here: 143 us
  waiting for transfers between devices  66.7 us (46%)
  starting transfers between devices  39.3 us (27%)
  Pallas kernels  26.3 us (18%)
  other arithmetic  5.24 us (4%)
  blocking collectives  4.95 us (3%)
    ppermute x27, waiting for transfers between devices, flip(): return lax.ppermute(value, axis, [(i, i ^ bits) for i in range(size)])  66.7 us
    ppermute x27, starting transfers between devices, flip(): return lax.ppermute(value, axis, [(i, i ^ bits) for i in range(size)])  39.3 us
    pallas_call x5, Pallas kernels, products(): pl.pallas_call(kernel, grid=(steps,), out_shape=[jax.ShapeDtypeStruct((he...  14 us
    convert_element_type x1, other arithmetic, local(): up_grad = (hidden_grad * activated).astype(jnp.bfloat16)  3.96 us
    pallas_call x1, Pallas kernels, final_update(): pl.pallas_call(kernel, grid=(units // tile,), out_shape=[jax.ShapeDtypeSt...  3.89 us
    pallas_call x1, Pallas kernels, first_stage(): pl.pallas_call(kernel, grid=(tokens // step,), out_shape=[jax.ShapeDtypeS...  3.84 us
  transfers between devices with their start and end apart: 27, of which 13 were waited for; matrix products, arithmetic and copies ran while one was open for 3% of the time, Pallas kernels for 13%

profile of v14, /device:TPU:0, one launch (start us, length us, event | category | flops | bytes accessed | tf_op | source)
XLA Modules:
  0.0 143.4 jit_solution(9445851515505712865)
XLA Ops:
  1.2 3.8 %shard_map.109 = (bf16[128,1024]{1,0:T(8,128)(2,1)}, bf16[128,1280]{1,0:T(8,128)(2,1)}, bf16[128,1792]{1,0:T(8,128)(2,1)}, bf16[128,1792]{1,0:T(8,128)(2,1)}, bf16[128,512]{1,0:T(8,128)(2,1)}) custom-call(s32[2]{0:T(128)} %pad_add_fusion.place, bf16[128,4096]{1,0:T(8,128)(2,1)} %source.1, bf16[128,2560]{1,0:T(8,128)(2,1)} %gate.1, bf16[128,2560]{1,0:T(8,128)(2,1)} %up.1), custom_call_target="tpu_custom_call" | custom-call | tf_op jit(solution)/shard_map/pallas_call | solution.py:116
  5.1 3.0 %collective-permute-start.3 = (bf16[256,2560]{1,0:T(8,128)(2,1)S(1)}, bf16[256,2560]{1,0:T(8,128)(2,1)S(1)}, u32[]{:S(2)}, u32[]{:S(2)}) collective-permute-start(bf16[256,2560]{1,0:T(8,128)(2,1)S(1)} %copy-done), channel_id=1, source_target_pairs={{0,2},{2,0},{4,6},{6,4},{8,10},{10,8},{12,14},{14,12},{16,18},{18,... | collective-permute-start | bytes 3932168 | tf_op jit(solution)/shard_map/ppermute | solution.py:28
  11.2 2.6 %collective-permute-start.1 = (bf16[128,1792]{1,0:T(8,128)(2,1)}, bf16[128,1792]{1,0:T(8,128)(2,1)S(1)}, u32[]{:S(2)}, u32[]{:S(2)}) collective-permute-start(bf16[128,1792]{1,0:T(8,128)(2,1)} %get-tuple-element.68), channel_id=1, source_target_pairs={{0,16},{2,18},{4,20},{6,22},{8,24},{10,26},{12,28},{14,30},{16,0},... | collective-permute-start | bytes 1376264 | tf_op jit(solution)/shard_map/ppermute | solution.py:28
  14.0 22.3 %collective-permute-done.2.refs_2_ = bf16[128,512]{1,0:T(8,128)(2,1)S(1)} collective-permute-done((bf16[128,512]{1,0:T(8,128)(2,1)}, bf16[128,512]{1,0:T(8,128)(2,1)S(1)}, u32[]{:S(2)}, u32[]{:S(2)}) %collective-permute-start.2) | collective-permute-done | bytes 131104 | tf_op jit(solution)/shard_map/ppermute | solution.py:28
  40.6 2.6 %collective-permute-start.6 = (bf16[128,1280]{1,0:T(8,128)(2,1)S(1)}, bf16[128,1280]{1,0:T(8,128)(2,1)S(1)}, u32[]{:S(2)}, u32[]{:S(2)}) collective-permute-start(bf16[128,1280]{1,0:T(8,128)(2,1)S(1)} %copy-done.1), channel_id=1, source_target_pairs={{0,16},{2,18},{4,20},{6,22},{8,24},{10,26},{12,28},{14,30},{16,0},... | collective-permute-start | bytes 983048 | tf_op jit(solution)/shard_map/ppermute | solution.py:28
  45.9 10.1 %collective-permute-done.5.refs_4_ = bf16[128,1280]{1,0:T(8,128)(2,1)S(1)} collective-permute-done((bf16[128,1280]{1,0:T(8,128)(2,1)S(1)}, bf16[128,1280]{1,0:T(8,128)(2,1)S(1)}, u32[]{:S(2)}, u32[]{:S(2)}) %collective-permute-start.5) | collective-permute-done | bytes 327712 | tf_op jit(solution)/shard_map/ppermute | solution.py:28
  56.0 2.4 %collective-permute-done.6.refs_0_.refs_3_ = bf16[128,1280]{1,0:T(8,128)(2,1)S(1)} collective-permute-done((bf16[128,1280]{1,0:T(8,128)(2,1)S(1)}, bf16[128,1280]{1,0:T(8,128)(2,1)S(1)}, u32[]{:S(2)}, u32[]{:S(2)}) %collective-permute-start.6) | collective-permute-done | bytes 327712 | tf_op jit(solution)/shard_map/ppermute | solution.py:28
  59.0 2.0 %shard_map.114 = (bf16[256,1280]{1,0:T(8,128)(2,1)S(1)}, bf16[256,1280]{1,0:T(8,128)(2,1)S(1)}) custom-call(bf16[512,1024]{1,0:T(8,128)(2,1)S(1)} %shard_map.112.refs_0_, bf16[128,1792]{1,0:T(8,128)(2,1)S(1)} %copy-done.2, bf16[128,1792]{1,0:T(8,128)(2,1)S(1)} %collective-permute-done.refs_0_.refs_2_, ...), custom_call_target="tpu_custom_call" | custom-call | tf_op jit(solution)/shard_map/pallas_call | solution.py:359
  63.1 2.8 %shard_map.115 = (bf16[128,2560]{1,0:T(8,128)(2,1)S(1)}, bf16[128,2560]{1,0:T(8,128)(2,1)S(1)}) custom-call(bf16[512,1024]{1,0:T(8,128)(2,1)S(1)} %shard_map.112.refs_0_, bf16[256,2560]{1,0:T(8,128)(2,1)S(1)} %copy-done, bf16[256,2560]{1,0:T(8,128)(2,1)S(1)} %collective-permute-done.3.refs_0_.refs_2_.refs_6_, ...), custom_call_target="tpu_custom_call" | custom-call | tf_op jit(solution)/shard_map/pallas_call | solution.py:359
  65.9 7.6 %collective-permute-done.8.refs_2_.refs_4_ = bf16[128,2560]{1,0:T(8,128)(2,1)S(1)} collective-permute-done((bf16[128,2560]{1,0:T(8,128)(2,1)S(1)}, bf16[128,2560]{1,0:T(8,128)(2,1)S(1)}, u32[]{:S(2)}, u32[]{:S(2)}) %collective-permute-start.8) | collective-permute-done | bytes 655392 | tf_op jit(solution)/shard_map/ppermute | solution.py:28
  73.5 2.1 %shard_map.116 = (bf16[256,1280]{1,0:T(8,128)(2,1)S(1)}, bf16[256,1280]{1,0:T(8,128)(2,1)S(1)}) custom-call(bf16[512,1024]{1,0:T(8,128)(2,1)S(1)} %shard_map.112.refs_0_, bf16[128,1280]{1,0:T(8,128)(2,1)S(1)} %copy-done.1, bf16[128,2560]{1,0:T(8,128)(2,1)S(1)} %collective-permute-done.8.refs_2_.refs_4_, ...), custom_call_target="tpu_custom_call" | custom-call | tf_op jit(solution)/shard_map/pallas_call | solution.py:359
  77.6 2.3 %collective-permute-start.18 = (bf16[128,2560]{1,0:T(8,128)(2,1)S(1)}, bf16[128,2560]{1,0:T(8,128)(2,1)S(1)}, u32[]{:S(2)}, u32[]{:S(2)}) collective-permute-start(bf16[128,2560]{1,0:T(8,128)(2,1)S(1)} %get-tuple-element.108), channel_id=1, source_target_pairs={{0,16},{2,18},{4,20},{6,22},{8,24},{10,26},{12,28},{14,30},{16,0},... | collective-permute-start | bytes 1966088 | tf_op jit(solution)/shard_map/ppermute | solution.py:28
  81.7 2.1 %shard_map.117 = (f32[256,1280]{1,0:T(8,128)S(1)}, f32[128,1280]{1,0:T(8,128)S(1)}, f32[128,1280]{1,0:T(8,128)S(1)}) custom-call(bf16[512,1024]{1,0:T(8,128)(2,1)S(1)} %shard_map.112.refs_0_, bf16[128,1792]{1,0:T(8,128)(2,1)S(1)} %copy-done.2, bf16[128,1792]{1,0:T(8,128)(2,1)S(1)} %collective-permute-done.refs_0_.refs_2_, ...), custom_call_target="tpu_custom_call" | custom-call | tf_op jit(solution)/shard_map/pallas_call | solution.py:359
  83.8 5.1 %shard_map.118 = (f32[256,1280]{1,0:T(8,128)S(1)}, f32[128,1280]{1,0:T(8,128)S(1)}, f32[128,1280]{1,0:T(8,128)S(1)}, f32[128,2560]{1,0:T(8,128)S(1)}, f32[64,2560]{1,0:T(8,128)S(1)}, /*index=5*/f32[64,2560]{1,0:T(8,128)S(1)}) custom-call(bf16[512,1024]{1,0:T(8,128)(2,1)S(1)} %shard_map.112.refs_0_, bf16[128,1280]{1,0:T(8,128)(2,1)S(1)} %copy-done.1, ...), custom_call_target="tpu_custom_call" | custom-call | tf_op jit(solution)/shard_map/pallas_call | solution.py:359
  88.9 2.4 %collective-permute-done.14.refs_3_.refs_5_ = bf16[256,1280]{1,0:T(8,128)(2,1)S(1)} collective-permute-done((bf16[256,1280]{1,0:T(8,128)(2,1)S(1)}, bf16[256,1280]{1,0:T(8,128)(2,1)S(1)}, u32[]{:S(2)}, u32[]{:S(2)}) %collective-permute-start.14) | collective-permute-done | bytes 655392 | tf_op jit(solution)/shard_map/ppermute | solution.py:28
  94.7 12.3 %collective-permute-done.18.refs_1_ = bf16[128,2560]{1,0:T(8,128)(2,1)S(1)} collective-permute-done((bf16[128,2560]{1,0:T(8,128)(2,1)S(1)}, bf16[128,2560]{1,0:T(8,128)(2,1)S(1)}, u32[]{:S(2)}, u32[]{:S(2)}) %collective-permute-start.18) | collective-permute-done | bytes 655392 | tf_op jit(solution)/shard_map/ppermute | solution.py:28
  109.4 3.4 %collective-permute-start.22 = (bf16[64,2560]{1,0:T(8,128)(2,1)}, bf16[64,2560]{1,0:T(8,128)(2,1)}, u32[]{:S(2)}, u32[]{:S(2)}) collective-permute-start(bf16[64,2560]{1,0:T(8,128)(2,1)} %shard_map.121), channel_id=1, source_target_pairs={{0,16},{2,18},{4,20},{6,22},{8,24},{10,26},{12,28},{14,30},{16,0},... | collective-permute-start | bytes 983048 | tf_op jit(solution)/shard_map/ppermute | solution.py:28
  113.6 2.5 %psum.14.row_sum = f32[1,256]{1,0:T(1,128)S(1)} all-reduce(f32[1,256]{1,0:T(1,128)S(1)} %get-tuple-element.112), channel_id=1, replica_groups=mesh['dp'=16,'mp'=2] {'mp'}, use_global_device_ids=true, to_apply=%region_0.0 | all-reduce | flops 256 | bytes 2048 | tf_op jit(solution)/shard_map/psum | solution.py:464
  120.7 1.8 %collective-permute-done.20 = f32[5248]{0:T(1024)S(1)} collective-permute-done((f32[5248]{0:T(1024)S(1)}, f32[5248]{0:T(1024)S(1)}, u32[]{:S(2)}, u32[]{:S(2)}) %collective-permute-start.20) | collective-permute-done | bytes 21024 | tf_op jit(solution)/shard_map/ppermute | solution.py:28
  123.6 4.1 %collective-permute-done.22 = bf16[64,2560]{1,0:T(8,128)(2,1)} collective-permute-done((bf16[64,2560]{1,0:T(8,128)(2,1)}, bf16[64,2560]{1,0:T(8,128)(2,1)}, u32[]{:S(2)}, u32[]{:S(2)}) %collective-permute-start.22) | collective-permute-done | bytes 327712 | tf_op jit(solution)/shard_map/ppermute | solution.py:28
  127.8 2.9 %collective-permute-start.25 = (f32[5248]{0:T(1024)S(1)}, f32[5248]{0:T(1024)S(1)}, u32[]{:S(2)}, u32[]{:S(2)}) collective-permute-start(f32[5248]{0:T(1024)S(1)} %add_add_fusion.1), channel_id=1, source_target_pairs={{0,16},{2,18},{4,20},{6,22},{8,24},{10,26},{12,28},{14,30},{16,0},... | collective-permute-start | bytes 62984 | tf_op jit(solution)/shard_map/ppermute | solution.py:28
  132.2 4.0 %fusion.8 = (bf16[128,2560]{1,0:T(8,128)(2,1)}, bf16[128,2560]{1,0:T(8,128)(2,1)}) fusion(bf16[128,2560]{1,0:T(8,128)(2,1)S(1)} %copy-done.9, bf16[64,2560]{1,0:T(8,128)(2,1)} %collective-permute-done.23, bf16[64,2560]{1,0:T(8,128)(2,1)} %collective-permute-done.22, f32[128,2560]{1,0:T(8,128)} %copy-done.4, bf16[64,2560]{1,0:T(8,128)(2,1)S(1)} %slice.13, ...), kind=kLoop, calls=%fused_computation.15 | loop fusion | flops 11468800 | bytes 5242880 | tf_op jit(solution)/shard_map/convert_element_type | solution.py:513
  136.4 2.5 %psum.15.terms = f32[1,128]{1,0:T(1,128)S(1)} all-reduce(f32[1,128]{1,0:T(1,128)S(1)} %get-tuple-element.118), channel_id=1, replica_groups=mesh['dp'=16,'mp'=2] {'mp'}, use_global_device_ids=true, to_apply=%region_1.0 | all-reduce | flops 128 | bytes 1024 | tf_op jit(solution)/shard_map/psum | solution.py:487
  139.5 3.9 %shard_map.126 = (f32[256,2560]{1,0:T(8,128)}, f32[1,128]{1,0:T(1,128)}) custom-call(f32[256,2560]{1,0:T(8,128)S(1)} %get-tuple-element.111.grad, f32[1,256]{1,0:T(1,128)S(1)} %copy-done.8, f32[1,2560]{1,0:T(1,128)S(1)} %get-tuple-element.117.col_moment_new, f32[1,128]{1,0:T(1,128)S(1)} %psum.15.terms, f32[1,5248]{1,0:T(1,128)S(1)} %broadcast_in_dim.10.sums.row_total), custom_call_target="tpu_custom_call" | custom-call | tf_op jit(solution)/shard_map/pallas_call | solution.py:313
  (83 shorter events, 32.1 us)
Async XLA Ops:
  5.1 31.8 %collective-permute-start.3 = (bf16[256,2560]{1,0:T(8,128)(2,1)S(1)}, bf16[256,2560]{1,0:T(8,128)(2,1)S(1)}, u32[]{:S(2)}, u32[]{:S(2)}) collective-permute-start(bf16[256,2560]{1,0:T(8,128)(2,1)S(1)} %copy-done), channel_id=1, source_target_pairs={{0,2},{2,0},{4,6},{6,4},{8,10},{10,8},{12,14},{14,12},{16,18},{18,... | collective-permute-start | bytes 3932168 | tf_op jit(solution)/shard_map/ppermute | solution.py:28
  8.1 30.2 %collective-permute-start.4 = (bf16[256,2560]{1,0:T(8,128)(2,1)S(1)}, bf16[256,2560]{1,0:T(8,128)(2,1)S(1)}, u32[]{:S(2)}, u32[]{:S(2)}) collective-permute-start(bf16[256,2560]{1,0:T(8,128)(2,1)S(1)} %copy-done), channel_id=1, source_target_pairs={{0,4},{2,6},{4,0},{6,2},{8,12},{10,14},{12,8},{14,10},{16,20},{18,... | collective-permute-start | bytes 3932168 | tf_op jit(solution)/shard_map/ppermute | solution.py:28
  9.6 29.2 %collective-permute-start = (bf16[128,1792]{1,0:T(8,128)(2,1)}, bf16[128,1792]{1,0:T(8,128)(2,1)S(1)}, u32[]{:S(2)}, u32[]{:S(2)}) collective-permute-start(bf16[128,1792]{1,0:T(8,128)(2,1)} %get-tuple-element.67.refs_1_), channel_id=1, source_target_pairs={{0,8},{2,10},{4,12},{6,14},{8,0},{10,2},{12,4},{14,6},{16,24},{18,... | collective-permute-start | bytes 1376264 | tf_op jit(solution)/shard_map/ppermute | solution.py:28
  11.2 27.6 %collective-permute-start.1 = (bf16[128,1792]{1,0:T(8,128)(2,1)}, bf16[128,1792]{1,0:T(8,128)(2,1)S(1)}, u32[]{:S(2)}, u32[]{:S(2)}) collective-permute-start(bf16[128,1792]{1,0:T(8,128)(2,1)} %get-tuple-element.68), channel_id=1, source_target_pairs={{0,16},{2,18},{4,20},{6,22},{8,24},{10,26},{12,28},{14,30},{16,0},... | collective-permute-start | bytes 1376264 | tf_op jit(solution)/shard_map/ppermute | solution.py:28
  13.8 22.5 %collective-permute-start.2 = (bf16[128,512]{1,0:T(8,128)(2,1)}, bf16[128,512]{1,0:T(8,128)(2,1)S(1)}, u32[]{:S(2)}, u32[]{:S(2)}) collective-permute-start(bf16[128,512]{1,0:T(8,128)(2,1)} %get-tuple-element.69), channel_id=1, source_target_pairs={{0,24},{2,26},{4,28},{6,30},{8,16},{10,18},{12,20},{14,22},{16,8},... | collective-permute-start | bytes 393224 | tf_op jit(solution)/shard_map/ppermute | solution.py:28
  38.9 6.4 %collective-permute-start.7 = (bf16[128,1536]{1,0:T(8,128)(2,1)S(1)}, bf16[128,1536]{1,0:T(8,128)(2,1)S(1)}, u32[]{:S(2)}, u32[]{:S(2)}) collective-permute-start(bf16[128,1536]{1,0:T(8,128)(2,1)S(1)} %get-tuple-element.83.mine), channel_id=1, source_target_pairs={{0,1},{1,0},{2,3},{3,2},{4,5},{5,4},{6,7},{7,6},{8,9},{9,8},{10,11... | collective-permute-start | bytes 1179656 | tf_op jit(solution)/shard_map/ppermute | solution.py:28
  39.0 17.0 %collective-permute-start.5 = (bf16[128,1280]{1,0:T(8,128)(2,1)S(1)}, bf16[128,1280]{1,0:T(8,128)(2,1)S(1)}, u32[]{:S(2)}, u32[]{:S(2)}) collective-permute-start(bf16[128,1280]{1,0:T(8,128)(2,1)S(1)} %get-tuple-element.80), channel_id=1, source_target_pairs={{0,8},{2,10},{4,12},{6,14},{8,0},{10,2},{12,4},{14,6},{16,24},{18,... | collective-permute-start | bytes 983048 | tf_op jit(solution)/shard_map/ppermute | solution.py:28
  40.6 17.7 %collective-permute-start.6 = (bf16[128,1280]{1,0:T(8,128)(2,1)S(1)}, bf16[128,1280]{1,0:T(8,128)(2,1)S(1)}, u32[]{:S(2)}, u32[]{:S(2)}) collective-permute-start(bf16[128,1280]{1,0:T(8,128)(2,1)S(1)} %copy-done.1), channel_id=1, source_target_pairs={{0,16},{2,18},{4,20},{6,22},{8,24},{10,26},{12,28},{14,30},{16,0},... | collective-permute-start | bytes 983048 | tf_op jit(solution)/shard_map/ppermute | solution.py:28
  43.2 19.9 %collective-permute-start.10 = (bf16[128,2560]{1,0:T(8,128)(2,1)S(1)}, bf16[128,2560]{1,0:T(8,128)(2,1)S(1)}, u32[]{:S(2)}, u32[]{:S(2)}) collective-permute-start(bf16[128,2560]{1,0:T(8,128)(2,1)S(1)} %get-tuple-element.76), channel_id=1, source_target_pairs={{0,2},{2,0},{4,6},{6,4},{8,10},{10,8},{12,14},{14,12},{16,18},{18,... | collective-permute-start | bytes 1966088 | tf_op jit(solution)/shard_map/ppermute | solution.py:28
  43.7 19.4 %collective-permute-start.9 = (bf16[128,2560]{1,0:T(8,128)(2,1)S(1)}, bf16[128,2560]{1,0:T(8,128)(2,1)S(1)}, u32[]{:S(2)}, u32[]{:S(2)}) collective-permute-start(bf16[128,2560]{1,0:T(8,128)(2,1)S(1)} %get-tuple-element.75), channel_id=1, source_target_pairs={{0,4},{2,6},{4,0},{6,2},{8,12},{10,14},{12,8},{14,10},{16,20},{18,... | collective-permute-start | bytes 1966088 | tf_op jit(solution)/shard_map/ppermute | solution.py:28
  58.4 15.0 %collective-permute-start.8 = (bf16[128,2560]{1,0:T(8,128)(2,1)S(1)}, bf16[128,2560]{1,0:T(8,128)(2,1)S(1)}, u32[]{:S(2)}, u32[]{:S(2)}) collective-permute-start(bf16[128,2560]{1,0:T(8,128)(2,1)S(1)} %shard_map.113), channel_id=1, source_target_pairs={{0,8},{2,10},{4,12},{6,14},{8,0},{10,2},{12,4},{14,6},{16,24},{18,... | collective-permute-start | bytes 1966088 | tf_op jit(solution)/shard_map/ppermute | solution.py:28
  61.0 19.0 %collective-permute-start.11 = (bf16[256,1280]{1,0:T(8,128)(2,1)S(1)}, bf16[256,1280]{1,0:T(8,128)(2,1)S(1)}, u32[]{:S(2)}, u32[]{:S(2)}) collective-permute-start(bf16[256,1280]{1,0:T(8,128)(2,1)S(1)} %get-tuple-element.87), channel_id=1, source_target_pairs={{0,2},{2,0},{4,6},{6,4},{8,10},{10,8},{12,14},{14,12},{16,18},{18,... | collective-permute-start | bytes 1966088 | tf_op jit(solution)/shard_map/ppermute | solution.py:28
  61.6 20.1 %collective-permute-start.12 = (bf16[256,1280]{1,0:T(8,128)(2,1)S(1)}, bf16[256,1280]{1,0:T(8,128)(2,1)S(1)}, u32[]{:S(2)}, u32[]{:S(2)}) collective-permute-start(bf16[256,1280]{1,0:T(8,128)(2,1)S(1)} %get-tuple-element.92), channel_id=1, source_target_pairs={{0,4},{2,6},{4,0},{6,2},{8,12},{10,14},{12,8},{14,10},{16,20},{18,... | collective-permute-start | bytes 1966088 | tf_op jit(solution)/shard_map/ppermute | solution.py:28
  75.5 15.8 %collective-permute-start.14 = (bf16[256,1280]{1,0:T(8,128)(2,1)S(1)}, bf16[256,1280]{1,0:T(8,128)(2,1)S(1)}, u32[]{:S(2)}, u32[]{:S(2)}) collective-permute-start(bf16[256,1280]{1,0:T(8,128)(2,1)S(1)} %get-tuple-element.100), channel_id=1, source_target_pairs={{0,4},{2,6},{4,0},{6,2},{8,12},{10,14},{12,8},{14,10},{16,20},{18,... | collective-permute-start | bytes 1966088 | tf_op jit(solution)/shard_map/ppermute | solution.py:28
  77.1 15.9 %collective-permute-start.13 = (bf16[256,1280]{1,0:T(8,128)(2,1)S(1)}, bf16[256,1280]{1,0:T(8,128)(2,1)S(1)}, u32[]{:S(2)}, u32[]{:S(2)}) collective-permute-start(bf16[256,1280]{1,0:T(8,128)(2,1)S(1)} %get-tuple-element.94), channel_id=1, source_target_pairs={{0,2},{2,0},{4,6},{6,4},{8,10},{10,8},{12,14},{14,12},{16,18},{18,... | collective-permute-start | bytes 1966088 | tf_op jit(solution)/shard_map/ppermute | solution.py:28
  77.6 29.4 %collective-permute-start.18 = (bf16[128,2560]{1,0:T(8,128)(2,1)S(1)}, bf16[128,2560]{1,0:T(8,128)(2,1)S(1)}, u32[]{:S(2)}, u32[]{:S(2)}) collective-permute-start(bf16[128,2560]{1,0:T(8,128)(2,1)S(1)} %get-tuple-element.108), channel_id=1, source_target_pairs={{0,16},{2,18},{4,20},{6,22},{8,24},{10,26},{12,28},{14,30},{16,0},... | collective-permute-start | bytes 1966088 | tf_op jit(solution)/shard_map/ppermute | solution.py:28
  80.0 28.6 %collective-permute-start.17 = (bf16[128,2560]{1,0:T(8,128)(2,1)S(1)}, bf16[128,2560]{1,0:T(8,128)(2,1)S(1)}, u32[]{:S(2)}, u32[]{:S(2)}) collective-permute-start(bf16[128,2560]{1,0:T(8,128)(2,1)S(1)} %get-tuple-element.106), channel_id=1, source_target_pairs={{0,8},{2,10},{4,12},{6,14},{8,0},{10,2},{12,4},{14,6},{16,24},{18,... | collective-permute-start | bytes 1966088 | tf_op jit(solution)/shard_map/ppermute | solution.py:28
  91.4 21.4 %collective-permute-start.16 = (bf16[128,2560]{1,0:T(8,128)(2,1)S(1)}, bf16[128,2560]{1,0:T(8,128)(2,1)S(1)}, u32[]{:S(2)}, u32[]{:S(2)}) collective-permute-start(bf16[128,2560]{1,0:T(8,128)(2,1)S(1)} %shard_map.120), channel_id=1, source_target_pairs={{0,2},{2,0},{4,6},{6,4},{8,10},{10,8},{12,14},{14,12},{16,18},{18,... | collective-permute-start | bytes 1966088 | tf_op jit(solution)/shard_map/ppermute | solution.py:28
  93.1 19.7 %collective-permute-start.15 = (bf16[128,2560]{1,0:T(8,128)(2,1)S(1)}, bf16[128,2560]{1,0:T(8,128)(2,1)S(1)}, u32[]{:S(2)}, u32[]{:S(2)}) collective-permute-start(bf16[128,2560]{1,0:T(8,128)(2,1)S(1)} %shard_map.119), channel_id=1, source_target_pairs={{0,4},{2,6},{4,0},{6,2},{8,12},{10,14},{12,8},{14,10},{16,20},{18,... | collective-permute-start | bytes 1966088 | tf_op jit(solution)/shard_map/ppermute | solution.py:28
  107.8 15.8 %collective-permute-start.23 = (bf16[64,2560]{1,0:T(8,128)(2,1)}, bf16[64,2560]{1,0:T(8,128)(2,1)}, u32[]{:S(2)}, u32[]{:S(2)}) collective-permute-start(bf16[64,2560]{1,0:T(8,128)(2,1)} %shard_map.122), channel_id=1, source_target_pairs={{0,8},{2,10},{4,12},{6,14},{8,0},{10,2},{12,4},{14,6},{16,24},{18,... | collective-permute-start | bytes 983048 | tf_op jit(solution)/shard_map/ppermute | solution.py:28
  109.4 18.4 %collective-permute-start.22 = (bf16[64,2560]{1,0:T(8,128)(2,1)}, bf16[64,2560]{1,0:T(8,128)(2,1)}, u32[]{:S(2)}, u32[]{:S(2)}) collective-permute-start(bf16[64,2560]{1,0:T(8,128)(2,1)} %shard_map.121), channel_id=1, source_target_pairs={{0,16},{2,18},{4,20},{6,22},{8,24},{10,26},{12,28},{14,30},{16,0},... | collective-permute-start | bytes 983048 | tf_op jit(solution)/shard_map/ppermute | solution.py:28
  127.8 8.4 %collective-permute-start.24 = (f32[5248]{0:T(1024)S(1)}, f32[5248]{0:T(1024)S(1)}, u32[]{:S(2)}, u32[]{:S(2)}) collective-permute-start(f32[5248]{0:T(1024)S(1)} %add_add_fusion.1), channel_id=1, source_target_pairs={{0,8},{2,10},{4,12},{6,14},{8,0},{10,2},{12,4},{14,6},{16,24},{18,... | collective-permute-start | bytes 62984 | tf_op jit(solution)/shard_map/ppermute | solution.py:28
  127.8 8.4 %collective-permute-start.25 = (f32[5248]{0:T(1024)S(1)}, f32[5248]{0:T(1024)S(1)}, u32[]{:S(2)}, u32[]{:S(2)}) collective-permute-start(f32[5248]{0:T(1024)S(1)} %add_add_fusion.1), channel_id=1, source_target_pairs={{0,16},{2,18},{4,20},{6,22},{8,24},{10,26},{12,28},{14,30},{16,0},... | collective-permute-start | bytes 62984 | tf_op jit(solution)/shard_map/ppermute | solution.py:28
  130.7 5.6 %collective-permute-start.26 = (f32[5248]{0:T(1024)S(1)}, f32[5248]{0:T(1024)S(1)}, u32[]{:S(2)}, u32[]{:S(2)}) collective-permute-start(f32[5248]{0:T(1024)S(1)} %add_add_fusion.1), channel_id=1, source_target_pairs={{0,24},{2,26},{4,28},{6,30},{8,16},{10,18},{12,20},{14,22},{16,8},... | collective-permute-start | bytes 62984 | tf_op jit(solution)/shard_map/ppermute | solution.py:28
  (15 other events, 177.6 us)

commit v15 on v14

--- a/solution.py
+++ b/solution.py
@@ -294,7 +294,7 @@
 
 def final_update(grad, row_moment_new, col_moment_new, terms, sums, total_rows, total_units):
     rows, units = grad.shape
-    tile = units // 5
+    tile = units // 2
 
     def kernel(grad, row_moment_new, col_moment_new, terms, row_total, update, row_mean):
         mean = row_total[...] / total_rows
@@ -386,7 +386,6 @@
     place = jnp.stack([me, core]).astype(jnp.int32)
     own, right, message1, message2, message3 = first_stage(out_grad, gate_pre, up_pre, place, rows)
 
-    down_weight, message1 = barrier((down_weight, message1))
     extra, every, whole = (split, 2 * rows), (0, tokens), (0, units)
     left1, left2, message3 = flip(message1, z_bit), flip(message2, w_bit), flip(message3, z_bit | w_bit)
     weight1, weight2 = flip(down_weight, x_bit), flip(down_weight, y_bit)
@@ -395,16 +394,17 @@
     weight3a, weight3b = flip(to_y, y_bit), flip(to_x, x_bit)
     left1, left2, message3, right, _, _ = barrier((left1, left2, message3, right, to_y, to_x))
     to_z, mine = cut(
-        [left1, left2, message3],
+        [left1, left2, message3, right],
         [
             (1, every, (0, split), 0, 0),
+            (3, every, (0, units - split), 0, split),
             (0, every, extra, 1, 0),
             (1, every, extra, 1, 2 * rows),
             (2, every, (0, 2 * rows), 1, 4 * rows),
         ],
-        [(tokens, split), (tokens, 6 * rows)],
+        [(tokens, units), (tokens, 6 * rows)],
     )
-    left3 = flip(to_z, z_bit)
+    from_near = flip(to_z, z_bit)
     right2 = flip(right, w_bit)
     theirs = flip(mine, 1, "mp")
     share = assemble(own, mine, theirs, place, rows)
@@ -422,14 +422,9 @@
         ranges = [(0, 2 * size)], [(4 * size, 5 * size)], [(3 * size, 4 * size)]
         return [(r, jnp.float32) for r in ranges]
 
-    left3, right2, share = barrier((left3, right2, share))
-    (to_z,) = cut(
-        [right2, right],
-        [(0, every, (0, units - split), 0, 0), (1, every, (0, units - split), 0, units - split)],
-        [(tokens, 2 * (units - split))],
-    )
-    from_near = flip(to_z, z_bit)
-    lefts = [(message1, 0), (left1, 0), (left2, 0), (left3, 0)]
+    from_near, right2, share = barrier((from_near, right2, share))
+    right3 = flip(right2, z_bit)
+    lefts = [(message1, 0), (left1, 0), (left2, 0), (from_near, 0)]
     left_to_x, left_to_y = products(share, [(lefts, split, sent(q), True)], steps)
     left_from_x, left_from_y = flip(left_to_x, x_bit), flip(left_to_y, y_bit)
 
@@ -438,9 +433,9 @@
     to_w, to_z = products(
         share, [(weights, units, [(high_sent(t), jnp.bfloat16), (low_sent(t), jnp.bfloat16)], False)], steps
     )
-    from_near, share, to_w, to_z = barrier((from_near, share, to_w, to_z))
+    right3, share, to_w, to_z = barrier((right3, share, to_w, to_z))
     from_w, from_z = flip(to_w, w_bit), flip(to_z, z_bit)
-    rights = [(right, 0), (from_near, units - split), (right2, 0), (from_near, 0)]
+    rights = [(right, 0), (from_near, split), (right2, 0), (right3, 0)]
     right_to_x, right_to_y = products(share, [(rights, units - split, sent(q), True)], steps)
     right_from_x, right_from_y = flip(right_to_x, x_bit), flip(right_to_y, y_bit)
     share, left_from_x, left_from_y, _ = barrier((share, left_from_x, left_from_y, right_to_x))

time: 144 us -> 136 us (0.944)
  starting transfers between devices: 39.3 us -> 32.2 us
  Pallas kernels: 26.3 us -> 24.6 us
    ppermute x27, starting transfers between devices: 39.3 us -> 32.2 us  [flip(): return lax.ppermute(value, axis, [(i, i ^ bits) for i in range(size)])]
    pallas_call x1, Pallas kernels: 3.89 us -> 2.23 us  [final_update(): pl.pallas_call(kernel, grid=(units // tile,), out_shape=[jax.ShapeDtypeSt...]
  transfers between devices with their start and end apart: 27 -> 27, of which waited for: 13 -> 15; matrix products, arithmetic and copies ran while one was open for 3% -> 3% of each run, Pallas kernels for 13% -> 16%
where the time goes in v15:
time: 136 us; the launch traced here: 135 us
  waiting for transfers between devices  67.3 us (49%)
  starting transfers between devices  32.2 us (24%)
  Pallas kernels  24.6 us (18%)
  other arithmetic  5.24 us (4%)
  blocking collectives  4.95 us (4%)
    ppermute x27, waiting for transfers between devices, flip(): return lax.ppermute(value, axis, [(i, i ^ bits) for i in range(size)])  67.3 us
    ppermute x27, starting transfers between devices, flip(): return lax.ppermute(value, axis, [(i, i ^ bits) for i in range(size)])  32.2 us
    pallas_call x5, Pallas kernels, products(): pl.pallas_call(kernel, grid=(steps,), out_shape=[jax.ShapeDtypeStruct((he...  14 us
    convert_element_type x1, other arithmetic, local(): up_grad = (hidden_grad * activated).astype(jnp.bfloat16)  3.96 us
    pallas_call x1, Pallas kernels, first_stage(): pl.pallas_call(kernel, grid=(tokens // step,), out_shape=[jax.ShapeDtypeS...  3.84 us
  transfers between devices with their start and end apart: 27, of which 15 were waited for; matrix products, arithmetic and copies ran while one was open for 3% of the time, Pallas kernels for 16%

profile of v15, /device:TPU:0, one launch (start us, length us, event | category | flops | bytes accessed | tf_op | source)
XLA Modules:
  0.0 135.3 jit_solution(2789832180207955372)
XLA Ops:
  0.6 3.0 %collective-permute-start.3 = (bf16[256,2560]{1,0:T(8,128)(2,1)}, bf16[256,2560]{1,0:T(8,128)(2,1)S(1)}, u32[]{:S(2)}, u32[]{:S(2)}) collective-permute-start(bf16[256,2560]{1,0:T(8,128)(2,1)} %refs_5_.1), channel_id=1, source_target_pairs={{0,2},{2,0},{4,6},{6,4},{8,10},{10,8},{12,14},{14,12},{16,18},{18,... | collective-permute-start | bytes 3932168 | tf_op jit(solution)/shard_map/ppermute | solution.py:28
  5.7 3.8 %shard_map.109 = (bf16[128,1024]{1,0:T(8,128)(2,1)}, bf16[128,1280]{1,0:T(8,128)(2,1)}, bf16[128,1792]{1,0:T(8,128)(2,1)}, bf16[128,1792]{1,0:T(8,128)(2,1)}, bf16[128,512]{1,0:T(8,128)(2,1)}) custom-call(s32[2]{0:T(128)} %pad_add_fusion.place, bf16[128,4096]{1,0:T(8,128)(2,1)} %source.1, bf16[128,2560]{1,0:T(8,128)(2,1)} %gate.1, bf16[128,2560]{1,0:T(8,128)(2,1)} %up.1), custom_call_target="tpu_custom_call" | custom-call | tf_op jit(solution)/shard_map/pallas_call | solution.py:116
  11.2 2.6 %collective-permute-start.1 = (bf16[128,1792]{1,0:T(8,128)(2,1)}, bf16[128,1792]{1,0:T(8,128)(2,1)S(1)}, u32[]{:S(2)}, u32[]{:S(2)}) collective-permute-start(bf16[128,1792]{1,0:T(8,128)(2,1)} %get-tuple-element.65), channel_id=1, source_target_pairs={{0,16},{2,18},{4,20},{6,22},{8,24},{10,26},{12,28},{14,30},{16,0},... | collective-permute-start | bytes 1376264 | tf_op jit(solution)/shard_map/ppermute | solution.py:28
  14.0 22.3 %collective-permute-done.2.refs_2_ = bf16[128,512]{1,0:T(8,128)(2,1)S(1)} collective-permute-done((bf16[128,512]{1,0:T(8,128)(2,1)}, bf16[128,512]{1,0:T(8,128)(2,1)S(1)}, u32[]{:S(2)}, u32[]{:S(2)}) %collective-permute-start.2) | collective-permute-done | bytes 131104 | tf_op jit(solution)/shard_map/ppermute | solution.py:28
  38.0 2.5 %collective-permute-start.5 = (bf16[128,2560]{1,0:T(8,128)(2,1)S(1)}, bf16[128,2560]{1,0:T(8,128)(2,1)S(1)}, u32[]{:S(2)}, u32[]{:S(2)}) collective-permute-start(bf16[128,2560]{1,0:T(8,128)(2,1)S(1)} %get-tuple-element.77), channel_id=1, source_target_pairs={{0,8},{2,10},{4,12},{6,14},{8,0},{10,2},{12,4},{14,6},{16,24},{18,... | collective-permute-start | bytes 1966088 | tf_op jit(solution)/shard_map/ppermute | solution.py:28
  43.4 16.1 %collective-permute-done.6.refs_3_ = bf16[128,1280]{1,0:T(8,128)(2,1)S(1)} collective-permute-done((bf16[128,1280]{1,0:T(8,128)(2,1)S(1)}, bf16[128,1280]{1,0:T(8,128)(2,1)S(1)}, u32[]{:S(2)}, u32[]{:S(2)}) %collective-permute-start.6) | collective-permute-done | bytes 327712 | tf_op jit(solution)/shard_map/ppermute | solution.py:28
  60.2 3.3 %collective-permute-start.8 = (bf16[128,1280]{1,0:T(8,128)(2,1)S(1)}, bf16[128,1280]{1,0:T(8,128)(2,1)S(1)}, u32[]{:S(2)}, u32[]{:S(2)}) collective-permute-start(bf16[128,1280]{1,0:T(8,128)(2,1)S(1)} %collective-permute-done.6.refs_3_), channel_id=1, source_target_pairs={{0,8},{2,10},{4,12},{6,14},{8,0},{10,2},{12,4},{14,6},{16,24},{18,... | collective-permute-start | bytes 983048 | tf_op jit(solution)/shard_map/ppermute | solution.py:28
  63.5 2.0 %shard_map.113 = (bf16[256,1280]{1,0:T(8,128)(2,1)S(1)}, bf16[256,1280]{1,0:T(8,128)(2,1)S(1)}) custom-call(bf16[512,1024]{1,0:T(8,128)(2,1)S(1)} %shard_map.112.refs_0_, bf16[128,1792]{1,0:T(8,128)(2,1)S(1)} %copy-done.2, bf16[128,1792]{1,0:T(8,128)(2,1)S(1)} %collective-permute-done.refs_0_.refs_2_, ...), custom_call_target="tpu_custom_call" | custom-call | tf_op jit(solution)/shard_map/pallas_call | solution.py:359
  66.7 2.8 %shard_map.114 = (bf16[128,2560]{1,0:T(8,128)(2,1)S(1)}, bf16[128,2560]{1,0:T(8,128)(2,1)S(1)}) custom-call(bf16[512,1024]{1,0:T(8,128)(2,1)S(1)} %shard_map.112.refs_0_, bf16[256,2560]{1,0:T(8,128)(2,1)S(1)} %copy-done, bf16[256,2560]{1,0:T(8,128)(2,1)S(1)} %collective-permute-done.3.refs_0_.refs_2_.refs_6_, ...), custom_call_target="tpu_custom_call" | custom-call | tf_op jit(solution)/shard_map/pallas_call | solution.py:359
  69.5 2.1 %shard_map.115 = (bf16[256,1280]{1,0:T(8,128)(2,1)S(1)}, bf16[256,1280]{1,0:T(8,128)(2,1)S(1)}) custom-call(bf16[512,1024]{1,0:T(8,128)(2,1)S(1)} %shard_map.112.refs_0_, bf16[128,1280]{1,0:T(8,128)(2,1)S(1)} %copy-done.1, bf16[128,2560]{1,0:T(8,128)(2,1)S(1)} %collective-permute-done.5.refs_4_.refs_2_, ...), custom_call_target="tpu_custom_call" | custom-call | tf_op jit(solution)/shard_map/pallas_call | solution.py:359
  74.7 8.7 %collective-permute-done.11.refs_2_ = bf16[256,1280]{1,0:T(8,128)(2,1)S(1)} collective-permute-done((bf16[256,1280]{1,0:T(8,128)(2,1)S(1)}, bf16[256,1280]{1,0:T(8,128)(2,1)S(1)}, u32[]{:S(2)}, u32[]{:S(2)}) %collective-permute-start.11) | collective-permute-done | bytes 655392 | tf_op jit(solution)/shard_map/ppermute | solution.py:28
  83.8 2.1 %shard_map.116 = (f32[256,1280]{1,0:T(8,128)S(1)}, f32[128,1280]{1,0:T(8,128)S(1)}, f32[128,1280]{1,0:T(8,128)S(1)}) custom-call(bf16[512,1024]{1,0:T(8,128)(2,1)S(1)} %shard_map.112.refs_0_, bf16[128,1792]{1,0:T(8,128)(2,1)S(1)} %copy-done.2, bf16[128,1792]{1,0:T(8,128)(2,1)S(1)} %collective-permute-done.refs_0_.refs_2_, ...), custom_call_target="tpu_custom_call" | custom-call | tf_op jit(solution)/shard_map/pallas_call | solution.py:359
  86.0 5.1 %shard_map.117 = (f32[256,1280]{1,0:T(8,128)S(1)}, f32[128,1280]{1,0:T(8,128)S(1)}, f32[128,1280]{1,0:T(8,128)S(1)}, f32[128,2560]{1,0:T(8,128)S(1)}, f32[64,2560]{1,0:T(8,128)S(1)}, /*index=5*/f32[64,2560]{1,0:T(8,128)S(1)}) custom-call(bf16[512,1024]{1,0:T(8,128)(2,1)S(1)} %shard_map.112.refs_0_, bf16[128,1280]{1,0:T(8,128)(2,1)S(1)} %copy-done.1, ...), custom_call_target="tpu_custom_call" | custom-call | tf_op jit(solution)/shard_map/pallas_call | solution.py:359
  91.0 2.5 %collective-permute-done.14.refs_3_.refs_5_ = bf16[256,1280]{1,0:T(8,128)(2,1)S(1)} collective-permute-done((bf16[256,1280]{1,0:T(8,128)(2,1)S(1)}, bf16[256,1280]{1,0:T(8,128)(2,1)S(1)}, u32[]{:S(2)}, u32[]{:S(2)}) %collective-permute-start.14) | collective-permute-done | bytes 655392 | tf_op jit(solution)/shard_map/ppermute | solution.py:28
  93.7 2.4 %collective-permute-start.16 = (bf16[128,2560]{1,0:T(8,128)(2,1)S(1)}, bf16[128,2560]{1,0:T(8,128)(2,1)S(1)}, u32[]{:S(2)}, u32[]{:S(2)}) collective-permute-start(bf16[128,2560]{1,0:T(8,128)(2,1)S(1)} %shard_map.119), channel_id=1, source_target_pairs={{0,2},{2,0},{4,6},{6,4},{8,10},{10,8},{12,14},{14,12},{16,18},{18,... | collective-permute-start | bytes 1966088 | tf_op jit(solution)/shard_map/ppermute | solution.py:28
  96.9 4.2 %collective-permute-done.18.refs_1_ = bf16[128,2560]{1,0:T(8,128)(2,1)S(1)} collective-permute-done((bf16[128,2560]{1,0:T(8,128)(2,1)S(1)}, bf16[128,2560]{1,0:T(8,128)(2,1)S(1)}, u32[]{:S(2)}, u32[]{:S(2)}) %collective-permute-start.18) | collective-permute-done | bytes 655392 | tf_op jit(solution)/shard_map/ppermute | solution.py:28
  101.8 3.6 %collective-permute-done.17.refs_1_ = bf16[128,2560]{1,0:T(8,128)(2,1)S(1)} collective-permute-done((bf16[128,2560]{1,0:T(8,128)(2,1)S(1)}, bf16[128,2560]{1,0:T(8,128)(2,1)S(1)}, u32[]{:S(2)}, u32[]{:S(2)}) %collective-permute-start.17) | collective-permute-done | bytes 655392 | tf_op jit(solution)/shard_map/ppermute | solution.py:28
  107.7 2.5 %psum.14.row_sum = f32[1,256]{1,0:T(1,128)S(1)} all-reduce(f32[1,256]{1,0:T(1,128)S(1)} %get-tuple-element.108), channel_id=1, replica_groups=mesh['dp'=16,'mp'=2] {'mp'}, use_global_device_ids=true, to_apply=%region_0.0 | all-reduce | flops 256 | bytes 2048 | tf_op jit(solution)/shard_map/psum | solution.py:459
  117.5 4.0 %collective-permute-done.22 = bf16[64,2560]{1,0:T(8,128)(2,1)} collective-permute-done((bf16[64,2560]{1,0:T(8,128)(2,1)}, bf16[64,2560]{1,0:T(8,128)(2,1)}, u32[]{:S(2)}, u32[]{:S(2)}) %collective-permute-start.22) | collective-permute-done | bytes 327712 | tf_op jit(solution)/shard_map/ppermute | solution.py:28
  121.5 1.9 %collective-permute-start.25 = (f32[5248]{0:T(1024)S(1)}, f32[5248]{0:T(1024)S(1)}, u32[]{:S(2)}, u32[]{:S(2)}) collective-permute-start(f32[5248]{0:T(1024)S(1)} %add_add_fusion.1), channel_id=1, source_target_pairs={{0,16},{2,18},{4,20},{6,22},{8,24},{10,26},{12,28},{14,30},{16,0},... | collective-permute-start | bytes 62984 | tf_op jit(solution)/shard_map/ppermute | solution.py:28
  123.4 2.5 %collective-permute-start.26 = (f32[5248]{0:T(1024)S(1)}, f32[5248]{0:T(1024)S(1)}, u32[]{:S(2)}, u32[]{:S(2)}) collective-permute-start(f32[5248]{0:T(1024)S(1)} %add_add_fusion.1), channel_id=1, source_target_pairs={{0,24},{2,26},{4,28},{6,30},{8,16},{10,18},{12,20},{14,22},{16,8},... | collective-permute-start | bytes 62984 | tf_op jit(solution)/shard_map/ppermute | solution.py:28
  125.9 4.0 %fusion.8 = (bf16[128,2560]{1,0:T(8,128)(2,1)}, bf16[128,2560]{1,0:T(8,128)(2,1)}) fusion(bf16[128,2560]{1,0:T(8,128)(2,1)S(1)} %copy-done.9, bf16[64,2560]{1,0:T(8,128)(2,1)} %collective-permute-done.23, bf16[64,2560]{1,0:T(8,128)(2,1)} %collective-permute-done.22, f32[128,2560]{1,0:T(8,128)} %copy-done.4, bf16[64,2560]{1,0:T(8,128)(2,1)S(1)} %slice.13, ...), kind=kLoop, calls=%fused_computation.15 | loop fusion | flops 11468800 | bytes 5242880 | tf_op jit(solution)/shard_map/convert_element_type | solution.py:508
  130.0 2.5 %psum.15.terms = f32[1,128]{1,0:T(1,128)S(1)} all-reduce(f32[1,128]{1,0:T(1,128)S(1)} %get-tuple-element.114), channel_id=1, replica_groups=mesh['dp'=16,'mp'=2] {'mp'}, use_global_device_ids=true, to_apply=%region_1.0 | all-reduce | flops 128 | bytes 1024 | tf_op jit(solution)/shard_map/psum | solution.py:482
  133.1 2.2 %shard_map.125 = (f32[256,2560]{1,0:T(8,128)}, f32[1,128]{1,0:T(1,128)}) custom-call(f32[256,2560]{1,0:T(8,128)S(1)} %get-tuple-element.107.grad, f32[1,256]{1,0:T(1,128)S(1)} %copy-done.8, f32[1,2560]{1,0:T(1,128)S(1)} %get-tuple-element.113.col_moment_new, f32[1,128]{1,0:T(1,128)S(1)} %psum.15.terms, f32[1,5248]{1,0:T(1,128)S(1)} %broadcast_in_dim.10.sums.row_total), custom_call_target="tpu_custom_call" | custom-call | tf_op jit(solution)/shard_map/pallas_call | solution.py:313
  (82 shorter events, 25.8 us)
Async XLA Ops:
  0.6 35.7 %collective-permute-start.3 = (bf16[256,2560]{1,0:T(8,128)(2,1)}, bf16[256,2560]{1,0:T(8,128)(2,1)S(1)}, u32[]{:S(2)}, u32[]{:S(2)}) collective-permute-start(bf16[256,2560]{1,0:T(8,128)(2,1)} %refs_5_.1), channel_id=1, source_target_pairs={{0,2},{2,0},{4,6},{6,4},{8,10},{10,8},{12,14},{14,12},{16,18},{18,... | collective-permute-start | bytes 3932168 | tf_op jit(solution)/shard_map/ppermute | solution.py:28
  3.6 32.7 %collective-permute-start.4 = (bf16[256,2560]{1,0:T(8,128)(2,1)}, bf16[256,2560]{1,0:T(8,128)(2,1)S(1)}, u32[]{:S(2)}, u32[]{:S(2)}) collective-permute-start(bf16[256,2560]{1,0:T(8,128)(2,1)} %refs_5_.1), channel_id=1, source_target_pairs={{0,4},{2,6},{4,0},{6,2},{8,12},{10,14},{12,8},{14,10},{16,20},{18,... | collective-permute-start | bytes 3932168 | tf_op jit(solution)/shard_map/ppermute | solution.py:28
  9.6 27.2 %collective-permute-start = (bf16[128,1792]{1,0:T(8,128)(2,1)}, bf16[128,1792]{1,0:T(8,128)(2,1)S(1)}, u32[]{:S(2)}, u32[]{:S(2)}) collective-permute-start(bf16[128,1792]{1,0:T(8,128)(2,1)} %get-tuple-element.64.refs_1_), channel_id=1, source_target_pairs={{0,8},{2,10},{4,12},{6,14},{8,0},{10,2},{12,4},{14,6},{16,24},{18,... | collective-permute-start | bytes 1376264 | tf_op jit(solution)/shard_map/ppermute | solution.py:28
  11.2 26.6 %collective-permute-start.1 = (bf16[128,1792]{1,0:T(8,128)(2,1)}, bf16[128,1792]{1,0:T(8,128)(2,1)S(1)}, u32[]{:S(2)}, u32[]{:S(2)}) collective-permute-start(bf16[128,1792]{1,0:T(8,128)(2,1)} %get-tuple-element.65), channel_id=1, source_target_pairs={{0,16},{2,18},{4,20},{6,22},{8,24},{10,26},{12,28},{14,30},{16,0},... | collective-permute-start | bytes 1376264 | tf_op jit(solution)/shard_map/ppermute | solution.py:28
  13.8 22.5 %collective-permute-start.2 = (bf16[128,512]{1,0:T(8,128)(2,1)}, bf16[128,512]{1,0:T(8,128)(2,1)S(1)}, u32[]{:S(2)}, u32[]{:S(2)}) collective-permute-start(bf16[128,512]{1,0:T(8,128)(2,1)} %get-tuple-element.66), channel_id=1, source_target_pairs={{0,24},{2,26},{4,28},{6,30},{8,16},{10,18},{12,20},{14,22},{16,8},... | collective-permute-start | bytes 393224 | tf_op jit(solution)/shard_map/ppermute | solution.py:28
  38.0 22.3 %collective-permute-start.5 = (bf16[128,2560]{1,0:T(8,128)(2,1)S(1)}, bf16[128,2560]{1,0:T(8,128)(2,1)S(1)}, u32[]{:S(2)}, u32[]{:S(2)}) collective-permute-start(bf16[128,2560]{1,0:T(8,128)(2,1)S(1)} %get-tuple-element.77), channel_id=1, source_target_pairs={{0,8},{2,10},{4,12},{6,14},{8,0},{10,2},{12,4},{14,6},{16,24},{18,... | collective-permute-start | bytes 1966088 | tf_op jit(solution)/shard_map/ppermute | solution.py:28
  40.5 19.0 %collective-permute-start.6 = (bf16[128,1280]{1,0:T(8,128)(2,1)S(1)}, bf16[128,1280]{1,0:T(8,128)(2,1)S(1)}, u32[]{:S(2)}, u32[]{:S(2)}) collective-permute-start(bf16[128,1280]{1,0:T(8,128)(2,1)S(1)} %copy-done.1), channel_id=1, source_target_pairs={{0,16},{2,18},{4,20},{6,22},{8,24},{10,26},{12,28},{14,30},{16,0},... | collective-permute-start | bytes 983048 | tf_op jit(solution)/shard_map/ppermute | solution.py:28
  41.7 25.0 %collective-permute-start.10 = (bf16[128,2560]{1,0:T(8,128)(2,1)S(1)}, bf16[128,2560]{1,0:T(8,128)(2,1)S(1)}, u32[]{:S(2)}, u32[]{:S(2)}) collective-permute-start(bf16[128,2560]{1,0:T(8,128)(2,1)S(1)} %get-tuple-element.72), channel_id=1, source_target_pairs={{0,2},{2,0},{4,6},{6,4},{8,10},{10,8},{12,14},{14,12},{16,18},{18,... | collective-permute-start | bytes 1966088 | tf_op jit(solution)/shard_map/ppermute | solution.py:28
  42.2 24.5 %collective-permute-start.9 = (bf16[128,2560]{1,0:T(8,128)(2,1)S(1)}, bf16[128,2560]{1,0:T(8,128)(2,1)S(1)}, u32[]{:S(2)}, u32[]{:S(2)}) collective-permute-start(bf16[128,2560]{1,0:T(8,128)(2,1)S(1)} %get-tuple-element.71), channel_id=1, source_target_pairs={{0,4},{2,6},{4,0},{6,2},{8,12},{10,14},{12,8},{14,10},{16,20},{18,... | collective-permute-start | bytes 1966088 | tf_op jit(solution)/shard_map/ppermute | solution.py:28
  60.2 9.2 %collective-permute-start.8 = (bf16[128,1280]{1,0:T(8,128)(2,1)S(1)}, bf16[128,1280]{1,0:T(8,128)(2,1)S(1)}, u32[]{:S(2)}, u32[]{:S(2)}) collective-permute-start(bf16[128,1280]{1,0:T(8,128)(2,1)S(1)} %collective-permute-done.6.refs_3_), channel_id=1, source_target_pairs={{0,8},{2,10},{4,12},{6,14},{8,0},{10,2},{12,4},{14,6},{16,24},{18,... | collective-permute-start | bytes 983048 | tf_op jit(solution)/shard_map/ppermute | solution.py:28
  65.6 17.7 %collective-permute-start.11 = (bf16[256,1280]{1,0:T(8,128)(2,1)S(1)}, bf16[256,1280]{1,0:T(8,128)(2,1)S(1)}, u32[]{:S(2)}, u32[]{:S(2)}) collective-permute-start(bf16[256,1280]{1,0:T(8,128)(2,1)S(1)} %get-tuple-element.83), channel_id=1, source_target_pairs={{0,2},{2,0},{4,6},{6,4},{8,10},{10,8},{12,14},{14,12},{16,18},{18,... | collective-permute-start | bytes 1966088 | tf_op jit(solution)/shard_map/ppermute | solution.py:28
  66.2 17.7 %collective-permute-start.12 = (bf16[256,1280]{1,0:T(8,128)(2,1)S(1)}, bf16[256,1280]{1,0:T(8,128)(2,1)S(1)}, u32[]{:S(2)}, u32[]{:S(2)}) collective-permute-start(bf16[256,1280]{1,0:T(8,128)(2,1)S(1)} %get-tuple-element.88), channel_id=1, source_target_pairs={{0,4},{2,6},{4,0},{6,2},{8,12},{10,14},{12,8},{14,10},{16,20},{18,... | collective-permute-start | bytes 1966088 | tf_op jit(solution)/shard_map/ppermute | solution.py:28
  71.6 22.0 %collective-permute-start.14 = (bf16[256,1280]{1,0:T(8,128)(2,1)S(1)}, bf16[256,1280]{1,0:T(8,128)(2,1)S(1)}, u32[]{:S(2)}, u32[]{:S(2)}) collective-permute-start(bf16[256,1280]{1,0:T(8,128)(2,1)S(1)} %get-tuple-element.96), channel_id=1, source_target_pairs={{0,4},{2,6},{4,0},{6,2},{8,12},{10,14},{12,8},{14,10},{16,20},{18,... | collective-permute-start | bytes 1966088 | tf_op jit(solution)/shard_map/ppermute | solution.py:28
  73.2 23.0 %collective-permute-start.13 = (bf16[256,1280]{1,0:T(8,128)(2,1)S(1)}, bf16[256,1280]{1,0:T(8,128)(2,1)S(1)}, u32[]{:S(2)}, u32[]{:S(2)}) collective-permute-start(bf16[256,1280]{1,0:T(8,128)(2,1)S(1)} %get-tuple-element.90), channel_id=1, source_target_pairs={{0,2},{2,0},{4,6},{6,4},{8,10},{10,8},{12,14},{14,12},{16,18},{18,... | collective-permute-start | bytes 1966088 | tf_op jit(solution)/shard_map/ppermute | solution.py:28
  74.7 26.4 %collective-permute-start.18 = (bf16[128,2560]{1,0:T(8,128)(2,1)S(1)}, bf16[128,2560]{1,0:T(8,128)(2,1)S(1)}, u32[]{:S(2)}, u32[]{:S(2)}) collective-permute-start(bf16[128,2560]{1,0:T(8,128)(2,1)S(1)} %get-tuple-element.104), channel_id=1, source_target_pairs={{0,16},{2,18},{4,20},{6,22},{8,24},{10,26},{12,28},{14,30},{16,0},... | collective-permute-start | bytes 1966088 | tf_op jit(solution)/shard_map/ppermute | solution.py:28
  83.3 22.1 %collective-permute-start.17 = (bf16[128,2560]{1,0:T(8,128)(2,1)S(1)}, bf16[128,2560]{1,0:T(8,128)(2,1)S(1)}, u32[]{:S(2)}, u32[]{:S(2)}) collective-permute-start(bf16[128,2560]{1,0:T(8,128)(2,1)S(1)} %get-tuple-element.102), channel_id=1, source_target_pairs={{0,8},{2,10},{4,12},{6,14},{8,0},{10,2},{12,4},{14,6},{16,24},{18,... | collective-permute-start | bytes 1966088 | tf_op jit(solution)/shard_map/ppermute | solution.py:28
  93.7 12.7 %collective-permute-start.16 = (bf16[128,2560]{1,0:T(8,128)(2,1)S(1)}, bf16[128,2560]{1,0:T(8,128)(2,1)S(1)}, u32[]{:S(2)}, u32[]{:S(2)}) collective-permute-start(bf16[128,2560]{1,0:T(8,128)(2,1)S(1)} %shard_map.119), channel_id=1, source_target_pairs={{0,2},{2,0},{4,6},{6,4},{8,10},{10,8},{12,14},{14,12},{16,18},{18,... | collective-permute-start | bytes 1966088 | tf_op jit(solution)/shard_map/ppermute | solution.py:28
  96.3 10.7 %collective-permute-start.15 = (bf16[128,2560]{1,0:T(8,128)(2,1)S(1)}, bf16[128,2560]{1,0:T(8,128)(2,1)S(1)}, u32[]{:S(2)}, u32[]{:S(2)}) collective-permute-start(bf16[128,2560]{1,0:T(8,128)(2,1)S(1)} %shard_map.118), channel_id=1, source_target_pairs={{0,4},{2,6},{4,0},{6,2},{8,12},{10,14},{12,8},{14,10},{16,20},{18,... | collective-permute-start | bytes 1966088 | tf_op jit(solution)/shard_map/ppermute | solution.py:28
  101.8 15.7 %collective-permute-start.23 = (bf16[64,2560]{1,0:T(8,128)(2,1)}, bf16[64,2560]{1,0:T(8,128)(2,1)}, u32[]{:S(2)}, u32[]{:S(2)}) collective-permute-start(bf16[64,2560]{1,0:T(8,128)(2,1)} %shard_map.121), channel_id=1, source_target_pairs={{0,8},{2,10},{4,12},{6,14},{8,0},{10,2},{12,4},{14,6},{16,24},{18,... | collective-permute-start | bytes 983048 | tf_op jit(solution)/shard_map/ppermute | solution.py:28
  106.4 15.2 %collective-permute-start.22 = (bf16[64,2560]{1,0:T(8,128)(2,1)}, bf16[64,2560]{1,0:T(8,128)(2,1)}, u32[]{:S(2)}, u32[]{:S(2)}) collective-permute-start(bf16[64,2560]{1,0:T(8,128)(2,1)} %shard_map.120), channel_id=1, source_target_pairs={{0,16},{2,18},{4,20},{6,22},{8,24},{10,26},{12,28},{14,30},{16,0},... | collective-permute-start | bytes 983048 | tf_op jit(solution)/shard_map/ppermute | solution.py:28
  112.8 4.7 %collective-permute-start.21 = (f32[5248]{0:T(1024)S(1)}, f32[5248]{0:T(1024)S(1)}, u32[]{:S(2)}, u32[]{:S(2)}) collective-permute-start(f32[5248]{0:T(1024)S(1)} %reduce), channel_id=1, source_target_pairs={{0,6},{2,4},{4,2},{6,0},{8,14},{10,12},{12,10},{14,8},{16,22},{18,... | collective-permute-start | bytes 62984 | tf_op jit(solution)/shard_map/ppermute | solution.py:28
  121.5 8.4 %collective-permute-start.24 = (f32[5248]{0:T(1024)S(1)}, f32[5248]{0:T(1024)S(1)}, u32[]{:S(2)}, u32[]{:S(2)}) collective-permute-start(f32[5248]{0:T(1024)S(1)} %add_add_fusion.1), channel_id=1, source_target_pairs={{0,8},{2,10},{4,12},{6,14},{8,0},{10,2},{12,4},{14,6},{16,24},{18,... | collective-permute-start | bytes 62984 | tf_op jit(solution)/shard_map/ppermute | solution.py:28
  121.5 8.4 %collective-permute-start.25 = (f32[5248]{0:T(1024)S(1)}, f32[5248]{0:T(1024)S(1)}, u32[]{:S(2)}, u32[]{:S(2)}) collective-permute-start(f32[5248]{0:T(1024)S(1)} %add_add_fusion.1), channel_id=1, source_target_pairs={{0,16},{2,18},{4,20},{6,22},{8,24},{10,26},{12,28},{14,30},{16,0},... | collective-permute-start | bytes 62984 | tf_op jit(solution)/shard_map/ppermute | solution.py:28
  123.4 6.5 %collective-permute-start.26 = (f32[5248]{0:T(1024)S(1)}, f32[5248]{0:T(1024)S(1)}, u32[]{:S(2)}, u32[]{:S(2)}) collective-permute-start(f32[5248]{0:T(1024)S(1)} %add_add_fusion.1), channel_id=1, source_target_pairs={{0,24},{2,26},{4,28},{6,30},{8,16},{10,18},{12,20},{14,22},{16,8},... | collective-permute-start | bytes 62984 | tf_op jit(solution)/shard_map/ppermute | solution.py:28
  (15 other events, 148.4 us)

commit v16 on v15

--- a/solution.py
+++ b/solution.py
@@ -90,13 +90,13 @@
     return product, hidden_grad
 
 
-def first_stage(out_grad, gate_pre, up_pre, place, rows):
+def first_stage(out_grad, gate_pre, up_pre, rows):
     tokens, units = gate_pre.shape
     half = units // 2
     step = 32
 
-    def kernel(place, source, gate, up, own, right, message1, message2, message3):
-        me, core = place[0], place[1]
+    def kernel(source, gate, up, own, right, message1, message2, message3):
+        me, core = lax.axis_index("dp"), lax.axis_index("mp")
 
         def block(k, j):
             return pl.ds(pl.multiple_of((me ^ (4 * k + j)) * rows, rows), rows)
@@ -117,12 +117,32 @@
         kernel,
         grid=(tokens // step,),
         out_shape=[jax.ShapeDtypeStruct((tokens, width), jnp.bfloat16) for width in widths],
-        in_specs=[pl.BlockSpec(memory_space=pltpu.SMEM)]
-        + [pl.BlockSpec((step, array.shape[1]), lambda i: (i, 0)) for array in (out_grad, gate_pre, up_pre)],
+        in_specs=[pl.BlockSpec((step, array.shape[1]), lambda i: (i, 0)) for array in (out_grad, gate_pre, up_pre)],
         out_specs=[pl.BlockSpec((step, width), lambda i: (i, 0)) for width in widths],
         compiler_params=pltpu.CompilerParams(vmem_limit_bytes=56 << 20),
         cost_estimate=EAGER,
-    )(place, out_grad, gate_pre, up_pre)
+    )(out_grad, gate_pre, up_pre)
+
+
+def gelu_terms(gate_pre, up_pre):
+    tokens, units = gate_pre.shape
+    step = 32
+
+    def kernel(gate, up, activated, slope):
+        value, derivative = gelu_parts(gate[...].astype(jnp.float32))
+        activated[...] = value
+        slope[...] = up[...].astype(jnp.float32) * derivative
+
+    block = pl.BlockSpec((step, units), lambda i: (i, 0))
+    return pl.pallas_call(
+        kernel,
+        grid=(tokens // step,),
+        out_shape=[jax.ShapeDtypeStruct((tokens, units), jnp.float32)] * 2,
+        in_specs=[block] * 2,
+        out_specs=[block] * 2,
+        compiler_params=pltpu.CompilerParams(vmem_limit_bytes=10 << 20),
+        cost_estimate=EAGER,
+    )(gate_pre, up_pre)
 
 
 def cut(sources, parts, shapes):
@@ -384,20 +404,21 @@
     split = units // 2
     barrier = lax.optimization_barrier
     place = jnp.stack([me, core]).astype(jnp.int32)
-    own, right, message1, message2, message3 = first_stage(out_grad, gate_pre, up_pre, place, rows)
+    own, right, message1, message2, message3 = first_stage(out_grad, gate_pre, up_pre, rows)
 
     extra, every, whole = (split, 2 * rows), (0, tokens), (0, units)
     left1, left2, message3 = flip(message1, z_bit), flip(message2, w_bit), flip(message3, z_bit | w_bit)
     weight1, weight2 = flip(down_weight, x_bit), flip(down_weight, y_bit)
-    message3, weight1, weight2 = barrier((message3, weight1, weight2))
+    activated, slope = gelu_terms(gate_pre, up_pre)
+    message3, weight1, weight2, activated, slope = barrier((message3, weight1, weight2, activated, slope))
     to_y, to_x = cut([weight1, weight2], [(0, (0, q), whole, 0, 0), (1, (q, q), whole, 1, 0)], [(q, units)] * 2)
     weight3a, weight3b = flip(to_y, y_bit), flip(to_x, x_bit)
     left1, left2, message3, right, _, _ = barrier((left1, left2, message3, right, to_y, to_x))
     to_z, mine = cut(
         [left1, left2, message3, right],
         [
-            (1, every, (0, split), 0, 0),
-            (3, every, (0, units - split), 0, split),
+            (3, every, (0, units - split), 0, 0),
+            (1, every, (0, split), 0, units - split),
             (0, every, extra, 1, 0),
             (1, every, extra, 1, 2 * rows),
             (2, every, (0, 2 * rows), 1, 4 * rows),
@@ -424,7 +445,7 @@
 
     from_near, right2, share = barrier((from_near, right2, share))
     right3 = flip(right2, z_bit)
-    lefts = [(message1, 0), (left1, 0), (left2, 0), (from_near, 0)]
+    lefts = [(message1, 0), (left1, 0), (left2, 0), (from_near, units - split)]
     left_to_x, left_to_y = products(share, [(lefts, split, sent(q), True)], steps)
     left_from_x, left_from_y = flip(left_to_x, x_bit), flip(left_to_y, y_bit)
 
@@ -435,7 +456,7 @@
     )
     right3, share, to_w, to_z = barrier((right3, share, to_w, to_z))
     from_w, from_z = flip(to_w, w_bit), flip(to_z, z_bit)
-    rights = [(right, 0), (from_near, split), (right2, 0), (right3, 0)]
+    rights = [(right, 0), (from_near, 0), (right2, 0), (right3, 0)]
     right_to_x, right_to_y = products(share, [(rights, units - split, sent(q), True)], steps)
     right_from_x, right_from_y = flip(right_to_x, x_bit), flip(right_to_y, y_bit)
     share, left_from_x, left_from_y, _ = barrier((share, left_from_x, left_from_y, right_to_x))
@@ -457,7 +478,7 @@
     )
 
     row_sum = lax.psum(row_part, "mp")
-    return grad, row_sum, (parts[3], from_z[:t], from_w[:t], last_a, last_b)
+    return grad, row_sum, (parts[3], from_z[:t], from_w[:t], last_a, last_b, activated, slope)
 
 
 def local(out_grad, gate_pre, up_pre, down_weight, row_moment, col_moment):
@@ -474,7 +495,7 @@
         row_moment_new, sums = column_sums(grad, row_sum, row_moment[None, :], decay, total_units)
         sums = group_sum(sums[0], all_bits[:INNER_BITS])
         sums, terms = lax.optimization_barrier((sums, terms))
-        own_part, from_low, from_high, last_a, last_b = terms
+        own_part, from_low, from_high, last_a, last_b, activated, slope = terms
         arrived = jnp.concatenate([from_low, from_high], axis=0).astype(jnp.float32)
         hidden_grad = own_part + arrived + jnp.concatenate([last_a, last_b], axis=0).astype(jnp.float32)
         sums = group_sum(sums, all_bits[INNER_BITS:])[None, :]
@@ -486,6 +507,8 @@
         product, hidden_grad = general_products(
             out_grad, gate_pre, up_pre, down_weight, all_bits[:INNER_BITS], all_bits[INNER_BITS:]
         )
+        activated, derivative = gelu_parts(gate_pre.astype(jnp.float32))
+        slope = up_pre.astype(jnp.float32) * derivative
         grad = product * (1.0 / math.sqrt(tokens * size))
         powers = grad * grad
         squares = powers + 1e-30
@@ -503,8 +526,7 @@
         col_factor = 1.0 / jnp.sqrt(col_moment_new)
         update = grad * row_factor[:, None] * col_factor[None, :]
 
-    activated, derivative = gelu_parts(gate_pre.astype(jnp.float32))
-    gate_grad = (hidden_grad * up_pre.astype(jnp.float32) * derivative).astype(jnp.bfloat16)
+    gate_grad = (hidden_grad * slope).astype(jnp.bfloat16)
     up_grad = (hidden_grad * activated).astype(jnp.bfloat16)
     return (update, row_moment_new, col_moment_new, row_mean, gate_grad, up_grad)
 

time: 136 us -> 150 us (1.10)
  Pallas kernels: 24.6 us -> 42.4 us
  waiting for transfers between devices: 67.3 us -> 62.8 us
    pallas_call x2, Pallas kernels: 0.56 us -> 12.2 us  [cut(): pl.pallas_call(kernel, out_shape=[jax.ShapeDtypeStruct(shape, jnp.bfloat1...]
    ppermute x27, waiting for transfers between devices: 67.3 us -> 62.8 us  [flip(): return lax.ppermute(value, axis, [(i, i ^ bits) for i in range(size)])]
    pallas_call x5, Pallas kernels: 14 us -> 18.4 us  [products(): pl.pallas_call(kernel, grid=(steps,), out_shape=[jax.ShapeDtypeStruct((he...]
  transfers between devices with their start and end apart: 27 -> 27, of which waited for: 15 -> 14; matrix products, arithmetic and copies ran while one was open for 3% -> 3% of each run, Pallas kernels for 16% -> 19%
where the time goes in v16:
time: 150 us; the launch traced here: 149 us
  waiting for transfers between devices  62.8 us (42%)
  Pallas kernels  42.4 us (28%)
  starting transfers between devices  33.5 us (22%)
  blocking collectives  4.94 us (3%)
  other arithmetic  4.56 us (3%)
    ppermute x27, waiting for transfers between devices, flip(): return lax.ppermute(value, axis, [(i, i ^ bits) for i in range(size)])  62.8 us
    ppermute x27, starting transfers between devices, flip(): return lax.ppermute(value, axis, [(i, i ^ bits) for i in range(size)])  33.5 us
    pallas_call x5, Pallas kernels, products(): pl.pallas_call(kernel, grid=(steps,), out_shape=[jax.ShapeDtypeStruct((he...  18.4 us
    pallas_call x2, Pallas kernels, cut(): pl.pallas_call(kernel, out_shape=[jax.ShapeDtypeStruct(shape, jnp.bfloat1...  12.2 us
    pallas_call x1, Pallas kernels, first_stage(): pl.pallas_call(kernel, grid=(tokens // step,), out_shape=[jax.ShapeDtypeS...  3.83 us
    convert_element_type x1, other arithmetic, local(): up_grad = (hidden_grad * activated).astype(jnp.bfloat16)  3.79 us
  transfers between devices with their start and end apart: 27, of which 14 were waited for; matrix products, arithmetic and copies ran while one was open for 3% of the time, Pallas kernels for 19%

profile of v16, /device:TPU:0, one launch (start us, length us, event | category | flops | bytes accessed | tf_op | source)
XLA Modules:
  0.0 149.2 jit_solution(7025071285536855950)
XLA Ops:
  0.7 3.0 %collective-permute-start.3 = (bf16[256,2560]{1,0:T(8,128)(2,1)}, bf16[256,2560]{1,0:T(8,128)(2,1)S(1)}, u32[]{:S(2)}, u32[]{:S(2)}) collective-permute-start(bf16[256,2560]{1,0:T(8,128)(2,1)} %refs_5_.1), channel_id=1, source_target_pairs={{0,2},{2,0},{4,6},{6,4},{8,10},{10,8},{12,14},{14,12},{16,18},{18,... | collective-permute-start | bytes 3932168 | tf_op jit(solution)/shard_map/ppermute | solution.py:28
  5.2 3.8 %shard_map.109 = (bf16[128,1024]{1,0:T(8,128)(2,1)}, bf16[128,1280]{1,0:T(8,128)(2,1)}, bf16[128,1792]{1,0:T(8,128)(2,1)}, bf16[128,1792]{1,0:T(8,128)(2,1)}, bf16[128,512]{1,0:T(8,128)(2,1)}) custom-call(bf16[128,4096]{1,0:T(8,128)(2,1)} %source.1, bf16[128,2560]{1,0:T(8,128)(2,1)} %gate.3, bf16[128,2560]{1,0:T(8,128)(2,1)} %up.3), custom_call_target="tpu_custom_call" | custom-call | tf_op jit(solution)/shard_map/pallas_call | solution.py:116
  10.6 2.6 %collective-permute-start.1 = (bf16[128,1792]{1,0:T(8,128)(2,1)}, bf16[128,1792]{1,0:T(8,128)(2,1)S(1)}, u32[]{:S(2)}, u32[]{:S(2)}) collective-permute-start(bf16[128,1792]{1,0:T(8,128)(2,1)} %get-tuple-element.71), channel_id=1, source_target_pairs={{0,16},{2,18},{4,20},{6,22},{8,24},{10,26},{12,28},{14,30},{16,0},... | collective-permute-start | bytes 1376264 | tf_op jit(solution)/shard_map/ppermute | solution.py:28
  14.5 21.2 %collective-permute-done.2.refs_2_ = bf16[128,512]{1,0:T(8,128)(2,1)S(1)} collective-permute-done((bf16[128,512]{1,0:T(8,128)(2,1)}, bf16[128,512]{1,0:T(8,128)(2,1)S(1)}, u32[]{:S(2)}, u32[]{:S(2)}) %collective-permute-start.2) | collective-permute-done | bytes 131104 | tf_op jit(solution)/shard_map/ppermute | solution.py:28
  37.2 11.1 %shard_map.112 = (bf16[128,2560]{1,0:T(8,128)(2,1)}, bf16[128,1536]{1,0:T(8,128)(2,1)}) custom-call(bf16[128,1792]{1,0:T(8,128)(2,1)S(1)} %collective-permute-done.refs_0_.refs_2_, bf16[128,1792]{1,0:T(8,128)(2,1)S(1)} %collective-permute-done.1.refs_1_.refs_3_, bf16[128,512]{1,0:T(8,128)(2,1)S(1)} %collective-permute-done.2.refs_2_, ...), custom_call_target="tpu_custom_call" | custom-call | tf_op jit(solution)/shard_map/pallas_call | solution.py:162
  48.3 3.2 %collective-permute-start.5 = (bf16[128,2560]{1,0:T(8,128)(2,1)}, bf16[128,2560]{1,0:T(8,128)(2,1)S(1)}, u32[]{:S(2)}, u32[]{:S(2)}) collective-permute-start(bf16[128,2560]{1,0:T(8,128)(2,1)} %get-tuple-element.85), channel_id=1, source_target_pairs={{0,8},{2,10},{4,12},{6,14},{8,0},{10,2},{12,4},{14,6},{16,24},{18,... | collective-permute-start | bytes 1966088 | tf_op jit(solution)/shard_map/ppermute | solution.py:28
  55.1 15.7 %collective-permute-done.6.refs_3_ = bf16[128,1280]{1,0:T(8,128)(2,1)} collective-permute-done((bf16[128,1280]{1,0:T(8,128)(2,1)}, bf16[128,1280]{1,0:T(8,128)(2,1)}, u32[]{:S(2)}, u32[]{:S(2)}) %collective-permute-start.6) | collective-permute-done | bytes 327712 | tf_op jit(solution)/shard_map/ppermute | solution.py:28
  71.5 3.1 %collective-permute-start.8 = (bf16[128,1280]{1,0:T(8,128)(2,1)}, bf16[128,1280]{1,0:T(8,128)(2,1)S(1)}, u32[]{:S(2)}, u32[]{:S(2)}) collective-permute-start(bf16[128,1280]{1,0:T(8,128)(2,1)} %collective-permute-done.6.refs_3_), channel_id=1, source_target_pairs={{0,8},{2,10},{4,12},{6,14},{8,0},{10,2},{12,4},{14,6},{16,24},{18,... | collective-permute-start | bytes 983048 | tf_op jit(solution)/shard_map/ppermute | solution.py:28
  74.6 2.1 %shard_map.114 = (bf16[256,1280]{1,0:T(8,128)(2,1)S(1)}, bf16[256,1280]{1,0:T(8,128)(2,1)S(1)}) custom-call(bf16[512,1024]{1,0:T(8,128)(2,1)S(1)} %shard_map.113.refs_0_, bf16[128,1792]{1,0:T(8,128)(2,1)S(1)} %copy-done.7, bf16[128,1792]{1,0:T(8,128)(2,1)S(1)} %copy-done.2, bf16[128,1792]{1,0:T(8,128)(2,1)S(1)} %copy-done.4, ...), custom_call_target="tpu_custom_call" | custom-call | tf_op jit(solution)/shard_map/pallas_call | solution.py:379
  77.8 4.5 %shard_map.115 = (bf16[128,2560]{1,0:T(8,128)(2,1)S(1)}, bf16[128,2560]{1,0:T(8,128)(2,1)S(1)}) custom-call(bf16[512,1024]{1,0:T(8,128)(2,1)S(1)} %shard_map.113.refs_0_, bf16[256,2560]{1,0:T(8,128)(2,1)S(1)} %copy-done, bf16[256,2560]{1,0:T(8,128)(2,1)S(1)} %collective-permute-done.3.refs_0_.refs_2_.refs_6_, ...), custom_call_target="tpu_custom_call" | custom-call | tf_op jit(solution)/shard_map/pallas_call | solution.py:379
  82.3 3.8 %shard_map.116 = (bf16[256,1280]{1,0:T(8,128)(2,1)S(1)}, bf16[256,1280]{1,0:T(8,128)(2,1)S(1)}) custom-call(bf16[512,1024]{1,0:T(8,128)(2,1)S(1)} %shard_map.113.refs_0_, bf16[128,1280]{1,0:T(8,128)(2,1)} %get-tuple-element.84.refs_3_.refs_1_, bf16[128,2560]{1,0:T(8,128)(2,1)S(1)} %collective-permute-done.5.refs_4_.refs_2_, ...), custom_call_target="tpu_custom_call" | custom-call | tf_op jit(solution)/shard_map/pallas_call | solution.py:379
  89.2 4.4 %collective-permute-done.11.refs_2_ = bf16[256,1280]{1,0:T(8,128)(2,1)S(1)} collective-permute-done((bf16[256,1280]{1,0:T(8,128)(2,1)S(1)}, bf16[256,1280]{1,0:T(8,128)(2,1)S(1)}, u32[]{:S(2)}, u32[]{:S(2)}) %collective-permute-start.11) | collective-permute-done | bytes 655392 | tf_op jit(solution)/shard_map/ppermute | solution.py:28
  94.9 2.1 %shard_map.117 = (f32[256,1280]{1,0:T(8,128)S(1)}, f32[128,1280]{1,0:T(8,128)S(1)}, f32[128,1280]{1,0:T(8,128)S(1)}) custom-call(bf16[512,1024]{1,0:T(8,128)(2,1)S(1)} %shard_map.113.refs_0_, bf16[128,1792]{1,0:T(8,128)(2,1)S(1)} %copy-done.7, bf16[128,1792]{1,0:T(8,128)(2,1)S(1)} %copy-done.2, bf16[128,1792]{1,0:T(8,128)(2,1)S(1)} %copy-done.4, ...), custom_call_target="tpu_custom_call" | custom-call | tf_op jit(solution)/shard_map/pallas_call | solution.py:379
  97.0 5.9 %shard_map.118 = (f32[256,1280]{1,0:T(8,128)S(1)}, f32[128,1280]{1,0:T(8,128)S(1)}, f32[128,1280]{1,0:T(8,128)S(1)}, f32[128,2560]{1,0:T(8,128)S(1)}, f32[64,2560]{1,0:T(8,128)S(1)}, /*index=5*/f32[64,2560]{1,0:T(8,128)S(1)}) custom-call(bf16[512,1024]{1,0:T(8,128)(2,1)S(1)} %shard_map.113.refs_0_, bf16[128,1280]{1,0:T(8,128)(2,1)} %get-tuple-element.84.refs_3_.refs_1_, ...), custom_call_target="tpu_custom_call" | custom-call | tf_op jit(solution)/shard_map/pallas_call | solution.py:379
  104.7 2.1 %collective-permute-start.16 = (bf16[128,2560]{1,0:T(8,128)(2,1)S(1)}, bf16[128,2560]{1,0:T(8,128)(2,1)S(1)}, u32[]{:S(2)}, u32[]{:S(2)}) collective-permute-start(bf16[128,2560]{1,0:T(8,128)(2,1)S(1)} %shard_map.120), channel_id=1, source_target_pairs={{0,2},{2,0},{4,6},{6,4},{8,10},{10,8},{12,14},{14,12},{16,18},{18,... | collective-permute-start | bytes 1966088 | tf_op jit(solution)/shard_map/ppermute | solution.py:28
  107.3 8.6 %collective-permute-done.18.refs_1_ = bf16[128,2560]{1,0:T(8,128)(2,1)S(1)} collective-permute-done((bf16[128,2560]{1,0:T(8,128)(2,1)S(1)}, bf16[128,2560]{1,0:T(8,128)(2,1)S(1)}, u32[]{:S(2)}, u32[]{:S(2)}) %collective-permute-start.18) | collective-permute-done | bytes 655392 | tf_op jit(solution)/shard_map/ppermute | solution.py:28
  120.6 2.5 %psum.14.row_sum = f32[1,256]{1,0:T(1,128)S(1)} all-reduce(f32[1,256]{1,0:T(1,128)S(1)} %get-tuple-element.116), channel_id=1, replica_groups=mesh['dp'=16,'mp'=2] {'mp'}, use_global_device_ids=true, to_apply=%region_0.0 | all-reduce | flops 256 | bytes 2048 | tf_op jit(solution)/shard_map/psum | solution.py:480
  124.9 2.4 %collective-permute-start.21 = (f32[5248]{0:T(1024)S(1)}, f32[5248]{0:T(1024)S(1)}, u32[]{:S(2)}, u32[]{:S(2)}) collective-permute-start(f32[5248]{0:T(1024)S(1)} %reduce), channel_id=1, source_target_pairs={{0,6},{2,4},{4,2},{6,0},{8,14},{10,12},{12,10},{14,8},{16,22},{18,... | collective-permute-start | bytes 62984 | tf_op jit(solution)/shard_map/ppermute | solution.py:28
  129.7 2.0 %collective-permute-done.23 = bf16[64,2560]{1,0:T(8,128)(2,1)} collective-permute-done((bf16[64,2560]{1,0:T(8,128)(2,1)}, bf16[64,2560]{1,0:T(8,128)(2,1)}, u32[]{:S(2)}, u32[]{:S(2)}) %collective-permute-start.23) | collective-permute-done | bytes 327712 | tf_op jit(solution)/shard_map/ppermute | solution.py:28
  131.7 3.9 %collective-permute-done.22 = bf16[64,2560]{1,0:T(8,128)(2,1)} collective-permute-done((bf16[64,2560]{1,0:T(8,128)(2,1)}, bf16[64,2560]{1,0:T(8,128)(2,1)}, u32[]{:S(2)}, u32[]{:S(2)}) %collective-permute-start.22) | collective-permute-done | bytes 327712 | tf_op jit(solution)/shard_map/ppermute | solution.py:28
  137.6 2.4 %collective-permute-start.26 = (f32[5248]{0:T(1024)S(1)}, f32[5248]{0:T(1024)S(1)}, u32[]{:S(2)}, u32[]{:S(2)}) collective-permute-start(f32[5248]{0:T(1024)S(1)} %add_add_fusion.1), channel_id=1, source_target_pairs={{0,24},{2,26},{4,28},{6,30},{8,16},{10,18},{12,20},{14,22},{16,8},... | collective-permute-start | bytes 62984 | tf_op jit(solution)/shard_map/ppermute | solution.py:28
  140.0 3.8 %multiply_convert_fusion = (bf16[128,2560]{1,0:T(8,128)(2,1)}, bf16[128,2560]{1,0:T(8,128)(2,1)}) fusion(f32[128,2560]{1,0:T(8,128)} %copy-done.10, bf16[64,2560]{1,0:T(8,128)(2,1)} %collective-permute-done.23, bf16[64,2560]{1,0:T(8,128)(2,1)} %collective-permute-done.22, f32[128,2560]{1,0:T(8,128)} %copy-done.12, bf16[64,2560]{1,0:T(8,128)(2,1)S(1)} %slice-done, ...), kind=kLoop, calls=%fused_computation | loop fusion | flops 4587520 | bytes 6553600 | tf_op jit(solution)/shard_map/convert_element_type | solution.py:530
  143.9 2.5 %psum.15.terms = f32[1,128]{1,0:T(1,128)S(1)} all-reduce(f32[1,128]{1,0:T(1,128)S(1)} %get-tuple-element.124), channel_id=1, replica_groups=mesh['dp'=16,'mp'=2] {'mp'}, use_global_device_ids=true, to_apply=%region_1.0 | all-reduce | flops 128 | bytes 1024 | tf_op jit(solution)/shard_map/psum | solution.py:503
  147.0 2.2 %shard_map.126 = (f32[256,2560]{1,0:T(8,128)}, f32[1,128]{1,0:T(1,128)}) custom-call(f32[256,2560]{1,0:T(8,128)S(1)} %get-tuple-element.115.grad, f32[1,256]{1,0:T(1,128)S(1)} %copy-done.15, f32[1,2560]{1,0:T(1,128)S(1)} %get-tuple-element.123.col_moment_new, f32[1,128]{1,0:T(1,128)S(1)} %psum.15.terms, f32[1,5248]{1,0:T(1,128)S(1)} %broadcast_in_dim.10.sums.row_total), custom_call_target="tpu_custom_call" | custom-call | tf_op jit(solution)/shard_map/pallas_call | solution.py:333
  (96 shorter events, 29.4 us)
Async XLA Ops:
  0.7 35.1 %collective-permute-start.3 = (bf16[256,2560]{1,0:T(8,128)(2,1)}, bf16[256,2560]{1,0:T(8,128)(2,1)S(1)}, u32[]{:S(2)}, u32[]{:S(2)}) collective-permute-start(bf16[256,2560]{1,0:T(8,128)(2,1)} %refs_5_.1), channel_id=1, source_target_pairs={{0,2},{2,0},{4,6},{6,4},{8,10},{10,8},{12,14},{14,12},{16,18},{18,... | collective-permute-start | bytes 3932168 | tf_op jit(solution)/shard_map/ppermute | solution.py:28
  3.7 32.1 %collective-permute-start.4 = (bf16[256,2560]{1,0:T(8,128)(2,1)}, bf16[256,2560]{1,0:T(8,128)(2,1)S(1)}, u32[]{:S(2)}, u32[]{:S(2)}) collective-permute-start(bf16[256,2560]{1,0:T(8,128)(2,1)} %refs_5_.1), channel_id=1, source_target_pairs={{0,4},{2,6},{4,0},{6,2},{8,12},{10,14},{12,8},{14,10},{16,20},{18,... | collective-permute-start | bytes 3932168 | tf_op jit(solution)/shard_map/ppermute | solution.py:28
  9.0 27.8 %collective-permute-start = (bf16[128,1792]{1,0:T(8,128)(2,1)}, bf16[128,1792]{1,0:T(8,128)(2,1)S(1)}, u32[]{:S(2)}, u32[]{:S(2)}) collective-permute-start(bf16[128,1792]{1,0:T(8,128)(2,1)} %get-tuple-element.70.refs_1_), channel_id=1, source_target_pairs={{0,8},{2,10},{4,12},{6,14},{8,0},{10,2},{12,4},{14,6},{16,24},{18,... | collective-permute-start | bytes 1376264 | tf_op jit(solution)/shard_map/ppermute | solution.py:28
  10.6 26.6 %collective-permute-start.1 = (bf16[128,1792]{1,0:T(8,128)(2,1)}, bf16[128,1792]{1,0:T(8,128)(2,1)S(1)}, u32[]{:S(2)}, u32[]{:S(2)}) collective-permute-start(bf16[128,1792]{1,0:T(8,128)(2,1)} %get-tuple-element.71), channel_id=1, source_target_pairs={{0,16},{2,18},{4,20},{6,22},{8,24},{10,26},{12,28},{14,30},{16,0},... | collective-permute-start | bytes 1376264 | tf_op jit(solution)/shard_map/ppermute | solution.py:28
  13.2 22.5 %collective-permute-start.2 = (bf16[128,512]{1,0:T(8,128)(2,1)}, bf16[128,512]{1,0:T(8,128)(2,1)S(1)}, u32[]{:S(2)}, u32[]{:S(2)}) collective-permute-start(bf16[128,512]{1,0:T(8,128)(2,1)} %get-tuple-element.72), channel_id=1, source_target_pairs={{0,24},{2,26},{4,28},{6,30},{8,16},{10,18},{12,20},{14,22},{16,8},... | collective-permute-start | bytes 393224 | tf_op jit(solution)/shard_map/ppermute | solution.py:28
  48.3 23.2 %collective-permute-start.5 = (bf16[128,2560]{1,0:T(8,128)(2,1)}, bf16[128,2560]{1,0:T(8,128)(2,1)S(1)}, u32[]{:S(2)}, u32[]{:S(2)}) collective-permute-start(bf16[128,2560]{1,0:T(8,128)(2,1)} %get-tuple-element.85), channel_id=1, source_target_pairs={{0,8},{2,10},{4,12},{6,14},{8,0},{10,2},{12,4},{14,6},{16,24},{18,... | collective-permute-start | bytes 1966088 | tf_op jit(solution)/shard_map/ppermute | solution.py:28
  51.5 19.3 %collective-permute-start.6 = (bf16[128,1280]{1,0:T(8,128)(2,1)}, bf16[128,1280]{1,0:T(8,128)(2,1)}, u32[]{:S(2)}, u32[]{:S(2)}) collective-permute-start(bf16[128,1280]{1,0:T(8,128)(2,1)} %get-tuple-element.84.refs_3_.refs_1_), channel_id=1, source_target_pairs={{0,16},{2,18},{4,20},{6,22},{8,24},{10,26},{12,28},{14,30},{16,0},... | collective-permute-start | bytes 983048 | tf_op jit(solution)/shard_map/ppermute | solution.py:28
  52.7 25.1 %collective-permute-start.10 = (bf16[128,2560]{1,0:T(8,128)(2,1)}, bf16[128,2560]{1,0:T(8,128)(2,1)}, u32[]{:S(2)}, u32[]{:S(2)}) collective-permute-start(bf16[128,2560]{1,0:T(8,128)(2,1)} %get-tuple-element.80), channel_id=1, source_target_pairs={{0,2},{2,0},{4,6},{6,4},{8,10},{10,8},{12,14},{14,12},{16,18},{18,... | collective-permute-start | bytes 1966088 | tf_op jit(solution)/shard_map/ppermute | solution.py:28
  53.2 24.5 %collective-permute-start.9 = (bf16[128,2560]{1,0:T(8,128)(2,1)}, bf16[128,2560]{1,0:T(8,128)(2,1)}, u32[]{:S(2)}, u32[]{:S(2)}) collective-permute-start(bf16[128,2560]{1,0:T(8,128)(2,1)} %get-tuple-element.79), channel_id=1, source_target_pairs={{0,4},{2,6},{4,0},{6,2},{8,12},{10,14},{12,8},{14,10},{16,20},{18,... | collective-permute-start | bytes 1966088 | tf_op jit(solution)/shard_map/ppermute | solution.py:28
  71.5 10.8 %collective-permute-start.8 = (bf16[128,1280]{1,0:T(8,128)(2,1)}, bf16[128,1280]{1,0:T(8,128)(2,1)S(1)}, u32[]{:S(2)}, u32[]{:S(2)}) collective-permute-start(bf16[128,1280]{1,0:T(8,128)(2,1)} %collective-permute-done.6.refs_3_), channel_id=1, source_target_pairs={{0,8},{2,10},{4,12},{6,14},{8,0},{10,2},{12,4},{14,6},{16,24},{18,... | collective-permute-start | bytes 983048 | tf_op jit(solution)/shard_map/ppermute | solution.py:28
  76.7 16.9 %collective-permute-start.11 = (bf16[256,1280]{1,0:T(8,128)(2,1)S(1)}, bf16[256,1280]{1,0:T(8,128)(2,1)S(1)}, u32[]{:S(2)}, u32[]{:S(2)}) collective-permute-start(bf16[256,1280]{1,0:T(8,128)(2,1)S(1)} %get-tuple-element.91), channel_id=1, source_target_pairs={{0,2},{2,0},{4,6},{6,4},{8,10},{10,8},{12,14},{14,12},{16,18},{18,... | collective-permute-start | bytes 1966088 | tf_op jit(solution)/shard_map/ppermute | solution.py:28
  77.3 17.7 %collective-permute-start.12 = (bf16[256,1280]{1,0:T(8,128)(2,1)S(1)}, bf16[256,1280]{1,0:T(8,128)(2,1)S(1)}, u32[]{:S(2)}, u32[]{:S(2)}) collective-permute-start(bf16[256,1280]{1,0:T(8,128)(2,1)S(1)} %get-tuple-element.96), channel_id=1, source_target_pairs={{0,4},{2,6},{4,0},{6,2},{8,12},{10,14},{12,8},{14,10},{16,20},{18,... | collective-permute-start | bytes 1966088 | tf_op jit(solution)/shard_map/ppermute | solution.py:28
  86.1 18.5 %collective-permute-start.14 = (bf16[256,1280]{1,0:T(8,128)(2,1)S(1)}, bf16[256,1280]{1,0:T(8,128)(2,1)S(1)}, u32[]{:S(2)}, u32[]{:S(2)}) collective-permute-start(bf16[256,1280]{1,0:T(8,128)(2,1)S(1)} %get-tuple-element.104), channel_id=1, source_target_pairs={{0,4},{2,6},{4,0},{6,2},{8,12},{10,14},{12,8},{14,10},{16,20},{18,... | collective-permute-start | bytes 1966088 | tf_op jit(solution)/shard_map/ppermute | solution.py:28
  87.7 19.2 %collective-permute-start.13 = (bf16[256,1280]{1,0:T(8,128)(2,1)S(1)}, bf16[256,1280]{1,0:T(8,128)(2,1)S(1)}, u32[]{:S(2)}, u32[]{:S(2)}) collective-permute-start(bf16[256,1280]{1,0:T(8,128)(2,1)S(1)} %get-tuple-element.98), channel_id=1, source_target_pairs={{0,2},{2,0},{4,6},{6,4},{8,10},{10,8},{12,14},{14,12},{16,18},{18,... | collective-permute-start | bytes 1966088 | tf_op jit(solution)/shard_map/ppermute | solution.py:28
  89.2 26.7 %collective-permute-start.18 = (bf16[128,2560]{1,0:T(8,128)(2,1)S(1)}, bf16[128,2560]{1,0:T(8,128)(2,1)S(1)}, u32[]{:S(2)}, u32[]{:S(2)}) collective-permute-start(bf16[128,2560]{1,0:T(8,128)(2,1)S(1)} %get-tuple-element.112), channel_id=1, source_target_pairs={{0,16},{2,18},{4,20},{6,22},{8,24},{10,26},{12,28},{14,30},{16,0},... | collective-permute-start | bytes 1966088 | tf_op jit(solution)/shard_map/ppermute | solution.py:28
  93.6 24.2 %collective-permute-start.17 = (bf16[128,2560]{1,0:T(8,128)(2,1)S(1)}, bf16[128,2560]{1,0:T(8,128)(2,1)S(1)}, u32[]{:S(2)}, u32[]{:S(2)}) collective-permute-start(bf16[128,2560]{1,0:T(8,128)(2,1)S(1)} %get-tuple-element.110), channel_id=1, source_target_pairs={{0,8},{2,10},{4,12},{6,14},{8,0},{10,2},{12,4},{14,6},{16,24},{18,... | collective-permute-start | bytes 1966088 | tf_op jit(solution)/shard_map/ppermute | solution.py:28
  104.7 15.1 %collective-permute-start.16 = (bf16[128,2560]{1,0:T(8,128)(2,1)S(1)}, bf16[128,2560]{1,0:T(8,128)(2,1)S(1)}, u32[]{:S(2)}, u32[]{:S(2)}) collective-permute-start(bf16[128,2560]{1,0:T(8,128)(2,1)S(1)} %shard_map.120), channel_id=1, source_target_pairs={{0,2},{2,0},{4,6},{6,4},{8,10},{10,8},{12,14},{14,12},{16,18},{18,... | collective-permute-start | bytes 1966088 | tf_op jit(solution)/shard_map/ppermute | solution.py:28
  107.0 12.8 %collective-permute-start.15 = (bf16[128,2560]{1,0:T(8,128)(2,1)S(1)}, bf16[128,2560]{1,0:T(8,128)(2,1)S(1)}, u32[]{:S(2)}, u32[]{:S(2)}) collective-permute-start(bf16[128,2560]{1,0:T(8,128)(2,1)S(1)} %shard_map.119), channel_id=1, source_target_pairs={{0,4},{2,6},{4,0},{6,2},{8,12},{10,14},{12,8},{14,10},{16,20},{18,... | collective-permute-start | bytes 1966088 | tf_op jit(solution)/shard_map/ppermute | solution.py:28
  116.8 14.9 %collective-permute-start.23 = (bf16[64,2560]{1,0:T(8,128)(2,1)}, bf16[64,2560]{1,0:T(8,128)(2,1)}, u32[]{:S(2)}, u32[]{:S(2)}) collective-permute-start(bf16[64,2560]{1,0:T(8,128)(2,1)} %shard_map.122), channel_id=1, source_target_pairs={{0,8},{2,10},{4,12},{6,14},{8,0},{10,2},{12,4},{14,6},{16,24},{18,... | collective-permute-start | bytes 983048 | tf_op jit(solution)/shard_map/ppermute | solution.py:28
  118.7 17.0 %collective-permute-start.22 = (bf16[64,2560]{1,0:T(8,128)(2,1)}, bf16[64,2560]{1,0:T(8,128)(2,1)}, u32[]{:S(2)}, u32[]{:S(2)}) collective-permute-start(bf16[64,2560]{1,0:T(8,128)(2,1)} %shard_map.121), channel_id=1, source_target_pairs={{0,16},{2,18},{4,20},{6,22},{8,24},{10,26},{12,28},{14,30},{16,0},... | collective-permute-start | bytes 983048 | tf_op jit(solution)/shard_map/ppermute | solution.py:28
  124.9 4.7 %collective-permute-start.21 = (f32[5248]{0:T(1024)S(1)}, f32[5248]{0:T(1024)S(1)}, u32[]{:S(2)}, u32[]{:S(2)}) collective-permute-start(f32[5248]{0:T(1024)S(1)} %reduce), channel_id=1, source_target_pairs={{0,6},{2,4},{4,2},{6,0},{8,14},{10,12},{12,10},{14,8},{16,22},{18,... | collective-permute-start | bytes 62984 | tf_op jit(solution)/shard_map/ppermute | solution.py:28
  135.6 8.2 %collective-permute-start.24 = (f32[5248]{0:T(1024)S(1)}, f32[5248]{0:T(1024)S(1)}, u32[]{:S(2)}, u32[]{:S(2)}) collective-permute-start(f32[5248]{0:T(1024)S(1)} %add_add_fusion.1), channel_id=1, source_target_pairs={{0,8},{2,10},{4,12},{6,14},{8,0},{10,2},{12,4},{14,6},{16,24},{18,... | collective-permute-start | bytes 62984 | tf_op jit(solution)/shard_map/ppermute | solution.py:28
  135.6 8.2 %collective-permute-start.25 = (f32[5248]{0:T(1024)S(1)}, f32[5248]{0:T(1024)S(1)}, u32[]{:S(2)}, u32[]{:S(2)}) collective-permute-start(f32[5248]{0:T(1024)S(1)} %add_add_fusion.1), channel_id=1, source_target_pairs={{0,16},{2,18},{4,20},{6,22},{8,24},{10,26},{12,28},{14,30},{16,0},... | collective-permute-start | bytes 62984 | tf_op jit(solution)/shard_map/ppermute | solution.py:28
  137.6 6.2 %collective-permute-start.26 = (f32[5248]{0:T(1024)S(1)}, f32[5248]{0:T(1024)S(1)}, u32[]{:S(2)}, u32[]{:S(2)}) collective-permute-start(f32[5248]{0:T(1024)S(1)} %add_add_fusion.1), channel_id=1, source_target_pairs={{0,24},{2,26},{4,28},{6,30},{8,16},{10,18},{12,20},{14,22},{16,8},... | collective-permute-start | bytes 62984 | tf_op jit(solution)/shard_map/ppermute | solution.py:28
  (22 other events, 263.9 us)

commit v17 on v15

--- a/solution.py
+++ b/solution.py
@@ -90,13 +90,13 @@
     return product, hidden_grad
 
 
-def first_stage(out_grad, gate_pre, up_pre, place, rows):
+def first_stage(out_grad, gate_pre, up_pre, rows):
     tokens, units = gate_pre.shape
     half = units // 2
     step = 32
 
-    def kernel(place, source, gate, up, own, right, message1, message2, message3):
-        me, core = place[0], place[1]
+    def kernel(source, gate, up, own, right, message1, message2, message3):
+        me, core = lax.axis_index("dp"), lax.axis_index("mp")
 
         def block(k, j):
             return pl.ds(pl.multiple_of((me ^ (4 * k + j)) * rows, rows), rows)
@@ -104,25 +104,24 @@
         activated, _ = gelu_parts(gate[...].astype(jnp.float32))
         value = (activated * up[...].astype(jnp.float32)).astype(jnp.bfloat16)
         right[...] = value[:, half:]
-        message1[:, :half] = value[:, :half]
+        message1[:, :units] = value
         message2[:, :half] = value[:, :half]
         for j in range(4):
             own[:, j * rows : (j + 1) * rows] = source[:, block(0, j)]
-        for k, target, base in ((1, message1, half), (2, message2, half), (3, message3, 0)):
+        for k, target, base in ((1, message1, units), (2, message2, half), (3, message3, 0)):
             for j in range(2):
                 target[:, base + j * rows : base + (j + 1) * rows] = source[:, block(k, 2 * core + j)]
 
-    widths = [4 * rows, units - half, half + 2 * rows, half + 2 * rows, 2 * rows]
+    widths = [4 * rows, units - half, units + 2 * rows, half + 2 * rows, 2 * rows]
     return pl.pallas_call(
         kernel,
         grid=(tokens // step,),
         out_shape=[jax.ShapeDtypeStruct((tokens, width), jnp.bfloat16) for width in widths],
-        in_specs=[pl.BlockSpec(memory_space=pltpu.SMEM)]
-        + [pl.BlockSpec((step, array.shape[1]), lambda i: (i, 0)) for array in (out_grad, gate_pre, up_pre)],
+        in_specs=[pl.BlockSpec((step, array.shape[1]), lambda i: (i, 0)) for array in (out_grad, gate_pre, up_pre)],
         out_specs=[pl.BlockSpec((step, width), lambda i: (i, 0)) for width in widths],
         compiler_params=pltpu.CompilerParams(vmem_limit_bytes=56 << 20),
         cost_estimate=EAGER,
-    )(place, out_grad, gate_pre, up_pre)
+    )(out_grad, gate_pre, up_pre)
 
 
 def cut(sources, parts, shapes):
@@ -384,27 +383,25 @@
     split = units // 2
     barrier = lax.optimization_barrier
     place = jnp.stack([me, core]).astype(jnp.int32)
-    own, right, message1, message2, message3 = first_stage(out_grad, gate_pre, up_pre, place, rows)
-
-    extra, every, whole = (split, 2 * rows), (0, tokens), (0, units)
-    left1, left2, message3 = flip(message1, z_bit), flip(message2, w_bit), flip(message3, z_bit | w_bit)
+    own, right, message1, message2, message3 = first_stage(out_grad, gate_pre, up_pre, rows)
+
+    every, whole = (0, tokens), (0, units)
+    near, left2, message3 = flip(message1, z_bit), flip(message2, w_bit), flip(message3, z_bit | w_bit)
     weight1, weight2 = flip(down_weight, x_bit), flip(down_weight, y_bit)
-    message3, weight1, weight2 = barrier((message3, weight1, weight2))
     to_y, to_x = cut([weight1, weight2], [(0, (0, q), whole, 0, 0), (1, (q, q), whole, 1, 0)], [(q, units)] * 2)
     weight3a, weight3b = flip(to_y, y_bit), flip(to_x, x_bit)
-    left1, left2, message3, right, _, _ = barrier((left1, left2, message3, right, to_y, to_x))
+    near, left2, message3, right = barrier((near, left2, message3, right))
     to_z, mine = cut(
-        [left1, left2, message3, right],
+        [near, left2, message3],
         [
             (1, every, (0, split), 0, 0),
-            (3, every, (0, units - split), 0, split),
-            (0, every, extra, 1, 0),
-            (1, every, extra, 1, 2 * rows),
+            (0, every, (units, 2 * rows), 1, 0),
+            (1, every, (split, 2 * rows), 1, 2 * rows),
             (2, every, (0, 2 * rows), 1, 4 * rows),
         ],
-        [(tokens, units), (tokens, 6 * rows)],
+        [(tokens, split), (tokens, 6 * rows)],
     )
-    from_near = flip(to_z, z_bit)
+    left3 = flip(to_z, z_bit)
     right2 = flip(right, w_bit)
     theirs = flip(mine, 1, "mp")
     share = assemble(own, mine, theirs, place, rows)
@@ -422,9 +419,9 @@
         ranges = [(0, 2 * size)], [(4 * size, 5 * size)], [(3 * size, 4 * size)]
         return [(r, jnp.float32) for r in ranges]
 
-    from_near, right2, share = barrier((from_near, right2, share))
+    left3, right2, share = barrier((left3, right2, share))
     right3 = flip(right2, z_bit)
-    lefts = [(message1, 0), (left1, 0), (left2, 0), (from_near, 0)]
+    lefts = [(message1, 0), (near, 0), (left2, 0), (left3, 0)]
     left_to_x, left_to_y = products(share, [(lefts, split, sent(q), True)], steps)
     left_from_x, left_from_y = flip(left_to_x, x_bit), flip(left_to_y, y_bit)
 
@@ -435,7 +432,7 @@
     )
     right3, share, to_w, to_z = barrier((right3, share, to_w, to_z))
     from_w, from_z = flip(to_w, w_bit), flip(to_z, z_bit)
-    rights = [(right, 0), (from_near, split), (right2, 0), (right3, 0)]
+    rights = [(right, 0), (near, split), (right2, 0), (right3, 0)]
     right_to_x, right_to_y = products(share, [(rights, units - split, sent(q), True)], steps)
     right_from_x, right_from_y = flip(right_to_x, x_bit), flip(right_to_y, y_bit)
     share, left_from_x, left_from_y, _ = barrier((share, left_from_x, left_from_y, right_to_x))

time: 136 us -> 143 us (1.051)
  Pallas kernels: 24.6 us -> 34.5 us
  waiting for transfers between devices: 67.3 us -> 63.3 us
    pallas_call x5, Pallas kernels: 14 us -> 21.8 us  [products(): pl.pallas_call(kernel, grid=(steps,), out_shape=[jax.ShapeDtypeStruct((he...]
    ppermute x27, waiting for transfers between devices: 67.3 us -> 63.3 us  [flip(): return lax.ppermute(value, axis, [(i, i ^ bits) for i in range(size)])]
    pallas_call x2, Pallas kernels: 0.56 us -> 1.99 us  [cut(): pl.pallas_call(kernel, out_shape=[jax.ShapeDtypeStruct(shape, jnp.bfloat1...]
  transfers between devices with their start and end apart: 27 -> 27, of which waited for: 15 -> 14; matrix products, arithmetic and copies ran while one was open for 3% -> 3% of each run, Pallas kernels for 16% -> 23%
where the time goes in v17:
time: 143 us; the launch traced here: 142 us
  waiting for transfers between devices  63.3 us (44%)
  Pallas kernels  34.5 us (24%)
  starting transfers between devices  32.1 us (22%)
  blocking collectives  4.95 us (3%)
  other arithmetic  4.73 us (3%)
    ppermute x27, waiting for transfers between devices, flip(): return lax.ppermute(value, axis, [(i, i ^ bits) for i in range(size)])  63.3 us
    ppermute x27, starting transfers between devices, flip(): return lax.ppermute(value, axis, [(i, i ^ bits) for i in range(size)])  32.1 us
    pallas_call x5, Pallas kernels, products(): pl.pallas_call(kernel, grid=(steps,), out_shape=[jax.ShapeDtypeStruct((he...  21.8 us
    convert_element_type x1, other arithmetic, local(): up_grad = (hidden_grad * activated).astype(jnp.bfloat16)  3.96 us
    pallas_call x1, Pallas kernels, first_stage(): pl.pallas_call(kernel, grid=(tokens // step,), out_shape=[jax.ShapeDtypeS...  3.89 us
  transfers between devices with their start and end apart: 27, of which 14 were waited for; matrix products, arithmetic and copies ran while one was open for 3% of the time, Pallas kernels for 23%

profile of v17, /device:TPU:0, one launch (start us, length us, event | category | flops | bytes accessed | tf_op | source)
XLA Modules:
  0.0 141.6 jit_solution(11339112976658871044)
XLA Ops:
  0.6 3.0 %collective-permute-start.7 = (bf16[256,2560]{1,0:T(8,128)(2,1)}, bf16[256,2560]{1,0:T(8,128)(2,1)S(1)}, u32[]{:S(2)}, u32[]{:S(2)}) collective-permute-start(bf16[256,2560]{1,0:T(8,128)(2,1)} %refs_5_.1), channel_id=1, source_target_pairs={{0,2},{2,0},{4,6},{6,4},{8,10},{10,8},{12,14},{14,12},{16,18},{18,... | collective-permute-start | bytes 3932168 | tf_op jit(solution)/shard_map/ppermute | solution.py:28
  5.2 3.9 %shard_map.109 = (bf16[128,1024]{1,0:T(8,128)(2,1)}, bf16[128,1280]{1,0:T(8,128)(2,1)}, bf16[128,3072]{1,0:T(8,128)(2,1)}, bf16[128,1792]{1,0:T(8,128)(2,1)}, bf16[128,512]{1,0:T(8,128)(2,1)}) custom-call(bf16[128,4096]{1,0:T(8,128)(2,1)} %source.1, bf16[128,2560]{1,0:T(8,128)(2,1)} %gate.1, bf16[128,2560]{1,0:T(8,128)(2,1)} %up.1), custom_call_target="tpu_custom_call" | custom-call | tf_op jit(solution)/shard_map/pallas_call | solution.py:116
  9.0 1.6 %collective-permute-start = (bf16[128,3072]{1,0:T(8,128)(2,1)}, bf16[128,3072]{1,0:T(8,128)(2,1)S(1)}, u32[]{:S(2)}, u32[]{:S(2)}) collective-permute-start(bf16[128,3072]{1,0:T(8,128)(2,1)} %get-tuple-element.61.refs_1_), channel_id=1, source_target_pairs={{0,8},{2,10},{4,12},{6,14},{8,0},{10,2},{12,4},{14,6},{16,24},{18,... | collective-permute-start | bytes 2359304 | tf_op jit(solution)/shard_map/ppermute | solution.py:28
  10.6 2.6 %collective-permute-start.1 = (bf16[128,1792]{1,0:T(8,128)(2,1)}, bf16[128,1792]{1,0:T(8,128)(2,1)S(1)}, u32[]{:S(2)}, u32[]{:S(2)}) collective-permute-start(bf16[128,1792]{1,0:T(8,128)(2,1)} %get-tuple-element.62), channel_id=1, source_target_pairs={{0,16},{2,18},{4,20},{6,22},{8,24},{10,26},{12,28},{14,30},{16,0},... | collective-permute-start | bytes 1376264 | tf_op jit(solution)/shard_map/ppermute | solution.py:28
  13.4 29.2 %collective-permute-done.2.refs_2_ = bf16[128,512]{1,0:T(8,128)(2,1)S(1)} collective-permute-done((bf16[128,512]{1,0:T(8,128)(2,1)}, bf16[128,512]{1,0:T(8,128)(2,1)S(1)}, u32[]{:S(2)}, u32[]{:S(2)}) %collective-permute-start.2) | collective-permute-done | bytes 131104 | tf_op jit(solution)/shard_map/ppermute | solution.py:28
  43.8 2.2 %collective-permute-start.4 = (bf16[128,1280]{1,0:T(8,128)(2,1)}, bf16[128,1280]{1,0:T(8,128)(2,1)}, u32[]{:S(2)}, u32[]{:S(2)}) collective-permute-start(bf16[128,1280]{1,0:T(8,128)(2,1)} %get-tuple-element.69.refs_1_), channel_id=1, source_target_pairs={{0,16},{2,18},{4,20},{6,22},{8,24},{10,26},{12,28},{14,30},{16,0},... | collective-permute-start | bytes 983048 | tf_op jit(solution)/shard_map/ppermute | solution.py:28
  50.4 9.7 %collective-permute-done.3.refs_4_ = bf16[128,1280]{1,0:T(8,128)(2,1)} collective-permute-done((bf16[128,1280]{1,0:T(8,128)(2,1)}, bf16[128,1280]{1,0:T(8,128)(2,1)}, u32[]{:S(2)}, u32[]{:S(2)}) %collective-permute-start.3) | collective-permute-done | bytes 327712 | tf_op jit(solution)/shard_map/ppermute | solution.py:28
  60.2 1.9 %collective-permute-done.4.refs_3_ = bf16[128,1280]{1,0:T(8,128)(2,1)} collective-permute-done((bf16[128,1280]{1,0:T(8,128)(2,1)}, bf16[128,1280]{1,0:T(8,128)(2,1)}, u32[]{:S(2)}, u32[]{:S(2)}) %collective-permute-start.4) | collective-permute-done | bytes 327712 | tf_op jit(solution)/shard_map/ppermute | solution.py:28
  62.1 3.8 %shard_map.112 = (bf16[256,1280]{1,0:T(8,128)(2,1)S(1)}, bf16[256,1280]{1,0:T(8,128)(2,1)S(1)}) custom-call(bf16[512,1024]{1,0:T(8,128)(2,1)S(1)} %shard_map.111.refs_0_, bf16[128,3072]{1,0:T(8,128)(2,1)S(1)} %copy-done.3, bf16[128,3072]{1,0:T(8,128)(2,1)S(1)} %collective-permute-done.refs_0_.refs_2_, bf16[128,1792]{1,0:T(8,128)(2,1)S(1)} %copy-done.2, ...), custom_call_target="tpu_custom_call" | custom-call | tf_op jit(solution)/shard_map/pallas_call | solution.py:358
  67.0 4.5 %shard_map.114 = (bf16[128,2560]{1,0:T(8,128)(2,1)S(1)}, bf16[128,2560]{1,0:T(8,128)(2,1)S(1)}) custom-call(bf16[512,1024]{1,0:T(8,128)(2,1)S(1)} %shard_map.111.refs_0_, bf16[256,2560]{1,0:T(8,128)(2,1)S(1)} %copy-done, bf16[256,2560]{1,0:T(8,128)(2,1)S(1)} %collective-permute-done.7.refs_0_.refs_2_.refs_6_, ...), custom_call_target="tpu_custom_call" | custom-call | tf_op jit(solution)/shard_map/pallas_call | solution.py:358
  71.5 3.8 %shard_map.115 = (bf16[256,1280]{1,0:T(8,128)(2,1)S(1)}, bf16[256,1280]{1,0:T(8,128)(2,1)S(1)}) custom-call(bf16[512,1024]{1,0:T(8,128)(2,1)S(1)} %shard_map.111.refs_0_, bf16[128,1280]{1,0:T(8,128)(2,1)} %get-tuple-element.69.refs_1_, bf16[128,3072]{1,0:T(8,128)(2,1)S(1)} %collective-permute-done.refs_0_.refs_2_, ...), custom_call_target="tpu_custom_call" | custom-call | tf_op jit(solution)/shard_map/pallas_call | solution.py:358
  78.4 2.1 %collective-permute-start.18 = (bf16[128,2560]{1,0:T(8,128)(2,1)S(1)}, bf16[128,2560]{1,0:T(8,128)(2,1)S(1)}, u32[]{:S(2)}, u32[]{:S(2)}) collective-permute-start(bf16[128,2560]{1,0:T(8,128)(2,1)S(1)} %get-tuple-element.98), channel_id=1, source_target_pairs={{0,16},{2,18},{4,20},{6,22},{8,24},{10,26},{12,28},{14,30},{16,0},... | collective-permute-start | bytes 1966088 | tf_op jit(solution)/shard_map/ppermute | solution.py:28
  80.6 3.0 %collective-permute-done.11.refs_2_ = bf16[256,1280]{1,0:T(8,128)(2,1)S(1)} collective-permute-done((bf16[256,1280]{1,0:T(8,128)(2,1)S(1)}, bf16[256,1280]{1,0:T(8,128)(2,1)S(1)}, u32[]{:S(2)}, u32[]{:S(2)}) %collective-permute-start.11) | collective-permute-done | bytes 655392 | tf_op jit(solution)/shard_map/ppermute | solution.py:28
  83.6 2.0 %collective-permute-start.17 = (bf16[128,2560]{1,0:T(8,128)(2,1)S(1)}, bf16[128,2560]{1,0:T(8,128)(2,1)S(1)}, u32[]{:S(2)}, u32[]{:S(2)}) collective-permute-start(bf16[128,2560]{1,0:T(8,128)(2,1)S(1)} %get-tuple-element.96), channel_id=1, source_target_pairs={{0,8},{2,10},{4,12},{6,14},{8,0},{10,2},{12,4},{14,6},{16,24},{18,... | collective-permute-start | bytes 1966088 | tf_op jit(solution)/shard_map/ppermute | solution.py:28
  85.6 3.8 %shard_map.116 = (f32[256,1280]{1,0:T(8,128)S(1)}, f32[128,1280]{1,0:T(8,128)S(1)}, f32[128,1280]{1,0:T(8,128)S(1)}) custom-call(bf16[512,1024]{1,0:T(8,128)(2,1)S(1)} %shard_map.111.refs_0_, bf16[128,3072]{1,0:T(8,128)(2,1)S(1)} %copy-done.3, bf16[128,3072]{1,0:T(8,128)(2,1)S(1)} %collective-permute-done.refs_0_.refs_2_, bf16[128,1792]{1,0:T(8,128)(2,1)S(1)} %copy-done.2, ...), custom_call_target="tpu_custom_call" | custom-call | tf_op jit(solution)/shard_map/pallas_call | solution.py:358
  89.4 6.0 %shard_map.117 = (f32[256,1280]{1,0:T(8,128)S(1)}, f32[128,1280]{1,0:T(8,128)S(1)}, f32[128,1280]{1,0:T(8,128)S(1)}, f32[128,2560]{1,0:T(8,128)S(1)}, f32[64,2560]{1,0:T(8,128)S(1)}, /*index=5*/f32[64,2560]{1,0:T(8,128)S(1)}) custom-call(bf16[512,1024]{1,0:T(8,128)(2,1)S(1)} %shard_map.111.refs_0_, bf16[128,1280]{1,0:T(8,128)(2,1)} %get-tuple-element.69.refs_1_, ...), custom_call_target="tpu_custom_call" | custom-call | tf_op jit(solution)/shard_map/pallas_call | solution.py:358
  98.8 9.8 %collective-permute-done.18.refs_1_ = bf16[128,2560]{1,0:T(8,128)(2,1)S(1)} collective-permute-done((bf16[128,2560]{1,0:T(8,128)(2,1)S(1)}, bf16[128,2560]{1,0:T(8,128)(2,1)S(1)}, u32[]{:S(2)}, u32[]{:S(2)}) %collective-permute-start.18) | collective-permute-done | bytes 655392 | tf_op jit(solution)/shard_map/ppermute | solution.py:28
  113.7 2.5 %psum.14.row_sum = f32[1,256]{1,0:T(1,128)S(1)} all-reduce(f32[1,256]{1,0:T(1,128)S(1)} %get-tuple-element.102), channel_id=1, replica_groups=mesh['dp'=16,'mp'=2] {'mp'}, use_global_device_ids=true, to_apply=%region_0.0 | all-reduce | flops 256 | bytes 2048 | tf_op jit(solution)/shard_map/psum | solution.py:456
  118.1 2.4 %collective-permute-start.21 = (f32[5248]{0:T(1024)S(1)}, f32[5248]{0:T(1024)S(1)}, u32[]{:S(2)}, u32[]{:S(2)}) collective-permute-start(f32[5248]{0:T(1024)S(1)} %reduce), channel_id=1, source_target_pairs={{0,6},{2,4},{4,2},{6,0},{8,14},{10,12},{12,10},{14,8},{16,22},{18,... | collective-permute-start | bytes 62984 | tf_op jit(solution)/shard_map/ppermute | solution.py:28
  124.0 3.4 %collective-permute-done.22 = bf16[64,2560]{1,0:T(8,128)(2,1)} collective-permute-done((bf16[64,2560]{1,0:T(8,128)(2,1)}, bf16[64,2560]{1,0:T(8,128)(2,1)}, u32[]{:S(2)}, u32[]{:S(2)}) %collective-permute-start.22) | collective-permute-done | bytes 327712 | tf_op jit(solution)/shard_map/ppermute | solution.py:28
  127.4 3.2 %collective-permute-start.25 = (f32[5248]{0:T(1024)S(1)}, f32[5248]{0:T(1024)S(1)}, u32[]{:S(2)}, u32[]{:S(2)}) collective-permute-start(f32[5248]{0:T(1024)S(1)} %add_add_fusion.1), channel_id=1, source_target_pairs={{0,16},{2,18},{4,20},{6,22},{8,24},{10,26},{12,28},{14,30},{16,0},... | collective-permute-start | bytes 62984 | tf_op jit(solution)/shard_map/ppermute | solution.py:28
  131.8 4.0 %fusion.8 = (bf16[128,2560]{1,0:T(8,128)(2,1)}, bf16[128,2560]{1,0:T(8,128)(2,1)}) fusion(bf16[128,2560]{1,0:T(8,128)(2,1)S(1)} %copy-done.10, bf16[64,2560]{1,0:T(8,128)(2,1)} %collective-permute-done.23, bf16[64,2560]{1,0:T(8,128)(2,1)} %collective-permute-done.22, f32[128,2560]{1,0:T(8,128)} %copy-done.6, bf16[64,2560]{1,0:T(8,128)(2,1)S(1)} %slice-done, ...), kind=kLoop, calls=%fused_computation.15 | loop fusion | flops 11468800 | bytes 5242880 | tf_op jit(solution)/shard_map/convert_element_type | solution.py:505
  136.3 2.5 %psum.15.terms = f32[1,128]{1,0:T(1,128)S(1)} all-reduce(f32[1,128]{1,0:T(1,128)S(1)} %get-tuple-element.108), channel_id=1, replica_groups=mesh['dp'=16,'mp'=2] {'mp'}, use_global_device_ids=true, to_apply=%region_1.0 | all-reduce | flops 128 | bytes 1024 | tf_op jit(solution)/shard_map/psum | solution.py:479
  139.4 2.2 %shard_map.125 = (f32[256,2560]{1,0:T(8,128)}, f32[1,128]{1,0:T(1,128)}) custom-call(f32[256,2560]{1,0:T(8,128)S(1)} %get-tuple-element.101.grad, f32[1,256]{1,0:T(1,128)S(1)} %copy-done.9, f32[1,2560]{1,0:T(1,128)S(1)} %get-tuple-element.107.col_moment_new, f32[1,128]{1,0:T(1,128)S(1)} %psum.15.terms, f32[1,5248]{1,0:T(1,128)S(1)} %broadcast_in_dim.10.sums.row_total), custom_call_target="tpu_custom_call" | custom-call | tf_op jit(solution)/shard_map/pallas_call | solution.py:312
  (85 shorter events, 27.7 us)
Async XLA Ops:
  0.6 45.3 %collective-permute-start.7 = (bf16[256,2560]{1,0:T(8,128)(2,1)}, bf16[256,2560]{1,0:T(8,128)(2,1)S(1)}, u32[]{:S(2)}, u32[]{:S(2)}) collective-permute-start(bf16[256,2560]{1,0:T(8,128)(2,1)} %refs_5_.1), channel_id=1, source_target_pairs={{0,2},{2,0},{4,6},{6,4},{8,10},{10,8},{12,14},{14,12},{16,18},{18,... | collective-permute-start | bytes 3932168 | tf_op jit(solution)/shard_map/ppermute | solution.py:28
  3.6 42.3 %collective-permute-start.8 = (bf16[256,2560]{1,0:T(8,128)(2,1)}, bf16[256,2560]{1,0:T(8,128)(2,1)S(1)}, u32[]{:S(2)}, u32[]{:S(2)}) collective-permute-start(bf16[256,2560]{1,0:T(8,128)(2,1)} %refs_5_.1), channel_id=1, source_target_pairs={{0,4},{2,6},{4,0},{6,2},{8,12},{10,14},{12,8},{14,10},{16,20},{18,... | collective-permute-start | bytes 3932168 | tf_op jit(solution)/shard_map/ppermute | solution.py:28
  9.0 33.6 %collective-permute-start = (bf16[128,3072]{1,0:T(8,128)(2,1)}, bf16[128,3072]{1,0:T(8,128)(2,1)S(1)}, u32[]{:S(2)}, u32[]{:S(2)}) collective-permute-start(bf16[128,3072]{1,0:T(8,128)(2,1)} %get-tuple-element.61.refs_1_), channel_id=1, source_target_pairs={{0,8},{2,10},{4,12},{6,14},{8,0},{10,2},{12,4},{14,6},{16,24},{18,... | collective-permute-start | bytes 2359304 | tf_op jit(solution)/shard_map/ppermute | solution.py:28
  10.6 32.0 %collective-permute-start.1 = (bf16[128,1792]{1,0:T(8,128)(2,1)}, bf16[128,1792]{1,0:T(8,128)(2,1)S(1)}, u32[]{:S(2)}, u32[]{:S(2)}) collective-permute-start(bf16[128,1792]{1,0:T(8,128)(2,1)} %get-tuple-element.62), channel_id=1, source_target_pairs={{0,16},{2,18},{4,20},{6,22},{8,24},{10,26},{12,28},{14,30},{16,0},... | collective-permute-start | bytes 1376264 | tf_op jit(solution)/shard_map/ppermute | solution.py:28
  13.2 29.4 %collective-permute-start.2 = (bf16[128,512]{1,0:T(8,128)(2,1)}, bf16[128,512]{1,0:T(8,128)(2,1)S(1)}, u32[]{:S(2)}, u32[]{:S(2)}) collective-permute-start(bf16[128,512]{1,0:T(8,128)(2,1)} %get-tuple-element.63), channel_id=1, source_target_pairs={{0,24},{2,26},{4,28},{6,30},{8,16},{10,18},{12,20},{14,22},{16,8},... | collective-permute-start | bytes 393224 | tf_op jit(solution)/shard_map/ppermute | solution.py:28
  43.7 16.5 %collective-permute-start.3 = (bf16[128,1280]{1,0:T(8,128)(2,1)}, bf16[128,1280]{1,0:T(8,128)(2,1)}, u32[]{:S(2)}, u32[]{:S(2)}) collective-permute-start(bf16[128,1280]{1,0:T(8,128)(2,1)} %get-tuple-element.68), channel_id=1, source_target_pairs={{0,8},{2,10},{4,12},{6,14},{8,0},{10,2},{12,4},{14,6},{16,24},{18,... | collective-permute-start | bytes 983048 | tf_op jit(solution)/shard_map/ppermute | solution.py:28
  43.8 18.3 %collective-permute-start.4 = (bf16[128,1280]{1,0:T(8,128)(2,1)}, bf16[128,1280]{1,0:T(8,128)(2,1)}, u32[]{:S(2)}, u32[]{:S(2)}) collective-permute-start(bf16[128,1280]{1,0:T(8,128)(2,1)} %get-tuple-element.69.refs_1_), channel_id=1, source_target_pairs={{0,16},{2,18},{4,20},{6,22},{8,24},{10,26},{12,28},{14,30},{16,0},... | collective-permute-start | bytes 983048 | tf_op jit(solution)/shard_map/ppermute | solution.py:28
  47.0 20.0 %collective-permute-start.10 = (bf16[128,2560]{1,0:T(8,128)(2,1)}, bf16[128,2560]{1,0:T(8,128)(2,1)}, u32[]{:S(2)}, u32[]{:S(2)}) collective-permute-start(bf16[128,2560]{1,0:T(8,128)(2,1)} %get-tuple-element.78), channel_id=1, source_target_pairs={{0,2},{2,0},{4,6},{6,4},{8,10},{10,8},{12,14},{14,12},{16,18},{18,... | collective-permute-start | bytes 1966088 | tf_op jit(solution)/shard_map/ppermute | solution.py:28
  47.6 19.4 %collective-permute-start.9 = (bf16[128,2560]{1,0:T(8,128)(2,1)}, bf16[128,2560]{1,0:T(8,128)(2,1)}, u32[]{:S(2)}, u32[]{:S(2)}) collective-permute-start(bf16[128,2560]{1,0:T(8,128)(2,1)} %get-tuple-element.77), channel_id=1, source_target_pairs={{0,4},{2,6},{4,0},{6,2},{8,12},{10,14},{12,8},{14,10},{16,20},{18,... | collective-permute-start | bytes 1966088 | tf_op jit(solution)/shard_map/ppermute | solution.py:28
  62.1 9.4 %collective-permute-start.6 = (bf16[128,1280]{1,0:T(8,128)(2,1)}, bf16[128,1280]{1,0:T(8,128)(2,1)S(1)}, u32[]{:S(2)}, u32[]{:S(2)}) collective-permute-start(bf16[128,1280]{1,0:T(8,128)(2,1)} %collective-permute-done.4.refs_3_), channel_id=1, source_target_pairs={{0,8},{2,10},{4,12},{6,14},{8,0},{10,2},{12,4},{14,6},{16,24},{18,... | collective-permute-start | bytes 983048 | tf_op jit(solution)/shard_map/ppermute | solution.py:28
  65.8 17.7 %collective-permute-start.11 = (bf16[256,1280]{1,0:T(8,128)(2,1)S(1)}, bf16[256,1280]{1,0:T(8,128)(2,1)S(1)}, u32[]{:S(2)}, u32[]{:S(2)}) collective-permute-start(bf16[256,1280]{1,0:T(8,128)(2,1)S(1)} %get-tuple-element.75), channel_id=1, source_target_pairs={{0,2},{2,0},{4,6},{6,4},{8,10},{10,8},{12,14},{14,12},{16,18},{18,... | collective-permute-start | bytes 1966088 | tf_op jit(solution)/shard_map/ppermute | solution.py:28
  66.4 19.1 %collective-permute-start.12 = (bf16[256,1280]{1,0:T(8,128)(2,1)S(1)}, bf16[256,1280]{1,0:T(8,128)(2,1)S(1)}, u32[]{:S(2)}, u32[]{:S(2)}) collective-permute-start(bf16[256,1280]{1,0:T(8,128)(2,1)S(1)} %get-tuple-element.82), channel_id=1, source_target_pairs={{0,4},{2,6},{4,0},{6,2},{8,12},{10,14},{12,8},{14,10},{16,20},{18,... | collective-permute-start | bytes 1966088 | tf_op jit(solution)/shard_map/ppermute | solution.py:28
  75.3 21.1 %collective-permute-start.14 = (bf16[256,1280]{1,0:T(8,128)(2,1)S(1)}, bf16[256,1280]{1,0:T(8,128)(2,1)S(1)}, u32[]{:S(2)}, u32[]{:S(2)}) collective-permute-start(bf16[256,1280]{1,0:T(8,128)(2,1)S(1)} %get-tuple-element.90), channel_id=1, source_target_pairs={{0,4},{2,6},{4,0},{6,2},{8,12},{10,14},{12,8},{14,10},{16,20},{18,... | collective-permute-start | bytes 1966088 | tf_op jit(solution)/shard_map/ppermute | solution.py:28
  76.9 21.2 %collective-permute-start.13 = (bf16[256,1280]{1,0:T(8,128)(2,1)S(1)}, bf16[256,1280]{1,0:T(8,128)(2,1)S(1)}, u32[]{:S(2)}, u32[]{:S(2)}) collective-permute-start(bf16[256,1280]{1,0:T(8,128)(2,1)S(1)} %get-tuple-element.84), channel_id=1, source_target_pairs={{0,2},{2,0},{4,6},{6,4},{8,10},{10,8},{12,14},{14,12},{16,18},{18,... | collective-permute-start | bytes 1966088 | tf_op jit(solution)/shard_map/ppermute | solution.py:28
  78.4 30.1 %collective-permute-start.18 = (bf16[128,2560]{1,0:T(8,128)(2,1)S(1)}, bf16[128,2560]{1,0:T(8,128)(2,1)S(1)}, u32[]{:S(2)}, u32[]{:S(2)}) collective-permute-start(bf16[128,2560]{1,0:T(8,128)(2,1)S(1)} %get-tuple-element.98), channel_id=1, source_target_pairs={{0,16},{2,18},{4,20},{6,22},{8,24},{10,26},{12,28},{14,30},{16,0},... | collective-permute-start | bytes 1966088 | tf_op jit(solution)/shard_map/ppermute | solution.py:28
  83.6 26.6 %collective-permute-start.17 = (bf16[128,2560]{1,0:T(8,128)(2,1)S(1)}, bf16[128,2560]{1,0:T(8,128)(2,1)S(1)}, u32[]{:S(2)}, u32[]{:S(2)}) collective-permute-start(bf16[128,2560]{1,0:T(8,128)(2,1)S(1)} %get-tuple-element.96), channel_id=1, source_target_pairs={{0,8},{2,10},{4,12},{6,14},{8,0},{10,2},{12,4},{14,6},{16,24},{18,... | collective-permute-start | bytes 1966088 | tf_op jit(solution)/shard_map/ppermute | solution.py:28
  96.5 15.9 %collective-permute-start.16 = (bf16[128,2560]{1,0:T(8,128)(2,1)S(1)}, bf16[128,2560]{1,0:T(8,128)(2,1)S(1)}, u32[]{:S(2)}, u32[]{:S(2)}) collective-permute-start(bf16[128,2560]{1,0:T(8,128)(2,1)S(1)} %shard_map.119), channel_id=1, source_target_pairs={{0,2},{2,0},{4,6},{6,4},{8,10},{10,8},{12,14},{14,12},{16,18},{18,... | collective-permute-start | bytes 1966088 | tf_op jit(solution)/shard_map/ppermute | solution.py:28
  98.2 14.8 %collective-permute-start.15 = (bf16[128,2560]{1,0:T(8,128)(2,1)S(1)}, bf16[128,2560]{1,0:T(8,128)(2,1)S(1)}, u32[]{:S(2)}, u32[]{:S(2)}) collective-permute-start(bf16[128,2560]{1,0:T(8,128)(2,1)S(1)} %shard_map.118), channel_id=1, source_target_pairs={{0,4},{2,6},{4,0},{6,2},{8,12},{10,14},{12,8},{14,10},{16,20},{18,... | collective-permute-start | bytes 1966088 | tf_op jit(solution)/shard_map/ppermute | solution.py:28
  109.4 14.6 %collective-permute-start.23 = (bf16[64,2560]{1,0:T(8,128)(2,1)}, bf16[64,2560]{1,0:T(8,128)(2,1)}, u32[]{:S(2)}, u32[]{:S(2)}) collective-permute-start(bf16[64,2560]{1,0:T(8,128)(2,1)} %shard_map.121), channel_id=1, source_target_pairs={{0,8},{2,10},{4,12},{6,14},{8,0},{10,2},{12,4},{14,6},{16,24},{18,... | collective-permute-start | bytes 983048 | tf_op jit(solution)/shard_map/ppermute | solution.py:28
  111.0 16.3 %collective-permute-start.22 = (bf16[64,2560]{1,0:T(8,128)(2,1)}, bf16[64,2560]{1,0:T(8,128)(2,1)}, u32[]{:S(2)}, u32[]{:S(2)}) collective-permute-start(bf16[64,2560]{1,0:T(8,128)(2,1)} %shard_map.120), channel_id=1, source_target_pairs={{0,16},{2,18},{4,20},{6,22},{8,24},{10,26},{12,28},{14,30},{16,0},... | collective-permute-start | bytes 983048 | tf_op jit(solution)/shard_map/ppermute | solution.py:28
  118.1 4.7 %collective-permute-start.21 = (f32[5248]{0:T(1024)S(1)}, f32[5248]{0:T(1024)S(1)}, u32[]{:S(2)}, u32[]{:S(2)}) collective-permute-start(f32[5248]{0:T(1024)S(1)} %reduce), channel_id=1, source_target_pairs={{0,6},{2,4},{4,2},{6,0},{8,14},{10,12},{12,10},{14,8},{16,22},{18,... | collective-permute-start | bytes 62984 | tf_op jit(solution)/shard_map/ppermute | solution.py:28
  127.4 8.4 %collective-permute-start.24 = (f32[5248]{0:T(1024)S(1)}, f32[5248]{0:T(1024)S(1)}, u32[]{:S(2)}, u32[]{:S(2)}) collective-permute-start(f32[5248]{0:T(1024)S(1)} %add_add_fusion.1), channel_id=1, source_target_pairs={{0,8},{2,10},{4,12},{6,14},{8,0},{10,2},{12,4},{14,6},{16,24},{18,... | collective-permute-start | bytes 62984 | tf_op jit(solution)/shard_map/ppermute | solution.py:28
  127.4 8.4 %collective-permute-start.25 = (f32[5248]{0:T(1024)S(1)}, f32[5248]{0:T(1024)S(1)}, u32[]{:S(2)}, u32[]{:S(2)}) collective-permute-start(f32[5248]{0:T(1024)S(1)} %add_add_fusion.1), channel_id=1, source_target_pairs={{0,16},{2,18},{4,20},{6,22},{8,24},{10,26},{12,28},{14,30},{16,0},... | collective-permute-start | bytes 62984 | tf_op jit(solution)/shard_map/ppermute | solution.py:28
  130.6 5.6 %collective-permute-start.26 = (f32[5248]{0:T(1024)S(1)}, f32[5248]{0:T(1024)S(1)}, u32[]{:S(2)}, u32[]{:S(2)}) collective-permute-start(f32[5248]{0:T(1024)S(1)} %add_add_fusion.1), channel_id=1, source_target_pairs={{0,24},{2,26},{4,28},{6,30},{8,16},{10,18},{12,20},{14,22},{16,8},... | collective-permute-start | bytes 62984 | tf_op jit(solution)/shard_map/ppermute | solution.py:28
  (17 other events, 135.0 us)

commit v18 on v15

--- a/solution.py
+++ b/solution.py
@@ -90,13 +90,13 @@
     return product, hidden_grad
 
 
-def first_stage(out_grad, gate_pre, up_pre, place, rows):
+def first_stage(out_grad, gate_pre, up_pre, rows):
     tokens, units = gate_pre.shape
     half = units // 2
     step = 32
 
-    def kernel(place, source, gate, up, own, right, message1, message2, message3):
-        me, core = place[0], place[1]
+    def kernel(source, gate, up, own, right, message1, message2, message3):
+        me, core = lax.axis_index("dp"), lax.axis_index("mp")
 
         def block(k, j):
             return pl.ds(pl.multiple_of((me ^ (4 * k + j)) * rows, rows), rows)
@@ -117,12 +117,11 @@
         kernel,
         grid=(tokens // step,),
         out_shape=[jax.ShapeDtypeStruct((tokens, width), jnp.bfloat16) for width in widths],
-        in_specs=[pl.BlockSpec(memory_space=pltpu.SMEM)]
-        + [pl.BlockSpec((step, array.shape[1]), lambda i: (i, 0)) for array in (out_grad, gate_pre, up_pre)],
+        in_specs=[pl.BlockSpec((step, array.shape[1]), lambda i: (i, 0)) for array in (out_grad, gate_pre, up_pre)],
         out_specs=[pl.BlockSpec((step, width), lambda i: (i, 0)) for width in widths],
         compiler_params=pltpu.CompilerParams(vmem_limit_bytes=56 << 20),
         cost_estimate=EAGER,
-    )(place, out_grad, gate_pre, up_pre)
+    )(out_grad, gate_pre, up_pre)
 
 
 def cut(sources, parts, shapes):
@@ -168,7 +167,7 @@
         out_shape=jax.ShapeDtypeStruct((4 * tokens, 4 * rows), jnp.bfloat16),
         in_specs=[pl.BlockSpec(memory_space=pltpu.SMEM), vmem, vmem, vmem],
         out_specs=vmem,
-        compiler_params=pltpu.CompilerParams(vmem_limit_bytes=8 << 20),
+        compiler_params=pltpu.CompilerParams(vmem_limit_bytes=4 << 20),
         cost_estimate=EAGER,
     )(place, own, mine, theirs)
 
@@ -189,7 +188,7 @@
         out_shape=jax.ShapeDtypeStruct((rows, sum(widths)), jnp.bfloat16),
         in_specs=[vmem] * (2 * len(parts)),
         out_specs=vmem,
-        compiler_params=pltpu.CompilerParams(vmem_limit_bytes=8 << 20),
+        compiler_params=pltpu.CompilerParams(vmem_limit_bytes=4 << 20),
         cost_estimate=EAGER,
     )(*parts, *arrived)
 
@@ -231,7 +230,7 @@
         out_shape=[jax.ShapeDtypeStruct((rows, units), jnp.float32), jax.ShapeDtypeStruct((1, rows), jnp.float32)],
         in_specs=[vmem] * 8,
         out_specs=[vmem] * 2,
-        compiler_params=pltpu.CompilerParams(vmem_limit_bytes=14 << 20),
+        compiler_params=pltpu.CompilerParams(vmem_limit_bytes=10 << 20),
         cost_estimate=EAGER,
     )(*kept, *from_low, *from_high, last_a, last_b)
 
@@ -264,7 +263,7 @@
         ],
         in_specs=[vmem] * 3,
         out_specs=[vmem] * 2,
-        compiler_params=pltpu.CompilerParams(vmem_limit_bytes=14 << 20),
+        compiler_params=pltpu.CompilerParams(vmem_limit_bytes=5 << 20),
         cost_estimate=EAGER,
     )(grad, row_sum, row_moment)
 
@@ -287,7 +286,7 @@
         out_shape=[jax.ShapeDtypeStruct((1, units), jnp.float32), jax.ShapeDtypeStruct((1, 128), jnp.float32)],
         in_specs=[vmem] * 2,
         out_specs=[vmem] * 2,
-        compiler_params=pltpu.CompilerParams(vmem_limit_bytes=4 << 20),
+        compiler_params=pltpu.CompilerParams(vmem_limit_bytes=2 << 20),
         cost_estimate=EAGER,
     )(sums, col_moment)
 
@@ -322,7 +321,7 @@
             fixed(128, 2 * units // 128),
         ],
         out_specs=[pl.BlockSpec((rows, tile), lambda i: (0, i)), fixed(128)],
-        compiler_params=pltpu.CompilerParams(vmem_limit_bytes=14 << 20),
+        compiler_params=pltpu.CompilerParams(vmem_limit_bytes=7 << 20),
         cost_estimate=EAGER,
     )(grad, row_moment_new, col_moment_new, terms, sums)
 
@@ -369,7 +368,7 @@
         scratch_shapes=[
             pltpu.VMEM((sum(piece.shape[0] for piece, _ in group[0]), group[1] // steps), jnp.bfloat16) for group in groups
         ],
-        compiler_params=pltpu.CompilerParams(vmem_limit_bytes=14 << 20),
+        compiler_params=pltpu.CompilerParams(vmem_limit_bytes=9 << 20),
         cost_estimate=EAGER,
     )(share, *[piece for (piece, _), _ in pieces])
 
@@ -384,15 +383,14 @@
     split = units // 2
     barrier = lax.optimization_barrier
     place = jnp.stack([me, core]).astype(jnp.int32)
-    own, right, message1, message2, message3 = first_stage(out_grad, gate_pre, up_pre, place, rows)
+    own, right, message1, message2, message3 = first_stage(out_grad, gate_pre, up_pre, rows)
 
     extra, every, whole = (split, 2 * rows), (0, tokens), (0, units)
     left1, left2, message3 = flip(message1, z_bit), flip(message2, w_bit), flip(message3, z_bit | w_bit)
     weight1, weight2 = flip(down_weight, x_bit), flip(down_weight, y_bit)
-    message3, weight1, weight2 = barrier((message3, weight1, weight2))
     to_y, to_x = cut([weight1, weight2], [(0, (0, q), whole, 0, 0), (1, (q, q), whole, 1, 0)], [(q, units)] * 2)
     weight3a, weight3b = flip(to_y, y_bit), flip(to_x, x_bit)
-    left1, left2, message3, right, _, _ = barrier((left1, left2, message3, right, to_y, to_x))
+    left1, left2, message3, right = barrier((left1, left2, message3, right))
     to_z, mine = cut(
         [left1, left2, message3, right],
         [

time: 136 us -> 149 us (1.096)
  Pallas kernels: 24.6 us -> 41.4 us
  waiting for transfers between devices: 67.3 us -> 63.8 us
    pallas_call x2, Pallas kernels: 0.56 us -> 12.1 us  [cut(): pl.pallas_call(kernel, out_shape=[jax.ShapeDtypeStruct(shape, jnp.bfloat1...]
    pallas_call x5, Pallas kernels: 14 us -> 18.4 us  [products(): pl.pallas_call(kernel, grid=(steps,), out_shape=[jax.ShapeDtypeStruct((he...]
    ppermute x27, waiting for transfers between devices: 67.3 us -> 63.8 us  [flip(): return lax.ppermute(value, axis, [(i, i ^ bits) for i in range(size)])]
  transfers between devices with their start and end apart: 27 -> 27, of which waited for: 15 -> 14; matrix products, arithmetic and copies ran while one was open for 3% -> 3% of each run, Pallas kernels for 16% -> 26%
where the time goes in v18:
time: 149 us; the launch traced here: 148 us
  waiting for transfers between devices  63.8 us (43%)
  Pallas kernels  41.4 us (28%)
  starting transfers between devices  32.5 us (22%)
  blocking collectives  4.95 us (3%)
  other arithmetic  4.73 us (3%)
    ppermute x27, waiting for transfers between devices, flip(): return lax.ppermute(value, axis, [(i, i ^ bits) for i in range(size)])  63.8 us
    ppermute x27, starting transfers between devices, flip(): return lax.ppermute(value, axis, [(i, i ^ bits) for i in range(size)])  32.5 us
    pallas_call x5, Pallas kernels, products(): pl.pallas_call(kernel, grid=(steps,), out_shape=[jax.ShapeDtypeStruct((he...  18.4 us
    pallas_call x2, Pallas kernels, cut(): pl.pallas_call(kernel, out_shape=[jax.ShapeDtypeStruct(shape, jnp.bfloat1...  12.1 us
    convert_element_type x1, other arithmetic, local(): up_grad = (hidden_grad * activated).astype(jnp.bfloat16)  3.96 us
    pallas_call x1, Pallas kernels, first_stage(): pl.pallas_call(kernel, grid=(tokens // step,), out_shape=[jax.ShapeDtypeS...  3.84 us
  transfers between devices with their start and end apart: 27, of which 14 were waited for; matrix products, arithmetic and copies ran while one was open for 3% of the time, Pallas kernels for 26%

profile of v18, /device:TPU:0, one launch (start us, length us, event | category | flops | bytes accessed | tf_op | source)
XLA Modules:
  0.0 148.3 jit_solution(4623671414810471971)
XLA Ops:
  0.6 3.0 %collective-permute-start.7 = (bf16[256,2560]{1,0:T(8,128)(2,1)}, bf16[256,2560]{1,0:T(8,128)(2,1)S(1)}, u32[]{:S(2)}, u32[]{:S(2)}) collective-permute-start(bf16[256,2560]{1,0:T(8,128)(2,1)} %refs_5_.1), channel_id=1, source_target_pairs={{0,2},{2,0},{4,6},{6,4},{8,10},{10,8},{12,14},{14,12},{16,18},{18,... | collective-permute-start | bytes 3932168 | tf_op jit(solution)/shard_map/ppermute | solution.py:28
  5.2 3.8 %shard_map.109 = (bf16[128,1024]{1,0:T(8,128)(2,1)}, bf16[128,1280]{1,0:T(8,128)(2,1)}, bf16[128,1792]{1,0:T(8,128)(2,1)}, bf16[128,1792]{1,0:T(8,128)(2,1)}, bf16[128,512]{1,0:T(8,128)(2,1)}) custom-call(bf16[128,4096]{1,0:T(8,128)(2,1)} %source.1, bf16[128,2560]{1,0:T(8,128)(2,1)} %gate.1, bf16[128,2560]{1,0:T(8,128)(2,1)} %up.1), custom_call_target="tpu_custom_call" | custom-call | tf_op jit(solution)/shard_map/pallas_call | solution.py:116
  10.6 2.6 %collective-permute-start.1 = (bf16[128,1792]{1,0:T(8,128)(2,1)}, bf16[128,1792]{1,0:T(8,128)(2,1)S(1)}, u32[]{:S(2)}, u32[]{:S(2)}) collective-permute-start(bf16[128,1792]{1,0:T(8,128)(2,1)} %get-tuple-element.62), channel_id=1, source_target_pairs={{0,16},{2,18},{4,20},{6,22},{8,24},{10,26},{12,28},{14,30},{16,0},... | collective-permute-start | bytes 1376264 | tf_op jit(solution)/shard_map/ppermute | solution.py:28
  13.4 22.3 %collective-permute-done.2.refs_2_ = bf16[128,512]{1,0:T(8,128)(2,1)S(1)} collective-permute-done((bf16[128,512]{1,0:T(8,128)(2,1)}, bf16[128,512]{1,0:T(8,128)(2,1)S(1)}, u32[]{:S(2)}, u32[]{:S(2)}) %collective-permute-start.2) | collective-permute-done | bytes 131104 | tf_op jit(solution)/shard_map/ppermute | solution.py:28
  37.2 11.1 %shard_map.110 = (bf16[128,2560]{1,0:T(8,128)(2,1)}, bf16[128,1536]{1,0:T(8,128)(2,1)}) custom-call(bf16[128,1792]{1,0:T(8,128)(2,1)S(1)} %collective-permute-done.refs_0_.refs_2_, bf16[128,1792]{1,0:T(8,128)(2,1)S(1)} %collective-permute-done.1.refs_1_.refs_3_, bf16[128,512]{1,0:T(8,128)(2,1)S(1)} %collective-permute-done.2.refs_2_, ...), custom_call_target="tpu_custom_call" | custom-call | tf_op jit(solution)/shard_map/pallas_call | solution.py:141
  48.3 2.1 %collective-permute-start.3 = (bf16[128,2560]{1,0:T(8,128)(2,1)}, bf16[128,2560]{1,0:T(8,128)(2,1)S(1)}, u32[]{:S(2)}, u32[]{:S(2)}) collective-permute-start(bf16[128,2560]{1,0:T(8,128)(2,1)} %get-tuple-element.69), channel_id=1, source_target_pairs={{0,8},{2,10},{4,12},{6,14},{8,0},{10,2},{12,4},{14,6},{16,24},{18,... | collective-permute-start | bytes 1966088 | tf_op jit(solution)/shard_map/ppermute | solution.py:28
  55.1 14.5 %collective-permute-done.4.refs_3_ = bf16[128,1280]{1,0:T(8,128)(2,1)} collective-permute-done((bf16[128,1280]{1,0:T(8,128)(2,1)}, bf16[128,1280]{1,0:T(8,128)(2,1)}, u32[]{:S(2)}, u32[]{:S(2)}) %collective-permute-start.4) | collective-permute-done | bytes 327712 | tf_op jit(solution)/shard_map/ppermute | solution.py:28
  70.3 3.1 %collective-permute-start.6 = (bf16[128,1280]{1,0:T(8,128)(2,1)}, bf16[128,1280]{1,0:T(8,128)(2,1)S(1)}, u32[]{:S(2)}, u32[]{:S(2)}) collective-permute-start(bf16[128,1280]{1,0:T(8,128)(2,1)} %collective-permute-done.4.refs_3_), channel_id=1, source_target_pairs={{0,8},{2,10},{4,12},{6,14},{8,0},{10,2},{12,4},{14,6},{16,24},{18,... | collective-permute-start | bytes 983048 | tf_op jit(solution)/shard_map/ppermute | solution.py:28
  73.4 2.0 %shard_map.112 = (bf16[256,1280]{1,0:T(8,128)(2,1)S(1)}, bf16[256,1280]{1,0:T(8,128)(2,1)S(1)}) custom-call(bf16[512,1024]{1,0:T(8,128)(2,1)S(1)} %shard_map.111.refs_0_, bf16[128,1792]{1,0:T(8,128)(2,1)S(1)} %copy-done.5, bf16[128,1792]{1,0:T(8,128)(2,1)S(1)} %copy-done.2, bf16[128,1792]{1,0:T(8,128)(2,1)S(1)} %copy-done.4, ...), custom_call_target="tpu_custom_call" | custom-call | tf_op jit(solution)/shard_map/pallas_call | solution.py:358
  76.6 4.5 %shard_map.114 = (bf16[128,2560]{1,0:T(8,128)(2,1)S(1)}, bf16[128,2560]{1,0:T(8,128)(2,1)S(1)}) custom-call(bf16[512,1024]{1,0:T(8,128)(2,1)S(1)} %shard_map.111.refs_0_, bf16[256,2560]{1,0:T(8,128)(2,1)S(1)} %copy-done, bf16[256,2560]{1,0:T(8,128)(2,1)S(1)} %collective-permute-done.7.refs_0_.refs_2_.refs_6_, ...), custom_call_target="tpu_custom_call" | custom-call | tf_op jit(solution)/shard_map/pallas_call | solution.py:358
  81.1 3.8 %shard_map.115 = (bf16[256,1280]{1,0:T(8,128)(2,1)S(1)}, bf16[256,1280]{1,0:T(8,128)(2,1)S(1)}) custom-call(bf16[512,1024]{1,0:T(8,128)(2,1)S(1)} %shard_map.111.refs_0_, bf16[128,1280]{1,0:T(8,128)(2,1)} %get-tuple-element.68.refs_3_.refs_1_, bf16[128,2560]{1,0:T(8,128)(2,1)S(1)} %collective-permute-done.3.refs_4_.refs_2_, ...), custom_call_target="tpu_custom_call" | custom-call | tf_op jit(solution)/shard_map/pallas_call | solution.py:358
  88.0 4.3 %collective-permute-done.11.refs_2_ = bf16[256,1280]{1,0:T(8,128)(2,1)S(1)} collective-permute-done((bf16[256,1280]{1,0:T(8,128)(2,1)S(1)}, bf16[256,1280]{1,0:T(8,128)(2,1)S(1)}, u32[]{:S(2)}, u32[]{:S(2)}) %collective-permute-start.11) | collective-permute-done | bytes 655392 | tf_op jit(solution)/shard_map/ppermute | solution.py:28
  93.7 2.1 %shard_map.116 = (f32[256,1280]{1,0:T(8,128)S(1)}, f32[128,1280]{1,0:T(8,128)S(1)}, f32[128,1280]{1,0:T(8,128)S(1)}) custom-call(bf16[512,1024]{1,0:T(8,128)(2,1)S(1)} %shard_map.111.refs_0_, bf16[128,1792]{1,0:T(8,128)(2,1)S(1)} %copy-done.5, bf16[128,1792]{1,0:T(8,128)(2,1)S(1)} %copy-done.2, bf16[128,1792]{1,0:T(8,128)(2,1)S(1)} %copy-done.4, ...), custom_call_target="tpu_custom_call" | custom-call | tf_op jit(solution)/shard_map/pallas_call | solution.py:358
  95.8 6.0 %shard_map.117 = (f32[256,1280]{1,0:T(8,128)S(1)}, f32[128,1280]{1,0:T(8,128)S(1)}, f32[128,1280]{1,0:T(8,128)S(1)}, f32[128,2560]{1,0:T(8,128)S(1)}, f32[64,2560]{1,0:T(8,128)S(1)}, /*index=5*/f32[64,2560]{1,0:T(8,128)S(1)}) custom-call(bf16[512,1024]{1,0:T(8,128)(2,1)S(1)} %shard_map.111.refs_0_, bf16[128,1280]{1,0:T(8,128)(2,1)} %get-tuple-element.68.refs_3_.refs_1_, ...), custom_call_target="tpu_custom_call" | custom-call | tf_op jit(solution)/shard_map/pallas_call | solution.py:358
  103.5 2.1 %collective-permute-start.16 = (bf16[128,2560]{1,0:T(8,128)(2,1)S(1)}, bf16[128,2560]{1,0:T(8,128)(2,1)S(1)}, u32[]{:S(2)}, u32[]{:S(2)}) collective-permute-start(bf16[128,2560]{1,0:T(8,128)(2,1)S(1)} %shard_map.119), channel_id=1, source_target_pairs={{0,2},{2,0},{4,6},{6,4},{8,10},{10,8},{12,14},{14,12},{16,18},{18,... | collective-permute-start | bytes 1966088 | tf_op jit(solution)/shard_map/ppermute | solution.py:28
  106.1 8.6 %collective-permute-done.18.refs_1_ = bf16[128,2560]{1,0:T(8,128)(2,1)S(1)} collective-permute-done((bf16[128,2560]{1,0:T(8,128)(2,1)S(1)}, bf16[128,2560]{1,0:T(8,128)(2,1)S(1)}, u32[]{:S(2)}, u32[]{:S(2)}) %collective-permute-start.18) | collective-permute-done | bytes 655392 | tf_op jit(solution)/shard_map/ppermute | solution.py:28
  119.5 2.5 %psum.14.row_sum = f32[1,256]{1,0:T(1,128)S(1)} all-reduce(f32[1,256]{1,0:T(1,128)S(1)} %get-tuple-element.102), channel_id=1, replica_groups=mesh['dp'=16,'mp'=2] {'mp'}, use_global_device_ids=true, to_apply=%region_0.0 | all-reduce | flops 256 | bytes 2048 | tf_op jit(solution)/shard_map/psum | solution.py:457
  123.8 2.4 %collective-permute-start.21 = (f32[5248]{0:T(1024)S(1)}, f32[5248]{0:T(1024)S(1)}, u32[]{:S(2)}, u32[]{:S(2)}) collective-permute-start(f32[5248]{0:T(1024)S(1)} %reduce), channel_id=1, source_target_pairs={{0,6},{2,4},{4,2},{6,0},{8,14},{10,12},{12,10},{14,8},{16,22},{18,... | collective-permute-start | bytes 62984 | tf_op jit(solution)/shard_map/ppermute | solution.py:28
  130.6 3.9 %collective-permute-done.22 = bf16[64,2560]{1,0:T(8,128)(2,1)} collective-permute-done((bf16[64,2560]{1,0:T(8,128)(2,1)}, bf16[64,2560]{1,0:T(8,128)(2,1)}, u32[]{:S(2)}, u32[]{:S(2)}) %collective-permute-start.22) | collective-permute-done | bytes 327712 | tf_op jit(solution)/shard_map/ppermute | solution.py:28
  134.5 2.0 %collective-permute-start.25 = (f32[5248]{0:T(1024)S(1)}, f32[5248]{0:T(1024)S(1)}, u32[]{:S(2)}, u32[]{:S(2)}) collective-permute-start(f32[5248]{0:T(1024)S(1)} %add_add_fusion.1), channel_id=1, source_target_pairs={{0,16},{2,18},{4,20},{6,22},{8,24},{10,26},{12,28},{14,30},{16,0},... | collective-permute-start | bytes 62984 | tf_op jit(solution)/shard_map/ppermute | solution.py:28
  136.5 2.4 %collective-permute-start.26 = (f32[5248]{0:T(1024)S(1)}, f32[5248]{0:T(1024)S(1)}, u32[]{:S(2)}, u32[]{:S(2)}) collective-permute-start(f32[5248]{0:T(1024)S(1)} %add_add_fusion.1), channel_id=1, source_target_pairs={{0,24},{2,26},{4,28},{6,30},{8,16},{10,18},{12,20},{14,22},{16,8},... | collective-permute-start | bytes 62984 | tf_op jit(solution)/shard_map/ppermute | solution.py:28
  138.9 4.0 %fusion.8 = (bf16[128,2560]{1,0:T(8,128)(2,1)}, bf16[128,2560]{1,0:T(8,128)(2,1)}) fusion(bf16[128,2560]{1,0:T(8,128)(2,1)S(1)} %copy-done.12, bf16[64,2560]{1,0:T(8,128)(2,1)} %collective-permute-done.23, bf16[64,2560]{1,0:T(8,128)(2,1)} %collective-permute-done.22, f32[128,2560]{1,0:T(8,128)} %copy-done.8, bf16[64,2560]{1,0:T(8,128)(2,1)S(1)} %slice-done, ...), kind=kLoop, calls=%fused_computation.15 | loop fusion | flops 11468800 | bytes 5242880 | tf_op jit(solution)/shard_map/convert_element_type | solution.py:506
  142.9 2.5 %psum.15.terms = f32[1,128]{1,0:T(1,128)S(1)} all-reduce(f32[1,128]{1,0:T(1,128)S(1)} %get-tuple-element.108), channel_id=1, replica_groups=mesh['dp'=16,'mp'=2] {'mp'}, use_global_device_ids=true, to_apply=%region_1.0 | all-reduce | flops 128 | bytes 1024 | tf_op jit(solution)/shard_map/psum | solution.py:480
  146.0 2.2 %shard_map.125 = (f32[256,2560]{1,0:T(8,128)}, f32[1,128]{1,0:T(1,128)}) custom-call(f32[256,2560]{1,0:T(8,128)S(1)} %get-tuple-element.101.grad, f32[1,256]{1,0:T(1,128)S(1)} %copy-done.11, f32[1,2560]{1,0:T(1,128)S(1)} %get-tuple-element.107.col_moment_new, f32[1,128]{1,0:T(1,128)S(1)} %psum.15.terms, f32[1,5248]{1,0:T(1,128)S(1)} %broadcast_in_dim.10.sums.row_total), custom_call_target="tpu_custom_call" | custom-call | tf_op jit(solution)/shard_map/pallas_call | solution.py:312
  (89 shorter events, 29.5 us)
Async XLA Ops:
  0.6 50.9 %collective-permute-start.7 = (bf16[256,2560]{1,0:T(8,128)(2,1)}, bf16[256,2560]{1,0:T(8,128)(2,1)S(1)}, u32[]{:S(2)}, u32[]{:S(2)}) collective-permute-start(bf16[256,2560]{1,0:T(8,128)(2,1)} %refs_5_.1), channel_id=1, source_target_pairs={{0,2},{2,0},{4,6},{6,4},{8,10},{10,8},{12,14},{14,12},{16,18},{18,... | collective-permute-start | bytes 3932168 | tf_op jit(solution)/shard_map/ppermute | solution.py:28
  3.6 47.9 %collective-permute-start.8 = (bf16[256,2560]{1,0:T(8,128)(2,1)}, bf16[256,2560]{1,0:T(8,128)(2,1)S(1)}, u32[]{:S(2)}, u32[]{:S(2)}) collective-permute-start(bf16[256,2560]{1,0:T(8,128)(2,1)} %refs_5_.1), channel_id=1, source_target_pairs={{0,4},{2,6},{4,0},{6,2},{8,12},{10,14},{12,8},{14,10},{16,20},{18,... | collective-permute-start | bytes 3932168 | tf_op jit(solution)/shard_map/ppermute | solution.py:28
  9.0 26.7 %collective-permute-start = (bf16[128,1792]{1,0:T(8,128)(2,1)}, bf16[128,1792]{1,0:T(8,128)(2,1)S(1)}, u32[]{:S(2)}, u32[]{:S(2)}) collective-permute-start(bf16[128,1792]{1,0:T(8,128)(2,1)} %get-tuple-element.61.refs_1_), channel_id=1, source_target_pairs={{0,8},{2,10},{4,12},{6,14},{8,0},{10,2},{12,4},{14,6},{16,24},{18,... | collective-permute-start | bytes 1376264 | tf_op jit(solution)/shard_map/ppermute | solution.py:28
  10.6 26.6 %collective-permute-start.1 = (bf16[128,1792]{1,0:T(8,128)(2,1)}, bf16[128,1792]{1,0:T(8,128)(2,1)S(1)}, u32[]{:S(2)}, u32[]{:S(2)}) collective-permute-start(bf16[128,1792]{1,0:T(8,128)(2,1)} %get-tuple-element.62), channel_id=1, source_target_pairs={{0,16},{2,18},{4,20},{6,22},{8,24},{10,26},{12,28},{14,30},{16,0},... | collective-permute-start | bytes 1376264 | tf_op jit(solution)/shard_map/ppermute | solution.py:28
  13.2 22.5 %collective-permute-start.2 = (bf16[128,512]{1,0:T(8,128)(2,1)}, bf16[128,512]{1,0:T(8,128)(2,1)S(1)}, u32[]{:S(2)}, u32[]{:S(2)}) collective-permute-start(bf16[128,512]{1,0:T(8,128)(2,1)} %get-tuple-element.63), channel_id=1, source_target_pairs={{0,24},{2,26},{4,28},{6,30},{8,16},{10,18},{12,20},{14,22},{16,8},... | collective-permute-start | bytes 393224 | tf_op jit(solution)/shard_map/ppermute | solution.py:28
  48.3 22.0 %collective-permute-start.3 = (bf16[128,2560]{1,0:T(8,128)(2,1)}, bf16[128,2560]{1,0:T(8,128)(2,1)S(1)}, u32[]{:S(2)}, u32[]{:S(2)}) collective-permute-start(bf16[128,2560]{1,0:T(8,128)(2,1)} %get-tuple-element.69), channel_id=1, source_target_pairs={{0,8},{2,10},{4,12},{6,14},{8,0},{10,2},{12,4},{14,6},{16,24},{18,... | collective-permute-start | bytes 1966088 | tf_op jit(solution)/shard_map/ppermute | solution.py:28
  50.4 19.3 %collective-permute-start.4 = (bf16[128,1280]{1,0:T(8,128)(2,1)}, bf16[128,1280]{1,0:T(8,128)(2,1)}, u32[]{:S(2)}, u32[]{:S(2)}) collective-permute-start(bf16[128,1280]{1,0:T(8,128)(2,1)} %get-tuple-element.68.refs_3_.refs_1_), channel_id=1, source_target_pairs={{0,16},{2,18},{4,20},{6,22},{8,24},{10,26},{12,28},{14,30},{16,0},... | collective-permute-start | bytes 983048 | tf_op jit(solution)/shard_map/ppermute | solution.py:28
  52.6 23.9 %collective-permute-start.10 = (bf16[128,2560]{1,0:T(8,128)(2,1)}, bf16[128,2560]{1,0:T(8,128)(2,1)}, u32[]{:S(2)}, u32[]{:S(2)}) collective-permute-start(bf16[128,2560]{1,0:T(8,128)(2,1)} %get-tuple-element.78), channel_id=1, source_target_pairs={{0,2},{2,0},{4,6},{6,4},{8,10},{10,8},{12,14},{14,12},{16,18},{18,... | collective-permute-start | bytes 1966088 | tf_op jit(solution)/shard_map/ppermute | solution.py:28
  53.2 23.3 %collective-permute-start.9 = (bf16[128,2560]{1,0:T(8,128)(2,1)}, bf16[128,2560]{1,0:T(8,128)(2,1)}, u32[]{:S(2)}, u32[]{:S(2)}) collective-permute-start(bf16[128,2560]{1,0:T(8,128)(2,1)} %get-tuple-element.77), channel_id=1, source_target_pairs={{0,4},{2,6},{4,0},{6,2},{8,12},{10,14},{12,8},{14,10},{16,20},{18,... | collective-permute-start | bytes 1966088 | tf_op jit(solution)/shard_map/ppermute | solution.py:28
  70.3 10.8 %collective-permute-start.6 = (bf16[128,1280]{1,0:T(8,128)(2,1)}, bf16[128,1280]{1,0:T(8,128)(2,1)S(1)}, u32[]{:S(2)}, u32[]{:S(2)}) collective-permute-start(bf16[128,1280]{1,0:T(8,128)(2,1)} %collective-permute-done.4.refs_3_), channel_id=1, source_target_pairs={{0,8},{2,10},{4,12},{6,14},{8,0},{10,2},{12,4},{14,6},{16,24},{18,... | collective-permute-start | bytes 983048 | tf_op jit(solution)/shard_map/ppermute | solution.py:28
  75.5 16.9 %collective-permute-start.11 = (bf16[256,1280]{1,0:T(8,128)(2,1)S(1)}, bf16[256,1280]{1,0:T(8,128)(2,1)S(1)}, u32[]{:S(2)}, u32[]{:S(2)}) collective-permute-start(bf16[256,1280]{1,0:T(8,128)(2,1)S(1)} %get-tuple-element.75), channel_id=1, source_target_pairs={{0,2},{2,0},{4,6},{6,4},{8,10},{10,8},{12,14},{14,12},{16,18},{18,... | collective-permute-start | bytes 1966088 | tf_op jit(solution)/shard_map/ppermute | solution.py:28
  76.1 17.7 %collective-permute-start.12 = (bf16[256,1280]{1,0:T(8,128)(2,1)S(1)}, bf16[256,1280]{1,0:T(8,128)(2,1)S(1)}, u32[]{:S(2)}, u32[]{:S(2)}) collective-permute-start(bf16[256,1280]{1,0:T(8,128)(2,1)S(1)} %get-tuple-element.82), channel_id=1, source_target_pairs={{0,4},{2,6},{4,0},{6,2},{8,12},{10,14},{12,8},{14,10},{16,20},{18,... | collective-permute-start | bytes 1966088 | tf_op jit(solution)/shard_map/ppermute | solution.py:28
  84.9 18.5 %collective-permute-start.14 = (bf16[256,1280]{1,0:T(8,128)(2,1)S(1)}, bf16[256,1280]{1,0:T(8,128)(2,1)S(1)}, u32[]{:S(2)}, u32[]{:S(2)}) collective-permute-start(bf16[256,1280]{1,0:T(8,128)(2,1)S(1)} %get-tuple-element.90), channel_id=1, source_target_pairs={{0,4},{2,6},{4,0},{6,2},{8,12},{10,14},{12,8},{14,10},{16,20},{18,... | collective-permute-start | bytes 1966088 | tf_op jit(solution)/shard_map/ppermute | solution.py:28
  86.5 19.1 %collective-permute-start.13 = (bf16[256,1280]{1,0:T(8,128)(2,1)S(1)}, bf16[256,1280]{1,0:T(8,128)(2,1)S(1)}, u32[]{:S(2)}, u32[]{:S(2)}) collective-permute-start(bf16[256,1280]{1,0:T(8,128)(2,1)S(1)} %get-tuple-element.84), channel_id=1, source_target_pairs={{0,2},{2,0},{4,6},{6,4},{8,10},{10,8},{12,14},{14,12},{16,18},{18,... | collective-permute-start | bytes 1966088 | tf_op jit(solution)/shard_map/ppermute | solution.py:28
  88.0 26.7 %collective-permute-start.18 = (bf16[128,2560]{1,0:T(8,128)(2,1)S(1)}, bf16[128,2560]{1,0:T(8,128)(2,1)S(1)}, u32[]{:S(2)}, u32[]{:S(2)}) collective-permute-start(bf16[128,2560]{1,0:T(8,128)(2,1)S(1)} %get-tuple-element.98), channel_id=1, source_target_pairs={{0,16},{2,18},{4,20},{6,22},{8,24},{10,26},{12,28},{14,30},{16,0},... | collective-permute-start | bytes 1966088 | tf_op jit(solution)/shard_map/ppermute | solution.py:28
  92.4 24.2 %collective-permute-start.17 = (bf16[128,2560]{1,0:T(8,128)(2,1)S(1)}, bf16[128,2560]{1,0:T(8,128)(2,1)S(1)}, u32[]{:S(2)}, u32[]{:S(2)}) collective-permute-start(bf16[128,2560]{1,0:T(8,128)(2,1)S(1)} %get-tuple-element.96), channel_id=1, source_target_pairs={{0,8},{2,10},{4,12},{6,14},{8,0},{10,2},{12,4},{14,6},{16,24},{18,... | collective-permute-start | bytes 1966088 | tf_op jit(solution)/shard_map/ppermute | solution.py:28
  103.5 15.2 %collective-permute-start.16 = (bf16[128,2560]{1,0:T(8,128)(2,1)S(1)}, bf16[128,2560]{1,0:T(8,128)(2,1)S(1)}, u32[]{:S(2)}, u32[]{:S(2)}) collective-permute-start(bf16[128,2560]{1,0:T(8,128)(2,1)S(1)} %shard_map.119), channel_id=1, source_target_pairs={{0,2},{2,0},{4,6},{6,4},{8,10},{10,8},{12,14},{14,12},{16,18},{18,... | collective-permute-start | bytes 1966088 | tf_op jit(solution)/shard_map/ppermute | solution.py:28
  105.8 12.9 %collective-permute-start.15 = (bf16[128,2560]{1,0:T(8,128)(2,1)S(1)}, bf16[128,2560]{1,0:T(8,128)(2,1)S(1)}, u32[]{:S(2)}, u32[]{:S(2)}) collective-permute-start(bf16[128,2560]{1,0:T(8,128)(2,1)S(1)} %shard_map.118), channel_id=1, source_target_pairs={{0,4},{2,6},{4,0},{6,2},{8,12},{10,14},{12,8},{14,10},{16,20},{18,... | collective-permute-start | bytes 1966088 | tf_op jit(solution)/shard_map/ppermute | solution.py:28
  115.6 14.9 %collective-permute-start.23 = (bf16[64,2560]{1,0:T(8,128)(2,1)}, bf16[64,2560]{1,0:T(8,128)(2,1)}, u32[]{:S(2)}, u32[]{:S(2)}) collective-permute-start(bf16[64,2560]{1,0:T(8,128)(2,1)} %shard_map.121), channel_id=1, source_target_pairs={{0,8},{2,10},{4,12},{6,14},{8,0},{10,2},{12,4},{14,6},{16,24},{18,... | collective-permute-start | bytes 983048 | tf_op jit(solution)/shard_map/ppermute | solution.py:28
  117.5 17.0 %collective-permute-start.22 = (bf16[64,2560]{1,0:T(8,128)(2,1)}, bf16[64,2560]{1,0:T(8,128)(2,1)}, u32[]{:S(2)}, u32[]{:S(2)}) collective-permute-start(bf16[64,2560]{1,0:T(8,128)(2,1)} %shard_map.120), channel_id=1, source_target_pairs={{0,16},{2,18},{4,20},{6,22},{8,24},{10,26},{12,28},{14,30},{16,0},... | collective-permute-start | bytes 983048 | tf_op jit(solution)/shard_map/ppermute | solution.py:28
  123.8 4.7 %collective-permute-start.21 = (f32[5248]{0:T(1024)S(1)}, f32[5248]{0:T(1024)S(1)}, u32[]{:S(2)}, u32[]{:S(2)}) collective-permute-start(f32[5248]{0:T(1024)S(1)} %reduce), channel_id=1, source_target_pairs={{0,6},{2,4},{4,2},{6,0},{8,14},{10,12},{12,10},{14,8},{16,22},{18,... | collective-permute-start | bytes 62984 | tf_op jit(solution)/shard_map/ppermute | solution.py:28
  134.5 8.4 %collective-permute-start.24 = (f32[5248]{0:T(1024)S(1)}, f32[5248]{0:T(1024)S(1)}, u32[]{:S(2)}, u32[]{:S(2)}) collective-permute-start(f32[5248]{0:T(1024)S(1)} %add_add_fusion.1), channel_id=1, source_target_pairs={{0,8},{2,10},{4,12},{6,14},{8,0},{10,2},{12,4},{14,6},{16,24},{18,... | collective-permute-start | bytes 62984 | tf_op jit(solution)/shard_map/ppermute | solution.py:28
  134.5 8.4 %collective-permute-start.25 = (f32[5248]{0:T(1024)S(1)}, f32[5248]{0:T(1024)S(1)}, u32[]{:S(2)}, u32[]{:S(2)}) collective-permute-start(f32[5248]{0:T(1024)S(1)} %add_add_fusion.1), channel_id=1, source_target_pairs={{0,16},{2,18},{4,20},{6,22},{8,24},{10,26},{12,28},{14,30},{16,0},... | collective-permute-start | bytes 62984 | tf_op jit(solution)/shard_map/ppermute | solution.py:28
  136.5 6.4 %collective-permute-start.26 = (f32[5248]{0:T(1024)S(1)}, f32[5248]{0:T(1024)S(1)}, u32[]{:S(2)}, u32[]{:S(2)}) collective-permute-start(f32[5248]{0:T(1024)S(1)} %add_add_fusion.1), channel_id=1, source_target_pairs={{0,24},{2,26},{4,28},{6,30},{8,16},{10,18},{12,20},{14,22},{16,8},... | collective-permute-start | bytes 62984 | tf_op jit(solution)/shard_map/ppermute | solution.py:28
  (19 other events, 201.1 us)

commit v19 on v18

--- a/solution.py
+++ b/solution.py
@@ -90,13 +90,13 @@
     return product, hidden_grad
 
 
-def first_stage(out_grad, gate_pre, up_pre, rows):
+def first_stage(out_grad, gate_pre, up_pre, place, rows):
     tokens, units = gate_pre.shape
     half = units // 2
     step = 32
 
-    def kernel(source, gate, up, own, right, message1, message2, message3):
-        me, core = lax.axis_index("dp"), lax.axis_index("mp")
+    def kernel(place, source, gate, up, own, right, message1, message2, message3):
+        me, core = place[0], place[1]
 
         def block(k, j):
             return pl.ds(pl.multiple_of((me ^ (4 * k + j)) * rows, rows), rows)
@@ -117,11 +117,12 @@
         kernel,
         grid=(tokens // step,),
         out_shape=[jax.ShapeDtypeStruct((tokens, width), jnp.bfloat16) for width in widths],
-        in_specs=[pl.BlockSpec((step, array.shape[1]), lambda i: (i, 0)) for array in (out_grad, gate_pre, up_pre)],
+        in_specs=[pl.BlockSpec(memory_space=pltpu.SMEM)]
+        + [pl.BlockSpec((step, array.shape[1]), lambda i: (i, 0)) for array in (out_grad, gate_pre, up_pre)],
         out_specs=[pl.BlockSpec((step, width), lambda i: (i, 0)) for width in widths],
         compiler_params=pltpu.CompilerParams(vmem_limit_bytes=56 << 20),
         cost_estimate=EAGER,
-    )(out_grad, gate_pre, up_pre)
+    )(place, out_grad, gate_pre, up_pre)
 
 
 def cut(sources, parts, shapes):
@@ -383,7 +384,7 @@
     split = units // 2
     barrier = lax.optimization_barrier
     place = jnp.stack([me, core]).astype(jnp.int32)
-    own, right, message1, message2, message3 = first_stage(out_grad, gate_pre, up_pre, rows)
+    own, right, message1, message2, message3 = first_stage(out_grad, gate_pre, up_pre, place, rows)
 
     extra, every, whole = (split, 2 * rows), (0, tokens), (0, units)
     left1, left2, message3 = flip(message1, z_bit), flip(message2, w_bit), flip(message3, z_bit | w_bit)

time: 149 us -> 136 us (0.913)
  Pallas kernels: 41.4 us -> 24.6 us
  waiting for transfers between devices: 63.8 us -> 67.3 us
    pallas_call x2, Pallas kernels: 12.1 us -> 0.56 us  [cut(): pl.pallas_call(kernel, out_shape=[jax.ShapeDtypeStruct(shape, jnp.bfloat1...]
    pallas_call x5, Pallas kernels: 18.4 us -> 14 us  [products(): pl.pallas_call(kernel, grid=(steps,), out_shape=[jax.ShapeDtypeStruct((he...]
    ppermute x27, waiting for transfers between devices: 63.8 us -> 67.3 us  [flip(): return lax.ppermute(value, axis, [(i, i ^ bits) for i in range(size)])]
  transfers between devices with their start and end apart: 27 -> 27, of which waited for: 14 -> 15; matrix products, arithmetic and copies ran while one was open for 3% -> 3% of each run, Pallas kernels for 26% -> 16%
where the time goes in v19:
time: 136 us
  waiting for transfers between devices  67.3 us (49%)
  starting transfers between devices  31.8 us (23%)
  Pallas kernels  24.6 us (18%)
  other arithmetic  5.24 us (4%)
  blocking collectives  4.95 us (4%)
    ppermute x27, waiting for transfers between devices, flip(): return lax.ppermute(value, axis, [(i, i ^ bits) for i in range(size)])  67.3 us
    ppermute x27, starting transfers between devices, flip(): return lax.ppermute(value, axis, [(i, i ^ bits) for i in range(size)])  31.8 us
    pallas_call x5, Pallas kernels, products(): pl.pallas_call(kernel, grid=(steps,), out_shape=[jax.ShapeDtypeStruct((he...  14 us
    convert_element_type x1, other arithmetic, local(): up_grad = (hidden_grad * activated).astype(jnp.bfloat16)  3.96 us
    pallas_call x1, Pallas kernels, first_stage(): pl.pallas_call(kernel, grid=(tokens // step,), out_shape=[jax.ShapeDtypeS...  3.84 us
  transfers between devices with their start and end apart: 27, of which 15 were waited for; matrix products, arithmetic and copies ran while one was open for 3% of the time, Pallas kernels for 16%

profile of v19, /device:TPU:0, one launch (start us, length us, event | category | flops | bytes accessed | tf_op | source)
XLA Modules:
  0.0 135.8 jit_solution(5582972704752515835)
XLA Ops:
  0.6 3.0 %collective-permute-start.7 = (bf16[256,2560]{1,0:T(8,128)(2,1)}, bf16[256,2560]{1,0:T(8,128)(2,1)S(1)}, u32[]{:S(2)}, u32[]{:S(2)}) collective-permute-start(bf16[256,2560]{1,0:T(8,128)(2,1)} %refs_5_.1), channel_id=1, source_target_pairs={{0,2},{2,0},{4,6},{6,4},{8,10},{10,8},{12,14},{14,12},{16,18},{18,... | collective-permute-start | bytes 3932168 | tf_op jit(solution)/shard_map/ppermute | solution.py:28
  5.7 3.8 %shard_map.109 = (bf16[128,1024]{1,0:T(8,128)(2,1)}, bf16[128,1280]{1,0:T(8,128)(2,1)}, bf16[128,1792]{1,0:T(8,128)(2,1)}, bf16[128,1792]{1,0:T(8,128)(2,1)}, bf16[128,512]{1,0:T(8,128)(2,1)}) custom-call(s32[2]{0:T(128)} %pad_add_fusion.place, bf16[128,4096]{1,0:T(8,128)(2,1)} %source.1, bf16[128,2560]{1,0:T(8,128)(2,1)} %gate.1, bf16[128,2560]{1,0:T(8,128)(2,1)} %up.1), custom_call_target="tpu_custom_call" | custom-call | tf_op jit(solution)/shard_map/pallas_call | solution.py:116
  11.2 2.6 %collective-permute-start.1 = (bf16[128,1792]{1,0:T(8,128)(2,1)}, bf16[128,1792]{1,0:T(8,128)(2,1)S(1)}, u32[]{:S(2)}, u32[]{:S(2)}) collective-permute-start(bf16[128,1792]{1,0:T(8,128)(2,1)} %get-tuple-element.62), channel_id=1, source_target_pairs={{0,16},{2,18},{4,20},{6,22},{8,24},{10,26},{12,28},{14,30},{16,0},... | collective-permute-start | bytes 1376264 | tf_op jit(solution)/shard_map/ppermute | solution.py:28
  14.0 22.3 %collective-permute-done.2.refs_2_ = bf16[128,512]{1,0:T(8,128)(2,1)S(1)} collective-permute-done((bf16[128,512]{1,0:T(8,128)(2,1)}, bf16[128,512]{1,0:T(8,128)(2,1)S(1)}, u32[]{:S(2)}, u32[]{:S(2)}) %collective-permute-start.2) | collective-permute-done | bytes 131104 | tf_op jit(solution)/shard_map/ppermute | solution.py:28
  38.9 2.0 %collective-permute-start.3 = (bf16[128,2560]{1,0:T(8,128)(2,1)S(1)}, bf16[128,2560]{1,0:T(8,128)(2,1)S(1)}, u32[]{:S(2)}, u32[]{:S(2)}) collective-permute-start(bf16[128,2560]{1,0:T(8,128)(2,1)S(1)} %get-tuple-element.69), channel_id=1, source_target_pairs={{0,8},{2,10},{4,12},{6,14},{8,0},{10,2},{12,4},{14,6},{16,24},{18,... | collective-permute-start | bytes 1966088 | tf_op jit(solution)/shard_map/ppermute | solution.py:28
  44.4 15.6 %collective-permute-done.4.refs_3_ = bf16[128,1280]{1,0:T(8,128)(2,1)S(1)} collective-permute-done((bf16[128,1280]{1,0:T(8,128)(2,1)S(1)}, bf16[128,1280]{1,0:T(8,128)(2,1)S(1)}, u32[]{:S(2)}, u32[]{:S(2)}) %collective-permute-start.4) | collective-permute-done | bytes 327712 | tf_op jit(solution)/shard_map/ppermute | solution.py:28
  60.7 3.3 %collective-permute-start.6 = (bf16[128,1280]{1,0:T(8,128)(2,1)S(1)}, bf16[128,1280]{1,0:T(8,128)(2,1)S(1)}, u32[]{:S(2)}, u32[]{:S(2)}) collective-permute-start(bf16[128,1280]{1,0:T(8,128)(2,1)S(1)} %collective-permute-done.4.refs_3_), channel_id=1, source_target_pairs={{0,8},{2,10},{4,12},{6,14},{8,0},{10,2},{12,4},{14,6},{16,24},{18,... | collective-permute-start | bytes 983048 | tf_op jit(solution)/shard_map/ppermute | solution.py:28
  64.0 2.0 %shard_map.112 = (bf16[256,1280]{1,0:T(8,128)(2,1)S(1)}, bf16[256,1280]{1,0:T(8,128)(2,1)S(1)}) custom-call(bf16[512,1024]{1,0:T(8,128)(2,1)S(1)} %shard_map.111.refs_0_, bf16[128,1792]{1,0:T(8,128)(2,1)S(1)} %copy-done.2, bf16[128,1792]{1,0:T(8,128)(2,1)S(1)} %collective-permute-done.refs_0_.refs_2_, ...), custom_call_target="tpu_custom_call" | custom-call | tf_op jit(solution)/shard_map/pallas_call | solution.py:359
  67.2 2.8 %shard_map.114 = (bf16[128,2560]{1,0:T(8,128)(2,1)S(1)}, bf16[128,2560]{1,0:T(8,128)(2,1)S(1)}) custom-call(bf16[512,1024]{1,0:T(8,128)(2,1)S(1)} %shard_map.111.refs_0_, bf16[256,2560]{1,0:T(8,128)(2,1)S(1)} %copy-done, bf16[256,2560]{1,0:T(8,128)(2,1)S(1)} %collective-permute-done.7.refs_0_.refs_2_.refs_6_, ...), custom_call_target="tpu_custom_call" | custom-call | tf_op jit(solution)/shard_map/pallas_call | solution.py:359
  70.0 2.1 %shard_map.115 = (bf16[256,1280]{1,0:T(8,128)(2,1)S(1)}, bf16[256,1280]{1,0:T(8,128)(2,1)S(1)}) custom-call(bf16[512,1024]{1,0:T(8,128)(2,1)S(1)} %shard_map.111.refs_0_, bf16[128,1280]{1,0:T(8,128)(2,1)S(1)} %copy-done.1, bf16[128,2560]{1,0:T(8,128)(2,1)S(1)} %collective-permute-done.3.refs_4_.refs_2_, ...), custom_call_target="tpu_custom_call" | custom-call | tf_op jit(solution)/shard_map/pallas_call | solution.py:359
  75.1 8.7 %collective-permute-done.11.refs_2_ = bf16[256,1280]{1,0:T(8,128)(2,1)S(1)} collective-permute-done((bf16[256,1280]{1,0:T(8,128)(2,1)S(1)}, bf16[256,1280]{1,0:T(8,128)(2,1)S(1)}, u32[]{:S(2)}, u32[]{:S(2)}) %collective-permute-start.11) | collective-permute-done | bytes 655392 | tf_op jit(solution)/shard_map/ppermute | solution.py:28
  84.3 2.1 %shard_map.116 = (f32[256,1280]{1,0:T(8,128)S(1)}, f32[128,1280]{1,0:T(8,128)S(1)}, f32[128,1280]{1,0:T(8,128)S(1)}) custom-call(bf16[512,1024]{1,0:T(8,128)(2,1)S(1)} %shard_map.111.refs_0_, bf16[128,1792]{1,0:T(8,128)(2,1)S(1)} %copy-done.2, bf16[128,1792]{1,0:T(8,128)(2,1)S(1)} %collective-permute-done.refs_0_.refs_2_, ...), custom_call_target="tpu_custom_call" | custom-call | tf_op jit(solution)/shard_map/pallas_call | solution.py:359
  86.4 5.1 %shard_map.117 = (f32[256,1280]{1,0:T(8,128)S(1)}, f32[128,1280]{1,0:T(8,128)S(1)}, f32[128,1280]{1,0:T(8,128)S(1)}, f32[128,2560]{1,0:T(8,128)S(1)}, f32[64,2560]{1,0:T(8,128)S(1)}, /*index=5*/f32[64,2560]{1,0:T(8,128)S(1)}) custom-call(bf16[512,1024]{1,0:T(8,128)(2,1)S(1)} %shard_map.111.refs_0_, bf16[128,1280]{1,0:T(8,128)(2,1)S(1)} %copy-done.1, ...), custom_call_target="tpu_custom_call" | custom-call | tf_op jit(solution)/shard_map/pallas_call | solution.py:359
  91.5 2.6 %collective-permute-done.14.refs_3_.refs_5_ = bf16[256,1280]{1,0:T(8,128)(2,1)S(1)} collective-permute-done((bf16[256,1280]{1,0:T(8,128)(2,1)S(1)}, bf16[256,1280]{1,0:T(8,128)(2,1)S(1)}, u32[]{:S(2)}, u32[]{:S(2)}) %collective-permute-start.14) | collective-permute-done | bytes 655392 | tf_op jit(solution)/shard_map/ppermute | solution.py:28
  94.2 2.4 %collective-permute-start.16 = (bf16[128,2560]{1,0:T(8,128)(2,1)S(1)}, bf16[128,2560]{1,0:T(8,128)(2,1)S(1)}, u32[]{:S(2)}, u32[]{:S(2)}) collective-permute-start(bf16[128,2560]{1,0:T(8,128)(2,1)S(1)} %shard_map.119), channel_id=1, source_target_pairs={{0,2},{2,0},{4,6},{6,4},{8,10},{10,8},{12,14},{14,12},{16,18},{18,... | collective-permute-start | bytes 1966088 | tf_op jit(solution)/shard_map/ppermute | solution.py:28
  97.4 4.1 %collective-permute-done.18.refs_1_ = bf16[128,2560]{1,0:T(8,128)(2,1)S(1)} collective-permute-done((bf16[128,2560]{1,0:T(8,128)(2,1)S(1)}, bf16[128,2560]{1,0:T(8,128)(2,1)S(1)}, u32[]{:S(2)}, u32[]{:S(2)}) %collective-permute-start.18) | collective-permute-done | bytes 655392 | tf_op jit(solution)/shard_map/ppermute | solution.py:28
  102.3 3.6 %collective-permute-done.17.refs_1_ = bf16[128,2560]{1,0:T(8,128)(2,1)S(1)} collective-permute-done((bf16[128,2560]{1,0:T(8,128)(2,1)S(1)}, bf16[128,2560]{1,0:T(8,128)(2,1)S(1)}, u32[]{:S(2)}, u32[]{:S(2)}) %collective-permute-start.17) | collective-permute-done | bytes 655392 | tf_op jit(solution)/shard_map/ppermute | solution.py:28
  108.2 2.5 %psum.14.row_sum = f32[1,256]{1,0:T(1,128)S(1)} all-reduce(f32[1,256]{1,0:T(1,128)S(1)} %get-tuple-element.102), channel_id=1, replica_groups=mesh['dp'=16,'mp'=2] {'mp'}, use_global_device_ids=true, to_apply=%region_0.0 | all-reduce | flops 256 | bytes 2048 | tf_op jit(solution)/shard_map/psum | solution.py:458
  118.0 4.0 %collective-permute-done.22 = bf16[64,2560]{1,0:T(8,128)(2,1)} collective-permute-done((bf16[64,2560]{1,0:T(8,128)(2,1)}, bf16[64,2560]{1,0:T(8,128)(2,1)}, u32[]{:S(2)}, u32[]{:S(2)}) %collective-permute-start.22) | collective-permute-done | bytes 327712 | tf_op jit(solution)/shard_map/ppermute | solution.py:28
  122.0 1.8 %collective-permute-start.25 = (f32[5248]{0:T(1024)S(1)}, f32[5248]{0:T(1024)S(1)}, u32[]{:S(2)}, u32[]{:S(2)}) collective-permute-start(f32[5248]{0:T(1024)S(1)} %add_add_fusion.1), channel_id=1, source_target_pairs={{0,16},{2,18},{4,20},{6,22},{8,24},{10,26},{12,28},{14,30},{16,0},... | collective-permute-start | bytes 62984 | tf_op jit(solution)/shard_map/ppermute | solution.py:28
  123.8 2.6 %collective-permute-start.26 = (f32[5248]{0:T(1024)S(1)}, f32[5248]{0:T(1024)S(1)}, u32[]{:S(2)}, u32[]{:S(2)}) collective-permute-start(f32[5248]{0:T(1024)S(1)} %add_add_fusion.1), channel_id=1, source_target_pairs={{0,24},{2,26},{4,28},{6,30},{8,16},{10,18},{12,20},{14,22},{16,8},... | collective-permute-start | bytes 62984 | tf_op jit(solution)/shard_map/ppermute | solution.py:28
  126.4 4.0 %fusion.8 = (bf16[128,2560]{1,0:T(8,128)(2,1)}, bf16[128,2560]{1,0:T(8,128)(2,1)}) fusion(bf16[128,2560]{1,0:T(8,128)(2,1)S(1)} %copy-done.9, bf16[64,2560]{1,0:T(8,128)(2,1)} %collective-permute-done.23, bf16[64,2560]{1,0:T(8,128)(2,1)} %collective-permute-done.22, f32[128,2560]{1,0:T(8,128)} %copy-done.4, bf16[64,2560]{1,0:T(8,128)(2,1)S(1)} %slice.13, ...), kind=kLoop, calls=%fused_computation.15 | loop fusion | flops 11468800 | bytes 5242880 | tf_op jit(solution)/shard_map/convert_element_type | solution.py:507
  130.5 2.5 %psum.15.terms = f32[1,128]{1,0:T(1,128)S(1)} all-reduce(f32[1,128]{1,0:T(1,128)S(1)} %get-tuple-element.108), channel_id=1, replica_groups=mesh['dp'=16,'mp'=2] {'mp'}, use_global_device_ids=true, to_apply=%region_1.0 | all-reduce | flops 128 | bytes 1024 | tf_op jit(solution)/shard_map/psum | solution.py:481
  133.6 2.2 %shard_map.125 = (f32[256,2560]{1,0:T(8,128)}, f32[1,128]{1,0:T(1,128)}) custom-call(f32[256,2560]{1,0:T(8,128)S(1)} %get-tuple-element.101.grad, f32[1,256]{1,0:T(1,128)S(1)} %copy-done.8, f32[1,2560]{1,0:T(1,128)S(1)} %get-tuple-element.107.col_moment_new, f32[1,128]{1,0:T(1,128)S(1)} %psum.15.terms, f32[1,5248]{1,0:T(1,128)S(1)} %broadcast_in_dim.10.sums.row_total), custom_call_target="tpu_custom_call" | custom-call | tf_op jit(solution)/shard_map/pallas_call | solution.py:313
  (82 shorter events, 27.2 us)
Async XLA Ops:
  0.6 41.5 %collective-permute-start.7 = (bf16[256,2560]{1,0:T(8,128)(2,1)}, bf16[256,2560]{1,0:T(8,128)(2,1)S(1)}, u32[]{:S(2)}, u32[]{:S(2)}) collective-permute-start(bf16[256,2560]{1,0:T(8,128)(2,1)} %refs_5_.1), channel_id=1, source_target_pairs={{0,2},{2,0},{4,6},{6,4},{8,10},{10,8},{12,14},{14,12},{16,18},{18,... | collective-permute-start | bytes 3932168 | tf_op jit(solution)/shard_map/ppermute | solution.py:28
  3.6 38.5 %collective-permute-start.8 = (bf16[256,2560]{1,0:T(8,128)(2,1)}, bf16[256,2560]{1,0:T(8,128)(2,1)S(1)}, u32[]{:S(2)}, u32[]{:S(2)}) collective-permute-start(bf16[256,2560]{1,0:T(8,128)(2,1)} %refs_5_.1), channel_id=1, source_target_pairs={{0,4},{2,6},{4,0},{6,2},{8,12},{10,14},{12,8},{14,10},{16,20},{18,... | collective-permute-start | bytes 3932168 | tf_op jit(solution)/shard_map/ppermute | solution.py:28
  9.6 26.7 %collective-permute-start = (bf16[128,1792]{1,0:T(8,128)(2,1)}, bf16[128,1792]{1,0:T(8,128)(2,1)S(1)}, u32[]{:S(2)}, u32[]{:S(2)}) collective-permute-start(bf16[128,1792]{1,0:T(8,128)(2,1)} %get-tuple-element.61.refs_1_), channel_id=1, source_target_pairs={{0,8},{2,10},{4,12},{6,14},{8,0},{10,2},{12,4},{14,6},{16,24},{18,... | collective-permute-start | bytes 1376264 | tf_op jit(solution)/shard_map/ppermute | solution.py:28
  11.2 26.6 %collective-permute-start.1 = (bf16[128,1792]{1,0:T(8,128)(2,1)}, bf16[128,1792]{1,0:T(8,128)(2,1)S(1)}, u32[]{:S(2)}, u32[]{:S(2)}) collective-permute-start(bf16[128,1792]{1,0:T(8,128)(2,1)} %get-tuple-element.62), channel_id=1, source_target_pairs={{0,16},{2,18},{4,20},{6,22},{8,24},{10,26},{12,28},{14,30},{16,0},... | collective-permute-start | bytes 1376264 | tf_op jit(solution)/shard_map/ppermute | solution.py:28
  13.8 22.5 %collective-permute-start.2 = (bf16[128,512]{1,0:T(8,128)(2,1)}, bf16[128,512]{1,0:T(8,128)(2,1)S(1)}, u32[]{:S(2)}, u32[]{:S(2)}) collective-permute-start(bf16[128,512]{1,0:T(8,128)(2,1)} %get-tuple-element.63), channel_id=1, source_target_pairs={{0,24},{2,26},{4,28},{6,30},{8,16},{10,18},{12,20},{14,22},{16,8},... | collective-permute-start | bytes 393224 | tf_op jit(solution)/shard_map/ppermute | solution.py:28
  38.9 21.8 %collective-permute-start.3 = (bf16[128,2560]{1,0:T(8,128)(2,1)S(1)}, bf16[128,2560]{1,0:T(8,128)(2,1)S(1)}, u32[]{:S(2)}, u32[]{:S(2)}) collective-permute-start(bf16[128,2560]{1,0:T(8,128)(2,1)S(1)} %get-tuple-element.69), channel_id=1, source_target_pairs={{0,8},{2,10},{4,12},{6,14},{8,0},{10,2},{12,4},{14,6},{16,24},{18,... | collective-permute-start | bytes 1966088 | tf_op jit(solution)/shard_map/ppermute | solution.py:28
  41.0 19.0 %collective-permute-start.4 = (bf16[128,1280]{1,0:T(8,128)(2,1)S(1)}, bf16[128,1280]{1,0:T(8,128)(2,1)S(1)}, u32[]{:S(2)}, u32[]{:S(2)}) collective-permute-start(bf16[128,1280]{1,0:T(8,128)(2,1)S(1)} %copy-done.1), channel_id=1, source_target_pairs={{0,16},{2,18},{4,20},{6,22},{8,24},{10,26},{12,28},{14,30},{16,0},... | collective-permute-start | bytes 983048 | tf_op jit(solution)/shard_map/ppermute | solution.py:28
  42.6 24.5 %collective-permute-start.10 = (bf16[128,2560]{1,0:T(8,128)(2,1)S(1)}, bf16[128,2560]{1,0:T(8,128)(2,1)S(1)}, u32[]{:S(2)}, u32[]{:S(2)}) collective-permute-start(bf16[128,2560]{1,0:T(8,128)(2,1)S(1)} %get-tuple-element.78), channel_id=1, source_target_pairs={{0,2},{2,0},{4,6},{6,4},{8,10},{10,8},{12,14},{14,12},{16,18},{18,... | collective-permute-start | bytes 1966088 | tf_op jit(solution)/shard_map/ppermute | solution.py:28
  43.2 23.9 %collective-permute-start.9 = (bf16[128,2560]{1,0:T(8,128)(2,1)S(1)}, bf16[128,2560]{1,0:T(8,128)(2,1)S(1)}, u32[]{:S(2)}, u32[]{:S(2)}) collective-permute-start(bf16[128,2560]{1,0:T(8,128)(2,1)S(1)} %get-tuple-element.77), channel_id=1, source_target_pairs={{0,4},{2,6},{4,0},{6,2},{8,12},{10,14},{12,8},{14,10},{16,20},{18,... | collective-permute-start | bytes 1966088 | tf_op jit(solution)/shard_map/ppermute | solution.py:28
  60.7 9.2 %collective-permute-start.6 = (bf16[128,1280]{1,0:T(8,128)(2,1)S(1)}, bf16[128,1280]{1,0:T(8,128)(2,1)S(1)}, u32[]{:S(2)}, u32[]{:S(2)}) collective-permute-start(bf16[128,1280]{1,0:T(8,128)(2,1)S(1)} %collective-permute-done.4.refs_3_), channel_id=1, source_target_pairs={{0,8},{2,10},{4,12},{6,14},{8,0},{10,2},{12,4},{14,6},{16,24},{18,... | collective-permute-start | bytes 983048 | tf_op jit(solution)/shard_map/ppermute | solution.py:28
  66.1 17.7 %collective-permute-start.11 = (bf16[256,1280]{1,0:T(8,128)(2,1)S(1)}, bf16[256,1280]{1,0:T(8,128)(2,1)S(1)}, u32[]{:S(2)}, u32[]{:S(2)}) collective-permute-start(bf16[256,1280]{1,0:T(8,128)(2,1)S(1)} %get-tuple-element.75), channel_id=1, source_target_pairs={{0,2},{2,0},{4,6},{6,4},{8,10},{10,8},{12,14},{14,12},{16,18},{18,... | collective-permute-start | bytes 1966088 | tf_op jit(solution)/shard_map/ppermute | solution.py:28
  66.7 17.7 %collective-permute-start.12 = (bf16[256,1280]{1,0:T(8,128)(2,1)S(1)}, bf16[256,1280]{1,0:T(8,128)(2,1)S(1)}, u32[]{:S(2)}, u32[]{:S(2)}) collective-permute-start(bf16[256,1280]{1,0:T(8,128)(2,1)S(1)} %get-tuple-element.82), channel_id=1, source_target_pairs={{0,4},{2,6},{4,0},{6,2},{8,12},{10,14},{12,8},{14,10},{16,20},{18,... | collective-permute-start | bytes 1966088 | tf_op jit(solution)/shard_map/ppermute | solution.py:28
  72.0 22.0 %collective-permute-start.14 = (bf16[256,1280]{1,0:T(8,128)(2,1)S(1)}, bf16[256,1280]{1,0:T(8,128)(2,1)S(1)}, u32[]{:S(2)}, u32[]{:S(2)}) collective-permute-start(bf16[256,1280]{1,0:T(8,128)(2,1)S(1)} %get-tuple-element.90), channel_id=1, source_target_pairs={{0,4},{2,6},{4,0},{6,2},{8,12},{10,14},{12,8},{14,10},{16,20},{18,... | collective-permute-start | bytes 1966088 | tf_op jit(solution)/shard_map/ppermute | solution.py:28
  73.6 23.0 %collective-permute-start.13 = (bf16[256,1280]{1,0:T(8,128)(2,1)S(1)}, bf16[256,1280]{1,0:T(8,128)(2,1)S(1)}, u32[]{:S(2)}, u32[]{:S(2)}) collective-permute-start(bf16[256,1280]{1,0:T(8,128)(2,1)S(1)} %get-tuple-element.84), channel_id=1, source_target_pairs={{0,2},{2,0},{4,6},{6,4},{8,10},{10,8},{12,14},{14,12},{16,18},{18,... | collective-permute-start | bytes 1966088 | tf_op jit(solution)/shard_map/ppermute | solution.py:28
  75.1 26.4 %collective-permute-start.18 = (bf16[128,2560]{1,0:T(8,128)(2,1)S(1)}, bf16[128,2560]{1,0:T(8,128)(2,1)S(1)}, u32[]{:S(2)}, u32[]{:S(2)}) collective-permute-start(bf16[128,2560]{1,0:T(8,128)(2,1)S(1)} %get-tuple-element.98), channel_id=1, source_target_pairs={{0,16},{2,18},{4,20},{6,22},{8,24},{10,26},{12,28},{14,30},{16,0},... | collective-permute-start | bytes 1966088 | tf_op jit(solution)/shard_map/ppermute | solution.py:28
  83.8 22.1 %collective-permute-start.17 = (bf16[128,2560]{1,0:T(8,128)(2,1)S(1)}, bf16[128,2560]{1,0:T(8,128)(2,1)S(1)}, u32[]{:S(2)}, u32[]{:S(2)}) collective-permute-start(bf16[128,2560]{1,0:T(8,128)(2,1)S(1)} %get-tuple-element.96), channel_id=1, source_target_pairs={{0,8},{2,10},{4,12},{6,14},{8,0},{10,2},{12,4},{14,6},{16,24},{18,... | collective-permute-start | bytes 1966088 | tf_op jit(solution)/shard_map/ppermute | solution.py:28
  94.2 12.7 %collective-permute-start.16 = (bf16[128,2560]{1,0:T(8,128)(2,1)S(1)}, bf16[128,2560]{1,0:T(8,128)(2,1)S(1)}, u32[]{:S(2)}, u32[]{:S(2)}) collective-permute-start(bf16[128,2560]{1,0:T(8,128)(2,1)S(1)} %shard_map.119), channel_id=1, source_target_pairs={{0,2},{2,0},{4,6},{6,4},{8,10},{10,8},{12,14},{14,12},{16,18},{18,... | collective-permute-start | bytes 1966088 | tf_op jit(solution)/shard_map/ppermute | solution.py:28
  96.7 10.7 %collective-permute-start.15 = (bf16[128,2560]{1,0:T(8,128)(2,1)S(1)}, bf16[128,2560]{1,0:T(8,128)(2,1)S(1)}, u32[]{:S(2)}, u32[]{:S(2)}) collective-permute-start(bf16[128,2560]{1,0:T(8,128)(2,1)S(1)} %shard_map.118), channel_id=1, source_target_pairs={{0,4},{2,6},{4,0},{6,2},{8,12},{10,14},{12,8},{14,10},{16,20},{18,... | collective-permute-start | bytes 1966088 | tf_op jit(solution)/shard_map/ppermute | solution.py:28
  102.3 15.7 %collective-permute-start.23 = (bf16[64,2560]{1,0:T(8,128)(2,1)}, bf16[64,2560]{1,0:T(8,128)(2,1)}, u32[]{:S(2)}, u32[]{:S(2)}) collective-permute-start(bf16[64,2560]{1,0:T(8,128)(2,1)} %shard_map.121), channel_id=1, source_target_pairs={{0,8},{2,10},{4,12},{6,14},{8,0},{10,2},{12,4},{14,6},{16,24},{18,... | collective-permute-start | bytes 983048 | tf_op jit(solution)/shard_map/ppermute | solution.py:28
  106.8 15.2 %collective-permute-start.22 = (bf16[64,2560]{1,0:T(8,128)(2,1)}, bf16[64,2560]{1,0:T(8,128)(2,1)}, u32[]{:S(2)}, u32[]{:S(2)}) collective-permute-start(bf16[64,2560]{1,0:T(8,128)(2,1)} %shard_map.120), channel_id=1, source_target_pairs={{0,16},{2,18},{4,20},{6,22},{8,24},{10,26},{12,28},{14,30},{16,0},... | collective-permute-start | bytes 983048 | tf_op jit(solution)/shard_map/ppermute | solution.py:28
  113.2 4.7 %collective-permute-start.21 = (f32[5248]{0:T(1024)S(1)}, f32[5248]{0:T(1024)S(1)}, u32[]{:S(2)}, u32[]{:S(2)}) collective-permute-start(f32[5248]{0:T(1024)S(1)} %reduce), channel_id=1, source_target_pairs={{0,6},{2,4},{4,2},{6,0},{8,14},{10,12},{12,10},{14,8},{16,22},{18,... | collective-permute-start | bytes 62984 | tf_op jit(solution)/shard_map/ppermute | solution.py:28
  122.0 8.4 %collective-permute-start.24 = (f32[5248]{0:T(1024)S(1)}, f32[5248]{0:T(1024)S(1)}, u32[]{:S(2)}, u32[]{:S(2)}) collective-permute-start(f32[5248]{0:T(1024)S(1)} %add_add_fusion.1), channel_id=1, source_target_pairs={{0,8},{2,10},{4,12},{6,14},{8,0},{10,2},{12,4},{14,6},{16,24},{18,... | collective-permute-start | bytes 62984 | tf_op jit(solution)/shard_map/ppermute | solution.py:28
  122.0 8.4 %collective-permute-start.25 = (f32[5248]{0:T(1024)S(1)}, f32[5248]{0:T(1024)S(1)}, u32[]{:S(2)}, u32[]{:S(2)}) collective-permute-start(f32[5248]{0:T(1024)S(1)} %add_add_fusion.1), channel_id=1, source_target_pairs={{0,16},{2,18},{4,20},{6,22},{8,24},{10,26},{12,28},{14,30},{16,0},... | collective-permute-start | bytes 62984 | tf_op jit(solution)/shard_map/ppermute | solution.py:28
  123.8 6.6 %collective-permute-start.26 = (f32[5248]{0:T(1024)S(1)}, f32[5248]{0:T(1024)S(1)}, u32[]{:S(2)}, u32[]{:S(2)}) collective-permute-start(f32[5248]{0:T(1024)S(1)} %add_add_fusion.1), channel_id=1, source_target_pairs={{0,24},{2,26},{4,28},{6,30},{8,16},{10,18},{12,20},{14,22},{16,8},... | collective-permute-start | bytes 62984 | tf_op jit(solution)/shard_map/ppermute | solution.py:28
  (15 other events, 114.8 us)

commit v20 on v15

--- a/solution.py
+++ b/solution.py
@@ -21,6 +21,12 @@
         1.0 + 3.0 * 0.044715 * values * values
     )
     return (activated, derivative)
+
+
+def gradients(hidden_grad, gate_pre, up_pre):
+    activated, derivative = gelu_parts(gate_pre.astype(jnp.float32))
+    gate_grad = (hidden_grad * up_pre.astype(jnp.float32) * derivative).astype(jnp.bfloat16)
+    return gate_grad, (hidden_grad * activated).astype(jnp.bfloat16)
 
 
 def flip(value, bits, axis="dp"):
@@ -473,11 +479,13 @@
         grad, row_sum, terms = staged_products(out_grad, gate_pre, up_pre, down_weight)
         row_moment_new, sums = column_sums(grad, row_sum, row_moment[None, :], decay, total_units)
         sums = group_sum(sums[0], all_bits[:INNER_BITS])
-        sums, terms = lax.optimization_barrier((sums, terms))
         own_part, from_low, from_high, last_a, last_b = terms
         arrived = jnp.concatenate([from_low, from_high], axis=0).astype(jnp.float32)
         hidden_grad = own_part + arrived + jnp.concatenate([last_a, last_b], axis=0).astype(jnp.float32)
-        sums = group_sum(sums, all_bits[INNER_BITS:])[None, :]
+        gate_grad, up_grad = gradients(hidden_grad, gate_pre, up_pre)
+        first, second, third = [flip(sums, bits) for bits in (4, 8, 12)]
+        first, second, third, gate_grad, up_grad = lax.optimization_barrier((first, second, third, gate_grad, up_grad))
+        sums = ((sums + first) + (second + third))[None, :]
         col_moment_new, ratios = column_step(sums, col_moment[None, :], decay, total_rows)
         ratios = lax.psum(ratios, "mp")
         update, row_mean = final_update(grad, row_moment_new, col_moment_new, ratios, sums, total_rows, total_units)
@@ -502,10 +510,8 @@
         row_factor = jnp.sqrt(row_mean / row_moment_new) / jnp.maximum(1.0, clip_norm)
         col_factor = 1.0 / jnp.sqrt(col_moment_new)
         update = grad * row_factor[:, None] * col_factor[None, :]
-
-    activated, derivative = gelu_parts(gate_pre.astype(jnp.float32))
-    gate_grad = (hidden_grad * up_pre.astype(jnp.float32) * derivative).astype(jnp.bfloat16)
-    up_grad = (hidden_grad * activated).astype(jnp.bfloat16)
+        gate_grad, up_grad = gradients(hidden_grad, gate_pre, up_pre)
+
     return (update, row_moment_new, col_moment_new, row_mean, gate_grad, up_grad)
 
 

time: 136 us -> 132 us (0.971)
  waiting for transfers between devices: 67.3 us -> 63.6 us
    ppermute x27, waiting for transfers between devices: 67.3 us -> 63.6 us  [flip(): return lax.ppermute(value, axis, [(i, i ^ bits) for i in range(size)])]
  transfers between devices with their start and end apart: 27 -> 27, of which waited for: 15 -> 15; matrix products, arithmetic and copies ran while one was open for 3% -> 4% of each run, Pallas kernels for 16% -> 17%
where the time goes in v20:
time: 132 us
  waiting for transfers between devices  63.6 us (48%)
  starting transfers between devices  32.3 us (24%)
  Pallas kernels  24.6 us (19%)
  other arithmetic  5.25 us (4%)
  blocking collectives  4.94 us (4%)
    ppermute x27, waiting for transfers between devices, flip(): return lax.ppermute(value, axis, [(i, i ^ bits) for i in range(size)])  63.6 us
    ppermute x27, starting transfers between devices, flip(): return lax.ppermute(value, axis, [(i, i ^ bits) for i in range(size)])  32.3 us
    pallas_call x5, Pallas kernels, products(): pl.pallas_call(kernel, grid=(steps,), out_shape=[jax.ShapeDtypeStruct((he...  14 us
    convert_element_type x1, other arithmetic, gradients(): return (gate_grad, (hidden_grad * activated).astype(jnp.bfloat16))  3.97 us
    pallas_call x1, Pallas kernels, first_stage(): pl.pallas_call(kernel, grid=(tokens // step,), out_shape=[jax.ShapeDtypeS...  3.84 us
  transfers between devices with their start and end apart: 27, of which 15 were waited for; matrix products, arithmetic and copies ran while one was open for 4% of the time, Pallas kernels for 17%

profile of v20, /device:TPU:0, one launch (start us, length us, event | category | flops | bytes accessed | tf_op | source)
XLA Modules:
  0.0 131.7 jit_solution(8287263118437884055)
XLA Ops:
  0.6 3.0 %collective-permute-start.3 = (bf16[256,2560]{1,0:T(8,128)(2,1)}, bf16[256,2560]{1,0:T(8,128)(2,1)S(1)}, u32[]{:S(2)}, u32[]{:S(2)}) collective-permute-start(bf16[256,2560]{1,0:T(8,128)(2,1)} %refs_5_.1), channel_id=1, source_target_pairs={{0,2},{2,0},{4,6},{6,4},{8,10},{10,8},{12,14},{14,12},{16,18},{18,... | collective-permute-start | bytes 3932168 | tf_op jit(solution)/shard_map/ppermute | solution.py:34
  5.7 3.8 %shard_map.109 = (bf16[128,1024]{1,0:T(8,128)(2,1)}, bf16[128,1280]{1,0:T(8,128)(2,1)}, bf16[128,1792]{1,0:T(8,128)(2,1)}, bf16[128,1792]{1,0:T(8,128)(2,1)}, bf16[128,512]{1,0:T(8,128)(2,1)}) custom-call(s32[2]{0:T(128)} %pad_add_fusion.place, bf16[128,4096]{1,0:T(8,128)(2,1)} %source.1, bf16[128,2560]{1,0:T(8,128)(2,1)} %gate.1, bf16[128,2560]{1,0:T(8,128)(2,1)} %up.1), custom_call_target="tpu_custom_call" | custom-call | tf_op jit(solution)/shard_map/pallas_call | solution.py:122
  9.6 1.6 %collective-permute-start = (bf16[128,1792]{1,0:T(8,128)(2,1)}, bf16[128,1792]{1,0:T(8,128)(2,1)S(1)}, u32[]{:S(2)}, u32[]{:S(2)}) collective-permute-start(bf16[128,1792]{1,0:T(8,128)(2,1)} %get-tuple-element.63.refs_1_), channel_id=1, source_target_pairs={{0,8},{2,10},{4,12},{6,14},{8,0},{10,2},{12,4},{14,6},{16,24},{18,... | collective-permute-start | bytes 1376264 | tf_op jit(solution)/shard_map/ppermute | solution.py:34
  11.2 2.6 %collective-permute-start.1 = (bf16[128,1792]{1,0:T(8,128)(2,1)}, bf16[128,1792]{1,0:T(8,128)(2,1)S(1)}, u32[]{:S(2)}, u32[]{:S(2)}) collective-permute-start(bf16[128,1792]{1,0:T(8,128)(2,1)} %get-tuple-element.64), channel_id=1, source_target_pairs={{0,16},{2,18},{4,20},{6,22},{8,24},{10,26},{12,28},{14,30},{16,0},... | collective-permute-start | bytes 1376264 | tf_op jit(solution)/shard_map/ppermute | solution.py:34
  14.0 22.3 %collective-permute-done.2.refs_2_ = bf16[128,512]{1,0:T(8,128)(2,1)S(1)} collective-permute-done((bf16[128,512]{1,0:T(8,128)(2,1)}, bf16[128,512]{1,0:T(8,128)(2,1)S(1)}, u32[]{:S(2)}, u32[]{:S(2)}) %collective-permute-start.2) | collective-permute-done | bytes 131104 | tf_op jit(solution)/shard_map/ppermute | solution.py:34
  38.0 2.5 %collective-permute-start.5 = (bf16[128,2560]{1,0:T(8,128)(2,1)S(1)}, bf16[128,2560]{1,0:T(8,128)(2,1)S(1)}, u32[]{:S(2)}, u32[]{:S(2)}) collective-permute-start(bf16[128,2560]{1,0:T(8,128)(2,1)S(1)} %get-tuple-element.76), channel_id=1, source_target_pairs={{0,8},{2,10},{4,12},{6,14},{8,0},{10,2},{12,4},{14,6},{16,24},{18,... | collective-permute-start | bytes 1966088 | tf_op jit(solution)/shard_map/ppermute | solution.py:34
  43.4 16.1 %collective-permute-done.6.refs_3_ = bf16[128,1280]{1,0:T(8,128)(2,1)S(1)} collective-permute-done((bf16[128,1280]{1,0:T(8,128)(2,1)S(1)}, bf16[128,1280]{1,0:T(8,128)(2,1)S(1)}, u32[]{:S(2)}, u32[]{:S(2)}) %collective-permute-start.6) | collective-permute-done | bytes 327712 | tf_op jit(solution)/shard_map/ppermute | solution.py:34
  60.2 3.3 %collective-permute-start.8 = (bf16[128,1280]{1,0:T(8,128)(2,1)S(1)}, bf16[128,1280]{1,0:T(8,128)(2,1)S(1)}, u32[]{:S(2)}, u32[]{:S(2)}) collective-permute-start(bf16[128,1280]{1,0:T(8,128)(2,1)S(1)} %collective-permute-done.6.refs_3_), channel_id=1, source_target_pairs={{0,8},{2,10},{4,12},{6,14},{8,0},{10,2},{12,4},{14,6},{16,24},{18,... | collective-permute-start | bytes 983048 | tf_op jit(solution)/shard_map/ppermute | solution.py:34
  63.5 2.0 %shard_map.113 = (bf16[256,1280]{1,0:T(8,128)(2,1)S(1)}, bf16[256,1280]{1,0:T(8,128)(2,1)S(1)}) custom-call(bf16[512,1024]{1,0:T(8,128)(2,1)S(1)} %shard_map.112.refs_0_, bf16[128,1792]{1,0:T(8,128)(2,1)S(1)} %copy-done.2, bf16[128,1792]{1,0:T(8,128)(2,1)S(1)} %collective-permute-done.refs_0_.refs_2_, ...), custom_call_target="tpu_custom_call" | custom-call | tf_op jit(solution)/shard_map/pallas_call | solution.py:365
  66.7 2.8 %shard_map.114 = (bf16[128,2560]{1,0:T(8,128)(2,1)S(1)}, bf16[128,2560]{1,0:T(8,128)(2,1)S(1)}) custom-call(bf16[512,1024]{1,0:T(8,128)(2,1)S(1)} %shard_map.112.refs_0_, bf16[256,2560]{1,0:T(8,128)(2,1)S(1)} %copy-done, bf16[256,2560]{1,0:T(8,128)(2,1)S(1)} %collective-permute-done.3.refs_0_.refs_2_.refs_6_, ...), custom_call_target="tpu_custom_call" | custom-call | tf_op jit(solution)/shard_map/pallas_call | solution.py:365
  69.5 2.1 %shard_map.115 = (bf16[256,1280]{1,0:T(8,128)(2,1)S(1)}, bf16[256,1280]{1,0:T(8,128)(2,1)S(1)}) custom-call(bf16[512,1024]{1,0:T(8,128)(2,1)S(1)} %shard_map.112.refs_0_, bf16[128,1280]{1,0:T(8,128)(2,1)S(1)} %copy-done.1, bf16[128,2560]{1,0:T(8,128)(2,1)S(1)} %collective-permute-done.5.refs_4_.refs_2_, ...), custom_call_target="tpu_custom_call" | custom-call | tf_op jit(solution)/shard_map/pallas_call | solution.py:365
  74.7 8.7 %collective-permute-done.11.refs_2_ = bf16[256,1280]{1,0:T(8,128)(2,1)S(1)} collective-permute-done((bf16[256,1280]{1,0:T(8,128)(2,1)S(1)}, bf16[256,1280]{1,0:T(8,128)(2,1)S(1)}, u32[]{:S(2)}, u32[]{:S(2)}) %collective-permute-start.11) | collective-permute-done | bytes 655392 | tf_op jit(solution)/shard_map/ppermute | solution.py:34
  83.8 2.1 %shard_map.116 = (f32[256,1280]{1,0:T(8,128)S(1)}, f32[128,1280]{1,0:T(8,128)S(1)}, f32[128,1280]{1,0:T(8,128)S(1)}) custom-call(bf16[512,1024]{1,0:T(8,128)(2,1)S(1)} %shard_map.112.refs_0_, bf16[128,1792]{1,0:T(8,128)(2,1)S(1)} %copy-done.2, bf16[128,1792]{1,0:T(8,128)(2,1)S(1)} %collective-permute-done.refs_0_.refs_2_, ...), custom_call_target="tpu_custom_call" | custom-call | tf_op jit(solution)/shard_map/pallas_call | solution.py:365
  86.0 5.1 %shard_map.117 = (f32[256,1280]{1,0:T(8,128)S(1)}, f32[128,1280]{1,0:T(8,128)S(1)}, f32[128,1280]{1,0:T(8,128)S(1)}, f32[128,2560]{1,0:T(8,128)S(1)}, f32[64,2560]{1,0:T(8,128)S(1)}, /*index=5*/f32[64,2560]{1,0:T(8,128)S(1)}) custom-call(bf16[512,1024]{1,0:T(8,128)(2,1)S(1)} %shard_map.112.refs_0_, bf16[128,1280]{1,0:T(8,128)(2,1)S(1)} %copy-done.1, ...), custom_call_target="tpu_custom_call" | custom-call | tf_op jit(solution)/shard_map/pallas_call | solution.py:365
  91.0 2.5 %collective-permute-done.14.refs_3_.refs_5_ = bf16[256,1280]{1,0:T(8,128)(2,1)S(1)} collective-permute-done((bf16[256,1280]{1,0:T(8,128)(2,1)S(1)}, bf16[256,1280]{1,0:T(8,128)(2,1)S(1)}, u32[]{:S(2)}, u32[]{:S(2)}) %collective-permute-start.14) | collective-permute-done | bytes 655392 | tf_op jit(solution)/shard_map/ppermute | solution.py:34
  93.7 2.4 %collective-permute-start.16 = (bf16[128,2560]{1,0:T(8,128)(2,1)S(1)}, bf16[128,2560]{1,0:T(8,128)(2,1)S(1)}, u32[]{:S(2)}, u32[]{:S(2)}) collective-permute-start(bf16[128,2560]{1,0:T(8,128)(2,1)S(1)} %shard_map.119), channel_id=1, source_target_pairs={{0,2},{2,0},{4,6},{6,4},{8,10},{10,8},{12,14},{14,12},{16,18},{18,... | collective-permute-start | bytes 1966088 | tf_op jit(solution)/shard_map/ppermute | solution.py:34
  96.9 4.2 %collective-permute-done.18.refs_1_ = bf16[128,2560]{1,0:T(8,128)(2,1)S(1)} collective-permute-done((bf16[128,2560]{1,0:T(8,128)(2,1)S(1)}, bf16[128,2560]{1,0:T(8,128)(2,1)S(1)}, u32[]{:S(2)}, u32[]{:S(2)}) %collective-permute-start.18) | collective-permute-done | bytes 655392 | tf_op jit(solution)/shard_map/ppermute | solution.py:34
  101.8 3.6 %collective-permute-done.17.refs_1_ = bf16[128,2560]{1,0:T(8,128)(2,1)S(1)} collective-permute-done((bf16[128,2560]{1,0:T(8,128)(2,1)S(1)}, bf16[128,2560]{1,0:T(8,128)(2,1)S(1)}, u32[]{:S(2)}, u32[]{:S(2)}) %collective-permute-start.17) | collective-permute-done | bytes 655392 | tf_op jit(solution)/shard_map/ppermute | solution.py:34
  107.7 2.5 %psum.14.row_sum = f32[1,256]{1,0:T(1,128)S(1)} all-reduce(f32[1,256]{1,0:T(1,128)S(1)} %get-tuple-element.107), channel_id=1, replica_groups=mesh['dp'=16,'mp'=2] {'mp'}, use_global_device_ids=true, to_apply=%region_0.0 | all-reduce | flops 256 | bytes 2048 | tf_op jit(solution)/shard_map/psum | solution.py:465
  112.8 1.7 %collective-permute-start.21 = (f32[5248]{0:T(1024)S(1)}, f32[5248]{0:T(1024)S(1)}, u32[]{:S(2)}, u32[]{:S(2)}) collective-permute-start(f32[5248]{0:T(1024)S(1)} %reduce), channel_id=1, source_target_pairs={{0,6},{2,4},{4,2},{6,0},{8,14},{10,12},{12,10},{14,8},{16,22},{18,... | collective-permute-start | bytes 62984 | tf_op jit(solution)/shard_map/ppermute | solution.py:34
  119.5 2.5 %collective-permute-start.24 = (f32[5248]{0:T(1024)S(1)}, f32[5248]{0:T(1024)S(1)}, u32[]{:S(2)}, u32[]{:S(2)}) collective-permute-start(f32[5248]{0:T(1024)S(1)} %add_add_fusion.1), channel_id=1, source_target_pairs={{0,24},{2,26},{4,28},{6,30},{8,16},{10,18},{12,20},{14,22},{16,8},... | collective-permute-start | bytes 62984 | tf_op jit(solution)/shard_map/ppermute | solution.py:34
  122.3 4.0 %fusion.8 = (bf16[128,2560]{1,0:T(8,128)(2,1)}, bf16[128,2560]{1,0:T(8,128)(2,1)}) fusion(bf16[128,2560]{1,0:T(8,128)(2,1)S(1)} %copy-done.9, bf16[64,2560]{1,0:T(8,128)(2,1)} %collective-permute-done.26, bf16[64,2560]{1,0:T(8,128)(2,1)} %collective-permute-done.25, f32[128,2560]{1,0:T(8,128)} %copy-done.4, bf16[64,2560]{1,0:T(8,128)(2,1)S(1)} %slice.13, ...), kind=kLoop, calls=%fused_computation.15 | loop fusion | flops 11468800 | bytes 5242880 | tf_op jit(solution)/shard_map/convert_element_type | solution.py:29
  126.3 2.5 %psum.15.terms = f32[1,128]{1,0:T(1,128)S(1)} all-reduce(f32[1,128]{1,0:T(1,128)S(1)} %get-tuple-element.115), channel_id=1, replica_groups=mesh['dp'=16,'mp'=2] {'mp'}, use_global_device_ids=true, to_apply=%region_1.0 | all-reduce | flops 128 | bytes 1024 | tf_op jit(solution)/shard_map/psum | solution.py:490
  129.4 2.2 %shard_map.125 = (f32[256,2560]{1,0:T(8,128)}, f32[1,128]{1,0:T(1,128)}) custom-call(f32[256,2560]{1,0:T(8,128)S(1)} %get-tuple-element.106.grad, f32[1,256]{1,0:T(1,128)S(1)} %copy-done.8, f32[1,2560]{1,0:T(1,128)S(1)} %get-tuple-element.114.col_moment_new, f32[1,128]{1,0:T(1,128)S(1)} %psum.15.terms, f32[1,5248]{1,0:T(1,128)S(1)} %broadcast_in_dim.10.sums.row_total), custom_call_target="tpu_custom_call" | custom-call | tf_op jit(solution)/shard_map/pallas_call | solution.py:319
  (82 shorter events, 24.7 us)
Async XLA Ops:
  0.6 35.7 %collective-permute-start.3 = (bf16[256,2560]{1,0:T(8,128)(2,1)}, bf16[256,2560]{1,0:T(8,128)(2,1)S(1)}, u32[]{:S(2)}, u32[]{:S(2)}) collective-permute-start(bf16[256,2560]{1,0:T(8,128)(2,1)} %refs_5_.1), channel_id=1, source_target_pairs={{0,2},{2,0},{4,6},{6,4},{8,10},{10,8},{12,14},{14,12},{16,18},{18,... | collective-permute-start | bytes 3932168 | tf_op jit(solution)/shard_map/ppermute | solution.py:34
  3.6 32.7 %collective-permute-start.4 = (bf16[256,2560]{1,0:T(8,128)(2,1)}, bf16[256,2560]{1,0:T(8,128)(2,1)S(1)}, u32[]{:S(2)}, u32[]{:S(2)}) collective-permute-start(bf16[256,2560]{1,0:T(8,128)(2,1)} %refs_5_.1), channel_id=1, source_target_pairs={{0,4},{2,6},{4,0},{6,2},{8,12},{10,14},{12,8},{14,10},{16,20},{18,... | collective-permute-start | bytes 3932168 | tf_op jit(solution)/shard_map/ppermute | solution.py:34
  9.6 27.2 %collective-permute-start = (bf16[128,1792]{1,0:T(8,128)(2,1)}, bf16[128,1792]{1,0:T(8,128)(2,1)S(1)}, u32[]{:S(2)}, u32[]{:S(2)}) collective-permute-start(bf16[128,1792]{1,0:T(8,128)(2,1)} %get-tuple-element.63.refs_1_), channel_id=1, source_target_pairs={{0,8},{2,10},{4,12},{6,14},{8,0},{10,2},{12,4},{14,6},{16,24},{18,... | collective-permute-start | bytes 1376264 | tf_op jit(solution)/shard_map/ppermute | solution.py:34
  11.2 26.6 %collective-permute-start.1 = (bf16[128,1792]{1,0:T(8,128)(2,1)}, bf16[128,1792]{1,0:T(8,128)(2,1)S(1)}, u32[]{:S(2)}, u32[]{:S(2)}) collective-permute-start(bf16[128,1792]{1,0:T(8,128)(2,1)} %get-tuple-element.64), channel_id=1, source_target_pairs={{0,16},{2,18},{4,20},{6,22},{8,24},{10,26},{12,28},{14,30},{16,0},... | collective-permute-start | bytes 1376264 | tf_op jit(solution)/shard_map/ppermute | solution.py:34
  13.8 22.5 %collective-permute-start.2 = (bf16[128,512]{1,0:T(8,128)(2,1)}, bf16[128,512]{1,0:T(8,128)(2,1)S(1)}, u32[]{:S(2)}, u32[]{:S(2)}) collective-permute-start(bf16[128,512]{1,0:T(8,128)(2,1)} %get-tuple-element.65), channel_id=1, source_target_pairs={{0,24},{2,26},{4,28},{6,30},{8,16},{10,18},{12,20},{14,22},{16,8},... | collective-permute-start | bytes 393224 | tf_op jit(solution)/shard_map/ppermute | solution.py:34
  38.0 22.3 %collective-permute-start.5 = (bf16[128,2560]{1,0:T(8,128)(2,1)S(1)}, bf16[128,2560]{1,0:T(8,128)(2,1)S(1)}, u32[]{:S(2)}, u32[]{:S(2)}) collective-permute-start(bf16[128,2560]{1,0:T(8,128)(2,1)S(1)} %get-tuple-element.76), channel_id=1, source_target_pairs={{0,8},{2,10},{4,12},{6,14},{8,0},{10,2},{12,4},{14,6},{16,24},{18,... | collective-permute-start | bytes 1966088 | tf_op jit(solution)/shard_map/ppermute | solution.py:34
  40.5 19.0 %collective-permute-start.6 = (bf16[128,1280]{1,0:T(8,128)(2,1)S(1)}, bf16[128,1280]{1,0:T(8,128)(2,1)S(1)}, u32[]{:S(2)}, u32[]{:S(2)}) collective-permute-start(bf16[128,1280]{1,0:T(8,128)(2,1)S(1)} %copy-done.1), channel_id=1, source_target_pairs={{0,16},{2,18},{4,20},{6,22},{8,24},{10,26},{12,28},{14,30},{16,0},... | collective-permute-start | bytes 983048 | tf_op jit(solution)/shard_map/ppermute | solution.py:34
  41.7 25.0 %collective-permute-start.10 = (bf16[128,2560]{1,0:T(8,128)(2,1)S(1)}, bf16[128,2560]{1,0:T(8,128)(2,1)S(1)}, u32[]{:S(2)}, u32[]{:S(2)}) collective-permute-start(bf16[128,2560]{1,0:T(8,128)(2,1)S(1)} %get-tuple-element.71), channel_id=1, source_target_pairs={{0,2},{2,0},{4,6},{6,4},{8,10},{10,8},{12,14},{14,12},{16,18},{18,... | collective-permute-start | bytes 1966088 | tf_op jit(solution)/shard_map/ppermute | solution.py:34
  42.2 24.5 %collective-permute-start.9 = (bf16[128,2560]{1,0:T(8,128)(2,1)S(1)}, bf16[128,2560]{1,0:T(8,128)(2,1)S(1)}, u32[]{:S(2)}, u32[]{:S(2)}) collective-permute-start(bf16[128,2560]{1,0:T(8,128)(2,1)S(1)} %get-tuple-element.70), channel_id=1, source_target_pairs={{0,4},{2,6},{4,0},{6,2},{8,12},{10,14},{12,8},{14,10},{16,20},{18,... | collective-permute-start | bytes 1966088 | tf_op jit(solution)/shard_map/ppermute | solution.py:34
  60.2 9.2 %collective-permute-start.8 = (bf16[128,1280]{1,0:T(8,128)(2,1)S(1)}, bf16[128,1280]{1,0:T(8,128)(2,1)S(1)}, u32[]{:S(2)}, u32[]{:S(2)}) collective-permute-start(bf16[128,1280]{1,0:T(8,128)(2,1)S(1)} %collective-permute-done.6.refs_3_), channel_id=1, source_target_pairs={{0,8},{2,10},{4,12},{6,14},{8,0},{10,2},{12,4},{14,6},{16,24},{18,... | collective-permute-start | bytes 983048 | tf_op jit(solution)/shard_map/ppermute | solution.py:34
  65.6 17.7 %collective-permute-start.11 = (bf16[256,1280]{1,0:T(8,128)(2,1)S(1)}, bf16[256,1280]{1,0:T(8,128)(2,1)S(1)}, u32[]{:S(2)}, u32[]{:S(2)}) collective-permute-start(bf16[256,1280]{1,0:T(8,128)(2,1)S(1)} %get-tuple-element.82), channel_id=1, source_target_pairs={{0,2},{2,0},{4,6},{6,4},{8,10},{10,8},{12,14},{14,12},{16,18},{18,... | collective-permute-start | bytes 1966088 | tf_op jit(solution)/shard_map/ppermute | solution.py:34
  66.2 17.7 %collective-permute-start.12 = (bf16[256,1280]{1,0:T(8,128)(2,1)S(1)}, bf16[256,1280]{1,0:T(8,128)(2,1)S(1)}, u32[]{:S(2)}, u32[]{:S(2)}) collective-permute-start(bf16[256,1280]{1,0:T(8,128)(2,1)S(1)} %get-tuple-element.87), channel_id=1, source_target_pairs={{0,4},{2,6},{4,0},{6,2},{8,12},{10,14},{12,8},{14,10},{16,20},{18,... | collective-permute-start | bytes 1966088 | tf_op jit(solution)/shard_map/ppermute | solution.py:34
  71.6 22.0 %collective-permute-start.14 = (bf16[256,1280]{1,0:T(8,128)(2,1)S(1)}, bf16[256,1280]{1,0:T(8,128)(2,1)S(1)}, u32[]{:S(2)}, u32[]{:S(2)}) collective-permute-start(bf16[256,1280]{1,0:T(8,128)(2,1)S(1)} %get-tuple-element.95), channel_id=1, source_target_pairs={{0,4},{2,6},{4,0},{6,2},{8,12},{10,14},{12,8},{14,10},{16,20},{18,... | collective-permute-start | bytes 1966088 | tf_op jit(solution)/shard_map/ppermute | solution.py:34
  73.2 23.0 %collective-permute-start.13 = (bf16[256,1280]{1,0:T(8,128)(2,1)S(1)}, bf16[256,1280]{1,0:T(8,128)(2,1)S(1)}, u32[]{:S(2)}, u32[]{:S(2)}) collective-permute-start(bf16[256,1280]{1,0:T(8,128)(2,1)S(1)} %get-tuple-element.89), channel_id=1, source_target_pairs={{0,2},{2,0},{4,6},{6,4},{8,10},{10,8},{12,14},{14,12},{16,18},{18,... | collective-permute-start | bytes 1966088 | tf_op jit(solution)/shard_map/ppermute | solution.py:34
  74.7 26.4 %collective-permute-start.18 = (bf16[128,2560]{1,0:T(8,128)(2,1)S(1)}, bf16[128,2560]{1,0:T(8,128)(2,1)S(1)}, u32[]{:S(2)}, u32[]{:S(2)}) collective-permute-start(bf16[128,2560]{1,0:T(8,128)(2,1)S(1)} %get-tuple-element.103), channel_id=1, source_target_pairs={{0,16},{2,18},{4,20},{6,22},{8,24},{10,26},{12,28},{14,30},{16,0},... | collective-permute-start | bytes 1966088 | tf_op jit(solution)/shard_map/ppermute | solution.py:34
  83.3 22.1 %collective-permute-start.17 = (bf16[128,2560]{1,0:T(8,128)(2,1)S(1)}, bf16[128,2560]{1,0:T(8,128)(2,1)S(1)}, u32[]{:S(2)}, u32[]{:S(2)}) collective-permute-start(bf16[128,2560]{1,0:T(8,128)(2,1)S(1)} %get-tuple-element.101), channel_id=1, source_target_pairs={{0,8},{2,10},{4,12},{6,14},{8,0},{10,2},{12,4},{14,6},{16,24},{18,... | collective-permute-start | bytes 1966088 | tf_op jit(solution)/shard_map/ppermute | solution.py:34
  93.7 12.7 %collective-permute-start.16 = (bf16[128,2560]{1,0:T(8,128)(2,1)S(1)}, bf16[128,2560]{1,0:T(8,128)(2,1)S(1)}, u32[]{:S(2)}, u32[]{:S(2)}) collective-permute-start(bf16[128,2560]{1,0:T(8,128)(2,1)S(1)} %shard_map.119), channel_id=1, source_target_pairs={{0,2},{2,0},{4,6},{6,4},{8,10},{10,8},{12,14},{14,12},{16,18},{18,... | collective-permute-start | bytes 1966088 | tf_op jit(solution)/shard_map/ppermute | solution.py:34
  96.3 10.7 %collective-permute-start.15 = (bf16[128,2560]{1,0:T(8,128)(2,1)S(1)}, bf16[128,2560]{1,0:T(8,128)(2,1)S(1)}, u32[]{:S(2)}, u32[]{:S(2)}) collective-permute-start(bf16[128,2560]{1,0:T(8,128)(2,1)S(1)} %shard_map.118), channel_id=1, source_target_pairs={{0,4},{2,6},{4,0},{6,2},{8,12},{10,14},{12,8},{14,10},{16,20},{18,... | collective-permute-start | bytes 1966088 | tf_op jit(solution)/shard_map/ppermute | solution.py:34
  101.8 20.1 %collective-permute-start.26 = (bf16[64,2560]{1,0:T(8,128)(2,1)}, bf16[64,2560]{1,0:T(8,128)(2,1)}, u32[]{:S(2)}, u32[]{:S(2)}) collective-permute-start(bf16[64,2560]{1,0:T(8,128)(2,1)} %shard_map.121), channel_id=1, source_target_pairs={{0,8},{2,10},{4,12},{6,14},{8,0},{10,2},{12,4},{14,6},{16,24},{18,... | collective-permute-start | bytes 983048 | tf_op jit(solution)/shard_map/ppermute | solution.py:34
  106.4 15.9 %collective-permute-start.25 = (bf16[64,2560]{1,0:T(8,128)(2,1)}, bf16[64,2560]{1,0:T(8,128)(2,1)}, u32[]{:S(2)}, u32[]{:S(2)}) collective-permute-start(bf16[64,2560]{1,0:T(8,128)(2,1)} %shard_map.120), channel_id=1, source_target_pairs={{0,16},{2,18},{4,20},{6,22},{8,24},{10,26},{12,28},{14,30},{16,0},... | collective-permute-start | bytes 983048 | tf_op jit(solution)/shard_map/ppermute | solution.py:34
  112.8 4.7 %collective-permute-start.21 = (f32[5248]{0:T(1024)S(1)}, f32[5248]{0:T(1024)S(1)}, u32[]{:S(2)}, u32[]{:S(2)}) collective-permute-start(f32[5248]{0:T(1024)S(1)} %reduce), channel_id=1, source_target_pairs={{0,6},{2,4},{4,2},{6,0},{8,14},{10,12},{12,10},{14,8},{16,22},{18,... | collective-permute-start | bytes 62984 | tf_op jit(solution)/shard_map/ppermute | solution.py:34
  117.5 8.7 %collective-permute-start.22 = (f32[5248]{0:T(1024)S(1)}, f32[5248]{0:T(1024)S(1)}, u32[]{:S(2)}, u32[]{:S(2)}) collective-permute-start(f32[5248]{0:T(1024)S(1)} %add_add_fusion.1), channel_id=1, source_target_pairs={{0,8},{2,10},{4,12},{6,14},{8,0},{10,2},{12,4},{14,6},{16,24},{18,... | collective-permute-start | bytes 62984 | tf_op jit(solution)/shard_map/ppermute | solution.py:34
  118.2 8.0 %collective-permute-start.23 = (f32[5248]{0:T(1024)S(1)}, f32[5248]{0:T(1024)S(1)}, u32[]{:S(2)}, u32[]{:S(2)}) collective-permute-start(f32[5248]{0:T(1024)S(1)} %add_add_fusion.1), channel_id=1, source_target_pairs={{0,16},{2,18},{4,20},{6,22},{8,24},{10,26},{12,28},{14,30},{16,0},... | collective-permute-start | bytes 62984 | tf_op jit(solution)/shard_map/ppermute | solution.py:34
  119.5 6.8 %collective-permute-start.24 = (f32[5248]{0:T(1024)S(1)}, f32[5248]{0:T(1024)S(1)}, u32[]{:S(2)}, u32[]{:S(2)}) collective-permute-start(f32[5248]{0:T(1024)S(1)} %add_add_fusion.1), channel_id=1, source_target_pairs={{0,24},{2,26},{4,28},{6,30},{8,16},{10,18},{12,20},{14,22},{16,8},... | collective-permute-start | bytes 62984 | tf_op jit(solution)/shard_map/ppermute | solution.py:34
  (15 other events, 137.5 us)

commit v21 on v20

--- a/solution.py
+++ b/solution.py
@@ -278,21 +278,22 @@
 def column_step(sums, col_moment, decay, total_rows):
     units = col_moment.shape[1]
 
-    def kernel(sums, col_moment, col_moment_new, terms):
+    def kernel(sums, col_moment, col_moment_new, terms, flat_new):
         total = jnp.zeros((1, 128), jnp.float32)
         for at in range(0, units, 128):
             here = slice(at, at + 128)
             new = decay * col_moment[:, here] + (1.0 - decay) * (sums[:, here] / total_rows)
             col_moment_new[:, here] = new
+            flat_new[here] = new[0]
             total = total + sums[:, units + at : units + at + 128] / new
         terms[...] = total
 
     vmem = pl.BlockSpec(memory_space=pltpu.VMEM)
     return pl.pallas_call(
         kernel,
-        out_shape=[jax.ShapeDtypeStruct((1, units), jnp.float32), jax.ShapeDtypeStruct((1, 128), jnp.float32)],
+        out_shape=[jax.ShapeDtypeStruct(shape, jnp.float32) for shape in ((1, units), (1, 128), (units,))],
         in_specs=[vmem] * 2,
-        out_specs=[vmem] * 2,
+        out_specs=[vmem] * 3,
         compiler_params=pltpu.CompilerParams(vmem_limit_bytes=4 << 20),
         cost_estimate=EAGER,
     )(sums, col_moment)
@@ -481,15 +482,16 @@
         sums = group_sum(sums[0], all_bits[:INNER_BITS])
         own_part, from_low, from_high, last_a, last_b = terms
         arrived = jnp.concatenate([from_low, from_high], axis=0).astype(jnp.float32)
-        hidden_grad = own_part + arrived + jnp.concatenate([last_a, last_b], axis=0).astype(jnp.float32)
+        partial, sums = lax.optimization_barrier((own_part + arrived, sums))
+        hidden_grad = partial + jnp.concatenate([last_a, last_b], axis=0).astype(jnp.float32)
         gate_grad, up_grad = gradients(hidden_grad, gate_pre, up_pre)
         first, second, third = [flip(sums, bits) for bits in (4, 8, 12)]
         first, second, third, gate_grad, up_grad = lax.optimization_barrier((first, second, third, gate_grad, up_grad))
         sums = ((sums + first) + (second + third))[None, :]
-        col_moment_new, ratios = column_step(sums, col_moment[None, :], decay, total_rows)
+        moment_row, ratios, col_moment_new = column_step(sums, col_moment[None, :], decay, total_rows)
         ratios = lax.psum(ratios, "mp")
-        update, row_mean = final_update(grad, row_moment_new, col_moment_new, ratios, sums, total_rows, total_units)
-        row_moment_new, col_moment_new, row_mean = row_moment_new[0], col_moment_new[0], row_mean[0, 0]
+        update, row_mean = final_update(grad, row_moment_new, moment_row, ratios, sums, total_rows, total_units)
+        row_moment_new, row_mean = row_moment_new[0], row_mean[0, 0]
     else:
         product, hidden_grad = general_products(
             out_grad, gate_pre, up_pre, down_weight, all_bits[:INNER_BITS], all_bits[INNER_BITS:]

time: 132 us -> 131 us (level)
  waiting for transfers between devices: 63.6 us -> 61.9 us
    ppermute x27, waiting for transfers between devices: 63.6 us -> 61.9 us  [flip(): return lax.ppermute(value, axis, [(i, i ^ bits) for i in range(size)])]
    add x0 -> x1, other arithmetic: none -> 1.54 us  [local(): partial, sums = lax.optimization_barrier((own_part + arrived, sums))]
  transfers between devices with their start and end apart: 27 -> 27, of which waited for: 15 -> 14; matrix products, arithmetic and copies ran while one was open for 4% -> 4% of each run, Pallas kernels for 17% -> 17%
where the time goes in v21:
time: 131 us
  waiting for transfers between devices  61.9 us (47%)
  starting transfers between devices  32.3 us (25%)
  Pallas kernels  25.3 us (19%)
  other arithmetic  5.46 us (4%)
  blocking collectives  4.92 us (4%)
    ppermute x27, waiting for transfers between devices, flip(): return lax.ppermute(value, axis, [(i, i ^ bits) for i in range(size)])  61.9 us
    ppermute x27, starting transfers between devices, flip(): return lax.ppermute(value, axis, [(i, i ^ bits) for i in range(size)])  32.3 us
    pallas_call x5, Pallas kernels, products(): pl.pallas_call(kernel, grid=(steps,), out_shape=[jax.ShapeDtypeStruct((he...  14 us
    pallas_call x1, Pallas kernels, first_stage(): pl.pallas_call(kernel, grid=(tokens // step,), out_shape=[jax.ShapeDtypeS...  3.85 us
    convert_element_type x1, other arithmetic, gradients(): return (gate_grad, (hidden_grad * activated).astype(jnp.bfloat16))  3.27 us
  transfers between devices with their start and end apart: 27, of which 14 were waited for; matrix products, arithmetic and copies ran while one was open for 4% of the time, Pallas kernels for 17%

profile of v21, /device:TPU:0, one launch (start us, length us, event | category | flops | bytes accessed | tf_op | source)
XLA Modules:
  0.0 130.9 jit_solution(15764782483974700836)
XLA Ops:
  0.6 3.0 %collective-permute-start.3 = (bf16[256,2560]{1,0:T(8,128)(2,1)}, bf16[256,2560]{1,0:T(8,128)(2,1)S(1)}, u32[]{:S(2)}, u32[]{:S(2)}) collective-permute-start(bf16[256,2560]{1,0:T(8,128)(2,1)} %refs_5_.1), channel_id=1, source_target_pairs={{0,2},{2,0},{4,6},{6,4},{8,10},{10,8},{12,14},{14,12},{16,18},{18,... | collective-permute-start | bytes 3932168 | tf_op jit(solution)/shard_map/ppermute | solution.py:34
  5.7 3.9 %shard_map.109 = (bf16[128,1024]{1,0:T(8,128)(2,1)}, bf16[128,1280]{1,0:T(8,128)(2,1)}, bf16[128,1792]{1,0:T(8,128)(2,1)}, bf16[128,1792]{1,0:T(8,128)(2,1)}, bf16[128,512]{1,0:T(8,128)(2,1)}) custom-call(s32[2]{0:T(128)} %pad_add_fusion.place, bf16[128,4096]{1,0:T(8,128)(2,1)} %source.1, bf16[128,2560]{1,0:T(8,128)(2,1)} %gate.1, bf16[128,2560]{1,0:T(8,128)(2,1)} %up.1), custom_call_target="tpu_custom_call" | custom-call | tf_op jit(solution)/shard_map/pallas_call | solution.py:122
  9.6 1.6 %collective-permute-start = (bf16[128,1792]{1,0:T(8,128)(2,1)}, bf16[128,1792]{1,0:T(8,128)(2,1)S(1)}, u32[]{:S(2)}, u32[]{:S(2)}) collective-permute-start(bf16[128,1792]{1,0:T(8,128)(2,1)} %get-tuple-element.66.refs_1_), channel_id=1, source_target_pairs={{0,8},{2,10},{4,12},{6,14},{8,0},{10,2},{12,4},{14,6},{16,24},{18,... | collective-permute-start | bytes 1376264 | tf_op jit(solution)/shard_map/ppermute | solution.py:34
  11.2 2.6 %collective-permute-start.1 = (bf16[128,1792]{1,0:T(8,128)(2,1)}, bf16[128,1792]{1,0:T(8,128)(2,1)S(1)}, u32[]{:S(2)}, u32[]{:S(2)}) collective-permute-start(bf16[128,1792]{1,0:T(8,128)(2,1)} %get-tuple-element.67), channel_id=1, source_target_pairs={{0,16},{2,18},{4,20},{6,22},{8,24},{10,26},{12,28},{14,30},{16,0},... | collective-permute-start | bytes 1376264 | tf_op jit(solution)/shard_map/ppermute | solution.py:34
  14.0 22.3 %collective-permute-done.2.refs_2_ = bf16[128,512]{1,0:T(8,128)(2,1)S(1)} collective-permute-done((bf16[128,512]{1,0:T(8,128)(2,1)}, bf16[128,512]{1,0:T(8,128)(2,1)S(1)}, u32[]{:S(2)}, u32[]{:S(2)}) %collective-permute-start.2) | collective-permute-done | bytes 131104 | tf_op jit(solution)/shard_map/ppermute | solution.py:34
  38.0 2.5 %collective-permute-start.5 = (bf16[128,2560]{1,0:T(8,128)(2,1)S(1)}, bf16[128,2560]{1,0:T(8,128)(2,1)S(1)}, u32[]{:S(2)}, u32[]{:S(2)}) collective-permute-start(bf16[128,2560]{1,0:T(8,128)(2,1)S(1)} %get-tuple-element.79), channel_id=1, source_target_pairs={{0,8},{2,10},{4,12},{6,14},{8,0},{10,2},{12,4},{14,6},{16,24},{18,... | collective-permute-start | bytes 1966088 | tf_op jit(solution)/shard_map/ppermute | solution.py:34
  43.4 16.1 %collective-permute-done.6.refs_3_ = bf16[128,1280]{1,0:T(8,128)(2,1)S(1)} collective-permute-done((bf16[128,1280]{1,0:T(8,128)(2,1)S(1)}, bf16[128,1280]{1,0:T(8,128)(2,1)S(1)}, u32[]{:S(2)}, u32[]{:S(2)}) %collective-permute-start.6) | collective-permute-done | bytes 327712 | tf_op jit(solution)/shard_map/ppermute | solution.py:34
  60.2 3.3 %collective-permute-start.8 = (bf16[128,1280]{1,0:T(8,128)(2,1)S(1)}, bf16[128,1280]{1,0:T(8,128)(2,1)S(1)}, u32[]{:S(2)}, u32[]{:S(2)}) collective-permute-start(bf16[128,1280]{1,0:T(8,128)(2,1)S(1)} %collective-permute-done.6.refs_3_), channel_id=1, source_target_pairs={{0,8},{2,10},{4,12},{6,14},{8,0},{10,2},{12,4},{14,6},{16,24},{18,... | collective-permute-start | bytes 983048 | tf_op jit(solution)/shard_map/ppermute | solution.py:34
  63.6 2.0 %shard_map.113 = (bf16[256,1280]{1,0:T(8,128)(2,1)S(1)}, bf16[256,1280]{1,0:T(8,128)(2,1)S(1)}) custom-call(bf16[512,1024]{1,0:T(8,128)(2,1)S(1)} %shard_map.112.refs_0_, bf16[128,1792]{1,0:T(8,128)(2,1)S(1)} %copy-done.2, bf16[128,1792]{1,0:T(8,128)(2,1)S(1)} %collective-permute-done.refs_0_.refs_2_, ...), custom_call_target="tpu_custom_call" | custom-call | tf_op jit(solution)/shard_map/pallas_call | solution.py:366
  66.7 2.8 %shard_map.114 = (bf16[128,2560]{1,0:T(8,128)(2,1)S(1)}, bf16[128,2560]{1,0:T(8,128)(2,1)S(1)}) custom-call(bf16[512,1024]{1,0:T(8,128)(2,1)S(1)} %shard_map.112.refs_0_, bf16[256,2560]{1,0:T(8,128)(2,1)S(1)} %copy-done, bf16[256,2560]{1,0:T(8,128)(2,1)S(1)} %collective-permute-done.3.refs_0_.refs_2_.refs_6_, ...), custom_call_target="tpu_custom_call" | custom-call | tf_op jit(solution)/shard_map/pallas_call | solution.py:366
  69.5 2.1 %shard_map.115 = (bf16[256,1280]{1,0:T(8,128)(2,1)S(1)}, bf16[256,1280]{1,0:T(8,128)(2,1)S(1)}) custom-call(bf16[512,1024]{1,0:T(8,128)(2,1)S(1)} %shard_map.112.refs_0_, bf16[128,1280]{1,0:T(8,128)(2,1)S(1)} %copy-done.1, bf16[128,2560]{1,0:T(8,128)(2,1)S(1)} %collective-permute-done.5.refs_4_.refs_2_, ...), custom_call_target="tpu_custom_call" | custom-call | tf_op jit(solution)/shard_map/pallas_call | solution.py:366
  74.7 8.7 %collective-permute-done.11.refs_2_ = bf16[256,1280]{1,0:T(8,128)(2,1)S(1)} collective-permute-done((bf16[256,1280]{1,0:T(8,128)(2,1)S(1)}, bf16[256,1280]{1,0:T(8,128)(2,1)S(1)}, u32[]{:S(2)}, u32[]{:S(2)}) %collective-permute-start.11) | collective-permute-done | bytes 655392 | tf_op jit(solution)/shard_map/ppermute | solution.py:34
  83.9 2.1 %shard_map.116 = (f32[256,1280]{1,0:T(8,128)S(1)}, f32[128,1280]{1,0:T(8,128)S(1)}, f32[128,1280]{1,0:T(8,128)S(1)}) custom-call(bf16[512,1024]{1,0:T(8,128)(2,1)S(1)} %shard_map.112.refs_0_, bf16[128,1792]{1,0:T(8,128)(2,1)S(1)} %copy-done.2, bf16[128,1792]{1,0:T(8,128)(2,1)S(1)} %collective-permute-done.refs_0_.refs_2_, ...), custom_call_target="tpu_custom_call" | custom-call | tf_op jit(solution)/shard_map/pallas_call | solution.py:366
  86.0 5.1 %shard_map.117 = (f32[256,1280]{1,0:T(8,128)S(1)}, f32[128,1280]{1,0:T(8,128)S(1)}, f32[128,1280]{1,0:T(8,128)S(1)}, f32[128,2560]{1,0:T(8,128)S(1)}, f32[64,2560]{1,0:T(8,128)S(1)}, /*index=5*/f32[64,2560]{1,0:T(8,128)S(1)}) custom-call(bf16[512,1024]{1,0:T(8,128)(2,1)S(1)} %shard_map.112.refs_0_, bf16[128,1280]{1,0:T(8,128)(2,1)S(1)} %copy-done.1, ...), custom_call_target="tpu_custom_call" | custom-call | tf_op jit(solution)/shard_map/pallas_call | solution.py:366
  91.0 2.5 %collective-permute-done.14.refs_3_.refs_5_ = bf16[256,1280]{1,0:T(8,128)(2,1)S(1)} collective-permute-done((bf16[256,1280]{1,0:T(8,128)(2,1)S(1)}, bf16[256,1280]{1,0:T(8,128)(2,1)S(1)}, u32[]{:S(2)}, u32[]{:S(2)}) %collective-permute-start.14) | collective-permute-done | bytes 655392 | tf_op jit(solution)/shard_map/ppermute | solution.py:34
  93.7 2.5 %collective-permute-start.16 = (bf16[128,2560]{1,0:T(8,128)(2,1)S(1)}, bf16[128,2560]{1,0:T(8,128)(2,1)S(1)}, u32[]{:S(2)}, u32[]{:S(2)}) collective-permute-start(bf16[128,2560]{1,0:T(8,128)(2,1)S(1)} %shard_map.119), channel_id=1, source_target_pairs={{0,2},{2,0},{4,6},{6,4},{8,10},{10,8},{12,14},{14,12},{16,18},{18,... | collective-permute-start | bytes 1966088 | tf_op jit(solution)/shard_map/ppermute | solution.py:34
  96.9 4.1 %collective-permute-done.18.refs_1_ = bf16[128,2560]{1,0:T(8,128)(2,1)S(1)} collective-permute-done((bf16[128,2560]{1,0:T(8,128)(2,1)S(1)}, bf16[128,2560]{1,0:T(8,128)(2,1)S(1)}, u32[]{:S(2)}, u32[]{:S(2)}) %collective-permute-start.18) | collective-permute-done | bytes 655392 | tf_op jit(solution)/shard_map/ppermute | solution.py:34
  101.9 3.5 %collective-permute-done.17.refs_1_ = bf16[128,2560]{1,0:T(8,128)(2,1)S(1)} collective-permute-done((bf16[128,2560]{1,0:T(8,128)(2,1)S(1)}, bf16[128,2560]{1,0:T(8,128)(2,1)S(1)}, u32[]{:S(2)}, u32[]{:S(2)}) %collective-permute-start.17) | collective-permute-done | bytes 655392 | tf_op jit(solution)/shard_map/ppermute | solution.py:34
  107.7 2.5 %psum.14.row_sum = f32[1,256]{1,0:T(1,128)S(1)} all-reduce(f32[1,256]{1,0:T(1,128)S(1)} %get-tuple-element.110), channel_id=1, replica_groups=mesh['dp'=16,'mp'=2] {'mp'}, use_global_device_ids=true, to_apply=%region_0.0 | all-reduce | flops 256 | bytes 2048 | tf_op jit(solution)/shard_map/psum | solution.py:466
  112.8 1.7 %collective-permute-start.21 = (f32[5248]{0:T(1024)S(1)}, f32[5248]{0:T(1024)S(1)}, u32[]{:S(2)}, u32[]{:S(2)}) collective-permute-start(f32[5248]{0:T(1024)S(1)} %reduce), channel_id=1, source_target_pairs={{0,6},{2,4},{4,2},{6,0},{8,14},{10,12},{12,10},{14,8},{16,22},{18,... | collective-permute-start | bytes 62984 | tf_op jit(solution)/shard_map/ppermute | solution.py:34
  119.5 2.5 %collective-permute-start.24 = (f32[5248]{0:T(1024)S(1)}, f32[5248]{0:T(1024)S(1)}, u32[]{:S(2)}, u32[]{:S(2)}) collective-permute-start(f32[5248]{0:T(1024)S(1)} %add_add_fusion.1), channel_id=1, source_target_pairs={{0,24},{2,26},{4,28},{6,30},{8,16},{10,18},{12,20},{14,22},{16,8},... | collective-permute-start | bytes 62984 | tf_op jit(solution)/shard_map/ppermute | solution.py:34
  122.3 3.3 %fusion.8 = (bf16[128,2560]{1,0:T(8,128)(2,1)}, bf16[128,2560]{1,0:T(8,128)(2,1)}) fusion(bf16[128,2560]{1,0:T(8,128)(2,1)S(1)} %copy-done.10, f32[128,2560]{1,0:T(8,128)S(1)} %convert_add_fusion.2, bf16[64,2560]{1,0:T(8,128)(2,1)} %collective-permute-done.26, bf16[64,2560]{1,0:T(8,128)(2,1)} %collective-permute-done.25, bf16[128,2560]{1,0:T(8,128)(2,1)S(1)} %copy-done.11), kind=kLoop, calls=%fused_computation.15 | loop fusion | flops 9830400 | bytes 4587520 | tf_op jit(solution)/shard_map/convert_element_type | solution.py:29
  126.2 2.4 %psum.15.terms = f32[1,128]{1,0:T(1,128)S(1)} all-reduce(f32[1,128]{1,0:T(1,128)S(1)} %get-tuple-element.120), channel_id=1, replica_groups=mesh['dp'=16,'mp'=2] {'mp'}, use_global_device_ids=true, to_apply=%region_1.0 | all-reduce | flops 128 | bytes 1024 | tf_op jit(solution)/shard_map/psum | solution.py:492
  128.7 2.2 %shard_map.125 = (f32[256,2560]{1,0:T(8,128)}, f32[1,128]{1,0:T(1,128)}) custom-call(f32[256,2560]{1,0:T(8,128)S(1)} %get-tuple-element.109.grad, f32[1,256]{1,0:T(1,128)S(1)} %copy-done.9, f32[1,2560]{1,0:T(1,128)S(1)} %get-tuple-element.119.col_moment_new, f32[1,128]{1,0:T(1,128)S(1)} %psum.15.terms, f32[1,5248]{1,0:T(1,128)S(1)} %broadcast_in_dim.10.sums.row_total), custom_call_target="tpu_custom_call" | custom-call | tf_op jit(solution)/shard_map/pallas_call | solution.py:320
  (87 shorter events, 24.8 us)
Async XLA Ops:
  0.6 35.7 %collective-permute-start.3 = (bf16[256,2560]{1,0:T(8,128)(2,1)}, bf16[256,2560]{1,0:T(8,128)(2,1)S(1)}, u32[]{:S(2)}, u32[]{:S(2)}) collective-permute-start(bf16[256,2560]{1,0:T(8,128)(2,1)} %refs_5_.1), channel_id=1, source_target_pairs={{0,2},{2,0},{4,6},{6,4},{8,10},{10,8},{12,14},{14,12},{16,18},{18,... | collective-permute-start | bytes 3932168 | tf_op jit(solution)/shard_map/ppermute | solution.py:34
  3.6 32.7 %collective-permute-start.4 = (bf16[256,2560]{1,0:T(8,128)(2,1)}, bf16[256,2560]{1,0:T(8,128)(2,1)S(1)}, u32[]{:S(2)}, u32[]{:S(2)}) collective-permute-start(bf16[256,2560]{1,0:T(8,128)(2,1)} %refs_5_.1), channel_id=1, source_target_pairs={{0,4},{2,6},{4,0},{6,2},{8,12},{10,14},{12,8},{14,10},{16,20},{18,... | collective-permute-start | bytes 3932168 | tf_op jit(solution)/shard_map/ppermute | solution.py:34
  9.6 27.2 %collective-permute-start = (bf16[128,1792]{1,0:T(8,128)(2,1)}, bf16[128,1792]{1,0:T(8,128)(2,1)S(1)}, u32[]{:S(2)}, u32[]{:S(2)}) collective-permute-start(bf16[128,1792]{1,0:T(8,128)(2,1)} %get-tuple-element.66.refs_1_), channel_id=1, source_target_pairs={{0,8},{2,10},{4,12},{6,14},{8,0},{10,2},{12,4},{14,6},{16,24},{18,... | collective-permute-start | bytes 1376264 | tf_op jit(solution)/shard_map/ppermute | solution.py:34
  11.2 26.6 %collective-permute-start.1 = (bf16[128,1792]{1,0:T(8,128)(2,1)}, bf16[128,1792]{1,0:T(8,128)(2,1)S(1)}, u32[]{:S(2)}, u32[]{:S(2)}) collective-permute-start(bf16[128,1792]{1,0:T(8,128)(2,1)} %get-tuple-element.67), channel_id=1, source_target_pairs={{0,16},{2,18},{4,20},{6,22},{8,24},{10,26},{12,28},{14,30},{16,0},... | collective-permute-start | bytes 1376264 | tf_op jit(solution)/shard_map/ppermute | solution.py:34
  13.8 22.5 %collective-permute-start.2 = (bf16[128,512]{1,0:T(8,128)(2,1)}, bf16[128,512]{1,0:T(8,128)(2,1)S(1)}, u32[]{:S(2)}, u32[]{:S(2)}) collective-permute-start(bf16[128,512]{1,0:T(8,128)(2,1)} %get-tuple-element.68), channel_id=1, source_target_pairs={{0,24},{2,26},{4,28},{6,30},{8,16},{10,18},{12,20},{14,22},{16,8},... | collective-permute-start | bytes 393224 | tf_op jit(solution)/shard_map/ppermute | solution.py:34
  38.0 22.3 %collective-permute-start.5 = (bf16[128,2560]{1,0:T(8,128)(2,1)S(1)}, bf16[128,2560]{1,0:T(8,128)(2,1)S(1)}, u32[]{:S(2)}, u32[]{:S(2)}) collective-permute-start(bf16[128,2560]{1,0:T(8,128)(2,1)S(1)} %get-tuple-element.79), channel_id=1, source_target_pairs={{0,8},{2,10},{4,12},{6,14},{8,0},{10,2},{12,4},{14,6},{16,24},{18,... | collective-permute-start | bytes 1966088 | tf_op jit(solution)/shard_map/ppermute | solution.py:34
  40.5 19.0 %collective-permute-start.6 = (bf16[128,1280]{1,0:T(8,128)(2,1)S(1)}, bf16[128,1280]{1,0:T(8,128)(2,1)S(1)}, u32[]{:S(2)}, u32[]{:S(2)}) collective-permute-start(bf16[128,1280]{1,0:T(8,128)(2,1)S(1)} %copy-done.1), channel_id=1, source_target_pairs={{0,16},{2,18},{4,20},{6,22},{8,24},{10,26},{12,28},{14,30},{16,0},... | collective-permute-start | bytes 983048 | tf_op jit(solution)/shard_map/ppermute | solution.py:34
  41.7 25.0 %collective-permute-start.10 = (bf16[128,2560]{1,0:T(8,128)(2,1)S(1)}, bf16[128,2560]{1,0:T(8,128)(2,1)S(1)}, u32[]{:S(2)}, u32[]{:S(2)}) collective-permute-start(bf16[128,2560]{1,0:T(8,128)(2,1)S(1)} %get-tuple-element.74), channel_id=1, source_target_pairs={{0,2},{2,0},{4,6},{6,4},{8,10},{10,8},{12,14},{14,12},{16,18},{18,... | collective-permute-start | bytes 1966088 | tf_op jit(solution)/shard_map/ppermute | solution.py:34
  42.2 24.5 %collective-permute-start.9 = (bf16[128,2560]{1,0:T(8,128)(2,1)S(1)}, bf16[128,2560]{1,0:T(8,128)(2,1)S(1)}, u32[]{:S(2)}, u32[]{:S(2)}) collective-permute-start(bf16[128,2560]{1,0:T(8,128)(2,1)S(1)} %get-tuple-element.73), channel_id=1, source_target_pairs={{0,4},{2,6},{4,0},{6,2},{8,12},{10,14},{12,8},{14,10},{16,20},{18,... | collective-permute-start | bytes 1966088 | tf_op jit(solution)/shard_map/ppermute | solution.py:34
  60.2 9.2 %collective-permute-start.8 = (bf16[128,1280]{1,0:T(8,128)(2,1)S(1)}, bf16[128,1280]{1,0:T(8,128)(2,1)S(1)}, u32[]{:S(2)}, u32[]{:S(2)}) collective-permute-start(bf16[128,1280]{1,0:T(8,128)(2,1)S(1)} %collective-permute-done.6.refs_3_), channel_id=1, source_target_pairs={{0,8},{2,10},{4,12},{6,14},{8,0},{10,2},{12,4},{14,6},{16,24},{18,... | collective-permute-start | bytes 983048 | tf_op jit(solution)/shard_map/ppermute | solution.py:34
  65.6 17.7 %collective-permute-start.11 = (bf16[256,1280]{1,0:T(8,128)(2,1)S(1)}, bf16[256,1280]{1,0:T(8,128)(2,1)S(1)}, u32[]{:S(2)}, u32[]{:S(2)}) collective-permute-start(bf16[256,1280]{1,0:T(8,128)(2,1)S(1)} %get-tuple-element.85), channel_id=1, source_target_pairs={{0,2},{2,0},{4,6},{6,4},{8,10},{10,8},{12,14},{14,12},{16,18},{18,... | collective-permute-start | bytes 1966088 | tf_op jit(solution)/shard_map/ppermute | solution.py:34
  66.2 17.7 %collective-permute-start.12 = (bf16[256,1280]{1,0:T(8,128)(2,1)S(1)}, bf16[256,1280]{1,0:T(8,128)(2,1)S(1)}, u32[]{:S(2)}, u32[]{:S(2)}) collective-permute-start(bf16[256,1280]{1,0:T(8,128)(2,1)S(1)} %get-tuple-element.90), channel_id=1, source_target_pairs={{0,4},{2,6},{4,0},{6,2},{8,12},{10,14},{12,8},{14,10},{16,20},{18,... | collective-permute-start | bytes 1966088 | tf_op jit(solution)/shard_map/ppermute | solution.py:34
  71.6 22.0 %collective-permute-start.14 = (bf16[256,1280]{1,0:T(8,128)(2,1)S(1)}, bf16[256,1280]{1,0:T(8,128)(2,1)S(1)}, u32[]{:S(2)}, u32[]{:S(2)}) collective-permute-start(bf16[256,1280]{1,0:T(8,128)(2,1)S(1)} %get-tuple-element.98), channel_id=1, source_target_pairs={{0,4},{2,6},{4,0},{6,2},{8,12},{10,14},{12,8},{14,10},{16,20},{18,... | collective-permute-start | bytes 1966088 | tf_op jit(solution)/shard_map/ppermute | solution.py:34
  73.2 23.0 %collective-permute-start.13 = (bf16[256,1280]{1,0:T(8,128)(2,1)S(1)}, bf16[256,1280]{1,0:T(8,128)(2,1)S(1)}, u32[]{:S(2)}, u32[]{:S(2)}) collective-permute-start(bf16[256,1280]{1,0:T(8,128)(2,1)S(1)} %get-tuple-element.92), channel_id=1, source_target_pairs={{0,2},{2,0},{4,6},{6,4},{8,10},{10,8},{12,14},{14,12},{16,18},{18,... | collective-permute-start | bytes 1966088 | tf_op jit(solution)/shard_map/ppermute | solution.py:34
  74.7 26.4 %collective-permute-start.18 = (bf16[128,2560]{1,0:T(8,128)(2,1)S(1)}, bf16[128,2560]{1,0:T(8,128)(2,1)S(1)}, u32[]{:S(2)}, u32[]{:S(2)}) collective-permute-start(bf16[128,2560]{1,0:T(8,128)(2,1)S(1)} %get-tuple-element.106), channel_id=1, source_target_pairs={{0,16},{2,18},{4,20},{6,22},{8,24},{10,26},{12,28},{14,30},{16,0},... | collective-permute-start | bytes 1966088 | tf_op jit(solution)/shard_map/ppermute | solution.py:34
  83.3 22.1 %collective-permute-start.17 = (bf16[128,2560]{1,0:T(8,128)(2,1)S(1)}, bf16[128,2560]{1,0:T(8,128)(2,1)S(1)}, u32[]{:S(2)}, u32[]{:S(2)}) collective-permute-start(bf16[128,2560]{1,0:T(8,128)(2,1)S(1)} %get-tuple-element.104), channel_id=1, source_target_pairs={{0,8},{2,10},{4,12},{6,14},{8,0},{10,2},{12,4},{14,6},{16,24},{18,... | collective-permute-start | bytes 1966088 | tf_op jit(solution)/shard_map/ppermute | solution.py:34
  93.7 12.8 %collective-permute-start.16 = (bf16[128,2560]{1,0:T(8,128)(2,1)S(1)}, bf16[128,2560]{1,0:T(8,128)(2,1)S(1)}, u32[]{:S(2)}, u32[]{:S(2)}) collective-permute-start(bf16[128,2560]{1,0:T(8,128)(2,1)S(1)} %shard_map.119), channel_id=1, source_target_pairs={{0,2},{2,0},{4,6},{6,4},{8,10},{10,8},{12,14},{14,12},{16,18},{18,... | collective-permute-start | bytes 1966088 | tf_op jit(solution)/shard_map/ppermute | solution.py:34
  96.3 10.7 %collective-permute-start.15 = (bf16[128,2560]{1,0:T(8,128)(2,1)S(1)}, bf16[128,2560]{1,0:T(8,128)(2,1)S(1)}, u32[]{:S(2)}, u32[]{:S(2)}) collective-permute-start(bf16[128,2560]{1,0:T(8,128)(2,1)S(1)} %shard_map.118), channel_id=1, source_target_pairs={{0,4},{2,6},{4,0},{6,2},{8,12},{10,14},{12,8},{14,10},{16,20},{18,... | collective-permute-start | bytes 1966088 | tf_op jit(solution)/shard_map/ppermute | solution.py:34
  101.9 20.1 %collective-permute-start.26 = (bf16[64,2560]{1,0:T(8,128)(2,1)}, bf16[64,2560]{1,0:T(8,128)(2,1)}, u32[]{:S(2)}, u32[]{:S(2)}) collective-permute-start(bf16[64,2560]{1,0:T(8,128)(2,1)} %shard_map.121), channel_id=1, source_target_pairs={{0,8},{2,10},{4,12},{6,14},{8,0},{10,2},{12,4},{14,6},{16,24},{18,... | collective-permute-start | bytes 983048 | tf_op jit(solution)/shard_map/ppermute | solution.py:34
  106.3 16.0 %collective-permute-start.25 = (bf16[64,2560]{1,0:T(8,128)(2,1)}, bf16[64,2560]{1,0:T(8,128)(2,1)}, u32[]{:S(2)}, u32[]{:S(2)}) collective-permute-start(bf16[64,2560]{1,0:T(8,128)(2,1)} %shard_map.120), channel_id=1, source_target_pairs={{0,16},{2,18},{4,20},{6,22},{8,24},{10,26},{12,28},{14,30},{16,0},... | collective-permute-start | bytes 983048 | tf_op jit(solution)/shard_map/ppermute | solution.py:34
  110.9 5.1 %collective-permute-start.19 = (f32[5248]{0:T(1024)S(1)}, f32[5248]{0:T(1024)S(1)}, u32[]{:S(2)}, u32[]{:S(2)}) collective-permute-start(f32[5248]{0:T(1024)S(1)} %reduce), channel_id=1, source_target_pairs={{0,2},{2,0},{4,6},{6,4},{8,10},{10,8},{12,14},{14,12},{16,18},{18,... | collective-permute-start | bytes 62984 | tf_op jit(solution)/shard_map/ppermute | solution.py:34
  117.5 8.0 %collective-permute-start.22 = (f32[5248]{0:T(1024)S(1)}, f32[5248]{0:T(1024)S(1)}, u32[]{:S(2)}, u32[]{:S(2)}) collective-permute-start(f32[5248]{0:T(1024)S(1)} %add_add_fusion.1), channel_id=1, source_target_pairs={{0,8},{2,10},{4,12},{6,14},{8,0},{10,2},{12,4},{14,6},{16,24},{18,... | collective-permute-start | bytes 62984 | tf_op jit(solution)/shard_map/ppermute | solution.py:34
  118.2 7.4 %collective-permute-start.23 = (f32[5248]{0:T(1024)S(1)}, f32[5248]{0:T(1024)S(1)}, u32[]{:S(2)}, u32[]{:S(2)}) collective-permute-start(f32[5248]{0:T(1024)S(1)} %add_add_fusion.1), channel_id=1, source_target_pairs={{0,16},{2,18},{4,20},{6,22},{8,24},{10,26},{12,28},{14,30},{16,0},... | collective-permute-start | bytes 62984 | tf_op jit(solution)/shard_map/ppermute | solution.py:34
  119.5 6.0 %collective-permute-start.24 = (f32[5248]{0:T(1024)S(1)}, f32[5248]{0:T(1024)S(1)}, u32[]{:S(2)}, u32[]{:S(2)}) collective-permute-start(f32[5248]{0:T(1024)S(1)} %add_add_fusion.1), channel_id=1, source_target_pairs={{0,24},{2,26},{4,28},{6,30},{8,16},{10,18},{12,20},{14,22},{16,8},... | collective-permute-start | bytes 62984 | tf_op jit(solution)/shard_map/ppermute | solution.py:34
  (18 other events, 144.1 us)

commit v22 on v21

--- a/solution.py
+++ b/solution.py
@@ -99,7 +99,7 @@
 def first_stage(out_grad, gate_pre, up_pre, place, rows):
     tokens, units = gate_pre.shape
     half = units // 2
-    step = 32
+    step = 64
 
     def kernel(place, source, gate, up, own, right, message1, message2, message3):
         me, core = place[0], place[1]
@@ -432,7 +432,7 @@
     from_near, right2, share = barrier((from_near, right2, share))
     right3 = flip(right2, z_bit)
     lefts = [(message1, 0), (left1, 0), (left2, 0), (from_near, 0)]
-    left_to_x, left_to_y = products(share, [(lefts, split, sent(q), True)], steps)
+    left_to_x, left_to_y = products(share, [(lefts, split, sent(q), True)], 2)
     left_from_x, left_from_y = flip(left_to_x, x_bit), flip(left_to_y, y_bit)
 
     share, _ = barrier((share, left_to_x))
@@ -443,7 +443,7 @@
     right3, share, to_w, to_z = barrier((right3, share, to_w, to_z))
     from_w, from_z = flip(to_w, w_bit), flip(to_z, z_bit)
     rights = [(right, 0), (from_near, split), (right2, 0), (right3, 0)]
-    right_to_x, right_to_y = products(share, [(rights, units - split, sent(q), True)], steps)
+    right_to_x, right_to_y = products(share, [(rights, units - split, sent(q), True)], 2)
     right_from_x, right_from_y = flip(right_to_x, x_bit), flip(right_to_y, y_bit)
     share, left_from_x, left_from_y, _ = barrier((share, left_from_x, left_from_y, right_to_x))
     left_parts = products(share, [(lefts, split, kept(q), True)], steps)

time: 131 us -> 130 us (level)
  Pallas kernels: 25.3 us -> 23.2 us
  transfers between devices with their start and end apart: 27 -> 27, of which waited for: 14 -> 12; matrix products, arithmetic and copies ran while one was open for 4% -> 4% of each run, Pallas kernels for 17% -> 16%
where the time goes in v22:
time: 130 us
  waiting for transfers between devices  62.7 us (48%)
  starting transfers between devices  32.3 us (25%)
  Pallas kernels  23.2 us (18%)
  other arithmetic  5.46 us (4%)
  blocking collectives  4.92 us (4%)
    ppermute x27, waiting for transfers between devices, flip(): return lax.ppermute(value, axis, [(i, i ^ bits) for i in range(size)])  62.7 us
    ppermute x27, starting transfers between devices, flip(): return lax.ppermute(value, axis, [(i, i ^ bits) for i in range(size)])  32.3 us
    pallas_call x5, Pallas kernels, products(): pl.pallas_call(kernel, grid=(steps,), out_shape=[jax.ShapeDtypeStruct((he...  13.1 us
    convert_element_type x1, other arithmetic, gradients(): return (gate_grad, (hidden_grad * activated).astype(jnp.bfloat16))  3.27 us
    pallas_call x1, Pallas kernels, first_stage(): pl.pallas_call(kernel, grid=(tokens // step,), out_shape=[jax.ShapeDtypeS...  2.72 us
  transfers between devices with their start and end apart: 27, of which 12 were waited for; matrix products, arithmetic and copies ran while one was open for 4% of the time, Pallas kernels for 16%

profile of v22, /device:TPU:0, one launch (start us, length us, event | category | flops | bytes accessed | tf_op | source)
XLA Modules:
  0.0 129.7 jit_solution(6387019482540229526)
XLA Ops:
  0.6 3.0 %collective-permute-start.3 = (bf16[256,2560]{1,0:T(8,128)(2,1)}, bf16[256,2560]{1,0:T(8,128)(2,1)S(1)}, u32[]{:S(2)}, u32[]{:S(2)}) collective-permute-start(bf16[256,2560]{1,0:T(8,128)(2,1)} %refs_5_.1), channel_id=1, source_target_pairs={{0,2},{2,0},{4,6},{6,4},{8,10},{10,8},{12,14},{14,12},{16,18},{18,... | collective-permute-start | bytes 3932168 | tf_op jit(solution)/shard_map/ppermute | solution.py:34
  5.7 2.7 %shard_map.109 = (bf16[128,1024]{1,0:T(8,128)(2,1)}, bf16[128,1280]{1,0:T(8,128)(2,1)}, bf16[128,1792]{1,0:T(8,128)(2,1)}, bf16[128,1792]{1,0:T(8,128)(2,1)}, bf16[128,512]{1,0:T(8,128)(2,1)}) custom-call(s32[2]{0:T(128)} %pad_add_fusion.place, bf16[128,4096]{1,0:T(8,128)(2,1)} %source.1, bf16[128,2560]{1,0:T(8,128)(2,1)} %gate.1, bf16[128,2560]{1,0:T(8,128)(2,1)} %up.1), custom_call_target="tpu_custom_call" | custom-call | tf_op jit(solution)/shard_map/pallas_call | solution.py:122
  8.5 1.6 %collective-permute-start = (bf16[128,1792]{1,0:T(8,128)(2,1)}, bf16[128,1792]{1,0:T(8,128)(2,1)S(1)}, u32[]{:S(2)}, u32[]{:S(2)}) collective-permute-start(bf16[128,1792]{1,0:T(8,128)(2,1)} %get-tuple-element.66.refs_1_), channel_id=1, source_target_pairs={{0,8},{2,10},{4,12},{6,14},{8,0},{10,2},{12,4},{14,6},{16,24},{18,... | collective-permute-start | bytes 1376264 | tf_op jit(solution)/shard_map/ppermute | solution.py:34
  10.0 2.6 %collective-permute-start.1 = (bf16[128,1792]{1,0:T(8,128)(2,1)}, bf16[128,1792]{1,0:T(8,128)(2,1)S(1)}, u32[]{:S(2)}, u32[]{:S(2)}) collective-permute-start(bf16[128,1792]{1,0:T(8,128)(2,1)} %get-tuple-element.67), channel_id=1, source_target_pairs={{0,16},{2,18},{4,20},{6,22},{8,24},{10,26},{12,28},{14,30},{16,0},... | collective-permute-start | bytes 1376264 | tf_op jit(solution)/shard_map/ppermute | solution.py:34
  12.9 22.3 %collective-permute-done.2.refs_2_ = bf16[128,512]{1,0:T(8,128)(2,1)S(1)} collective-permute-done((bf16[128,512]{1,0:T(8,128)(2,1)}, bf16[128,512]{1,0:T(8,128)(2,1)S(1)}, u32[]{:S(2)}, u32[]{:S(2)}) %collective-permute-start.2) | collective-permute-done | bytes 131104 | tf_op jit(solution)/shard_map/ppermute | solution.py:34
  36.8 2.5 %collective-permute-start.5 = (bf16[128,2560]{1,0:T(8,128)(2,1)S(1)}, bf16[128,2560]{1,0:T(8,128)(2,1)S(1)}, u32[]{:S(2)}, u32[]{:S(2)}) collective-permute-start(bf16[128,2560]{1,0:T(8,128)(2,1)S(1)} %get-tuple-element.79), channel_id=1, source_target_pairs={{0,8},{2,10},{4,12},{6,14},{8,0},{10,2},{12,4},{14,6},{16,24},{18,... | collective-permute-start | bytes 1966088 | tf_op jit(solution)/shard_map/ppermute | solution.py:34
  42.2 16.1 %collective-permute-done.6.refs_3_ = bf16[128,1280]{1,0:T(8,128)(2,1)S(1)} collective-permute-done((bf16[128,1280]{1,0:T(8,128)(2,1)S(1)}, bf16[128,1280]{1,0:T(8,128)(2,1)S(1)}, u32[]{:S(2)}, u32[]{:S(2)}) %collective-permute-start.6) | collective-permute-done | bytes 327712 | tf_op jit(solution)/shard_map/ppermute | solution.py:34
  59.1 3.3 %collective-permute-start.8 = (bf16[128,1280]{1,0:T(8,128)(2,1)S(1)}, bf16[128,1280]{1,0:T(8,128)(2,1)S(1)}, u32[]{:S(2)}, u32[]{:S(2)}) collective-permute-start(bf16[128,1280]{1,0:T(8,128)(2,1)S(1)} %collective-permute-done.6.refs_3_), channel_id=1, source_target_pairs={{0,8},{2,10},{4,12},{6,14},{8,0},{10,2},{12,4},{14,6},{16,24},{18,... | collective-permute-start | bytes 983048 | tf_op jit(solution)/shard_map/ppermute | solution.py:34
  62.4 1.6 %shard_map.113 = (bf16[256,1280]{1,0:T(8,128)(2,1)S(1)}, bf16[256,1280]{1,0:T(8,128)(2,1)S(1)}) custom-call(bf16[512,1024]{1,0:T(8,128)(2,1)S(1)} %shard_map.112.refs_0_, bf16[128,1792]{1,0:T(8,128)(2,1)S(1)} %copy-done.2, bf16[128,1792]{1,0:T(8,128)(2,1)S(1)} %collective-permute-done.refs_0_.refs_2_, ...), custom_call_target="tpu_custom_call" | custom-call | tf_op jit(solution)/shard_map/pallas_call | solution.py:366
  65.2 2.8 %shard_map.114 = (bf16[128,2560]{1,0:T(8,128)(2,1)S(1)}, bf16[128,2560]{1,0:T(8,128)(2,1)S(1)}) custom-call(bf16[512,1024]{1,0:T(8,128)(2,1)S(1)} %shard_map.112.refs_0_, bf16[256,2560]{1,0:T(8,128)(2,1)S(1)} %copy-done, bf16[256,2560]{1,0:T(8,128)(2,1)S(1)} %collective-permute-done.3.refs_0_.refs_2_.refs_6_, ...), custom_call_target="tpu_custom_call" | custom-call | tf_op jit(solution)/shard_map/pallas_call | solution.py:366
  69.5 1.6 %collective-permute-start.14 = (bf16[256,1280]{1,0:T(8,128)(2,1)S(1)}, bf16[256,1280]{1,0:T(8,128)(2,1)S(1)}, u32[]{:S(2)}, u32[]{:S(2)}) collective-permute-start(bf16[256,1280]{1,0:T(8,128)(2,1)S(1)} %get-tuple-element.98), channel_id=1, source_target_pairs={{0,4},{2,6},{4,0},{6,2},{8,12},{10,14},{12,8},{14,10},{16,20},{18,... | collective-permute-start | bytes 1966088 | tf_op jit(solution)/shard_map/ppermute | solution.py:34
  72.5 9.2 %collective-permute-done.11.refs_2_ = bf16[256,1280]{1,0:T(8,128)(2,1)S(1)} collective-permute-done((bf16[256,1280]{1,0:T(8,128)(2,1)S(1)}, bf16[256,1280]{1,0:T(8,128)(2,1)S(1)}, u32[]{:S(2)}, u32[]{:S(2)}) %collective-permute-start.11) | collective-permute-done | bytes 655392 | tf_op jit(solution)/shard_map/ppermute | solution.py:34
  82.3 2.1 %shard_map.116 = (f32[256,1280]{1,0:T(8,128)S(1)}, f32[128,1280]{1,0:T(8,128)S(1)}, f32[128,1280]{1,0:T(8,128)S(1)}) custom-call(bf16[512,1024]{1,0:T(8,128)(2,1)S(1)} %shard_map.112.refs_0_, bf16[128,1792]{1,0:T(8,128)(2,1)S(1)} %copy-done.2, bf16[128,1792]{1,0:T(8,128)(2,1)S(1)} %collective-permute-done.refs_0_.refs_2_, ...), custom_call_target="tpu_custom_call" | custom-call | tf_op jit(solution)/shard_map/pallas_call | solution.py:366
  84.4 5.1 %shard_map.117 = (f32[256,1280]{1,0:T(8,128)S(1)}, f32[128,1280]{1,0:T(8,128)S(1)}, f32[128,1280]{1,0:T(8,128)S(1)}, f32[128,2560]{1,0:T(8,128)S(1)}, f32[64,2560]{1,0:T(8,128)S(1)}, /*index=5*/f32[64,2560]{1,0:T(8,128)S(1)}) custom-call(bf16[512,1024]{1,0:T(8,128)(2,1)S(1)} %shard_map.112.refs_0_, bf16[128,1280]{1,0:T(8,128)(2,1)S(1)} %copy-done.1, ...), custom_call_target="tpu_custom_call" | custom-call | tf_op jit(solution)/shard_map/pallas_call | solution.py:366
  89.5 2.5 %collective-permute-done.14.refs_3_.refs_5_ = bf16[256,1280]{1,0:T(8,128)(2,1)S(1)} collective-permute-done((bf16[256,1280]{1,0:T(8,128)(2,1)S(1)}, bf16[256,1280]{1,0:T(8,128)(2,1)S(1)}, u32[]{:S(2)}, u32[]{:S(2)}) %collective-permute-start.14) | collective-permute-done | bytes 655392 | tf_op jit(solution)/shard_map/ppermute | solution.py:34
  92.1 2.5 %collective-permute-start.16 = (bf16[128,2560]{1,0:T(8,128)(2,1)S(1)}, bf16[128,2560]{1,0:T(8,128)(2,1)S(1)}, u32[]{:S(2)}, u32[]{:S(2)}) collective-permute-start(bf16[128,2560]{1,0:T(8,128)(2,1)S(1)} %shard_map.119), channel_id=1, source_target_pairs={{0,2},{2,0},{4,6},{6,4},{8,10},{10,8},{12,14},{14,12},{16,18},{18,... | collective-permute-start | bytes 1966088 | tf_op jit(solution)/shard_map/ppermute | solution.py:34
  95.4 3.6 %collective-permute-done.18.refs_1_ = bf16[128,2560]{1,0:T(8,128)(2,1)S(1)} collective-permute-done((bf16[128,2560]{1,0:T(8,128)(2,1)S(1)}, bf16[128,2560]{1,0:T(8,128)(2,1)S(1)}, u32[]{:S(2)}, u32[]{:S(2)}) %collective-permute-start.18) | collective-permute-done | bytes 655392 | tf_op jit(solution)/shard_map/ppermute | solution.py:34
  99.8 4.1 %collective-permute-done.17.refs_1_ = bf16[128,2560]{1,0:T(8,128)(2,1)S(1)} collective-permute-done((bf16[128,2560]{1,0:T(8,128)(2,1)S(1)}, bf16[128,2560]{1,0:T(8,128)(2,1)S(1)}, u32[]{:S(2)}, u32[]{:S(2)}) %collective-permute-start.17) | collective-permute-done | bytes 655392 | tf_op jit(solution)/shard_map/ppermute | solution.py:34
  106.2 2.5 %psum.14.row_sum = f32[1,256]{1,0:T(1,128)S(1)} all-reduce(f32[1,256]{1,0:T(1,128)S(1)} %get-tuple-element.110), channel_id=1, replica_groups=mesh['dp'=16,'mp'=2] {'mp'}, use_global_device_ids=true, to_apply=%region_0.0 | all-reduce | flops 256 | bytes 2048 | tf_op jit(solution)/shard_map/psum | solution.py:466
  114.5 2.0 %collective-permute-done.21 = f32[5248]{0:T(1024)S(1)} collective-permute-done((f32[5248]{0:T(1024)S(1)}, f32[5248]{0:T(1024)S(1)}, u32[]{:S(2)}, u32[]{:S(2)}) %collective-permute-start.21) | collective-permute-done | bytes 21024 | tf_op jit(solution)/shard_map/ppermute | solution.py:34
  118.5 2.5 %collective-permute-start.24 = (f32[5248]{0:T(1024)S(1)}, f32[5248]{0:T(1024)S(1)}, u32[]{:S(2)}, u32[]{:S(2)}) collective-permute-start(f32[5248]{0:T(1024)S(1)} %add_add_fusion.1), channel_id=1, source_target_pairs={{0,24},{2,26},{4,28},{6,30},{8,16},{10,18},{12,20},{14,22},{16,8},... | collective-permute-start | bytes 62984 | tf_op jit(solution)/shard_map/ppermute | solution.py:34
  121.0 3.3 %fusion.8 = (bf16[128,2560]{1,0:T(8,128)(2,1)}, bf16[128,2560]{1,0:T(8,128)(2,1)}) fusion(bf16[128,2560]{1,0:T(8,128)(2,1)S(1)} %copy-done.10, f32[128,2560]{1,0:T(8,128)S(1)} %convert_add_fusion.2, bf16[64,2560]{1,0:T(8,128)(2,1)} %collective-permute-done.26, bf16[64,2560]{1,0:T(8,128)(2,1)} %collective-permute-done.25, bf16[128,2560]{1,0:T(8,128)(2,1)S(1)} %copy-done.11), kind=kLoop, calls=%fused_computation.15 | loop fusion | flops 9830400 | bytes 4587520 | tf_op jit(solution)/shard_map/convert_element_type | solution.py:29
  125.0 2.4 %psum.15.terms = f32[1,128]{1,0:T(1,128)S(1)} all-reduce(f32[1,128]{1,0:T(1,128)S(1)} %get-tuple-element.120), channel_id=1, replica_groups=mesh['dp'=16,'mp'=2] {'mp'}, use_global_device_ids=true, to_apply=%region_1.0 | all-reduce | flops 128 | bytes 1024 | tf_op jit(solution)/shard_map/psum | solution.py:492
  127.4 2.2 %shard_map.125 = (f32[256,2560]{1,0:T(8,128)}, f32[1,128]{1,0:T(1,128)}) custom-call(f32[256,2560]{1,0:T(8,128)S(1)} %get-tuple-element.109.grad, f32[1,256]{1,0:T(1,128)S(1)} %copy-done.9, f32[1,2560]{1,0:T(1,128)S(1)} %get-tuple-element.119.col_moment_new, f32[1,128]{1,0:T(1,128)S(1)} %psum.15.terms, f32[1,5248]{1,0:T(1,128)S(1)} %broadcast_in_dim.10.sums.row_total), custom_call_target="tpu_custom_call" | custom-call | tf_op jit(solution)/shard_map/pallas_call | solution.py:320
  (87 shorter events, 24.7 us)
Async XLA Ops:
  0.6 34.5 %collective-permute-start.3 = (bf16[256,2560]{1,0:T(8,128)(2,1)}, bf16[256,2560]{1,0:T(8,128)(2,1)S(1)}, u32[]{:S(2)}, u32[]{:S(2)}) collective-permute-start(bf16[256,2560]{1,0:T(8,128)(2,1)} %refs_5_.1), channel_id=1, source_target_pairs={{0,2},{2,0},{4,6},{6,4},{8,10},{10,8},{12,14},{14,12},{16,18},{18,... | collective-permute-start | bytes 3932168 | tf_op jit(solution)/shard_map/ppermute | solution.py:34
  3.6 31.5 %collective-permute-start.4 = (bf16[256,2560]{1,0:T(8,128)(2,1)}, bf16[256,2560]{1,0:T(8,128)(2,1)S(1)}, u32[]{:S(2)}, u32[]{:S(2)}) collective-permute-start(bf16[256,2560]{1,0:T(8,128)(2,1)} %refs_5_.1), channel_id=1, source_target_pairs={{0,4},{2,6},{4,0},{6,2},{8,12},{10,14},{12,8},{14,10},{16,20},{18,... | collective-permute-start | bytes 3932168 | tf_op jit(solution)/shard_map/ppermute | solution.py:34
  8.5 27.2 %collective-permute-start = (bf16[128,1792]{1,0:T(8,128)(2,1)}, bf16[128,1792]{1,0:T(8,128)(2,1)S(1)}, u32[]{:S(2)}, u32[]{:S(2)}) collective-permute-start(bf16[128,1792]{1,0:T(8,128)(2,1)} %get-tuple-element.66.refs_1_), channel_id=1, source_target_pairs={{0,8},{2,10},{4,12},{6,14},{8,0},{10,2},{12,4},{14,6},{16,24},{18,... | collective-permute-start | bytes 1376264 | tf_op jit(solution)/shard_map/ppermute | solution.py:34
  10.0 26.6 %collective-permute-start.1 = (bf16[128,1792]{1,0:T(8,128)(2,1)}, bf16[128,1792]{1,0:T(8,128)(2,1)S(1)}, u32[]{:S(2)}, u32[]{:S(2)}) collective-permute-start(bf16[128,1792]{1,0:T(8,128)(2,1)} %get-tuple-element.67), channel_id=1, source_target_pairs={{0,16},{2,18},{4,20},{6,22},{8,24},{10,26},{12,28},{14,30},{16,0},... | collective-permute-start | bytes 1376264 | tf_op jit(solution)/shard_map/ppermute | solution.py:34
  12.6 22.5 %collective-permute-start.2 = (bf16[128,512]{1,0:T(8,128)(2,1)}, bf16[128,512]{1,0:T(8,128)(2,1)S(1)}, u32[]{:S(2)}, u32[]{:S(2)}) collective-permute-start(bf16[128,512]{1,0:T(8,128)(2,1)} %get-tuple-element.68), channel_id=1, source_target_pairs={{0,24},{2,26},{4,28},{6,30},{8,16},{10,18},{12,20},{14,22},{16,8},... | collective-permute-start | bytes 393224 | tf_op jit(solution)/shard_map/ppermute | solution.py:34
  36.8 22.3 %collective-permute-start.5 = (bf16[128,2560]{1,0:T(8,128)(2,1)S(1)}, bf16[128,2560]{1,0:T(8,128)(2,1)S(1)}, u32[]{:S(2)}, u32[]{:S(2)}) collective-permute-start(bf16[128,2560]{1,0:T(8,128)(2,1)S(1)} %get-tuple-element.79), channel_id=1, source_target_pairs={{0,8},{2,10},{4,12},{6,14},{8,0},{10,2},{12,4},{14,6},{16,24},{18,... | collective-permute-start | bytes 1966088 | tf_op jit(solution)/shard_map/ppermute | solution.py:34
  39.4 19.0 %collective-permute-start.6 = (bf16[128,1280]{1,0:T(8,128)(2,1)S(1)}, bf16[128,1280]{1,0:T(8,128)(2,1)S(1)}, u32[]{:S(2)}, u32[]{:S(2)}) collective-permute-start(bf16[128,1280]{1,0:T(8,128)(2,1)S(1)} %copy-done.1), channel_id=1, source_target_pairs={{0,16},{2,18},{4,20},{6,22},{8,24},{10,26},{12,28},{14,30},{16,0},... | collective-permute-start | bytes 983048 | tf_op jit(solution)/shard_map/ppermute | solution.py:34
  40.5 24.6 %collective-permute-start.10 = (bf16[128,2560]{1,0:T(8,128)(2,1)S(1)}, bf16[128,2560]{1,0:T(8,128)(2,1)S(1)}, u32[]{:S(2)}, u32[]{:S(2)}) collective-permute-start(bf16[128,2560]{1,0:T(8,128)(2,1)S(1)} %get-tuple-element.74), channel_id=1, source_target_pairs={{0,2},{2,0},{4,6},{6,4},{8,10},{10,8},{12,14},{14,12},{16,18},{18,... | collective-permute-start | bytes 1966088 | tf_op jit(solution)/shard_map/ppermute | solution.py:34
  41.1 24.1 %collective-permute-start.9 = (bf16[128,2560]{1,0:T(8,128)(2,1)S(1)}, bf16[128,2560]{1,0:T(8,128)(2,1)S(1)}, u32[]{:S(2)}, u32[]{:S(2)}) collective-permute-start(bf16[128,2560]{1,0:T(8,128)(2,1)S(1)} %get-tuple-element.73), channel_id=1, source_target_pairs={{0,4},{2,6},{4,0},{6,2},{8,12},{10,14},{12,8},{14,10},{16,20},{18,... | collective-permute-start | bytes 1966088 | tf_op jit(solution)/shard_map/ppermute | solution.py:34
  59.1 8.8 %collective-permute-start.8 = (bf16[128,1280]{1,0:T(8,128)(2,1)S(1)}, bf16[128,1280]{1,0:T(8,128)(2,1)S(1)}, u32[]{:S(2)}, u32[]{:S(2)}) collective-permute-start(bf16[128,1280]{1,0:T(8,128)(2,1)S(1)} %collective-permute-done.6.refs_3_), channel_id=1, source_target_pairs={{0,8},{2,10},{4,12},{6,14},{8,0},{10,2},{12,4},{14,6},{16,24},{18,... | collective-permute-start | bytes 983048 | tf_op jit(solution)/shard_map/ppermute | solution.py:34
  64.0 17.7 %collective-permute-start.11 = (bf16[256,1280]{1,0:T(8,128)(2,1)S(1)}, bf16[256,1280]{1,0:T(8,128)(2,1)S(1)}, u32[]{:S(2)}, u32[]{:S(2)}) collective-permute-start(bf16[256,1280]{1,0:T(8,128)(2,1)S(1)} %get-tuple-element.85), channel_id=1, source_target_pairs={{0,2},{2,0},{4,6},{6,4},{8,10},{10,8},{12,14},{14,12},{16,18},{18,... | collective-permute-start | bytes 1966088 | tf_op jit(solution)/shard_map/ppermute | solution.py:34
  64.6 17.7 %collective-permute-start.12 = (bf16[256,1280]{1,0:T(8,128)(2,1)S(1)}, bf16[256,1280]{1,0:T(8,128)(2,1)S(1)}, u32[]{:S(2)}, u32[]{:S(2)}) collective-permute-start(bf16[256,1280]{1,0:T(8,128)(2,1)S(1)} %get-tuple-element.90), channel_id=1, source_target_pairs={{0,4},{2,6},{4,0},{6,2},{8,12},{10,14},{12,8},{14,10},{16,20},{18,... | collective-permute-start | bytes 1966088 | tf_op jit(solution)/shard_map/ppermute | solution.py:34
  69.5 22.5 %collective-permute-start.14 = (bf16[256,1280]{1,0:T(8,128)(2,1)S(1)}, bf16[256,1280]{1,0:T(8,128)(2,1)S(1)}, u32[]{:S(2)}, u32[]{:S(2)}) collective-permute-start(bf16[256,1280]{1,0:T(8,128)(2,1)S(1)} %get-tuple-element.98), channel_id=1, source_target_pairs={{0,4},{2,6},{4,0},{6,2},{8,12},{10,14},{12,8},{14,10},{16,20},{18,... | collective-permute-start | bytes 1966088 | tf_op jit(solution)/shard_map/ppermute | solution.py:34
  71.1 23.6 %collective-permute-start.13 = (bf16[256,1280]{1,0:T(8,128)(2,1)S(1)}, bf16[256,1280]{1,0:T(8,128)(2,1)S(1)}, u32[]{:S(2)}, u32[]{:S(2)}) collective-permute-start(bf16[256,1280]{1,0:T(8,128)(2,1)S(1)} %get-tuple-element.92), channel_id=1, source_target_pairs={{0,2},{2,0},{4,6},{6,4},{8,10},{10,8},{12,14},{14,12},{16,18},{18,... | collective-permute-start | bytes 1966088 | tf_op jit(solution)/shard_map/ppermute | solution.py:34
  72.5 26.4 %collective-permute-start.18 = (bf16[128,2560]{1,0:T(8,128)(2,1)S(1)}, bf16[128,2560]{1,0:T(8,128)(2,1)S(1)}, u32[]{:S(2)}, u32[]{:S(2)}) collective-permute-start(bf16[128,2560]{1,0:T(8,128)(2,1)S(1)} %get-tuple-element.106), channel_id=1, source_target_pairs={{0,16},{2,18},{4,20},{6,22},{8,24},{10,26},{12,28},{14,30},{16,0},... | collective-permute-start | bytes 1966088 | tf_op jit(solution)/shard_map/ppermute | solution.py:34
  81.8 22.1 %collective-permute-start.17 = (bf16[128,2560]{1,0:T(8,128)(2,1)S(1)}, bf16[128,2560]{1,0:T(8,128)(2,1)S(1)}, u32[]{:S(2)}, u32[]{:S(2)}) collective-permute-start(bf16[128,2560]{1,0:T(8,128)(2,1)S(1)} %get-tuple-element.104), channel_id=1, source_target_pairs={{0,8},{2,10},{4,12},{6,14},{8,0},{10,2},{12,4},{14,6},{16,24},{18,... | collective-permute-start | bytes 1966088 | tf_op jit(solution)/shard_map/ppermute | solution.py:34
  92.1 12.8 %collective-permute-start.16 = (bf16[128,2560]{1,0:T(8,128)(2,1)S(1)}, bf16[128,2560]{1,0:T(8,128)(2,1)S(1)}, u32[]{:S(2)}, u32[]{:S(2)}) collective-permute-start(bf16[128,2560]{1,0:T(8,128)(2,1)S(1)} %shard_map.119), channel_id=1, source_target_pairs={{0,2},{2,0},{4,6},{6,4},{8,10},{10,8},{12,14},{14,12},{16,18},{18,... | collective-permute-start | bytes 1966088 | tf_op jit(solution)/shard_map/ppermute | solution.py:34
  94.8 10.7 %collective-permute-start.15 = (bf16[128,2560]{1,0:T(8,128)(2,1)S(1)}, bf16[128,2560]{1,0:T(8,128)(2,1)S(1)}, u32[]{:S(2)}, u32[]{:S(2)}) collective-permute-start(bf16[128,2560]{1,0:T(8,128)(2,1)S(1)} %shard_map.118), channel_id=1, source_target_pairs={{0,4},{2,6},{4,0},{6,2},{8,12},{10,14},{12,8},{14,10},{16,20},{18,... | collective-permute-start | bytes 1966088 | tf_op jit(solution)/shard_map/ppermute | solution.py:34
  99.8 21.2 %collective-permute-start.26 = (bf16[64,2560]{1,0:T(8,128)(2,1)}, bf16[64,2560]{1,0:T(8,128)(2,1)}, u32[]{:S(2)}, u32[]{:S(2)}) collective-permute-start(bf16[64,2560]{1,0:T(8,128)(2,1)} %shard_map.121), channel_id=1, source_target_pairs={{0,8},{2,10},{4,12},{6,14},{8,0},{10,2},{12,4},{14,6},{16,24},{18,... | collective-permute-start | bytes 983048 | tf_op jit(solution)/shard_map/ppermute | solution.py:34
  104.8 16.3 %collective-permute-start.25 = (bf16[64,2560]{1,0:T(8,128)(2,1)}, bf16[64,2560]{1,0:T(8,128)(2,1)}, u32[]{:S(2)}, u32[]{:S(2)}) collective-permute-start(bf16[64,2560]{1,0:T(8,128)(2,1)} %shard_map.120), channel_id=1, source_target_pairs={{0,16},{2,18},{4,20},{6,22},{8,24},{10,26},{12,28},{14,30},{16,0},... | collective-permute-start | bytes 983048 | tf_op jit(solution)/shard_map/ppermute | solution.py:34
  109.4 5.1 %collective-permute-start.19 = (f32[5248]{0:T(1024)S(1)}, f32[5248]{0:T(1024)S(1)}, u32[]{:S(2)}, u32[]{:S(2)}) collective-permute-start(f32[5248]{0:T(1024)S(1)} %reduce), channel_id=1, source_target_pairs={{0,2},{2,0},{4,6},{6,4},{8,10},{10,8},{12,14},{14,12},{16,18},{18,... | collective-permute-start | bytes 62984 | tf_op jit(solution)/shard_map/ppermute | solution.py:34
  116.6 7.7 %collective-permute-start.22 = (f32[5248]{0:T(1024)S(1)}, f32[5248]{0:T(1024)S(1)}, u32[]{:S(2)}, u32[]{:S(2)}) collective-permute-start(f32[5248]{0:T(1024)S(1)} %add_add_fusion.1), channel_id=1, source_target_pairs={{0,8},{2,10},{4,12},{6,14},{8,0},{10,2},{12,4},{14,6},{16,24},{18,... | collective-permute-start | bytes 62984 | tf_op jit(solution)/shard_map/ppermute | solution.py:34
  117.0 7.4 %collective-permute-start.23 = (f32[5248]{0:T(1024)S(1)}, f32[5248]{0:T(1024)S(1)}, u32[]{:S(2)}, u32[]{:S(2)}) collective-permute-start(f32[5248]{0:T(1024)S(1)} %add_add_fusion.1), channel_id=1, source_target_pairs={{0,16},{2,18},{4,20},{6,22},{8,24},{10,26},{12,28},{14,30},{16,0},... | collective-permute-start | bytes 62984 | tf_op jit(solution)/shard_map/ppermute | solution.py:34
  118.5 5.8 %collective-permute-start.24 = (f32[5248]{0:T(1024)S(1)}, f32[5248]{0:T(1024)S(1)}, u32[]{:S(2)}, u32[]{:S(2)}) collective-permute-start(f32[5248]{0:T(1024)S(1)} %add_add_fusion.1), channel_id=1, source_target_pairs={{0,24},{2,26},{4,28},{6,30},{8,16},{10,18},{12,20},{14,22},{16,8},... | collective-permute-start | bytes 62984 | tf_op jit(solution)/shard_map/ppermute | solution.py:34
  (18 other events, 144.2 us)

commit v23 on v22

--- a/solution.py
+++ b/solution.py
@@ -438,7 +438,7 @@
     share, _ = barrier((share, left_to_x))
     weights = [(piece, 0) for piece in (down_weight, weight1, weight2, weight3a, weight3b)]
     to_w, to_z = products(
-        share, [(weights, units, [(high_sent(t), jnp.bfloat16), (low_sent(t), jnp.bfloat16)], False)], steps
+        share, [(weights, units, [(high_sent(t), jnp.bfloat16), (low_sent(t), jnp.bfloat16)], False)], 2
     )
     right3, share, to_w, to_z = barrier((right3, share, to_w, to_z))
     from_w, from_z = flip(to_w, w_bit), flip(to_z, z_bit)

time: 130 us -> 133 us (1.023)
  starting transfers between devices: 32.3 us -> 34.7 us
  waiting for transfers between devices: 62.7 us -> 64.1 us
    ppermute x27, starting transfers between devices: 32.3 us -> 34.7 us  [flip(): return lax.ppermute(value, axis, [(i, i ^ bits) for i in range(size)])]
  transfers between devices with their start and end apart: 27 -> 27, of which waited for: 12 -> 14; matrix products, arithmetic and copies ran while one was open for 4% -> 4% of each run, Pallas kernels for 16% -> 15%
where the time goes in v23:
time: 133 us
  waiting for transfers between devices  64.1 us (48%)
  starting transfers between devices  34.7 us (26%)
  Pallas kernels  22.6 us (17%)
  other arithmetic  5.46 us (4%)
  blocking collectives  4.92 us (4%)
    ppermute x27, waiting for transfers between devices, flip(): return lax.ppermute(value, axis, [(i, i ^ bits) for i in range(size)])  64.1 us
    ppermute x27, starting transfers between devices, flip(): return lax.ppermute(value, axis, [(i, i ^ bits) for i in range(size)])  34.7 us
    pallas_call x5, Pallas kernels, products(): pl.pallas_call(kernel, grid=(steps,), out_shape=[jax.ShapeDtypeStruct((he...  12.5 us
    convert_element_type x1, other arithmetic, gradients(): return (gate_grad, (hidden_grad * activated).astype(jnp.bfloat16))  3.27 us
    pallas_call x1, Pallas kernels, first_stage(): pl.pallas_call(kernel, grid=(tokens // step,), out_shape=[jax.ShapeDtypeS...  2.72 us
  transfers between devices with their start and end apart: 27, of which 14 were waited for; matrix products, arithmetic and copies ran while one was open for 4% of the time, Pallas kernels for 15%

profile of v23, /device:TPU:0, one launch (start us, length us, event | category | flops | bytes accessed | tf_op | source)
XLA Modules:
  0.0 132.7 jit_solution(13814773500814886673)
XLA Ops:
  0.6 3.0 %collective-permute-start.3 = (bf16[256,2560]{1,0:T(8,128)(2,1)}, bf16[256,2560]{1,0:T(8,128)(2,1)S(1)}, u32[]{:S(2)}, u32[]{:S(2)}) collective-permute-start(bf16[256,2560]{1,0:T(8,128)(2,1)} %refs_5_.1), channel_id=1, source_target_pairs={{0,2},{2,0},{4,6},{6,4},{8,10},{10,8},{12,14},{14,12},{16,18},{18,... | collective-permute-start | bytes 3932168 | tf_op jit(solution)/shard_map/ppermute | solution.py:34
  5.7 2.7 %shard_map.109 = (bf16[128,1024]{1,0:T(8,128)(2,1)}, bf16[128,1280]{1,0:T(8,128)(2,1)}, bf16[128,1792]{1,0:T(8,128)(2,1)}, bf16[128,1792]{1,0:T(8,128)(2,1)}, bf16[128,512]{1,0:T(8,128)(2,1)}) custom-call(s32[2]{0:T(128)} %pad_add_fusion.place, bf16[128,4096]{1,0:T(8,128)(2,1)} %source.1, bf16[128,2560]{1,0:T(8,128)(2,1)} %gate.1, bf16[128,2560]{1,0:T(8,128)(2,1)} %up.1), custom_call_target="tpu_custom_call" | custom-call | tf_op jit(solution)/shard_map/pallas_call | solution.py:122
  8.5 1.6 %collective-permute-start = (bf16[128,1792]{1,0:T(8,128)(2,1)}, bf16[128,1792]{1,0:T(8,128)(2,1)S(1)}, u32[]{:S(2)}, u32[]{:S(2)}) collective-permute-start(bf16[128,1792]{1,0:T(8,128)(2,1)} %get-tuple-element.66.refs_1_), channel_id=1, source_target_pairs={{0,8},{2,10},{4,12},{6,14},{8,0},{10,2},{12,4},{14,6},{16,24},{18,... | collective-permute-start | bytes 1376264 | tf_op jit(solution)/shard_map/ppermute | solution.py:34
  10.0 2.6 %collective-permute-start.1 = (bf16[128,1792]{1,0:T(8,128)(2,1)}, bf16[128,1792]{1,0:T(8,128)(2,1)S(1)}, u32[]{:S(2)}, u32[]{:S(2)}) collective-permute-start(bf16[128,1792]{1,0:T(8,128)(2,1)} %get-tuple-element.67), channel_id=1, source_target_pairs={{0,16},{2,18},{4,20},{6,22},{8,24},{10,26},{12,28},{14,30},{16,0},... | collective-permute-start | bytes 1376264 | tf_op jit(solution)/shard_map/ppermute | solution.py:34
  12.9 22.3 %collective-permute-done.2.refs_2_ = bf16[128,512]{1,0:T(8,128)(2,1)S(1)} collective-permute-done((bf16[128,512]{1,0:T(8,128)(2,1)}, bf16[128,512]{1,0:T(8,128)(2,1)S(1)}, u32[]{:S(2)}, u32[]{:S(2)}) %collective-permute-start.2) | collective-permute-done | bytes 131104 | tf_op jit(solution)/shard_map/ppermute | solution.py:34
  36.8 2.5 %collective-permute-start.5 = (bf16[128,2560]{1,0:T(8,128)(2,1)S(1)}, bf16[128,2560]{1,0:T(8,128)(2,1)S(1)}, u32[]{:S(2)}, u32[]{:S(2)}) collective-permute-start(bf16[128,2560]{1,0:T(8,128)(2,1)S(1)} %get-tuple-element.79), channel_id=1, source_target_pairs={{0,8},{2,10},{4,12},{6,14},{8,0},{10,2},{12,4},{14,6},{16,24},{18,... | collective-permute-start | bytes 1966088 | tf_op jit(solution)/shard_map/ppermute | solution.py:34
  42.2 16.1 %collective-permute-done.6.refs_3_ = bf16[128,1280]{1,0:T(8,128)(2,1)S(1)} collective-permute-done((bf16[128,1280]{1,0:T(8,128)(2,1)S(1)}, bf16[128,1280]{1,0:T(8,128)(2,1)S(1)}, u32[]{:S(2)}, u32[]{:S(2)}) %collective-permute-start.6) | collective-permute-done | bytes 327712 | tf_op jit(solution)/shard_map/ppermute | solution.py:34
  59.1 3.3 %collective-permute-start.8 = (bf16[128,1280]{1,0:T(8,128)(2,1)S(1)}, bf16[128,1280]{1,0:T(8,128)(2,1)S(1)}, u32[]{:S(2)}, u32[]{:S(2)}) collective-permute-start(bf16[128,1280]{1,0:T(8,128)(2,1)S(1)} %collective-permute-done.6.refs_3_), channel_id=1, source_target_pairs={{0,8},{2,10},{4,12},{6,14},{8,0},{10,2},{12,4},{14,6},{16,24},{18,... | collective-permute-start | bytes 983048 | tf_op jit(solution)/shard_map/ppermute | solution.py:34
  62.4 1.6 %shard_map.113 = (bf16[256,1280]{1,0:T(8,128)(2,1)S(1)}, bf16[256,1280]{1,0:T(8,128)(2,1)S(1)}) custom-call(bf16[512,1024]{1,0:T(8,128)(2,1)S(1)} %shard_map.112.refs_0_, bf16[128,1792]{1,0:T(8,128)(2,1)S(1)} %copy-done.2, bf16[128,1792]{1,0:T(8,128)(2,1)S(1)} %collective-permute-done.refs_0_.refs_2_, ...), custom_call_target="tpu_custom_call" | custom-call | tf_op jit(solution)/shard_map/pallas_call | solution.py:366
  65.2 2.2 %shard_map.114 = (bf16[128,2560]{1,0:T(8,128)(2,1)S(1)}, bf16[128,2560]{1,0:T(8,128)(2,1)S(1)}) custom-call(bf16[512,1024]{1,0:T(8,128)(2,1)S(1)} %shard_map.112.refs_0_, bf16[256,2560]{1,0:T(8,128)(2,1)S(1)} %copy-done, bf16[256,2560]{1,0:T(8,128)(2,1)S(1)} %collective-permute-done.3.refs_0_.refs_2_.refs_6_, ...), custom_call_target="tpu_custom_call" | custom-call | tf_op jit(solution)/shard_map/pallas_call | solution.py:366
  72.0 9.8 %collective-permute-done.11.refs_2_ = bf16[256,1280]{1,0:T(8,128)(2,1)S(1)} collective-permute-done((bf16[256,1280]{1,0:T(8,128)(2,1)S(1)}, bf16[256,1280]{1,0:T(8,128)(2,1)S(1)}, u32[]{:S(2)}, u32[]{:S(2)}) %collective-permute-start.11) | collective-permute-done | bytes 655392 | tf_op jit(solution)/shard_map/ppermute | solution.py:34
  82.3 2.1 %shard_map.116 = (f32[256,1280]{1,0:T(8,128)S(1)}, f32[128,1280]{1,0:T(8,128)S(1)}, f32[128,1280]{1,0:T(8,128)S(1)}) custom-call(bf16[512,1024]{1,0:T(8,128)(2,1)S(1)} %shard_map.112.refs_0_, bf16[128,1792]{1,0:T(8,128)(2,1)S(1)} %copy-done.2, bf16[128,1792]{1,0:T(8,128)(2,1)S(1)} %collective-permute-done.refs_0_.refs_2_, ...), custom_call_target="tpu_custom_call" | custom-call | tf_op jit(solution)/shard_map/pallas_call | solution.py:366
  84.4 5.1 %shard_map.117 = (f32[256,1280]{1,0:T(8,128)S(1)}, f32[128,1280]{1,0:T(8,128)S(1)}, f32[128,1280]{1,0:T(8,128)S(1)}, f32[128,2560]{1,0:T(8,128)S(1)}, f32[64,2560]{1,0:T(8,128)S(1)}, /*index=5*/f32[64,2560]{1,0:T(8,128)S(1)}) custom-call(bf16[512,1024]{1,0:T(8,128)(2,1)S(1)} %shard_map.112.refs_0_, bf16[128,1280]{1,0:T(8,128)(2,1)S(1)} %copy-done.1, ...), custom_call_target="tpu_custom_call" | custom-call | tf_op jit(solution)/shard_map/pallas_call | solution.py:366
  89.5 2.5 %collective-permute-done.14.refs_3_.refs_5_ = bf16[256,1280]{1,0:T(8,128)(2,1)S(1)} collective-permute-done((bf16[256,1280]{1,0:T(8,128)(2,1)S(1)}, bf16[256,1280]{1,0:T(8,128)(2,1)S(1)}, u32[]{:S(2)}, u32[]{:S(2)}) %collective-permute-start.14) | collective-permute-done | bytes 655392 | tf_op jit(solution)/shard_map/ppermute | solution.py:34
  92.1 2.5 %collective-permute-start.16 = (bf16[128,2560]{1,0:T(8,128)(2,1)S(1)}, bf16[128,2560]{1,0:T(8,128)(2,1)S(1)}, u32[]{:S(2)}, u32[]{:S(2)}) collective-permute-start(bf16[128,2560]{1,0:T(8,128)(2,1)S(1)} %shard_map.119), channel_id=1, source_target_pairs={{0,2},{2,0},{4,6},{6,4},{8,10},{10,8},{12,14},{14,12},{16,18},{18,... | collective-permute-start | bytes 1966088 | tf_op jit(solution)/shard_map/ppermute | solution.py:34
  95.4 3.0 %collective-permute-done.18.refs_1_ = bf16[128,2560]{1,0:T(8,128)(2,1)S(1)} collective-permute-done((bf16[128,2560]{1,0:T(8,128)(2,1)S(1)}, bf16[128,2560]{1,0:T(8,128)(2,1)S(1)}, u32[]{:S(2)}, u32[]{:S(2)}) %collective-permute-start.18) | collective-permute-done | bytes 655392 | tf_op jit(solution)/shard_map/ppermute | solution.py:34
  99.3 4.6 %collective-permute-done.17.refs_1_ = bf16[128,2560]{1,0:T(8,128)(2,1)S(1)} collective-permute-done((bf16[128,2560]{1,0:T(8,128)(2,1)S(1)}, bf16[128,2560]{1,0:T(8,128)(2,1)S(1)}, u32[]{:S(2)}, u32[]{:S(2)}) %collective-permute-start.17) | collective-permute-done | bytes 655392 | tf_op jit(solution)/shard_map/ppermute | solution.py:34
  106.2 2.5 %psum.14.row_sum = f32[1,256]{1,0:T(1,128)S(1)} all-reduce(f32[1,256]{1,0:T(1,128)S(1)} %get-tuple-element.110), channel_id=1, replica_groups=mesh['dp'=16,'mp'=2] {'mp'}, use_global_device_ids=true, to_apply=%region_0.0 | all-reduce | flops 256 | bytes 2048 | tf_op jit(solution)/shard_map/psum | solution.py:466
  109.4 3.3 %collective-permute-start.19 = (f32[5248]{0:T(1024)S(1)}, f32[5248]{0:T(1024)S(1)}, u32[]{:S(2)}, u32[]{:S(2)}) collective-permute-start(f32[5248]{0:T(1024)S(1)} %reduce), channel_id=1, source_target_pairs={{0,2},{2,0},{4,6},{6,4},{8,10},{10,8},{12,14},{14,12},{16,18},{18,... | collective-permute-start | bytes 62984 | tf_op jit(solution)/shard_map/ppermute | solution.py:34
  116.9 1.8 %collective-permute-done.21 = f32[5248]{0:T(1024)S(1)} collective-permute-done((f32[5248]{0:T(1024)S(1)}, f32[5248]{0:T(1024)S(1)}, u32[]{:S(2)}, u32[]{:S(2)}) %collective-permute-start.21) | collective-permute-done | bytes 21024 | tf_op jit(solution)/shard_map/ppermute | solution.py:34
  118.7 2.0 %collective-permute-start.22 = (f32[5248]{0:T(1024)S(1)}, f32[5248]{0:T(1024)S(1)}, u32[]{:S(2)}, u32[]{:S(2)}) collective-permute-start(f32[5248]{0:T(1024)S(1)} %add_add_fusion.1), channel_id=1, source_target_pairs={{0,8},{2,10},{4,12},{6,14},{8,0},{10,2},{12,4},{14,6},{16,24},{18,... | collective-permute-start | bytes 62984 | tf_op jit(solution)/shard_map/ppermute | solution.py:34
  123.2 3.3 %fusion.8 = (bf16[128,2560]{1,0:T(8,128)(2,1)}, bf16[128,2560]{1,0:T(8,128)(2,1)}) fusion(bf16[128,2560]{1,0:T(8,128)(2,1)S(1)} %copy-done.10, f32[128,2560]{1,0:T(8,128)S(1)} %convert_add_fusion.2, bf16[64,2560]{1,0:T(8,128)(2,1)} %collective-permute-done.26, bf16[64,2560]{1,0:T(8,128)(2,1)} %collective-permute-done.25, bf16[128,2560]{1,0:T(8,128)(2,1)S(1)} %copy-done.11), kind=kLoop, calls=%fused_computation.15 | loop fusion | flops 9830400 | bytes 4587520 | tf_op jit(solution)/shard_map/convert_element_type | solution.py:29
  128.1 2.4 %psum.15.terms = f32[1,128]{1,0:T(1,128)S(1)} all-reduce(f32[1,128]{1,0:T(1,128)S(1)} %get-tuple-element.120), channel_id=1, replica_groups=mesh['dp'=16,'mp'=2] {'mp'}, use_global_device_ids=true, to_apply=%region_1.0 | all-reduce | flops 128 | bytes 1024 | tf_op jit(solution)/shard_map/psum | solution.py:492
  130.5 2.2 %shard_map.125 = (f32[256,2560]{1,0:T(8,128)}, f32[1,128]{1,0:T(1,128)}) custom-call(f32[256,2560]{1,0:T(8,128)S(1)} %get-tuple-element.109.grad, f32[1,256]{1,0:T(1,128)S(1)} %copy-done.9, f32[1,2560]{1,0:T(1,128)S(1)} %get-tuple-element.119.col_moment_new, f32[1,128]{1,0:T(1,128)S(1)} %psum.15.terms, f32[1,5248]{1,0:T(1,128)S(1)} %broadcast_in_dim.10.sums.row_total), custom_call_target="tpu_custom_call" | custom-call | tf_op jit(solution)/shard_map/pallas_call | solution.py:320
  (87 shorter events, 26.8 us)
Async XLA Ops:
  0.6 34.5 %collective-permute-start.3 = (bf16[256,2560]{1,0:T(8,128)(2,1)}, bf16[256,2560]{1,0:T(8,128)(2,1)S(1)}, u32[]{:S(2)}, u32[]{:S(2)}) collective-permute-start(bf16[256,2560]{1,0:T(8,128)(2,1)} %refs_5_.1), channel_id=1, source_target_pairs={{0,2},{2,0},{4,6},{6,4},{8,10},{10,8},{12,14},{14,12},{16,18},{18,... | collective-permute-start | bytes 3932168 | tf_op jit(solution)/shard_map/ppermute | solution.py:34
  3.6 31.5 %collective-permute-start.4 = (bf16[256,2560]{1,0:T(8,128)(2,1)}, bf16[256,2560]{1,0:T(8,128)(2,1)S(1)}, u32[]{:S(2)}, u32[]{:S(2)}) collective-permute-start(bf16[256,2560]{1,0:T(8,128)(2,1)} %refs_5_.1), channel_id=1, source_target_pairs={{0,4},{2,6},{4,0},{6,2},{8,12},{10,14},{12,8},{14,10},{16,20},{18,... | collective-permute-start | bytes 3932168 | tf_op jit(solution)/shard_map/ppermute | solution.py:34
  8.5 27.2 %collective-permute-start = (bf16[128,1792]{1,0:T(8,128)(2,1)}, bf16[128,1792]{1,0:T(8,128)(2,1)S(1)}, u32[]{:S(2)}, u32[]{:S(2)}) collective-permute-start(bf16[128,1792]{1,0:T(8,128)(2,1)} %get-tuple-element.66.refs_1_), channel_id=1, source_target_pairs={{0,8},{2,10},{4,12},{6,14},{8,0},{10,2},{12,4},{14,6},{16,24},{18,... | collective-permute-start | bytes 1376264 | tf_op jit(solution)/shard_map/ppermute | solution.py:34
  10.0 26.6 %collective-permute-start.1 = (bf16[128,1792]{1,0:T(8,128)(2,1)}, bf16[128,1792]{1,0:T(8,128)(2,1)S(1)}, u32[]{:S(2)}, u32[]{:S(2)}) collective-permute-start(bf16[128,1792]{1,0:T(8,128)(2,1)} %get-tuple-element.67), channel_id=1, source_target_pairs={{0,16},{2,18},{4,20},{6,22},{8,24},{10,26},{12,28},{14,30},{16,0},... | collective-permute-start | bytes 1376264 | tf_op jit(solution)/shard_map/ppermute | solution.py:34
  12.6 22.5 %collective-permute-start.2 = (bf16[128,512]{1,0:T(8,128)(2,1)}, bf16[128,512]{1,0:T(8,128)(2,1)S(1)}, u32[]{:S(2)}, u32[]{:S(2)}) collective-permute-start(bf16[128,512]{1,0:T(8,128)(2,1)} %get-tuple-element.68), channel_id=1, source_target_pairs={{0,24},{2,26},{4,28},{6,30},{8,16},{10,18},{12,20},{14,22},{16,8},... | collective-permute-start | bytes 393224 | tf_op jit(solution)/shard_map/ppermute | solution.py:34
  36.8 22.3 %collective-permute-start.5 = (bf16[128,2560]{1,0:T(8,128)(2,1)S(1)}, bf16[128,2560]{1,0:T(8,128)(2,1)S(1)}, u32[]{:S(2)}, u32[]{:S(2)}) collective-permute-start(bf16[128,2560]{1,0:T(8,128)(2,1)S(1)} %get-tuple-element.79), channel_id=1, source_target_pairs={{0,8},{2,10},{4,12},{6,14},{8,0},{10,2},{12,4},{14,6},{16,24},{18,... | collective-permute-start | bytes 1966088 | tf_op jit(solution)/shard_map/ppermute | solution.py:34
  39.4 19.0 %collective-permute-start.6 = (bf16[128,1280]{1,0:T(8,128)(2,1)S(1)}, bf16[128,1280]{1,0:T(8,128)(2,1)S(1)}, u32[]{:S(2)}, u32[]{:S(2)}) collective-permute-start(bf16[128,1280]{1,0:T(8,128)(2,1)S(1)} %copy-done.1), channel_id=1, source_target_pairs={{0,16},{2,18},{4,20},{6,22},{8,24},{10,26},{12,28},{14,30},{16,0},... | collective-permute-start | bytes 983048 | tf_op jit(solution)/shard_map/ppermute | solution.py:34
  40.5 24.6 %collective-permute-start.10 = (bf16[128,2560]{1,0:T(8,128)(2,1)S(1)}, bf16[128,2560]{1,0:T(8,128)(2,1)S(1)}, u32[]{:S(2)}, u32[]{:S(2)}) collective-permute-start(bf16[128,2560]{1,0:T(8,128)(2,1)S(1)} %get-tuple-element.74), channel_id=1, source_target_pairs={{0,2},{2,0},{4,6},{6,4},{8,10},{10,8},{12,14},{14,12},{16,18},{18,... | collective-permute-start | bytes 1966088 | tf_op jit(solution)/shard_map/ppermute | solution.py:34
  41.1 24.1 %collective-permute-start.9 = (bf16[128,2560]{1,0:T(8,128)(2,1)S(1)}, bf16[128,2560]{1,0:T(8,128)(2,1)S(1)}, u32[]{:S(2)}, u32[]{:S(2)}) collective-permute-start(bf16[128,2560]{1,0:T(8,128)(2,1)S(1)} %get-tuple-element.73), channel_id=1, source_target_pairs={{0,4},{2,6},{4,0},{6,2},{8,12},{10,14},{12,8},{14,10},{16,20},{18,... | collective-permute-start | bytes 1966088 | tf_op jit(solution)/shard_map/ppermute | solution.py:34
  59.1 8.3 %collective-permute-start.8 = (bf16[128,1280]{1,0:T(8,128)(2,1)S(1)}, bf16[128,1280]{1,0:T(8,128)(2,1)S(1)}, u32[]{:S(2)}, u32[]{:S(2)}) collective-permute-start(bf16[128,1280]{1,0:T(8,128)(2,1)S(1)} %collective-permute-done.6.refs_3_), channel_id=1, source_target_pairs={{0,8},{2,10},{4,12},{6,14},{8,0},{10,2},{12,4},{14,6},{16,24},{18,... | collective-permute-start | bytes 983048 | tf_op jit(solution)/shard_map/ppermute | solution.py:34
  64.0 17.7 %collective-permute-start.11 = (bf16[256,1280]{1,0:T(8,128)(2,1)S(1)}, bf16[256,1280]{1,0:T(8,128)(2,1)S(1)}, u32[]{:S(2)}, u32[]{:S(2)}) collective-permute-start(bf16[256,1280]{1,0:T(8,128)(2,1)S(1)} %get-tuple-element.85), channel_id=1, source_target_pairs={{0,2},{2,0},{4,6},{6,4},{8,10},{10,8},{12,14},{14,12},{16,18},{18,... | collective-permute-start | bytes 1966088 | tf_op jit(solution)/shard_map/ppermute | solution.py:34
  64.6 17.7 %collective-permute-start.12 = (bf16[256,1280]{1,0:T(8,128)(2,1)S(1)}, bf16[256,1280]{1,0:T(8,128)(2,1)S(1)}, u32[]{:S(2)}, u32[]{:S(2)}) collective-permute-start(bf16[256,1280]{1,0:T(8,128)(2,1)S(1)} %get-tuple-element.90), channel_id=1, source_target_pairs={{0,4},{2,6},{4,0},{6,2},{8,12},{10,14},{12,8},{14,10},{16,20},{18,... | collective-permute-start | bytes 1966088 | tf_op jit(solution)/shard_map/ppermute | solution.py:34
  68.9 23.1 %collective-permute-start.14 = (bf16[256,1280]{1,0:T(8,128)(2,1)S(1)}, bf16[256,1280]{1,0:T(8,128)(2,1)S(1)}, u32[]{:S(2)}, u32[]{:S(2)}) collective-permute-start(bf16[256,1280]{1,0:T(8,128)(2,1)S(1)} %get-tuple-element.98), channel_id=1, source_target_pairs={{0,4},{2,6},{4,0},{6,2},{8,12},{10,14},{12,8},{14,10},{16,20},{18,... | collective-permute-start | bytes 1966088 | tf_op jit(solution)/shard_map/ppermute | solution.py:34
  70.5 24.2 %collective-permute-start.13 = (bf16[256,1280]{1,0:T(8,128)(2,1)S(1)}, bf16[256,1280]{1,0:T(8,128)(2,1)S(1)}, u32[]{:S(2)}, u32[]{:S(2)}) collective-permute-start(bf16[256,1280]{1,0:T(8,128)(2,1)S(1)} %get-tuple-element.92), channel_id=1, source_target_pairs={{0,2},{2,0},{4,6},{6,4},{8,10},{10,8},{12,14},{14,12},{16,18},{18,... | collective-permute-start | bytes 1966088 | tf_op jit(solution)/shard_map/ppermute | solution.py:34
  72.0 26.5 %collective-permute-start.18 = (bf16[128,2560]{1,0:T(8,128)(2,1)S(1)}, bf16[128,2560]{1,0:T(8,128)(2,1)S(1)}, u32[]{:S(2)}, u32[]{:S(2)}) collective-permute-start(bf16[128,2560]{1,0:T(8,128)(2,1)S(1)} %get-tuple-element.106), channel_id=1, source_target_pairs={{0,16},{2,18},{4,20},{6,22},{8,24},{10,26},{12,28},{14,30},{16,0},... | collective-permute-start | bytes 1966088 | tf_op jit(solution)/shard_map/ppermute | solution.py:34
  81.8 22.1 %collective-permute-start.17 = (bf16[128,2560]{1,0:T(8,128)(2,1)S(1)}, bf16[128,2560]{1,0:T(8,128)(2,1)S(1)}, u32[]{:S(2)}, u32[]{:S(2)}) collective-permute-start(bf16[128,2560]{1,0:T(8,128)(2,1)S(1)} %get-tuple-element.104), channel_id=1, source_target_pairs={{0,8},{2,10},{4,12},{6,14},{8,0},{10,2},{12,4},{14,6},{16,24},{18,... | collective-permute-start | bytes 1966088 | tf_op jit(solution)/shard_map/ppermute | solution.py:34
  92.1 12.8 %collective-permute-start.16 = (bf16[128,2560]{1,0:T(8,128)(2,1)S(1)}, bf16[128,2560]{1,0:T(8,128)(2,1)S(1)}, u32[]{:S(2)}, u32[]{:S(2)}) collective-permute-start(bf16[128,2560]{1,0:T(8,128)(2,1)S(1)} %shard_map.119), channel_id=1, source_target_pairs={{0,2},{2,0},{4,6},{6,4},{8,10},{10,8},{12,14},{14,12},{16,18},{18,... | collective-permute-start | bytes 1966088 | tf_op jit(solution)/shard_map/ppermute | solution.py:34
  94.8 10.7 %collective-permute-start.15 = (bf16[128,2560]{1,0:T(8,128)(2,1)S(1)}, bf16[128,2560]{1,0:T(8,128)(2,1)S(1)}, u32[]{:S(2)}, u32[]{:S(2)}) collective-permute-start(bf16[128,2560]{1,0:T(8,128)(2,1)S(1)} %shard_map.118), channel_id=1, source_target_pairs={{0,4},{2,6},{4,0},{6,2},{8,12},{10,14},{12,8},{14,10},{16,20},{18,... | collective-permute-start | bytes 1966088 | tf_op jit(solution)/shard_map/ppermute | solution.py:34
  99.3 23.9 %collective-permute-start.26 = (bf16[64,2560]{1,0:T(8,128)(2,1)}, bf16[64,2560]{1,0:T(8,128)(2,1)}, u32[]{:S(2)}, u32[]{:S(2)}) collective-permute-start(bf16[64,2560]{1,0:T(8,128)(2,1)} %shard_map.121), channel_id=1, source_target_pairs={{0,8},{2,10},{4,12},{6,14},{8,0},{10,2},{12,4},{14,6},{16,24},{18,... | collective-permute-start | bytes 983048 | tf_op jit(solution)/shard_map/ppermute | solution.py:34
  104.8 18.4 %collective-permute-start.25 = (bf16[64,2560]{1,0:T(8,128)(2,1)}, bf16[64,2560]{1,0:T(8,128)(2,1)}, u32[]{:S(2)}, u32[]{:S(2)}) collective-permute-start(bf16[64,2560]{1,0:T(8,128)(2,1)} %shard_map.120), channel_id=1, source_target_pairs={{0,16},{2,18},{4,20},{6,22},{8,24},{10,26},{12,28},{14,30},{16,0},... | collective-permute-start | bytes 983048 | tf_op jit(solution)/shard_map/ppermute | solution.py:34
  109.4 7.5 %collective-permute-start.19 = (f32[5248]{0:T(1024)S(1)}, f32[5248]{0:T(1024)S(1)}, u32[]{:S(2)}, u32[]{:S(2)}) collective-permute-start(f32[5248]{0:T(1024)S(1)} %reduce), channel_id=1, source_target_pairs={{0,2},{2,0},{4,6},{6,4},{8,10},{10,8},{12,14},{14,12},{16,18},{18,... | collective-permute-start | bytes 62984 | tf_op jit(solution)/shard_map/ppermute | solution.py:34
  118.7 7.7 %collective-permute-start.22 = (f32[5248]{0:T(1024)S(1)}, f32[5248]{0:T(1024)S(1)}, u32[]{:S(2)}, u32[]{:S(2)}) collective-permute-start(f32[5248]{0:T(1024)S(1)} %add_add_fusion.1), channel_id=1, source_target_pairs={{0,8},{2,10},{4,12},{6,14},{8,0},{10,2},{12,4},{14,6},{16,24},{18,... | collective-permute-start | bytes 62984 | tf_op jit(solution)/shard_map/ppermute | solution.py:34
  120.7 5.8 %collective-permute-start.23 = (f32[5248]{0:T(1024)S(1)}, f32[5248]{0:T(1024)S(1)}, u32[]{:S(2)}, u32[]{:S(2)}) collective-permute-start(f32[5248]{0:T(1024)S(1)} %add_add_fusion.1), channel_id=1, source_target_pairs={{0,16},{2,18},{4,20},{6,22},{8,24},{10,26},{12,28},{14,30},{16,0},... | collective-permute-start | bytes 62984 | tf_op jit(solution)/shard_map/ppermute | solution.py:34
  121.8 5.6 %collective-permute-start.24 = (f32[5248]{0:T(1024)S(1)}, f32[5248]{0:T(1024)S(1)}, u32[]{:S(2)}, u32[]{:S(2)}) collective-permute-start(f32[5248]{0:T(1024)S(1)} %add_add_fusion.1), channel_id=1, source_target_pairs={{0,24},{2,26},{4,28},{6,30},{8,16},{10,18},{12,20},{14,22},{16,8},... | collective-permute-start | bytes 62984 | tf_op jit(solution)/shard_map/ppermute | solution.py:34
  (18 other events, 150.5 us)
